TPU v7x, 32 devices: a whole 2x2x4 slice. The times are simulated.
32 devices in a mesh: group: 2 (over x), term: 16 (over z, y, core).
Axes of the slice: x: 2, y: 2, z: 4, core: 2. Of those that a mesh axis runs over, the one named last changes fastest.
Arguments:
- wavefn: float32 [64, 128, 128], P(('group', 'term')), parts along dimension 0, may hold values from -6 to 6
- left_ops: float32 [256, 128, 128], P(('group', 'term')), parts along dimension 0, may hold values from -0.5 to 1.1
- right_ops: float32 [256, 128, 128], P(('group', 'term')), parts along dimension 0, may hold values from -0.5 to 1.1
- precond: float32 [64, 128, 128], P(('group', 'term')), parts along dimension 0, may hold values from 0.02 to 0.2
- fetch_map: int32 [16, 16], replicated, may hold values from 0 to 1
- store_map: int32 [16, 16], replicated, may hold values from 0 to 1
- pair_list: int32 [16, 128, 3], P('term'), may hold values from 0 to 15, as said below
- live_count: int32 [16], P('term'), may hold values from 32 to 128, as said below
Outputs:
- next_vector: float32 [64, 128, 128], P(('group', 'term')), parts along dimension 0
- residual: float32 [64, 128, 128], P(('group', 'term')), parts along dimension 0
There are 2 independent parts, one for each index of `group`. A program takes and returns all parts, laid end to end along the dimension named above; an argument that names none is the same for every part. Nothing has to cross between parts.
Inputs may be any that keep to these rules, and one draw needn't show every extreme that they name: `pair_list`: column 0 is a window slot below 16, column 1 a local term below 8, column 2 a result slot below 16. `live_count`: some device has all 128 pairs live, some only 32.
All inputs are finite; a program needn't handle non-finite values.
Results may differ from a plain program's by a relative error of at most 0.0003.
Values sent between devices are 32-bit elements; how exact they have to be, the bound alone decides.
No kernel may reach another device: no remote copies, remote signals or barrier semaphores. Data moves between devices by JAX's collectives and lax.ppermute only.
A program may use at most 128 MiB of HBM per device.

v0:
```python
import functools

import jax
import jax.numpy as jnp
from jax import lax
from jax.experimental import pallas as pl
from jax.experimental.pallas import tpu as pltpu
from jax.sharding import PartitionSpec as P

ITERS = 2
CORE, ROW = 1, 2
SMEM = pl.BlockSpec(memory_space=pltpu.SMEM)
VMEM = pl.BlockSpec(memory_space=pltpu.VMEM)
PARAMS = pltpu.CompilerParams(vmem_limit_bytes=56 * 2**20)


def halves(x):
    high = x.astype(jnp.bfloat16)
    return high, (x - high.astype(jnp.float32)).astype(jnp.bfloat16)


def tile_sum(x):
    return jnp.sum(x.reshape(-1, 8, x.shape[-1]), axis=0)


def prep_kernel(n, spare, me_ref, pairs_ref, live_ref, left_ref, right_ref,
                l4_ref, rr_ref, first_ref, second_ref, dst_ref, one_ref, two_ref, count_ref, seen_ref):
    me = me_ref[0]
    terms = left_ref.shape[0]
    width = left_ref.shape[1]
    zero = terms * n

    def clear(cell, carry):
        first_ref[cell] = zero
        second_ref[cell] = zero
        seen_ref[cell] = 0
        return carry

    lax.fori_loop(0, terms * n, clear, 0, unroll=8)

    def pair(p, carry):
        extra, ops = carry
        a = lax.bitwise_xor(pairs_ref[3 * p], me)
        j = pairs_ref[3 * p + 1]
        o = lax.bitwise_xor(pairs_ref[3 * p + 2], me)
        cell = j * n + o
        source = a * terms + j
        seen = seen_ref[cell]
        seen_ref[cell] = seen + 1
        before = second_ref[cell]
        place = jnp.where(seen == 2, spare + extra, before)
        first_ref[cell] = jnp.where(seen == 0, source, first_ref[cell])
        second_ref[cell] = jnp.where(seen == 0, before, jnp.where(seen == 1, source, place))
        dst_ref[ops] = place
        one_ref[ops] = before
        two_ref[ops] = source
        return extra + (seen == 2).astype(jnp.int32), ops + (seen >= 2).astype(jnp.int32)

    _, ops = lax.fori_loop(0, live_ref[0], pair, (jnp.int32(0), jnp.int32(0)))
    count_ref[0] = ops

    for j in range(terms):
        high, low = halves(left_ref[j])
        for k, part in enumerate((high, low, high, low)):
            l4_ref[j, :, k * width:(k + 1) * width] = part
        high, low = halves(right_ref[j])
        for k in range(2):
            row = (k * terms + j) * width
            rr_ref[row:row + width, :width] = high
            rr_ref[row:row + width, width:] = low


def prep(n, me, pairs, live, left_ops, right_ops):
    terms, width = left_ops.shape[:2]
    npairs = pairs.shape[0] // 3
    table = jax.ShapeDtypeStruct((terms * n,), jnp.int32)
    listed = jax.ShapeDtypeStruct((npairs,), jnp.int32)
    return pl.pallas_call(
        functools.partial(prep_kernel, n, terms * n + 1),
        out_shape=(
            jax.ShapeDtypeStruct((terms, width, 4 * width), jnp.bfloat16),
            jax.ShapeDtypeStruct((2 * terms * width, 2 * width), jnp.bfloat16),
            table, table, listed, listed, listed,
            jax.ShapeDtypeStruct((1,), jnp.int32),
        ),
        in_specs=[SMEM] * 3 + [VMEM] * 2,
        out_specs=[VMEM] * 2 + [SMEM] * 6,
        scratch_shapes=[pltpu.SMEM((terms * n,), jnp.int32)],
        compiler_params=PARAMS,
        name="prep",
    )(me, pairs, live, left_ops, right_ops)


def apply_kernel(n, rows, me_ref, fetch_ref, store_ref, first_ref, second_ref, dst_ref, one_ref, two_ref,
                 count_ref, l4_ref, rr_ref, *refs):
    pieces, (out_ref, square_ref, field, block, total) = refs[:n], refs[n:]
    me = me_ref[0]
    terms, width = l4_ref.shape[:2]
    for r in range(n):
        high, low = halves(pieces[r][fetch_ref[lax.bitwise_xor(me, r) * n + me]])
        at = (r % 2) * width
        for k, part in enumerate((high, high, low, low)):
            field[r // 2, k * width:(k + 1) * width, at:at + width] = part
    square = jnp.zeros((8, width), jnp.float32)
    for r in range(n):
        square = square + tile_sum(pieces[r][...] * pieces[r][...])
    square_ref[...] = square
    product = jnp.zeros((8, width), jnp.float32)
    block[terms * n] = jnp.zeros((rows, width), jnp.float32)
    for start in range(0, width, rows):
        left = l4_ref[:, start:start + rows, :].reshape(terms * rows, 4 * width)

        def products(c, carry):
            both = jnp.dot(left, field[c], preferred_element_type=jnp.float32)
            for k in range(2):
                at = pl.multiple_of((2 * c + k) * terms, terms)
                block[pl.ds(at, terms)] = both[:, k * width:(k + 1) * width].reshape(terms, rows, width)
            return carry

        lax.fori_loop(0, n // 2, products, 0)

        def add(i, carry):
            block[dst_ref[i]] = block[one_ref[i]] + block[two_ref[i]]
            return carry

        lax.fori_loop(0, count_ref[0], add, 0)
        for j in range(terms):

            def cell(o, carry):
                at = j * n + o
                high, low = halves(block[first_ref[at]] + block[second_ref[at]])
                total[o, :, j * width:(j + 1) * width] = high
                total[o, :, (terms + j) * width:(terms + j + 1) * width] = low
                return carry

            lax.fori_loop(0, n, cell, 0, unroll=4)
        group = 8
        for o in range(0, n, group):
            both = jnp.dot(total[o:o + group].reshape(group * rows, 2 * terms * width), rr_ref[...],
                           preferred_element_type=jnp.float32)
            slots = both[:, :width] + both[:, width:]
            for k in range(group):
                slot = slots[k * rows:(k + 1) * rows]
                owner = lax.bitwise_xor(me, o + k)
                out_ref[owner, start:start + rows, :] = slot
                held = pieces[o + k][store_ref[me * n + owner], start:start + rows, :]
                product = product + tile_sum(held * slot)
    for r in range(n):
        out_ref[r, width:, :] = product


def apply(n, me, fetch, store, tables, pieces):
    l4 = tables[0]
    terms, width = l4.shape[:2]
    npairs = tables[4].shape[0]
    rows = width if n <= 16 else width // 4
    return pl.pallas_call(
        functools.partial(apply_kernel, n, rows),
        out_shape=(
            jax.ShapeDtypeStruct((n, width + 8, width), jnp.float32),
            jax.ShapeDtypeStruct((8, width), jnp.float32),
        ),
        in_specs=[SMEM] * 9 + [VMEM] * (2 + n),
        out_specs=[VMEM] * 2,
        scratch_shapes=[
            pltpu.VMEM((n // 2, 4 * width, 2 * width), jnp.bfloat16),
            pltpu.VMEM((terms * n + 1 + npairs // 3, rows, width), jnp.float32),
            pltpu.VMEM((n, rows, 2 * terms * width), jnp.bfloat16),
        ],
        compiler_params=PARAMS,
        name="apply",
    )(me, fetch, store, *tables[2:], *tables[:2], *pieces)


def landed(n, me_ref, store_ref, arrived_ref):
    me = me_ref[0]
    width = arrived_ref.shape[2]
    sums = [jnp.zeros((width, width), jnp.float32) for _ in range(2)]
    tile = jnp.zeros((8, width), jnp.float32)
    for r in range(n):
        mine = store_ref[r * n + me]
        for b in range(2):
            sums[b] = sums[b] + (mine == b).astype(jnp.float32) * arrived_ref[r, :width, :]
        tile = tile + arrived_ref[r, width:, :]
    return sums, jnp.sum(tile)


def step_kernel(n, me_ref, store_ref, arrived_ref, square_ref, vector_ref, precond_ref, out_ref):
    sigma, product = landed(n, me_ref, store_ref, arrived_ref)
    theta = product / jnp.sum(square_ref[...])
    for b in range(2):
        v = vector_ref[b]
        out_ref[b] = v - precond_ref[b] * (sigma[b] - theta * v)


def last_kernel(n, cells, me_ref, store_ref, arrived_ref, square_ref, vector_ref, precond_ref,
                residual_ref, out_ref, tile_ref):
    sigma, product = landed(n, me_ref, store_ref, arrived_ref)
    square = jnp.sum(square_ref[...])
    theta = product / square
    scale = 1.0 / jnp.sqrt(square / cells + 1e-06)
    tile = jnp.zeros(tile_ref.shape, jnp.float32)
    for b in range(2):
        v = vector_ref[b]
        residual = (sigma[b] - theta * v) * scale
        residual_ref[b] = residual
        corrected = v * scale - precond_ref[b] * residual
        out_ref[b] = corrected
        tile = tile + tile_sum(corrected * corrected)
    tile_ref[...] = tile


def gathered(n, x):
    def send(y, k):
        return lax.ppermute(y, "term", [(i, i ^ k) for i in range(n)])

    pieces = {0: x, ROW: send(x, ROW)}
    for k in range(4, n, 4):
        pieces[k] = send(x, k)
    for k in range(4, n, 4):
        pieces[k + ROW] = send(pieces[ROW], k) if k == 4 else send(pieces[k], ROW)
    for k in range(0, n, 2):
        pieces[k + CORE] = send(pieces[k], CORE)
    return [pieces[k] for k in range(n)]


def shards(wavefn, left_ops, right_ops, precond, fetch_map, store_map, pair_list, live_count):
    n = lax.axis_size("term")
    me = lax.axis_index("term").astype(jnp.int32).reshape(1)
    width = wavefn.shape[1]
    cells = wavefn.size * n
    fetch, store = fetch_map.reshape(-1), store_map.reshape(-1)
    tables = prep(n, me, pair_list.reshape(-1), live_count, left_ops, right_ops)
    block = jax.ShapeDtypeStruct(wavefn.shape, jnp.float32)
    tile = jax.ShapeDtypeStruct((8, width), jnp.float32)
    vector = wavefn
    for iteration in range(ITERS):
        slots, square = apply(n, me, fetch, store, tables, gathered(n, vector))
        arrived = lax.all_to_all(slots, "term", split_axis=0, concat_axis=0, tiled=True)
        last = iteration == ITERS - 1
        result = pl.pallas_call(
            functools.partial(last_kernel, n, cells) if last else functools.partial(step_kernel, n),
            out_shape=(block, block, tile) if last else block,
            in_specs=[SMEM] * 2 + [VMEM] * 4,
            out_specs=[VMEM] * 3 if last else VMEM,
            compiler_params=PARAMS,
            name="last" if last else "step",
        )(me, store, arrived, square, vector, precond)
        if not last:
            vector = result
    residual, corrected, partial = result
    tiles = lax.all_to_all(jnp.broadcast_to(partial[None], (n, 8, width)), "term",
                           split_axis=0, concat_axis=0, tiled=True)
    return corrected / jnp.sqrt(jnp.sum(tiles) / cells + 1e-06), residual


def solution(mesh):
    field = P(("group", "term"), None, None)
    return jax.shard_map(
        shards,
        mesh=mesh,
        in_specs=(field, field, field, field, P(), P(), P("term", None, None), P("term")),
        out_specs=(field, field),
        check_vma=False,
    )
```

profile of v0, /device:TPU:0, one launch (start us, length us, event | category | flops | bytes accessed | tf_op | source)
XLA Modules:
  0.0 167.2 jit_solution(17690520449039807219)
XLA Ops:
  0.6 5.1 %collective-permute-start.11 = (f32[2,128,128]{2,1,0:T(8,128)}, f32[2,128,128]{2,1,0:T(8,128)S(1)}, u32[]{:S(2)}, u32[]{:S(2)}) collective-permute-start(f32[2,128,128]{2,1,0:T(8,128)} %vector_ref.1), channel_id=1, source_target_pairs={{0,12},{1,13},{2,14},{3,15},{4,8},{5,9},{6,10},{7,11},{8,4},{9,5},... | collective-permute-start | bytes 393224 | tf_op jit(solution)/shard_map/ppermute | solution.py:215
  5.7 0.0 collective-permute-start.7
  5.7 0.6 collective-permute-start.3
  6.4 1.7 collective-permute-start.1
  8.1 0.0 collective-permute-start
  8.1 2.3 %collective-permute-done.11.refs_12_ = f32[2,128,128]{2,1,0:T(8,128)S(1)} collective-permute-done((f32[2,128,128]{2,1,0:T(8,128)}, f32[2,128,128]{2,1,0:T(8,128)S(1)}, u32[]{:S(2)}, u32[]{:S(2)}) %collective-permute-start.11) | collective-permute-done | bytes 131104 | tf_op jit(solution)/shard_map/ppermute | solution.py:215
  10.4 1.7 %collective-permute-start.13 = (f32[2,128,128]{2,1,0:T(8,128)S(1)}, f32[2,128,128]{2,1,0:T(8,128)S(1)}, u32[]{:S(2)}, u32[]{:S(2)}) collective-permute-start(f32[2,128,128]{2,1,0:T(8,128)S(1)} %collective-permute-done.11.refs_12_), channel_id=1, source_target_pairs={{0,2},{1,3},{2,0},{3,1},{4,6},{5,7},{6,4},{7,5},{8,10},{9,11},{10,... | collective-permute-start | bytes 393224 | tf_op jit(solution)/shard_map/ppermute | solution.py:215
  12.1 4.9 %collective-permute-done.7.refs_8_ = f32[2,128,128]{2,1,0:T(8,128)S(1)} collective-permute-done((f32[2,128,128]{2,1,0:T(8,128)}, f32[2,128,128]{2,1,0:T(8,128)S(1)}, u32[]{:S(2)}, u32[]{:S(2)}) %collective-permute-start.7) | collective-permute-done | bytes 131104 | tf_op jit(solution)/shard_map/ppermute | solution.py:215
  17.1 1.6 collective-permute-start.9
  18.6 0.0 collective-permute-done.1.refs_2_
  18.6 0.2 collective-permute-start.8
  18.8 0.0 collective-permute-start.5
  18.8 0.0 collective-permute-done.13.refs_14_
  18.8 0.4 collective-permute-start.2
  19.2 0.0 collective-permute-done.12.refs_13_
  19.3 0.2 collective-permute-start.4
  19.4 3.5 %collective-permute-done.9.refs_10_ = f32[2,128,128]{2,1,0:T(8,128)S(1)} collective-permute-done((f32[2,128,128]{2,1,0:T(8,128)S(1)}, f32[2,128,128]{2,1,0:T(8,128)S(1)}, u32[]{:S(2)}, u32[]{:S(2)}) %collective-permute-start.9) | collective-permute-done | bytes 131104 | tf_op jit(solution)/shard_map/ppermute | solution.py:215
  23.0 0.5 collective-permute-start.10
  23.5 1.1 collective-permute-done.5.refs_6_
  24.6 0.0 collective-permute-start.6
  25.2 1.4 reshape.18.store_ref
  26.6 1.3 reshape.19.fetch_ref
  27.9 0.8 copy.11
  28.6 0.8 reshape.20.pairs_ref
  29.4 4.0 %prep.1 = (bf16[8,128,512]{2,1,0:T(8,128)(2,1)}, bf16[2048,256]{1,0:T(8,128)(2,1)}, s32[128]{0:T(128)}, s32[128]{0:T(128)}, s32[128]{0:T(128)}, /*index=5*/s32[128]{0:T(128)}, s32[128]{0:T(128)}, s32[1]{0:T(128)}) custom-call(s32[1]{0:T(128)} %bitcast.me_ref, s32[384]{0:T(512)} %reshape.20.pairs_ref, s32[1]{0:T(128)S(6)} %copy.12.live_ref, ...), custom_call_target="tpu_custom_call" | custom-call | tf_op jit(solution)/shard_map/prep/pallas_call | solution.py:78
  33.5 0.0 collective-permute-done.4.refs_5_
  33.5 0.0 collective-permute-done.2.refs_3_
  33.5 0.0 collective-permute-done.10.refs_11_
  33.7 0.5 copy-done.20
  34.2 0.0 copy-done.18
  34.2 0.1 copy-done.22
  34.3 0.1 copy-done.24
  34.3 0.1 copy-done.26
  34.4 12.7 %apply.2 = (f32[16,136,128]{2,1,0:T(8,128)}, f32[8,128]{1,0:T(8,128)}) custom-call(s32[1]{0:T(128)} %bitcast.me_ref, s32[256]{0:T(256)} %reshape.19.fetch_ref, s32[256]{0:T(256)} %reshape.18.store_ref, s32[128]{0:T(128)} %get-tuple-element.17.first_ref, s32[128]{0:T(128)} %get-tuple-element.18.second_ref, s32[128]{0:T(128)} %get-tuple-element.19.dst_ref, ...), custom_call_target="tpu_custom_call" | custom-call | tf_op jit(solution)/shard_map/apply/pallas_call | solution.py:157
  47.1 33.8 %all_to_all.15.arrived_ref = f32[16,136,128]{2,1,0:T(8,128)} all-to-all(f32[16,136,128]{2,1,0:T(8,128)} %get-tuple-element.25), channel_id=1, replica_groups=mesh['group'=2,'term'=16] {'term'}, dimensions={0} | all-to-all | bytes 2228224 | tf_op jit(solution)/shard_map/all_to_all | solution.py:239
  80.9 2.2 %step.1.refs_0_.vector_ref = f32[2,128,128]{2,1,0:T(8,128)} custom-call(s32[1]{0:T(128)} %bitcast.me_ref, s32[256]{0:T(256)} %reshape.18.store_ref, f32[16,136,128]{2,1,0:T(8,128)} %all_to_all.15.arrived_ref, f32[8,128]{1,0:T(8,128)} %get-tuple-element.26.square_ref, f32[2,128,128]{2,1,0:T(8,128)} %vector_ref.1, f32[2,128,128]{2,1,0:T(8,128)} %precond_ref.3), custom_call_target="tpu_custom_call" | custom-call | tf_op jit(solution)/shard_map/step/pallas_call | solution.py:241
  83.0 1.5 collective-permute-start.26
  84.5 0.6 collective-permute-start.22
  85.2 2.3 %collective-permute-start.18 = (f32[2,128,128]{2,1,0:T(8,128)}, f32[2,128,128]{2,1,0:T(8,128)S(1)}, u32[]{:S(2)}, u32[]{:S(2)}) collective-permute-start(f32[2,128,128]{2,1,0:T(8,128)} %step.1.refs_0_.vector_ref), channel_id=1, source_target_pairs={{0,4},{1,5},{2,6},{3,7},{4,0},{5,1},{6,2},{7,3},{8,12},{9,13},{10,... | collective-permute-start | bytes 393224 | tf_op jit(solution)/shard_map/ppermute | solution.py:215
  87.4 0.6 collective-permute-start.16
  88.0 3.5 %collective-permute-done.26.refs_12_ = f32[2,128,128]{2,1,0:T(8,128)S(1)} collective-permute-done((f32[2,128,128]{2,1,0:T(8,128)}, f32[2,128,128]{2,1,0:T(8,128)S(1)}, u32[]{:S(2)}, u32[]{:S(2)}) %collective-permute-start.26) | collective-permute-done | bytes 131104 | tf_op jit(solution)/shard_map/ppermute | solution.py:215
  91.5 0.6 collective-permute-start.28
  92.1 5.1 %collective-permute-done.22.refs_8_ = f32[2,128,128]{2,1,0:T(8,128)S(1)} collective-permute-done((f32[2,128,128]{2,1,0:T(8,128)}, f32[2,128,128]{2,1,0:T(8,128)S(1)}, u32[]{:S(2)}, u32[]{:S(2)}) %collective-permute-start.22) | collective-permute-done | bytes 131104 | tf_op jit(solution)/shard_map/ppermute | solution.py:215
  97.3 0.7 collective-permute-start.24
  98.0 0.2 collective-permute-start.23
  98.2 0.0 collective-permute-start.20
  98.2 0.4 collective-permute-start.17
  98.6 0.0 collective-permute-done.27.refs_13_
  98.6 0.1 collective-permute-start.19
  98.8 4.4 %collective-permute-done.24.refs_10_ = f32[2,128,128]{2,1,0:T(8,128)S(1)} collective-permute-done((f32[2,128,128]{2,1,0:T(8,128)S(1)}, f32[2,128,128]{2,1,0:T(8,128)S(1)}, u32[]{:S(2)}, u32[]{:S(2)}) %collective-permute-start.24) | collective-permute-done | bytes 131104 | tf_op jit(solution)/shard_map/ppermute | solution.py:215
  103.2 0.5 collective-permute-start.25
  103.7 0.2 collective-permute-done.20.refs_6_
  104.0 0.6 collective-permute-done.29.refs_15_
  104.6 0.2 collective-permute-done.25.refs_11_
  104.8 0.5 collective-permute-done.21.refs_7_
  105.4 0.1 copy-done.28
  105.4 0.7 copy-done.29
  106.1 12.7 %apply.3 = (f32[16,136,128]{2,1,0:T(8,128)}, f32[8,128]{1,0:T(8,128)}) custom-call(s32[1]{0:T(128)} %bitcast.me_ref, s32[256]{0:T(256)} %reshape.19.fetch_ref, s32[256]{0:T(256)} %reshape.18.store_ref, s32[128]{0:T(128)} %get-tuple-element.17.first_ref, s32[128]{0:T(128)} %get-tuple-element.18.second_ref, s32[128]{0:T(128)} %get-tuple-element.19.dst_ref, ...), custom_call_target="tpu_custom_call" | custom-call | tf_op jit(solution)/shard_map/apply/pallas_call | solution.py:157
  118.8 32.9 %all_to_all.16.arrived_ref = f32[16,136,128]{2,1,0:T(8,128)} all-to-all(f32[16,136,128]{2,1,0:T(8,128)} %get-tuple-element.27), channel_id=1, replica_groups=mesh['group'=2,'term'=16] {'term'}, dimensions={0} | all-to-all | bytes 2228224 | tf_op jit(solution)/shard_map/all_to_all | solution.py:239
  151.7 2.2 %last.1 = (f32[2,128,128]{2,1,0:T(8,128)}, f32[2,128,128]{2,1,0:T(8,128)}, f32[8,128]{1,0:T(8,128)}) custom-call(s32[1]{0:T(128)} %bitcast.me_ref, s32[256]{0:T(256)} %reshape.18.store_ref, f32[16,136,128]{2,1,0:T(8,128)} %all_to_all.16.arrived_ref, f32[8,128]{1,0:T(8,128)} %get-tuple-element.28.square_ref, f32[2,128,128]{2,1,0:T(8,128)} %step.1.refs_0_.vector_ref, ...), custom_call_target="tpu_custom_call" | custom-call | tf_op jit(solution)/shard_map/last/pallas_call | solution.py:241
  154.0 0.7 broadcast_in_dim.2
  154.6 9.6 %all_to_all.17 = f32[16,8,128]{2,1,0:T(8,128)S(1)} all-to-all(f32[16,8,128]{2,1,0:T(8,128)S(1)} %broadcast_in_dim.2), channel_id=1, replica_groups=mesh['group'=2,'term'=16] {'term'}, dimensions={0} | all-to-all | bytes 131072 | tf_op jit(solution)/shard_map/all_to_all | solution.py:252
  164.3 0.6 reduce_sum.9
  165.6 1.6 broadcast_divide_fusion
  (71 shorter events, 0.2 us)
Async XLA Ops:
  0.6 9.8 %collective-permute-start.11 = (f32[2,128,128]{2,1,0:T(8,128)}, f32[2,128,128]{2,1,0:T(8,128)S(1)}, u32[]{:S(2)}, u32[]{:S(2)}) collective-permute-start(f32[2,128,128]{2,1,0:T(8,128)} %vector_ref.1), channel_id=1, source_target_pairs={{0,12},{1,13},{2,14},{3,15},{4,8},{5,9},{6,10},{7,11},{8,4},{9,5},... | collective-permute-start | bytes 393224 | tf_op jit(solution)/shard_map/ppermute | solution.py:215
  5.7 11.3 %collective-permute-start.7 = (f32[2,128,128]{2,1,0:T(8,128)}, f32[2,128,128]{2,1,0:T(8,128)S(1)}, u32[]{:S(2)}, u32[]{:S(2)}) collective-permute-start(f32[2,128,128]{2,1,0:T(8,128)} %vector_ref.1), channel_id=1, source_target_pairs={{0,8},{1,9},{2,10},{3,11},{4,12},{5,13},{6,14},{7,15},{8,0},{9,1},... | collective-permute-start | bytes 393224 | tf_op jit(solution)/shard_map/ppermute | solution.py:215
  5.7 11.3 %collective-permute-start.3 = (f32[2,128,128]{2,1,0:T(8,128)}, f32[2,128,128]{2,1,0:T(8,128)S(1)}, u32[]{:S(2)}, u32[]{:S(2)}) collective-permute-start(f32[2,128,128]{2,1,0:T(8,128)} %vector_ref.1), channel_id=1, source_target_pairs={{0,4},{1,5},{2,6},{3,7},{4,0},{5,1},{6,2},{7,3},{8,12},{9,13},{10,... | collective-permute-start | bytes 393224 | tf_op jit(solution)/shard_map/ppermute | solution.py:215
  6.4 12.2 %collective-permute-start.1 = (f32[2,128,128]{2,1,0:T(8,128)}, f32[2,128,128]{2,1,0:T(8,128)S(1)}, u32[]{:S(2)}, u32[]{:S(2)}) collective-permute-start(f32[2,128,128]{2,1,0:T(8,128)} %vector_ref.1), channel_id=1, source_target_pairs={{0,2},{1,3},{2,0},{3,1},{4,6},{5,7},{6,4},{7,5},{8,10},{9,11},{10,... | collective-permute-start | bytes 393224 | tf_op jit(solution)/shard_map/ppermute | solution.py:215
  8.1 10.8 %collective-permute-start = (f32[2,128,128]{2,1,0:T(8,128)}, f32[2,128,128]{2,1,0:T(8,128)S(1)}, u32[]{:S(2)}, u32[]{:S(2)}) collective-permute-start(f32[2,128,128]{2,1,0:T(8,128)} %vector_ref.1), channel_id=1, source_target_pairs={{0,1},{1,0},{2,3},{3,2},{4,5},{5,4},{6,7},{7,6},{8,9},{9,8},{10,11... | collective-permute-start | bytes 393224 | tf_op jit(solution)/shard_map/ppermute | solution.py:215
  10.4 23.2 %copy-start = (f32[2,128,128]{2,1,0:T(8,128)}, f32[2,128,128]{2,1,0:T(8,128)S(1)}, u32[]{:S(2)}) copy-start(f32[2,128,128]{2,1,0:T(8,128)S(1)} %collective-permute-done.11.refs_12_) | copy-start | bytes 393220
  10.4 8.4 %collective-permute-start.13 = (f32[2,128,128]{2,1,0:T(8,128)S(1)}, f32[2,128,128]{2,1,0:T(8,128)S(1)}, u32[]{:S(2)}, u32[]{:S(2)}) collective-permute-start(f32[2,128,128]{2,1,0:T(8,128)S(1)} %collective-permute-done.11.refs_12_), channel_id=1, source_target_pairs={{0,2},{1,3},{2,0},{3,1},{4,6},{5,7},{6,4},{7,5},{8,10},{9,11},{10,... | collective-permute-start | bytes 393224 | tf_op jit(solution)/shard_map/ppermute | solution.py:215
  17.0 16.6 %copy-start.1 = (f32[2,128,128]{2,1,0:T(8,128)}, f32[2,128,128]{2,1,0:T(8,128)S(1)}, u32[]{:S(2)}) copy-start(f32[2,128,128]{2,1,0:T(8,128)S(1)} %collective-permute-done.7.refs_8_) | copy-start | bytes 393220
  17.0 2.2 %collective-permute-start.12 = (f32[2,128,128]{2,1,0:T(8,128)S(1)}, f32[2,128,128]{2,1,0:T(8,128)S(1)}, u32[]{:S(2)}, u32[]{:S(2)}) collective-permute-start(f32[2,128,128]{2,1,0:T(8,128)S(1)} %collective-permute-done.11.refs_12_), channel_id=1, source_target_pairs={{0,1},{1,0},{2,3},{3,2},{4,5},{5,4},{6,7},{7,6},{8,9},{9,8},{10,11... | collective-permute-start | bytes 393224 | tf_op jit(solution)/shard_map/ppermute | solution.py:215
  17.0 16.6 %copy-start.2 = (f32[2,128,128]{2,1,0:T(8,128)}, f32[2,128,128]{2,1,0:T(8,128)S(1)}, u32[]{:S(2)}) copy-start(f32[2,128,128]{2,1,0:T(8,128)S(1)} %collective-permute-done.3.refs_4_) | copy-start | bytes 393220
  17.1 5.9 %collective-permute-start.9 = (f32[2,128,128]{2,1,0:T(8,128)S(1)}, f32[2,128,128]{2,1,0:T(8,128)S(1)}, u32[]{:S(2)}, u32[]{:S(2)}) collective-permute-start(f32[2,128,128]{2,1,0:T(8,128)S(1)} %collective-permute-done.7.refs_8_), channel_id=1, source_target_pairs={{0,2},{1,3},{2,0},{3,1},{4,6},{5,7},{6,4},{7,5},{8,10},{9,11},{10,... | collective-permute-start | bytes 393224 | tf_op jit(solution)/shard_map/ppermute | solution.py:215
  18.6 15.0 %copy-start.3 = (f32[2,128,128]{2,1,0:T(8,128)}, f32[2,128,128]{2,1,0:T(8,128)S(1)}, u32[]{:S(2)}) copy-start(f32[2,128,128]{2,1,0:T(8,128)S(1)} %collective-permute-done.1.refs_2_) | copy-start | bytes 393220
  18.6 4.3 %collective-permute-start.8 = (f32[2,128,128]{2,1,0:T(8,128)S(1)}, f32[2,128,128]{2,1,0:T(8,128)S(1)}, u32[]{:S(2)}, u32[]{:S(2)}) collective-permute-start(f32[2,128,128]{2,1,0:T(8,128)S(1)} %collective-permute-done.7.refs_8_), channel_id=1, source_target_pairs={{0,1},{1,0},{2,3},{3,2},{4,5},{5,4},{6,7},{7,6},{8,9},{9,8},{10,11... | collective-permute-start | bytes 393224 | tf_op jit(solution)/shard_map/ppermute | solution.py:215
  18.8 14.8 %copy-start.4 = (f32[2,128,128]{2,1,0:T(8,128)}, f32[2,128,128]{2,1,0:T(8,128)S(1)}, u32[]{:S(2)}) copy-start(f32[2,128,128]{2,1,0:T(8,128)S(1)} %collective-permute-done.refs_1_) | copy-start | bytes 393220
  18.8 5.7 %collective-permute-start.5 = (f32[2,128,128]{2,1,0:T(8,128)S(1)}, f32[2,128,128]{2,1,0:T(8,128)S(1)}, u32[]{:S(2)}, u32[]{:S(2)}) collective-permute-start(f32[2,128,128]{2,1,0:T(8,128)S(1)} %collective-permute-done.1.refs_2_), channel_id=1, source_target_pairs={{0,4},{1,5},{2,6},{3,7},{4,0},{5,1},{6,2},{7,3},{8,12},{9,13},{10,... | collective-permute-start | bytes 393224 | tf_op jit(solution)/shard_map/ppermute | solution.py:215
  18.8 14.8 %copy-start.6 = (f32[2,128,128]{2,1,0:T(8,128)}, f32[2,128,128]{2,1,0:T(8,128)S(1)}, u32[]{:S(2)}) copy-start(f32[2,128,128]{2,1,0:T(8,128)S(1)} %collective-permute-done.13.refs_14_) | copy-start | bytes 393220
  18.8 14.7 %collective-permute-start.2 = (f32[2,128,128]{2,1,0:T(8,128)S(1)}, f32[2,128,128]{2,1,0:T(8,128)S(1)}, u32[]{:S(2)}, u32[]{:S(2)}) collective-permute-start(f32[2,128,128]{2,1,0:T(8,128)S(1)} %collective-permute-done.1.refs_2_), channel_id=1, source_target_pairs={{0,1},{1,0},{2,3},{3,2},{4,5},{5,4},{6,7},{7,6},{8,9},{9,8},{10,11... | collective-permute-start | bytes 393224 | tf_op jit(solution)/shard_map/ppermute | solution.py:215
  19.3 14.4 %copy-start.9 = (f32[2,128,128]{2,1,0:T(8,128)}, f32[2,128,128]{2,1,0:T(8,128)S(1)}, u32[]{:S(2)}) copy-start(f32[2,128,128]{2,1,0:T(8,128)S(1)} %collective-permute-done.12.refs_13_) | copy-start | bytes 393220
  19.3 14.2 %collective-permute-start.4 = (f32[2,128,128]{2,1,0:T(8,128)S(1)}, f32[2,128,128]{2,1,0:T(8,128)S(1)}, u32[]{:S(2)}, u32[]{:S(2)}) collective-permute-start(f32[2,128,128]{2,1,0:T(8,128)S(1)} %collective-permute-done.3.refs_4_), channel_id=1, source_target_pairs={{0,1},{1,0},{2,3},{3,2},{4,5},{5,4},{6,7},{7,6},{8,9},{9,8},{10,11... | collective-permute-start | bytes 393224 | tf_op jit(solution)/shard_map/ppermute | solution.py:215
  23.0 10.7 %copy-start.12 = (f32[2,128,128]{2,1,0:T(8,128)}, f32[2,128,128]{2,1,0:T(8,128)S(1)}, u32[]{:S(2)}) copy-start(f32[2,128,128]{2,1,0:T(8,128)S(1)} %collective-permute-done.9.refs_10_) | copy-start | bytes 393220
  23.0 10.6 %collective-permute-start.14 = (f32[2,128,128]{2,1,0:T(8,128)S(1)}, f32[2,128,128]{2,1,0:T(8,128)S(1)}, u32[]{:S(2)}, u32[]{:S(2)}) collective-permute-start(f32[2,128,128]{2,1,0:T(8,128)S(1)} %collective-permute-done.13.refs_14_), channel_id=1, source_target_pairs={{0,1},{1,0},{2,3},{3,2},{4,5},{5,4},{6,7},{7,6},{8,9},{9,8},{10,11... | collective-permute-start | bytes 393224 | tf_op jit(solution)/shard_map/ppermute | solution.py:215
  23.0 10.7 %copy-start.14 = (f32[2,128,128]{2,1,0:T(8,128)}, f32[2,128,128]{2,1,0:T(8,128)S(1)}, u32[]{:S(2)}) copy-start(f32[2,128,128]{2,1,0:T(8,128)S(1)} %collective-permute-done.8.refs_9_) | copy-start | bytes 393220
  23.0 10.6 %collective-permute-start.10 = (f32[2,128,128]{2,1,0:T(8,128)S(1)}, f32[2,128,128]{2,1,0:T(8,128)S(1)}, u32[]{:S(2)}, u32[]{:S(2)}) collective-permute-start(f32[2,128,128]{2,1,0:T(8,128)S(1)} %collective-permute-done.9.refs_10_), channel_id=1, source_target_pairs={{0,1},{1,0},{2,3},{3,2},{4,5},{5,4},{6,7},{7,6},{8,9},{9,8},{10,11... | collective-permute-start | bytes 393224 | tf_op jit(solution)/shard_map/ppermute | solution.py:215
  24.6 9.1 %copy-start.16 = (f32[2,128,128]{2,1,0:T(8,128)}, f32[2,128,128]{2,1,0:T(8,128)S(1)}, u32[]{:S(2)}) copy-start(f32[2,128,128]{2,1,0:T(8,128)S(1)} %collective-permute-done.5.refs_6_) | copy-start | bytes 393220
  24.6 9.0 %collective-permute-start.6 = (f32[2,128,128]{2,1,0:T(8,128)S(1)}, f32[2,128,128]{2,1,0:T(8,128)S(1)}, u32[]{:S(2)}, u32[]{:S(2)}) collective-permute-start(f32[2,128,128]{2,1,0:T(8,128)S(1)} %collective-permute-done.5.refs_6_), channel_id=1, source_target_pairs={{0,1},{1,0},{2,3},{3,2},{4,5},{5,4},{6,7},{7,6},{8,9},{9,8},{10,11... | collective-permute-start | bytes 393224 | tf_op jit(solution)/shard_map/ppermute | solution.py:215
  33.5 0.7 copy-start.20
  33.5 0.7 copy-start.18
  33.5 0.7 copy-start.22
  33.6 0.8 copy-start.24
  33.6 0.8 copy-start.26
  83.0 8.5 %collective-permute-start.26 = (f32[2,128,128]{2,1,0:T(8,128)}, f32[2,128,128]{2,1,0:T(8,128)S(1)}, u32[]{:S(2)}, u32[]{:S(2)}) collective-permute-start(f32[2,128,128]{2,1,0:T(8,128)} %step.1.refs_0_.vector_ref), channel_id=1, source_target_pairs={{0,12},{1,13},{2,14},{3,15},{4,8},{5,9},{6,10},{7,11},{8,4},{9,5},... | collective-permute-start | bytes 393224 | tf_op jit(solution)/shard_map/ppermute | solution.py:215
  84.5 12.8 %collective-permute-start.22 = (f32[2,128,128]{2,1,0:T(8,128)}, f32[2,128,128]{2,1,0:T(8,128)S(1)}, u32[]{:S(2)}, u32[]{:S(2)}) collective-permute-start(f32[2,128,128]{2,1,0:T(8,128)} %step.1.refs_0_.vector_ref), channel_id=1, source_target_pairs={{0,8},{1,9},{2,10},{3,11},{4,12},{5,13},{6,14},{7,15},{8,0},{9,1},... | collective-permute-start | bytes 393224 | tf_op jit(solution)/shard_map/ppermute | solution.py:215
  85.2 12.1 %collective-permute-start.18 = (f32[2,128,128]{2,1,0:T(8,128)}, f32[2,128,128]{2,1,0:T(8,128)S(1)}, u32[]{:S(2)}, u32[]{:S(2)}) collective-permute-start(f32[2,128,128]{2,1,0:T(8,128)} %step.1.refs_0_.vector_ref), channel_id=1, source_target_pairs={{0,4},{1,5},{2,6},{3,7},{4,0},{5,1},{6,2},{7,3},{8,12},{9,13},{10,... | collective-permute-start | bytes 393224 | tf_op jit(solution)/shard_map/ppermute | solution.py:215
  87.4 10.6 %collective-permute-start.16 = (f32[2,128,128]{2,1,0:T(8,128)}, f32[2,128,128]{2,1,0:T(8,128)S(1)}, u32[]{:S(2)}, u32[]{:S(2)}) collective-permute-start(f32[2,128,128]{2,1,0:T(8,128)} %step.1.refs_0_.vector_ref), channel_id=1, source_target_pairs={{0,2},{1,3},{2,0},{3,1},{4,6},{5,7},{6,4},{7,5},{8,10},{9,11},{10,... | collective-permute-start | bytes 393224 | tf_op jit(solution)/shard_map/ppermute | solution.py:215
  88.0 10.1 %collective-permute-start.15 = (f32[2,128,128]{2,1,0:T(8,128)}, f32[2,128,128]{2,1,0:T(8,128)S(1)}, u32[]{:S(2)}, u32[]{:S(2)}) collective-permute-start(f32[2,128,128]{2,1,0:T(8,128)} %step.1.refs_0_.vector_ref), channel_id=1, source_target_pairs={{0,1},{1,0},{2,3},{3,2},{4,5},{5,4},{6,7},{7,6},{8,9},{9,8},{10,11... | collective-permute-start | bytes 393224 | tf_op jit(solution)/shard_map/ppermute | solution.py:215
  91.5 13.7 %copy-start.5 = (f32[2,128,128]{2,1,0:T(8,128)}, f32[2,128,128]{2,1,0:T(8,128)S(1)}, u32[]{:S(2)}) copy-start(f32[2,128,128]{2,1,0:T(8,128)S(1)} %collective-permute-done.26.refs_12_) | copy-start | bytes 393220
  91.5 6.6 %collective-permute-start.28 = (f32[2,128,128]{2,1,0:T(8,128)S(1)}, f32[2,128,128]{2,1,0:T(8,128)S(1)}, u32[]{:S(2)}, u32[]{:S(2)}) collective-permute-start(f32[2,128,128]{2,1,0:T(8,128)S(1)} %collective-permute-done.26.refs_12_), channel_id=1, source_target_pairs={{0,2},{1,3},{2,0},{3,1},{4,6},{5,7},{6,4},{7,5},{8,10},{9,11},{10,... | collective-permute-start | bytes 393224 | tf_op jit(solution)/shard_map/ppermute | solution.py:215
  97.3 8.0 %copy-start.7 = (f32[2,128,128]{2,1,0:T(8,128)}, f32[2,128,128]{2,1,0:T(8,128)S(1)}, u32[]{:S(2)}) copy-start(f32[2,128,128]{2,1,0:T(8,128)S(1)} %collective-permute-done.22.refs_8_) | copy-start | bytes 393220
  97.3 1.3 collective-permute-start.27
  97.3 8.0 %copy-start.8 = (f32[2,128,128]{2,1,0:T(8,128)}, f32[2,128,128]{2,1,0:T(8,128)S(1)}, u32[]{:S(2)}) copy-start(f32[2,128,128]{2,1,0:T(8,128)S(1)} %collective-permute-done.18.refs_4_) | copy-start | bytes 393220
  97.3 5.9 %collective-permute-start.24 = (f32[2,128,128]{2,1,0:T(8,128)S(1)}, f32[2,128,128]{2,1,0:T(8,128)S(1)}, u32[]{:S(2)}, u32[]{:S(2)}) collective-permute-start(f32[2,128,128]{2,1,0:T(8,128)S(1)} %collective-permute-done.22.refs_8_), channel_id=1, source_target_pairs={{0,2},{1,3},{2,0},{3,1},{4,6},{5,7},{6,4},{7,5},{8,10},{9,11},{10,... | collective-permute-start | bytes 393224 | tf_op jit(solution)/shard_map/ppermute | solution.py:215
  98.0 7.3 %copy-start.10 = (f32[2,128,128]{2,1,0:T(8,128)}, f32[2,128,128]{2,1,0:T(8,128)S(1)}, u32[]{:S(2)}) copy-start(f32[2,128,128]{2,1,0:T(8,128)S(1)} %collective-permute-done.16.refs_2_) | copy-start | bytes 393220
  98.0 5.2 %collective-permute-start.23 = (f32[2,128,128]{2,1,0:T(8,128)S(1)}, f32[2,128,128]{2,1,0:T(8,128)S(1)}, u32[]{:S(2)}, u32[]{:S(2)}) collective-permute-start(f32[2,128,128]{2,1,0:T(8,128)S(1)} %collective-permute-done.22.refs_8_), channel_id=1, source_target_pairs={{0,1},{1,0},{2,3},{3,2},{4,5},{5,4},{6,7},{7,6},{8,9},{9,8},{10,11... | collective-permute-start | bytes 393224 | tf_op jit(solution)/shard_map/ppermute | solution.py:215
  98.2 7.1 %copy-start.11 = (f32[2,128,128]{2,1,0:T(8,128)}, f32[2,128,128]{2,1,0:T(8,128)S(1)}, u32[]{:S(2)}) copy-start(f32[2,128,128]{2,1,0:T(8,128)S(1)} %collective-permute-done.15.refs_1_) | copy-start | bytes 393220
  98.2 5.7 %collective-permute-start.20 = (f32[2,128,128]{2,1,0:T(8,128)S(1)}, f32[2,128,128]{2,1,0:T(8,128)S(1)}, u32[]{:S(2)}, u32[]{:S(2)}) collective-permute-start(f32[2,128,128]{2,1,0:T(8,128)S(1)} %collective-permute-done.16.refs_2_), channel_id=1, source_target_pairs={{0,4},{1,5},{2,6},{3,7},{4,0},{5,1},{6,2},{7,3},{8,12},{9,13},{10,... | collective-permute-start | bytes 393224 | tf_op jit(solution)/shard_map/ppermute | solution.py:215
  98.2 7.1 %copy-start.13 = (f32[2,128,128]{2,1,0:T(8,128)}, f32[2,128,128]{2,1,0:T(8,128)S(1)}, u32[]{:S(2)}) copy-start(f32[2,128,128]{2,1,0:T(8,128)S(1)} %collective-permute-done.28.refs_14_) | copy-start | bytes 393220
  98.2 5.7 %collective-permute-start.17 = (f32[2,128,128]{2,1,0:T(8,128)S(1)}, f32[2,128,128]{2,1,0:T(8,128)S(1)}, u32[]{:S(2)}, u32[]{:S(2)}) collective-permute-start(f32[2,128,128]{2,1,0:T(8,128)S(1)} %collective-permute-done.16.refs_2_), channel_id=1, source_target_pairs={{0,1},{1,0},{2,3},{3,2},{4,5},{5,4},{6,7},{7,6},{8,9},{9,8},{10,11... | collective-permute-start | bytes 393224 | tf_op jit(solution)/shard_map/ppermute | solution.py:215
  98.6 6.7 %copy-start.15 = (f32[2,128,128]{2,1,0:T(8,128)}, f32[2,128,128]{2,1,0:T(8,128)S(1)}, u32[]{:S(2)}) copy-start(f32[2,128,128]{2,1,0:T(8,128)S(1)} %collective-permute-done.27.refs_13_) | copy-start | bytes 393220
  98.6 5.3 %collective-permute-start.19 = (f32[2,128,128]{2,1,0:T(8,128)S(1)}, f32[2,128,128]{2,1,0:T(8,128)S(1)}, u32[]{:S(2)}, u32[]{:S(2)}) collective-permute-start(f32[2,128,128]{2,1,0:T(8,128)S(1)} %collective-permute-done.18.refs_4_), channel_id=1, source_target_pairs={{0,1},{1,0},{2,3},{3,2},{4,5},{5,4},{6,7},{7,6},{8,9},{9,8},{10,11... | collective-permute-start | bytes 393224 | tf_op jit(solution)/shard_map/ppermute | solution.py:215
  103.2 2.1 %copy-start.17 = (f32[2,128,128]{2,1,0:T(8,128)}, f32[2,128,128]{2,1,0:T(8,128)S(1)}, u32[]{:S(2)}) copy-start(f32[2,128,128]{2,1,0:T(8,128)S(1)} %collective-permute-done.24.refs_10_) | copy-start | bytes 393220
  103.2 1.3 collective-permute-start.29
  103.2 2.1 %copy-start.19 = (f32[2,128,128]{2,1,0:T(8,128)}, f32[2,128,128]{2,1,0:T(8,128)S(1)}, u32[]{:S(2)}) copy-start(f32[2,128,128]{2,1,0:T(8,128)S(1)} %collective-permute-done.23.refs_9_) | copy-start | bytes 393220
  103.2 1.5 collective-permute-start.25
  103.9 1.4 copy-start.21
  103.9 1.3 collective-permute-start.21
  103.9 1.4 copy-start.25
  103.9 1.4 copy-start.23
  104.6 0.8 copy-start.27
  104.8 0.7 copy-start.28
  105.4 0.7 copy-start.29
where the time goes:
time: 168 us; the launch traced here: 167 us
  blocking collectives  76.3 us (45%)
  Pallas kernels  33.9 us (20%)
  waiting for transfers between devices  26.5 us (16%)
  starting transfers between devices  19.5 us (12%)
  local copies, waits for them, and re-layouts  6.39 us (4%)
  between operations  2.38 us (1%)
  other arithmetic  2.19 us (1%)
    all_to_all x2, blocking collectives, shards(): lax.all_to_all(slots, 'term', split_axis=0, concat_axis=0, tiled=True)  66.7 us
    ppermute x30, waiting for transfers between devices, send(): return lax.ppermute(y, 'term', [(i, i ^ k) for i in range(n)])  26.5 us
    pallas_call x2, Pallas kernels, apply(): pl.pallas_call(functools.partial(apply_kernel, n, rows), out_shape=(jax.S...  25.5 us
    ppermute x30, starting transfers between devices, send(): return lax.ppermute(y, 'term', [(i, i ^ k) for i in range(n)])  19.5 us
    all_to_all x1, blocking collectives, shards(): lax.all_to_all(jnp.broadcast_to(partial[None], (n, 8, width)), 'term', sp...  9.64 us
    pallas_call x2, Pallas kernels, shards(): pl.pallas_call(functools.partial(last_kernel, n, cells) if last else func...  4.4 us
    pallas_call x1, Pallas kernels, prep(): pl.pallas_call(functools.partial(prep_kernel, n, terms * n + 1), out_shap...  4.04 us
  transfers between devices with their start and end apart: 30, of which 11 were waited for; matrix products, arithmetic and copies ran while one was open for 3% of the time, Pallas kernels for 2%

commit v1 on v0

--- a/solution.py
+++ b/solution.py
@@ -11,7 +11,10 @@
 CORE, ROW = 1, 2
 SMEM = pl.BlockSpec(memory_space=pltpu.SMEM)
 VMEM = pl.BlockSpec(memory_space=pltpu.VMEM)
-PARAMS = pltpu.CompilerParams(vmem_limit_bytes=56 * 2**20)
+
+
+def params(mebibytes):
+    return pltpu.CompilerParams(vmem_limit_bytes=mebibytes * 2**20)
 
 
 def halves(x):
@@ -40,9 +43,9 @@
 
     def pair(p, carry):
         extra, ops = carry
-        a = lax.bitwise_xor(pairs_ref[3 * p], me)
-        j = pairs_ref[3 * p + 1]
-        o = lax.bitwise_xor(pairs_ref[3 * p + 2], me)
+        a = lax.bitwise_xor(pairs_ref[p, 0], me)
+        j = pairs_ref[p, 1]
+        o = lax.bitwise_xor(pairs_ref[p, 2], me)
         cell = j * n + o
         source = a * terms + j
         seen = seen_ref[cell]
@@ -72,7 +75,7 @@
 
 def prep(n, me, pairs, live, left_ops, right_ops):
     terms, width = left_ops.shape[:2]
-    npairs = pairs.shape[0] // 3
+    npairs = pairs.shape[0]
     table = jax.ShapeDtypeStruct((terms * n,), jnp.int32)
     listed = jax.ShapeDtypeStruct((npairs,), jnp.int32)
     return pl.pallas_call(
@@ -86,56 +89,47 @@
         in_specs=[SMEM] * 3 + [VMEM] * 2,
         out_specs=[VMEM] * 2 + [SMEM] * 6,
         scratch_shapes=[pltpu.SMEM((terms * n,), jnp.int32)],
-        compiler_params=PARAMS,
+        compiler_params=params(16),
         name="prep",
     )(me, pairs, live, left_ops, right_ops)
 
 
 def apply_kernel(n, rows, me_ref, fetch_ref, store_ref, first_ref, second_ref, dst_ref, one_ref, two_ref,
                  count_ref, l4_ref, rr_ref, *refs):
-    pieces, (out_ref, square_ref, field, block, total) = refs[:n], refs[n:]
+    pieces, (out_ref, square_ref, block, total) = refs[:n], refs[n:]
     me = me_ref[0]
     terms, width = l4_ref.shape[:2]
-    for r in range(n):
-        high, low = halves(pieces[r][fetch_ref[lax.bitwise_xor(me, r) * n + me]])
-        at = (r % 2) * width
-        for k, part in enumerate((high, high, low, low)):
-            field[r // 2, k * width:(k + 1) * width, at:at + width] = part
     square = jnp.zeros((8, width), jnp.float32)
-    for r in range(n):
-        square = square + tile_sum(pieces[r][...] * pieces[r][...])
-    square_ref[...] = square
     product = jnp.zeros((8, width), jnp.float32)
     block[terms * n] = jnp.zeros((rows, width), jnp.float32)
     for start in range(0, width, rows):
         left = l4_ref[:, start:start + rows, :].reshape(terms * rows, 4 * width)
 
-        def products(c, carry):
-            both = jnp.dot(left, field[c], preferred_element_type=jnp.float32)
+        for c in range(n // 2):
+            columns = []
+            for r in (2 * c, 2 * c + 1):
+                high, low = halves(pieces[r][fetch_ref[lax.bitwise_xor(me, r), me]])
+                columns.append(jnp.concatenate([high, high, low, low], axis=0))
+                if start == 0:
+                    square = square + tile_sum(pieces[r][...] * pieces[r][...])
+            both = jnp.dot(left, jnp.concatenate(columns, axis=1), preferred_element_type=jnp.float32)
             for k in range(2):
-                at = pl.multiple_of((2 * c + k) * terms, terms)
-                block[pl.ds(at, terms)] = both[:, k * width:(k + 1) * width].reshape(terms, rows, width)
-            return carry
-
-        lax.fori_loop(0, n // 2, products, 0)
+                at = (2 * c + k) * terms
+                block[at:at + terms] = both[:, k * width:(k + 1) * width].reshape(terms, rows, width)
 
         def add(i, carry):
             block[dst_ref[i]] = block[one_ref[i]] + block[two_ref[i]]
             return carry
 
         lax.fori_loop(0, count_ref[0], add, 0)
-        for j in range(terms):
-
-            def cell(o, carry):
-                at = j * n + o
-                high, low = halves(block[first_ref[at]] + block[second_ref[at]])
-                total[o, :, j * width:(j + 1) * width] = high
-                total[o, :, (terms + j) * width:(terms + j + 1) * width] = low
-                return carry
-
-            lax.fori_loop(0, n, cell, 0, unroll=4)
-        group = 8
+        group = 4
         for o in range(0, n, group):
+            for k in range(group):
+                for j in range(terms):
+                    at = j * n + o + k
+                    high, low = halves(block[first_ref[at]] + block[second_ref[at]])
+                    total[o + k, :, j * width:(j + 1) * width] = high
+                    total[o + k, :, (terms + j) * width:(terms + j + 1) * width] = low
             both = jnp.dot(total[o:o + group].reshape(group * rows, 2 * terms * width), rr_ref[...],
                            preferred_element_type=jnp.float32)
             slots = both[:, :width] + both[:, width:]
@@ -143,8 +137,9 @@
                 slot = slots[k * rows:(k + 1) * rows]
                 owner = lax.bitwise_xor(me, o + k)
                 out_ref[owner, start:start + rows, :] = slot
-                held = pieces[o + k][store_ref[me * n + owner], start:start + rows, :]
+                held = pieces[o + k][store_ref[me, owner], start:start + rows, :]
                 product = product + tile_sum(held * slot)
+    square_ref[...] = square
     for r in range(n):
         out_ref[r, width:, :] = product
 
@@ -163,11 +158,10 @@
         in_specs=[SMEM] * 9 + [VMEM] * (2 + n),
         out_specs=[VMEM] * 2,
         scratch_shapes=[
-            pltpu.VMEM((n // 2, 4 * width, 2 * width), jnp.bfloat16),
             pltpu.VMEM((terms * n + 1 + npairs // 3, rows, width), jnp.float32),
             pltpu.VMEM((n, rows, 2 * terms * width), jnp.bfloat16),
         ],
-        compiler_params=PARAMS,
+        compiler_params=params(32 if n <= 16 else 56),
         name="apply",
     )(me, fetch, store, *tables[2:], *tables[:2], *pieces)
 
@@ -178,7 +172,7 @@
     sums = [jnp.zeros((width, width), jnp.float32) for _ in range(2)]
     tile = jnp.zeros((8, width), jnp.float32)
     for r in range(n):
-        mine = store_ref[r * n + me]
+        mine = store_ref[r, me]
         for b in range(2):
             sums[b] = sums[b] + (mine == b).astype(jnp.float32) * arrived_ref[r, :width, :]
         tile = tile + arrived_ref[r, width:, :]
@@ -210,13 +204,15 @@
     tile_ref[...] = tile
 
 
-def gathered(n, x):
+def gathered(n, x, beside=None):
     def send(y, k):
         return lax.ppermute(y, "term", [(i, i ^ k) for i in range(n)])
 
     pieces = {0: x, ROW: send(x, ROW)}
     for k in range(4, n, 4):
         pieces[k] = send(x, k)
+    if beside is not None:
+        pieces[4], _ = lax.optimization_barrier((pieces[4], beside))
     for k in range(4, n, 4):
         pieces[k + ROW] = send(pieces[ROW], k) if k == 4 else send(pieces[k], ROW)
     for k in range(0, n, 2):
@@ -229,13 +225,12 @@
     me = lax.axis_index("term").astype(jnp.int32).reshape(1)
     width = wavefn.shape[1]
     cells = wavefn.size * n
-    fetch, store = fetch_map.reshape(-1), store_map.reshape(-1)
-    tables = prep(n, me, pair_list.reshape(-1), live_count, left_ops, right_ops)
+    tables = prep(n, me, pair_list[0], live_count, left_ops, right_ops)
     block = jax.ShapeDtypeStruct(wavefn.shape, jnp.float32)
     tile = jax.ShapeDtypeStruct((8, width), jnp.float32)
     vector = wavefn
     for iteration in range(ITERS):
-        slots, square = apply(n, me, fetch, store, tables, gathered(n, vector))
+        slots, square = apply(n, me, fetch_map, store_map, tables, gathered(n, vector, tables if iteration == 0 else None))
         arrived = lax.all_to_all(slots, "term", split_axis=0, concat_axis=0, tiled=True)
         last = iteration == ITERS - 1
         result = pl.pallas_call(
@@ -243,9 +238,9 @@
             out_shape=(block, block, tile) if last else block,
             in_specs=[SMEM] * 2 + [VMEM] * 4,
             out_specs=[VMEM] * 3 if last else VMEM,
-            compiler_params=PARAMS,
+            compiler_params=params(16),
             name="last" if last else "step",
-        )(me, store, arrived, square, vector, precond)
+        )(me, store_map, arrived, square, vector, precond)
         if not last:
             vector = result
     residual, corrected, partial = result

time: 168 us -> 145 us (0.86)
  Pallas kernels: 33.9 us -> 20.9 us
  waiting for transfers between devices: 26.5 us -> 23 us
  local copies, waits for them, and re-layouts: 6.39 us -> 2.89 us
    pallas_call x2, Pallas kernels: 25.5 us -> 14.2 us  [apply(): pl.pallas_call(functools.partial(apply_kernel, n, rows), out_shape=(jax.S...]
    ppermute x30, waiting for transfers between devices: 26.5 us -> 23 us  [send(): return lax.ppermute(y, 'term', [(i, i ^ k) for i in range(n)])]
    reshape x3 -> x0, local copies, waits for them, and re-layouts: 3.43 us -> none  [the longest x2 2.63 us: shards(): fetch, store = (fetch_map.reshape(-1), store_map.reshape(-1))]
    pallas_call x2, Pallas kernels: 4.4 us -> 2.44 us  [shards(): pl.pallas_call(functools.partial(last_kernel, n, cells) if last else func...]
  transfers between devices with their start and end apart: 30 -> 30, of which waited for: 11 -> 14; matrix products, arithmetic and copies ran while one was open for 3% -> 1% of each run, Pallas kernels for 2% -> 3%
where the time goes in v1:
time: 145 us
  blocking collectives  75 us (52%)
  waiting for transfers between devices  23 us (16%)
  Pallas kernels  20.9 us (14%)
  starting transfers between devices  19.6 us (14%)
  local copies, waits for them, and re-layouts  2.89 us (2%)
  between operations  2.1 us (1%)
    all_to_all x2, blocking collectives, shards(): lax.all_to_all(slots, 'term', split_axis=0, concat_axis=0, tiled=True)  65.3 us
    ppermute x30, waiting for transfers between devices, send(): return lax.ppermute(y, 'term', [(i, i ^ k) for i in range(n)])  23 us
    ppermute x30, starting transfers between devices, send(): return lax.ppermute(y, 'term', [(i, i ^ k) for i in range(n)])  19.6 us
    pallas_call x2, Pallas kernels, apply(): pl.pallas_call(functools.partial(apply_kernel, n, rows), out_shape=(jax.S...  14.2 us
    all_to_all x1, blocking collectives, shards(): lax.all_to_all(jnp.broadcast_to(partial[None], (n, 8, width)), 'term', sp...  9.7 us
    pallas_call x1, Pallas kernels, prep(): pl.pallas_call(functools.partial(prep_kernel, n, terms * n + 1), out_shap...  4.2 us
  transfers between devices with their start and end apart: 30, of which 14 were waited for; matrix products, arithmetic and copies ran while one was open for 1% of the time, Pallas kernels for 3%

profile of v1, /device:TPU:0, one launch (start us, length us, event | category | flops | bytes accessed | tf_op | source)
XLA Modules:
  0.0 144.7 jit_solution(15612785366025315225)
XLA Ops:
  0.7 5.1 %collective-permute-start.11 = (f32[2,128,128]{2,1,0:T(8,128)}, f32[2,128,128]{2,1,0:T(8,128)S(1)}, u32[]{:S(2)}, u32[]{:S(2)}) collective-permute-start(f32[2,128,128]{2,1,0:T(8,128)} %vector_ref.1), channel_id=1, source_target_pairs={{0,12},{1,13},{2,14},{3,15},{4,8},{5,9},{6,10},{7,11},{8,4},{9,5},... | collective-permute-start | bytes 393224 | tf_op jit(solution)/shard_map/ppermute | solution.py:209
  5.8 0.0 collective-permute-start.7
  5.8 0.6 collective-permute-start.3
  6.4 1.7 %collective-permute-start.1 = (f32[2,128,128]{2,1,0:T(8,128)}, f32[2,128,128]{2,1,0:T(8,128)S(1)}, u32[]{:S(2)}, u32[]{:S(2)}) collective-permute-start(f32[2,128,128]{2,1,0:T(8,128)} %vector_ref.1), channel_id=1, source_target_pairs={{0,2},{1,3},{2,0},{3,1},{4,6},{5,7},{6,4},{7,5},{8,10},{9,11},{10,... | collective-permute-start | bytes 393224 | tf_op jit(solution)/shard_map/ppermute | solution.py:209
  8.1 0.0 collective-permute-start
  8.1 2.3 %collective-permute-done.11.refs_12_ = f32[2,128,128]{2,1,0:T(8,128)S(1)} collective-permute-done((f32[2,128,128]{2,1,0:T(8,128)}, f32[2,128,128]{2,1,0:T(8,128)S(1)}, u32[]{:S(2)}, u32[]{:S(2)}) %collective-permute-start.11) | collective-permute-done | bytes 131104 | tf_op jit(solution)/shard_map/ppermute | solution.py:209
  10.4 1.7 %collective-permute-start.13 = (f32[2,128,128]{2,1,0:T(8,128)S(1)}, f32[2,128,128]{2,1,0:T(8,128)S(1)}, u32[]{:S(2)}, u32[]{:S(2)}) collective-permute-start(f32[2,128,128]{2,1,0:T(8,128)S(1)} %collective-permute-done.11.refs_12_), channel_id=1, source_target_pairs={{0,2},{1,3},{2,0},{3,1},{4,6},{5,7},{6,4},{7,5},{8,10},{9,11},{10,... | collective-permute-start | bytes 393224 | tf_op jit(solution)/shard_map/ppermute | solution.py:209
  12.1 4.9 %collective-permute-done.7.refs_8_ = f32[2,128,128]{2,1,0:T(8,128)S(1)} collective-permute-done((f32[2,128,128]{2,1,0:T(8,128)}, f32[2,128,128]{2,1,0:T(8,128)S(1)}, u32[]{:S(2)}, u32[]{:S(2)}) %collective-permute-start.7) | collective-permute-done | bytes 131104 | tf_op jit(solution)/shard_map/ppermute | solution.py:209
  17.1 0.0 collective-permute-start.12
  17.1 0.0 collective-permute-done.3.refs_4_
  17.1 1.5 %collective-permute-start.9 = (f32[2,128,128]{2,1,0:T(8,128)S(1)}, f32[2,128,128]{2,1,0:T(8,128)S(1)}, u32[]{:S(2)}, u32[]{:S(2)}) collective-permute-start(f32[2,128,128]{2,1,0:T(8,128)S(1)} %collective-permute-done.7.refs_8_), channel_id=1, source_target_pairs={{0,2},{1,3},{2,0},{3,1},{4,6},{5,7},{6,4},{7,5},{8,10},{9,11},{10,... | collective-permute-start | bytes 393224 | tf_op jit(solution)/shard_map/ppermute | solution.py:209
  18.6 0.2 collective-permute-start.8
  18.8 0.0 collective-permute-done.refs_1_
  19.5 0.8 copy.11
  20.3 1.0 copy-done
  21.3 1.0 copy-done.1
  22.3 4.2 %prep.1 = (bf16[8,128,512]{2,1,0:T(8,128)(2,1)S(1)}, bf16[2048,256]{1,0:T(8,128)(2,1)S(1)}, s32[128]{0:T(128)S(1)}, s32[128]{0:T(128)S(1)}, s32[128]{0:T(128)S(1...) custom-call(s32[1]{0:T(128)} %bitcast.me_ref, s32[128,3]{1,0:T(8,128)S(1)} %bitcast.2, s32[1]{0:T(128)S(6)} %copy.12.live_ref, ...), custom_call_target="tpu_custom_call" | custom-call | tf_op jit(solution)/shard_map/prep/pallas_call | solution.py:81
  26.6 0.1 collective-permute-start.4
  26.6 0.0 collective-permute-done.12.refs_13_
  26.7 0.5 collective-permute-start.2
  27.1 0.0 collective-permute-done.9.refs_10_
  27.1 0.1 collective-permute-start.14
  27.2 0.4 collective-permute-start.10
  27.7 0.0 collective-permute-done.5.refs_6_
  27.7 0.1 collective-permute-start.6
  27.8 0.4 collective-permute-done.2.refs_3_
  28.2 0.0 collective-permute-done.4.refs_5_
  28.2 0.3 collective-permute-done.14.refs_15_
  28.5 0.2 collective-permute-done.10.refs_11_
  28.7 0.3 collective-permute-done.6.refs_7_
  29.0 7.0 %apply.2 = (f32[16,136,128]{2,1,0:T(8,128)S(1)}, f32[8,128]{1,0:T(8,128)S(1)}) custom-call(s32[1]{0:T(128)} %bitcast.me_ref, s32[16,16]{1,0:T(8,128)S(1)} %copy-done.5, s32[16,16]{1,0:T(8,128)S(1)} %copy-done.4, s32[128]{0:T(128)S(1)} %get-tuple-element.18.first_ref, s32[128]{0:T(128)S(1)} %get-tuple-element.19.second_ref, ...), custom_call_target="tpu_custom_call" | custom-call | tf_op jit(solution)/shard_map/apply/pallas_call | solution.py:152
  36.1 0.0 copy-start.3
  36.1 33.3 %all_to_all.15.arrived_ref = f32[16,136,128]{2,1,0:T(8,128)S(1)} all-to-all(f32[16,136,128]{2,1,0:T(8,128)S(1)} %get-tuple-element.27), channel_id=1, replica_groups=mesh['group'=2,'term'=16] {'term'}, dimensions={0} | all-to-all | bytes 2228224 | tf_op jit(solution)/shard_map/all_to_all | solution.py:234
  69.4 0.9 step.1.refs_0_.vector_ref
  70.3 1.5 %collective-permute-start.26 = (f32[2,128,128]{2,1,0:T(8,128)S(1)}, f32[2,128,128]{2,1,0:T(8,128)S(1)}, u32[]{:S(2)}, u32[]{:S(2)}) collective-permute-start(f32[2,128,128]{2,1,0:T(8,128)S(1)} %step.1.refs_0_.vector_ref), channel_id=1, source_target_pairs={{0,12},{1,13},{2,14},{3,15},{4,8},{5,9},{6,10},{7,11},{8,4},{9,5},... | collective-permute-start | bytes 393224 | tf_op jit(solution)/shard_map/ppermute | solution.py:209
  71.8 0.6 collective-permute-start.22
  72.4 2.3 %collective-permute-start.18 = (f32[2,128,128]{2,1,0:T(8,128)S(1)}, f32[2,128,128]{2,1,0:T(8,128)S(1)}, u32[]{:S(2)}, u32[]{:S(2)}) collective-permute-start(f32[2,128,128]{2,1,0:T(8,128)S(1)} %step.1.refs_0_.vector_ref), channel_id=1, source_target_pairs={{0,4},{1,5},{2,6},{3,7},{4,0},{5,1},{6,2},{7,3},{8,12},{9,13},{10,... | collective-permute-start | bytes 393224 | tf_op jit(solution)/shard_map/ppermute | solution.py:209
  74.7 0.6 collective-permute-start.16
  75.3 0.0 collective-permute-start.15
  75.3 3.3 %collective-permute-done.26.refs_12_ = f32[2,128,128]{2,1,0:T(8,128)S(1)} collective-permute-done((f32[2,128,128]{2,1,0:T(8,128)S(1)}, f32[2,128,128]{2,1,0:T(8,128)S(1)}, u32[]{:S(2)}, u32[]{:S(2)}) %collective-permute-start.26) | collective-permute-done | bytes 131104 | tf_op jit(solution)/shard_map/ppermute | solution.py:209
  78.6 0.6 collective-permute-start.28
  79.2 5.1 %collective-permute-done.22.refs_8_ = f32[2,128,128]{2,1,0:T(8,128)S(1)} collective-permute-done((f32[2,128,128]{2,1,0:T(8,128)S(1)}, f32[2,128,128]{2,1,0:T(8,128)S(1)}, u32[]{:S(2)}, u32[]{:S(2)}) %collective-permute-start.22) | collective-permute-done | bytes 131104 | tf_op jit(solution)/shard_map/ppermute | solution.py:209
  84.4 0.0 collective-permute-start.27
  84.4 0.0 collective-permute-done.18.refs_4_
  84.4 0.6 collective-permute-start.24
  85.0 0.2 collective-permute-start.23
  85.2 0.0 collective-permute-start.20
  85.2 0.3 collective-permute-start.17
  85.6 0.1 collective-permute-done.27.refs_13_
  85.7 0.1 collective-permute-start.19
  85.9 4.4 %collective-permute-done.24.refs_10_ = f32[2,128,128]{2,1,0:T(8,128)S(1)} collective-permute-done((f32[2,128,128]{2,1,0:T(8,128)S(1)}, f32[2,128,128]{2,1,0:T(8,128)S(1)}, u32[]{:S(2)}, u32[]{:S(2)}) %collective-permute-start.24) | collective-permute-done | bytes 131104 | tf_op jit(solution)/shard_map/ppermute | solution.py:209
  90.3 0.0 collective-permute-start.29
  90.3 0.0 collective-permute-done.23.refs_9_
  90.3 0.5 collective-permute-start.25
  90.8 0.1 collective-permute-done.20.refs_6_
  90.9 0.7 collective-permute-done.29.refs_15_
  91.6 0.2 collective-permute-done.25.refs_11_
  91.8 0.4 collective-permute-done.21.refs_7_
  92.3 7.2 %apply.3 = (f32[16,136,128]{2,1,0:T(8,128)S(1)}, f32[8,128]{1,0:T(8,128)S(1)}) custom-call(s32[1]{0:T(128)} %bitcast.me_ref, s32[16,16]{1,0:T(8,128)S(1)} %copy-done.5, s32[16,16]{1,0:T(8,128)S(1)} %copy-done.4, s32[128]{0:T(128)S(1)} %get-tuple-element.18.first_ref, s32[128]{0:T(128)S(1)} %get-tuple-element.19.second_ref, ...), custom_call_target="tpu_custom_call" | custom-call | tf_op jit(solution)/shard_map/apply/pallas_call | solution.py:152
  99.5 32.0 %all_to_all.16.arrived_ref = f32[16,136,128]{2,1,0:T(8,128)S(1)} all-to-all(f32[16,136,128]{2,1,0:T(8,128)S(1)} %get-tuple-element.29), channel_id=1, replica_groups=mesh['group'=2,'term'=16] {'term'}, dimensions={0} | all-to-all | bytes 2228224 | tf_op jit(solution)/shard_map/all_to_all | solution.py:234
  131.5 1.6 %last.1 = (f32[2,128,128]{2,1,0:T(8,128)}, f32[2,128,128]{2,1,0:T(8,128)S(1)}, f32[8,128]{1,0:T(8,128)S(1)}) custom-call(s32[1]{0:T(128)} %bitcast.me_ref, s32[16,16]{1,0:T(8,128)S(1)} %copy-done.4, f32[16,136,128]{2,1,0:T(8,128)S(1)} %all_to_all.16.arrived_ref, f32[8,128]{1,0:T(8,128)S(1)} %get-tuple-element.30.square_ref, ...), custom_call_target="tpu_custom_call" | custom-call | tf_op jit(solution)/shard_map/last/pallas_call | solution.py:236
  133.0 9.7 %all_to_all.17 = f32[16,8,128]{2,1,0:T(8,128)S(1)} all-to-all(f32[16,8,128]{2,1,0:T(8,128)S(1)} %broadcast_in_dim.2), channel_id=1, replica_groups=mesh['group'=2,'term'=16] {'term'}, dimensions={0} | all-to-all | bytes 131072 | tf_op jit(solution)/shard_map/all_to_all | solution.py:247
  142.7 0.6 reduce_sum.9
  144.1 0.7 broadcast_divide_fusion
  (20 shorter events, 0.0 us)
Async XLA Ops:
  0.6 28.4 %copy-start.4 = (s32[16,16]{1,0:T(8,128)S(1)}, s32[16,16]{1,0:T(8,128)}, u32[]{:S(2)}) copy-start(s32[16,16]{1,0:T(8,128)} %store_ref.7) | copy-start | bytes 3076
  0.6 28.4 %copy-start.5 = (s32[16,16]{1,0:T(8,128)S(1)}, s32[16,16]{1,0:T(8,128)}, u32[]{:S(2)}) copy-start(s32[16,16]{1,0:T(8,128)} %fetch_ref.3) | copy-start | bytes 3076
  0.7 9.8 %collective-permute-start.11 = (f32[2,128,128]{2,1,0:T(8,128)}, f32[2,128,128]{2,1,0:T(8,128)S(1)}, u32[]{:S(2)}, u32[]{:S(2)}) collective-permute-start(f32[2,128,128]{2,1,0:T(8,128)} %vector_ref.1), channel_id=1, source_target_pairs={{0,12},{1,13},{2,14},{3,15},{4,8},{5,9},{6,10},{7,11},{8,4},{9,5},... | collective-permute-start | bytes 393224 | tf_op jit(solution)/shard_map/ppermute | solution.py:209
  5.8 11.3 %collective-permute-start.7 = (f32[2,128,128]{2,1,0:T(8,128)}, f32[2,128,128]{2,1,0:T(8,128)S(1)}, u32[]{:S(2)}, u32[]{:S(2)}) collective-permute-start(f32[2,128,128]{2,1,0:T(8,128)} %vector_ref.1), channel_id=1, source_target_pairs={{0,8},{1,9},{2,10},{3,11},{4,12},{5,13},{6,14},{7,15},{8,0},{9,1},... | collective-permute-start | bytes 393224 | tf_op jit(solution)/shard_map/ppermute | solution.py:209
  5.8 11.3 %collective-permute-start.3 = (f32[2,128,128]{2,1,0:T(8,128)}, f32[2,128,128]{2,1,0:T(8,128)S(1)}, u32[]{:S(2)}, u32[]{:S(2)}) collective-permute-start(f32[2,128,128]{2,1,0:T(8,128)} %vector_ref.1), channel_id=1, source_target_pairs={{0,4},{1,5},{2,6},{3,7},{4,0},{5,1},{6,2},{7,3},{8,12},{9,13},{10,... | collective-permute-start | bytes 393224 | tf_op jit(solution)/shard_map/ppermute | solution.py:209
  6.4 12.2 %collective-permute-start.1 = (f32[2,128,128]{2,1,0:T(8,128)}, f32[2,128,128]{2,1,0:T(8,128)S(1)}, u32[]{:S(2)}, u32[]{:S(2)}) collective-permute-start(f32[2,128,128]{2,1,0:T(8,128)} %vector_ref.1), channel_id=1, source_target_pairs={{0,2},{1,3},{2,0},{3,1},{4,6},{5,7},{6,4},{7,5},{8,10},{9,11},{10,... | collective-permute-start | bytes 393224 | tf_op jit(solution)/shard_map/ppermute | solution.py:209
  8.1 10.7 %collective-permute-start = (f32[2,128,128]{2,1,0:T(8,128)}, f32[2,128,128]{2,1,0:T(8,128)S(1)}, u32[]{:S(2)}, u32[]{:S(2)}) collective-permute-start(f32[2,128,128]{2,1,0:T(8,128)} %vector_ref.1), channel_id=1, source_target_pairs={{0,1},{1,0},{2,3},{3,2},{4,5},{5,4},{6,7},{7,6},{8,9},{9,8},{10,11... | collective-permute-start | bytes 393224 | tf_op jit(solution)/shard_map/ppermute | solution.py:209
  10.4 16.2 %collective-permute-start.13 = (f32[2,128,128]{2,1,0:T(8,128)S(1)}, f32[2,128,128]{2,1,0:T(8,128)S(1)}, u32[]{:S(2)}, u32[]{:S(2)}) collective-permute-start(f32[2,128,128]{2,1,0:T(8,128)S(1)} %collective-permute-done.11.refs_12_), channel_id=1, source_target_pairs={{0,2},{1,3},{2,0},{3,1},{4,6},{5,7},{6,4},{7,5},{8,10},{9,11},{10,... | collective-permute-start | bytes 393224 | tf_op jit(solution)/shard_map/ppermute | solution.py:209
  17.1 9.6 %collective-permute-start.12 = (f32[2,128,128]{2,1,0:T(8,128)S(1)}, f32[2,128,128]{2,1,0:T(8,128)S(1)}, u32[]{:S(2)}, u32[]{:S(2)}) collective-permute-start(f32[2,128,128]{2,1,0:T(8,128)S(1)} %collective-permute-done.11.refs_12_), channel_id=1, source_target_pairs={{0,1},{1,0},{2,3},{3,2},{4,5},{5,4},{6,7},{7,6},{8,9},{9,8},{10,11... | collective-permute-start | bytes 393224 | tf_op jit(solution)/shard_map/ppermute | solution.py:209
  17.1 10.1 %collective-permute-start.9 = (f32[2,128,128]{2,1,0:T(8,128)S(1)}, f32[2,128,128]{2,1,0:T(8,128)S(1)}, u32[]{:S(2)}, u32[]{:S(2)}) collective-permute-start(f32[2,128,128]{2,1,0:T(8,128)S(1)} %collective-permute-done.7.refs_8_), channel_id=1, source_target_pairs={{0,2},{1,3},{2,0},{3,1},{4,6},{5,7},{6,4},{7,5},{8,10},{9,11},{10,... | collective-permute-start | bytes 393224 | tf_op jit(solution)/shard_map/ppermute | solution.py:209
  18.6 8.7 %collective-permute-start.8 = (f32[2,128,128]{2,1,0:T(8,128)S(1)}, f32[2,128,128]{2,1,0:T(8,128)S(1)}, u32[]{:S(2)}, u32[]{:S(2)}) collective-permute-start(f32[2,128,128]{2,1,0:T(8,128)S(1)} %collective-permute-done.7.refs_8_), channel_id=1, source_target_pairs={{0,1},{1,0},{2,3},{3,2},{4,5},{5,4},{6,7},{7,6},{8,9},{9,8},{10,11... | collective-permute-start | bytes 393224 | tf_op jit(solution)/shard_map/ppermute | solution.py:209
  18.8 8.9 %collective-permute-start.5 = (f32[2,128,128]{2,1,0:T(8,128)S(1)}, f32[2,128,128]{2,1,0:T(8,128)S(1)}, u32[]{:S(2)}, u32[]{:S(2)}) collective-permute-start(f32[2,128,128]{2,1,0:T(8,128)S(1)} %collective-permute-done.1.refs_2_), channel_id=1, source_target_pairs={{0,4},{1,5},{2,6},{3,7},{4,0},{5,1},{6,2},{7,3},{8,12},{9,13},{10,... | collective-permute-start | bytes 393224 | tf_op jit(solution)/shard_map/ppermute | solution.py:209
  20.3 1.0 copy-start
  21.3 1.0 copy-start.1
  22.3 6.7 %copy-start.2 = (f32[2,128,128]{2,1,0:T(8,128)S(1)}, f32[2,128,128]{2,1,0:T(8,128)}, u32[]{:S(2)}) copy-start(f32[2,128,128]{2,1,0:T(8,128)} %vector_ref.1) | copy-start | bytes 393220
  26.6 1.6 %collective-permute-start.4 = (f32[2,128,128]{2,1,0:T(8,128)S(1)}, f32[2,128,128]{2,1,0:T(8,128)S(1)}, u32[]{:S(2)}, u32[]{:S(2)}) collective-permute-start(f32[2,128,128]{2,1,0:T(8,128)S(1)} %collective-permute-done.3.refs_4_), channel_id=1, source_target_pairs={{0,1},{1,0},{2,3},{3,2},{4,5},{5,4},{6,7},{7,6},{8,9},{9,8},{10,11... | collective-permute-start | bytes 393224 | tf_op jit(solution)/shard_map/ppermute | solution.py:209
  26.7 1.5 %collective-permute-start.2 = (f32[2,128,128]{2,1,0:T(8,128)S(1)}, f32[2,128,128]{2,1,0:T(8,128)S(1)}, u32[]{:S(2)}, u32[]{:S(2)}) collective-permute-start(f32[2,128,128]{2,1,0:T(8,128)S(1)} %collective-permute-done.1.refs_2_), channel_id=1, source_target_pairs={{0,1},{1,0},{2,3},{3,2},{4,5},{5,4},{6,7},{7,6},{8,9},{9,8},{10,11... | collective-permute-start | bytes 393224 | tf_op jit(solution)/shard_map/ppermute | solution.py:209
  27.1 1.3 collective-permute-start.14
  27.2 1.4 collective-permute-start.10
  27.7 1.3 collective-permute-start.6
  36.1 33.3 %copy-start.3 = (f32[2,128,128]{2,1,0:T(8,128)S(1)}, f32[2,128,128]{2,1,0:T(8,128)}, u32[]{:S(2)}) copy-start(f32[2,128,128]{2,1,0:T(8,128)} %precond_ref.3) | copy-start | bytes 393220
  70.3 8.3 %collective-permute-start.26 = (f32[2,128,128]{2,1,0:T(8,128)S(1)}, f32[2,128,128]{2,1,0:T(8,128)S(1)}, u32[]{:S(2)}, u32[]{:S(2)}) collective-permute-start(f32[2,128,128]{2,1,0:T(8,128)S(1)} %step.1.refs_0_.vector_ref), channel_id=1, source_target_pairs={{0,12},{1,13},{2,14},{3,15},{4,8},{5,9},{6,10},{7,11},{8,4},{9,5},... | collective-permute-start | bytes 393224 | tf_op jit(solution)/shard_map/ppermute | solution.py:209
  71.8 12.6 %collective-permute-start.22 = (f32[2,128,128]{2,1,0:T(8,128)S(1)}, f32[2,128,128]{2,1,0:T(8,128)S(1)}, u32[]{:S(2)}, u32[]{:S(2)}) collective-permute-start(f32[2,128,128]{2,1,0:T(8,128)S(1)} %step.1.refs_0_.vector_ref), channel_id=1, source_target_pairs={{0,8},{1,9},{2,10},{3,11},{4,12},{5,13},{6,14},{7,15},{8,0},{9,1},... | collective-permute-start | bytes 393224 | tf_op jit(solution)/shard_map/ppermute | solution.py:209
  72.4 11.9 %collective-permute-start.18 = (f32[2,128,128]{2,1,0:T(8,128)S(1)}, f32[2,128,128]{2,1,0:T(8,128)S(1)}, u32[]{:S(2)}, u32[]{:S(2)}) collective-permute-start(f32[2,128,128]{2,1,0:T(8,128)S(1)} %step.1.refs_0_.vector_ref), channel_id=1, source_target_pairs={{0,4},{1,5},{2,6},{3,7},{4,0},{5,1},{6,2},{7,3},{8,12},{9,13},{10,... | collective-permute-start | bytes 393224 | tf_op jit(solution)/shard_map/ppermute | solution.py:209
  74.7 10.3 %collective-permute-start.16 = (f32[2,128,128]{2,1,0:T(8,128)S(1)}, f32[2,128,128]{2,1,0:T(8,128)S(1)}, u32[]{:S(2)}, u32[]{:S(2)}) collective-permute-start(f32[2,128,128]{2,1,0:T(8,128)S(1)} %step.1.refs_0_.vector_ref), channel_id=1, source_target_pairs={{0,2},{1,3},{2,0},{3,1},{4,6},{5,7},{6,4},{7,5},{8,10},{9,11},{10,... | collective-permute-start | bytes 393224 | tf_op jit(solution)/shard_map/ppermute | solution.py:209
  75.3 9.9 %collective-permute-start.15 = (f32[2,128,128]{2,1,0:T(8,128)S(1)}, f32[2,128,128]{2,1,0:T(8,128)S(1)}, u32[]{:S(2)}, u32[]{:S(2)}) collective-permute-start(f32[2,128,128]{2,1,0:T(8,128)S(1)} %step.1.refs_0_.vector_ref), channel_id=1, source_target_pairs={{0,1},{1,0},{2,3},{3,2},{4,5},{5,4},{6,7},{7,6},{8,9},{9,8},{10,11... | collective-permute-start | bytes 393224 | tf_op jit(solution)/shard_map/ppermute | solution.py:209
  78.6 6.6 %collective-permute-start.28 = (f32[2,128,128]{2,1,0:T(8,128)S(1)}, f32[2,128,128]{2,1,0:T(8,128)S(1)}, u32[]{:S(2)}, u32[]{:S(2)}) collective-permute-start(f32[2,128,128]{2,1,0:T(8,128)S(1)} %collective-permute-done.26.refs_12_), channel_id=1, source_target_pairs={{0,2},{1,3},{2,0},{3,1},{4,6},{5,7},{6,4},{7,5},{8,10},{9,11},{10,... | collective-permute-start | bytes 393224 | tf_op jit(solution)/shard_map/ppermute | solution.py:209
  84.4 1.3 collective-permute-start.27
  84.4 5.9 %collective-permute-start.24 = (f32[2,128,128]{2,1,0:T(8,128)S(1)}, f32[2,128,128]{2,1,0:T(8,128)S(1)}, u32[]{:S(2)}, u32[]{:S(2)}) collective-permute-start(f32[2,128,128]{2,1,0:T(8,128)S(1)} %collective-permute-done.22.refs_8_), channel_id=1, source_target_pairs={{0,2},{1,3},{2,0},{3,1},{4,6},{5,7},{6,4},{7,5},{8,10},{9,11},{10,... | collective-permute-start | bytes 393224 | tf_op jit(solution)/shard_map/ppermute | solution.py:209
  85.0 5.3 %collective-permute-start.23 = (f32[2,128,128]{2,1,0:T(8,128)S(1)}, f32[2,128,128]{2,1,0:T(8,128)S(1)}, u32[]{:S(2)}, u32[]{:S(2)}) collective-permute-start(f32[2,128,128]{2,1,0:T(8,128)S(1)} %collective-permute-done.22.refs_8_), channel_id=1, source_target_pairs={{0,1},{1,0},{2,3},{3,2},{4,5},{5,4},{6,7},{7,6},{8,9},{9,8},{10,11... | collective-permute-start | bytes 393224 | tf_op jit(solution)/shard_map/ppermute | solution.py:209
  85.2 5.7 %collective-permute-start.20 = (f32[2,128,128]{2,1,0:T(8,128)S(1)}, f32[2,128,128]{2,1,0:T(8,128)S(1)}, u32[]{:S(2)}, u32[]{:S(2)}) collective-permute-start(f32[2,128,128]{2,1,0:T(8,128)S(1)} %collective-permute-done.16.refs_2_), channel_id=1, source_target_pairs={{0,4},{1,5},{2,6},{3,7},{4,0},{5,1},{6,2},{7,3},{8,12},{9,13},{10,... | collective-permute-start | bytes 393224 | tf_op jit(solution)/shard_map/ppermute | solution.py:209
  85.2 5.7 %collective-permute-start.17 = (f32[2,128,128]{2,1,0:T(8,128)S(1)}, f32[2,128,128]{2,1,0:T(8,128)S(1)}, u32[]{:S(2)}, u32[]{:S(2)}) collective-permute-start(f32[2,128,128]{2,1,0:T(8,128)S(1)} %collective-permute-done.16.refs_2_), channel_id=1, source_target_pairs={{0,1},{1,0},{2,3},{3,2},{4,5},{5,4},{6,7},{7,6},{8,9},{9,8},{10,11... | collective-permute-start | bytes 393224 | tf_op jit(solution)/shard_map/ppermute | solution.py:209
  85.7 5.2 %collective-permute-start.19 = (f32[2,128,128]{2,1,0:T(8,128)S(1)}, f32[2,128,128]{2,1,0:T(8,128)S(1)}, u32[]{:S(2)}, u32[]{:S(2)}) collective-permute-start(f32[2,128,128]{2,1,0:T(8,128)S(1)} %collective-permute-done.18.refs_4_), channel_id=1, source_target_pairs={{0,1},{1,0},{2,3},{3,2},{4,5},{5,4},{6,7},{7,6},{8,9},{9,8},{10,11... | collective-permute-start | bytes 393224 | tf_op jit(solution)/shard_map/ppermute | solution.py:209
  90.3 1.3 collective-permute-start.29
  90.3 1.5 %collective-permute-start.25 = (f32[2,128,128]{2,1,0:T(8,128)S(1)}, f32[2,128,128]{2,1,0:T(8,128)S(1)}, u32[]{:S(2)}, u32[]{:S(2)}) collective-permute-start(f32[2,128,128]{2,1,0:T(8,128)S(1)} %collective-permute-done.24.refs_10_), channel_id=1, source_target_pairs={{0,1},{1,0},{2,3},{3,2},{4,5},{5,4},{6,7},{7,6},{8,9},{9,8},{10,11... | collective-permute-start | bytes 393224 | tf_op jit(solution)/shard_map/ppermute | solution.py:209
  90.9 1.3 collective-permute-start.21

commit v2 on v1

--- a/solution.py
+++ b/solution.py
@@ -8,7 +8,7 @@
 from jax.sharding import PartitionSpec as P
 
 ITERS = 2
-CORE, ROW = 1, 2
+CORE, ROW, COLUMN = 1, 2, 4
 SMEM = pl.BlockSpec(memory_space=pltpu.SMEM)
 VMEM = pl.BlockSpec(memory_space=pltpu.VMEM)
 
@@ -96,7 +96,7 @@
 
 def apply_kernel(n, rows, me_ref, fetch_ref, store_ref, first_ref, second_ref, dst_ref, one_ref, two_ref,
                  count_ref, l4_ref, rr_ref, *refs):
-    pieces, (out_ref, square_ref, block, total) = refs[:n], refs[n:]
+    pieces, (near_ref, far_ref, square_ref, block, total) = refs[:n], refs[n:]
     me = me_ref[0]
     terms, width = l4_ref.shape[:2]
     square = jnp.zeros((8, width), jnp.float32)
@@ -136,12 +136,15 @@
             for k in range(group):
                 slot = slots[k * rows:(k + 1) * rows]
                 owner = lax.bitwise_xor(me, o + k)
-                out_ref[owner, start:start + rows, :] = slot
+                chip = (o + k) // 2
+                if (o + k) % 2:
+                    far_ref[chip * width + start:chip * width + start + rows, :] = slot
+                else:
+                    near_ref[chip, start:start + rows, :] = slot
                 held = pieces[o + k][store_ref[me, owner], start:start + rows, :]
                 product = product + tile_sum(held * slot)
     square_ref[...] = square
-    for r in range(n):
-        out_ref[r, width:, :] = product
+    far_ref[n // 2 * width:, :] = product
 
 
 def apply(n, me, fetch, store, tables, pieces):
@@ -152,11 +155,12 @@
     return pl.pallas_call(
         functools.partial(apply_kernel, n, rows),
         out_shape=(
-            jax.ShapeDtypeStruct((n, width + 8, width), jnp.float32),
+            jax.ShapeDtypeStruct((n // 2, width, width), jnp.float32),
+            jax.ShapeDtypeStruct((n // 2 * width + 8, width), jnp.float32),
             jax.ShapeDtypeStruct((8, width), jnp.float32),
         ),
         in_specs=[SMEM] * 9 + [VMEM] * (2 + n),
-        out_specs=[VMEM] * 2,
+        out_specs=[VMEM] * 3,
         scratch_shapes=[
             pltpu.VMEM((terms * n + 1 + npairs // 3, rows, width), jnp.float32),
             pltpu.VMEM((n, rows, 2 * terms * width), jnp.bfloat16),
@@ -166,30 +170,88 @@
     )(me, fetch, store, *tables[2:], *tables[:2], *pieces)
 
 
-def landed(n, me_ref, store_ref, arrived_ref):
+def swapped(x, k):
+    n = lax.axis_size("term")
+    return lax.ppermute(x, "term", [(i, i ^ k) for i in range(n)])
+
+
+def local(kernel, name, out_shape, scalars, arrays):
+    many = isinstance(out_shape, tuple)
+    return pl.pallas_call(
+        kernel,
+        out_shape=out_shape,
+        in_specs=[SMEM] * len(scalars) + [VMEM] * len(arrays),
+        out_specs=[VMEM] * len(out_shape) if many else VMEM,
+        compiler_params=params(16),
+        name=name,
+    )(*scalars, *arrays)
+
+
+def merge_kernel(over_rows, me_ref, store_ref, near_ref, far_ref, other_ref, keep_ref, column_ref, rows_ref, tile_ref):
     me = me_ref[0]
-    width = arrived_ref.shape[2]
-    sums = [jnp.zeros((width, width), jnp.float32) for _ in range(2)]
-    tile = jnp.zeros((8, width), jnp.float32)
-    for r in range(n):
-        mine = store_ref[r, me]
+    chips, width = near_ref.shape[:2]
+    kept = 0
+    for g in range(chips):
+        owner = lax.bitwise_xor(me, 2 * g)
+        mine = store_ref[me, owner]
+        others = store_ref[lax.bitwise_xor(me, CORE), owner]
         for b in range(2):
-            sums[b] = sums[b] + (mine == b).astype(jnp.float32) * arrived_ref[r, :width, :]
-        tile = tile + arrived_ref[r, width:, :]
+            block = (near_ref[g] * (mine == b).astype(jnp.float32)
+                     + other_ref[g * width:(g + 1) * width] * (others == b).astype(jnp.float32))
+            if g == 3:
+                column_ref[b] = block
+            elif g in over_rows:
+                at = (2 * over_rows.index(g) + b) * width
+                rows_ref[at:at + width] = block
+            else:
+                keep_ref[kept, b] = block
+        kept += g != 3 and g not in over_rows
+    tile = far_ref[chips * width:] + other_ref[chips * width:]
+    rows_ref[2 * len(over_rows) * width:] = tile
+    tile_ref[...] = tile
+
+
+def fold_kernel(over_rows, keep_ref, column_ref, rows_ref, tile_ref, step_ref, *send_refs):
+    width = keep_ref.shape[2]
+    tile = tile_ref[...] + rows_ref[2 * len(over_rows) * width:]
+    step_ref[...] = keep_ref[1] + column_ref[...]
+    for i, send_ref in enumerate(send_refs):
+        for b in range(2):
+            block = keep_ref[2 + i, b]
+            if 2 * i + 3 in over_rows:
+                at = (2 * over_rows.index(2 * i + 3) + b) * width
+                block = block + rows_ref[at:at + width]
+            send_ref[b * width:(b + 1) * width] = block
+        send_ref[2 * width:] = tile
+
+
+def landed(keep_ref, step_ref, refs):
+    width = keep_ref.shape[2]
+    sent, came = refs[0], refs[1:]
+    tile = sent[2 * width:]
+    for ref in came:
+        tile = tile + ref[2 * width:]
+    sums = []
+    for b in range(2):
+        total = keep_ref[0, b] + step_ref[b]
+        for ref in came:
+            total = total + ref[b * width:(b + 1) * width]
+        sums.append(total)
     return sums, jnp.sum(tile)
 
 
-def step_kernel(n, me_ref, store_ref, arrived_ref, square_ref, vector_ref, precond_ref, out_ref):
-    sigma, product = landed(n, me_ref, store_ref, arrived_ref)
+def step_kernel(keep_ref, step_ref, square_ref, vector_ref, precond_ref, *refs):
+    out_ref = refs[-1]
+    sigma, product = landed(keep_ref, step_ref, refs[:-1])
     theta = product / jnp.sum(square_ref[...])
     for b in range(2):
         v = vector_ref[b]
         out_ref[b] = v - precond_ref[b] * (sigma[b] - theta * v)
 
 
-def last_kernel(n, cells, me_ref, store_ref, arrived_ref, square_ref, vector_ref, precond_ref,
-                residual_ref, out_ref, tile_ref):
-    sigma, product = landed(n, me_ref, store_ref, arrived_ref)
+def last_kernel(cells, keep_ref, step_ref, square_ref, vector_ref, precond_ref, *refs):
+    residual_ref, out_ref, tile_ref = refs[-3:]
+    sigma, product = landed(keep_ref, step_ref, refs[:-3])
     square = jnp.sum(square_ref[...])
     theta = product / square
     scale = 1.0 / jnp.sqrt(square / cells + 1e-06)
@@ -204,19 +266,41 @@
     tile_ref[...] = tile
 
 
+def scattered(n, me, store, near, far):
+    width = near.shape[1]
+    chips = n // 2
+    other = swapped(far, CORE)
+    over_rows = [g for g in range(5, chips, 2)][::-1]
+    kept = chips - 1 - len(over_rows)
+    shape = lambda *dims: jax.ShapeDtypeStruct(dims, jnp.float32)
+    keep, column, rows, tile = local(
+        functools.partial(merge_kernel, over_rows), "merge",
+        (shape(kept, 2, width, width), shape(2, width, width),
+         shape(2 * len(over_rows) * width + 8, width), shape(8, width)),
+        (me, store), (near, far, other))
+    rows = swapped(rows, ROW)
+    column = swapped(column, COLUMN)
+    step, *sends = local(
+        functools.partial(fold_kernel, over_rows), "fold",
+        (shape(2, width, width),) + (shape(2 * width + 8, width),) * (chips // 2 - 1),
+        (), (keep, column, rows, tile))
+    came = [swapped(x, 2 * ROW * (i + 1)) for i, x in reversed(list(enumerate(sends)))]
+    return keep, swapped(step, ROW), [sends[0], *came]
+
+
 def gathered(n, x, beside=None):
-    def send(y, k):
-        return lax.ppermute(y, "term", [(i, i ^ k) for i in range(n)])
-
-    pieces = {0: x, ROW: send(x, ROW)}
-    for k in range(4, n, 4):
-        pieces[k] = send(x, k)
+    pieces = {0: x}
+    for k in reversed(range(8, n, 4)):
+        pieces[k] = swapped(x, k)
     if beside is not None:
-        pieces[4], _ = lax.optimization_barrier((pieces[4], beside))
-    for k in range(4, n, 4):
-        pieces[k + ROW] = send(pieces[ROW], k) if k == 4 else send(pieces[k], ROW)
+        x, _ = lax.optimization_barrier((x, beside))
+    pieces[ROW] = swapped(x, ROW)
+    pieces[COLUMN] = swapped(x, COLUMN)
+    for k in reversed(range(8, n, 4)):
+        pieces[k + ROW] = swapped(pieces[k], ROW)
+    pieces[COLUMN + ROW] = swapped(pieces[ROW], COLUMN)
     for k in range(0, n, 2):
-        pieces[k + CORE] = send(pieces[k], CORE)
+        pieces[k + CORE] = swapped(pieces[k], CORE)
     return [pieces[k] for k in range(n)]
 
 
@@ -230,20 +314,14 @@
     tile = jax.ShapeDtypeStruct((8, width), jnp.float32)
     vector = wavefn
     for iteration in range(ITERS):
-        slots, square = apply(n, me, fetch_map, store_map, tables, gathered(n, vector, tables if iteration == 0 else None))
-        arrived = lax.all_to_all(slots, "term", split_axis=0, concat_axis=0, tiled=True)
-        last = iteration == ITERS - 1
-        result = pl.pallas_call(
-            functools.partial(last_kernel, n, cells) if last else functools.partial(step_kernel, n),
-            out_shape=(block, block, tile) if last else block,
-            in_specs=[SMEM] * 2 + [VMEM] * 4,
-            out_specs=[VMEM] * 3 if last else VMEM,
-            compiler_params=params(16),
-            name="last" if last else "step",
-        )(me, store_map, arrived, square, vector, precond)
-        if not last:
-            vector = result
-    residual, corrected, partial = result
+        pieces = gathered(n, vector, tables if iteration == 0 else None)
+        near, far, square = apply(n, me, fetch_map, store_map, tables, pieces)
+        keep, step, parts = scattered(n, me, store_map, near, far)
+        arrays = (keep, step, square, vector, precond, *parts)
+        if iteration < ITERS - 1:
+            vector = local(step_kernel, "step", block, (), arrays)
+    residual, corrected, partial = local(
+        functools.partial(last_kernel, cells), "last", (block, block, tile), (), arrays)
     tiles = lax.all_to_all(jnp.broadcast_to(partial[None], (n, 8, width)), "term",
                            split_axis=0, concat_axis=0, tiled=True)
     return corrected / jnp.sqrt(jnp.sum(tiles) / cells + 1e-06), residual

time: 145 us -> 127 us (0.88)
  blocking collectives: 75 us -> 10.3 us
  waiting for transfers between devices: 23 us -> 55.4 us
  starting transfers between devices: 19.6 us -> 33.8 us
    all_to_all x2 -> x0, blocking collectives: 65.3 us -> none  [shards(): lax.all_to_all(slots, 'term', split_axis=0, concat_axis=0, tiled=True)]
    ppermute x30 -> x44, waiting for transfers between devices: 23 us -> 55.4 us  [swapped(): return lax.ppermute(x, 'term', [(i, i ^ k) for i in range(n)])]
    ppermute x30 -> x44, starting transfers between devices: 19.6 us -> 33.8 us  [swapped(): return lax.ppermute(x, 'term', [(i, i ^ k) for i in range(n)])]
  transfers between devices with their start and end apart: 30 -> 44, of which waited for: 14 -> 25; matrix products, arithmetic and copies ran while one was open for 1% -> 0% of each run, Pallas kernels for 3% -> 3%
where the time goes in v2:
time: 127 us; the launch traced here: 126 us
  waiting for transfers between devices  55.4 us (44%)
  starting transfers between devices  33.8 us (27%)
  Pallas kernels  21.4 us (17%)
  blocking collectives  10.3 us (8%)
  local copies, waits for them, and re-layouts  2.23 us (2%)
  between operations  2.12 us (2%)
  other arithmetic  1.29 us (1%)
    ppermute x44, waiting for transfers between devices, swapped(): return lax.ppermute(x, 'term', [(i, i ^ k) for i in range(n)])  55.4 us
    ppermute x44, starting transfers between devices, swapped(): return lax.ppermute(x, 'term', [(i, i ^ k) for i in range(n)])  33.8 us
    pallas_call x2, Pallas kernels, apply(): pl.pallas_call(functools.partial(apply_kernel, n, rows), out_shape=(jax.S...  14.2 us
    all_to_all x1, blocking collectives, shards(): lax.all_to_all(jnp.broadcast_to(partial[None], (n, 8, width)), 'term', sp...  10.3 us
    pallas_call x1, Pallas kernels, prep(): pl.pallas_call(functools.partial(prep_kernel, n, terms * n + 1), out_shap...  4.37 us
    pallas_call x6, Pallas kernels, local(): pl.pallas_call(kernel, out_shape=out_shape, in_specs=[SMEM] * len(scalars...  2.77 us
  transfers between devices with their start and end apart: 44, of which 25 were waited for; matrix products, arithmetic and copies ran while one was open for 0% of the time, Pallas kernels for 3%

profile of v2, /device:TPU:0, one launch (start us, length us, event | category | flops | bytes accessed | tf_op | source)
XLA Modules:
  0.0 126.5 jit_solution(10422855887583291222)
XLA Ops:
  0.6 5.1 %collective-permute-start.11 = (f32[2,128,128]{2,1,0:T(8,128)}, f32[2,128,128]{2,1,0:T(8,128)S(1)}, u32[]{:S(2)}, u32[]{:S(2)}) collective-permute-start(f32[2,128,128]{2,1,0:T(8,128)} %vector_ref.1), channel_id=1, source_target_pairs={{0,12},{1,13},{2,14},{3,15},{4,8},{5,9},{6,10},{7,11},{8,4},{9,5},... | collective-permute-start | bytes 393224 | tf_op jit(solution)/shard_map/ppermute | solution.py:175
  6.6 1.0 copy-done
  7.6 1.0 copy-done.1
  8.6 4.4 %prep.1 = (bf16[8,128,512]{2,1,0:T(8,128)(2,1)S(1)}, bf16[2048,256]{1,0:T(8,128)(2,1)S(1)}, s32[128]{0:T(128)S(1)}, s32[128]{0:T(128)S(1)}, s32[128]{0:T(128)S(1...) custom-call(s32[1]{0:T(128)} %bitcast.me_ref, s32[128,3]{1,0:T(8,128)S(1)} %bitcast.2, s32[1]{0:T(128)S(6)} %copy.12.live_ref, ...), custom_call_target="tpu_custom_call" | custom-call | tf_op jit(solution)/shard_map/prep/pallas_call | solution.py:81
  13.1 2.0 %collective-permute-start.1 = (f32[2,128,128]{2,1,0:T(8,128)S(1)}, f32[2,128,128]{2,1,0:T(8,128)S(1)}, u32[]{:S(2)}, u32[]{:S(2)}) collective-permute-start(f32[2,128,128]{2,1,0:T(8,128)S(1)} %copy-done.2), channel_id=1, source_target_pairs={{0,2},{1,3},{2,0},{3,1},{4,6},{5,7},{6,4},{7,5},{8,10},{9,11},{10,... | collective-permute-start | bytes 393224 | tf_op jit(solution)/shard_map/ppermute | solution.py:175
  15.2 1.9 %collective-permute-done.7.refs_8_ = f32[2,128,128]{2,1,0:T(8,128)S(1)} collective-permute-done((f32[2,128,128]{2,1,0:T(8,128)}, f32[2,128,128]{2,1,0:T(8,128)S(1)}, u32[]{:S(2)}, u32[]{:S(2)}) %collective-permute-start.7) | collective-permute-done | bytes 131104 | tf_op jit(solution)/shard_map/ppermute | solution.py:175
  17.1 1.5 %collective-permute-start.9 = (f32[2,128,128]{2,1,0:T(8,128)S(1)}, f32[2,128,128]{2,1,0:T(8,128)S(1)}, u32[]{:S(2)}, u32[]{:S(2)}) collective-permute-start(f32[2,128,128]{2,1,0:T(8,128)S(1)} %collective-permute-done.7.refs_8_), channel_id=1, source_target_pairs={{0,2},{1,3},{2,0},{3,1},{4,6},{5,7},{6,4},{7,5},{8,10},{9,11},{10,... | collective-permute-start | bytes 393224 | tf_op jit(solution)/shard_map/ppermute | solution.py:175
  18.7 1.2 collective-permute-done.3.refs_4_
  19.9 1.7 %collective-permute-start.5 = (f32[2,128,128]{2,1,0:T(8,128)S(1)}, f32[2,128,128]{2,1,0:T(8,128)S(1)}, u32[]{:S(2)}, u32[]{:S(2)}) collective-permute-start(f32[2,128,128]{2,1,0:T(8,128)S(1)} %collective-permute-done.1.refs_2_), channel_id=1, source_target_pairs={{0,4},{1,5},{2,6},{3,7},{4,0},{5,1},{6,2},{7,3},{8,12},{9,13},{10,... | collective-permute-start | bytes 393224 | tf_op jit(solution)/shard_map/ppermute | solution.py:175
  21.6 0.7 collective-permute-done.13.refs_14_
  22.2 0.4 collective-permute-start.2
  22.7 2.3 %collective-permute-done.9.refs_10_ = f32[2,128,128]{2,1,0:T(8,128)S(1)} collective-permute-done((f32[2,128,128]{2,1,0:T(8,128)S(1)}, f32[2,128,128]{2,1,0:T(8,128)S(1)}, u32[]{:S(2)}, u32[]{:S(2)}) %collective-permute-start.9) | collective-permute-done | bytes 131104 | tf_op jit(solution)/shard_map/ppermute | solution.py:175
  25.0 0.3 collective-permute-start.14
  25.3 0.3 collective-permute-start.10
  25.5 0.2 collective-permute-done.5.refs_6_
  25.8 0.6 collective-permute-done.14.refs_15_
  26.4 0.3 collective-permute-done.10.refs_11_
  26.6 0.5 collective-permute-done.6.refs_7_
  27.1 7.0 %apply.2 = (f32[8,128,128]{2,1,0:T(8,128)S(1)}, f32[1032,128]{1,0:T(8,128)S(1)}, f32[8,128]{1,0:T(8,128)S(1)}) custom-call(s32[1]{0:T(128)} %bitcast.me_ref, s32[16,16]{1,0:T(8,128)S(1)} %copy-done.5, s32[16,16]{1,0:T(8,128)S(1)} %copy-done.4, s32[128]{0:T(128)S(1)} %get-tuple-element.36.first_ref, s32[128]{0:T(128)S(1)} %get-tuple-element.37.second_ref, ...), custom_call_target="tpu_custom_call" | custom-call | tf_op jit(solution)/shard_map/apply/pallas_call | solution.py:155
  34.2 1.9 %collective-permute-done.15.other_ref = f32[1032,128]{1,0:T(8,128)S(1)} collective-permute-done((f32[1032,128]{1,0:T(8,128)S(1)}, f32[1032,128]{1,0:T(8,128)S(1)}, u32[]{:S(2)}, u32[]{:S(2)}) %collective-permute-start.15) | collective-permute-done | bytes 528416 | tf_op jit(solution)/shard_map/ppermute | solution.py:175
  36.1 0.8 merge.2
  36.9 1.4 %collective-permute-start.17 = (f32[520,128]{1,0:T(8,128)S(1)}, f32[520,128]{1,0:T(8,128)S(1)}, u32[]{:S(2)}, u32[]{:S(2)}) collective-permute-start(f32[520,128]{1,0:T(8,128)S(1)} %get-tuple-element.49), channel_id=1, source_target_pairs={{0,2},{1,3},{2,0},{3,1},{4,6},{5,7},{6,4},{7,5},{8,10},{9,11},{10,... | collective-permute-start | bytes 798728 | tf_op jit(solution)/shard_map/ppermute | solution.py:175
  38.3 0.3 collective-permute-start.16
  38.6 4.9 %collective-permute-done.16.column_ref = f32[2,128,128]{2,1,0:T(8,128)S(1)} collective-permute-done((f32[2,128,128]{2,1,0:T(8,128)S(1)}, f32[2,128,128]{2,1,0:T(8,128)S(1)}, u32[]{:S(2)}, u32[]{:S(2)}) %collective-permute-start.16) | collective-permute-done | bytes 131104 | tf_op jit(solution)/shard_map/ppermute | solution.py:175
  43.6 1.9 %collective-permute-done.17.rows_ref = f32[520,128]{1,0:T(8,128)S(1)} collective-permute-done((f32[520,128]{1,0:T(8,128)S(1)}, f32[520,128]{1,0:T(8,128)S(1)}, u32[]{:S(2)}, u32[]{:S(2)}) %collective-permute-start.17) | collective-permute-done | bytes 266272 | tf_op jit(solution)/shard_map/ppermute | solution.py:175
  45.5 3.8 %collective-permute-start.19 = (f32[264,128]{1,0:T(8,128)S(1)}, f32[264,128]{1,0:T(8,128)S(1)}, u32[]{:S(2)}, u32[]{:S(2)}) collective-permute-start(f32[264,128]{1,0:T(8,128)S(1)} %get-tuple-element.54), channel_id=1, source_target_pairs={{0,12},{1,13},{2,14},{3,15},{4,8},{5,9},{6,10},{7,11},{8,4},{9,5},... | collective-permute-start | bytes 405512 | tf_op jit(solution)/shard_map/ppermute | solution.py:175
  49.3 0.7 collective-permute-start.21
  49.9 1.3 %collective-permute-start.18 = (f32[2,128,128]{2,1,0:T(8,128)S(1)}, f32[2,128,128]{2,1,0:T(8,128)S(1)}, u32[]{:S(2)}, u32[]{:S(2)}) collective-permute-start(f32[2,128,128]{2,1,0:T(8,128)S(1)} %get-tuple-element.51), channel_id=1, source_target_pairs={{0,2},{1,3},{2,0},{3,1},{4,6},{5,7},{6,4},{7,5},{8,10},{9,11},{10,... | collective-permute-start | bytes 393224 | tf_op jit(solution)/shard_map/ppermute | solution.py:175
  51.2 3.6 %collective-permute-done.18.step_ref = f32[2,128,128]{2,1,0:T(8,128)S(1)} collective-permute-done((f32[2,128,128]{2,1,0:T(8,128)S(1)}, f32[2,128,128]{2,1,0:T(8,128)S(1)}, u32[]{:S(2)}, u32[]{:S(2)}) %collective-permute-start.18) | collective-permute-done | bytes 131104 | tf_op jit(solution)/shard_map/ppermute | solution.py:175
  54.9 5.1 %collective-permute-done.20.refs_2_ = f32[264,128]{1,0:T(8,128)S(1)} collective-permute-done((f32[264,128]{1,0:T(8,128)S(1)}, f32[264,128]{1,0:T(8,128)S(1)}, u32[]{:S(2)}, u32[]{:S(2)}) %collective-permute-start.20) | collective-permute-done | bytes 135200 | tf_op jit(solution)/shard_map/ppermute | solution.py:175
  60.0 0.2 step.1.refs_0_.vector_ref
  60.2 3.0 %collective-permute-start.33 = (f32[2,128,128]{2,1,0:T(8,128)S(1)}, f32[2,128,128]{2,1,0:T(8,128)S(1)}, u32[]{:S(2)}, u32[]{:S(2)}) collective-permute-start(f32[2,128,128]{2,1,0:T(8,128)S(1)} %step.1.refs_0_.vector_ref), channel_id=1, source_target_pairs={{0,12},{1,13},{2,14},{3,15},{4,8},{5,9},{6,10},{7,11},{8,4},{9,5},... | collective-permute-start | bytes 393224 | tf_op jit(solution)/shard_map/ppermute | solution.py:175
  63.2 1.5 %collective-permute-start.25 = (f32[2,128,128]{2,1,0:T(8,128)S(1)}, f32[2,128,128]{2,1,0:T(8,128)S(1)}, u32[]{:S(2)}, u32[]{:S(2)}) collective-permute-start(f32[2,128,128]{2,1,0:T(8,128)S(1)} %step.1.refs_0_.vector_ref), channel_id=1, source_target_pairs={{0,4},{1,5},{2,6},{3,7},{4,0},{5,1},{6,2},{7,3},{8,12},{9,13},{10,... | collective-permute-start | bytes 393224 | tf_op jit(solution)/shard_map/ppermute | solution.py:175
  64.7 0.3 collective-permute-start.23
  65.0 3.6 %collective-permute-done.33.refs_12_ = f32[2,128,128]{2,1,0:T(8,128)S(1)} collective-permute-done((f32[2,128,128]{2,1,0:T(8,128)S(1)}, f32[2,128,128]{2,1,0:T(8,128)S(1)}, u32[]{:S(2)}, u32[]{:S(2)}) %collective-permute-start.33) | collective-permute-done | bytes 131104 | tf_op jit(solution)/shard_map/ppermute | solution.py:175
  68.5 0.3 collective-permute-start.35
  68.8 4.4 %collective-permute-done.29.refs_8_ = f32[2,128,128]{2,1,0:T(8,128)S(1)} collective-permute-done((f32[2,128,128]{2,1,0:T(8,128)S(1)}, f32[2,128,128]{2,1,0:T(8,128)S(1)}, u32[]{:S(2)}, u32[]{:S(2)}) %collective-permute-start.29) | collective-permute-done | bytes 131104 | tf_op jit(solution)/shard_map/ppermute | solution.py:175
  73.2 0.3 collective-permute-start.31
  73.5 0.3 collective-permute-start.30
  73.8 0.4 collective-permute-start.27
  74.3 0.3 collective-permute-done.34.refs_13_
  74.6 0.2 collective-permute-start.26
  74.7 4.4 %collective-permute-done.31.refs_10_ = f32[2,128,128]{2,1,0:T(8,128)S(1)} collective-permute-done((f32[2,128,128]{2,1,0:T(8,128)S(1)}, f32[2,128,128]{2,1,0:T(8,128)S(1)}, u32[]{:S(2)}, u32[]{:S(2)}) %collective-permute-start.31) | collective-permute-done | bytes 131104 | tf_op jit(solution)/shard_map/ppermute | solution.py:175
  79.1 0.5 collective-permute-start.32
  79.7 0.8 collective-permute-done.36.refs_15_
  80.5 0.2 collective-permute-done.32.refs_11_
  80.7 0.3 collective-permute-done.28.refs_7_
  81.0 7.2 %apply.3 = (f32[8,128,128]{2,1,0:T(8,128)S(1)}, f32[1032,128]{1,0:T(8,128)S(1)}, f32[8,128]{1,0:T(8,128)S(1)}) custom-call(s32[1]{0:T(128)} %bitcast.me_ref, s32[16,16]{1,0:T(8,128)S(1)} %copy-done.5, s32[16,16]{1,0:T(8,128)S(1)} %copy-done.4, s32[128]{0:T(128)S(1)} %get-tuple-element.36.first_ref, s32[128]{0:T(128)S(1)} %get-tuple-element.37.second_ref, ...), custom_call_target="tpu_custom_call" | custom-call | tf_op jit(solution)/shard_map/apply/pallas_call | solution.py:155
  88.3 1.9 %collective-permute-done.37.other_ref = f32[1032,128]{1,0:T(8,128)S(1)} collective-permute-done((f32[1032,128]{1,0:T(8,128)S(1)}, f32[1032,128]{1,0:T(8,128)S(1)}, u32[]{:S(2)}, u32[]{:S(2)}) %collective-permute-start.37) | collective-permute-done | bytes 528416 | tf_op jit(solution)/shard_map/ppermute | solution.py:175
  90.2 0.8 merge.3
  91.0 1.5 %collective-permute-start.39 = (f32[520,128]{1,0:T(8,128)S(1)}, f32[520,128]{1,0:T(8,128)S(1)}, u32[]{:S(2)}, u32[]{:S(2)}) collective-permute-start(f32[520,128]{1,0:T(8,128)S(1)} %get-tuple-element.60), channel_id=1, source_target_pairs={{0,2},{1,3},{2,0},{3,1},{4,6},{5,7},{6,4},{7,5},{8,10},{9,11},{10,... | collective-permute-start | bytes 798728 | tf_op jit(solution)/shard_map/ppermute | solution.py:175
  92.5 0.4 collective-permute-start.38
  92.8 4.9 %collective-permute-done.38.column_ref = f32[2,128,128]{2,1,0:T(8,128)S(1)} collective-permute-done((f32[2,128,128]{2,1,0:T(8,128)S(1)}, f32[2,128,128]{2,1,0:T(8,128)S(1)}, u32[]{:S(2)}, u32[]{:S(2)}) %collective-permute-start.38) | collective-permute-done | bytes 131104 | tf_op jit(solution)/shard_map/ppermute | solution.py:175
  97.7 1.8 %collective-permute-done.39.rows_ref = f32[520,128]{1,0:T(8,128)S(1)} collective-permute-done((f32[520,128]{1,0:T(8,128)S(1)}, f32[520,128]{1,0:T(8,128)S(1)}, u32[]{:S(2)}, u32[]{:S(2)}) %collective-permute-start.39) | collective-permute-done | bytes 266272 | tf_op jit(solution)/shard_map/ppermute | solution.py:175
  99.6 1.7 %collective-permute-start.41 = (f32[264,128]{1,0:T(8,128)S(1)}, f32[264,128]{1,0:T(8,128)S(1)}, u32[]{:S(2)}, u32[]{:S(2)}) collective-permute-start(f32[264,128]{1,0:T(8,128)S(1)} %get-tuple-element.65), channel_id=1, source_target_pairs={{0,12},{1,13},{2,14},{3,15},{4,8},{5,9},{6,10},{7,11},{8,4},{9,5},... | collective-permute-start | bytes 405512 | tf_op jit(solution)/shard_map/ppermute | solution.py:175
  101.2 0.4 collective-permute-start.42
  101.6 2.4 %collective-permute-start.43 = (f32[264,128]{1,0:T(8,128)S(1)}, f32[264,128]{1,0:T(8,128)S(1)}, u32[]{:S(2)}, u32[]{:S(2)}) collective-permute-start(f32[264,128]{1,0:T(8,128)S(1)} %get-tuple-element.64.refs_0_), channel_id=1, source_target_pairs={{0,4},{1,5},{2,6},{3,7},{4,0},{5,1},{6,2},{7,3},{8,12},{9,13},{10,... | collective-permute-start | bytes 405512 | tf_op jit(solution)/shard_map/ppermute | solution.py:175
  104.0 1.4 %collective-permute-start.40 = (f32[2,128,128]{2,1,0:T(8,128)S(1)}, f32[2,128,128]{2,1,0:T(8,128)S(1)}, u32[]{:S(2)}, u32[]{:S(2)}) collective-permute-start(f32[2,128,128]{2,1,0:T(8,128)S(1)} %get-tuple-element.62), channel_id=1, source_target_pairs={{0,2},{1,3},{2,0},{3,1},{4,6},{5,7},{6,4},{7,5},{8,10},{9,11},{10,... | collective-permute-start | bytes 393224 | tf_op jit(solution)/shard_map/ppermute | solution.py:175
  105.4 3.6 %collective-permute-done.40.step_ref = f32[2,128,128]{2,1,0:T(8,128)S(1)} collective-permute-done((f32[2,128,128]{2,1,0:T(8,128)S(1)}, f32[2,128,128]{2,1,0:T(8,128)S(1)}, u32[]{:S(2)}, u32[]{:S(2)}) %collective-permute-start.40) | collective-permute-done | bytes 131104 | tf_op jit(solution)/shard_map/ppermute | solution.py:175
  109.0 4.4 %collective-permute-done.42.refs_2_ = f32[264,128]{1,0:T(8,128)S(1)} collective-permute-done((f32[264,128]{1,0:T(8,128)S(1)}, f32[264,128]{1,0:T(8,128)S(1)}, u32[]{:S(2)}, u32[]{:S(2)}) %collective-permute-start.42) | collective-permute-done | bytes 135200 | tf_op jit(solution)/shard_map/ppermute | solution.py:175
  113.3 0.9 last.1
  114.2 10.3 %all_to_all.5 = f32[16,8,128]{2,1,0:T(8,128)S(1)} all-to-all(f32[16,8,128]{2,1,0:T(8,128)S(1)} %broadcast_in_dim.2), channel_id=1, replica_groups=mesh['group'=2,'term'=16] {'term'}, dimensions={0} | all-to-all | bytes 131072 | tf_op jit(solution)/shard_map/all_to_all | solution.py:325
  124.5 0.6 reduce_sum.9
  125.8 0.7 broadcast_divide_fusion
  (52 shorter events, 1.1 us)
Async XLA Ops:
  0.6 14.5 %collective-permute-start.11 = (f32[2,128,128]{2,1,0:T(8,128)}, f32[2,128,128]{2,1,0:T(8,128)S(1)}, u32[]{:S(2)}, u32[]{:S(2)}) collective-permute-start(f32[2,128,128]{2,1,0:T(8,128)} %vector_ref.1), channel_id=1, source_target_pairs={{0,12},{1,13},{2,14},{3,15},{4,8},{5,9},{6,10},{7,11},{8,4},{9,5},... | collective-permute-start | bytes 393224 | tf_op jit(solution)/shard_map/ppermute | solution.py:175
  5.7 11.4 %collective-permute-start.7 = (f32[2,128,128]{2,1,0:T(8,128)}, f32[2,128,128]{2,1,0:T(8,128)S(1)}, u32[]{:S(2)}, u32[]{:S(2)}) collective-permute-start(f32[2,128,128]{2,1,0:T(8,128)} %vector_ref.1), channel_id=1, source_target_pairs={{0,8},{1,9},{2,10},{3,11},{4,12},{5,13},{6,14},{7,15},{8,0},{9,1},... | collective-permute-start | bytes 393224 | tf_op jit(solution)/shard_map/ppermute | solution.py:175
  5.7 11.4 %collective-permute-start = (f32[2,128,128]{2,1,0:T(8,128)}, f32[2,128,128]{2,1,0:T(8,128)S(1)}, u32[]{:S(2)}, u32[]{:S(2)}) collective-permute-start(f32[2,128,128]{2,1,0:T(8,128)} %vector_ref.1), channel_id=1, source_target_pairs={{0,1},{1,0},{2,3},{3,2},{4,5},{5,4},{6,7},{7,6},{8,9},{9,8},{10,11... | collective-permute-start | bytes 393224 | tf_op jit(solution)/shard_map/ppermute | solution.py:175
  5.8 0.7 copy-start.6
  6.5 1.0 copy-start
  7.6 1.0 copy-start.1
  8.6 4.4 %copy-start.2 = (f32[2,128,128]{2,1,0:T(8,128)S(1)}, f32[2,128,128]{2,1,0:T(8,128)}, u32[]{:S(2)}) copy-start(f32[2,128,128]{2,1,0:T(8,128)} %vector_ref.1) | copy-start | bytes 393220
  8.6 18.5 %copy-start.5 = (s32[16,16]{1,0:T(8,128)S(1)}, s32[16,16]{1,0:T(8,128)}, u32[]{:S(2)}) copy-start(s32[16,16]{1,0:T(8,128)} %fetch_ref.3) | copy-start | bytes 3076
  13.0 14.1 %copy-start.4 = (s32[16,16]{1,0:T(8,128)S(1)}, s32[16,16]{1,0:T(8,128)}, u32[]{:S(2)}) copy-start(s32[16,16]{1,0:T(8,128)} %store_ref.7) | copy-start | bytes 3076
  13.0 6.8 %collective-permute-start.3 = (f32[2,128,128]{2,1,0:T(8,128)S(1)}, f32[2,128,128]{2,1,0:T(8,128)S(1)}, u32[]{:S(2)}, u32[]{:S(2)}) collective-permute-start(f32[2,128,128]{2,1,0:T(8,128)S(1)} %copy-done.2), channel_id=1, source_target_pairs={{0,4},{1,5},{2,6},{3,7},{4,0},{5,1},{6,2},{7,3},{8,12},{9,13},{10,... | collective-permute-start | bytes 393224 | tf_op jit(solution)/shard_map/ppermute | solution.py:175
  13.1 6.7 %collective-permute-start.1 = (f32[2,128,128]{2,1,0:T(8,128)S(1)}, f32[2,128,128]{2,1,0:T(8,128)S(1)}, u32[]{:S(2)}, u32[]{:S(2)}) collective-permute-start(f32[2,128,128]{2,1,0:T(8,128)S(1)} %copy-done.2), channel_id=1, source_target_pairs={{0,2},{1,3},{2,0},{3,1},{4,6},{5,7},{6,4},{7,5},{8,10},{9,11},{10,... | collective-permute-start | bytes 393224 | tf_op jit(solution)/shard_map/ppermute | solution.py:175
  15.1 7.1 %collective-permute-start.13 = (f32[2,128,128]{2,1,0:T(8,128)S(1)}, f32[2,128,128]{2,1,0:T(8,128)S(1)}, u32[]{:S(2)}, u32[]{:S(2)}) collective-permute-start(f32[2,128,128]{2,1,0:T(8,128)S(1)} %collective-permute-done.11.refs_12_), channel_id=1, source_target_pairs={{0,2},{1,3},{2,0},{3,1},{4,6},{5,7},{6,4},{7,5},{8,10},{9,11},{10,... | collective-permute-start | bytes 393224 | tf_op jit(solution)/shard_map/ppermute | solution.py:175
  17.1 5.5 %collective-permute-start.12 = (f32[2,128,128]{2,1,0:T(8,128)S(1)}, f32[2,128,128]{2,1,0:T(8,128)S(1)}, u32[]{:S(2)}, u32[]{:S(2)}) collective-permute-start(f32[2,128,128]{2,1,0:T(8,128)S(1)} %collective-permute-done.11.refs_12_), channel_id=1, source_target_pairs={{0,1},{1,0},{2,3},{3,2},{4,5},{5,4},{6,7},{7,6},{8,9},{9,8},{10,11... | collective-permute-start | bytes 393224 | tf_op jit(solution)/shard_map/ppermute | solution.py:175
  17.1 7.9 %collective-permute-start.9 = (f32[2,128,128]{2,1,0:T(8,128)S(1)}, f32[2,128,128]{2,1,0:T(8,128)S(1)}, u32[]{:S(2)}, u32[]{:S(2)}) collective-permute-start(f32[2,128,128]{2,1,0:T(8,128)S(1)} %collective-permute-done.7.refs_8_), channel_id=1, source_target_pairs={{0,2},{1,3},{2,0},{3,1},{4,6},{5,7},{6,4},{7,5},{8,10},{9,11},{10,... | collective-permute-start | bytes 393224 | tf_op jit(solution)/shard_map/ppermute | solution.py:175
  19.8 5.5 %collective-permute-start.8 = (f32[2,128,128]{2,1,0:T(8,128)S(1)}, f32[2,128,128]{2,1,0:T(8,128)S(1)}, u32[]{:S(2)}, u32[]{:S(2)}) collective-permute-start(f32[2,128,128]{2,1,0:T(8,128)S(1)} %collective-permute-done.7.refs_8_), channel_id=1, source_target_pairs={{0,1},{1,0},{2,3},{3,2},{4,5},{5,4},{6,7},{7,6},{8,9},{9,8},{10,11... | collective-permute-start | bytes 393224 | tf_op jit(solution)/shard_map/ppermute | solution.py:175
  19.9 5.9 %collective-permute-start.5 = (f32[2,128,128]{2,1,0:T(8,128)S(1)}, f32[2,128,128]{2,1,0:T(8,128)S(1)}, u32[]{:S(2)}, u32[]{:S(2)}) collective-permute-start(f32[2,128,128]{2,1,0:T(8,128)S(1)} %collective-permute-done.1.refs_2_), channel_id=1, source_target_pairs={{0,4},{1,5},{2,6},{3,7},{4,0},{5,1},{6,2},{7,3},{8,12},{9,13},{10,... | collective-permute-start | bytes 393224 | tf_op jit(solution)/shard_map/ppermute | solution.py:175
  22.2 3.6 %collective-permute-start.2 = (f32[2,128,128]{2,1,0:T(8,128)S(1)}, f32[2,128,128]{2,1,0:T(8,128)S(1)}, u32[]{:S(2)}, u32[]{:S(2)}) collective-permute-start(f32[2,128,128]{2,1,0:T(8,128)S(1)} %collective-permute-done.1.refs_2_), channel_id=1, source_target_pairs={{0,1},{1,0},{2,3},{3,2},{4,5},{5,4},{6,7},{7,6},{8,9},{9,8},{10,11... | collective-permute-start | bytes 393224 | tf_op jit(solution)/shard_map/ppermute | solution.py:175
  22.6 3.2 %collective-permute-start.4 = (f32[2,128,128]{2,1,0:T(8,128)S(1)}, f32[2,128,128]{2,1,0:T(8,128)S(1)}, u32[]{:S(2)}, u32[]{:S(2)}) collective-permute-start(f32[2,128,128]{2,1,0:T(8,128)S(1)} %collective-permute-done.3.refs_4_), channel_id=1, source_target_pairs={{0,1},{1,0},{2,3},{3,2},{4,5},{5,4},{6,7},{7,6},{8,9},{9,8},{10,11... | collective-permute-start | bytes 393224 | tf_op jit(solution)/shard_map/ppermute | solution.py:175
  25.0 1.3 %collective-permute-start.14 = (f32[2,128,128]{2,1,0:T(8,128)S(1)}, f32[2,128,128]{2,1,0:T(8,128)S(1)}, u32[]{:S(2)}, u32[]{:S(2)}) collective-permute-start(f32[2,128,128]{2,1,0:T(8,128)S(1)} %collective-permute-done.13.refs_14_), channel_id=1, source_target_pairs={{0,1},{1,0},{2,3},{3,2},{4,5},{5,4},{6,7},{7,6},{8,9},{9,8},{10,11... | collective-permute-start | bytes 393224 | tf_op jit(solution)/shard_map/ppermute | solution.py:175
  25.3 1.3 %collective-permute-start.10 = (f32[2,128,128]{2,1,0:T(8,128)S(1)}, f32[2,128,128]{2,1,0:T(8,128)S(1)}, u32[]{:S(2)}, u32[]{:S(2)}) collective-permute-start(f32[2,128,128]{2,1,0:T(8,128)S(1)} %collective-permute-done.9.refs_10_), channel_id=1, source_target_pairs={{0,1},{1,0},{2,3},{3,2},{4,5},{5,4},{6,7},{7,6},{8,9},{9,8},{10,11... | collective-permute-start | bytes 393224 | tf_op jit(solution)/shard_map/ppermute | solution.py:175
  25.8 1.3 %collective-permute-start.6 = (f32[2,128,128]{2,1,0:T(8,128)S(1)}, f32[2,128,128]{2,1,0:T(8,128)S(1)}, u32[]{:S(2)}, u32[]{:S(2)}) collective-permute-start(f32[2,128,128]{2,1,0:T(8,128)S(1)} %collective-permute-done.5.refs_6_), channel_id=1, source_target_pairs={{0,1},{1,0},{2,3},{3,2},{4,5},{5,4},{6,7},{7,6},{8,9},{9,8},{10,11... | collective-permute-start | bytes 393224 | tf_op jit(solution)/shard_map/ppermute | solution.py:175
  34.1 2.0 %collective-permute-start.15 = (f32[1032,128]{1,0:T(8,128)S(1)}, f32[1032,128]{1,0:T(8,128)S(1)}, u32[]{:S(2)}, u32[]{:S(2)}) collective-permute-start(f32[1032,128]{1,0:T(8,128)S(1)} %get-tuple-element.46.far_ref), channel_id=1, source_target_pairs={{0,1},{1,0},{2,3},{3,2},{4,5},{5,4},{6,7},{7,6},{8,9},{9,8},{10,11... | collective-permute-start | bytes 1585160 | tf_op jit(solution)/shard_map/ppermute | solution.py:175
  36.9 8.5 %collective-permute-start.17 = (f32[520,128]{1,0:T(8,128)S(1)}, f32[520,128]{1,0:T(8,128)S(1)}, u32[]{:S(2)}, u32[]{:S(2)}) collective-permute-start(f32[520,128]{1,0:T(8,128)S(1)} %get-tuple-element.49), channel_id=1, source_target_pairs={{0,2},{1,3},{2,0},{3,1},{4,6},{5,7},{6,4},{7,5},{8,10},{9,11},{10,... | collective-permute-start | bytes 798728 | tf_op jit(solution)/shard_map/ppermute | solution.py:175
  38.3 5.3 %collective-permute-start.16 = (f32[2,128,128]{2,1,0:T(8,128)S(1)}, f32[2,128,128]{2,1,0:T(8,128)S(1)}, u32[]{:S(2)}, u32[]{:S(2)}) collective-permute-start(f32[2,128,128]{2,1,0:T(8,128)S(1)} %get-tuple-element.48), channel_id=1, source_target_pairs={{0,4},{1,5},{2,6},{3,7},{4,0},{5,1},{6,2},{7,3},{8,12},{9,13},{10,... | collective-permute-start | bytes 393224 | tf_op jit(solution)/shard_map/ppermute | solution.py:175
  45.4 14.6 %copy-start.3 = (f32[2,128,128]{2,1,0:T(8,128)S(1)}, f32[2,128,128]{2,1,0:T(8,128)}, u32[]{:S(2)}) copy-start(f32[2,128,128]{2,1,0:T(8,128)} %precond_ref.3) | copy-start | bytes 393220
  45.5 9.4 %collective-permute-start.19 = (f32[264,128]{1,0:T(8,128)S(1)}, f32[264,128]{1,0:T(8,128)S(1)}, u32[]{:S(2)}, u32[]{:S(2)}) collective-permute-start(f32[264,128]{1,0:T(8,128)S(1)} %get-tuple-element.54), channel_id=1, source_target_pairs={{0,12},{1,13},{2,14},{3,15},{4,8},{5,9},{6,10},{7,11},{8,4},{9,5},... | collective-permute-start | bytes 405512 | tf_op jit(solution)/shard_map/ppermute | solution.py:175
  49.3 10.8 %collective-permute-start.20 = (f32[264,128]{1,0:T(8,128)S(1)}, f32[264,128]{1,0:T(8,128)S(1)}, u32[]{:S(2)}, u32[]{:S(2)}) collective-permute-start(f32[264,128]{1,0:T(8,128)S(1)} %get-tuple-element.55), channel_id=1, source_target_pairs={{0,8},{1,9},{2,10},{3,11},{4,12},{5,13},{6,14},{7,15},{8,0},{9,1},... | collective-permute-start | bytes 405512 | tf_op jit(solution)/shard_map/ppermute | solution.py:175
  49.3 10.8 %collective-permute-start.21 = (f32[264,128]{1,0:T(8,128)S(1)}, f32[264,128]{1,0:T(8,128)S(1)}, u32[]{:S(2)}, u32[]{:S(2)}) collective-permute-start(f32[264,128]{1,0:T(8,128)S(1)} %get-tuple-element.53.refs_0_), channel_id=1, source_target_pairs={{0,4},{1,5},{2,6},{3,7},{4,0},{5,1},{6,2},{7,3},{8,12},{9,13},{10,... | collective-permute-start | bytes 405512 | tf_op jit(solution)/shard_map/ppermute | solution.py:175
  49.9 5.0 %collective-permute-start.18 = (f32[2,128,128]{2,1,0:T(8,128)S(1)}, f32[2,128,128]{2,1,0:T(8,128)S(1)}, u32[]{:S(2)}, u32[]{:S(2)}) collective-permute-start(f32[2,128,128]{2,1,0:T(8,128)S(1)} %get-tuple-element.51), channel_id=1, source_target_pairs={{0,2},{1,3},{2,0},{3,1},{4,6},{5,7},{6,4},{7,5},{8,10},{9,11},{10,... | collective-permute-start | bytes 393224 | tf_op jit(solution)/shard_map/ppermute | solution.py:175
  60.2 8.3 %collective-permute-start.33 = (f32[2,128,128]{2,1,0:T(8,128)S(1)}, f32[2,128,128]{2,1,0:T(8,128)S(1)}, u32[]{:S(2)}, u32[]{:S(2)}) collective-permute-start(f32[2,128,128]{2,1,0:T(8,128)S(1)} %step.1.refs_0_.vector_ref), channel_id=1, source_target_pairs={{0,12},{1,13},{2,14},{3,15},{4,8},{5,9},{6,10},{7,11},{8,4},{9,5},... | collective-permute-start | bytes 393224 | tf_op jit(solution)/shard_map/ppermute | solution.py:175
  63.2 10.0 %collective-permute-start.29 = (f32[2,128,128]{2,1,0:T(8,128)S(1)}, f32[2,128,128]{2,1,0:T(8,128)S(1)}, u32[]{:S(2)}, u32[]{:S(2)}) collective-permute-start(f32[2,128,128]{2,1,0:T(8,128)S(1)} %step.1.refs_0_.vector_ref), channel_id=1, source_target_pairs={{0,8},{1,9},{2,10},{3,11},{4,12},{5,13},{6,14},{7,15},{8,0},{9,1},... | collective-permute-start | bytes 393224 | tf_op jit(solution)/shard_map/ppermute | solution.py:175
  63.2 10.0 %collective-permute-start.25 = (f32[2,128,128]{2,1,0:T(8,128)S(1)}, f32[2,128,128]{2,1,0:T(8,128)S(1)}, u32[]{:S(2)}, u32[]{:S(2)}) collective-permute-start(f32[2,128,128]{2,1,0:T(8,128)S(1)} %step.1.refs_0_.vector_ref), channel_id=1, source_target_pairs={{0,4},{1,5},{2,6},{3,7},{4,0},{5,1},{6,2},{7,3},{8,12},{9,13},{10,... | collective-permute-start | bytes 393224 | tf_op jit(solution)/shard_map/ppermute | solution.py:175
  64.7 8.8 %collective-permute-start.23 = (f32[2,128,128]{2,1,0:T(8,128)S(1)}, f32[2,128,128]{2,1,0:T(8,128)S(1)}, u32[]{:S(2)}, u32[]{:S(2)}) collective-permute-start(f32[2,128,128]{2,1,0:T(8,128)S(1)} %step.1.refs_0_.vector_ref), channel_id=1, source_target_pairs={{0,2},{1,3},{2,0},{3,1},{4,6},{5,7},{6,4},{7,5},{8,10},{9,11},{10,... | collective-permute-start | bytes 393224 | tf_op jit(solution)/shard_map/ppermute | solution.py:175
  65.0 8.8 %collective-permute-start.22 = (f32[2,128,128]{2,1,0:T(8,128)S(1)}, f32[2,128,128]{2,1,0:T(8,128)S(1)}, u32[]{:S(2)}, u32[]{:S(2)}) collective-permute-start(f32[2,128,128]{2,1,0:T(8,128)S(1)} %step.1.refs_0_.vector_ref), channel_id=1, source_target_pairs={{0,1},{1,0},{2,3},{3,2},{4,5},{5,4},{6,7},{7,6},{8,9},{9,8},{10,11... | collective-permute-start | bytes 393224 | tf_op jit(solution)/shard_map/ppermute | solution.py:175
  68.5 5.7 %collective-permute-start.35 = (f32[2,128,128]{2,1,0:T(8,128)S(1)}, f32[2,128,128]{2,1,0:T(8,128)S(1)}, u32[]{:S(2)}, u32[]{:S(2)}) collective-permute-start(f32[2,128,128]{2,1,0:T(8,128)S(1)} %collective-permute-done.33.refs_12_), channel_id=1, source_target_pairs={{0,2},{1,3},{2,0},{3,1},{4,6},{5,7},{6,4},{7,5},{8,10},{9,11},{10,... | collective-permute-start | bytes 393224 | tf_op jit(solution)/shard_map/ppermute | solution.py:175
  73.2 1.3 %collective-permute-start.34 = (f32[2,128,128]{2,1,0:T(8,128)S(1)}, f32[2,128,128]{2,1,0:T(8,128)S(1)}, u32[]{:S(2)}, u32[]{:S(2)}) collective-permute-start(f32[2,128,128]{2,1,0:T(8,128)S(1)} %collective-permute-done.33.refs_12_), channel_id=1, source_target_pairs={{0,1},{1,0},{2,3},{3,2},{4,5},{5,4},{6,7},{7,6},{8,9},{9,8},{10,11... | collective-permute-start | bytes 393224 | tf_op jit(solution)/shard_map/ppermute | solution.py:175
  73.2 5.9 %collective-permute-start.31 = (f32[2,128,128]{2,1,0:T(8,128)S(1)}, f32[2,128,128]{2,1,0:T(8,128)S(1)}, u32[]{:S(2)}, u32[]{:S(2)}) collective-permute-start(f32[2,128,128]{2,1,0:T(8,128)S(1)} %collective-permute-done.29.refs_8_), channel_id=1, source_target_pairs={{0,2},{1,3},{2,0},{3,1},{4,6},{5,7},{6,4},{7,5},{8,10},{9,11},{10,... | collective-permute-start | bytes 393224 | tf_op jit(solution)/shard_map/ppermute | solution.py:175
  73.5 5.6 %collective-permute-start.30 = (f32[2,128,128]{2,1,0:T(8,128)S(1)}, f32[2,128,128]{2,1,0:T(8,128)S(1)}, u32[]{:S(2)}, u32[]{:S(2)}) collective-permute-start(f32[2,128,128]{2,1,0:T(8,128)S(1)} %collective-permute-done.29.refs_8_), channel_id=1, source_target_pairs={{0,1},{1,0},{2,3},{3,2},{4,5},{5,4},{6,7},{7,6},{8,9},{9,8},{10,11... | collective-permute-start | bytes 393224 | tf_op jit(solution)/shard_map/ppermute | solution.py:175
  73.8 5.8 %collective-permute-start.27 = (f32[2,128,128]{2,1,0:T(8,128)S(1)}, f32[2,128,128]{2,1,0:T(8,128)S(1)}, u32[]{:S(2)}, u32[]{:S(2)}) collective-permute-start(f32[2,128,128]{2,1,0:T(8,128)S(1)} %collective-permute-done.23.refs_2_), channel_id=1, source_target_pairs={{0,4},{1,5},{2,6},{3,7},{4,0},{5,1},{6,2},{7,3},{8,12},{9,13},{10,... | collective-permute-start | bytes 393224 | tf_op jit(solution)/shard_map/ppermute | solution.py:175
  74.2 5.5 %collective-permute-start.24 = (f32[2,128,128]{2,1,0:T(8,128)S(1)}, f32[2,128,128]{2,1,0:T(8,128)S(1)}, u32[]{:S(2)}, u32[]{:S(2)}) collective-permute-start(f32[2,128,128]{2,1,0:T(8,128)S(1)} %collective-permute-done.23.refs_2_), channel_id=1, source_target_pairs={{0,1},{1,0},{2,3},{3,2},{4,5},{5,4},{6,7},{7,6},{8,9},{9,8},{10,11... | collective-permute-start | bytes 393224 | tf_op jit(solution)/shard_map/ppermute | solution.py:175
  74.6 5.2 %collective-permute-start.26 = (f32[2,128,128]{2,1,0:T(8,128)S(1)}, f32[2,128,128]{2,1,0:T(8,128)S(1)}, u32[]{:S(2)}, u32[]{:S(2)}) collective-permute-start(f32[2,128,128]{2,1,0:T(8,128)S(1)} %collective-permute-done.25.refs_4_), channel_id=1, source_target_pairs={{0,1},{1,0},{2,3},{3,2},{4,5},{5,4},{6,7},{7,6},{8,9},{9,8},{10,11... | collective-permute-start | bytes 393224 | tf_op jit(solution)/shard_map/ppermute | solution.py:175
  79.1 1.3 %collective-permute-start.36 = (f32[2,128,128]{2,1,0:T(8,128)S(1)}, f32[2,128,128]{2,1,0:T(8,128)S(1)}, u32[]{:S(2)}, u32[]{:S(2)}) collective-permute-start(f32[2,128,128]{2,1,0:T(8,128)S(1)} %collective-permute-done.35.refs_14_), channel_id=1, source_target_pairs={{0,1},{1,0},{2,3},{3,2},{4,5},{5,4},{6,7},{7,6},{8,9},{9,8},{10,11... | collective-permute-start | bytes 393224 | tf_op jit(solution)/shard_map/ppermute | solution.py:175
  79.1 1.5 %collective-permute-start.32 = (f32[2,128,128]{2,1,0:T(8,128)S(1)}, f32[2,128,128]{2,1,0:T(8,128)S(1)}, u32[]{:S(2)}, u32[]{:S(2)}) collective-permute-start(f32[2,128,128]{2,1,0:T(8,128)S(1)} %collective-permute-done.31.refs_10_), channel_id=1, source_target_pairs={{0,1},{1,0},{2,3},{3,2},{4,5},{5,4},{6,7},{7,6},{8,9},{9,8},{10,11... | collective-permute-start | bytes 393224 | tf_op jit(solution)/shard_map/ppermute | solution.py:175
  79.6 1.3 %collective-permute-start.28 = (f32[2,128,128]{2,1,0:T(8,128)S(1)}, f32[2,128,128]{2,1,0:T(8,128)S(1)}, u32[]{:S(2)}, u32[]{:S(2)}) collective-permute-start(f32[2,128,128]{2,1,0:T(8,128)S(1)} %collective-permute-done.27.refs_6_), channel_id=1, source_target_pairs={{0,1},{1,0},{2,3},{3,2},{4,5},{5,4},{6,7},{7,6},{8,9},{9,8},{10,11... | collective-permute-start | bytes 393224 | tf_op jit(solution)/shard_map/ppermute | solution.py:175
  88.2 2.0 %collective-permute-start.37 = (f32[1032,128]{1,0:T(8,128)S(1)}, f32[1032,128]{1,0:T(8,128)S(1)}, u32[]{:S(2)}, u32[]{:S(2)}) collective-permute-start(f32[1032,128]{1,0:T(8,128)S(1)} %get-tuple-element.57.far_ref), channel_id=1, source_target_pairs={{0,1},{1,0},{2,3},{3,2},{4,5},{5,4},{6,7},{7,6},{8,9},{9,8},{10,11... | collective-permute-start | bytes 1585160 | tf_op jit(solution)/shard_map/ppermute | solution.py:175
  91.0 8.5 %collective-permute-start.39 = (f32[520,128]{1,0:T(8,128)S(1)}, f32[520,128]{1,0:T(8,128)S(1)}, u32[]{:S(2)}, u32[]{:S(2)}) collective-permute-start(f32[520,128]{1,0:T(8,128)S(1)} %get-tuple-element.60), channel_id=1, source_target_pairs={{0,2},{1,3},{2,0},{3,1},{4,6},{5,7},{6,4},{7,5},{8,10},{9,11},{10,... | collective-permute-start | bytes 798728 | tf_op jit(solution)/shard_map/ppermute | solution.py:175
  92.5 5.3 %collective-permute-start.38 = (f32[2,128,128]{2,1,0:T(8,128)S(1)}, f32[2,128,128]{2,1,0:T(8,128)S(1)}, u32[]{:S(2)}, u32[]{:S(2)}) collective-permute-start(f32[2,128,128]{2,1,0:T(8,128)S(1)} %get-tuple-element.59), channel_id=1, source_target_pairs={{0,4},{1,5},{2,6},{3,7},{4,0},{5,1},{6,2},{7,3},{8,12},{9,13},{10,... | collective-permute-start | bytes 393224 | tf_op jit(solution)/shard_map/ppermute | solution.py:175
  99.6 9.4 %collective-permute-start.41 = (f32[264,128]{1,0:T(8,128)S(1)}, f32[264,128]{1,0:T(8,128)S(1)}, u32[]{:S(2)}, u32[]{:S(2)}) collective-permute-start(f32[264,128]{1,0:T(8,128)S(1)} %get-tuple-element.65), channel_id=1, source_target_pairs={{0,12},{1,13},{2,14},{3,15},{4,8},{5,9},{6,10},{7,11},{8,4},{9,5},... | collective-permute-start | bytes 405512 | tf_op jit(solution)/shard_map/ppermute | solution.py:175
  101.2 12.1 %collective-permute-start.42 = (f32[264,128]{1,0:T(8,128)S(1)}, f32[264,128]{1,0:T(8,128)S(1)}, u32[]{:S(2)}, u32[]{:S(2)}) collective-permute-start(f32[264,128]{1,0:T(8,128)S(1)} %get-tuple-element.66), channel_id=1, source_target_pairs={{0,8},{1,9},{2,10},{3,11},{4,12},{5,13},{6,14},{7,15},{8,0},{9,1},... | collective-permute-start | bytes 405512 | tf_op jit(solution)/shard_map/ppermute | solution.py:175
  101.6 11.7 %collective-permute-start.43 = (f32[264,128]{1,0:T(8,128)S(1)}, f32[264,128]{1,0:T(8,128)S(1)}, u32[]{:S(2)}, u32[]{:S(2)}) collective-permute-start(f32[264,128]{1,0:T(8,128)S(1)} %get-tuple-element.64.refs_0_), channel_id=1, source_target_pairs={{0,4},{1,5},{2,6},{3,7},{4,0},{5,1},{6,2},{7,3},{8,12},{9,13},{10,... | collective-permute-start | bytes 405512 | tf_op jit(solution)/shard_map/ppermute | solution.py:175
  104.0 5.0 %collective-permute-start.40 = (f32[2,128,128]{2,1,0:T(8,128)S(1)}, f32[2,128,128]{2,1,0:T(8,128)S(1)}, u32[]{:S(2)}, u32[]{:S(2)}) collective-permute-start(f32[2,128,128]{2,1,0:T(8,128)S(1)} %get-tuple-element.62), channel_id=1, source_target_pairs={{0,2},{1,3},{2,0},{3,1},{4,6},{5,7},{6,4},{7,5},{8,10},{9,11},{10,... | collective-permute-start | bytes 393224 | tf_op jit(solution)/shard_map/ppermute | solution.py:175

commit v3 on v2

v3 whole, which is shorter than its diff:
```python
import functools

import jax
import jax.numpy as jnp
from jax import lax
from jax.experimental import pallas as pl
from jax.experimental.pallas import tpu as pltpu
from jax.sharding import PartitionSpec as P

ITERS = 2
CORE, ROW, COLUMN = 1, 2, 4
SMEM = pl.BlockSpec(memory_space=pltpu.SMEM)
VMEM = pl.BlockSpec(memory_space=pltpu.VMEM)


def params(mebibytes):
    return pltpu.CompilerParams(vmem_limit_bytes=mebibytes * 2**20)


def halves(x):
    high = x.astype(jnp.bfloat16)
    return high, (x - high.astype(jnp.float32)).astype(jnp.bfloat16)


def tile_sum(x):
    return jnp.sum(x.reshape(-1, 8, x.shape[-1]), axis=0)


def prep_kernel(n, spare, me_ref, fetch_ref, store_ref, pairs_ref, live_ref, vector_in, left_in, right_in, l4_ref, rr_ref,
                pick_ref, mine_ref, other_ref, first_ref, second_ref, dst_ref, one_ref, two_ref, count_ref, vector_ref,
                seen_ref, left_ref, right_ref, sems):
    copies = [pltpu.make_async_copy(source, target, sems.at[i]) for i, (source, target) in enumerate(
        ((left_in, left_ref), (right_in, right_ref), (vector_in, vector_ref)))]
    for copy in copies:
        copy.start()
    me = me_ref[0]
    terms = left_ref.shape[0]
    width = left_ref.shape[1]
    zero = terms * n
    for r in range(n):
        device = lax.bitwise_xor(me, r)
        pick_ref[r] = fetch_ref[device, me]
        mine_ref[r] = store_ref[me, device]
        other_ref[r] = store_ref[lax.bitwise_xor(me, CORE), device]

    def clear(cell, carry):
        first_ref[cell] = zero
        second_ref[cell] = zero
        seen_ref[cell] = 0
        return carry

    lax.fori_loop(0, terms * n, clear, 0, unroll=8)

    def pair(p, carry):
        extra, ops = carry
        a = lax.bitwise_xor(pairs_ref[p, 0], me)
        j = pairs_ref[p, 1]
        o = lax.bitwise_xor(pairs_ref[p, 2], me)
        cell = j * n + o
        source = a * terms + j
        seen = seen_ref[cell]
        seen_ref[cell] = seen + 1
        before = second_ref[cell]
        place = jnp.where(seen == 2, spare + extra, before)
        first_ref[cell] = jnp.where(seen == 0, source, first_ref[cell])
        second_ref[cell] = jnp.where(seen == 0, before, jnp.where(seen == 1, source, place))
        dst_ref[ops] = place
        one_ref[ops] = before
        two_ref[ops] = source
        return extra + (seen == 2).astype(jnp.int32), ops + (seen >= 2).astype(jnp.int32)

    _, ops = lax.fori_loop(0, live_ref[0], pair, (jnp.int32(0), jnp.int32(0)))
    count_ref[0] = ops
    for copy in copies:
        copy.wait()

    for j in range(terms):
        high, low = halves(left_ref[j])
        for k, part in enumerate((high, low, high, low)):
            l4_ref[j, :, k * width:(k + 1) * width] = part
        high, low = halves(right_ref[j])
        for k in range(2):
            row = (k * terms + j) * width
            rr_ref[row:row + width, :width] = high
            rr_ref[row:row + width, width:] = low


def prep(n, me, fetch, store, pairs, live, vector, left_ops, right_ops):
    terms, width = left_ops.shape[:2]
    npairs = pairs.shape[0]
    table = jax.ShapeDtypeStruct((terms * n,), jnp.int32)
    listed = jax.ShapeDtypeStruct((npairs,), jnp.int32)
    relative = jax.ShapeDtypeStruct((n,), jnp.int32)
    return pl.pallas_call(
        functools.partial(prep_kernel, n, terms * n + 1),
        out_shape=(
            jax.ShapeDtypeStruct((terms, width, 4 * width), jnp.bfloat16),
            jax.ShapeDtypeStruct((2 * terms * width, 2 * width), jnp.bfloat16),
            relative, relative, relative, table, table, listed, listed, listed,
            jax.ShapeDtypeStruct((1,), jnp.int32),
            jax.ShapeDtypeStruct(vector.shape, jnp.float32),
        ),
        in_specs=[SMEM] * 5 + [pl.BlockSpec(memory_space=pl.ANY)] * 3,
        out_specs=[VMEM] * 2 + [SMEM] * 9 + [VMEM],
        scratch_shapes=[
            pltpu.SMEM((terms * n,), jnp.int32),
            pltpu.VMEM(left_ops.shape, jnp.float32),
            pltpu.VMEM(left_ops.shape, jnp.float32),
            pltpu.SemaphoreType.DMA((3,)),
        ],
        compiler_params=params(16),
        name="prep",
    )(me, fetch, store, pairs, live, vector, left_ops, right_ops)


def right_products(picked, rows, start, mine_ref, first_ref, second_ref, rr_ref, pieces, block, total, near_ref, far_ref):
    width = block.shape[2]
    terms = rr_ref.shape[0] // (2 * width)
    n = len(pieces)
    product = jnp.zeros((8, width), jnp.float32)
    order = [(g, core) for g in picked for core in range(2)]
    for low_end in range(0, len(order), 4):
        group = order[low_end:low_end + 4]
        for k, (g, core) in enumerate(group):
            for j in range(terms):
                at = j * n + 2 * g + core
                high, low = halves(block[first_ref[at]] + block[second_ref[at]])
                total[low_end + k, :, j * width:(j + 1) * width] = high
                total[low_end + k, :, (terms + j) * width:(terms + j + 1) * width] = low
        both = jnp.dot(total[low_end:low_end + len(group)].reshape(len(group) * rows, 2 * terms * width), rr_ref[...],
                       preferred_element_type=jnp.float32)
        slots = both[:, :width] + both[:, width:]
        for k, (g, core) in enumerate(group):
            slot = slots[k * rows:(k + 1) * rows]
            at = picked.index(g) * rows
            if core and isinstance(far_ref, tuple):
                far_ref[picked.index(g)][...] = slot
            else:
                (far_ref if core else near_ref)[at:at + rows, :] = slot
            held = pieces[2 * g + core][mine_ref[2 * g + core], start:start + rows, :]
            product = product + tile_sum(held * slot)
    return product


def left_kernel(n, picked, rows, start, pick_ref, mine_ref, first_ref, second_ref, dst_ref, one_ref, two_ref,
                count_ref, l4_ref, rr_ref, *refs):
    pieces, (near_ref, far_ref, tile_ref, square_ref, block, total) = refs[:n], refs[n:]
    terms, width = l4_ref.shape[:2]
    square = jnp.zeros((8, width), jnp.float32)
    block[terms * n] = jnp.zeros((rows, width), jnp.float32)
    left = l4_ref[:, start:start + rows, :].reshape(terms * rows, 4 * width)
    for c in range(n // 2):
        columns = []
        for r in (2 * c, 2 * c + 1):
            high, low = halves(pieces[r][pick_ref[r]])
            columns.append(jnp.concatenate([high, high, low, low], axis=0))
            held = pieces[r][:, start:start + rows, :]
            square = square + tile_sum(held * held)
        both = jnp.dot(left, jnp.concatenate(columns, axis=1), preferred_element_type=jnp.float32)
        for k in range(2):
            at = (2 * c + k) * terms
            block[at:at + terms] = both[:, k * width:(k + 1) * width].reshape(terms, rows, width)
    square_ref[...] = square

    def add(i, carry):
        block[dst_ref[i]] = block[one_ref[i]] + block[two_ref[i]]
        return carry

    lax.fori_loop(0, count_ref[0], add, 0)
    tile_ref[...] = right_products(picked, rows, start, mine_ref, first_ref, second_ref, rr_ref, pieces, block,
                                   total, near_ref, far_ref)


def right_kernel(n, picked, rows, start, mine_ref, first_ref, second_ref, rr_ref, block, tile_ref, *refs):
    pieces, (near_ref, sum_ref), far_refs, total = refs[:n], refs[n:n + 2], refs[n + 2:-1], refs[-1]
    product = right_products(picked, rows, start, mine_ref, first_ref, second_ref, rr_ref, pieces, block,
                             total, near_ref, far_refs)
    sum_ref[...] = tile_ref[...] + product


def left(n, picked, rows, start, tables, pieces):
    terms, width = tables[0].shape[:2]
    spare = tables[7].shape[0] // 3
    shape = lambda *dims: jax.ShapeDtypeStruct(dims, jnp.float32)
    return pl.pallas_call(
        functools.partial(left_kernel, n, picked, rows, start),
        out_shape=(shape(len(picked) * rows, width), shape(len(picked) * rows, width), shape(8, width), shape(8, width),
                   shape(terms * n + 1 + spare, rows, width)),
        in_specs=[SMEM] * 8 + [VMEM] * (2 + n),
        out_specs=[VMEM] * 5,
        scratch_shapes=[pltpu.VMEM((2 * len(picked), rows, 2 * terms * width), jnp.bfloat16)],
        compiler_params=params(12 if n <= 16 else 48),
        name="left",
    )(*tables[2:4], *tables[5:], *tables[:2], *pieces)


def right(n, picked, rows, start, tables, blocks, tile, pieces):
    terms, width = tables[0].shape[:2]
    shape = lambda *dims: jax.ShapeDtypeStruct(dims, jnp.float32)
    return pl.pallas_call(
        functools.partial(right_kernel, n, picked, rows, start),
        out_shape=(shape(len(picked) * rows, width), shape(8, width)) + (shape(rows, width),) * len(picked),
        in_specs=[SMEM] * 3 + [VMEM] * (3 + n),
        out_specs=[VMEM] * (2 + len(picked)),
        scratch_shapes=[pltpu.VMEM((2 * len(picked), rows, 2 * terms * width), jnp.bfloat16)],
        compiler_params=params(12 if n <= 16 else 48),
        cost_estimate=pl.CostEstimate(flops=2 * 2 * len(picked) * rows * 2 * terms * width * 2 * width,
                                      bytes_accessed=2**20, transcendentals=0),
        name="right",
    )(tables[3], *tables[5:7], tables[1], blocks, tile, *pieces)


def joined(parts, count):
    if len(parts) == 1:
        return parts[0]
    width = parts[0].shape[1]
    return jnp.concatenate([x.reshape(count, -1, width) for x in parts], axis=1).reshape(-1, width)


def swapped(x, k):
    n = lax.axis_size("term")
    return lax.ppermute(x, "term", [(i, i ^ k) for i in range(n)])


def local(kernel, name, out_shape, scalars, arrays):
    many = isinstance(out_shape, tuple)
    return pl.pallas_call(
        kernel,
        out_shape=out_shape,
        in_specs=[SMEM] * len(scalars) + [VMEM] * len(arrays),
        out_specs=[VMEM] * len(out_shape) if many else VMEM,
        compiler_params=params(16),
        name=name,
    )(*scalars, *arrays)


def placed(mine_ref, other_ref, g, b, near, other):
    mine, others = mine_ref[2 * g], other_ref[2 * g]
    return near * (mine == b).astype(jnp.float32) + other * (others == b).astype(jnp.float32)


def merge_kernel(picked, mine_ref, others_ref, near_ref, other_ref, column_ref, rows_ref):
    width = near_ref.shape[1]
    column_ref[2] = jnp.zeros((width, width), jnp.float32)
    for i, g in enumerate(picked):
        for b in range(2):
            block = placed(mine_ref, others_ref, g, b, near_ref[i * width:(i + 1) * width],
                           other_ref[i * width:(i + 1) * width])
            if i == 0:
                column_ref[b] = block
            else:
                at = (2 * (i - 1) + b) * width
                rows_ref[at:at + width] = block


def fold_kernel(picked, early, mine_ref, others_ref, near_ref, column_ref, rows_ref, tile_ref, other_ref, *refs):
    far_refs, (own_ref, step_ref), send_refs = refs[:len(picked)], refs[len(picked):len(picked) + 2], refs[len(picked) + 2:]
    width = near_ref.shape[1]
    for i, g in enumerate(picked):
        for b in range(2):
            block = placed(mine_ref, others_ref, g, b, near_ref[i * width:(i + 1) * width],
                           far_refs[i][...])
            if g == 0:
                own_ref[b] = block
            elif g == 1:
                step_ref[b] = block + column_ref[b]
            else:
                if g + 1 in early[1:]:
                    at = (2 * early[1:].index(g + 1) + b) * width
                    block = block + rows_ref[at:at + width]
                send_refs[g // 2 - 1][b * width:(b + 1) * width] = block
    for send_ref in send_refs:
        send_ref[2 * width:] = tile_ref[...] + other_ref[...]


def landed(own_ref, step_ref, refs):
    width = own_ref.shape[2]
    sent, came = refs[0], refs[1:]
    tile = sent[2 * width:]
    for ref in came:
        tile = tile + ref[2 * width:]
    sums = []
    for b in range(2):
        total = own_ref[b] + step_ref[b]
        for ref in came:
            total = total + ref[b * width:(b + 1) * width]
        sums.append(total)
    return sums, jnp.sum(tile)


def step_kernel(own_ref, step_ref, square_ref, vector_ref, precond_ref, *refs):
    out_ref = refs[-1]
    sigma, product = landed(own_ref, step_ref, refs[:-1])
    theta = product / jnp.sum(square_ref[...])
    for b in range(2):
        v = vector_ref[b]
        out_ref[b] = v - precond_ref[b] * (sigma[b] - theta * v)


def last_kernel(cells, own_ref, step_ref, square_ref, vector_ref, precond_ref, *refs):
    residual_ref, out_ref, tile_ref = refs[-3:]
    sigma, product = landed(own_ref, step_ref, refs[:-3])
    square = jnp.sum(square_ref[...])
    theta = product / square
    scale = 1.0 / jnp.sqrt(square / cells + 1e-06)
    tile = jnp.zeros(tile_ref.shape, jnp.float32)
    for b in range(2):
        v = vector_ref[b]
        residual = (sigma[b] - theta * v) * scale
        residual_ref[b] = residual
        corrected = v * scale - precond_ref[b] * residual
        out_ref[b] = corrected
        tile = tile + tile_sum(corrected * corrected)
    tile_ref[...] = tile


def norm_kernel(cells, corrected_ref, tiles_ref, out_ref):
    scale = 1.0 / jnp.sqrt(jnp.sum(jnp.sum(tiles_ref[...], axis=0)) / cells + 1e-06)
    out_ref[...] = corrected_ref[...] * scale


def scattered(n, tables, pieces):
    width = pieces[0].shape[1]
    chips = n // 2
    rows = width if n <= 16 else width // 4
    starts = range(0, width, rows)
    over_rows = list(range(chips - 1, 3, -2))
    early = [3] + over_rows
    late = [g for g in range(chips) if g not in early]
    shape = lambda *dims: jax.ShapeDtypeStruct(dims, jnp.float32)

    firsts = [left(n, early, rows, start, tables, pieces) for start in starts]
    near, far = (joined([x[i] for x in firsts], len(early)) for i in range(2))
    square = sum(x[3] for x in firsts[1:]) + firsts[0][3] if len(firsts) > 1 else firsts[0][3]
    column, over = local(
        functools.partial(merge_kernel, early), "merge",
        (shape(3, width, width), shape(2 * len(over_rows) * width, width)), tables[3:5], (near, swapped(far, CORE)))
    tiles, column, over = lax.optimization_barrier(([x[2] for x in firsts], column, over))
    over_came = swapped(over, ROW)
    column_came = swapped(column, COLUMN)

    seconds = [right(n, late, rows, start, tables, x[4], tile, pieces)
               for start, x, tile in zip(starts, firsts, tiles)]
    near = joined([x[0] for x in seconds], len(late))
    far = [swapped(joined([x[2 + i] for x in seconds], 1), CORE) for i in range(len(late))]
    tile = sum(x[1] for x in seconds[1:]) + seconds[0][1] if len(seconds) > 1 else seconds[0][1]
    tile = tile + swapped(tile, CORE)
    own, step, *sends = local(
        functools.partial(fold_kernel, late, early), "fold",
        (shape(2, width, width),) * 2 + (shape(2 * width + 8, width),) * (chips // 2 - 1), tables[3:5],
        (near, column_came, over_came, tile, swapped(tile, ROW), *far))
    came = [swapped(x, 2 * ROW * (i + 1)) for i, x in reversed(list(enumerate(sends)))]
    return square, (own, swapped(step, ROW)), [sends[0], *came]


def gathered(n, x, held=None):
    pieces = {0: x}
    for k in reversed(range(8, n, 4)):
        pieces[k] = swapped(x, k)
    pieces[ROW] = swapped(x, ROW)
    pieces[COLUMN] = swapped(x, COLUMN)
    if held is not None:
        pieces[n - 4], pieces[0] = lax.optimization_barrier((pieces[n - 4], held))
    for k in reversed(range(8, n, 4)):
        pieces[k + ROW] = swapped(pieces[k], ROW)
    pieces[COLUMN + ROW] = swapped(pieces[ROW], COLUMN)
    for k in range(0, n, 2):
        pieces[k + CORE] = swapped(pieces[k], CORE)
    return [pieces[k] for k in range(n)]


def shards(wavefn, left_ops, right_ops, precond, fetch_map, store_map, pair_list, live_count):
    n = lax.axis_size("term")
    me = lax.axis_index("term").astype(jnp.int32).reshape(1)
    width = wavefn.shape[1]
    cells = wavefn.size * n
    *tables, held = prep(n, me, fetch_map, store_map, pair_list[0], live_count, wavefn, left_ops, right_ops)
    block = jax.ShapeDtypeStruct(wavefn.shape, jnp.float32)
    tile = jax.ShapeDtypeStruct((8, width), jnp.float32)
    vector = wavefn
    for iteration in range(ITERS):
        pieces = gathered(n, vector, held if iteration == 0 else None)
        vector = pieces[0]
        square, sums, parts = scattered(n, tables, pieces)
        arrays = (*sums, square, vector, precond, *parts)
        if iteration < ITERS - 1:
            vector = local(step_kernel, "step", block, (), arrays)
    residual, corrected, partial = local(
        functools.partial(last_kernel, cells), "last", (block, block, tile), (), arrays)
    tiles = lax.all_to_all(jnp.broadcast_to(partial[None], (n, 8, width)), "term",
                           split_axis=0, concat_axis=0, tiled=True)
    return local(functools.partial(norm_kernel, cells), "norm", block, (), (corrected, tiles)), residual


def solution(mesh):
    field = P(("group", "term"), None, None)
    return jax.shard_map(
        shards,
        mesh=mesh,
        in_specs=(field, field, field, field, P(), P(), P("term", None, None), P("term")),
        out_specs=(field, field),
        check_vma=False,
    )
```

time: 127 us -> 134 us (1.055)
  Pallas kernels: 21.4 us -> 25.1 us
  local copies, waits for them, and re-layouts: 2.23 us -> 5.17 us
  starting transfers between devices: 33.8 us -> 36.2 us
    unnamed x15 -> x13, local copies, waits for them, and re-layouts: 2.22 us -> 5.17 us
    pallas_call x2 -> x4, Pallas kernels: 14.2 us -> 16.8 us  [the longest x2 11.4 us: left(): pl.pallas_call(functools.partial(left_kernel, n, picked, rows, start), ou...]
    ppermute x44 -> x58, starting transfers between devices: 33.8 us -> 36.2 us  [swapped(): return lax.ppermute(x, 'term', [(i, i ^ k) for i in range(n)])]
    pallas_call x6 -> x7, Pallas kernels: 2.77 us -> 4.43 us  [local(): pl.pallas_call(kernel, out_shape=out_shape, in_specs=[SMEM] * len(scalars...]
    ppermute x44 -> x58, waiting for transfers between devices: 55.4 us -> 56.6 us  [swapped(): return lax.ppermute(x, 'term', [(i, i ^ k) for i in range(n)])]
  transfers between devices with their start and end apart: 44 -> 58, of which waited for: 25 -> 27; matrix products, arithmetic and copies ran while one was open for 0% -> 1% of each run, Pallas kernels for 3% -> 7%
where the time goes in v3:
time: 134 us
  waiting for transfers between devices  56.6 us (42%)
  starting transfers between devices  36.2 us (27%)
  Pallas kernels  25.1 us (19%)
  blocking collectives  9.51 us (7%)
  local copies, waits for them, and re-layouts  5.17 us (4%)
  between operations  1.47 us (1%)
    ppermute x58, waiting for transfers between devices, swapped(): return lax.ppermute(x, 'term', [(i, i ^ k) for i in range(n)])  56.6 us
    ppermute x58, starting transfers between devices, swapped(): return lax.ppermute(x, 'term', [(i, i ^ k) for i in range(n)])  36.2 us
    pallas_call x2, Pallas kernels, left(): pl.pallas_call(functools.partial(left_kernel, n, picked, rows, start), ou...  11.4 us
    all_to_all x1, blocking collectives, shards(): lax.all_to_all(jnp.broadcast_to(partial[None], (n, 8, width)), 'term', sp...  9.51 us
    pallas_call x2, Pallas kernels, right(): pl.pallas_call(functools.partial(right_kernel, n, picked, rows, start), o...  5.42 us
    unnamed x13, local copies, waits for them, and re-layouts  5.17 us
    pallas_call x7, Pallas kernels, local(): pl.pallas_call(kernel, out_shape=out_shape, in_specs=[SMEM] * len(scalars...  4.43 us
    pallas_call x1, Pallas kernels, prep(): pl.pallas_call(functools.partial(prep_kernel, n, terms * n + 1), out_shap...  3.89 us
  transfers between devices with their start and end apart: 58, of which 27 were waited for; matrix products, arithmetic and copies ran while one was open for 1% of the time, Pallas kernels for 7%

profile of v3, /device:TPU:0, one launch (start us, length us, event | category | flops | bytes accessed | tf_op | source)
XLA Modules:
  0.0 134.1 jit_solution(11571876220157223746)
XLA Ops:
  0.6 3.0 %collective-permute-start.2 = (f32[2,128,128]{2,1,0:T(8,128)}, f32[2,128,128]{2,1,0:T(8,128)S(1)}, u32[]{:S(2)}, u32[]{:S(2)}) collective-permute-start(f32[2,128,128]{2,1,0:T(8,128)} %vector_in.1), channel_id=1, source_target_pairs={{0,2},{1,3},{2,0},{3,1},{4,6},{5,7},{6,4},{7,5},{8,10},{9,11},{10,... | collective-permute-start | bytes 393224 | tf_op jit(solution)/shard_map/ppermute | solution.py:222
  3.7 2.6 %collective-permute-start.8 = (f32[2,128,128]{2,1,0:T(8,128)}, f32[2,128,128]{2,1,0:T(8,128)S(1)}, u32[]{:S(2)}, u32[]{:S(2)}) collective-permute-start(f32[2,128,128]{2,1,0:T(8,128)} %vector_in.1), channel_id=1, source_target_pairs={{0,8},{1,9},{2,10},{3,11},{4,12},{5,13},{6,14},{7,15},{8,0},{9,1},... | collective-permute-start | bytes 393224 | tf_op jit(solution)/shard_map/ppermute | solution.py:222
  6.3 1.3 %collective-permute-start = (f32[2,128,128]{2,1,0:T(8,128)}, f32[2,128,128]{2,1,0:T(8,128)S(1)}, u32[]{:S(2)}, u32[]{:S(2)}) collective-permute-start(f32[2,128,128]{2,1,0:T(8,128)} %vector_in.1), channel_id=1, source_target_pairs={{0,12},{1,13},{2,14},{3,15},{4,8},{5,9},{6,10},{7,11},{8,4},{9,5},... | collective-permute-start | bytes 393224 | tf_op jit(solution)/shard_map/ppermute | solution.py:222
  7.8 1.8 %collective-permute-start.6 = (f32[2,128,128]{2,1,0:T(8,128)S(1)}, f32[2,128,128]{2,1,0:T(8,128)S(1)}, u32[]{:S(2)}, u32[]{:S(2)}) collective-permute-start(f32[2,128,128]{2,1,0:T(8,128)S(1)} %collective-permute-done.2.refs_2_), channel_id=1, source_target_pairs={{0,4},{1,5},{2,6},{3,7},{4,0},{5,1},{6,2},{7,3},{8,12},{9,13},{10,... | collective-permute-start | bytes 393224 | tf_op jit(solution)/shard_map/ppermute | solution.py:222
  10.3 0.8 copy.10
  11.1 1.0 copy-done
  12.1 1.0 copy-done.1
  13.2 0.9 copy-done.3
  14.1 0.7 copy-done.4
  14.8 0.7 copy-done.5
  15.5 3.9 %prep.1 = (bf16[8,128,512]{2,1,0:T(8,128)(2,1)S(1)}, bf16[2048,256]{1,0:T(8,128)(2,1)S(1)}, s32[16]{0:T(128)S(1)}, s32[16]{0:T(128)S(1)}, s32[16]{0:T(128)S(1)},...) custom-call(s32[1]{0:T(128)} %bitcast.me_ref, ...), custom_call_target="tpu_custom_call" | custom-call | tf_op jit(solution)/shard_map/prep/pallas_call | solution.py:94
  19.4 2.6 %collective-permute-start.10 = (f32[2,128,128]{2,1,0:T(8,128)S(1)}, f32[2,128,128]{2,1,0:T(8,128)S(1)}, u32[]{:S(2)}, u32[]{:S(2)}) collective-permute-start(f32[2,128,128]{2,1,0:T(8,128)S(1)} %collective-permute-done.8.refs_8_), channel_id=1, source_target_pairs={{0,2},{1,3},{2,0},{3,1},{4,6},{5,7},{6,4},{7,5},{8,10},{9,11},{10,... | collective-permute-start | bytes 393224 | tf_op jit(solution)/shard_map/ppermute | solution.py:222
  22.8 3.6 %collective-permute-done.10.refs_10_ = f32[2,128,128]{2,1,0:T(8,128)S(1)} collective-permute-done((f32[2,128,128]{2,1,0:T(8,128)S(1)}, f32[2,128,128]{2,1,0:T(8,128)S(1)}, u32[]{:S(2)}, u32[]{:S(2)}) %collective-permute-start.10) | collective-permute-done | bytes 131104 | tf_op jit(solution)/shard_map/ppermute | solution.py:222
  26.4 0.5 collective-permute-start.7
  26.9 2.0 %collective-permute-done.13.refs_14_ = f32[2,128,128]{2,1,0:T(8,128)S(1)} collective-permute-done((f32[2,128,128]{2,1,0:T(8,128)S(1)}, f32[2,128,128]{2,1,0:T(8,128)S(1)}, u32[]{:S(2)}, u32[]{:S(2)}) %collective-permute-start.13) | collective-permute-done | bytes 131104 | tf_op jit(solution)/shard_map/ppermute | solution.py:222
  28.9 1.3 collective-permute-done.14.refs_15_
  30.3 5.7 %left.2 = (f32[384,128]{1,0:T(8,128)S(1)}, f32[384,128]{1,0:T(8,128)S(1)}, f32[8,128]{1,0:T(8,128)S(1)}, f32[8,128]{1,0:T(8,128)S(1)}, f32[171,128,128]{2,1,0:T(8,128)S(1)}) custom-call(s32[16]{0:T(128)S(1)} %get-tuple-element.68.pick_ref, s32[16]{0:T(128)S(1)} %get-tuple-element.63.mine_ref, s32[128]{0:T(128)S(1)} %get-tuple-element.65.first_ref, ...), custom_call_target="tpu_custom_call" | custom-call | tf_op jit(solution)/shard_map/left/pallas_call | solution.py:185
  36.2 1.3 collective-permute-done.15.other_ref
  37.5 0.6 merge.2
  38.1 2.0 %collective-permute-start.17 = (f32[512,128]{1,0:T(8,128)S(1)}, f32[512,128]{1,0:T(8,128)S(1)}, u32[]{:S(2)}, u32[]{:S(2)}) collective-permute-start(f32[512,128]{1,0:T(8,128)S(1)} %get-tuple-element.86), channel_id=1, source_target_pairs={{0,2},{1,3},{2,0},{3,1},{4,6},{5,7},{6,4},{7,5},{8,10},{9,11},{10,... | collective-permute-start | bytes 786440 | tf_op jit(solution)/shard_map/ppermute | solution.py:222
  40.2 2.7 %right.2 = (f32[640,128]{1,0:T(8,128)S(1)}, f32[8,128]{1,0:T(8,128)S(1)}, f32[128,128]{1,0:T(8,128)S(1)}, f32[128,128]{1,0:T(8,128)S(1)}, f32[128,128]{1,0:T(8,1...) custom-call(s32[16]{0:T(128)S(1)} %get-tuple-element.63.mine_ref, s32[128]{0:T(128)S(1)} %get-tuple-element.65.first_ref, ...), custom_call_target="tpu_custom_call" | custom-call | flops 1342177280 | bytes 1048576 | tf_op jit(solution)/shard_map/right/pallas_call | solution.py:200
  42.9 0.5 collective-permute-start.21
  43.5 1.1 collective-permute-done.18
  44.6 0.5 collective-permute-start.19
  45.1 3.1 %collective-permute-done.19.other_ref = f32[8,128]{1,0:T(8,128)S(1)} collective-permute-done((f32[8,128]{1,0:T(8,128)S(1)}, f32[8,128]{1,0:T(8,128)S(1)}, u32[]{:S(2)}, u32[]{:S(2)}) %collective-permute-start.19) | collective-permute-done | bytes 4128 | tf_op jit(solution)/shard_map/ppermute | solution.py:222
  48.2 0.5 collective-permute-start.23
  48.8 0.7 collective-permute-done.22.refs_2_
  49.6 0.4 collective-permute-done.24.refs_4_
  50.0 0.6 fold.2
  50.7 2.4 %collective-permute-start.26 = (f32[264,128]{1,0:T(8,128)S(1)}, f32[264,128]{1,0:T(8,128)S(1)}, u32[]{:S(2)}, u32[]{:S(2)}) collective-permute-start(f32[264,128]{1,0:T(8,128)S(1)} %get-tuple-element.97), channel_id=1, source_target_pairs={{0,12},{1,13},{2,14},{3,15},{4,8},{5,9},{6,10},{7,11},{8,4},{9,5},... | collective-permute-start | bytes 405512 | tf_op jit(solution)/shard_map/ppermute | solution.py:222
  53.0 1.1 collective-permute-start.27
  54.1 1.0 collective-permute-start.28
  55.1 0.5 collective-permute-start.25
  55.6 4.4 %collective-permute-done.25.step_ref = f32[2,128,128]{2,1,0:T(8,128)S(1)} collective-permute-done((f32[2,128,128]{2,1,0:T(8,128)S(1)}, f32[2,128,128]{2,1,0:T(8,128)S(1)}, u32[]{:S(2)}, u32[]{:S(2)}) %collective-permute-start.25) | collective-permute-done | bytes 131104 | tf_op jit(solution)/shard_map/ppermute | solution.py:222
  60.1 6.3 %collective-permute-done.27.refs_2_ = f32[264,128]{1,0:T(8,128)S(1)} collective-permute-done((f32[264,128]{1,0:T(8,128)S(1)}, f32[264,128]{1,0:T(8,128)S(1)}, u32[]{:S(2)}, u32[]{:S(2)}) %collective-permute-start.27) | collective-permute-done | bytes 135200 | tf_op jit(solution)/shard_map/ppermute | solution.py:222
  66.6 1.7 %collective-permute-start.40 = (f32[2,128,128]{2,1,0:T(8,128)S(1)}, f32[2,128,128]{2,1,0:T(8,128)S(1)}, u32[]{:S(2)}, u32[]{:S(2)}) collective-permute-start(f32[2,128,128]{2,1,0:T(8,128)S(1)} %step.1.refs_0_.vector_ref), channel_id=1, source_target_pairs={{0,12},{1,13},{2,14},{3,15},{4,8},{5,9},{6,10},{7,11},{8,4},{9,5},... | collective-permute-start | bytes 393224 | tf_op jit(solution)/shard_map/ppermute | solution.py:222
  68.3 2.8 %collective-permute-start.32 = (f32[2,128,128]{2,1,0:T(8,128)S(1)}, f32[2,128,128]{2,1,0:T(8,128)S(1)}, u32[]{:S(2)}, u32[]{:S(2)}) collective-permute-start(f32[2,128,128]{2,1,0:T(8,128)S(1)} %step.1.refs_0_.vector_ref), channel_id=1, source_target_pairs={{0,4},{1,5},{2,6},{3,7},{4,0},{5,1},{6,2},{7,3},{8,12},{9,13},{10,... | collective-permute-start | bytes 393224 | tf_op jit(solution)/shard_map/ppermute | solution.py:222
  71.2 3.8 %collective-permute-done.40.refs_12_ = f32[2,128,128]{2,1,0:T(8,128)S(1)} collective-permute-done((f32[2,128,128]{2,1,0:T(8,128)S(1)}, f32[2,128,128]{2,1,0:T(8,128)S(1)}, u32[]{:S(2)}, u32[]{:S(2)}) %collective-permute-start.40) | collective-permute-done | bytes 131104 | tf_op jit(solution)/shard_map/ppermute | solution.py:222
  75.1 4.0 %collective-permute-done.36.refs_8_ = f32[2,128,128]{2,1,0:T(8,128)S(1)} collective-permute-done((f32[2,128,128]{2,1,0:T(8,128)S(1)}, f32[2,128,128]{2,1,0:T(8,128)S(1)}, u32[]{:S(2)}, u32[]{:S(2)}) %collective-permute-start.36) | collective-permute-done | bytes 131104 | tf_op jit(solution)/shard_map/ppermute | solution.py:222
  79.1 0.6 collective-permute-start.37
  80.0 0.5 collective-permute-done.41.refs_13_
  80.6 4.4 %collective-permute-done.38.refs_10_ = f32[2,128,128]{2,1,0:T(8,128)S(1)} collective-permute-done((f32[2,128,128]{2,1,0:T(8,128)S(1)}, f32[2,128,128]{2,1,0:T(8,128)S(1)}, u32[]{:S(2)}, u32[]{:S(2)}) %collective-permute-start.38) | collective-permute-done | bytes 131104 | tf_op jit(solution)/shard_map/ppermute | solution.py:222
  85.0 0.5 collective-permute-start.39
  85.6 0.8 collective-permute-done.43.refs_15_
  86.9 5.7 %left.3 = (f32[384,128]{1,0:T(8,128)S(1)}, f32[384,128]{1,0:T(8,128)S(1)}, f32[8,128]{1,0:T(8,128)S(1)}, f32[8,128]{1,0:T(8,128)S(1)}, f32[171,128,128]{2,1,0:T(8,128)S(1)}) custom-call(s32[16]{0:T(128)S(1)} %get-tuple-element.68.pick_ref, s32[16]{0:T(128)S(1)} %get-tuple-element.63.mine_ref, s32[128]{0:T(128)S(1)} %get-tuple-element.65.first_ref, ...), custom_call_target="tpu_custom_call" | custom-call | tf_op jit(solution)/shard_map/left/pallas_call | solution.py:185
  92.9 1.2 collective-permute-done.44.other_ref
  94.1 0.6 merge.3
  94.7 1.8 %collective-permute-start.46 = (f32[512,128]{1,0:T(8,128)S(1)}, f32[512,128]{1,0:T(8,128)S(1)}, u32[]{:S(2)}, u32[]{:S(2)}) collective-permute-start(f32[512,128]{1,0:T(8,128)S(1)} %get-tuple-element.108), channel_id=1, source_target_pairs={{0,2},{1,3},{2,0},{3,1},{4,6},{5,7},{6,4},{7,5},{8,10},{9,11},{10,... | collective-permute-start | bytes 786440 | tf_op jit(solution)/shard_map/ppermute | solution.py:222
  96.7 2.7 %right.3 = (f32[640,128]{1,0:T(8,128)S(1)}, f32[8,128]{1,0:T(8,128)S(1)}, f32[128,128]{1,0:T(8,128)S(1)}, f32[128,128]{1,0:T(8,128)S(1)}, f32[128,128]{1,0:T(8,1...) custom-call(s32[16]{0:T(128)S(1)} %get-tuple-element.63.mine_ref, s32[128]{0:T(128)S(1)} %get-tuple-element.65.first_ref, ...), custom_call_target="tpu_custom_call" | custom-call | flops 1342177280 | bytes 1048576 | tf_op jit(solution)/shard_map/right/pallas_call | solution.py:200
  99.5 0.5 collective-permute-start.50
  100.1 1.1 collective-permute-done.47
  101.3 3.5 %collective-permute-done.48.other_ref = f32[8,128]{1,0:T(8,128)S(1)} collective-permute-done((f32[8,128]{1,0:T(8,128)S(1)}, f32[8,128]{1,0:T(8,128)S(1)}, u32[]{:S(2)}, u32[]{:S(2)}) %collective-permute-start.48) | collective-permute-done | bytes 4128 | tf_op jit(solution)/shard_map/ppermute | solution.py:222
  104.8 0.5 collective-permute-start.52
  105.4 0.7 collective-permute-done.51.refs_2_
  106.2 0.4 collective-permute-done.53.refs_4_
  106.6 0.6 fold.3
  107.2 1.7 %collective-permute-start.55 = (f32[264,128]{1,0:T(8,128)S(1)}, f32[264,128]{1,0:T(8,128)S(1)}, u32[]{:S(2)}, u32[]{:S(2)}) collective-permute-start(f32[264,128]{1,0:T(8,128)S(1)} %get-tuple-element.119), channel_id=1, source_target_pairs={{0,12},{1,13},{2,14},{3,15},{4,8},{5,9},{6,10},{7,11},{8,4},{9,5},... | collective-permute-start | bytes 405512 | tf_op jit(solution)/shard_map/ppermute | solution.py:222
  108.9 1.6 %collective-permute-start.56 = (f32[264,128]{1,0:T(8,128)S(1)}, f32[264,128]{1,0:T(8,128)S(1)}, u32[]{:S(2)}, u32[]{:S(2)}) collective-permute-start(f32[264,128]{1,0:T(8,128)S(1)} %get-tuple-element.120), channel_id=1, source_target_pairs={{0,8},{1,9},{2,10},{3,11},{4,12},{5,13},{6,14},{7,15},{8,0},{9,1},... | collective-permute-start | bytes 405512 | tf_op jit(solution)/shard_map/ppermute | solution.py:222
  110.5 1.2 collective-permute-start.57
  111.8 4.9 %collective-permute-done.54.step_ref = f32[2,128,128]{2,1,0:T(8,128)S(1)} collective-permute-done((f32[2,128,128]{2,1,0:T(8,128)S(1)}, f32[2,128,128]{2,1,0:T(8,128)S(1)}, u32[]{:S(2)}, u32[]{:S(2)}) %collective-permute-start.54) | collective-permute-done | bytes 131104 | tf_op jit(solution)/shard_map/ppermute | solution.py:222
  116.7 6.2 %collective-permute-done.56.refs_2_ = f32[264,128]{1,0:T(8,128)S(1)} collective-permute-done((f32[264,128]{1,0:T(8,128)S(1)}, f32[264,128]{1,0:T(8,128)S(1)}, u32[]{:S(2)}, u32[]{:S(2)}) %collective-permute-start.56) | collective-permute-done | bytes 135200 | tf_op jit(solution)/shard_map/ppermute | solution.py:222
  122.9 0.9 last.1
  123.7 9.5 %all_to_all.5.tiles_ref = f32[16,8,128]{2,1,0:T(8,128)S(1)} all-to-all(f32[16,8,128]{2,1,0:T(8,128)S(1)} %broadcast_in_dim.2), channel_id=1, replica_groups=mesh['group'=2,'term'=16] {'term'}, dimensions={0} | all-to-all | bytes 131072 | tf_op jit(solution)/shard_map/all_to_all | solution.py:390
  133.3 0.9 norm.1
  (81 shorter events, 4.5 us)
Async XLA Ops:
  0.6 7.2 %collective-permute-start.2 = (f32[2,128,128]{2,1,0:T(8,128)}, f32[2,128,128]{2,1,0:T(8,128)S(1)}, u32[]{:S(2)}, u32[]{:S(2)}) collective-permute-start(f32[2,128,128]{2,1,0:T(8,128)} %vector_in.1), channel_id=1, source_target_pairs={{0,2},{1,3},{2,0},{3,1},{4,6},{5,7},{6,4},{7,5},{8,10},{9,11},{10,... | collective-permute-start | bytes 393224 | tf_op jit(solution)/shard_map/ppermute | solution.py:222
  3.7 15.8 %collective-permute-start.8 = (f32[2,128,128]{2,1,0:T(8,128)}, f32[2,128,128]{2,1,0:T(8,128)S(1)}, u32[]{:S(2)}, u32[]{:S(2)}) collective-permute-start(f32[2,128,128]{2,1,0:T(8,128)} %vector_in.1), channel_id=1, source_target_pairs={{0,8},{1,9},{2,10},{3,11},{4,12},{5,13},{6,14},{7,15},{8,0},{9,1},... | collective-permute-start | bytes 393224 | tf_op jit(solution)/shard_map/ppermute | solution.py:222
  6.3 15.8 %collective-permute-start = (f32[2,128,128]{2,1,0:T(8,128)}, f32[2,128,128]{2,1,0:T(8,128)S(1)}, u32[]{:S(2)}, u32[]{:S(2)}) collective-permute-start(f32[2,128,128]{2,1,0:T(8,128)} %vector_in.1), channel_id=1, source_target_pairs={{0,12},{1,13},{2,14},{3,15},{4,8},{5,9},{6,10},{7,11},{8,4},{9,5},... | collective-permute-start | bytes 393224 | tf_op jit(solution)/shard_map/ppermute | solution.py:222
  7.6 14.6 %collective-permute-start.4 = (f32[2,128,128]{2,1,0:T(8,128)}, f32[2,128,128]{2,1,0:T(8,128)S(1)}, u32[]{:S(2)}, u32[]{:S(2)}) collective-permute-start(f32[2,128,128]{2,1,0:T(8,128)} %vector_in.1), channel_id=1, source_target_pairs={{0,4},{1,5},{2,6},{3,7},{4,0},{5,1},{6,2},{7,3},{8,12},{9,13},{10,... | collective-permute-start | bytes 393224 | tf_op jit(solution)/shard_map/ppermute | solution.py:222
  7.8 14.7 %collective-permute-start.6 = (f32[2,128,128]{2,1,0:T(8,128)S(1)}, f32[2,128,128]{2,1,0:T(8,128)S(1)}, u32[]{:S(2)}, u32[]{:S(2)}) collective-permute-start(f32[2,128,128]{2,1,0:T(8,128)S(1)} %collective-permute-done.2.refs_2_), channel_id=1, source_target_pairs={{0,4},{1,5},{2,6},{3,7},{4,0},{5,1},{6,2},{7,3},{8,12},{9,13},{10,... | collective-permute-start | bytes 393224 | tf_op jit(solution)/shard_map/ppermute | solution.py:222
  11.1 1.0 copy-start
  12.1 1.0 copy-start.1
  13.2 0.9 copy-start.3
  14.1 0.7 copy-start.4
  14.8 0.7 copy-start.5
  15.5 51.0 %copy-start.2 = (f32[2,128,128]{2,1,0:T(8,128)S(1)}, f32[2,128,128]{2,1,0:T(8,128)}, u32[]{:S(2)}) copy-start(f32[2,128,128]{2,1,0:T(8,128)} %precond_ref.3) | copy-start | bytes 393220
  19.4 3.3 %collective-permute-start.3 = (f32[2,128,128]{2,1,0:T(8,128)S(1)}, f32[2,128,128]{2,1,0:T(8,128)S(1)}, u32[]{:S(2)}, u32[]{:S(2)}) collective-permute-start(f32[2,128,128]{2,1,0:T(8,128)S(1)} %collective-permute-done.2.refs_2_), channel_id=1, source_target_pairs={{0,1},{1,0},{2,3},{3,2},{4,5},{5,4},{6,7},{7,6},{8,9},{9,8},{10,11... | collective-permute-start | bytes 393224 | tf_op jit(solution)/shard_map/ppermute | solution.py:222
  19.4 6.9 %collective-permute-start.10 = (f32[2,128,128]{2,1,0:T(8,128)S(1)}, f32[2,128,128]{2,1,0:T(8,128)S(1)}, u32[]{:S(2)}, u32[]{:S(2)}) collective-permute-start(f32[2,128,128]{2,1,0:T(8,128)S(1)} %collective-permute-done.8.refs_8_), channel_id=1, source_target_pairs={{0,2},{1,3},{2,0},{3,1},{4,6},{5,7},{6,4},{7,5},{8,10},{9,11},{10,... | collective-permute-start | bytes 393224 | tf_op jit(solution)/shard_map/ppermute | solution.py:222
  22.0 4.4 %collective-permute-start.9 = (f32[2,128,128]{2,1,0:T(8,128)S(1)}, f32[2,128,128]{2,1,0:T(8,128)S(1)}, u32[]{:S(2)}, u32[]{:S(2)}) collective-permute-start(f32[2,128,128]{2,1,0:T(8,128)S(1)} %collective-permute-done.8.refs_8_), channel_id=1, source_target_pairs={{0,1},{1,0},{2,3},{3,2},{4,5},{5,4},{6,7},{7,6},{8,9},{9,8},{10,11... | collective-permute-start | bytes 393224 | tf_op jit(solution)/shard_map/ppermute | solution.py:222
  22.2 4.7 %collective-permute-start.5 = (f32[2,128,128]{2,1,0:T(8,128)S(1)}, f32[2,128,128]{2,1,0:T(8,128)S(1)}, u32[]{:S(2)}, u32[]{:S(2)}) collective-permute-start(f32[2,128,128]{2,1,0:T(8,128)S(1)} %collective-permute-done.4.refs_4_), channel_id=1, source_target_pairs={{0,1},{1,0},{2,3},{3,2},{4,5},{5,4},{6,7},{7,6},{8,9},{9,8},{10,11... | collective-permute-start | bytes 393224 | tf_op jit(solution)/shard_map/ppermute | solution.py:222
  22.5 6.4 %collective-permute-start.13 = (f32[2,128,128]{2,1,0:T(8,128)S(1)}, f32[2,128,128]{2,1,0:T(8,128)S(1)}, u32[]{:S(2)}, u32[]{:S(2)}) collective-permute-start(f32[2,128,128]{2,1,0:T(8,128)S(1)} %collective-permute-done.refs_12_), channel_id=1, source_target_pairs={{0,2},{1,3},{2,0},{3,1},{4,6},{5,7},{6,4},{7,5},{8,10},{9,11},{10,... | collective-permute-start | bytes 393224 | tf_op jit(solution)/shard_map/ppermute | solution.py:222
  22.6 6.3 %collective-permute-start.12 = (f32[2,128,128]{2,1,0:T(8,128)S(1)}, f32[2,128,128]{2,1,0:T(8,128)S(1)}, u32[]{:S(2)}, u32[]{:S(2)}) collective-permute-start(f32[2,128,128]{2,1,0:T(8,128)S(1)} %collective-permute-done.refs_12_), channel_id=1, source_target_pairs={{0,1},{1,0},{2,3},{3,2},{4,5},{5,4},{6,7},{7,6},{8,9},{9,8},{10,11... | collective-permute-start | bytes 393224 | tf_op jit(solution)/shard_map/ppermute | solution.py:222
  26.4 2.6 %collective-permute-start.1 = (f32[2,128,128]{2,1,0:T(8,128)S(1)}, f32[2,128,128]{2,1,0:T(8,128)S(1)}, u32[]{:S(2)}, u32[]{:S(2)}) collective-permute-start(f32[2,128,128]{2,1,0:T(8,128)S(1)} %get-tuple-element.75.refs_0_.vector_ref), channel_id=1, source_target_pairs={{0,1},{1,0},{2,3},{3,2},{4,5},{5,4},{6,7},{7,6},{8,9},{9,8},{10,11... | collective-permute-start | bytes 393224 | tf_op jit(solution)/shard_map/ppermute | solution.py:222
  26.4 2.6 %collective-permute-start.7 = (f32[2,128,128]{2,1,0:T(8,128)S(1)}, f32[2,128,128]{2,1,0:T(8,128)S(1)}, u32[]{:S(2)}, u32[]{:S(2)}) collective-permute-start(f32[2,128,128]{2,1,0:T(8,128)S(1)} %collective-permute-done.6.refs_6_), channel_id=1, source_target_pairs={{0,1},{1,0},{2,3},{3,2},{4,5},{5,4},{6,7},{7,6},{8,9},{9,8},{10,11... | collective-permute-start | bytes 393224 | tf_op jit(solution)/shard_map/ppermute | solution.py:222
  26.9 2.1 %collective-permute-start.11 = (f32[2,128,128]{2,1,0:T(8,128)S(1)}, f32[2,128,128]{2,1,0:T(8,128)S(1)}, u32[]{:S(2)}, u32[]{:S(2)}) collective-permute-start(f32[2,128,128]{2,1,0:T(8,128)S(1)} %collective-permute-done.10.refs_10_), channel_id=1, source_target_pairs={{0,1},{1,0},{2,3},{3,2},{4,5},{5,4},{6,7},{7,6},{8,9},{9,8},{10,11... | collective-permute-start | bytes 393224 | tf_op jit(solution)/shard_map/ppermute | solution.py:222
  28.9 1.3 %collective-permute-start.14 = (f32[2,128,128]{2,1,0:T(8,128)S(1)}, f32[2,128,128]{2,1,0:T(8,128)S(1)}, u32[]{:S(2)}, u32[]{:S(2)}) collective-permute-start(f32[2,128,128]{2,1,0:T(8,128)S(1)} %collective-permute-done.13.refs_14_), channel_id=1, source_target_pairs={{0,1},{1,0},{2,3},{3,2},{4,5},{5,4},{6,7},{7,6},{8,9},{9,8},{10,11... | collective-permute-start | bytes 393224 | tf_op jit(solution)/shard_map/ppermute | solution.py:222
  35.9 1.5 %collective-permute-start.15 = (f32[384,128]{1,0:T(8,128)S(1)}, f32[384,128]{1,0:T(8,128)S(1)}, u32[]{:S(2)}, u32[]{:S(2)}) collective-permute-start(f32[384,128]{1,0:T(8,128)S(1)} %get-tuple-element.80), channel_id=1, source_target_pairs={{0,1},{1,0},{2,3},{3,2},{4,5},{5,4},{6,7},{7,6},{8,9},{9,8},{10,11... | collective-permute-start | bytes 589832 | tf_op jit(solution)/shard_map/ppermute | solution.py:222
  38.1 11.9 %collective-permute-start.17 = (f32[512,128]{1,0:T(8,128)S(1)}, f32[512,128]{1,0:T(8,128)S(1)}, u32[]{:S(2)}, u32[]{:S(2)}) collective-permute-start(f32[512,128]{1,0:T(8,128)S(1)} %get-tuple-element.86), channel_id=1, source_target_pairs={{0,2},{1,3},{2,0},{3,1},{4,6},{5,7},{6,4},{7,5},{8,10},{9,11},{10,... | collective-permute-start | bytes 786440 | tf_op jit(solution)/shard_map/ppermute | solution.py:222
  40.0 9.9 %collective-permute-start.16 = (f32[3,128,128]{2,1,0:T(8,128)S(1)}, f32[3,128,128]{2,1,0:T(8,128)S(1)}, u32[]{:S(2)}, u32[]{:S(2)}) collective-permute-start(f32[3,128,128]{2,1,0:T(8,128)S(1)} %get-tuple-element.85), channel_id=1, source_target_pairs={{0,4},{1,5},{2,6},{3,7},{4,0},{5,1},{6,2},{7,3},{8,12},{9,13},{10,... | collective-permute-start | bytes 589832 | tf_op jit(solution)/shard_map/ppermute | solution.py:222
  42.9 5.4 %collective-permute-start.20 = (f32[128,128]{1,0:T(8,128)S(1)}, f32[128,128]{1,0:T(8,128)S(1)}, u32[]{:S(2)}, u32[]{:S(2)}) collective-permute-start(f32[128,128]{1,0:T(8,128)S(1)} %get-tuple-element.88), channel_id=1, source_target_pairs={{0,1},{1,0},{2,3},{3,2},{4,5},{5,4},{6,7},{7,6},{8,9},{9,8},{10,11... | collective-permute-start | bytes 196616 | tf_op jit(solution)/shard_map/ppermute | solution.py:222
  42.9 5.8 %collective-permute-start.21 = (f32[128,128]{1,0:T(8,128)S(1)}, f32[128,128]{1,0:T(8,128)S(1)}, u32[]{:S(2)}, u32[]{:S(2)}) collective-permute-start(f32[128,128]{1,0:T(8,128)S(1)} %get-tuple-element.89), channel_id=1, source_target_pairs={{0,1},{1,0},{2,3},{3,2},{4,5},{5,4},{6,7},{7,6},{8,9},{9,8},{10,11... | collective-permute-start | bytes 196616 | tf_op jit(solution)/shard_map/ppermute | solution.py:222
  43.4 1.2 collective-permute-start.18
  44.6 3.6 %collective-permute-start.19 = (f32[8,128]{1,0:T(8,128)S(1)}, f32[8,128]{1,0:T(8,128)S(1)}, u32[]{:S(2)}, u32[]{:S(2)}) collective-permute-start(f32[8,128]{1,0:T(8,128)S(1)} %add.6.tile_ref), channel_id=1, source_target_pairs={{0,2},{1,3},{2,0},{3,1},{4,6},{5,7},{6,4},{7,5},{8,10},{9,11},{10,... | collective-permute-start | bytes 12296 | tf_op jit(solution)/shard_map/ppermute | solution.py:222
  48.2 1.3 collective-permute-start.22
  48.2 1.4 %collective-permute-start.23 = (f32[128,128]{1,0:T(8,128)S(1)}, f32[128,128]{1,0:T(8,128)S(1)}, u32[]{:S(2)}, u32[]{:S(2)}) collective-permute-start(f32[128,128]{1,0:T(8,128)S(1)} %get-tuple-element.91), channel_id=1, source_target_pairs={{0,1},{1,0},{2,3},{3,2},{4,5},{5,4},{6,7},{7,6},{8,9},{9,8},{10,11... | collective-permute-start | bytes 196616 | tf_op jit(solution)/shard_map/ppermute | solution.py:222
  48.7 1.3 collective-permute-start.24
  50.7 9.4 %collective-permute-start.26 = (f32[264,128]{1,0:T(8,128)S(1)}, f32[264,128]{1,0:T(8,128)S(1)}, u32[]{:S(2)}, u32[]{:S(2)}) collective-permute-start(f32[264,128]{1,0:T(8,128)S(1)} %get-tuple-element.97), channel_id=1, source_target_pairs={{0,12},{1,13},{2,14},{3,15},{4,8},{5,9},{6,10},{7,11},{8,4},{9,5},... | collective-permute-start | bytes 405512 | tf_op jit(solution)/shard_map/ppermute | solution.py:222
  53.0 13.4 %collective-permute-start.27 = (f32[264,128]{1,0:T(8,128)S(1)}, f32[264,128]{1,0:T(8,128)S(1)}, u32[]{:S(2)}, u32[]{:S(2)}) collective-permute-start(f32[264,128]{1,0:T(8,128)S(1)} %get-tuple-element.98), channel_id=1, source_target_pairs={{0,8},{1,9},{2,10},{3,11},{4,12},{5,13},{6,14},{7,15},{8,0},{9,1},... | collective-permute-start | bytes 405512 | tf_op jit(solution)/shard_map/ppermute | solution.py:222
  54.1 12.3 %collective-permute-start.28 = (f32[264,128]{1,0:T(8,128)S(1)}, f32[264,128]{1,0:T(8,128)S(1)}, u32[]{:S(2)}, u32[]{:S(2)}) collective-permute-start(f32[264,128]{1,0:T(8,128)S(1)} %get-tuple-element.96.refs_0_), channel_id=1, source_target_pairs={{0,4},{1,5},{2,6},{3,7},{4,0},{5,1},{6,2},{7,3},{8,12},{9,13},{10,... | collective-permute-start | bytes 405512 | tf_op jit(solution)/shard_map/ppermute | solution.py:222
  55.1 5.0 %collective-permute-start.25 = (f32[2,128,128]{2,1,0:T(8,128)S(1)}, f32[2,128,128]{2,1,0:T(8,128)S(1)}, u32[]{:S(2)}, u32[]{:S(2)}) collective-permute-start(f32[2,128,128]{2,1,0:T(8,128)S(1)} %get-tuple-element.94), channel_id=1, source_target_pairs={{0,2},{1,3},{2,0},{3,1},{4,6},{5,7},{6,4},{7,5},{8,10},{9,11},{10,... | collective-permute-start | bytes 393224 | tf_op jit(solution)/shard_map/ppermute | solution.py:222
  66.6 8.4 %collective-permute-start.40 = (f32[2,128,128]{2,1,0:T(8,128)S(1)}, f32[2,128,128]{2,1,0:T(8,128)S(1)}, u32[]{:S(2)}, u32[]{:S(2)}) collective-permute-start(f32[2,128,128]{2,1,0:T(8,128)S(1)} %step.1.refs_0_.vector_ref), channel_id=1, source_target_pairs={{0,12},{1,13},{2,14},{3,15},{4,8},{5,9},{6,10},{7,11},{8,4},{9,5},... | collective-permute-start | bytes 393224 | tf_op jit(solution)/shard_map/ppermute | solution.py:222
  68.3 10.8 %collective-permute-start.36 = (f32[2,128,128]{2,1,0:T(8,128)S(1)}, f32[2,128,128]{2,1,0:T(8,128)S(1)}, u32[]{:S(2)}, u32[]{:S(2)}) collective-permute-start(f32[2,128,128]{2,1,0:T(8,128)S(1)} %step.1.refs_0_.vector_ref), channel_id=1, source_target_pairs={{0,8},{1,9},{2,10},{3,11},{4,12},{5,13},{6,14},{7,15},{8,0},{9,1},... | collective-permute-start | bytes 393224 | tf_op jit(solution)/shard_map/ppermute | solution.py:222
  68.3 10.8 %collective-permute-start.32 = (f32[2,128,128]{2,1,0:T(8,128)S(1)}, f32[2,128,128]{2,1,0:T(8,128)S(1)}, u32[]{:S(2)}, u32[]{:S(2)}) collective-permute-start(f32[2,128,128]{2,1,0:T(8,128)S(1)} %step.1.refs_0_.vector_ref), channel_id=1, source_target_pairs={{0,4},{1,5},{2,6},{3,7},{4,0},{5,1},{6,2},{7,3},{8,12},{9,13},{10,... | collective-permute-start | bytes 393224 | tf_op jit(solution)/shard_map/ppermute | solution.py:222
  71.1 8.1 %collective-permute-start.30 = (f32[2,128,128]{2,1,0:T(8,128)S(1)}, f32[2,128,128]{2,1,0:T(8,128)S(1)}, u32[]{:S(2)}, u32[]{:S(2)}) collective-permute-start(f32[2,128,128]{2,1,0:T(8,128)S(1)} %step.1.refs_0_.vector_ref), channel_id=1, source_target_pairs={{0,2},{1,3},{2,0},{3,1},{4,6},{5,7},{6,4},{7,5},{8,10},{9,11},{10,... | collective-permute-start | bytes 393224 | tf_op jit(solution)/shard_map/ppermute | solution.py:222
  71.2 8.5 %collective-permute-start.29 = (f32[2,128,128]{2,1,0:T(8,128)S(1)}, f32[2,128,128]{2,1,0:T(8,128)S(1)}, u32[]{:S(2)}, u32[]{:S(2)}) collective-permute-start(f32[2,128,128]{2,1,0:T(8,128)S(1)} %step.1.refs_0_.vector_ref), channel_id=1, source_target_pairs={{0,1},{1,0},{2,3},{3,2},{4,5},{5,4},{6,7},{7,6},{8,9},{9,8},{10,11... | collective-permute-start | bytes 393224 | tf_op jit(solution)/shard_map/ppermute | solution.py:222
  75.0 5.0 %collective-permute-start.42 = (f32[2,128,128]{2,1,0:T(8,128)S(1)}, f32[2,128,128]{2,1,0:T(8,128)S(1)}, u32[]{:S(2)}, u32[]{:S(2)}) collective-permute-start(f32[2,128,128]{2,1,0:T(8,128)S(1)} %collective-permute-done.40.refs_12_), channel_id=1, source_target_pairs={{0,2},{1,3},{2,0},{3,1},{4,6},{5,7},{6,4},{7,5},{8,10},{9,11},{10,... | collective-permute-start | bytes 393224 | tf_op jit(solution)/shard_map/ppermute | solution.py:222
  79.1 1.3 %collective-permute-start.41 = (f32[2,128,128]{2,1,0:T(8,128)S(1)}, f32[2,128,128]{2,1,0:T(8,128)S(1)}, u32[]{:S(2)}, u32[]{:S(2)}) collective-permute-start(f32[2,128,128]{2,1,0:T(8,128)S(1)} %collective-permute-done.40.refs_12_), channel_id=1, source_target_pairs={{0,1},{1,0},{2,3},{3,2},{4,5},{5,4},{6,7},{7,6},{8,9},{9,8},{10,11... | collective-permute-start | bytes 393224 | tf_op jit(solution)/shard_map/ppermute | solution.py:222
  79.1 5.9 %collective-permute-start.38 = (f32[2,128,128]{2,1,0:T(8,128)S(1)}, f32[2,128,128]{2,1,0:T(8,128)S(1)}, u32[]{:S(2)}, u32[]{:S(2)}) collective-permute-start(f32[2,128,128]{2,1,0:T(8,128)S(1)} %collective-permute-done.36.refs_8_), channel_id=1, source_target_pairs={{0,2},{1,3},{2,0},{3,1},{4,6},{5,7},{6,4},{7,5},{8,10},{9,11},{10,... | collective-permute-start | bytes 393224 | tf_op jit(solution)/shard_map/ppermute | solution.py:222
  79.1 5.9 %collective-permute-start.37 = (f32[2,128,128]{2,1,0:T(8,128)S(1)}, f32[2,128,128]{2,1,0:T(8,128)S(1)}, u32[]{:S(2)}, u32[]{:S(2)}) collective-permute-start(f32[2,128,128]{2,1,0:T(8,128)S(1)} %collective-permute-done.36.refs_8_), channel_id=1, source_target_pairs={{0,1},{1,0},{2,3},{3,2},{4,5},{5,4},{6,7},{7,6},{8,9},{9,8},{10,11... | collective-permute-start | bytes 393224 | tf_op jit(solution)/shard_map/ppermute | solution.py:222
  79.7 5.8 %collective-permute-start.34 = (f32[2,128,128]{2,1,0:T(8,128)S(1)}, f32[2,128,128]{2,1,0:T(8,128)S(1)}, u32[]{:S(2)}, u32[]{:S(2)}) collective-permute-start(f32[2,128,128]{2,1,0:T(8,128)S(1)} %collective-permute-done.30.refs_2_), channel_id=1, source_target_pairs={{0,4},{1,5},{2,6},{3,7},{4,0},{5,1},{6,2},{7,3},{8,12},{9,13},{10,... | collective-permute-start | bytes 393224 | tf_op jit(solution)/shard_map/ppermute | solution.py:222
  80.0 5.7 %collective-permute-start.31 = (f32[2,128,128]{2,1,0:T(8,128)S(1)}, f32[2,128,128]{2,1,0:T(8,128)S(1)}, u32[]{:S(2)}, u32[]{:S(2)}) collective-permute-start(f32[2,128,128]{2,1,0:T(8,128)S(1)} %collective-permute-done.30.refs_2_), channel_id=1, source_target_pairs={{0,1},{1,0},{2,3},{3,2},{4,5},{5,4},{6,7},{7,6},{8,9},{9,8},{10,11... | collective-permute-start | bytes 393224 | tf_op jit(solution)/shard_map/ppermute | solution.py:222
  80.5 5.2 %collective-permute-start.33 = (f32[2,128,128]{2,1,0:T(8,128)S(1)}, f32[2,128,128]{2,1,0:T(8,128)S(1)}, u32[]{:S(2)}, u32[]{:S(2)}) collective-permute-start(f32[2,128,128]{2,1,0:T(8,128)S(1)} %collective-permute-done.32.refs_4_), channel_id=1, source_target_pairs={{0,1},{1,0},{2,3},{3,2},{4,5},{5,4},{6,7},{7,6},{8,9},{9,8},{10,11... | collective-permute-start | bytes 393224 | tf_op jit(solution)/shard_map/ppermute | solution.py:222
  85.0 1.3 %collective-permute-start.43 = (f32[2,128,128]{2,1,0:T(8,128)S(1)}, f32[2,128,128]{2,1,0:T(8,128)S(1)}, u32[]{:S(2)}, u32[]{:S(2)}) collective-permute-start(f32[2,128,128]{2,1,0:T(8,128)S(1)} %collective-permute-done.42.refs_14_), channel_id=1, source_target_pairs={{0,1},{1,0},{2,3},{3,2},{4,5},{5,4},{6,7},{7,6},{8,9},{9,8},{10,11... | collective-permute-start | bytes 393224 | tf_op jit(solution)/shard_map/ppermute | solution.py:222
  85.0 1.5 %collective-permute-start.39 = (f32[2,128,128]{2,1,0:T(8,128)S(1)}, f32[2,128,128]{2,1,0:T(8,128)S(1)}, u32[]{:S(2)}, u32[]{:S(2)}) collective-permute-start(f32[2,128,128]{2,1,0:T(8,128)S(1)} %collective-permute-done.38.refs_10_), channel_id=1, source_target_pairs={{0,1},{1,0},{2,3},{3,2},{4,5},{5,4},{6,7},{7,6},{8,9},{9,8},{10,11... | collective-permute-start | bytes 393224 | tf_op jit(solution)/shard_map/ppermute | solution.py:222
  85.5 1.3 %collective-permute-start.35 = (f32[2,128,128]{2,1,0:T(8,128)S(1)}, f32[2,128,128]{2,1,0:T(8,128)S(1)}, u32[]{:S(2)}, u32[]{:S(2)}) collective-permute-start(f32[2,128,128]{2,1,0:T(8,128)S(1)} %collective-permute-done.34.refs_6_), channel_id=1, source_target_pairs={{0,1},{1,0},{2,3},{3,2},{4,5},{5,4},{6,7},{7,6},{8,9},{9,8},{10,11... | collective-permute-start | bytes 393224 | tf_op jit(solution)/shard_map/ppermute | solution.py:222
  92.6 1.5 %collective-permute-start.44 = (f32[384,128]{1,0:T(8,128)S(1)}, f32[384,128]{1,0:T(8,128)S(1)}, u32[]{:S(2)}, u32[]{:S(2)}) collective-permute-start(f32[384,128]{1,0:T(8,128)S(1)} %get-tuple-element.102), channel_id=1, source_target_pairs={{0,1},{1,0},{2,3},{3,2},{4,5},{5,4},{6,7},{7,6},{8,9},{9,8},{10,11... | collective-permute-start | bytes 589832 | tf_op jit(solution)/shard_map/ppermute | solution.py:222
  94.7 11.9 %collective-permute-start.46 = (f32[512,128]{1,0:T(8,128)S(1)}, f32[512,128]{1,0:T(8,128)S(1)}, u32[]{:S(2)}, u32[]{:S(2)}) collective-permute-start(f32[512,128]{1,0:T(8,128)S(1)} %get-tuple-element.108), channel_id=1, source_target_pairs={{0,2},{1,3},{2,0},{3,1},{4,6},{5,7},{6,4},{7,5},{8,10},{9,11},{10,... | collective-permute-start | bytes 786440 | tf_op jit(solution)/shard_map/ppermute | solution.py:222
  96.5 10.1 %collective-permute-start.45 = (f32[3,128,128]{2,1,0:T(8,128)S(1)}, f32[3,128,128]{2,1,0:T(8,128)S(1)}, u32[]{:S(2)}, u32[]{:S(2)}) collective-permute-start(f32[3,128,128]{2,1,0:T(8,128)S(1)} %get-tuple-element.107), channel_id=1, source_target_pairs={{0,4},{1,5},{2,6},{3,7},{4,0},{5,1},{6,2},{7,3},{8,12},{9,13},{10,... | collective-permute-start | bytes 589832 | tf_op jit(solution)/shard_map/ppermute | solution.py:222
  99.5 5.4 %collective-permute-start.49 = (f32[128,128]{1,0:T(8,128)S(1)}, f32[128,128]{1,0:T(8,128)S(1)}, u32[]{:S(2)}, u32[]{:S(2)}) collective-permute-start(f32[128,128]{1,0:T(8,128)S(1)} %get-tuple-element.110), channel_id=1, source_target_pairs={{0,1},{1,0},{2,3},{3,2},{4,5},{5,4},{6,7},{7,6},{8,9},{9,8},{10,11... | collective-permute-start | bytes 196616 | tf_op jit(solution)/shard_map/ppermute | solution.py:222
  99.5 5.8 %collective-permute-start.50 = (f32[128,128]{1,0:T(8,128)S(1)}, f32[128,128]{1,0:T(8,128)S(1)}, u32[]{:S(2)}, u32[]{:S(2)}) collective-permute-start(f32[128,128]{1,0:T(8,128)S(1)} %get-tuple-element.111), channel_id=1, source_target_pairs={{0,1},{1,0},{2,3},{3,2},{4,5},{5,4},{6,7},{7,6},{8,9},{9,8},{10,11... | collective-permute-start | bytes 196616 | tf_op jit(solution)/shard_map/ppermute | solution.py:222
  100.0 1.2 collective-permute-start.47
  101.2 3.6 %collective-permute-start.48 = (f32[8,128]{1,0:T(8,128)S(1)}, f32[8,128]{1,0:T(8,128)S(1)}, u32[]{:S(2)}, u32[]{:S(2)}) collective-permute-start(f32[8,128]{1,0:T(8,128)S(1)} %add.7.tile_ref), channel_id=1, source_target_pairs={{0,2},{1,3},{2,0},{3,1},{4,6},{5,7},{6,4},{7,5},{8,10},{9,11},{10,... | collective-permute-start | bytes 12296 | tf_op jit(solution)/shard_map/ppermute | solution.py:222
  104.8 1.3 collective-permute-start.51
  104.8 1.4 %collective-permute-start.52 = (f32[128,128]{1,0:T(8,128)S(1)}, f32[128,128]{1,0:T(8,128)S(1)}, u32[]{:S(2)}, u32[]{:S(2)}) collective-permute-start(f32[128,128]{1,0:T(8,128)S(1)} %get-tuple-element.113), channel_id=1, source_target_pairs={{0,1},{1,0},{2,3},{3,2},{4,5},{5,4},{6,7},{7,6},{8,9},{9,8},{10,11... | collective-permute-start | bytes 196616 | tf_op jit(solution)/shard_map/ppermute | solution.py:222
  105.3 1.3 collective-permute-start.53
  107.2 9.4 %collective-permute-start.55 = (f32[264,128]{1,0:T(8,128)S(1)}, f32[264,128]{1,0:T(8,128)S(1)}, u32[]{:S(2)}, u32[]{:S(2)}) collective-permute-start(f32[264,128]{1,0:T(8,128)S(1)} %get-tuple-element.119), channel_id=1, source_target_pairs={{0,12},{1,13},{2,14},{3,15},{4,8},{5,9},{6,10},{7,11},{8,4},{9,5},... | collective-permute-start | bytes 405512 | tf_op jit(solution)/shard_map/ppermute | solution.py:222
  108.9 13.9 %collective-permute-start.56 = (f32[264,128]{1,0:T(8,128)S(1)}, f32[264,128]{1,0:T(8,128)S(1)}, u32[]{:S(2)}, u32[]{:S(2)}) collective-permute-start(f32[264,128]{1,0:T(8,128)S(1)} %get-tuple-element.120), channel_id=1, source_target_pairs={{0,8},{1,9},{2,10},{3,11},{4,12},{5,13},{6,14},{7,15},{8,0},{9,1},... | collective-permute-start | bytes 405512 | tf_op jit(solution)/shard_map/ppermute | solution.py:222
  110.5 12.3 %collective-permute-start.57 = (f32[264,128]{1,0:T(8,128)S(1)}, f32[264,128]{1,0:T(8,128)S(1)}, u32[]{:S(2)}, u32[]{:S(2)}) collective-permute-start(f32[264,128]{1,0:T(8,128)S(1)} %get-tuple-element.118.refs_0_), channel_id=1, source_target_pairs={{0,4},{1,5},{2,6},{3,7},{4,0},{5,1},{6,2},{7,3},{8,12},{9,13},{10,... | collective-permute-start | bytes 405512 | tf_op jit(solution)/shard_map/ppermute | solution.py:222
  111.7 5.0 %collective-permute-start.54 = (f32[2,128,128]{2,1,0:T(8,128)S(1)}, f32[2,128,128]{2,1,0:T(8,128)S(1)}, u32[]{:S(2)}, u32[]{:S(2)}) collective-permute-start(f32[2,128,128]{2,1,0:T(8,128)S(1)} %get-tuple-element.116), channel_id=1, source_target_pairs={{0,2},{1,3},{2,0},{3,1},{4,6},{5,7},{6,4},{7,5},{8,10},{9,11},{10,... | collective-permute-start | bytes 393224 | tf_op jit(solution)/shard_map/ppermute | solution.py:222

commit v4 on v3

v4 whole, which is shorter than its diff:
```python
import functools

import jax
import jax.numpy as jnp
from jax import lax
from jax.experimental import pallas as pl
from jax.experimental.pallas import tpu as pltpu
from jax.sharding import PartitionSpec as P

ITERS = 2
CORE, ROW, COLUMN = 1, 2, 4
SENDERS = 6
SMEM = pl.BlockSpec(memory_space=pltpu.SMEM)
VMEM = pl.BlockSpec(memory_space=pltpu.VMEM)


def params(mebibytes):
    return pltpu.CompilerParams(vmem_limit_bytes=mebibytes * 2**20)


def halves(x):
    high = x.astype(jnp.bfloat16)
    return high, (x - high.astype(jnp.float32)).astype(jnp.bfloat16)


def tile_sum(x):
    return jnp.sum(x.reshape(-1, 8, x.shape[-1]), axis=0)


def prep_kernel(n, spare, me_ref, fetch_in, store_in, pairs_in, live_in, vector_in, left_in, right_in, l4_ref, rr_ref,
                pick_ref, mine_ref, place_ref, first_ref, second_ref, dst_ref, one_ref, two_ref, count_ref, vector_ref,
                seen_ref, fetch_ref, store_ref, pairs_ref, live_ref, left_ref, right_ref, sems):
    copies = [pltpu.make_async_copy(source, target, sems.at[i]) for i, (source, target) in enumerate((
        (fetch_in, fetch_ref), (store_in, store_ref), (pairs_in, pairs_ref), (live_in, live_ref),
        (left_in, left_ref), (right_in, right_ref), (vector_in, vector_ref)))]
    for copy in copies:
        copy.start()
    me = me_ref[0]
    terms = left_ref.shape[0]
    width = left_ref.shape[1]
    zero = terms * n
    npairs = pairs_ref.shape[0] // 3

    def clear(cell, carry):
        first_ref[cell] = zero
        second_ref[cell] = zero
        seen_ref[cell] = 0
        return carry

    lax.fori_loop(0, terms * n, clear, 0, unroll=8)
    for copy in copies[:4]:
        copy.wait()

    def relative(r, carry):
        device = lax.bitwise_xor(me, r)
        pick_ref[r] = fetch_ref[device, me]
        mine_ref[r] = store_ref[me, device]
        return carry

    lax.fori_loop(0, n, relative, 0)

    def chip(g, carry):
        for q in range(SENDERS):
            place_ref[q * (n // 2) + g] = store_ref[lax.bitwise_xor(me, q), lax.bitwise_xor(me, 2 * g)]
        return carry

    lax.fori_loop(0, n // 2, chip, 0)

    def pair(p, carry):
        extra, ops = carry
        a = lax.bitwise_xor(pairs_ref[p], me)
        j = pairs_ref[npairs + p]
        o = lax.bitwise_xor(pairs_ref[2 * npairs + p], me)
        cell = j * n + o
        source = a * terms + j
        seen = seen_ref[cell]
        seen_ref[cell] = seen + 1
        before = second_ref[cell]
        place = jnp.where(seen == 2, spare + extra, before)
        first_ref[cell] = jnp.where(seen == 0, source, first_ref[cell])
        second_ref[cell] = jnp.where(seen == 0, before, jnp.where(seen == 1, source, place))
        dst_ref[ops] = place
        one_ref[ops] = before
        two_ref[ops] = source
        return extra + (seen == 2).astype(jnp.int32), ops + (seen >= 2).astype(jnp.int32)

    _, ops = lax.fori_loop(0, live_ref[0], pair, (jnp.int32(0), jnp.int32(0)))
    count_ref[0] = ops
    for copy in copies[4:]:
        copy.wait()

    for j in range(terms):
        high, low = halves(left_ref[j])
        for k, part in enumerate((high, low, high, low)):
            l4_ref[j, :, k * width:(k + 1) * width] = part
        high, low = halves(right_ref[j])
        for k in range(2):
            row = (k * terms + j) * width
            rr_ref[row:row + width, :width] = high
            rr_ref[row:row + width, width:] = low


def at_home(x):
    return pltpu.with_memory_space_constraint(x, pltpu.HBM)


def prep(n, me, fetch, store, pairs, live, vector, left_ops, right_ops):
    terms, width = left_ops.shape[:2]
    npairs = pairs.shape[0] // 3
    table = jax.ShapeDtypeStruct((terms * n,), jnp.int32)
    listed = jax.ShapeDtypeStruct((npairs,), jnp.int32)
    relative = jax.ShapeDtypeStruct((n,), jnp.int32)
    return pl.pallas_call(
        functools.partial(prep_kernel, n, terms * n + 1),
        out_shape=(
            jax.ShapeDtypeStruct((terms, width, 4 * width), jnp.bfloat16),
            jax.ShapeDtypeStruct((2 * terms * width, 2 * width), jnp.bfloat16),
            relative, relative, jax.ShapeDtypeStruct((SENDERS * n // 2,), jnp.int32), table, table, listed, listed, listed,
            jax.ShapeDtypeStruct((1,), jnp.int32),
            jax.ShapeDtypeStruct(vector.shape, jnp.float32),
        ),
        in_specs=[SMEM] + [pl.BlockSpec(memory_space=pltpu.HBM)] * 7,
        out_specs=[VMEM] * 2 + [SMEM] * 9 + [VMEM],
        scratch_shapes=[
            pltpu.SMEM((terms * n,), jnp.int32),
            pltpu.SMEM(fetch.shape, jnp.int32),
            pltpu.SMEM(store.shape, jnp.int32),
            pltpu.SMEM(pairs.shape, jnp.int32),
            pltpu.SMEM((1,), jnp.int32),
            pltpu.VMEM(left_ops.shape, jnp.float32),
            pltpu.VMEM(left_ops.shape, jnp.float32),
            pltpu.SemaphoreType.DMA((7,)),
        ],
        compiler_params=params(16),
        name="prep",
    )(me, at_home(fetch), at_home(store), at_home(pairs), live, at_home(vector), at_home(left_ops), at_home(right_ops))


def apply_kernel(n, over_rows, rows, start, pick_ref, mine_ref, first_ref, second_ref, dst_ref, one_ref, two_ref, count_ref,
                 l4_ref, rr_ref, *refs):
    pieces, (near_ref, far_ref, row_ref, row_far_ref, column_ref, column_far_ref, square_ref, block, total) = refs[:n], refs[n:]
    terms, width = l4_ref.shape[:2]
    square = jnp.zeros((8, width), jnp.float32)
    product = jnp.zeros((8, width), jnp.float32)
    block[terms * n] = jnp.zeros((rows, width), jnp.float32)
    left = l4_ref[:, start:start + rows, :].reshape(terms * rows, 4 * width)
    for c in range(n // 2):
        columns = []
        for r in (2 * c, 2 * c + 1):
            high, low = halves(pieces[r][pick_ref[r]])
            columns.append(jnp.concatenate([high, high, low, low], axis=0))
            held = pieces[r][:, start:start + rows, :]
            square = square + tile_sum(held * held)
        both = jnp.dot(left, jnp.concatenate(columns, axis=1), preferred_element_type=jnp.float32)
        for k in range(2):
            at = (2 * c + k) * terms
            block[at:at + terms] = both[:, k * width:(k + 1) * width].reshape(terms, rows, width)
    square_ref[...] = square

    def add(i, carry):
        block[dst_ref[i]] = block[one_ref[i]] + block[two_ref[i]]
        return carry

    lax.fori_loop(0, count_ref[0], add, 0)
    late = 0
    for low_end in range(0, n, 4):
        for r in range(low_end, low_end + 4):
            for j in range(terms):
                at = j * n + r
                high, low = halves(block[first_ref[at]] + block[second_ref[at]])
                total[r, :, j * width:(j + 1) * width] = high
                total[r, :, (terms + j) * width:(terms + j + 1) * width] = low
        both = jnp.dot(total[low_end:low_end + 4].reshape(4 * rows, 2 * terms * width), rr_ref[...],
                       preferred_element_type=jnp.float32)
        slots = both[:, :width] + both[:, width:]
        for r in range(low_end, low_end + 4):
            slot = slots[(r - low_end) * rows:(r - low_end + 1) * rows]
            product = product + tile_sum(pieces[r][mine_ref[r], start:start + rows, :] * slot)
            g, core = divmod(r, 2)
            if g == 3:
                (column_far_ref if core else column_ref)[...] = slot
            elif g in over_rows:
                at = over_rows.index(g) * rows
                (row_far_ref if core else row_ref)[at:at + rows, :] = slot
            else:
                (far_ref if core else near_ref)[late * rows:(late + 1) * rows, :] = slot
                late += core
    for ref in (far_ref, row_ref, row_far_ref):
        ref[ref.shape[0] - 8:, :] = product


def apply(n, over_rows, rows, start, tables, pieces):
    terms, width = tables[0].shape[:2]
    spare = tables[7].shape[0] // 3
    late = n // 2 - 1 - len(over_rows)
    shape = lambda *dims: jax.ShapeDtypeStruct(dims, jnp.float32)
    return pl.pallas_call(
        functools.partial(apply_kernel, n, over_rows, rows, start),
        out_shape=(shape(late * rows, width), shape(late * rows + 8, width)) + (shape(len(over_rows) * rows + 8, width),) * 2
        + (shape(rows, width),) * 2 + (shape(8, width),),
        in_specs=[SMEM] * 8 + [VMEM] * (2 + n),
        out_specs=[VMEM] * 7,
        scratch_shapes=[
            pltpu.VMEM((terms * n + 1 + spare, rows, width), jnp.float32),
            pltpu.VMEM((n, rows, 2 * terms * width), jnp.bfloat16),
        ],
        compiler_params=params(32 if n <= 16 else 56),
        name="apply",
    )(*tables[2:4], *tables[5:], *tables[:2], *pieces)


def joined(parts, count):
    if len(parts) == 1:
        return parts[0]
    height, width = parts[0].shape
    end = height // (8 * count) * 8 * count
    whole = jnp.concatenate([x[:end].reshape(count, -1, width) for x in parts], axis=1).reshape(-1, width)
    return whole if end == height else jnp.concatenate([whole, sum(x[end:] for x in parts)])


def swapped(x, k):
    n = lax.axis_size("term")
    return lax.ppermute(x, "term", [(i, i ^ k) for i in range(n)])


def local(kernel, name, out_shape, scalars, arrays):
    many = isinstance(out_shape, tuple)
    return pl.pallas_call(
        kernel,
        out_shape=out_shape,
        in_specs=[SMEM] * len(scalars) + [VMEM] * len(arrays),
        out_specs=[VMEM] * len(out_shape) if many else VMEM,
        compiler_params=params(16),
        name=name,
    )(*scalars, *arrays)


def fold_kernel(late, over_rows, place_ref, near_ref, far_in, far_ref, row_ref, row_far_ref, column_ref, column_far_ref,
                own_ref, step_ref, *send_refs):
    width = near_ref.shape[1]
    chips = place_ref.shape[0] // SENDERS
    end = len(late) * width
    over = len(over_rows) * width
    tile = far_in[end:] + far_ref[end:] + row_ref[over:] + row_far_ref[over:]
    for i, g in enumerate(late):
        come = [(0, near_ref, i), (1, far_ref, i)]
        if g == 1:
            come += [(4, column_ref, 0), (5, column_far_ref, 0)]
        if g + 1 in over_rows:
            come += [(2, row_ref, over_rows.index(g + 1)), (3, row_far_ref, over_rows.index(g + 1))]
        for b in range(2):
            block = sum(ref[at * width:(at + 1) * width] * (place_ref[q * chips + g] == b).astype(jnp.float32)
                        for q, ref, at in come)
            if g == 0:
                own_ref[b] = block
            elif g == 1:
                step_ref[b] = block
            else:
                send_refs[g // 2 - 1][b * width:(b + 1) * width] = block
    for send_ref in send_refs:
        send_ref[2 * width:] = tile


def landed(own_ref, step_ref, refs):
    width = own_ref.shape[2]
    sent, came = refs[0], refs[1:]
    tile = sent[2 * width:]
    for ref in came:
        tile = tile + ref[2 * width:]
    sums = []
    for b in range(2):
        total = own_ref[b] + step_ref[b]
        for ref in came:
            total = total + ref[b * width:(b + 1) * width]
        sums.append(total)
    return sums, jnp.sum(tile)


def step_kernel(own_ref, step_ref, square_ref, vector_ref, precond_ref, *refs):
    out_ref = refs[-1]
    sigma, product = landed(own_ref, step_ref, refs[:-1])
    theta = product / jnp.sum(square_ref[...])
    for b in range(2):
        v = vector_ref[b]
        out_ref[b] = v - precond_ref[b] * (sigma[b] - theta * v)


def last_kernel(cells, own_ref, step_ref, square_ref, vector_ref, precond_ref, *refs):
    residual_ref, out_ref, tile_ref = refs[-3:]
    sigma, product = landed(own_ref, step_ref, refs[:-3])
    square = jnp.sum(square_ref[...])
    theta = product / square
    scale = 1.0 / jnp.sqrt(square / cells + 1e-06)
    tile = jnp.zeros(tile_ref.shape, jnp.float32)
    for b in range(2):
        v = vector_ref[b]
        residual = (sigma[b] - theta * v) * scale
        residual_ref[b] = residual
        corrected = v * scale - precond_ref[b] * residual
        out_ref[b] = corrected
        tile = tile + tile_sum(corrected * corrected)
    tile_ref[...] = tile


def norm_kernel(cells, corrected_ref, tiles_ref, out_ref):
    scale = 1.0 / jnp.sqrt(jnp.sum(jnp.sum(tiles_ref[...], axis=0)) / cells + 1e-06)
    out_ref[...] = corrected_ref[...] * scale


def scattered(n, tables, pieces):
    width = pieces[0].shape[1]
    chips = n // 2
    rows = width if n <= 16 else width // 4
    over_rows = list(range(chips - 1, 3, -2))
    late = [g for g in range(chips) if g != 3 and g not in over_rows]
    shape = lambda *dims: jax.ShapeDtypeStruct(dims, jnp.float32)
    runs = [apply(n, over_rows, rows, start, tables, pieces) for start in range(0, width, rows)]
    counts = (len(late), len(late), len(over_rows), len(over_rows), 1, 1)
    near, far, row, row_far, column, column_far = (joined([x[i] for x in runs], k) for i, k in enumerate(counts))
    square = functools.reduce(jnp.add, [x[6] for x in runs])
    own, step, *sends = local(
        functools.partial(fold_kernel, late, over_rows), "fold",
        (shape(2, width, width),) * 2 + (shape(2 * width + 8, width),) * (chips // 2 - 1), tables[4:5],
        (near, far, swapped(far, CORE), swapped(row, ROW), swapped(row_far, ROW + CORE), swapped(column, COLUMN),
         swapped(column_far, COLUMN + CORE)))
    came = [swapped(x, 2 * ROW * (i + 1)) for i, x in reversed(list(enumerate(sends)))]
    return square, (own, swapped(step, ROW)), [sends[0], *came]


def gathered(n, x, held=None):
    pieces = {0: x}
    for k in reversed(range(8, n, 4)):
        pieces[k] = swapped(x, k)
    pieces[ROW] = swapped(x, ROW)
    pieces[COLUMN] = swapped(x, COLUMN)
    if held is not None:
        pieces[n - 4], pieces[0] = lax.optimization_barrier((pieces[n - 4], held))
    for k in reversed(range(8, n, 4)):
        pieces[k + ROW] = swapped(pieces[k], ROW)
    pieces[COLUMN + ROW] = swapped(pieces[ROW], COLUMN)
    for k in range(0, n, 2):
        pieces[k + CORE] = swapped(pieces[k], CORE)
    return [pieces[k] for k in range(n)]


def shards(wavefn, left_ops, right_ops, precond, fetch_map, store_map, pair_list, live_count):
    n = lax.axis_size("term")
    me = lax.axis_index("term").astype(jnp.int32).reshape(1)
    width = wavefn.shape[1]
    cells = wavefn.size * n
    *tables, held = prep(n, me, fetch_map, store_map, pair_list[0].T.reshape(-1), live_count, wavefn, left_ops, right_ops)
    block = jax.ShapeDtypeStruct(wavefn.shape, jnp.float32)
    tile = jax.ShapeDtypeStruct((8, width), jnp.float32)
    vector = wavefn
    for iteration in range(ITERS):
        pieces = gathered(n, vector, held if iteration == 0 else None)
        vector = pieces[0]
        square, sums, parts = scattered(n, tables, pieces)
        arrays = (*sums, square, vector, precond, *parts)
        if iteration < ITERS - 1:
            vector = local(step_kernel, "step", block, (), arrays)
    residual, corrected, partial = local(
        functools.partial(last_kernel, cells), "last", (block, block, tile), (), arrays)
    tiles = lax.all_to_all(jnp.broadcast_to(partial[None], (n, 8, width)), "term",
                           split_axis=0, concat_axis=0, tiled=True)
    return local(functools.partial(norm_kernel, cells), "norm", block, (), (corrected, tiles)), residual


def solution(mesh):
    field = P(("group", "term"), None, None)
    return jax.shard_map(
        shards,
        mesh=mesh,
        in_specs=(field, field, field, field, P(), P(), P("term", None, None), P("term")),
        out_specs=(field, field),
        check_vma=False,
    )
```

time: 134 us -> 121 us (0.903)
  waiting for transfers between devices: 56.6 us -> 51.1 us
  local copies, waits for them, and re-layouts: 5.17 us -> 0.6 us
  Pallas kernels: 25.1 us -> 21 us
    ppermute x58 -> x48, waiting for transfers between devices: 56.6 us -> 51.1 us  [swapped(): return lax.ppermute(x, 'term', [(i, i ^ k) for i in range(n)])]
    unnamed x13 -> x5, local copies, waits for them, and re-layouts: 5.17 us -> 0.6 us
    pallas_call x4 -> x2, Pallas kernels: 16.8 us -> 13.5 us  [apply(): pl.pallas_call(functools.partial(apply_kernel, n, over_rows, rows, start)...]
    pallas_call x7 -> x5, Pallas kernels: 4.43 us -> 3.35 us  [local(): pl.pallas_call(kernel, out_shape=out_shape, in_specs=[SMEM] * len(scalars...]
    ppermute x58 -> x48, starting transfers between devices: 36.2 us -> 35.7 us  [swapped(): return lax.ppermute(x, 'term', [(i, i ^ k) for i in range(n)])]
  transfers between devices with their start and end apart: 58 -> 48, of which waited for: 27 -> 24; matrix products, arithmetic and copies ran while one was open for 1% -> 0% of each run, Pallas kernels for 7% -> 3%
where the time goes in v4:
time: 121 us
  waiting for transfers between devices  51.1 us (42%)
  starting transfers between devices  35.7 us (30%)
  Pallas kernels  21 us (17%)
  blocking collectives  10.8 us (9%)
  between operations  1.41 us (1%)
    ppermute x48, waiting for transfers between devices, swapped(): return lax.ppermute(x, 'term', [(i, i ^ k) for i in range(n)])  51.1 us
    ppermute x48, starting transfers between devices, swapped(): return lax.ppermute(x, 'term', [(i, i ^ k) for i in range(n)])  35.7 us
    pallas_call x2, Pallas kernels, apply(): pl.pallas_call(functools.partial(apply_kernel, n, over_rows, rows, start)...  13.5 us
    all_to_all x1, blocking collectives, shards(): lax.all_to_all(jnp.broadcast_to(partial[None], (n, 8, width)), 'term', sp...  10.8 us
    pallas_call x1, Pallas kernels, prep(): pl.pallas_call(functools.partial(prep_kernel, n, terms * n + 1), out_shap...  4.19 us
    pallas_call x5, Pallas kernels, local(): pl.pallas_call(kernel, out_shape=out_shape, in_specs=[SMEM] * len(scalars...  3.35 us
  transfers between devices with their start and end apart: 48, of which 24 were waited for; matrix products, arithmetic and copies ran while one was open for 0% of the time, Pallas kernels for 3%

profile of v4, /device:TPU:0, one launch (start us, length us, event | category | flops | bytes accessed | tf_op | source)
XLA Modules:
  0.0 120.7 jit_solution(15839778159828049666)
XLA Ops:
  0.6 3.0 %collective-permute-start.2 = (f32[2,128,128]{2,1,0:T(8,128)}, f32[2,128,128]{2,1,0:T(8,128)S(1)}, u32[]{:S(2)}, u32[]{:S(2)}) collective-permute-start(f32[2,128,128]{2,1,0:T(8,128)} %vector_in.1), channel_id=1, source_target_pairs={{0,2},{1,3},{2,0},{3,1},{4,6},{5,7},{6,4},{7,5},{8,10},{9,11},{10,... | collective-permute-start | bytes 393224 | tf_op jit(solution)/shard_map/ppermute | solution.py:223
  3.7 2.6 %collective-permute-start.8 = (f32[2,128,128]{2,1,0:T(8,128)}, f32[2,128,128]{2,1,0:T(8,128)S(1)}, u32[]{:S(2)}, u32[]{:S(2)}) collective-permute-start(f32[2,128,128]{2,1,0:T(8,128)} %vector_in.1), channel_id=1, source_target_pairs={{0,8},{1,9},{2,10},{3,11},{4,12},{5,13},{6,14},{7,15},{8,0},{9,1},... | collective-permute-start | bytes 393224 | tf_op jit(solution)/shard_map/ppermute | solution.py:223
  6.3 1.3 %collective-permute-start = (f32[2,128,128]{2,1,0:T(8,128)}, f32[2,128,128]{2,1,0:T(8,128)S(1)}, u32[]{:S(2)}, u32[]{:S(2)}) collective-permute-start(f32[2,128,128]{2,1,0:T(8,128)} %vector_in.1), channel_id=1, source_target_pairs={{0,12},{1,13},{2,14},{3,15},{4,8},{5,9},{6,10},{7,11},{8,4},{9,5},... | collective-permute-start | bytes 393224 | tf_op jit(solution)/shard_map/ppermute | solution.py:223
  7.6 0.2 collective-permute-start.4
  7.8 1.8 %collective-permute-start.6 = (f32[2,128,128]{2,1,0:T(8,128)S(1)}, f32[2,128,128]{2,1,0:T(8,128)S(1)}, u32[]{:S(2)}, u32[]{:S(2)}) collective-permute-start(f32[2,128,128]{2,1,0:T(8,128)S(1)} %collective-permute-done.2.refs_2_), channel_id=1, source_target_pairs={{0,4},{1,5},{2,6},{3,7},{4,0},{5,1},{6,2},{7,3},{8,12},{9,13},{10,... | collective-permute-start | bytes 393224 | tf_op jit(solution)/shard_map/ppermute | solution.py:223
  10.3 0.6 copy.12
  10.9 4.2 %prep.1 = (bf16[8,128,512]{2,1,0:T(8,128)(2,1)S(1)}, bf16[2048,256]{1,0:T(8,128)(2,1)S(1)}, s32[16]{0:T(128)S(1)}, s32[16]{0:T(128)S(1)}, s32[48]{0:T(128)S(1)},...) custom-call(s32[1]{0:T(128)} %bitcast.me_ref, ...), custom_call_target="tpu_custom_call" | custom-call | tf_op jit(solution)/shard_map/prep/pallas_call | solution.py:113
  15.2 1.4 %collective-permute-done.8.refs_8_ = f32[2,128,128]{2,1,0:T(8,128)S(1)} collective-permute-done((f32[2,128,128]{2,1,0:T(8,128)}, f32[2,128,128]{2,1,0:T(8,128)S(1)}, u32[]{:S(2)}, u32[]{:S(2)}) %collective-permute-start.8) | collective-permute-done | bytes 131104 | tf_op jit(solution)/shard_map/ppermute | solution.py:223
  16.5 0.4 collective-permute-start.10
  17.0 1.1 collective-permute-done.4.refs_4_
  18.1 1.4 %collective-permute-done.6.refs_6_ = f32[2,128,128]{2,1,0:T(8,128)S(1)} collective-permute-done((f32[2,128,128]{2,1,0:T(8,128)S(1)}, f32[2,128,128]{2,1,0:T(8,128)S(1)}, u32[]{:S(2)}, u32[]{:S(2)}) %collective-permute-start.6) | collective-permute-done | bytes 131104 | tf_op jit(solution)/shard_map/ppermute | solution.py:223
  19.5 0.5 collective-permute-start.13
  20.0 1.8 %collective-permute-done.10.refs_10_ = f32[2,128,128]{2,1,0:T(8,128)S(1)} collective-permute-done((f32[2,128,128]{2,1,0:T(8,128)S(1)}, f32[2,128,128]{2,1,0:T(8,128)S(1)}, u32[]{:S(2)}, u32[]{:S(2)}) %collective-permute-start.10) | collective-permute-done | bytes 131104 | tf_op jit(solution)/shard_map/ppermute | solution.py:223
  21.8 0.5 collective-permute-start.7
  22.3 2.1 %collective-permute-done.13.refs_14_ = f32[2,128,128]{2,1,0:T(8,128)S(1)} collective-permute-done((f32[2,128,128]{2,1,0:T(8,128)S(1)}, f32[2,128,128]{2,1,0:T(8,128)S(1)}, u32[]{:S(2)}, u32[]{:S(2)}) %collective-permute-start.13) | collective-permute-done | bytes 131104 | tf_op jit(solution)/shard_map/ppermute | solution.py:223
  24.5 1.3 %collective-permute-done.14.refs_15_ = f32[2,128,128]{2,1,0:T(8,128)S(1)} collective-permute-done((f32[2,128,128]{2,1,0:T(8,128)S(1)}, f32[2,128,128]{2,1,0:T(8,128)S(1)}, u32[]{:S(2)}, u32[]{:S(2)}) %collective-permute-start.14) | collective-permute-done | bytes 131104 | tf_op jit(solution)/shard_map/ppermute | solution.py:223
  25.8 6.6 %apply.2 = (f32[640,128]{1,0:T(8,128)S(1)}, f32[648,128]{1,0:T(8,128)S(1)}, f32[264,128]{1,0:T(8,128)S(1)}, f32[264,128]{1,0:T(8,128)S(1)}, f32[128,128]{1,0:T(8...) custom-call(s32[16]{0:T(128)S(1)} %get-tuple-element.44.pick_ref, s32[16]{0:T(128)S(1)} %get-tuple-element.45.mine_ref, ...), custom_call_target="tpu_custom_call" | custom-call | tf_op jit(solution)/shard_map/apply/pallas_call | solution.py:197
  32.6 0.5 collective-permute-start.16
  33.1 1.3 %collective-permute-start.17 = (f32[264,128]{1,0:T(8,128)S(1)}, f32[264,128]{1,0:T(8,128)S(1)}, u32[]{:S(2)}, u32[]{:S(2)}) collective-permute-start(f32[264,128]{1,0:T(8,128)S(1)} %get-tuple-element.60), channel_id=1, source_target_pairs={{0,3},{1,2},{2,1},{3,0},{4,7},{5,6},{6,5},{7,4},{8,11},{9,10},{10,... | collective-permute-start | bytes 405512 | tf_op jit(solution)/shard_map/ppermute | solution.py:223
  34.4 0.4 collective-permute-start.18
  34.8 1.3 %collective-permute-start.19 = (f32[128,128]{1,0:T(8,128)S(1)}, f32[128,128]{1,0:T(8,128)S(1)}, u32[]{:S(2)}, u32[]{:S(2)}) collective-permute-start(f32[128,128]{1,0:T(8,128)S(1)} %get-tuple-element.62), channel_id=1, source_target_pairs={{0,5},{1,4},{2,7},{3,6},{4,1},{5,0},{6,3},{7,2},{8,13},{9,12},{10,... | collective-permute-start | bytes 196616 | tf_op jit(solution)/shard_map/ppermute | solution.py:223
  36.1 3.2 %collective-permute-done.18.column_ref = f32[128,128]{1,0:T(8,128)S(1)} collective-permute-done((f32[128,128]{1,0:T(8,128)S(1)}, f32[128,128]{1,0:T(8,128)S(1)}, u32[]{:S(2)}, u32[]{:S(2)}) %collective-permute-start.18) | collective-permute-done | bytes 65568 | tf_op jit(solution)/shard_map/ppermute | solution.py:223
  39.3 0.3 collective-permute-done.19.column_far_ref
  39.6 1.4 %collective-permute-done.17.row_far_ref = f32[264,128]{1,0:T(8,128)S(1)} collective-permute-done((f32[264,128]{1,0:T(8,128)S(1)}, f32[264,128]{1,0:T(8,128)S(1)}, u32[]{:S(2)}, u32[]{:S(2)}) %collective-permute-start.17) | collective-permute-done | bytes 135200 | tf_op jit(solution)/shard_map/ppermute | solution.py:223
  41.0 0.7 fold.2
  41.7 3.3 %collective-permute-start.21 = (f32[264,128]{1,0:T(8,128)S(1)}, f32[264,128]{1,0:T(8,128)S(1)}, u32[]{:S(2)}, u32[]{:S(2)}) collective-permute-start(f32[264,128]{1,0:T(8,128)S(1)} %get-tuple-element.67), channel_id=1, source_target_pairs={{0,12},{1,13},{2,14},{3,15},{4,8},{5,9},{6,10},{7,11},{8,4},{9,5},... | collective-permute-start | bytes 405512 | tf_op jit(solution)/shard_map/ppermute | solution.py:223
  45.0 1.2 collective-permute-start.23
  46.2 0.5 collective-permute-start.20
  46.7 4.5 %collective-permute-done.20.step_ref = f32[2,128,128]{2,1,0:T(8,128)S(1)} collective-permute-done((f32[2,128,128]{2,1,0:T(8,128)S(1)}, f32[2,128,128]{2,1,0:T(8,128)S(1)}, u32[]{:S(2)}, u32[]{:S(2)}) %collective-permute-start.20) | collective-permute-done | bytes 131104 | tf_op jit(solution)/shard_map/ppermute | solution.py:223
  51.1 5.6 %collective-permute-done.22.refs_2_ = f32[264,128]{1,0:T(8,128)S(1)} collective-permute-done((f32[264,128]{1,0:T(8,128)S(1)}, f32[264,128]{1,0:T(8,128)S(1)}, u32[]{:S(2)}, u32[]{:S(2)}) %collective-permute-start.22) | collective-permute-done | bytes 135200 | tf_op jit(solution)/shard_map/ppermute | solution.py:223
  56.8 0.2 step.1.refs_0_.vector_ref
  57.0 2.7 %collective-permute-start.35 = (f32[2,128,128]{2,1,0:T(8,128)S(1)}, f32[2,128,128]{2,1,0:T(8,128)S(1)}, u32[]{:S(2)}, u32[]{:S(2)}) collective-permute-start(f32[2,128,128]{2,1,0:T(8,128)S(1)} %step.1.refs_0_.vector_ref), channel_id=1, source_target_pairs={{0,12},{1,13},{2,14},{3,15},{4,8},{5,9},{6,10},{7,11},{8,4},{9,5},... | collective-permute-start | bytes 393224 | tf_op jit(solution)/shard_map/ppermute | solution.py:223
  59.7 1.7 %collective-permute-start.27 = (f32[2,128,128]{2,1,0:T(8,128)S(1)}, f32[2,128,128]{2,1,0:T(8,128)S(1)}, u32[]{:S(2)}, u32[]{:S(2)}) collective-permute-start(f32[2,128,128]{2,1,0:T(8,128)S(1)} %step.1.refs_0_.vector_ref), channel_id=1, source_target_pairs={{0,4},{1,5},{2,6},{3,7},{4,0},{5,1},{6,2},{7,3},{8,12},{9,13},{10,... | collective-permute-start | bytes 393224 | tf_op jit(solution)/shard_map/ppermute | solution.py:223
  61.4 0.4 collective-permute-start.25
  61.8 3.5 %collective-permute-done.35.refs_12_ = f32[2,128,128]{2,1,0:T(8,128)S(1)} collective-permute-done((f32[2,128,128]{2,1,0:T(8,128)S(1)}, f32[2,128,128]{2,1,0:T(8,128)S(1)}, u32[]{:S(2)}, u32[]{:S(2)}) %collective-permute-start.35) | collective-permute-done | bytes 131104 | tf_op jit(solution)/shard_map/ppermute | solution.py:223
  65.3 0.4 collective-permute-start.37
  65.6 4.3 %collective-permute-done.31.refs_8_ = f32[2,128,128]{2,1,0:T(8,128)S(1)} collective-permute-done((f32[2,128,128]{2,1,0:T(8,128)S(1)}, f32[2,128,128]{2,1,0:T(8,128)S(1)}, u32[]{:S(2)}, u32[]{:S(2)}) %collective-permute-start.31) | collective-permute-done | bytes 131104 | tf_op jit(solution)/shard_map/ppermute | solution.py:223
  70.0 0.6 collective-permute-start.33
  70.6 0.2 collective-permute-start.32
  70.9 0.3 collective-permute-start.26
  71.2 0.1 collective-permute-done.36.refs_13_
  71.3 0.1 collective-permute-start.28
  71.5 4.4 %collective-permute-done.33.refs_10_ = f32[2,128,128]{2,1,0:T(8,128)S(1)} collective-permute-done((f32[2,128,128]{2,1,0:T(8,128)S(1)}, f32[2,128,128]{2,1,0:T(8,128)S(1)}, u32[]{:S(2)}, u32[]{:S(2)}) %collective-permute-start.33) | collective-permute-done | bytes 131104 | tf_op jit(solution)/shard_map/ppermute | solution.py:223
  75.9 0.5 collective-permute-start.34
  76.5 0.7 collective-permute-done.38.refs_15_
  77.2 0.2 collective-permute-done.34.refs_11_
  77.4 0.4 collective-permute-done.30.refs_7_
  77.9 6.8 %apply.3 = (f32[640,128]{1,0:T(8,128)S(1)}, f32[648,128]{1,0:T(8,128)S(1)}, f32[264,128]{1,0:T(8,128)S(1)}, f32[264,128]{1,0:T(8,128)S(1)}, f32[128,128]{1,0:T(8...) custom-call(s32[16]{0:T(128)S(1)} %get-tuple-element.44.pick_ref, s32[16]{0:T(128)S(1)} %get-tuple-element.45.mine_ref, ...), custom_call_target="tpu_custom_call" | custom-call | tf_op jit(solution)/shard_map/apply/pallas_call | solution.py:197
  84.8 1.5 %collective-permute-start.40 = (f32[264,128]{1,0:T(8,128)S(1)}, f32[264,128]{1,0:T(8,128)S(1)}, u32[]{:S(2)}, u32[]{:S(2)}) collective-permute-start(f32[264,128]{1,0:T(8,128)S(1)} %get-tuple-element.71), channel_id=1, source_target_pairs={{0,2},{1,3},{2,0},{3,1},{4,6},{5,7},{6,4},{7,5},{8,10},{9,11},{10,... | collective-permute-start | bytes 405512 | tf_op jit(solution)/shard_map/ppermute | solution.py:223
  86.3 0.4 collective-permute-start.41
  86.6 0.3 collective-permute-start.42
  86.9 1.4 %collective-permute-start.43 = (f32[128,128]{1,0:T(8,128)S(1)}, f32[128,128]{1,0:T(8,128)S(1)}, u32[]{:S(2)}, u32[]{:S(2)}) collective-permute-start(f32[128,128]{1,0:T(8,128)S(1)} %get-tuple-element.74), channel_id=1, source_target_pairs={{0,5},{1,4},{2,7},{3,6},{4,1},{5,0},{6,3},{7,2},{8,13},{9,12},{10,... | collective-permute-start | bytes 196616 | tf_op jit(solution)/shard_map/ppermute | solution.py:223
  88.3 3.2 %collective-permute-done.42.column_ref = f32[128,128]{1,0:T(8,128)S(1)} collective-permute-done((f32[128,128]{1,0:T(8,128)S(1)}, f32[128,128]{1,0:T(8,128)S(1)}, u32[]{:S(2)}, u32[]{:S(2)}) %collective-permute-start.42) | collective-permute-done | bytes 65568 | tf_op jit(solution)/shard_map/ppermute | solution.py:223
  91.5 0.3 collective-permute-done.43.column_far_ref
  91.8 1.4 %collective-permute-done.41.row_far_ref = f32[264,128]{1,0:T(8,128)S(1)} collective-permute-done((f32[264,128]{1,0:T(8,128)S(1)}, f32[264,128]{1,0:T(8,128)S(1)}, u32[]{:S(2)}, u32[]{:S(2)}) %collective-permute-start.41) | collective-permute-done | bytes 135200 | tf_op jit(solution)/shard_map/ppermute | solution.py:223
  93.2 0.7 fold.3
  93.9 1.8 %collective-permute-start.45 = (f32[264,128]{1,0:T(8,128)S(1)}, f32[264,128]{1,0:T(8,128)S(1)}, u32[]{:S(2)}, u32[]{:S(2)}) collective-permute-start(f32[264,128]{1,0:T(8,128)S(1)} %get-tuple-element.79), channel_id=1, source_target_pairs={{0,12},{1,13},{2,14},{3,15},{4,8},{5,9},{6,10},{7,11},{8,4},{9,5},... | collective-permute-start | bytes 405512 | tf_op jit(solution)/shard_map/ppermute | solution.py:223
  95.7 2.6 %collective-permute-start.47 = (f32[264,128]{1,0:T(8,128)S(1)}, f32[264,128]{1,0:T(8,128)S(1)}, u32[]{:S(2)}, u32[]{:S(2)}) collective-permute-start(f32[264,128]{1,0:T(8,128)S(1)} %get-tuple-element.78.refs_0_), channel_id=1, source_target_pairs={{0,4},{1,5},{2,6},{3,7},{4,0},{5,1},{6,2},{7,3},{8,12},{9,13},{10,... | collective-permute-start | bytes 405512 | tf_op jit(solution)/shard_map/ppermute | solution.py:223
  98.4 1.4 %collective-permute-start.44 = (f32[2,128,128]{2,1,0:T(8,128)S(1)}, f32[2,128,128]{2,1,0:T(8,128)S(1)}, u32[]{:S(2)}, u32[]{:S(2)}) collective-permute-start(f32[2,128,128]{2,1,0:T(8,128)S(1)} %get-tuple-element.76), channel_id=1, source_target_pairs={{0,2},{1,3},{2,0},{3,1},{4,6},{5,7},{6,4},{7,5},{8,10},{9,11},{10,... | collective-permute-start | bytes 393224 | tf_op jit(solution)/shard_map/ppermute | solution.py:223
  99.8 3.5 %collective-permute-done.44.step_ref = f32[2,128,128]{2,1,0:T(8,128)S(1)} collective-permute-done((f32[2,128,128]{2,1,0:T(8,128)S(1)}, f32[2,128,128]{2,1,0:T(8,128)S(1)}, u32[]{:S(2)}, u32[]{:S(2)}) %collective-permute-start.44) | collective-permute-done | bytes 131104 | tf_op jit(solution)/shard_map/ppermute | solution.py:223
  103.3 4.8 %collective-permute-done.46.refs_2_ = f32[264,128]{1,0:T(8,128)S(1)} collective-permute-done((f32[264,128]{1,0:T(8,128)S(1)}, f32[264,128]{1,0:T(8,128)S(1)}, u32[]{:S(2)}, u32[]{:S(2)}) %collective-permute-start.46) | collective-permute-done | bytes 135200 | tf_op jit(solution)/shard_map/ppermute | solution.py:223
  108.1 0.9 last.1
  109.0 10.8 %all_to_all.5.tiles_ref = f32[16,8,128]{2,1,0:T(8,128)S(1)} all-to-all(f32[16,8,128]{2,1,0:T(8,128)S(1)} %broadcast_in_dim.2), channel_id=1, replica_groups=mesh['group'=2,'term'=16] {'term'}, dimensions={0} | all-to-all | bytes 131072 | tf_op jit(solution)/shard_map/all_to_all | solution.py:364
  119.9 0.9 norm.1
  (47 shorter events, 0.6 us)
Async XLA Ops:
  0.6 7.2 %collective-permute-start.2 = (f32[2,128,128]{2,1,0:T(8,128)}, f32[2,128,128]{2,1,0:T(8,128)S(1)}, u32[]{:S(2)}, u32[]{:S(2)}) collective-permute-start(f32[2,128,128]{2,1,0:T(8,128)} %vector_in.1), channel_id=1, source_target_pairs={{0,2},{1,3},{2,0},{3,1},{4,6},{5,7},{6,4},{7,5},{8,10},{9,11},{10,... | collective-permute-start | bytes 393224 | tf_op jit(solution)/shard_map/ppermute | solution.py:223
  3.7 12.9 %collective-permute-start.8 = (f32[2,128,128]{2,1,0:T(8,128)}, f32[2,128,128]{2,1,0:T(8,128)S(1)}, u32[]{:S(2)}, u32[]{:S(2)}) collective-permute-start(f32[2,128,128]{2,1,0:T(8,128)} %vector_in.1), channel_id=1, source_target_pairs={{0,8},{1,9},{2,10},{3,11},{4,12},{5,13},{6,14},{7,15},{8,0},{9,1},... | collective-permute-start | bytes 393224 | tf_op jit(solution)/shard_map/ppermute | solution.py:223
  6.3 10.7 %collective-permute-start = (f32[2,128,128]{2,1,0:T(8,128)}, f32[2,128,128]{2,1,0:T(8,128)S(1)}, u32[]{:S(2)}, u32[]{:S(2)}) collective-permute-start(f32[2,128,128]{2,1,0:T(8,128)} %vector_in.1), channel_id=1, source_target_pairs={{0,12},{1,13},{2,14},{3,15},{4,8},{5,9},{6,10},{7,11},{8,4},{9,5},... | collective-permute-start | bytes 393224 | tf_op jit(solution)/shard_map/ppermute | solution.py:223
  7.6 10.5 %collective-permute-start.4 = (f32[2,128,128]{2,1,0:T(8,128)}, f32[2,128,128]{2,1,0:T(8,128)S(1)}, u32[]{:S(2)}, u32[]{:S(2)}) collective-permute-start(f32[2,128,128]{2,1,0:T(8,128)} %vector_in.1), channel_id=1, source_target_pairs={{0,4},{1,5},{2,6},{3,7},{4,0},{5,1},{6,2},{7,3},{8,12},{9,13},{10,... | collective-permute-start | bytes 393224 | tf_op jit(solution)/shard_map/ppermute | solution.py:223
  7.8 11.7 %collective-permute-start.6 = (f32[2,128,128]{2,1,0:T(8,128)S(1)}, f32[2,128,128]{2,1,0:T(8,128)S(1)}, u32[]{:S(2)}, u32[]{:S(2)}) collective-permute-start(f32[2,128,128]{2,1,0:T(8,128)S(1)} %collective-permute-done.2.refs_2_), channel_id=1, source_target_pairs={{0,4},{1,5},{2,6},{3,7},{4,0},{5,1},{6,2},{7,3},{8,12},{9,13},{10,... | collective-permute-start | bytes 393224 | tf_op jit(solution)/shard_map/ppermute | solution.py:223
  9.6 0.7 copy-start.1
  15.1 4.9 %collective-permute-start.3 = (f32[2,128,128]{2,1,0:T(8,128)S(1)}, f32[2,128,128]{2,1,0:T(8,128)S(1)}, u32[]{:S(2)}, u32[]{:S(2)}) collective-permute-start(f32[2,128,128]{2,1,0:T(8,128)S(1)} %collective-permute-done.2.refs_2_), channel_id=1, source_target_pairs={{0,1},{1,0},{2,3},{3,2},{4,5},{5,4},{6,7},{7,6},{8,9},{9,8},{10,11... | collective-permute-start | bytes 393224 | tf_op jit(solution)/shard_map/ppermute | solution.py:223
  16.5 5.2 %collective-permute-start.10 = (f32[2,128,128]{2,1,0:T(8,128)S(1)}, f32[2,128,128]{2,1,0:T(8,128)S(1)}, u32[]{:S(2)}, u32[]{:S(2)}) collective-permute-start(f32[2,128,128]{2,1,0:T(8,128)S(1)} %collective-permute-done.8.refs_8_), channel_id=1, source_target_pairs={{0,2},{1,3},{2,0},{3,1},{4,6},{5,7},{6,4},{7,5},{8,10},{9,11},{10,... | collective-permute-start | bytes 393224 | tf_op jit(solution)/shard_map/ppermute | solution.py:223
  17.0 4.8 %collective-permute-start.9 = (f32[2,128,128]{2,1,0:T(8,128)S(1)}, f32[2,128,128]{2,1,0:T(8,128)S(1)}, u32[]{:S(2)}, u32[]{:S(2)}) collective-permute-start(f32[2,128,128]{2,1,0:T(8,128)S(1)} %collective-permute-done.8.refs_8_), channel_id=1, source_target_pairs={{0,1},{1,0},{2,3},{3,2},{4,5},{5,4},{6,7},{7,6},{8,9},{9,8},{10,11... | collective-permute-start | bytes 393224 | tf_op jit(solution)/shard_map/ppermute | solution.py:223
  18.1 4.2 %collective-permute-start.5 = (f32[2,128,128]{2,1,0:T(8,128)S(1)}, f32[2,128,128]{2,1,0:T(8,128)S(1)}, u32[]{:S(2)}, u32[]{:S(2)}) collective-permute-start(f32[2,128,128]{2,1,0:T(8,128)S(1)} %collective-permute-done.4.refs_4_), channel_id=1, source_target_pairs={{0,1},{1,0},{2,3},{3,2},{4,5},{5,4},{6,7},{7,6},{8,9},{9,8},{10,11... | collective-permute-start | bytes 393224 | tf_op jit(solution)/shard_map/ppermute | solution.py:223
  19.5 5.0 %collective-permute-start.13 = (f32[2,128,128]{2,1,0:T(8,128)S(1)}, f32[2,128,128]{2,1,0:T(8,128)S(1)}, u32[]{:S(2)}, u32[]{:S(2)}) collective-permute-start(f32[2,128,128]{2,1,0:T(8,128)S(1)} %collective-permute-done.refs_12_), channel_id=1, source_target_pairs={{0,2},{1,3},{2,0},{3,1},{4,6},{5,7},{6,4},{7,5},{8,10},{9,11},{10,... | collective-permute-start | bytes 393224 | tf_op jit(solution)/shard_map/ppermute | solution.py:223
  20.0 4.5 %collective-permute-start.12 = (f32[2,128,128]{2,1,0:T(8,128)S(1)}, f32[2,128,128]{2,1,0:T(8,128)S(1)}, u32[]{:S(2)}, u32[]{:S(2)}) collective-permute-start(f32[2,128,128]{2,1,0:T(8,128)S(1)} %collective-permute-done.refs_12_), channel_id=1, source_target_pairs={{0,1},{1,0},{2,3},{3,2},{4,5},{5,4},{6,7},{7,6},{8,9},{9,8},{10,11... | collective-permute-start | bytes 393224 | tf_op jit(solution)/shard_map/ppermute | solution.py:223
  21.8 2.7 %collective-permute-start.1 = (f32[2,128,128]{2,1,0:T(8,128)S(1)}, f32[2,128,128]{2,1,0:T(8,128)S(1)}, u32[]{:S(2)}, u32[]{:S(2)}) collective-permute-start(f32[2,128,128]{2,1,0:T(8,128)S(1)} %get-tuple-element.55.refs_0_.vector_ref), channel_id=1, source_target_pairs={{0,1},{1,0},{2,3},{3,2},{4,5},{5,4},{6,7},{7,6},{8,9},{9,8},{10,11... | collective-permute-start | bytes 393224 | tf_op jit(solution)/shard_map/ppermute | solution.py:223
  21.8 2.7 %collective-permute-start.7 = (f32[2,128,128]{2,1,0:T(8,128)S(1)}, f32[2,128,128]{2,1,0:T(8,128)S(1)}, u32[]{:S(2)}, u32[]{:S(2)}) collective-permute-start(f32[2,128,128]{2,1,0:T(8,128)S(1)} %collective-permute-done.6.refs_6_), channel_id=1, source_target_pairs={{0,1},{1,0},{2,3},{3,2},{4,5},{5,4},{6,7},{7,6},{8,9},{9,8},{10,11... | collective-permute-start | bytes 393224 | tf_op jit(solution)/shard_map/ppermute | solution.py:223
  22.3 2.2 %collective-permute-start.11 = (f32[2,128,128]{2,1,0:T(8,128)S(1)}, f32[2,128,128]{2,1,0:T(8,128)S(1)}, u32[]{:S(2)}, u32[]{:S(2)}) collective-permute-start(f32[2,128,128]{2,1,0:T(8,128)S(1)} %collective-permute-done.10.refs_10_), channel_id=1, source_target_pairs={{0,1},{1,0},{2,3},{3,2},{4,5},{5,4},{6,7},{7,6},{8,9},{9,8},{10,11... | collective-permute-start | bytes 393224 | tf_op jit(solution)/shard_map/ppermute | solution.py:223
  24.5 1.3 %collective-permute-start.14 = (f32[2,128,128]{2,1,0:T(8,128)S(1)}, f32[2,128,128]{2,1,0:T(8,128)S(1)}, u32[]{:S(2)}, u32[]{:S(2)}) collective-permute-start(f32[2,128,128]{2,1,0:T(8,128)S(1)} %collective-permute-done.13.refs_14_), channel_id=1, source_target_pairs={{0,1},{1,0},{2,3},{3,2},{4,5},{5,4},{6,7},{7,6},{8,9},{9,8},{10,11... | collective-permute-start | bytes 393224 | tf_op jit(solution)/shard_map/ppermute | solution.py:223
  32.5 8.5 %collective-permute-start.15 = (f32[648,128]{1,0:T(8,128)S(1)}, f32[648,128]{1,0:T(8,128)S(1)}, u32[]{:S(2)}, u32[]{:S(2)}) collective-permute-start(f32[648,128]{1,0:T(8,128)S(1)} %get-tuple-element.58.far_in), channel_id=1, source_target_pairs={{0,1},{1,0},{2,3},{3,2},{4,5},{5,4},{6,7},{7,6},{8,9},{9,8},{10,11... | collective-permute-start | bytes 995336 | tf_op jit(solution)/shard_map/ppermute | solution.py:223
  32.6 7.0 %collective-permute-start.16 = (f32[264,128]{1,0:T(8,128)S(1)}, f32[264,128]{1,0:T(8,128)S(1)}, u32[]{:S(2)}, u32[]{:S(2)}) collective-permute-start(f32[264,128]{1,0:T(8,128)S(1)} %get-tuple-element.59), channel_id=1, source_target_pairs={{0,2},{1,3},{2,0},{3,1},{4,6},{5,7},{6,4},{7,5},{8,10},{9,11},{10,... | collective-permute-start | bytes 405512 | tf_op jit(solution)/shard_map/ppermute | solution.py:223
  33.1 7.9 %collective-permute-start.17 = (f32[264,128]{1,0:T(8,128)S(1)}, f32[264,128]{1,0:T(8,128)S(1)}, u32[]{:S(2)}, u32[]{:S(2)}) collective-permute-start(f32[264,128]{1,0:T(8,128)S(1)} %get-tuple-element.60), channel_id=1, source_target_pairs={{0,3},{1,2},{2,1},{3,0},{4,7},{5,6},{6,5},{7,4},{8,11},{9,10},{10,... | collective-permute-start | bytes 405512 | tf_op jit(solution)/shard_map/ppermute | solution.py:223
  34.4 4.9 %collective-permute-start.18 = (f32[128,128]{1,0:T(8,128)S(1)}, f32[128,128]{1,0:T(8,128)S(1)}, u32[]{:S(2)}, u32[]{:S(2)}) collective-permute-start(f32[128,128]{1,0:T(8,128)S(1)} %get-tuple-element.61), channel_id=1, source_target_pairs={{0,4},{1,5},{2,6},{3,7},{4,0},{5,1},{6,2},{7,3},{8,12},{9,13},{10,... | collective-permute-start | bytes 196616 | tf_op jit(solution)/shard_map/ppermute | solution.py:223
  34.8 4.8 %collective-permute-start.19 = (f32[128,128]{1,0:T(8,128)S(1)}, f32[128,128]{1,0:T(8,128)S(1)}, u32[]{:S(2)}, u32[]{:S(2)}) collective-permute-start(f32[128,128]{1,0:T(8,128)S(1)} %get-tuple-element.62), channel_id=1, source_target_pairs={{0,5},{1,4},{2,7},{3,6},{4,1},{5,0},{6,3},{7,2},{8,13},{9,12},{10,... | collective-permute-start | bytes 196616 | tf_op jit(solution)/shard_map/ppermute | solution.py:223
  41.0 15.7 %copy-start = (f32[2,128,128]{2,1,0:T(8,128)S(1)}, f32[2,128,128]{2,1,0:T(8,128)}, u32[]{:S(2)}) copy-start(f32[2,128,128]{2,1,0:T(8,128)} %precond_ref.3) | copy-start | bytes 393220
  41.7 9.4 %collective-permute-start.21 = (f32[264,128]{1,0:T(8,128)S(1)}, f32[264,128]{1,0:T(8,128)S(1)}, u32[]{:S(2)}, u32[]{:S(2)}) collective-permute-start(f32[264,128]{1,0:T(8,128)S(1)} %get-tuple-element.67), channel_id=1, source_target_pairs={{0,12},{1,13},{2,14},{3,15},{4,8},{5,9},{6,10},{7,11},{8,4},{9,5},... | collective-permute-start | bytes 405512 | tf_op jit(solution)/shard_map/ppermute | solution.py:223
  45.0 11.8 %collective-permute-start.22 = (f32[264,128]{1,0:T(8,128)S(1)}, f32[264,128]{1,0:T(8,128)S(1)}, u32[]{:S(2)}, u32[]{:S(2)}) collective-permute-start(f32[264,128]{1,0:T(8,128)S(1)} %get-tuple-element.68), channel_id=1, source_target_pairs={{0,8},{1,9},{2,10},{3,11},{4,12},{5,13},{6,14},{7,15},{8,0},{9,1},... | collective-permute-start | bytes 405512 | tf_op jit(solution)/shard_map/ppermute | solution.py:223
  45.0 11.8 %collective-permute-start.23 = (f32[264,128]{1,0:T(8,128)S(1)}, f32[264,128]{1,0:T(8,128)S(1)}, u32[]{:S(2)}, u32[]{:S(2)}) collective-permute-start(f32[264,128]{1,0:T(8,128)S(1)} %get-tuple-element.66.refs_0_), channel_id=1, source_target_pairs={{0,4},{1,5},{2,6},{3,7},{4,0},{5,1},{6,2},{7,3},{8,12},{9,13},{10,... | collective-permute-start | bytes 405512 | tf_op jit(solution)/shard_map/ppermute | solution.py:223
  46.2 5.0 %collective-permute-start.20 = (f32[2,128,128]{2,1,0:T(8,128)S(1)}, f32[2,128,128]{2,1,0:T(8,128)S(1)}, u32[]{:S(2)}, u32[]{:S(2)}) collective-permute-start(f32[2,128,128]{2,1,0:T(8,128)S(1)} %get-tuple-element.64), channel_id=1, source_target_pairs={{0,2},{1,3},{2,0},{3,1},{4,6},{5,7},{6,4},{7,5},{8,10},{9,11},{10,... | collective-permute-start | bytes 393224 | tf_op jit(solution)/shard_map/ppermute | solution.py:223
  57.0 8.3 %collective-permute-start.35 = (f32[2,128,128]{2,1,0:T(8,128)S(1)}, f32[2,128,128]{2,1,0:T(8,128)S(1)}, u32[]{:S(2)}, u32[]{:S(2)}) collective-permute-start(f32[2,128,128]{2,1,0:T(8,128)S(1)} %step.1.refs_0_.vector_ref), channel_id=1, source_target_pairs={{0,12},{1,13},{2,14},{3,15},{4,8},{5,9},{6,10},{7,11},{8,4},{9,5},... | collective-permute-start | bytes 393224 | tf_op jit(solution)/shard_map/ppermute | solution.py:223
  59.7 10.3 %collective-permute-start.31 = (f32[2,128,128]{2,1,0:T(8,128)S(1)}, f32[2,128,128]{2,1,0:T(8,128)S(1)}, u32[]{:S(2)}, u32[]{:S(2)}) collective-permute-start(f32[2,128,128]{2,1,0:T(8,128)S(1)} %step.1.refs_0_.vector_ref), channel_id=1, source_target_pairs={{0,8},{1,9},{2,10},{3,11},{4,12},{5,13},{6,14},{7,15},{8,0},{9,1},... | collective-permute-start | bytes 393224 | tf_op jit(solution)/shard_map/ppermute | solution.py:223
  59.7 10.3 %collective-permute-start.27 = (f32[2,128,128]{2,1,0:T(8,128)S(1)}, f32[2,128,128]{2,1,0:T(8,128)S(1)}, u32[]{:S(2)}, u32[]{:S(2)}) collective-permute-start(f32[2,128,128]{2,1,0:T(8,128)S(1)} %step.1.refs_0_.vector_ref), channel_id=1, source_target_pairs={{0,4},{1,5},{2,6},{3,7},{4,0},{5,1},{6,2},{7,3},{8,12},{9,13},{10,... | collective-permute-start | bytes 393224 | tf_op jit(solution)/shard_map/ppermute | solution.py:223
  61.4 9.2 %collective-permute-start.25 = (f32[2,128,128]{2,1,0:T(8,128)S(1)}, f32[2,128,128]{2,1,0:T(8,128)S(1)}, u32[]{:S(2)}, u32[]{:S(2)}) collective-permute-start(f32[2,128,128]{2,1,0:T(8,128)S(1)} %step.1.refs_0_.vector_ref), channel_id=1, source_target_pairs={{0,2},{1,3},{2,0},{3,1},{4,6},{5,7},{6,4},{7,5},{8,10},{9,11},{10,... | collective-permute-start | bytes 393224 | tf_op jit(solution)/shard_map/ppermute | solution.py:223
  61.8 9.0 %collective-permute-start.24 = (f32[2,128,128]{2,1,0:T(8,128)S(1)}, f32[2,128,128]{2,1,0:T(8,128)S(1)}, u32[]{:S(2)}, u32[]{:S(2)}) collective-permute-start(f32[2,128,128]{2,1,0:T(8,128)S(1)} %step.1.refs_0_.vector_ref), channel_id=1, source_target_pairs={{0,1},{1,0},{2,3},{3,2},{4,5},{5,4},{6,7},{7,6},{8,9},{9,8},{10,11... | collective-permute-start | bytes 393224 | tf_op jit(solution)/shard_map/ppermute | solution.py:223
  65.3 5.7 %collective-permute-start.37 = (f32[2,128,128]{2,1,0:T(8,128)S(1)}, f32[2,128,128]{2,1,0:T(8,128)S(1)}, u32[]{:S(2)}, u32[]{:S(2)}) collective-permute-start(f32[2,128,128]{2,1,0:T(8,128)S(1)} %collective-permute-done.35.refs_12_), channel_id=1, source_target_pairs={{0,2},{1,3},{2,0},{3,1},{4,6},{5,7},{6,4},{7,5},{8,10},{9,11},{10,... | collective-permute-start | bytes 393224 | tf_op jit(solution)/shard_map/ppermute | solution.py:223
  70.0 1.3 %collective-permute-start.36 = (f32[2,128,128]{2,1,0:T(8,128)S(1)}, f32[2,128,128]{2,1,0:T(8,128)S(1)}, u32[]{:S(2)}, u32[]{:S(2)}) collective-permute-start(f32[2,128,128]{2,1,0:T(8,128)S(1)} %collective-permute-done.35.refs_12_), channel_id=1, source_target_pairs={{0,1},{1,0},{2,3},{3,2},{4,5},{5,4},{6,7},{7,6},{8,9},{9,8},{10,11... | collective-permute-start | bytes 393224 | tf_op jit(solution)/shard_map/ppermute | solution.py:223
  70.0 5.9 %collective-permute-start.33 = (f32[2,128,128]{2,1,0:T(8,128)S(1)}, f32[2,128,128]{2,1,0:T(8,128)S(1)}, u32[]{:S(2)}, u32[]{:S(2)}) collective-permute-start(f32[2,128,128]{2,1,0:T(8,128)S(1)} %collective-permute-done.31.refs_8_), channel_id=1, source_target_pairs={{0,2},{1,3},{2,0},{3,1},{4,6},{5,7},{6,4},{7,5},{8,10},{9,11},{10,... | collective-permute-start | bytes 393224 | tf_op jit(solution)/shard_map/ppermute | solution.py:223
  70.6 5.3 %collective-permute-start.32 = (f32[2,128,128]{2,1,0:T(8,128)S(1)}, f32[2,128,128]{2,1,0:T(8,128)S(1)}, u32[]{:S(2)}, u32[]{:S(2)}) collective-permute-start(f32[2,128,128]{2,1,0:T(8,128)S(1)} %collective-permute-done.31.refs_8_), channel_id=1, source_target_pairs={{0,1},{1,0},{2,3},{3,2},{4,5},{5,4},{6,7},{7,6},{8,9},{9,8},{10,11... | collective-permute-start | bytes 393224 | tf_op jit(solution)/shard_map/ppermute | solution.py:223
  70.8 5.7 %collective-permute-start.29 = (f32[2,128,128]{2,1,0:T(8,128)S(1)}, f32[2,128,128]{2,1,0:T(8,128)S(1)}, u32[]{:S(2)}, u32[]{:S(2)}) collective-permute-start(f32[2,128,128]{2,1,0:T(8,128)S(1)} %collective-permute-done.25.refs_2_), channel_id=1, source_target_pairs={{0,4},{1,5},{2,6},{3,7},{4,0},{5,1},{6,2},{7,3},{8,12},{9,13},{10,... | collective-permute-start | bytes 393224 | tf_op jit(solution)/shard_map/ppermute | solution.py:223
  70.9 5.6 %collective-permute-start.26 = (f32[2,128,128]{2,1,0:T(8,128)S(1)}, f32[2,128,128]{2,1,0:T(8,128)S(1)}, u32[]{:S(2)}, u32[]{:S(2)}) collective-permute-start(f32[2,128,128]{2,1,0:T(8,128)S(1)} %collective-permute-done.25.refs_2_), channel_id=1, source_target_pairs={{0,1},{1,0},{2,3},{3,2},{4,5},{5,4},{6,7},{7,6},{8,9},{9,8},{10,11... | collective-permute-start | bytes 393224 | tf_op jit(solution)/shard_map/ppermute | solution.py:223
  71.3 5.2 %collective-permute-start.28 = (f32[2,128,128]{2,1,0:T(8,128)S(1)}, f32[2,128,128]{2,1,0:T(8,128)S(1)}, u32[]{:S(2)}, u32[]{:S(2)}) collective-permute-start(f32[2,128,128]{2,1,0:T(8,128)S(1)} %collective-permute-done.27.refs_4_), channel_id=1, source_target_pairs={{0,1},{1,0},{2,3},{3,2},{4,5},{5,4},{6,7},{7,6},{8,9},{9,8},{10,11... | collective-permute-start | bytes 393224 | tf_op jit(solution)/shard_map/ppermute | solution.py:223
  75.9 1.3 %collective-permute-start.38 = (f32[2,128,128]{2,1,0:T(8,128)S(1)}, f32[2,128,128]{2,1,0:T(8,128)S(1)}, u32[]{:S(2)}, u32[]{:S(2)}) collective-permute-start(f32[2,128,128]{2,1,0:T(8,128)S(1)} %collective-permute-done.37.refs_14_), channel_id=1, source_target_pairs={{0,1},{1,0},{2,3},{3,2},{4,5},{5,4},{6,7},{7,6},{8,9},{9,8},{10,11... | collective-permute-start | bytes 393224 | tf_op jit(solution)/shard_map/ppermute | solution.py:223
  75.9 1.5 %collective-permute-start.34 = (f32[2,128,128]{2,1,0:T(8,128)S(1)}, f32[2,128,128]{2,1,0:T(8,128)S(1)}, u32[]{:S(2)}, u32[]{:S(2)}) collective-permute-start(f32[2,128,128]{2,1,0:T(8,128)S(1)} %collective-permute-done.33.refs_10_), channel_id=1, source_target_pairs={{0,1},{1,0},{2,3},{3,2},{4,5},{5,4},{6,7},{7,6},{8,9},{9,8},{10,11... | collective-permute-start | bytes 393224 | tf_op jit(solution)/shard_map/ppermute | solution.py:223
  76.5 1.3 %collective-permute-start.30 = (f32[2,128,128]{2,1,0:T(8,128)S(1)}, f32[2,128,128]{2,1,0:T(8,128)S(1)}, u32[]{:S(2)}, u32[]{:S(2)}) collective-permute-start(f32[2,128,128]{2,1,0:T(8,128)S(1)} %collective-permute-done.29.refs_6_), channel_id=1, source_target_pairs={{0,1},{1,0},{2,3},{3,2},{4,5},{5,4},{6,7},{7,6},{8,9},{9,8},{10,11... | collective-permute-start | bytes 393224 | tf_op jit(solution)/shard_map/ppermute | solution.py:223
  84.7 8.5 %collective-permute-start.39 = (f32[648,128]{1,0:T(8,128)S(1)}, f32[648,128]{1,0:T(8,128)S(1)}, u32[]{:S(2)}, u32[]{:S(2)}) collective-permute-start(f32[648,128]{1,0:T(8,128)S(1)} %get-tuple-element.70.far_in), channel_id=1, source_target_pairs={{0,1},{1,0},{2,3},{3,2},{4,5},{5,4},{6,7},{7,6},{8,9},{9,8},{10,11... | collective-permute-start | bytes 995336 | tf_op jit(solution)/shard_map/ppermute | solution.py:223
  84.8 7.0 %collective-permute-start.40 = (f32[264,128]{1,0:T(8,128)S(1)}, f32[264,128]{1,0:T(8,128)S(1)}, u32[]{:S(2)}, u32[]{:S(2)}) collective-permute-start(f32[264,128]{1,0:T(8,128)S(1)} %get-tuple-element.71), channel_id=1, source_target_pairs={{0,2},{1,3},{2,0},{3,1},{4,6},{5,7},{6,4},{7,5},{8,10},{9,11},{10,... | collective-permute-start | bytes 405512 | tf_op jit(solution)/shard_map/ppermute | solution.py:223
  86.3 6.9 %collective-permute-start.41 = (f32[264,128]{1,0:T(8,128)S(1)}, f32[264,128]{1,0:T(8,128)S(1)}, u32[]{:S(2)}, u32[]{:S(2)}) collective-permute-start(f32[264,128]{1,0:T(8,128)S(1)} %get-tuple-element.72), channel_id=1, source_target_pairs={{0,3},{1,2},{2,1},{3,0},{4,7},{5,6},{6,5},{7,4},{8,11},{9,10},{10,... | collective-permute-start | bytes 405512 | tf_op jit(solution)/shard_map/ppermute | solution.py:223
  86.6 4.9 %collective-permute-start.42 = (f32[128,128]{1,0:T(8,128)S(1)}, f32[128,128]{1,0:T(8,128)S(1)}, u32[]{:S(2)}, u32[]{:S(2)}) collective-permute-start(f32[128,128]{1,0:T(8,128)S(1)} %get-tuple-element.73), channel_id=1, source_target_pairs={{0,4},{1,5},{2,6},{3,7},{4,0},{5,1},{6,2},{7,3},{8,12},{9,13},{10,... | collective-permute-start | bytes 196616 | tf_op jit(solution)/shard_map/ppermute | solution.py:223
  86.9 4.9 %collective-permute-start.43 = (f32[128,128]{1,0:T(8,128)S(1)}, f32[128,128]{1,0:T(8,128)S(1)}, u32[]{:S(2)}, u32[]{:S(2)}) collective-permute-start(f32[128,128]{1,0:T(8,128)S(1)} %get-tuple-element.74), channel_id=1, source_target_pairs={{0,5},{1,4},{2,7},{3,6},{4,1},{5,0},{6,3},{7,2},{8,13},{9,12},{10,... | collective-permute-start | bytes 196616 | tf_op jit(solution)/shard_map/ppermute | solution.py:223
  93.9 9.4 %collective-permute-start.45 = (f32[264,128]{1,0:T(8,128)S(1)}, f32[264,128]{1,0:T(8,128)S(1)}, u32[]{:S(2)}, u32[]{:S(2)}) collective-permute-start(f32[264,128]{1,0:T(8,128)S(1)} %get-tuple-element.79), channel_id=1, source_target_pairs={{0,12},{1,13},{2,14},{3,15},{4,8},{5,9},{6,10},{7,11},{8,4},{9,5},... | collective-permute-start | bytes 405512 | tf_op jit(solution)/shard_map/ppermute | solution.py:223
  95.7 12.4 %collective-permute-start.46 = (f32[264,128]{1,0:T(8,128)S(1)}, f32[264,128]{1,0:T(8,128)S(1)}, u32[]{:S(2)}, u32[]{:S(2)}) collective-permute-start(f32[264,128]{1,0:T(8,128)S(1)} %get-tuple-element.80), channel_id=1, source_target_pairs={{0,8},{1,9},{2,10},{3,11},{4,12},{5,13},{6,14},{7,15},{8,0},{9,1},... | collective-permute-start | bytes 405512 | tf_op jit(solution)/shard_map/ppermute | solution.py:223
  95.7 12.4 %collective-permute-start.47 = (f32[264,128]{1,0:T(8,128)S(1)}, f32[264,128]{1,0:T(8,128)S(1)}, u32[]{:S(2)}, u32[]{:S(2)}) collective-permute-start(f32[264,128]{1,0:T(8,128)S(1)} %get-tuple-element.78.refs_0_), channel_id=1, source_target_pairs={{0,4},{1,5},{2,6},{3,7},{4,0},{5,1},{6,2},{7,3},{8,12},{9,13},{10,... | collective-permute-start | bytes 405512 | tf_op jit(solution)/shard_map/ppermute | solution.py:223
  98.4 5.0 %collective-permute-start.44 = (f32[2,128,128]{2,1,0:T(8,128)S(1)}, f32[2,128,128]{2,1,0:T(8,128)S(1)}, u32[]{:S(2)}, u32[]{:S(2)}) collective-permute-start(f32[2,128,128]{2,1,0:T(8,128)S(1)} %get-tuple-element.76), channel_id=1, source_target_pairs={{0,2},{1,3},{2,0},{3,1},{4,6},{5,7},{6,4},{7,5},{8,10},{9,11},{10,... | collective-permute-start | bytes 393224 | tf_op jit(solution)/shard_map/ppermute | solution.py:223

commit v5 on v4

--- a/solution.py
+++ b/solution.py
@@ -136,9 +136,14 @@
     )(me, at_home(fetch), at_home(store), at_home(pairs), live, at_home(vector), at_home(left_ops), at_home(right_ops))
 
 
+def nearest_last(n):
+    return [*range(8), *(r for k in reversed(range(8, n, 4)) for r in range(k, k + 4))]
+
+
 def apply_kernel(n, over_rows, rows, start, pick_ref, mine_ref, first_ref, second_ref, dst_ref, one_ref, two_ref, count_ref,
                  l4_ref, rr_ref, *refs):
-    pieces, (near_ref, far_ref, row_ref, row_far_ref, column_ref, column_far_ref, square_ref, block, total) = refs[:n], refs[n:]
+    pieces = [refs[nearest_last(n).index(k)] for k in range(n)]
+    near_ref, far_ref, row_ref, row_far_ref, column_ref, column_far_ref, square_ref, block, total = refs[n:]
     terms, width = l4_ref.shape[:2]
     square = jnp.zeros((8, width), jnp.float32)
     product = jnp.zeros((8, width), jnp.float32)
@@ -206,7 +211,7 @@
         ],
         compiler_params=params(32 if n <= 16 else 56),
         name="apply",
-    )(*tables[2:4], *tables[5:], *tables[:2], *pieces)
+    )(*tables[2:4], *tables[5:], *tables[:2], *(pieces[k] for k in nearest_last(n)))
 
 
 def joined(parts, count):
@@ -323,19 +328,19 @@
         (shape(2, width, width),) * 2 + (shape(2 * width + 8, width),) * (chips // 2 - 1), tables[4:5],
         (near, far, swapped(far, CORE), swapped(row, ROW), swapped(row_far, ROW + CORE), swapped(column, COLUMN),
          swapped(column_far, COLUMN + CORE)))
-    came = [swapped(x, 2 * ROW * (i + 1)) for i, x in reversed(list(enumerate(sends)))]
+    came = [swapped(sends[i], 2 * ROW * (i + 1)) for i in (*range(1, len(sends)), 0)]
     return square, (own, swapped(step, ROW)), [sends[0], *came]
 
 
 def gathered(n, x, held=None):
     pieces = {0: x}
-    for k in reversed(range(8, n, 4)):
+    for k in range(8, n, 4):
         pieces[k] = swapped(x, k)
+    if held is not None:
+        x, pieces[0] = lax.optimization_barrier((x, held))
+    pieces[COLUMN] = swapped(x, COLUMN)
     pieces[ROW] = swapped(x, ROW)
-    pieces[COLUMN] = swapped(x, COLUMN)
-    if held is not None:
-        pieces[n - 4], pieces[0] = lax.optimization_barrier((pieces[n - 4], held))
-    for k in reversed(range(8, n, 4)):
+    for k in range(8, n, 4):
         pieces[k + ROW] = swapped(pieces[k], ROW)
     pieces[COLUMN + ROW] = swapped(pieces[ROW], COLUMN)
     for k in range(0, n, 2):

time: 121 us -> 122 us (level)
  starting transfers between devices: 35.7 us -> 39.5 us
  waiting for transfers between devices: 51.1 us -> 49.1 us
    ppermute x48, starting transfers between devices: 35.7 us -> 39.5 us  [swapped(): return lax.ppermute(x, 'term', [(i, i ^ k) for i in range(n)])]
    ppermute x48, waiting for transfers between devices: 51.1 us -> 49.1 us  [swapped(): return lax.ppermute(x, 'term', [(i, i ^ k) for i in range(n)])]
  transfers between devices with their start and end apart: 48 -> 48, of which waited for: 24 -> 25; matrix products, arithmetic and copies ran while one was open for 0% -> 0% of each run, Pallas kernels for 3% -> 3%
where the time goes in v5:
time: 122 us
  waiting for transfers between devices  49.1 us (40%)
  starting transfers between devices  39.5 us (32%)
  Pallas kernels  20.3 us (17%)
  blocking collectives  11 us (9%)
  between operations  1.41 us (1%)
    ppermute x48, waiting for transfers between devices, swapped(): return lax.ppermute(x, 'term', [(i, i ^ k) for i in range(n)])  49.1 us
    ppermute x48, starting transfers between devices, swapped(): return lax.ppermute(x, 'term', [(i, i ^ k) for i in range(n)])  39.5 us
    pallas_call x2, Pallas kernels, apply(): pl.pallas_call(functools.partial(apply_kernel, n, over_rows, rows, start)...  13.5 us
    all_to_all x1, blocking collectives, shards(): lax.all_to_all(jnp.broadcast_to(partial[None], (n, 8, width)), 'term', sp...  11 us
    pallas_call x1, Pallas kernels, prep(): pl.pallas_call(functools.partial(prep_kernel, n, terms * n + 1), out_shap...  3.48 us
    pallas_call x5, Pallas kernels, local(): pl.pallas_call(kernel, out_shape=out_shape, in_specs=[SMEM] * len(scalars...  3.35 us
  transfers between devices with their start and end apart: 48, of which 25 were waited for; matrix products, arithmetic and copies ran while one was open for 0% of the time, Pallas kernels for 3%

profile of v5, /device:TPU:0, one launch (start us, length us, event | category | flops | bytes accessed | tf_op | source)
XLA Modules:
  0.0 121.9 jit_solution(14468224824397852825)
XLA Ops:
  0.6 4.1 %collective-permute-start.11 = (f32[2,128,128]{2,1,0:T(8,128)}, f32[2,128,128]{2,1,0:T(8,128)S(1)}, u32[]{:S(2)}, u32[]{:S(2)}) collective-permute-start(f32[2,128,128]{2,1,0:T(8,128)} %vector_in.1), channel_id=1, source_target_pairs={{0,8},{1,9},{2,10},{3,11},{4,12},{5,13},{6,14},{7,15},{8,0},{9,1},... | collective-permute-start | bytes 393224 | tf_op jit(solution)/shard_map/ppermute | solution.py:228
  4.7 1.3 %collective-permute-start.7 = (f32[2,128,128]{2,1,0:T(8,128)}, f32[2,128,128]{2,1,0:T(8,128)S(1)}, u32[]{:S(2)}, u32[]{:S(2)}) collective-permute-start(f32[2,128,128]{2,1,0:T(8,128)} %vector_in.1), channel_id=1, source_target_pairs={{0,12},{1,13},{2,14},{3,15},{4,8},{5,9},{6,10},{7,11},{8,4},{9,5},... | collective-permute-start | bytes 393224 | tf_op jit(solution)/shard_map/ppermute | solution.py:228
  6.8 0.6 copy.12
  7.3 3.5 %prep.1 = (bf16[8,128,512]{2,1,0:T(8,128)(2,1)S(1)}, bf16[2048,256]{1,0:T(8,128)(2,1)S(1)}, s32[16]{0:T(128)S(1)}, s32[16]{0:T(128)S(1)}, s32[48]{0:T(128)S(1)},...) custom-call(s32[1]{0:T(128)} %bitcast.me_ref, ...), custom_call_target="tpu_custom_call" | custom-call | tf_op jit(solution)/shard_map/prep/pallas_call | solution.py:113
  11.0 2.2 %collective-permute-start.1 = (f32[2,128,128]{2,1,0:T(8,128)S(1)}, f32[2,128,128]{2,1,0:T(8,128)S(1)}, u32[]{:S(2)}, u32[]{:S(2)}) collective-permute-start(f32[2,128,128]{2,1,0:T(8,128)S(1)} %copy-done.1), channel_id=1, source_target_pairs={{0,2},{1,3},{2,0},{3,1},{4,6},{5,7},{6,4},{7,5},{8,10},{9,11},{10,... | collective-permute-start | bytes 393224 | tf_op jit(solution)/shard_map/ppermute | solution.py:228
  13.2 1.7 %collective-permute-done.11.refs_12_ = f32[2,128,128]{2,1,0:T(8,128)S(1)} collective-permute-done((f32[2,128,128]{2,1,0:T(8,128)}, f32[2,128,128]{2,1,0:T(8,128)S(1)}, u32[]{:S(2)}, u32[]{:S(2)}) %collective-permute-start.11) | collective-permute-done | bytes 131104 | tf_op jit(solution)/shard_map/ppermute | solution.py:228
  14.9 1.9 %collective-permute-start.13 = (f32[2,128,128]{2,1,0:T(8,128)S(1)}, f32[2,128,128]{2,1,0:T(8,128)S(1)}, u32[]{:S(2)}, u32[]{:S(2)}) collective-permute-start(f32[2,128,128]{2,1,0:T(8,128)S(1)} %collective-permute-done.11.refs_12_), channel_id=1, source_target_pairs={{0,2},{1,3},{2,0},{3,1},{4,6},{5,7},{6,4},{7,5},{8,10},{9,11},{10,... | collective-permute-start | bytes 393224 | tf_op jit(solution)/shard_map/ppermute | solution.py:228
  16.9 1.6 %collective-permute-start.9 = (f32[2,128,128]{2,1,0:T(8,128)S(1)}, f32[2,128,128]{2,1,0:T(8,128)S(1)}, u32[]{:S(2)}, u32[]{:S(2)}) collective-permute-start(f32[2,128,128]{2,1,0:T(8,128)S(1)} %collective-permute-done.7.refs_8_), channel_id=1, source_target_pairs={{0,2},{1,3},{2,0},{3,1},{4,6},{5,7},{6,4},{7,5},{8,10},{9,11},{10,... | collective-permute-start | bytes 393224 | tf_op jit(solution)/shard_map/ppermute | solution.py:228
  18.5 1.0 collective-permute-start.5
  19.5 1.2 collective-permute-done.13.refs_14_
  20.6 0.5 collective-permute-start.4
  21.2 1.5 %collective-permute-done.9.refs_10_ = f32[2,128,128]{2,1,0:T(8,128)S(1)} collective-permute-done((f32[2,128,128]{2,1,0:T(8,128)S(1)}, f32[2,128,128]{2,1,0:T(8,128)S(1)}, u32[]{:S(2)}, u32[]{:S(2)}) %collective-permute-start.9) | collective-permute-done | bytes 131104 | tf_op jit(solution)/shard_map/ppermute | solution.py:228
  22.7 0.5 collective-permute-start.10
  23.2 1.2 collective-permute-done.5.refs_6_
  24.4 1.3 %collective-permute-done.6.refs_7_ = f32[2,128,128]{2,1,0:T(8,128)S(1)} collective-permute-done((f32[2,128,128]{2,1,0:T(8,128)S(1)}, f32[2,128,128]{2,1,0:T(8,128)S(1)}, u32[]{:S(2)}, u32[]{:S(2)}) %collective-permute-start.6) | collective-permute-done | bytes 131104 | tf_op jit(solution)/shard_map/ppermute | solution.py:228
  25.7 6.7 %apply.2 = (f32[640,128]{1,0:T(8,128)S(1)}, f32[648,128]{1,0:T(8,128)S(1)}, f32[264,128]{1,0:T(8,128)S(1)}, f32[264,128]{1,0:T(8,128)S(1)}, f32[128,128]{1,0:T(8...) custom-call(s32[16]{0:T(128)S(1)} %get-tuple-element.44.pick_ref, s32[16]{0:T(128)S(1)} %get-tuple-element.45.mine_ref, ...), custom_call_target="tpu_custom_call" | custom-call | tf_op jit(solution)/shard_map/apply/pallas_call | solution.py:202
  32.6 0.8 collective-permute-start.16
  33.4 0.9 collective-permute-start.17
  34.4 0.7 collective-permute-start.18
  35.1 1.0 collective-permute-start.19
  36.1 3.2 %collective-permute-done.18.column_ref = f32[128,128]{1,0:T(8,128)S(1)} collective-permute-done((f32[128,128]{1,0:T(8,128)S(1)}, f32[128,128]{1,0:T(8,128)S(1)}, u32[]{:S(2)}, u32[]{:S(2)}) %collective-permute-start.18) | collective-permute-done | bytes 65568 | tf_op jit(solution)/shard_map/ppermute | solution.py:228
  39.3 0.3 collective-permute-done.19.column_far_ref
  39.6 1.4 %collective-permute-done.17.row_far_ref = f32[264,128]{1,0:T(8,128)S(1)} collective-permute-done((f32[264,128]{1,0:T(8,128)S(1)}, f32[264,128]{1,0:T(8,128)S(1)}, u32[]{:S(2)}, u32[]{:S(2)}) %collective-permute-start.17) | collective-permute-done | bytes 135200 | tf_op jit(solution)/shard_map/ppermute | solution.py:228
  40.9 0.7 fold.2
  41.6 2.5 %collective-permute-start.21 = (f32[264,128]{1,0:T(8,128)S(1)}, f32[264,128]{1,0:T(8,128)S(1)}, u32[]{:S(2)}, u32[]{:S(2)}) collective-permute-start(f32[264,128]{1,0:T(8,128)S(1)} %get-tuple-element.67), channel_id=1, source_target_pairs={{0,8},{1,9},{2,10},{3,11},{4,12},{5,13},{6,14},{7,15},{8,0},{9,1},... | collective-permute-start | bytes 405512 | tf_op jit(solution)/shard_map/ppermute | solution.py:228
  44.1 1.2 %collective-permute-start.22 = (f32[264,128]{1,0:T(8,128)S(1)}, f32[264,128]{1,0:T(8,128)S(1)}, u32[]{:S(2)}, u32[]{:S(2)}) collective-permute-start(f32[264,128]{1,0:T(8,128)S(1)} %get-tuple-element.68), channel_id=1, source_target_pairs={{0,12},{1,13},{2,14},{3,15},{4,8},{5,9},{6,10},{7,11},{8,4},{9,5},... | collective-permute-start | bytes 405512 | tf_op jit(solution)/shard_map/ppermute | solution.py:228
  45.4 0.5 collective-permute-start.23
  46.0 5.0 %collective-permute-done.20.step_ref = f32[2,128,128]{2,1,0:T(8,128)S(1)} collective-permute-done((f32[2,128,128]{2,1,0:T(8,128)S(1)}, f32[2,128,128]{2,1,0:T(8,128)S(1)}, u32[]{:S(2)}, u32[]{:S(2)}) %collective-permute-start.20) | collective-permute-done | bytes 131104 | tf_op jit(solution)/shard_map/ppermute | solution.py:228
  51.0 3.9 %collective-permute-done.21.refs_1_ = f32[264,128]{1,0:T(8,128)S(1)} collective-permute-done((f32[264,128]{1,0:T(8,128)S(1)}, f32[264,128]{1,0:T(8,128)S(1)}, u32[]{:S(2)}, u32[]{:S(2)}) %collective-permute-start.21) | collective-permute-done | bytes 135200 | tf_op jit(solution)/shard_map/ppermute | solution.py:228
  54.8 0.8 collective-permute-done.23.refs_3_
  55.6 0.2 step.1.refs_0_.vector_ref
  55.8 4.1 %collective-permute-start.35 = (f32[2,128,128]{2,1,0:T(8,128)S(1)}, f32[2,128,128]{2,1,0:T(8,128)S(1)}, u32[]{:S(2)}, u32[]{:S(2)}) collective-permute-start(f32[2,128,128]{2,1,0:T(8,128)S(1)} %step.1.refs_0_.vector_ref), channel_id=1, source_target_pairs={{0,8},{1,9},{2,10},{3,11},{4,12},{5,13},{6,14},{7,15},{8,0},{9,1},... | collective-permute-start | bytes 393224 | tf_op jit(solution)/shard_map/ppermute | solution.py:228
  59.9 0.5 collective-permute-start.31
  60.5 0.5 collective-permute-start.25
  61.1 8.4 %collective-permute-done.35.refs_12_ = f32[2,128,128]{2,1,0:T(8,128)S(1)} collective-permute-done((f32[2,128,128]{2,1,0:T(8,128)S(1)}, f32[2,128,128]{2,1,0:T(8,128)S(1)}, u32[]{:S(2)}, u32[]{:S(2)}) %collective-permute-start.35) | collective-permute-done | bytes 131104 | tf_op jit(solution)/shard_map/ppermute | solution.py:228
  69.5 0.4 collective-permute-start.37
  69.9 0.7 collective-permute-done.27.refs_4_
  70.6 1.0 collective-permute-start.33
  71.8 1.5 %collective-permute-start.29 = (f32[2,128,128]{2,1,0:T(8,128)S(1)}, f32[2,128,128]{2,1,0:T(8,128)S(1)}, u32[]{:S(2)}, u32[]{:S(2)}) collective-permute-start(f32[2,128,128]{2,1,0:T(8,128)S(1)} %collective-permute-done.25.refs_2_), channel_id=1, source_target_pairs={{0,4},{1,5},{2,6},{3,7},{4,0},{5,1},{6,2},{7,3},{8,12},{9,13},{10,... | collective-permute-start | bytes 393224 | tf_op jit(solution)/shard_map/ppermute | solution.py:228
  73.3 2.6 %collective-permute-done.37.refs_14_ = f32[2,128,128]{2,1,0:T(8,128)S(1)} collective-permute-done((f32[2,128,128]{2,1,0:T(8,128)S(1)}, f32[2,128,128]{2,1,0:T(8,128)S(1)}, u32[]{:S(2)}, u32[]{:S(2)}) %collective-permute-start.37) | collective-permute-done | bytes 131104 | tf_op jit(solution)/shard_map/ppermute | solution.py:228
  75.9 0.5 collective-permute-start.28
  76.4 0.9 collective-permute-done.33.refs_10_
  77.3 0.5 collective-permute-start.34
  77.9 0.8 collective-permute-done.38.refs_15_
  78.9 0.3 collective-permute-done.30.refs_7_
  79.2 6.8 %apply.3 = (f32[640,128]{1,0:T(8,128)S(1)}, f32[648,128]{1,0:T(8,128)S(1)}, f32[264,128]{1,0:T(8,128)S(1)}, f32[264,128]{1,0:T(8,128)S(1)}, f32[128,128]{1,0:T(8...) custom-call(s32[16]{0:T(128)S(1)} %get-tuple-element.44.pick_ref, s32[16]{0:T(128)S(1)} %get-tuple-element.45.mine_ref, ...), custom_call_target="tpu_custom_call" | custom-call | tf_op jit(solution)/shard_map/apply/pallas_call | solution.py:202
  86.0 0.2 collective-permute-start.39
  86.2 1.1 collective-permute-start.40
  87.3 0.7 collective-permute-start.41
  88.0 1.2 %collective-permute-start.42 = (f32[128,128]{1,0:T(8,128)S(1)}, f32[128,128]{1,0:T(8,128)S(1)}, u32[]{:S(2)}, u32[]{:S(2)}) collective-permute-start(f32[128,128]{1,0:T(8,128)S(1)} %get-tuple-element.73), channel_id=1, source_target_pairs={{0,4},{1,5},{2,6},{3,7},{4,0},{5,1},{6,2},{7,3},{8,12},{9,13},{10,... | collective-permute-start | bytes 196616 | tf_op jit(solution)/shard_map/ppermute | solution.py:228
  89.2 0.6 collective-permute-start.43
  89.7 2.9 %collective-permute-done.42.column_ref = f32[128,128]{1,0:T(8,128)S(1)} collective-permute-done((f32[128,128]{1,0:T(8,128)S(1)}, f32[128,128]{1,0:T(8,128)S(1)}, u32[]{:S(2)}, u32[]{:S(2)}) %collective-permute-start.42) | collective-permute-done | bytes 65568 | tf_op jit(solution)/shard_map/ppermute | solution.py:228
  92.7 0.9 collective-permute-done.43.column_far_ref
  93.5 0.9 collective-permute-done.41.row_far_ref
  94.4 0.7 fold.3
  95.1 1.0 collective-permute-start.45
  96.2 2.5 %collective-permute-start.46 = (f32[264,128]{1,0:T(8,128)S(1)}, f32[264,128]{1,0:T(8,128)S(1)}, u32[]{:S(2)}, u32[]{:S(2)}) collective-permute-start(f32[264,128]{1,0:T(8,128)S(1)} %get-tuple-element.80), channel_id=1, source_target_pairs={{0,12},{1,13},{2,14},{3,15},{4,8},{5,9},{6,10},{7,11},{8,4},{9,5},... | collective-permute-start | bytes 405512 | tf_op jit(solution)/shard_map/ppermute | solution.py:228
  98.7 1.5 %collective-permute-start.44 = (f32[2,128,128]{2,1,0:T(8,128)S(1)}, f32[2,128,128]{2,1,0:T(8,128)S(1)}, u32[]{:S(2)}, u32[]{:S(2)}) collective-permute-start(f32[2,128,128]{2,1,0:T(8,128)S(1)} %get-tuple-element.76), channel_id=1, source_target_pairs={{0,2},{1,3},{2,0},{3,1},{4,6},{5,7},{6,4},{7,5},{8,10},{9,11},{10,... | collective-permute-start | bytes 393224 | tf_op jit(solution)/shard_map/ppermute | solution.py:228
  100.2 3.8 %collective-permute-done.44.step_ref = f32[2,128,128]{2,1,0:T(8,128)S(1)} collective-permute-done((f32[2,128,128]{2,1,0:T(8,128)S(1)}, f32[2,128,128]{2,1,0:T(8,128)S(1)}, u32[]{:S(2)}, u32[]{:S(2)}) %collective-permute-start.44) | collective-permute-done | bytes 131104 | tf_op jit(solution)/shard_map/ppermute | solution.py:228
  104.0 4.4 %collective-permute-done.45.refs_1_ = f32[264,128]{1,0:T(8,128)S(1)} collective-permute-done((f32[264,128]{1,0:T(8,128)S(1)}, f32[264,128]{1,0:T(8,128)S(1)}, u32[]{:S(2)}, u32[]{:S(2)}) %collective-permute-start.45) | collective-permute-done | bytes 135200 | tf_op jit(solution)/shard_map/ppermute | solution.py:228
  108.4 0.8 collective-permute-done.47.refs_3_
  109.1 0.9 last.1
  110.0 11.0 %all_to_all.5.tiles_ref = f32[16,8,128]{2,1,0:T(8,128)S(1)} all-to-all(f32[16,8,128]{2,1,0:T(8,128)S(1)} %broadcast_in_dim.2), channel_id=1, replica_groups=mesh['group'=2,'term'=16] {'term'}, dimensions={0} | all-to-all | bytes 131072 | tf_op jit(solution)/shard_map/all_to_all | solution.py:369
  121.0 0.9 norm.1
  (49 shorter events, 1.3 us)
Async XLA Ops:
  0.6 14.3 %collective-permute-start.11 = (f32[2,128,128]{2,1,0:T(8,128)}, f32[2,128,128]{2,1,0:T(8,128)S(1)}, u32[]{:S(2)}, u32[]{:S(2)}) collective-permute-start(f32[2,128,128]{2,1,0:T(8,128)} %vector_in.1), channel_id=1, source_target_pairs={{0,8},{1,9},{2,10},{3,11},{4,12},{5,13},{6,14},{7,15},{8,0},{9,1},... | collective-permute-start | bytes 393224 | tf_op jit(solution)/shard_map/ppermute | solution.py:228
  4.7 12.0 %collective-permute-start.7 = (f32[2,128,128]{2,1,0:T(8,128)}, f32[2,128,128]{2,1,0:T(8,128)S(1)}, u32[]{:S(2)}, u32[]{:S(2)}) collective-permute-start(f32[2,128,128]{2,1,0:T(8,128)} %vector_in.1), channel_id=1, source_target_pairs={{0,12},{1,13},{2,14},{3,15},{4,8},{5,9},{6,10},{7,11},{8,4},{9,5},... | collective-permute-start | bytes 393224 | tf_op jit(solution)/shard_map/ppermute | solution.py:228
  6.1 0.7 copy-start.2
  7.3 3.5 %copy-start.1 = (f32[2,128,128]{2,1,0:T(8,128)S(1)}, f32[2,128,128]{2,1,0:T(8,128)}, u32[]{:S(2)}) copy-start(f32[2,128,128]{2,1,0:T(8,128)} %vector_in.1) | copy-start | bytes 393220
  10.8 6.0 %collective-permute-start.3 = (f32[2,128,128]{2,1,0:T(8,128)S(1)}, f32[2,128,128]{2,1,0:T(8,128)S(1)}, u32[]{:S(2)}, u32[]{:S(2)}) collective-permute-start(f32[2,128,128]{2,1,0:T(8,128)S(1)} %copy-done.1), channel_id=1, source_target_pairs={{0,4},{1,5},{2,6},{3,7},{4,0},{5,1},{6,2},{7,3},{8,12},{9,13},{10,... | collective-permute-start | bytes 393224 | tf_op jit(solution)/shard_map/ppermute | solution.py:228
  11.0 7.5 %collective-permute-start.1 = (f32[2,128,128]{2,1,0:T(8,128)S(1)}, f32[2,128,128]{2,1,0:T(8,128)S(1)}, u32[]{:S(2)}, u32[]{:S(2)}) collective-permute-start(f32[2,128,128]{2,1,0:T(8,128)S(1)} %copy-done.1), channel_id=1, source_target_pairs={{0,2},{1,3},{2,0},{3,1},{4,6},{5,7},{6,4},{7,5},{8,10},{9,11},{10,... | collective-permute-start | bytes 393224 | tf_op jit(solution)/shard_map/ppermute | solution.py:228
  13.2 5.3 %collective-permute-start = (f32[2,128,128]{2,1,0:T(8,128)S(1)}, f32[2,128,128]{2,1,0:T(8,128)S(1)}, u32[]{:S(2)}, u32[]{:S(2)}) collective-permute-start(f32[2,128,128]{2,1,0:T(8,128)S(1)} %get-tuple-element.55.refs_0_.vector_ref), channel_id=1, source_target_pairs={{0,1},{1,0},{2,3},{3,2},{4,5},{5,4},{6,7},{7,6},{8,9},{9,8},{10,11... | collective-permute-start | bytes 393224 | tf_op jit(solution)/shard_map/ppermute | solution.py:228
  14.9 5.7 %collective-permute-start.13 = (f32[2,128,128]{2,1,0:T(8,128)S(1)}, f32[2,128,128]{2,1,0:T(8,128)S(1)}, u32[]{:S(2)}, u32[]{:S(2)}) collective-permute-start(f32[2,128,128]{2,1,0:T(8,128)S(1)} %collective-permute-done.11.refs_12_), channel_id=1, source_target_pairs={{0,2},{1,3},{2,0},{3,1},{4,6},{5,7},{6,4},{7,5},{8,10},{9,11},{10,... | collective-permute-start | bytes 393224 | tf_op jit(solution)/shard_map/ppermute | solution.py:228
  16.8 3.9 %collective-permute-start.12 = (f32[2,128,128]{2,1,0:T(8,128)S(1)}, f32[2,128,128]{2,1,0:T(8,128)S(1)}, u32[]{:S(2)}, u32[]{:S(2)}) collective-permute-start(f32[2,128,128]{2,1,0:T(8,128)S(1)} %collective-permute-done.11.refs_12_), channel_id=1, source_target_pairs={{0,1},{1,0},{2,3},{3,2},{4,5},{5,4},{6,7},{7,6},{8,9},{9,8},{10,11... | collective-permute-start | bytes 393224 | tf_op jit(solution)/shard_map/ppermute | solution.py:228
  16.9 5.8 %collective-permute-start.9 = (f32[2,128,128]{2,1,0:T(8,128)S(1)}, f32[2,128,128]{2,1,0:T(8,128)S(1)}, u32[]{:S(2)}, u32[]{:S(2)}) collective-permute-start(f32[2,128,128]{2,1,0:T(8,128)S(1)} %collective-permute-done.7.refs_8_), channel_id=1, source_target_pairs={{0,2},{1,3},{2,0},{3,1},{4,6},{5,7},{6,4},{7,5},{8,10},{9,11},{10,... | collective-permute-start | bytes 393224 | tf_op jit(solution)/shard_map/ppermute | solution.py:228
  18.5 4.2 %collective-permute-start.8 = (f32[2,128,128]{2,1,0:T(8,128)S(1)}, f32[2,128,128]{2,1,0:T(8,128)S(1)}, u32[]{:S(2)}, u32[]{:S(2)}) collective-permute-start(f32[2,128,128]{2,1,0:T(8,128)S(1)} %collective-permute-done.7.refs_8_), channel_id=1, source_target_pairs={{0,1},{1,0},{2,3},{3,2},{4,5},{5,4},{6,7},{7,6},{8,9},{9,8},{10,11... | collective-permute-start | bytes 393224 | tf_op jit(solution)/shard_map/ppermute | solution.py:228
  18.5 5.9 %collective-permute-start.5 = (f32[2,128,128]{2,1,0:T(8,128)S(1)}, f32[2,128,128]{2,1,0:T(8,128)S(1)}, u32[]{:S(2)}, u32[]{:S(2)}) collective-permute-start(f32[2,128,128]{2,1,0:T(8,128)S(1)} %collective-permute-done.1.refs_2_), channel_id=1, source_target_pairs={{0,4},{1,5},{2,6},{3,7},{4,0},{5,1},{6,2},{7,3},{8,12},{9,13},{10,... | collective-permute-start | bytes 393224 | tf_op jit(solution)/shard_map/ppermute | solution.py:228
  20.6 3.8 %collective-permute-start.2 = (f32[2,128,128]{2,1,0:T(8,128)S(1)}, f32[2,128,128]{2,1,0:T(8,128)S(1)}, u32[]{:S(2)}, u32[]{:S(2)}) collective-permute-start(f32[2,128,128]{2,1,0:T(8,128)S(1)} %collective-permute-done.1.refs_2_), channel_id=1, source_target_pairs={{0,1},{1,0},{2,3},{3,2},{4,5},{5,4},{6,7},{7,6},{8,9},{9,8},{10,11... | collective-permute-start | bytes 393224 | tf_op jit(solution)/shard_map/ppermute | solution.py:228
  20.6 3.8 %collective-permute-start.4 = (f32[2,128,128]{2,1,0:T(8,128)S(1)}, f32[2,128,128]{2,1,0:T(8,128)S(1)}, u32[]{:S(2)}, u32[]{:S(2)}) collective-permute-start(f32[2,128,128]{2,1,0:T(8,128)S(1)} %collective-permute-done.3.refs_4_), channel_id=1, source_target_pairs={{0,1},{1,0},{2,3},{3,2},{4,5},{5,4},{6,7},{7,6},{8,9},{9,8},{10,11... | collective-permute-start | bytes 393224 | tf_op jit(solution)/shard_map/ppermute | solution.py:228
  22.7 1.7 %collective-permute-start.14 = (f32[2,128,128]{2,1,0:T(8,128)S(1)}, f32[2,128,128]{2,1,0:T(8,128)S(1)}, u32[]{:S(2)}, u32[]{:S(2)}) collective-permute-start(f32[2,128,128]{2,1,0:T(8,128)S(1)} %collective-permute-done.13.refs_14_), channel_id=1, source_target_pairs={{0,1},{1,0},{2,3},{3,2},{4,5},{5,4},{6,7},{7,6},{8,9},{9,8},{10,11... | collective-permute-start | bytes 393224 | tf_op jit(solution)/shard_map/ppermute | solution.py:228
  22.7 1.7 %collective-permute-start.10 = (f32[2,128,128]{2,1,0:T(8,128)S(1)}, f32[2,128,128]{2,1,0:T(8,128)S(1)}, u32[]{:S(2)}, u32[]{:S(2)}) collective-permute-start(f32[2,128,128]{2,1,0:T(8,128)S(1)} %collective-permute-done.9.refs_10_), channel_id=1, source_target_pairs={{0,1},{1,0},{2,3},{3,2},{4,5},{5,4},{6,7},{7,6},{8,9},{9,8},{10,11... | collective-permute-start | bytes 393224 | tf_op jit(solution)/shard_map/ppermute | solution.py:228
  24.4 1.3 %collective-permute-start.6 = (f32[2,128,128]{2,1,0:T(8,128)S(1)}, f32[2,128,128]{2,1,0:T(8,128)S(1)}, u32[]{:S(2)}, u32[]{:S(2)}) collective-permute-start(f32[2,128,128]{2,1,0:T(8,128)S(1)} %collective-permute-done.5.refs_6_), channel_id=1, source_target_pairs={{0,1},{1,0},{2,3},{3,2},{4,5},{5,4},{6,7},{7,6},{8,9},{9,8},{10,11... | collective-permute-start | bytes 393224 | tf_op jit(solution)/shard_map/ppermute | solution.py:228
  32.4 8.5 %collective-permute-start.15 = (f32[648,128]{1,0:T(8,128)S(1)}, f32[648,128]{1,0:T(8,128)S(1)}, u32[]{:S(2)}, u32[]{:S(2)}) collective-permute-start(f32[648,128]{1,0:T(8,128)S(1)} %get-tuple-element.58.far_in), channel_id=1, source_target_pairs={{0,1},{1,0},{2,3},{3,2},{4,5},{5,4},{6,7},{7,6},{8,9},{9,8},{10,11... | collective-permute-start | bytes 995336 | tf_op jit(solution)/shard_map/ppermute | solution.py:228
  32.6 7.0 %collective-permute-start.16 = (f32[264,128]{1,0:T(8,128)S(1)}, f32[264,128]{1,0:T(8,128)S(1)}, u32[]{:S(2)}, u32[]{:S(2)}) collective-permute-start(f32[264,128]{1,0:T(8,128)S(1)} %get-tuple-element.59), channel_id=1, source_target_pairs={{0,2},{1,3},{2,0},{3,1},{4,6},{5,7},{6,4},{7,5},{8,10},{9,11},{10,... | collective-permute-start | bytes 405512 | tf_op jit(solution)/shard_map/ppermute | solution.py:228
  33.4 7.5 %collective-permute-start.17 = (f32[264,128]{1,0:T(8,128)S(1)}, f32[264,128]{1,0:T(8,128)S(1)}, u32[]{:S(2)}, u32[]{:S(2)}) collective-permute-start(f32[264,128]{1,0:T(8,128)S(1)} %get-tuple-element.60), channel_id=1, source_target_pairs={{0,3},{1,2},{2,1},{3,0},{4,7},{5,6},{6,5},{7,4},{8,11},{9,10},{10,... | collective-permute-start | bytes 405512 | tf_op jit(solution)/shard_map/ppermute | solution.py:228
  34.4 4.9 %collective-permute-start.18 = (f32[128,128]{1,0:T(8,128)S(1)}, f32[128,128]{1,0:T(8,128)S(1)}, u32[]{:S(2)}, u32[]{:S(2)}) collective-permute-start(f32[128,128]{1,0:T(8,128)S(1)} %get-tuple-element.61), channel_id=1, source_target_pairs={{0,4},{1,5},{2,6},{3,7},{4,0},{5,1},{6,2},{7,3},{8,12},{9,13},{10,... | collective-permute-start | bytes 196616 | tf_op jit(solution)/shard_map/ppermute | solution.py:228
  35.1 4.5 %collective-permute-start.19 = (f32[128,128]{1,0:T(8,128)S(1)}, f32[128,128]{1,0:T(8,128)S(1)}, u32[]{:S(2)}, u32[]{:S(2)}) collective-permute-start(f32[128,128]{1,0:T(8,128)S(1)} %get-tuple-element.62), channel_id=1, source_target_pairs={{0,5},{1,4},{2,7},{3,6},{4,1},{5,0},{6,3},{7,2},{8,13},{9,12},{10,... | collective-permute-start | bytes 196616 | tf_op jit(solution)/shard_map/ppermute | solution.py:228
  40.9 14.7 %copy-start = (f32[2,128,128]{2,1,0:T(8,128)S(1)}, f32[2,128,128]{2,1,0:T(8,128)}, u32[]{:S(2)}) copy-start(f32[2,128,128]{2,1,0:T(8,128)} %precond_ref.3) | copy-start | bytes 393220
  41.6 13.2 %collective-permute-start.21 = (f32[264,128]{1,0:T(8,128)S(1)}, f32[264,128]{1,0:T(8,128)S(1)}, u32[]{:S(2)}, u32[]{:S(2)}) collective-permute-start(f32[264,128]{1,0:T(8,128)S(1)} %get-tuple-element.67), channel_id=1, source_target_pairs={{0,8},{1,9},{2,10},{3,11},{4,12},{5,13},{6,14},{7,15},{8,0},{9,1},... | collective-permute-start | bytes 405512 | tf_op jit(solution)/shard_map/ppermute | solution.py:228
  44.1 10.7 %collective-permute-start.22 = (f32[264,128]{1,0:T(8,128)S(1)}, f32[264,128]{1,0:T(8,128)S(1)}, u32[]{:S(2)}, u32[]{:S(2)}) collective-permute-start(f32[264,128]{1,0:T(8,128)S(1)} %get-tuple-element.68), channel_id=1, source_target_pairs={{0,12},{1,13},{2,14},{3,15},{4,8},{5,9},{6,10},{7,11},{8,4},{9,5},... | collective-permute-start | bytes 405512 | tf_op jit(solution)/shard_map/ppermute | solution.py:228
  45.4 10.2 %collective-permute-start.23 = (f32[264,128]{1,0:T(8,128)S(1)}, f32[264,128]{1,0:T(8,128)S(1)}, u32[]{:S(2)}, u32[]{:S(2)}) collective-permute-start(f32[264,128]{1,0:T(8,128)S(1)} %get-tuple-element.66.refs_0_), channel_id=1, source_target_pairs={{0,4},{1,5},{2,6},{3,7},{4,0},{5,1},{6,2},{7,3},{8,12},{9,13},{10,... | collective-permute-start | bytes 405512 | tf_op jit(solution)/shard_map/ppermute | solution.py:228
  45.9 5.1 %collective-permute-start.20 = (f32[2,128,128]{2,1,0:T(8,128)S(1)}, f32[2,128,128]{2,1,0:T(8,128)S(1)}, u32[]{:S(2)}, u32[]{:S(2)}) collective-permute-start(f32[2,128,128]{2,1,0:T(8,128)S(1)} %get-tuple-element.64), channel_id=1, source_target_pairs={{0,2},{1,3},{2,0},{3,1},{4,6},{5,7},{6,4},{7,5},{8,10},{9,11},{10,... | collective-permute-start | bytes 393224 | tf_op jit(solution)/shard_map/ppermute | solution.py:228
  55.8 13.7 %collective-permute-start.35 = (f32[2,128,128]{2,1,0:T(8,128)S(1)}, f32[2,128,128]{2,1,0:T(8,128)S(1)}, u32[]{:S(2)}, u32[]{:S(2)}) collective-permute-start(f32[2,128,128]{2,1,0:T(8,128)S(1)} %step.1.refs_0_.vector_ref), channel_id=1, source_target_pairs={{0,8},{1,9},{2,10},{3,11},{4,12},{5,13},{6,14},{7,15},{8,0},{9,1},... | collective-permute-start | bytes 393224 | tf_op jit(solution)/shard_map/ppermute | solution.py:228
  59.9 10.0 %collective-permute-start.31 = (f32[2,128,128]{2,1,0:T(8,128)S(1)}, f32[2,128,128]{2,1,0:T(8,128)S(1)}, u32[]{:S(2)}, u32[]{:S(2)}) collective-permute-start(f32[2,128,128]{2,1,0:T(8,128)S(1)} %step.1.refs_0_.vector_ref), channel_id=1, source_target_pairs={{0,12},{1,13},{2,14},{3,15},{4,8},{5,9},{6,10},{7,11},{8,4},{9,5},... | collective-permute-start | bytes 393224 | tf_op jit(solution)/shard_map/ppermute | solution.py:228
  60.3 10.3 %collective-permute-start.27 = (f32[2,128,128]{2,1,0:T(8,128)S(1)}, f32[2,128,128]{2,1,0:T(8,128)S(1)}, u32[]{:S(2)}, u32[]{:S(2)}) collective-permute-start(f32[2,128,128]{2,1,0:T(8,128)S(1)} %step.1.refs_0_.vector_ref), channel_id=1, source_target_pairs={{0,4},{1,5},{2,6},{3,7},{4,0},{5,1},{6,2},{7,3},{8,12},{9,13},{10,... | collective-permute-start | bytes 393224 | tf_op jit(solution)/shard_map/ppermute | solution.py:228
  60.5 11.1 %collective-permute-start.25 = (f32[2,128,128]{2,1,0:T(8,128)S(1)}, f32[2,128,128]{2,1,0:T(8,128)S(1)}, u32[]{:S(2)}, u32[]{:S(2)}) collective-permute-start(f32[2,128,128]{2,1,0:T(8,128)S(1)} %step.1.refs_0_.vector_ref), channel_id=1, source_target_pairs={{0,2},{1,3},{2,0},{3,1},{4,6},{5,7},{6,4},{7,5},{8,10},{9,11},{10,... | collective-permute-start | bytes 393224 | tf_op jit(solution)/shard_map/ppermute | solution.py:228
  61.1 10.7 %collective-permute-start.24 = (f32[2,128,128]{2,1,0:T(8,128)S(1)}, f32[2,128,128]{2,1,0:T(8,128)S(1)}, u32[]{:S(2)}, u32[]{:S(2)}) collective-permute-start(f32[2,128,128]{2,1,0:T(8,128)S(1)} %step.1.refs_0_.vector_ref), channel_id=1, source_target_pairs={{0,1},{1,0},{2,3},{3,2},{4,5},{5,4},{6,7},{7,6},{8,9},{9,8},{10,11... | collective-permute-start | bytes 393224 | tf_op jit(solution)/shard_map/ppermute | solution.py:228
  69.5 6.4 %collective-permute-start.37 = (f32[2,128,128]{2,1,0:T(8,128)S(1)}, f32[2,128,128]{2,1,0:T(8,128)S(1)}, u32[]{:S(2)}, u32[]{:S(2)}) collective-permute-start(f32[2,128,128]{2,1,0:T(8,128)S(1)} %collective-permute-done.35.refs_12_), channel_id=1, source_target_pairs={{0,2},{1,3},{2,0},{3,1},{4,6},{5,7},{6,4},{7,5},{8,10},{9,11},{10,... | collective-permute-start | bytes 393224 | tf_op jit(solution)/shard_map/ppermute | solution.py:228
  69.9 6.0 %collective-permute-start.36 = (f32[2,128,128]{2,1,0:T(8,128)S(1)}, f32[2,128,128]{2,1,0:T(8,128)S(1)}, u32[]{:S(2)}, u32[]{:S(2)}) collective-permute-start(f32[2,128,128]{2,1,0:T(8,128)S(1)} %collective-permute-done.35.refs_12_), channel_id=1, source_target_pairs={{0,1},{1,0},{2,3},{3,2},{4,5},{5,4},{6,7},{7,6},{8,9},{9,8},{10,11... | collective-permute-start | bytes 393224 | tf_op jit(solution)/shard_map/ppermute | solution.py:228
  70.6 6.7 %collective-permute-start.33 = (f32[2,128,128]{2,1,0:T(8,128)S(1)}, f32[2,128,128]{2,1,0:T(8,128)S(1)}, u32[]{:S(2)}, u32[]{:S(2)}) collective-permute-start(f32[2,128,128]{2,1,0:T(8,128)S(1)} %collective-permute-done.31.refs_8_), channel_id=1, source_target_pairs={{0,2},{1,3},{2,0},{3,1},{4,6},{5,7},{6,4},{7,5},{8,10},{9,11},{10,... | collective-permute-start | bytes 393224 | tf_op jit(solution)/shard_map/ppermute | solution.py:228
  71.6 5.7 %collective-permute-start.32 = (f32[2,128,128]{2,1,0:T(8,128)S(1)}, f32[2,128,128]{2,1,0:T(8,128)S(1)}, u32[]{:S(2)}, u32[]{:S(2)}) collective-permute-start(f32[2,128,128]{2,1,0:T(8,128)S(1)} %collective-permute-done.31.refs_8_), channel_id=1, source_target_pairs={{0,1},{1,0},{2,3},{3,2},{4,5},{5,4},{6,7},{7,6},{8,9},{9,8},{10,11... | collective-permute-start | bytes 393224 | tf_op jit(solution)/shard_map/ppermute | solution.py:228
  71.8 6.1 %collective-permute-start.29 = (f32[2,128,128]{2,1,0:T(8,128)S(1)}, f32[2,128,128]{2,1,0:T(8,128)S(1)}, u32[]{:S(2)}, u32[]{:S(2)}) collective-permute-start(f32[2,128,128]{2,1,0:T(8,128)S(1)} %collective-permute-done.25.refs_2_), channel_id=1, source_target_pairs={{0,4},{1,5},{2,6},{3,7},{4,0},{5,1},{6,2},{7,3},{8,12},{9,13},{10,... | collective-permute-start | bytes 393224 | tf_op jit(solution)/shard_map/ppermute | solution.py:228
  75.9 2.0 %collective-permute-start.26 = (f32[2,128,128]{2,1,0:T(8,128)S(1)}, f32[2,128,128]{2,1,0:T(8,128)S(1)}, u32[]{:S(2)}, u32[]{:S(2)}) collective-permute-start(f32[2,128,128]{2,1,0:T(8,128)S(1)} %collective-permute-done.25.refs_2_), channel_id=1, source_target_pairs={{0,1},{1,0},{2,3},{3,2},{4,5},{5,4},{6,7},{7,6},{8,9},{9,8},{10,11... | collective-permute-start | bytes 393224 | tf_op jit(solution)/shard_map/ppermute | solution.py:228
  75.9 2.0 %collective-permute-start.28 = (f32[2,128,128]{2,1,0:T(8,128)S(1)}, f32[2,128,128]{2,1,0:T(8,128)S(1)}, u32[]{:S(2)}, u32[]{:S(2)}) collective-permute-start(f32[2,128,128]{2,1,0:T(8,128)S(1)} %collective-permute-done.27.refs_4_), channel_id=1, source_target_pairs={{0,1},{1,0},{2,3},{3,2},{4,5},{5,4},{6,7},{7,6},{8,9},{9,8},{10,11... | collective-permute-start | bytes 393224 | tf_op jit(solution)/shard_map/ppermute | solution.py:228
  77.3 1.3 %collective-permute-start.38 = (f32[2,128,128]{2,1,0:T(8,128)S(1)}, f32[2,128,128]{2,1,0:T(8,128)S(1)}, u32[]{:S(2)}, u32[]{:S(2)}) collective-permute-start(f32[2,128,128]{2,1,0:T(8,128)S(1)} %collective-permute-done.37.refs_14_), channel_id=1, source_target_pairs={{0,1},{1,0},{2,3},{3,2},{4,5},{5,4},{6,7},{7,6},{8,9},{9,8},{10,11... | collective-permute-start | bytes 393224 | tf_op jit(solution)/shard_map/ppermute | solution.py:228
  77.3 1.5 %collective-permute-start.34 = (f32[2,128,128]{2,1,0:T(8,128)S(1)}, f32[2,128,128]{2,1,0:T(8,128)S(1)}, u32[]{:S(2)}, u32[]{:S(2)}) collective-permute-start(f32[2,128,128]{2,1,0:T(8,128)S(1)} %collective-permute-done.33.refs_10_), channel_id=1, source_target_pairs={{0,1},{1,0},{2,3},{3,2},{4,5},{5,4},{6,7},{7,6},{8,9},{9,8},{10,11... | collective-permute-start | bytes 393224 | tf_op jit(solution)/shard_map/ppermute | solution.py:228
  77.8 1.3 %collective-permute-start.30 = (f32[2,128,128]{2,1,0:T(8,128)S(1)}, f32[2,128,128]{2,1,0:T(8,128)S(1)}, u32[]{:S(2)}, u32[]{:S(2)}) collective-permute-start(f32[2,128,128]{2,1,0:T(8,128)S(1)} %collective-permute-done.29.refs_6_), channel_id=1, source_target_pairs={{0,1},{1,0},{2,3},{3,2},{4,5},{5,4},{6,7},{7,6},{8,9},{9,8},{10,11... | collective-permute-start | bytes 393224 | tf_op jit(solution)/shard_map/ppermute | solution.py:228
  86.0 8.4 %collective-permute-start.39 = (f32[648,128]{1,0:T(8,128)S(1)}, f32[648,128]{1,0:T(8,128)S(1)}, u32[]{:S(2)}, u32[]{:S(2)}) collective-permute-start(f32[648,128]{1,0:T(8,128)S(1)} %get-tuple-element.70.far_in), channel_id=1, source_target_pairs={{0,1},{1,0},{2,3},{3,2},{4,5},{5,4},{6,7},{7,6},{8,9},{9,8},{10,11... | collective-permute-start | bytes 995336 | tf_op jit(solution)/shard_map/ppermute | solution.py:228
  86.2 7.3 %collective-permute-start.40 = (f32[264,128]{1,0:T(8,128)S(1)}, f32[264,128]{1,0:T(8,128)S(1)}, u32[]{:S(2)}, u32[]{:S(2)}) collective-permute-start(f32[264,128]{1,0:T(8,128)S(1)} %get-tuple-element.71), channel_id=1, source_target_pairs={{0,2},{1,3},{2,0},{3,1},{4,6},{5,7},{6,4},{7,5},{8,10},{9,11},{10,... | collective-permute-start | bytes 405512 | tf_op jit(solution)/shard_map/ppermute | solution.py:228
  87.3 7.1 %collective-permute-start.41 = (f32[264,128]{1,0:T(8,128)S(1)}, f32[264,128]{1,0:T(8,128)S(1)}, u32[]{:S(2)}, u32[]{:S(2)}) collective-permute-start(f32[264,128]{1,0:T(8,128)S(1)} %get-tuple-element.72), channel_id=1, source_target_pairs={{0,3},{1,2},{2,1},{3,0},{4,7},{5,6},{6,5},{7,4},{8,11},{9,10},{10,... | collective-permute-start | bytes 405512 | tf_op jit(solution)/shard_map/ppermute | solution.py:228
  88.0 4.7 %collective-permute-start.42 = (f32[128,128]{1,0:T(8,128)S(1)}, f32[128,128]{1,0:T(8,128)S(1)}, u32[]{:S(2)}, u32[]{:S(2)}) collective-permute-start(f32[128,128]{1,0:T(8,128)S(1)} %get-tuple-element.73), channel_id=1, source_target_pairs={{0,4},{1,5},{2,6},{3,7},{4,0},{5,1},{6,2},{7,3},{8,12},{9,13},{10,... | collective-permute-start | bytes 196616 | tf_op jit(solution)/shard_map/ppermute | solution.py:228
  89.2 4.3 %collective-permute-start.43 = (f32[128,128]{1,0:T(8,128)S(1)}, f32[128,128]{1,0:T(8,128)S(1)}, u32[]{:S(2)}, u32[]{:S(2)}) collective-permute-start(f32[128,128]{1,0:T(8,128)S(1)} %get-tuple-element.74), channel_id=1, source_target_pairs={{0,5},{1,4},{2,7},{3,6},{4,1},{5,0},{6,3},{7,2},{8,13},{9,12},{10,... | collective-permute-start | bytes 196616 | tf_op jit(solution)/shard_map/ppermute | solution.py:228
  95.1 13.2 %collective-permute-start.45 = (f32[264,128]{1,0:T(8,128)S(1)}, f32[264,128]{1,0:T(8,128)S(1)}, u32[]{:S(2)}, u32[]{:S(2)}) collective-permute-start(f32[264,128]{1,0:T(8,128)S(1)} %get-tuple-element.79), channel_id=1, source_target_pairs={{0,8},{1,9},{2,10},{3,11},{4,12},{5,13},{6,14},{7,15},{8,0},{9,1},... | collective-permute-start | bytes 405512 | tf_op jit(solution)/shard_map/ppermute | solution.py:228
  96.2 12.2 %collective-permute-start.46 = (f32[264,128]{1,0:T(8,128)S(1)}, f32[264,128]{1,0:T(8,128)S(1)}, u32[]{:S(2)}, u32[]{:S(2)}) collective-permute-start(f32[264,128]{1,0:T(8,128)S(1)} %get-tuple-element.80), channel_id=1, source_target_pairs={{0,12},{1,13},{2,14},{3,15},{4,8},{5,9},{6,10},{7,11},{8,4},{9,5},... | collective-permute-start | bytes 405512 | tf_op jit(solution)/shard_map/ppermute | solution.py:228
  98.7 10.5 %collective-permute-start.47 = (f32[264,128]{1,0:T(8,128)S(1)}, f32[264,128]{1,0:T(8,128)S(1)}, u32[]{:S(2)}, u32[]{:S(2)}) collective-permute-start(f32[264,128]{1,0:T(8,128)S(1)} %get-tuple-element.78.refs_0_), channel_id=1, source_target_pairs={{0,4},{1,5},{2,6},{3,7},{4,0},{5,1},{6,2},{7,3},{8,12},{9,13},{10,... | collective-permute-start | bytes 405512 | tf_op jit(solution)/shard_map/ppermute | solution.py:228
  98.7 5.3 %collective-permute-start.44 = (f32[2,128,128]{2,1,0:T(8,128)S(1)}, f32[2,128,128]{2,1,0:T(8,128)S(1)}, u32[]{:S(2)}, u32[]{:S(2)}) collective-permute-start(f32[2,128,128]{2,1,0:T(8,128)S(1)} %get-tuple-element.76), channel_id=1, source_target_pairs={{0,2},{1,3},{2,0},{3,1},{4,6},{5,7},{6,4},{7,5},{8,10},{9,11},{10,... | collective-permute-start | bytes 393224 | tf_op jit(solution)/shard_map/ppermute | solution.py:228

commit v6 on v5

--- a/solution.py
+++ b/solution.py
@@ -9,6 +9,7 @@
 
 ITERS = 2
 CORE, ROW, COLUMN = 1, 2, 4
+LAST = 5
 SENDERS = 6
 SMEM = pl.BlockSpec(memory_space=pltpu.SMEM)
 VMEM = pl.BlockSpec(memory_space=pltpu.VMEM)
@@ -136,20 +137,11 @@
     )(me, at_home(fetch), at_home(store), at_home(pairs), live, at_home(vector), at_home(left_ops), at_home(right_ops))
 
 
-def nearest_last(n):
-    return [*range(8), *(r for k in reversed(range(8, n, 4)) for r in range(k, k + 4))]
-
-
-def apply_kernel(n, over_rows, rows, start, pick_ref, mine_ref, first_ref, second_ref, dst_ref, one_ref, two_ref, count_ref,
-                 l4_ref, rr_ref, *refs):
-    pieces = [refs[nearest_last(n).index(k)] for k in range(n)]
-    near_ref, far_ref, row_ref, row_far_ref, column_ref, column_far_ref, square_ref, block, total = refs[n:]
+def left_products(chunks, rows, start, pick_ref, l4_ref, pieces, block):
     terms, width = l4_ref.shape[:2]
     square = jnp.zeros((8, width), jnp.float32)
-    product = jnp.zeros((8, width), jnp.float32)
-    block[terms * n] = jnp.zeros((rows, width), jnp.float32)
     left = l4_ref[:, start:start + rows, :].reshape(terms * rows, 4 * width)
-    for c in range(n // 2):
+    for c in chunks:
         columns = []
         for r in (2 * c, 2 * c + 1):
             high, low = halves(pieces[r][pick_ref[r]])
@@ -160,6 +152,41 @@
         for k in range(2):
             at = (2 * c + k) * terms
             block[at:at + terms] = both[:, k * width:(k + 1) * width].reshape(terms, rows, width)
+    return square
+
+
+def early_kernel(chunks, rows, pick_ref, l4_ref, *refs):
+    pieces, (square_ref, block) = dict(zip([r for c in chunks for r in (2 * c, 2 * c + 1)], refs[:-2])), refs[-2:]
+    square_ref[...] = left_products(chunks, rows, 0, pick_ref, l4_ref, pieces, block)
+
+
+def early(n, tables, pieces):
+    terms, width = tables[0].shape[:2]
+    chunks = [c for c in range(n // 2) if c != LAST]
+    spare = tables[7].shape[0] // 3
+    return pl.pallas_call(
+        functools.partial(early_kernel, chunks, width),
+        out_shape=(jax.ShapeDtypeStruct((8, width), jnp.float32),
+                   pltpu.VMEM((terms * n + 1 + spare, width, width), jnp.float32)),
+        in_specs=[SMEM] + [VMEM] * (1 + 2 * len(chunks)),
+        out_specs=[VMEM] * 2,
+        compiler_params=params(12),
+        name="early",
+    )(tables[2], tables[0], *(pieces[r] for c in chunks for r in (2 * c, 2 * c + 1)))
+
+
+def apply_kernel(n, over_rows, rows, start, chunks, pick_ref, mine_ref, first_ref, second_ref, dst_ref, one_ref, two_ref,
+                 count_ref, l4_ref, rr_ref, *refs):
+    pieces, refs = refs[:n], refs[n:]
+    if len(chunks) < n // 2:
+        done_ref, refs = refs[0], refs[2:]
+    near_ref, far_ref, row_ref, row_far_ref, column_ref, column_far_ref, square_ref, block, total = refs
+    terms, width = l4_ref.shape[:2]
+    product = jnp.zeros((8, width), jnp.float32)
+    block[terms * n] = jnp.zeros((rows, width), jnp.float32)
+    square = left_products(chunks, rows, start, pick_ref, l4_ref, pieces, block)
+    if len(chunks) < n // 2:
+        square = square + done_ref[...]
     square_ref[...] = square
 
     def add(i, carry):
@@ -194,24 +221,27 @@
         ref[ref.shape[0] - 8:, :] = product
 
 
-def apply(n, over_rows, rows, start, tables, pieces):
+def apply(n, over_rows, rows, start, tables, pieces, done):
     terms, width = tables[0].shape[:2]
     spare = tables[7].shape[0] // 3
     late = n // 2 - 1 - len(over_rows)
+    chunks = [LAST] if done else range(n // 2)
     shape = lambda *dims: jax.ShapeDtypeStruct(dims, jnp.float32)
+    block = pltpu.VMEM((terms * n + 1 + spare, rows, width), jnp.float32)
+    total = pltpu.VMEM((n, rows, 2 * terms * width), jnp.bfloat16)
+    if done:
+        done = (done[0], pltpu.with_memory_space_constraint(done[1], pltpu.VMEM))
     return pl.pallas_call(
-        functools.partial(apply_kernel, n, over_rows, rows, start),
+        functools.partial(apply_kernel, n, over_rows, rows, start, chunks),
         out_shape=(shape(late * rows, width), shape(late * rows + 8, width)) + (shape(len(over_rows) * rows + 8, width),) * 2
-        + (shape(rows, width),) * 2 + (shape(8, width),),
-        in_specs=[SMEM] * 8 + [VMEM] * (2 + n),
-        out_specs=[VMEM] * 7,
-        scratch_shapes=[
-            pltpu.VMEM((terms * n + 1 + spare, rows, width), jnp.float32),
-            pltpu.VMEM((n, rows, 2 * terms * width), jnp.bfloat16),
-        ],
-        compiler_params=params(32 if n <= 16 else 56),
+        + (shape(rows, width),) * 2 + (shape(8, width),) + ((block,) if done else ()),
+        in_specs=[SMEM] * 8 + [VMEM] * (2 + n + len(done)),
+        out_specs=[VMEM] * (8 if done else 7),
+        scratch_shapes=[total] if done else [block, total],
+        input_output_aliases={8 + 2 + n + 1: 7} if done else {},
+        compiler_params=params(20 if n <= 16 else 56),
         name="apply",
-    )(*tables[2:4], *tables[5:], *tables[:2], *(pieces[k] for k in nearest_last(n)))
+    )(*tables[2:4], *tables[5:], *tables[:2], *pieces, *done)
 
 
 def joined(parts, count):
@@ -312,14 +342,14 @@
     out_ref[...] = corrected_ref[...] * scale
 
 
-def scattered(n, tables, pieces):
+def scattered(n, tables, pieces, done):
     width = pieces[0].shape[1]
     chips = n // 2
     rows = width if n <= 16 else width // 4
     over_rows = list(range(chips - 1, 3, -2))
     late = [g for g in range(chips) if g != 3 and g not in over_rows]
     shape = lambda *dims: jax.ShapeDtypeStruct(dims, jnp.float32)
-    runs = [apply(n, over_rows, rows, start, tables, pieces) for start in range(0, width, rows)]
+    runs = [apply(n, over_rows, rows, start, tables, pieces, done) for start in range(0, width, rows)]
     counts = (len(late), len(late), len(over_rows), len(over_rows), 1, 1)
     near, far, row, row_far, column, column_far = (joined([x[i] for x in runs], k) for i, k in enumerate(counts))
     square = functools.reduce(jnp.add, [x[6] for x in runs])
@@ -332,20 +362,26 @@
     return square, (own, swapped(step, ROW)), [sends[0], *came]
 
 
-def gathered(n, x, held=None):
+def gathered(n, x, tables, held=None):
     pieces = {0: x}
-    for k in range(8, n, 4):
+    for k in reversed(range(8, n, 4)):
         pieces[k] = swapped(x, k)
     if held is not None:
         x, pieces[0] = lax.optimization_barrier((x, held))
     pieces[COLUMN] = swapped(x, COLUMN)
     pieces[ROW] = swapped(x, ROW)
-    for k in range(8, n, 4):
+    for k in reversed(range(8, n, 4)):
         pieces[k + ROW] = swapped(pieces[k], ROW)
     pieces[COLUMN + ROW] = swapped(pieces[ROW], COLUMN)
     for k in range(0, n, 2):
-        pieces[k + CORE] = swapped(pieces[k], CORE)
-    return [pieces[k] for k in range(n)]
+        if k != 2 * LAST:
+            pieces[k + CORE] = swapped(pieces[k], CORE)
+    done = ()
+    if n <= 16:
+        done = early(n, tables, pieces)
+        pieces[2 * LAST], *done = lax.optimization_barrier((pieces[2 * LAST], *done))
+    pieces[2 * LAST + CORE] = swapped(pieces[2 * LAST], CORE)
+    return [pieces[k] for k in range(n)], done
 
 
 def shards(wavefn, left_ops, right_ops, precond, fetch_map, store_map, pair_list, live_count):
@@ -358,9 +394,9 @@
     tile = jax.ShapeDtypeStruct((8, width), jnp.float32)
     vector = wavefn
     for iteration in range(ITERS):
-        pieces = gathered(n, vector, held if iteration == 0 else None)
+        pieces, done = gathered(n, vector, tables, held if iteration == 0 else None)
         vector = pieces[0]
-        square, sums, parts = scattered(n, tables, pieces)
+        square, sums, parts = scattered(n, tables, pieces, done)
         arrays = (*sums, square, vector, precond, *parts)
         if iteration < ITERS - 1:
             vector = local(step_kernel, "step", block, (), arrays)

time: 122 us -> 128 us (1.049)
  waiting for transfers between devices: 49.1 us -> 52.8 us
  Pallas kernels: 20.3 us -> 22.5 us
  starting transfers between devices: 39.5 us -> 37.9 us
    ppermute x48, waiting for transfers between devices: 49.1 us -> 52.8 us  [swapped(): return lax.ppermute(x, 'term', [(i, i ^ k) for i in range(n)])]
    pallas_call x2 -> x4, Pallas kernels: 13.5 us -> 15.2 us  [the longest x2 9.92 us: apply(): pl.pallas_call(functools.partial(apply_kernel, n, over_rows, rows, start,...]
    ppermute x48, starting transfers between devices: 39.5 us -> 37.9 us  [swapped(): return lax.ppermute(x, 'term', [(i, i ^ k) for i in range(n)])]
  transfers between devices with their start and end apart: 48 -> 48, of which waited for: 25 -> 23; matrix products, arithmetic and copies ran while one was open for 0% -> 1% of each run, Pallas kernels for 3% -> 7%
where the time goes in v6:
time: 128 us
  waiting for transfers between devices  52.8 us (41%)
  starting transfers between devices  37.9 us (30%)
  Pallas kernels  22.5 us (18%)
  blocking collectives  12.1 us (9%)
  between operations  1.42 us (1%)
    ppermute x48, waiting for transfers between devices, swapped(): return lax.ppermute(x, 'term', [(i, i ^ k) for i in range(n)])  52.8 us
    ppermute x48, starting transfers between devices, swapped(): return lax.ppermute(x, 'term', [(i, i ^ k) for i in range(n)])  37.9 us
    all_to_all x1, blocking collectives, shards(): lax.all_to_all(jnp.broadcast_to(partial[None], (n, 8, width)), 'term', sp...  12.1 us
    pallas_call x2, Pallas kernels, apply(): pl.pallas_call(functools.partial(apply_kernel, n, over_rows, rows, start,...  9.92 us
    pallas_call x2, Pallas kernels, early(): pl.pallas_call(functools.partial(early_kernel, chunks, width), out_shape=...  5.31 us
    pallas_call x1, Pallas kernels, prep(): pl.pallas_call(functools.partial(prep_kernel, n, terms * n + 1), out_shap...  3.98 us
    pallas_call x5, Pallas kernels, local(): pl.pallas_call(kernel, out_shape=out_shape, in_specs=[SMEM] * len(scalars...  3.33 us
  transfers between devices with their start and end apart: 48, of which 23 were waited for; matrix products, arithmetic and copies ran while one was open for 1% of the time, Pallas kernels for 7%

profile of v6, /device:TPU:0, one launch (start us, length us, event | category | flops | bytes accessed | tf_op | source)
XLA Modules:
  0.0 128.0 jit_solution(7510743045985836444)
XLA Ops:
  0.6 5.1 %collective-permute-start.10 = (f32[2,128,128]{2,1,0:T(8,128)}, f32[2,128,128]{2,1,0:T(8,128)S(1)}, u32[]{:S(2)}, u32[]{:S(2)}) collective-permute-start(f32[2,128,128]{2,1,0:T(8,128)} %vector_in.1), channel_id=1, source_target_pairs={{0,12},{1,13},{2,14},{3,15},{4,8},{5,9},{6,10},{7,11},{8,4},{9,5},... | collective-permute-start | bytes 393224 | tf_op jit(solution)/shard_map/ppermute | solution.py:258
  6.4 1.3 copy.14
  7.7 4.0 %prep.1 = (bf16[8,128,512]{2,1,0:T(8,128)(2,1)S(1)}, bf16[2048,256]{1,0:T(8,128)(2,1)S(1)}, s32[16]{0:T(128)S(1)}, s32[16]{0:T(128)S(1)}, s32[48]{0:T(128)S(1)},...) custom-call(s32[1]{0:T(128)} %bitcast.me_ref, ...), custom_call_target="tpu_custom_call" | custom-call | tf_op jit(solution)/shard_map/prep/pallas_call | solution.py:114
  11.7 1.8 %collective-permute-start.1 = (f32[2,128,128]{2,1,0:T(8,128)}, f32[2,128,128]{2,1,0:T(8,128)S(1)}, u32[]{:S(2)}, u32[]{:S(2)}) collective-permute-start(f32[2,128,128]{2,1,0:T(8,128)} %vector_in.1), channel_id=1, source_target_pairs={{0,2},{1,3},{2,0},{3,1},{4,6},{5,7},{6,4},{7,5},{8,10},{9,11},{10,... | collective-permute-start | bytes 393224 | tf_op jit(solution)/shard_map/ppermute | solution.py:258
  13.5 0.3 collective-permute-start.3
  13.8 3.3 %collective-permute-done.7.refs_8_ = f32[2,128,128]{2,1,0:T(8,128)S(1)} collective-permute-done((f32[2,128,128]{2,1,0:T(8,128)}, f32[2,128,128]{2,1,0:T(8,128)S(1)}, u32[]{:S(2)}, u32[]{:S(2)}) %collective-permute-start.7) | collective-permute-done | bytes 131104 | tf_op jit(solution)/shard_map/ppermute | solution.py:258
  17.2 0.4 collective-permute-done.1.refs_2_
  17.6 1.8 %collective-permute-done.3.refs_4_ = f32[2,128,128]{2,1,0:T(8,128)S(1)} collective-permute-done((f32[2,128,128]{2,1,0:T(8,128)}, f32[2,128,128]{2,1,0:T(8,128)S(1)}, u32[]{:S(2)}, u32[]{:S(2)}) %collective-permute-start.3) | collective-permute-done | bytes 131104 | tf_op jit(solution)/shard_map/ppermute | solution.py:258
  19.4 0.5 collective-permute-start.2
  20.0 0.4 collective-permute-start.13
  20.4 2.7 %collective-permute-done.5.refs_6_ = f32[2,128,128]{2,1,0:T(8,128)S(1)} collective-permute-done((f32[2,128,128]{2,1,0:T(8,128)S(1)}, f32[2,128,128]{2,1,0:T(8,128)S(1)}, u32[]{:S(2)}, u32[]{:S(2)}) %collective-permute-start.5) | collective-permute-done | bytes 131104 | tf_op jit(solution)/shard_map/ppermute | solution.py:258
  23.1 1.9 %collective-permute-start.9 = (f32[2,128,128]{2,1,0:T(8,128)S(1)}, f32[2,128,128]{2,1,0:T(8,128)S(1)}, u32[]{:S(2)}, u32[]{:S(2)}) collective-permute-start(f32[2,128,128]{2,1,0:T(8,128)S(1)} %collective-permute-done.7.refs_8_), channel_id=1, source_target_pairs={{0,2},{1,3},{2,0},{3,1},{4,6},{5,7},{6,4},{7,5},{8,10},{9,11},{10,... | collective-permute-start | bytes 393224 | tf_op jit(solution)/shard_map/ppermute | solution.py:258
  25.0 2.7 %early.2 = (f32[8,128]{1,0:T(8,128)S(1)}, f32[171,128,128]{2,1,0:T(8,128)S(1)}) custom-call(s32[16]{0:T(128)S(1)} %get-tuple-element.54.pick_ref, bf16[8,128,512]{2,1,0:T(8,128)(2,1)S(1)} %get-tuple-element.62.l4_ref, f32[2,128,128]{2,1,0:T(8,128)S(1)} %get-tuple-element.65.refs_0_.vector_ref, f32[2,128,128]{2,1,0:T(8,128)S(1)} %collective-permute-done.refs_1_, ...), custom_call_target="tpu_custom_call" | custom-call | tf_op jit(solution)/shard_map/early/pallas_call | solution.py:167
  27.6 1.5 %collective-permute-done.9.refs_10_ = f32[2,128,128]{2,1,0:T(8,128)S(1)} collective-permute-done((f32[2,128,128]{2,1,0:T(8,128)S(1)}, f32[2,128,128]{2,1,0:T(8,128)S(1)}, u32[]{:S(2)}, u32[]{:S(2)}) %collective-permute-start.9) | collective-permute-done | bytes 131104 | tf_op jit(solution)/shard_map/ppermute | solution.py:258
  29.1 1.3 %collective-permute-done.14.refs_11_ = f32[2,128,128]{2,1,0:T(8,128)S(1)} collective-permute-done((f32[2,128,128]{2,1,0:T(8,128)S(1)}, f32[2,128,128]{2,1,0:T(8,128)S(1)}, u32[]{:S(2)}, u32[]{:S(2)}) %collective-permute-start.14) | collective-permute-done | bytes 131104 | tf_op jit(solution)/shard_map/ppermute | solution.py:258
  30.4 4.9 %apply.2 = (f32[640,128]{1,0:T(8,128)S(1)}, f32[648,128]{1,0:T(8,128)S(1)}, f32[264,128]{1,0:T(8,128)S(1)}, f32[264,128]{1,0:T(8,128)S(1)}, f32[128,128]{1,0:T(8...) custom-call(s32[16]{0:T(128)S(1)} %get-tuple-element.54.pick_ref, ...), custom_call_target="tpu_custom_call", output_to_operand_aliasing={{7}: (27, {})} | custom-call | tf_op jit(solution)/shard_map/apply/pallas_call | solution.py:234
  35.3 0.2 collective-permute-start.15
  35.5 1.8 %collective-permute-start.16 = (f32[264,128]{1,0:T(8,128)S(1)}, f32[264,128]{1,0:T(8,128)S(1)}, u32[]{:S(2)}, u32[]{:S(2)}) collective-permute-start(f32[264,128]{1,0:T(8,128)S(1)} %get-tuple-element.74), channel_id=1, source_target_pairs={{0,2},{1,3},{2,0},{3,1},{4,6},{5,7},{6,4},{7,5},{8,10},{9,11},{10,... | collective-permute-start | bytes 405512 | tf_op jit(solution)/shard_map/ppermute | solution.py:258
  37.4 1.6 %collective-permute-start.19 = (f32[128,128]{1,0:T(8,128)S(1)}, f32[128,128]{1,0:T(8,128)S(1)}, u32[]{:S(2)}, u32[]{:S(2)}) collective-permute-start(f32[128,128]{1,0:T(8,128)S(1)} %get-tuple-element.77), channel_id=1, source_target_pairs={{0,5},{1,4},{2,7},{3,6},{4,1},{5,0},{6,3},{7,2},{8,13},{9,12},{10,... | collective-permute-start | bytes 196616 | tf_op jit(solution)/shard_map/ppermute | solution.py:258
  39.0 3.3 %collective-permute-done.18.column_ref = f32[128,128]{1,0:T(8,128)S(1)} collective-permute-done((f32[128,128]{1,0:T(8,128)S(1)}, f32[128,128]{1,0:T(8,128)S(1)}, u32[]{:S(2)}, u32[]{:S(2)}) %collective-permute-start.18) | collective-permute-done | bytes 65568 | tf_op jit(solution)/shard_map/ppermute | solution.py:258
  42.3 1.7 %collective-permute-done.17.row_far_ref = f32[264,128]{1,0:T(8,128)S(1)} collective-permute-done((f32[264,128]{1,0:T(8,128)S(1)}, f32[264,128]{1,0:T(8,128)S(1)}, u32[]{:S(2)}, u32[]{:S(2)}) %collective-permute-start.17) | collective-permute-done | bytes 135200 | tf_op jit(solution)/shard_map/ppermute | solution.py:258
  44.1 0.7 fold.2
  44.7 1.8 %collective-permute-start.21 = (f32[264,128]{1,0:T(8,128)S(1)}, f32[264,128]{1,0:T(8,128)S(1)}, u32[]{:S(2)}, u32[]{:S(2)}) collective-permute-start(f32[264,128]{1,0:T(8,128)S(1)} %get-tuple-element.82), channel_id=1, source_target_pairs={{0,8},{1,9},{2,10},{3,11},{4,12},{5,13},{6,14},{7,15},{8,0},{9,1},... | collective-permute-start | bytes 405512 | tf_op jit(solution)/shard_map/ppermute | solution.py:258
  46.6 0.4 collective-permute-start.22
  47.0 1.3 %collective-permute-start.23 = (f32[264,128]{1,0:T(8,128)S(1)}, f32[264,128]{1,0:T(8,128)S(1)}, u32[]{:S(2)}, u32[]{:S(2)}) collective-permute-start(f32[264,128]{1,0:T(8,128)S(1)} %get-tuple-element.81.refs_0_), channel_id=1, source_target_pairs={{0,4},{1,5},{2,6},{3,7},{4,0},{5,1},{6,2},{7,3},{8,12},{9,13},{10,... | collective-permute-start | bytes 405512 | tf_op jit(solution)/shard_map/ppermute | solution.py:258
  48.3 1.7 %collective-permute-start.20 = (f32[2,128,128]{2,1,0:T(8,128)S(1)}, f32[2,128,128]{2,1,0:T(8,128)S(1)}, u32[]{:S(2)}, u32[]{:S(2)}) collective-permute-start(f32[2,128,128]{2,1,0:T(8,128)S(1)} %get-tuple-element.79), channel_id=1, source_target_pairs={{0,2},{1,3},{2,0},{3,1},{4,6},{5,7},{6,4},{7,5},{8,10},{9,11},{10,... | collective-permute-start | bytes 393224 | tf_op jit(solution)/shard_map/ppermute | solution.py:258
  50.0 3.3 %collective-permute-done.20.step_ref = f32[2,128,128]{2,1,0:T(8,128)S(1)} collective-permute-done((f32[2,128,128]{2,1,0:T(8,128)S(1)}, f32[2,128,128]{2,1,0:T(8,128)S(1)}, u32[]{:S(2)}, u32[]{:S(2)}) %collective-permute-start.20) | collective-permute-done | bytes 131104 | tf_op jit(solution)/shard_map/ppermute | solution.py:258
  53.3 3.5 %collective-permute-done.21.refs_1_ = f32[264,128]{1,0:T(8,128)S(1)} collective-permute-done((f32[264,128]{1,0:T(8,128)S(1)}, f32[264,128]{1,0:T(8,128)S(1)}, u32[]{:S(2)}, u32[]{:S(2)}) %collective-permute-start.21) | collective-permute-done | bytes 135200 | tf_op jit(solution)/shard_map/ppermute | solution.py:258
  56.8 1.3 %collective-permute-done.23.refs_3_ = f32[264,128]{1,0:T(8,128)S(1)} collective-permute-done((f32[264,128]{1,0:T(8,128)S(1)}, f32[264,128]{1,0:T(8,128)S(1)}, u32[]{:S(2)}, u32[]{:S(2)}) %collective-permute-start.23) | collective-permute-done | bytes 135200 | tf_op jit(solution)/shard_map/ppermute | solution.py:258
  58.1 0.2 step.1.refs_0_.vector_ref
  58.3 2.6 %collective-permute-start.34 = (f32[2,128,128]{2,1,0:T(8,128)S(1)}, f32[2,128,128]{2,1,0:T(8,128)S(1)}, u32[]{:S(2)}, u32[]{:S(2)}) collective-permute-start(f32[2,128,128]{2,1,0:T(8,128)S(1)} %step.1.refs_0_.vector_ref), channel_id=1, source_target_pairs={{0,12},{1,13},{2,14},{3,15},{4,8},{5,9},{6,10},{7,11},{8,4},{9,5},... | collective-permute-start | bytes 393224 | tf_op jit(solution)/shard_map/ppermute | solution.py:258
  61.0 1.0 collective-permute-start.31
  61.9 1.5 %collective-permute-start.25 = (f32[2,128,128]{2,1,0:T(8,128)S(1)}, f32[2,128,128]{2,1,0:T(8,128)S(1)}, u32[]{:S(2)}, u32[]{:S(2)}) collective-permute-start(f32[2,128,128]{2,1,0:T(8,128)S(1)} %step.1.refs_0_.vector_ref), channel_id=1, source_target_pairs={{0,2},{1,3},{2,0},{3,1},{4,6},{5,7},{6,4},{7,5},{8,10},{9,11},{10,... | collective-permute-start | bytes 393224 | tf_op jit(solution)/shard_map/ppermute | solution.py:258
  63.5 0.9 collective-permute-start.27
  64.3 1.7 %collective-permute-done.34.refs_10_.refs_12_ = f32[2,128,128]{2,1,0:T(8,128)S(1)} collective-permute-done((f32[2,128,128]{2,1,0:T(8,128)S(1)}, f32[2,128,128]{2,1,0:T(8,128)S(1)}, u32[]{:S(2)}, u32[]{:S(2)}) %collective-permute-start.34) | collective-permute-done | bytes 131104 | tf_op jit(solution)/shard_map/ppermute | solution.py:258
  66.0 1.4 %collective-permute-start.36 = (f32[2,128,128]{2,1,0:T(8,128)S(1)}, f32[2,128,128]{2,1,0:T(8,128)S(1)}, u32[]{:S(2)}, u32[]{:S(2)}) collective-permute-start(f32[2,128,128]{2,1,0:T(8,128)S(1)} %collective-permute-done.34.refs_10_.refs_12_), channel_id=1, source_target_pairs={{0,2},{1,3},{2,0},{3,1},{4,6},{5,7},{6,4},{7,5},{8,10},{9,11},{10,... | collective-permute-start | bytes 393224 | tf_op jit(solution)/shard_map/ppermute | solution.py:258
  67.4 5.8 %collective-permute-done.31.refs_8_ = f32[2,128,128]{2,1,0:T(8,128)S(1)} collective-permute-done((f32[2,128,128]{2,1,0:T(8,128)S(1)}, f32[2,128,128]{2,1,0:T(8,128)S(1)}, u32[]{:S(2)}, u32[]{:S(2)}) %collective-permute-start.31) | collective-permute-done | bytes 131104 | tf_op jit(solution)/shard_map/ppermute | solution.py:258
  73.2 0.6 collective-permute-start.32
  73.8 0.4 collective-permute-start.28
  74.2 0.2 collective-permute-done.35.refs_11_.refs_13_
  74.6 4.4 %collective-permute-done.29.refs_6_ = f32[2,128,128]{2,1,0:T(8,128)S(1)} collective-permute-done((f32[2,128,128]{2,1,0:T(8,128)S(1)}, f32[2,128,128]{2,1,0:T(8,128)S(1)}, u32[]{:S(2)}, u32[]{:S(2)}) %collective-permute-start.29) | collective-permute-done | bytes 131104 | tf_op jit(solution)/shard_map/ppermute | solution.py:258
  79.1 1.4 %collective-permute-start.33 = (f32[2,128,128]{2,1,0:T(8,128)S(1)}, f32[2,128,128]{2,1,0:T(8,128)S(1)}, u32[]{:S(2)}, u32[]{:S(2)}) collective-permute-start(f32[2,128,128]{2,1,0:T(8,128)S(1)} %collective-permute-done.31.refs_8_), channel_id=1, source_target_pairs={{0,2},{1,3},{2,0},{3,1},{4,6},{5,7},{6,4},{7,5},{8,10},{9,11},{10,... | collective-permute-start | bytes 393224 | tf_op jit(solution)/shard_map/ppermute | solution.py:258
  80.5 2.7 %early.3 = (f32[8,128]{1,0:T(8,128)S(1)}, f32[171,128,128]{2,1,0:T(8,128)S(1)}) custom-call(s32[16]{0:T(128)S(1)} %get-tuple-element.54.pick_ref, bf16[8,128,512]{2,1,0:T(8,128)(2,1)S(1)} %get-tuple-element.62.l4_ref, f32[2,128,128]{2,1,0:T(8,128)S(1)} %step.1.refs_0_.vector_ref, f32[2,128,128]{2,1,0:T(8,128)S(1)} %collective-permute-done.24.refs_1_, ...), custom_call_target="tpu_custom_call" | custom-call | tf_op jit(solution)/shard_map/early/pallas_call | solution.py:167
  83.2 1.8 %collective-permute-done.33.refs_10_ = f32[2,128,128]{2,1,0:T(8,128)S(1)} collective-permute-done((f32[2,128,128]{2,1,0:T(8,128)S(1)}, f32[2,128,128]{2,1,0:T(8,128)S(1)}, u32[]{:S(2)}, u32[]{:S(2)}) %collective-permute-start.33) | collective-permute-done | bytes 131104 | tf_op jit(solution)/shard_map/ppermute | solution.py:258
  85.0 1.3 %collective-permute-done.38.refs_11_ = f32[2,128,128]{2,1,0:T(8,128)S(1)} collective-permute-done((f32[2,128,128]{2,1,0:T(8,128)S(1)}, f32[2,128,128]{2,1,0:T(8,128)S(1)}, u32[]{:S(2)}, u32[]{:S(2)}) %collective-permute-start.38) | collective-permute-done | bytes 131104 | tf_op jit(solution)/shard_map/ppermute | solution.py:258
  86.3 5.1 %apply.3 = (f32[640,128]{1,0:T(8,128)S(1)}, f32[648,128]{1,0:T(8,128)S(1)}, f32[264,128]{1,0:T(8,128)S(1)}, f32[264,128]{1,0:T(8,128)S(1)}, f32[128,128]{1,0:T(8...) custom-call(s32[16]{0:T(128)S(1)} %get-tuple-element.54.pick_ref, ...), custom_call_target="tpu_custom_call", output_to_operand_aliasing={{7}: (27, {})} | custom-call | tf_op jit(solution)/shard_map/apply/pallas_call | solution.py:234
  91.6 1.5 %collective-permute-start.40 = (f32[264,128]{1,0:T(8,128)S(1)}, f32[264,128]{1,0:T(8,128)S(1)}, u32[]{:S(2)}, u32[]{:S(2)}) collective-permute-start(f32[264,128]{1,0:T(8,128)S(1)} %get-tuple-element.91), channel_id=1, source_target_pairs={{0,2},{1,3},{2,0},{3,1},{4,6},{5,7},{6,4},{7,5},{8,10},{9,11},{10,... | collective-permute-start | bytes 405512 | tf_op jit(solution)/shard_map/ppermute | solution.py:258
  93.1 0.3 collective-permute-start.41
  93.3 0.2 collective-permute-start.42
  93.5 1.5 %collective-permute-start.43 = (f32[128,128]{1,0:T(8,128)S(1)}, f32[128,128]{1,0:T(8,128)S(1)}, u32[]{:S(2)}, u32[]{:S(2)}) collective-permute-start(f32[128,128]{1,0:T(8,128)S(1)} %get-tuple-element.94), channel_id=1, source_target_pairs={{0,5},{1,4},{2,7},{3,6},{4,1},{5,0},{6,3},{7,2},{8,13},{9,12},{10,... | collective-permute-start | bytes 196616 | tf_op jit(solution)/shard_map/ppermute | solution.py:258
  95.0 3.2 %collective-permute-done.42.column_ref = f32[128,128]{1,0:T(8,128)S(1)} collective-permute-done((f32[128,128]{1,0:T(8,128)S(1)}, f32[128,128]{1,0:T(8,128)S(1)}, u32[]{:S(2)}, u32[]{:S(2)}) %collective-permute-start.42) | collective-permute-done | bytes 65568 | tf_op jit(solution)/shard_map/ppermute | solution.py:258
  98.3 0.3 collective-permute-done.43.column_far_ref
  98.5 1.4 %collective-permute-done.41.row_far_ref = f32[264,128]{1,0:T(8,128)S(1)} collective-permute-done((f32[264,128]{1,0:T(8,128)S(1)}, f32[264,128]{1,0:T(8,128)S(1)}, u32[]{:S(2)}, u32[]{:S(2)}) %collective-permute-start.41) | collective-permute-done | bytes 135200 | tf_op jit(solution)/shard_map/ppermute | solution.py:258
  99.9 0.7 fold.3
  100.6 0.9 collective-permute-start.45
  101.5 1.6 %collective-permute-start.46 = (f32[264,128]{1,0:T(8,128)S(1)}, f32[264,128]{1,0:T(8,128)S(1)}, u32[]{:S(2)}, u32[]{:S(2)}) collective-permute-start(f32[264,128]{1,0:T(8,128)S(1)} %get-tuple-element.100), channel_id=1, source_target_pairs={{0,12},{1,13},{2,14},{3,15},{4,8},{5,9},{6,10},{7,11},{8,4},{9,5},... | collective-permute-start | bytes 405512 | tf_op jit(solution)/shard_map/ppermute | solution.py:258
  103.2 1.0 collective-permute-start.47
  104.1 1.6 %collective-permute-start.44 = (f32[2,128,128]{2,1,0:T(8,128)S(1)}, f32[2,128,128]{2,1,0:T(8,128)S(1)}, u32[]{:S(2)}, u32[]{:S(2)}) collective-permute-start(f32[2,128,128]{2,1,0:T(8,128)S(1)} %get-tuple-element.96), channel_id=1, source_target_pairs={{0,2},{1,3},{2,0},{3,1},{4,6},{5,7},{6,4},{7,5},{8,10},{9,11},{10,... | collective-permute-start | bytes 393224 | tf_op jit(solution)/shard_map/ppermute | solution.py:258
  105.7 3.4 %collective-permute-done.44.step_ref = f32[2,128,128]{2,1,0:T(8,128)S(1)} collective-permute-done((f32[2,128,128]{2,1,0:T(8,128)S(1)}, f32[2,128,128]{2,1,0:T(8,128)S(1)}, u32[]{:S(2)}, u32[]{:S(2)}) %collective-permute-start.44) | collective-permute-done | bytes 131104 | tf_op jit(solution)/shard_map/ppermute | solution.py:258
  109.1 3.8 %collective-permute-done.45.refs_1_ = f32[264,128]{1,0:T(8,128)S(1)} collective-permute-done((f32[264,128]{1,0:T(8,128)S(1)}, f32[264,128]{1,0:T(8,128)S(1)}, u32[]{:S(2)}, u32[]{:S(2)}) %collective-permute-start.45) | collective-permute-done | bytes 135200 | tf_op jit(solution)/shard_map/ppermute | solution.py:258
  112.9 1.3 collective-permute-done.47.refs_3_
  114.1 0.9 last.1
  115.0 12.1 %all_to_all.5.tiles_ref = f32[16,8,128]{2,1,0:T(8,128)S(1)} all-to-all(f32[16,8,128]{2,1,0:T(8,128)S(1)} %broadcast_in_dim.2), channel_id=1, replica_groups=mesh['group'=2,'term'=16] {'term'}, dimensions={0} | all-to-all | bytes 131072 | tf_op jit(solution)/shard_map/all_to_all | solution.py:405
  127.1 0.9 norm.1
  (47 shorter events, 0.7 us)
Async XLA Ops:
  0.6 57.5 %copy-start = (f32[2,128,128]{2,1,0:T(8,128)S(1)}, f32[2,128,128]{2,1,0:T(8,128)}, u32[]{:S(2)}) copy-start(f32[2,128,128]{2,1,0:T(8,128)} %precond_ref.3) | copy-start | bytes 393220
  0.6 13.1 %collective-permute-start.10 = (f32[2,128,128]{2,1,0:T(8,128)}, f32[2,128,128]{2,1,0:T(8,128)S(1)}, u32[]{:S(2)}, u32[]{:S(2)}) collective-permute-start(f32[2,128,128]{2,1,0:T(8,128)} %vector_in.1), channel_id=1, source_target_pairs={{0,12},{1,13},{2,14},{3,15},{4,8},{5,9},{6,10},{7,11},{8,4},{9,5},... | collective-permute-start | bytes 393224 | tf_op jit(solution)/shard_map/ppermute | solution.py:258
  5.8 11.4 %collective-permute-start.7 = (f32[2,128,128]{2,1,0:T(8,128)}, f32[2,128,128]{2,1,0:T(8,128)S(1)}, u32[]{:S(2)}, u32[]{:S(2)}) collective-permute-start(f32[2,128,128]{2,1,0:T(8,128)} %vector_in.1), channel_id=1, source_target_pairs={{0,8},{1,9},{2,10},{3,11},{4,12},{5,13},{6,14},{7,15},{8,0},{9,1},... | collective-permute-start | bytes 393224 | tf_op jit(solution)/shard_map/ppermute | solution.py:258
  11.7 5.9 %collective-permute-start.1 = (f32[2,128,128]{2,1,0:T(8,128)}, f32[2,128,128]{2,1,0:T(8,128)S(1)}, u32[]{:S(2)}, u32[]{:S(2)}) collective-permute-start(f32[2,128,128]{2,1,0:T(8,128)} %vector_in.1), channel_id=1, source_target_pairs={{0,2},{1,3},{2,0},{3,1},{4,6},{5,7},{6,4},{7,5},{8,10},{9,11},{10,... | collective-permute-start | bytes 393224 | tf_op jit(solution)/shard_map/ppermute | solution.py:258
  13.5 5.9 %collective-permute-start.3 = (f32[2,128,128]{2,1,0:T(8,128)}, f32[2,128,128]{2,1,0:T(8,128)S(1)}, u32[]{:S(2)}, u32[]{:S(2)}) collective-permute-start(f32[2,128,128]{2,1,0:T(8,128)} %vector_in.1), channel_id=1, source_target_pairs={{0,4},{1,5},{2,6},{3,7},{4,0},{5,1},{6,2},{7,3},{8,12},{9,13},{10,... | collective-permute-start | bytes 393224 | tf_op jit(solution)/shard_map/ppermute | solution.py:258
  13.8 5.6 %collective-permute-start = (f32[2,128,128]{2,1,0:T(8,128)S(1)}, f32[2,128,128]{2,1,0:T(8,128)S(1)}, u32[]{:S(2)}, u32[]{:S(2)}) collective-permute-start(f32[2,128,128]{2,1,0:T(8,128)S(1)} %get-tuple-element.65.refs_0_.vector_ref), channel_id=1, source_target_pairs={{0,1},{1,0},{2,3},{3,2},{4,5},{5,4},{6,7},{7,6},{8,9},{9,8},{10,11... | collective-permute-start | bytes 393224 | tf_op jit(solution)/shard_map/ppermute | solution.py:258
  13.8 6.1 %collective-permute-start.12 = (f32[2,128,128]{2,1,0:T(8,128)S(1)}, f32[2,128,128]{2,1,0:T(8,128)S(1)}, u32[]{:S(2)}, u32[]{:S(2)}) collective-permute-start(f32[2,128,128]{2,1,0:T(8,128)S(1)} %collective-permute-done.10.refs_10_.refs_12_), channel_id=1, source_target_pairs={{0,2},{1,3},{2,0},{3,1},{4,6},{5,7},{6,4},{7,5},{8,10},{9,11},{10,... | collective-permute-start | bytes 393224 | tf_op jit(solution)/shard_map/ppermute | solution.py:258
  17.1 2.8 %collective-permute-start.11 = (f32[2,128,128]{2,1,0:T(8,128)S(1)}, f32[2,128,128]{2,1,0:T(8,128)S(1)}, u32[]{:S(2)}, u32[]{:S(2)}) collective-permute-start(f32[2,128,128]{2,1,0:T(8,128)S(1)} %collective-permute-done.10.refs_10_.refs_12_), channel_id=1, source_target_pairs={{0,1},{1,0},{2,3},{3,2},{4,5},{5,4},{6,7},{7,6},{8,9},{9,8},{10,11... | collective-permute-start | bytes 393224 | tf_op jit(solution)/shard_map/ppermute | solution.py:258
  17.6 5.5 %collective-permute-start.5 = (f32[2,128,128]{2,1,0:T(8,128)S(1)}, f32[2,128,128]{2,1,0:T(8,128)S(1)}, u32[]{:S(2)}, u32[]{:S(2)}) collective-permute-start(f32[2,128,128]{2,1,0:T(8,128)S(1)} %collective-permute-done.1.refs_2_), channel_id=1, source_target_pairs={{0,4},{1,5},{2,6},{3,7},{4,0},{5,1},{6,2},{7,3},{8,12},{9,13},{10,... | collective-permute-start | bytes 393224 | tf_op jit(solution)/shard_map/ppermute | solution.py:258
  19.4 3.7 %collective-permute-start.8 = (f32[2,128,128]{2,1,0:T(8,128)S(1)}, f32[2,128,128]{2,1,0:T(8,128)S(1)}, u32[]{:S(2)}, u32[]{:S(2)}) collective-permute-start(f32[2,128,128]{2,1,0:T(8,128)S(1)} %collective-permute-done.7.refs_8_), channel_id=1, source_target_pairs={{0,1},{1,0},{2,3},{3,2},{4,5},{5,4},{6,7},{7,6},{8,9},{9,8},{10,11... | collective-permute-start | bytes 393224 | tf_op jit(solution)/shard_map/ppermute | solution.py:258
  19.4 5.6 %collective-permute-start.2 = (f32[2,128,128]{2,1,0:T(8,128)S(1)}, f32[2,128,128]{2,1,0:T(8,128)S(1)}, u32[]{:S(2)}, u32[]{:S(2)}) collective-permute-start(f32[2,128,128]{2,1,0:T(8,128)S(1)} %collective-permute-done.1.refs_2_), channel_id=1, source_target_pairs={{0,1},{1,0},{2,3},{3,2},{4,5},{5,4},{6,7},{7,6},{8,9},{9,8},{10,11... | collective-permute-start | bytes 393224 | tf_op jit(solution)/shard_map/ppermute | solution.py:258
  19.9 5.0 %collective-permute-start.4 = (f32[2,128,128]{2,1,0:T(8,128)S(1)}, f32[2,128,128]{2,1,0:T(8,128)S(1)}, u32[]{:S(2)}, u32[]{:S(2)}) collective-permute-start(f32[2,128,128]{2,1,0:T(8,128)S(1)} %collective-permute-done.3.refs_4_), channel_id=1, source_target_pairs={{0,1},{1,0},{2,3},{3,2},{4,5},{5,4},{6,7},{7,6},{8,9},{9,8},{10,11... | collective-permute-start | bytes 393224 | tf_op jit(solution)/shard_map/ppermute | solution.py:258
  20.0 5.0 %collective-permute-start.13 = (f32[2,128,128]{2,1,0:T(8,128)S(1)}, f32[2,128,128]{2,1,0:T(8,128)S(1)}, u32[]{:S(2)}, u32[]{:S(2)}) collective-permute-start(f32[2,128,128]{2,1,0:T(8,128)S(1)} %collective-permute-done.12.refs_12_.refs_14_), channel_id=1, source_target_pairs={{0,1},{1,0},{2,3},{3,2},{4,5},{5,4},{6,7},{7,6},{8,9},{9,8},{10,11... | collective-permute-start | bytes 393224 | tf_op jit(solution)/shard_map/ppermute | solution.py:258
  23.1 1.9 %collective-permute-start.6 = (f32[2,128,128]{2,1,0:T(8,128)S(1)}, f32[2,128,128]{2,1,0:T(8,128)S(1)}, u32[]{:S(2)}, u32[]{:S(2)}) collective-permute-start(f32[2,128,128]{2,1,0:T(8,128)S(1)} %collective-permute-done.5.refs_6_), channel_id=1, source_target_pairs={{0,1},{1,0},{2,3},{3,2},{4,5},{5,4},{6,7},{7,6},{8,9},{9,8},{10,11... | collective-permute-start | bytes 393224 | tf_op jit(solution)/shard_map/ppermute | solution.py:258
  23.1 6.0 %collective-permute-start.9 = (f32[2,128,128]{2,1,0:T(8,128)S(1)}, f32[2,128,128]{2,1,0:T(8,128)S(1)}, u32[]{:S(2)}, u32[]{:S(2)}) collective-permute-start(f32[2,128,128]{2,1,0:T(8,128)S(1)} %collective-permute-done.7.refs_8_), channel_id=1, source_target_pairs={{0,2},{1,3},{2,0},{3,1},{4,6},{5,7},{6,4},{7,5},{8,10},{9,11},{10,... | collective-permute-start | bytes 393224 | tf_op jit(solution)/shard_map/ppermute | solution.py:258
  29.1 1.3 %collective-permute-start.14 = (f32[2,128,128]{2,1,0:T(8,128)S(1)}, f32[2,128,128]{2,1,0:T(8,128)S(1)}, u32[]{:S(2)}, u32[]{:S(2)}) collective-permute-start(f32[2,128,128]{2,1,0:T(8,128)S(1)} %collective-permute-done.9.refs_10_), channel_id=1, source_target_pairs={{0,1},{1,0},{2,3},{3,2},{4,5},{5,4},{6,7},{7,6},{8,9},{9,8},{10,11... | collective-permute-start | bytes 393224 | tf_op jit(solution)/shard_map/ppermute | solution.py:258
  35.3 8.7 %collective-permute-start.15 = (f32[648,128]{1,0:T(8,128)S(1)}, f32[648,128]{1,0:T(8,128)S(1)}, u32[]{:S(2)}, u32[]{:S(2)}) collective-permute-start(f32[648,128]{1,0:T(8,128)S(1)} %get-tuple-element.73.far_in), channel_id=1, source_target_pairs={{0,1},{1,0},{2,3},{3,2},{4,5},{5,4},{6,7},{7,6},{8,9},{9,8},{10,11... | collective-permute-start | bytes 995336 | tf_op jit(solution)/shard_map/ppermute | solution.py:258
  35.5 6.8 %collective-permute-start.16 = (f32[264,128]{1,0:T(8,128)S(1)}, f32[264,128]{1,0:T(8,128)S(1)}, u32[]{:S(2)}, u32[]{:S(2)}) collective-permute-start(f32[264,128]{1,0:T(8,128)S(1)} %get-tuple-element.74), channel_id=1, source_target_pairs={{0,2},{1,3},{2,0},{3,1},{4,6},{5,7},{6,4},{7,5},{8,10},{9,11},{10,... | collective-permute-start | bytes 405512 | tf_op jit(solution)/shard_map/ppermute | solution.py:258
  37.3 6.7 %collective-permute-start.17 = (f32[264,128]{1,0:T(8,128)S(1)}, f32[264,128]{1,0:T(8,128)S(1)}, u32[]{:S(2)}, u32[]{:S(2)}) collective-permute-start(f32[264,128]{1,0:T(8,128)S(1)} %get-tuple-element.75), channel_id=1, source_target_pairs={{0,3},{1,2},{2,1},{3,0},{4,7},{5,6},{6,5},{7,4},{8,11},{9,10},{10,... | collective-permute-start | bytes 405512 | tf_op jit(solution)/shard_map/ppermute | solution.py:258
  37.4 4.9 %collective-permute-start.18 = (f32[128,128]{1,0:T(8,128)S(1)}, f32[128,128]{1,0:T(8,128)S(1)}, u32[]{:S(2)}, u32[]{:S(2)}) collective-permute-start(f32[128,128]{1,0:T(8,128)S(1)} %get-tuple-element.76), channel_id=1, source_target_pairs={{0,4},{1,5},{2,6},{3,7},{4,0},{5,1},{6,2},{7,3},{8,12},{9,13},{10,... | collective-permute-start | bytes 196616 | tf_op jit(solution)/shard_map/ppermute | solution.py:258
  37.4 4.9 %collective-permute-start.19 = (f32[128,128]{1,0:T(8,128)S(1)}, f32[128,128]{1,0:T(8,128)S(1)}, u32[]{:S(2)}, u32[]{:S(2)}) collective-permute-start(f32[128,128]{1,0:T(8,128)S(1)} %get-tuple-element.77), channel_id=1, source_target_pairs={{0,5},{1,4},{2,7},{3,6},{4,1},{5,0},{6,3},{7,2},{8,13},{9,12},{10,... | collective-permute-start | bytes 196616 | tf_op jit(solution)/shard_map/ppermute | solution.py:258
  44.7 12.1 %collective-permute-start.21 = (f32[264,128]{1,0:T(8,128)S(1)}, f32[264,128]{1,0:T(8,128)S(1)}, u32[]{:S(2)}, u32[]{:S(2)}) collective-permute-start(f32[264,128]{1,0:T(8,128)S(1)} %get-tuple-element.82), channel_id=1, source_target_pairs={{0,8},{1,9},{2,10},{3,11},{4,12},{5,13},{6,14},{7,15},{8,0},{9,1},... | collective-permute-start | bytes 405512 | tf_op jit(solution)/shard_map/ppermute | solution.py:258
  46.6 10.2 %collective-permute-start.22 = (f32[264,128]{1,0:T(8,128)S(1)}, f32[264,128]{1,0:T(8,128)S(1)}, u32[]{:S(2)}, u32[]{:S(2)}) collective-permute-start(f32[264,128]{1,0:T(8,128)S(1)} %get-tuple-element.83), channel_id=1, source_target_pairs={{0,12},{1,13},{2,14},{3,15},{4,8},{5,9},{6,10},{7,11},{8,4},{9,5},... | collective-permute-start | bytes 405512 | tf_op jit(solution)/shard_map/ppermute | solution.py:258
  47.0 11.2 %collective-permute-start.23 = (f32[264,128]{1,0:T(8,128)S(1)}, f32[264,128]{1,0:T(8,128)S(1)}, u32[]{:S(2)}, u32[]{:S(2)}) collective-permute-start(f32[264,128]{1,0:T(8,128)S(1)} %get-tuple-element.81.refs_0_), channel_id=1, source_target_pairs={{0,4},{1,5},{2,6},{3,7},{4,0},{5,1},{6,2},{7,3},{8,12},{9,13},{10,... | collective-permute-start | bytes 405512 | tf_op jit(solution)/shard_map/ppermute | solution.py:258
  48.3 5.0 %collective-permute-start.20 = (f32[2,128,128]{2,1,0:T(8,128)S(1)}, f32[2,128,128]{2,1,0:T(8,128)S(1)}, u32[]{:S(2)}, u32[]{:S(2)}) collective-permute-start(f32[2,128,128]{2,1,0:T(8,128)S(1)} %get-tuple-element.79), channel_id=1, source_target_pairs={{0,2},{1,3},{2,0},{3,1},{4,6},{5,7},{6,4},{7,5},{8,10},{9,11},{10,... | collective-permute-start | bytes 393224 | tf_op jit(solution)/shard_map/ppermute | solution.py:258
  58.3 7.7 %collective-permute-start.34 = (f32[2,128,128]{2,1,0:T(8,128)S(1)}, f32[2,128,128]{2,1,0:T(8,128)S(1)}, u32[]{:S(2)}, u32[]{:S(2)}) collective-permute-start(f32[2,128,128]{2,1,0:T(8,128)S(1)} %step.1.refs_0_.vector_ref), channel_id=1, source_target_pairs={{0,12},{1,13},{2,14},{3,15},{4,8},{5,9},{6,10},{7,11},{8,4},{9,5},... | collective-permute-start | bytes 393224 | tf_op jit(solution)/shard_map/ppermute | solution.py:258
  61.0 12.2 %collective-permute-start.31 = (f32[2,128,128]{2,1,0:T(8,128)S(1)}, f32[2,128,128]{2,1,0:T(8,128)S(1)}, u32[]{:S(2)}, u32[]{:S(2)}) collective-permute-start(f32[2,128,128]{2,1,0:T(8,128)S(1)} %step.1.refs_0_.vector_ref), channel_id=1, source_target_pairs={{0,8},{1,9},{2,10},{3,11},{4,12},{5,13},{6,14},{7,15},{8,0},{9,1},... | collective-permute-start | bytes 393224 | tf_op jit(solution)/shard_map/ppermute | solution.py:258
  61.9 11.2 %collective-permute-start.25 = (f32[2,128,128]{2,1,0:T(8,128)S(1)}, f32[2,128,128]{2,1,0:T(8,128)S(1)}, u32[]{:S(2)}, u32[]{:S(2)}) collective-permute-start(f32[2,128,128]{2,1,0:T(8,128)S(1)} %step.1.refs_0_.vector_ref), channel_id=1, source_target_pairs={{0,2},{1,3},{2,0},{3,1},{4,6},{5,7},{6,4},{7,5},{8,10},{9,11},{10,... | collective-permute-start | bytes 393224 | tf_op jit(solution)/shard_map/ppermute | solution.py:258
  63.5 9.7 %collective-permute-start.27 = (f32[2,128,128]{2,1,0:T(8,128)S(1)}, f32[2,128,128]{2,1,0:T(8,128)S(1)}, u32[]{:S(2)}, u32[]{:S(2)}) collective-permute-start(f32[2,128,128]{2,1,0:T(8,128)S(1)} %step.1.refs_0_.vector_ref), channel_id=1, source_target_pairs={{0,4},{1,5},{2,6},{3,7},{4,0},{5,1},{6,2},{7,3},{8,12},{9,13},{10,... | collective-permute-start | bytes 393224 | tf_op jit(solution)/shard_map/ppermute | solution.py:258
  64.3 9.4 %collective-permute-start.24 = (f32[2,128,128]{2,1,0:T(8,128)S(1)}, f32[2,128,128]{2,1,0:T(8,128)S(1)}, u32[]{:S(2)}, u32[]{:S(2)}) collective-permute-start(f32[2,128,128]{2,1,0:T(8,128)S(1)} %step.1.refs_0_.vector_ref), channel_id=1, source_target_pairs={{0,1},{1,0},{2,3},{3,2},{4,5},{5,4},{6,7},{7,6},{8,9},{9,8},{10,11... | collective-permute-start | bytes 393224 | tf_op jit(solution)/shard_map/ppermute | solution.py:258
  66.0 7.8 %collective-permute-start.36 = (f32[2,128,128]{2,1,0:T(8,128)S(1)}, f32[2,128,128]{2,1,0:T(8,128)S(1)}, u32[]{:S(2)}, u32[]{:S(2)}) collective-permute-start(f32[2,128,128]{2,1,0:T(8,128)S(1)} %collective-permute-done.34.refs_10_.refs_12_), channel_id=1, source_target_pairs={{0,2},{1,3},{2,0},{3,1},{4,6},{5,7},{6,4},{7,5},{8,10},{9,11},{10,... | collective-permute-start | bytes 393224 | tf_op jit(solution)/shard_map/ppermute | solution.py:258
  73.1 1.3 %collective-permute-start.35 = (f32[2,128,128]{2,1,0:T(8,128)S(1)}, f32[2,128,128]{2,1,0:T(8,128)S(1)}, u32[]{:S(2)}, u32[]{:S(2)}) collective-permute-start(f32[2,128,128]{2,1,0:T(8,128)S(1)} %collective-permute-done.34.refs_10_.refs_12_), channel_id=1, source_target_pairs={{0,1},{1,0},{2,3},{3,2},{4,5},{5,4},{6,7},{7,6},{8,9},{9,8},{10,11... | collective-permute-start | bytes 393224 | tf_op jit(solution)/shard_map/ppermute | solution.py:258
  73.1 5.9 %collective-permute-start.29 = (f32[2,128,128]{2,1,0:T(8,128)S(1)}, f32[2,128,128]{2,1,0:T(8,128)S(1)}, u32[]{:S(2)}, u32[]{:S(2)}) collective-permute-start(f32[2,128,128]{2,1,0:T(8,128)S(1)} %collective-permute-done.25.refs_2_), channel_id=1, source_target_pairs={{0,4},{1,5},{2,6},{3,7},{4,0},{5,1},{6,2},{7,3},{8,12},{9,13},{10,... | collective-permute-start | bytes 393224 | tf_op jit(solution)/shard_map/ppermute | solution.py:258
  73.2 5.9 %collective-permute-start.32 = (f32[2,128,128]{2,1,0:T(8,128)S(1)}, f32[2,128,128]{2,1,0:T(8,128)S(1)}, u32[]{:S(2)}, u32[]{:S(2)}) collective-permute-start(f32[2,128,128]{2,1,0:T(8,128)S(1)} %collective-permute-done.31.refs_8_), channel_id=1, source_target_pairs={{0,1},{1,0},{2,3},{3,2},{4,5},{5,4},{6,7},{7,6},{8,9},{9,8},{10,11... | collective-permute-start | bytes 393224 | tf_op jit(solution)/shard_map/ppermute | solution.py:258
  73.7 6.8 %collective-permute-start.26 = (f32[2,128,128]{2,1,0:T(8,128)S(1)}, f32[2,128,128]{2,1,0:T(8,128)S(1)}, u32[]{:S(2)}, u32[]{:S(2)}) collective-permute-start(f32[2,128,128]{2,1,0:T(8,128)S(1)} %collective-permute-done.25.refs_2_), channel_id=1, source_target_pairs={{0,1},{1,0},{2,3},{3,2},{4,5},{5,4},{6,7},{7,6},{8,9},{9,8},{10,11... | collective-permute-start | bytes 393224 | tf_op jit(solution)/shard_map/ppermute | solution.py:258
  73.8 6.7 %collective-permute-start.28 = (f32[2,128,128]{2,1,0:T(8,128)S(1)}, f32[2,128,128]{2,1,0:T(8,128)S(1)}, u32[]{:S(2)}, u32[]{:S(2)}) collective-permute-start(f32[2,128,128]{2,1,0:T(8,128)S(1)} %collective-permute-done.27.refs_4_), channel_id=1, source_target_pairs={{0,1},{1,0},{2,3},{3,2},{4,5},{5,4},{6,7},{7,6},{8,9},{9,8},{10,11... | collective-permute-start | bytes 393224 | tf_op jit(solution)/shard_map/ppermute | solution.py:258
  74.5 6.0 %collective-permute-start.37 = (f32[2,128,128]{2,1,0:T(8,128)S(1)}, f32[2,128,128]{2,1,0:T(8,128)S(1)}, u32[]{:S(2)}, u32[]{:S(2)}) collective-permute-start(f32[2,128,128]{2,1,0:T(8,128)S(1)} %collective-permute-done.36.refs_12_.refs_14_), channel_id=1, source_target_pairs={{0,1},{1,0},{2,3},{3,2},{4,5},{5,4},{6,7},{7,6},{8,9},{9,8},{10,11... | collective-permute-start | bytes 393224 | tf_op jit(solution)/shard_map/ppermute | solution.py:258
  79.1 1.4 %collective-permute-start.30 = (f32[2,128,128]{2,1,0:T(8,128)S(1)}, f32[2,128,128]{2,1,0:T(8,128)S(1)}, u32[]{:S(2)}, u32[]{:S(2)}) collective-permute-start(f32[2,128,128]{2,1,0:T(8,128)S(1)} %collective-permute-done.29.refs_6_), channel_id=1, source_target_pairs={{0,1},{1,0},{2,3},{3,2},{4,5},{5,4},{6,7},{7,6},{8,9},{9,8},{10,11... | collective-permute-start | bytes 393224 | tf_op jit(solution)/shard_map/ppermute | solution.py:258
  79.1 5.9 %collective-permute-start.33 = (f32[2,128,128]{2,1,0:T(8,128)S(1)}, f32[2,128,128]{2,1,0:T(8,128)S(1)}, u32[]{:S(2)}, u32[]{:S(2)}) collective-permute-start(f32[2,128,128]{2,1,0:T(8,128)S(1)} %collective-permute-done.31.refs_8_), channel_id=1, source_target_pairs={{0,2},{1,3},{2,0},{3,1},{4,6},{5,7},{6,4},{7,5},{8,10},{9,11},{10,... | collective-permute-start | bytes 393224 | tf_op jit(solution)/shard_map/ppermute | solution.py:258
  85.0 1.3 %collective-permute-start.38 = (f32[2,128,128]{2,1,0:T(8,128)S(1)}, f32[2,128,128]{2,1,0:T(8,128)S(1)}, u32[]{:S(2)}, u32[]{:S(2)}) collective-permute-start(f32[2,128,128]{2,1,0:T(8,128)S(1)} %collective-permute-done.33.refs_10_), channel_id=1, source_target_pairs={{0,1},{1,0},{2,3},{3,2},{4,5},{5,4},{6,7},{7,6},{8,9},{9,8},{10,11... | collective-permute-start | bytes 393224 | tf_op jit(solution)/shard_map/ppermute | solution.py:258
  91.4 8.5 %collective-permute-start.39 = (f32[648,128]{1,0:T(8,128)S(1)}, f32[648,128]{1,0:T(8,128)S(1)}, u32[]{:S(2)}, u32[]{:S(2)}) collective-permute-start(f32[648,128]{1,0:T(8,128)S(1)} %get-tuple-element.90.far_in), channel_id=1, source_target_pairs={{0,1},{1,0},{2,3},{3,2},{4,5},{5,4},{6,7},{7,6},{8,9},{9,8},{10,11... | collective-permute-start | bytes 995336 | tf_op jit(solution)/shard_map/ppermute | solution.py:258
  91.6 7.0 %collective-permute-start.40 = (f32[264,128]{1,0:T(8,128)S(1)}, f32[264,128]{1,0:T(8,128)S(1)}, u32[]{:S(2)}, u32[]{:S(2)}) collective-permute-start(f32[264,128]{1,0:T(8,128)S(1)} %get-tuple-element.91), channel_id=1, source_target_pairs={{0,2},{1,3},{2,0},{3,1},{4,6},{5,7},{6,4},{7,5},{8,10},{9,11},{10,... | collective-permute-start | bytes 405512 | tf_op jit(solution)/shard_map/ppermute | solution.py:258
  93.1 6.8 %collective-permute-start.41 = (f32[264,128]{1,0:T(8,128)S(1)}, f32[264,128]{1,0:T(8,128)S(1)}, u32[]{:S(2)}, u32[]{:S(2)}) collective-permute-start(f32[264,128]{1,0:T(8,128)S(1)} %get-tuple-element.92), channel_id=1, source_target_pairs={{0,3},{1,2},{2,1},{3,0},{4,7},{5,6},{6,5},{7,4},{8,11},{9,10},{10,... | collective-permute-start | bytes 405512 | tf_op jit(solution)/shard_map/ppermute | solution.py:258
  93.3 4.9 %collective-permute-start.42 = (f32[128,128]{1,0:T(8,128)S(1)}, f32[128,128]{1,0:T(8,128)S(1)}, u32[]{:S(2)}, u32[]{:S(2)}) collective-permute-start(f32[128,128]{1,0:T(8,128)S(1)} %get-tuple-element.93), channel_id=1, source_target_pairs={{0,4},{1,5},{2,6},{3,7},{4,0},{5,1},{6,2},{7,3},{8,12},{9,13},{10,... | collective-permute-start | bytes 196616 | tf_op jit(solution)/shard_map/ppermute | solution.py:258
  93.5 5.0 %collective-permute-start.43 = (f32[128,128]{1,0:T(8,128)S(1)}, f32[128,128]{1,0:T(8,128)S(1)}, u32[]{:S(2)}, u32[]{:S(2)}) collective-permute-start(f32[128,128]{1,0:T(8,128)S(1)} %get-tuple-element.94), channel_id=1, source_target_pairs={{0,5},{1,4},{2,7},{3,6},{4,1},{5,0},{6,3},{7,2},{8,13},{9,12},{10,... | collective-permute-start | bytes 196616 | tf_op jit(solution)/shard_map/ppermute | solution.py:258
  100.6 12.3 %collective-permute-start.45 = (f32[264,128]{1,0:T(8,128)S(1)}, f32[264,128]{1,0:T(8,128)S(1)}, u32[]{:S(2)}, u32[]{:S(2)}) collective-permute-start(f32[264,128]{1,0:T(8,128)S(1)} %get-tuple-element.99), channel_id=1, source_target_pairs={{0,8},{1,9},{2,10},{3,11},{4,12},{5,13},{6,14},{7,15},{8,0},{9,1},... | collective-permute-start | bytes 405512 | tf_op jit(solution)/shard_map/ppermute | solution.py:258
  101.5 11.4 %collective-permute-start.46 = (f32[264,128]{1,0:T(8,128)S(1)}, f32[264,128]{1,0:T(8,128)S(1)}, u32[]{:S(2)}, u32[]{:S(2)}) collective-permute-start(f32[264,128]{1,0:T(8,128)S(1)} %get-tuple-element.100), channel_id=1, source_target_pairs={{0,12},{1,13},{2,14},{3,15},{4,8},{5,9},{6,10},{7,11},{8,4},{9,5},... | collective-permute-start | bytes 405512 | tf_op jit(solution)/shard_map/ppermute | solution.py:258
  103.2 11.0 %collective-permute-start.47 = (f32[264,128]{1,0:T(8,128)S(1)}, f32[264,128]{1,0:T(8,128)S(1)}, u32[]{:S(2)}, u32[]{:S(2)}) collective-permute-start(f32[264,128]{1,0:T(8,128)S(1)} %get-tuple-element.98.refs_0_), channel_id=1, source_target_pairs={{0,4},{1,5},{2,6},{3,7},{4,0},{5,1},{6,2},{7,3},{8,12},{9,13},{10,... | collective-permute-start | bytes 405512 | tf_op jit(solution)/shard_map/ppermute | solution.py:258
  104.1 5.0 %collective-permute-start.44 = (f32[2,128,128]{2,1,0:T(8,128)S(1)}, f32[2,128,128]{2,1,0:T(8,128)S(1)}, u32[]{:S(2)}, u32[]{:S(2)}) collective-permute-start(f32[2,128,128]{2,1,0:T(8,128)S(1)} %get-tuple-element.96), channel_id=1, source_target_pairs={{0,2},{1,3},{2,0},{3,1},{4,6},{5,7},{6,4},{7,5},{8,10},{9,11},{10,... | collective-permute-start | bytes 393224 | tf_op jit(solution)/shard_map/ppermute | solution.py:258

commit v7 on v4

--- a/solution.py
+++ b/solution.py
@@ -323,7 +323,7 @@
         (shape(2, width, width),) * 2 + (shape(2 * width + 8, width),) * (chips // 2 - 1), tables[4:5],
         (near, far, swapped(far, CORE), swapped(row, ROW), swapped(row_far, ROW + CORE), swapped(column, COLUMN),
          swapped(column_far, COLUMN + CORE)))
-    came = [swapped(x, 2 * ROW * (i + 1)) for i, x in reversed(list(enumerate(sends)))]
+    came = [swapped(sends[i], 2 * ROW * (i + 1)) for i in (*range(1, len(sends)), 0)]
     return square, (own, swapped(step, ROW)), [sends[0], *came]
 
 
@@ -331,10 +331,10 @@
     pieces = {0: x}
     for k in reversed(range(8, n, 4)):
         pieces[k] = swapped(x, k)
+    if held is not None:
+        x, pieces[0] = lax.optimization_barrier((x, held))
+    pieces[COLUMN] = swapped(x, COLUMN)
     pieces[ROW] = swapped(x, ROW)
-    pieces[COLUMN] = swapped(x, COLUMN)
-    if held is not None:
-        pieces[n - 4], pieces[0] = lax.optimization_barrier((pieces[n - 4], held))
     for k in reversed(range(8, n, 4)):
         pieces[k + ROW] = swapped(pieces[k], ROW)
     pieces[COLUMN + ROW] = swapped(pieces[ROW], COLUMN)

time: 121 us -> 123 us (1.017)
  waiting for transfers between devices: 51.1 us -> 53.4 us
    ppermute x48, waiting for transfers between devices: 51.1 us -> 53.4 us  [swapped(): return lax.ppermute(x, 'term', [(i, i ^ k) for i in range(n)])]
where the time goes in v7:
time: 123 us
  waiting for transfers between devices  53.4 us (43%)
  starting transfers between devices  36.4 us (30%)
  Pallas kernels  19.8 us (16%)
  blocking collectives  11.5 us (9%)
  between operations  1.43 us (1%)
    ppermute x48, waiting for transfers between devices, swapped(): return lax.ppermute(x, 'term', [(i, i ^ k) for i in range(n)])  53.4 us
    ppermute x48, starting transfers between devices, swapped(): return lax.ppermute(x, 'term', [(i, i ^ k) for i in range(n)])  36.4 us
    pallas_call x2, Pallas kernels, apply(): pl.pallas_call(functools.partial(apply_kernel, n, over_rows, rows, start)...  13.4 us
    all_to_all x1, blocking collectives, shards(): lax.all_to_all(jnp.broadcast_to(partial[None], (n, 8, width)), 'term', sp...  11.5 us
    pallas_call x5, Pallas kernels, local(): pl.pallas_call(kernel, out_shape=out_shape, in_specs=[SMEM] * len(scalars...  3.35 us
    pallas_call x1, Pallas kernels, prep(): pl.pallas_call(functools.partial(prep_kernel, n, terms * n + 1), out_shap...  3.08 us
  transfers between devices with their start and end apart: 48, of which 24 were waited for; matrix products, arithmetic and copies ran while one was open for 0% of the time, Pallas kernels for 3%

profile of v7, /device:TPU:0, one launch (start us, length us, event | category | flops | bytes accessed | tf_op | source)
XLA Modules:
  0.0 123.0 jit_solution(42099928016398918)
XLA Ops:
  0.6 5.1 %collective-permute-start.11 = (f32[2,128,128]{2,1,0:T(8,128)}, f32[2,128,128]{2,1,0:T(8,128)S(1)}, u32[]{:S(2)}, u32[]{:S(2)}) collective-permute-start(f32[2,128,128]{2,1,0:T(8,128)} %vector_in.1), channel_id=1, source_target_pairs={{0,12},{1,13},{2,14},{3,15},{4,8},{5,9},{6,10},{7,11},{8,4},{9,5},... | collective-permute-start | bytes 393224 | tf_op jit(solution)/shard_map/ppermute | solution.py:223
  6.4 0.6 copy.12
  7.0 3.1 %prep.1 = (bf16[8,128,512]{2,1,0:T(8,128)(2,1)S(1)}, bf16[2048,256]{1,0:T(8,128)(2,1)S(1)}, s32[16]{0:T(128)S(1)}, s32[16]{0:T(128)S(1)}, s32[48]{0:T(128)S(1)},...) custom-call(s32[1]{0:T(128)} %bitcast.me_ref, ...), custom_call_target="tpu_custom_call" | custom-call | tf_op jit(solution)/shard_map/prep/pallas_call | solution.py:113
  10.1 1.3 %collective-permute-start.3 = (f32[2,128,128]{2,1,0:T(8,128)S(1)}, f32[2,128,128]{2,1,0:T(8,128)S(1)}, u32[]{:S(2)}, u32[]{:S(2)}) collective-permute-start(f32[2,128,128]{2,1,0:T(8,128)S(1)} %copy-done.1), channel_id=1, source_target_pairs={{0,4},{1,5},{2,6},{3,7},{4,0},{5,1},{6,2},{7,3},{8,12},{9,13},{10,... | collective-permute-start | bytes 393224 | tf_op jit(solution)/shard_map/ppermute | solution.py:223
  11.4 2.1 %collective-permute-start.1 = (f32[2,128,128]{2,1,0:T(8,128)S(1)}, f32[2,128,128]{2,1,0:T(8,128)S(1)}, u32[]{:S(2)}, u32[]{:S(2)}) collective-permute-start(f32[2,128,128]{2,1,0:T(8,128)S(1)} %copy-done.1), channel_id=1, source_target_pairs={{0,2},{1,3},{2,0},{3,1},{4,6},{5,7},{6,4},{7,5},{8,10},{9,11},{10,... | collective-permute-start | bytes 393224 | tf_op jit(solution)/shard_map/ppermute | solution.py:223
  13.6 3.5 %collective-permute-done.7.refs_8_ = f32[2,128,128]{2,1,0:T(8,128)S(1)} collective-permute-done((f32[2,128,128]{2,1,0:T(8,128)}, f32[2,128,128]{2,1,0:T(8,128)S(1)}, u32[]{:S(2)}, u32[]{:S(2)}) %collective-permute-start.7) | collective-permute-done | bytes 131104 | tf_op jit(solution)/shard_map/ppermute | solution.py:223
  17.1 1.2 %collective-permute-done.3.refs_4_ = f32[2,128,128]{2,1,0:T(8,128)S(1)} collective-permute-done((f32[2,128,128]{2,1,0:T(8,128)S(1)}, f32[2,128,128]{2,1,0:T(8,128)S(1)}, u32[]{:S(2)}, u32[]{:S(2)}) %collective-permute-start.3) | collective-permute-done | bytes 131104 | tf_op jit(solution)/shard_map/ppermute | solution.py:223
  18.4 1.4 %collective-permute-start.9 = (f32[2,128,128]{2,1,0:T(8,128)S(1)}, f32[2,128,128]{2,1,0:T(8,128)S(1)}, u32[]{:S(2)}, u32[]{:S(2)}) collective-permute-start(f32[2,128,128]{2,1,0:T(8,128)S(1)} %collective-permute-done.7.refs_8_), channel_id=1, source_target_pairs={{0,2},{1,3},{2,0},{3,1},{4,6},{5,7},{6,4},{7,5},{8,10},{9,11},{10,... | collective-permute-start | bytes 393224 | tf_op jit(solution)/shard_map/ppermute | solution.py:223
  19.9 0.5 collective-permute-start.2
  20.5 2.8 %collective-permute-done.9.refs_10_ = f32[2,128,128]{2,1,0:T(8,128)S(1)} collective-permute-done((f32[2,128,128]{2,1,0:T(8,128)S(1)}, f32[2,128,128]{2,1,0:T(8,128)S(1)}, u32[]{:S(2)}, u32[]{:S(2)}) %collective-permute-start.9) | collective-permute-done | bytes 131104 | tf_op jit(solution)/shard_map/ppermute | solution.py:223
  23.4 0.5 collective-permute-start.10
  23.9 1.9 %collective-permute-done.5.refs_6_ = f32[2,128,128]{2,1,0:T(8,128)S(1)} collective-permute-done((f32[2,128,128]{2,1,0:T(8,128)S(1)}, f32[2,128,128]{2,1,0:T(8,128)S(1)}, u32[]{:S(2)}, u32[]{:S(2)}) %collective-permute-start.5) | collective-permute-done | bytes 131104 | tf_op jit(solution)/shard_map/ppermute | solution.py:223
  25.8 1.3 %collective-permute-done.6.refs_7_ = f32[2,128,128]{2,1,0:T(8,128)S(1)} collective-permute-done((f32[2,128,128]{2,1,0:T(8,128)S(1)}, f32[2,128,128]{2,1,0:T(8,128)S(1)}, u32[]{:S(2)}, u32[]{:S(2)}) %collective-permute-start.6) | collective-permute-done | bytes 131104 | tf_op jit(solution)/shard_map/ppermute | solution.py:223
  27.1 6.6 %apply.2 = (f32[640,128]{1,0:T(8,128)S(1)}, f32[648,128]{1,0:T(8,128)S(1)}, f32[264,128]{1,0:T(8,128)S(1)}, f32[264,128]{1,0:T(8,128)S(1)}, f32[128,128]{1,0:T(8...) custom-call(s32[16]{0:T(128)S(1)} %get-tuple-element.44.pick_ref, s32[16]{0:T(128)S(1)} %get-tuple-element.45.mine_ref, ...), custom_call_target="tpu_custom_call" | custom-call | tf_op jit(solution)/shard_map/apply/pallas_call | solution.py:197
  33.7 0.2 collective-permute-start.15
  33.9 0.6 collective-permute-start.16
  34.5 1.1 collective-permute-start.17
  35.6 0.3 collective-permute-start.18
  36.0 1.5 %collective-permute-start.19 = (f32[128,128]{1,0:T(8,128)S(1)}, f32[128,128]{1,0:T(8,128)S(1)}, u32[]{:S(2)}, u32[]{:S(2)}) collective-permute-start(f32[128,128]{1,0:T(8,128)S(1)} %get-tuple-element.62), channel_id=1, source_target_pairs={{0,5},{1,4},{2,7},{3,6},{4,1},{5,0},{6,3},{7,2},{8,13},{9,12},{10,... | collective-permute-start | bytes 196616 | tf_op jit(solution)/shard_map/ppermute | solution.py:223
  37.4 3.1 %collective-permute-done.18.column_ref = f32[128,128]{1,0:T(8,128)S(1)} collective-permute-done((f32[128,128]{1,0:T(8,128)S(1)}, f32[128,128]{1,0:T(8,128)S(1)}, u32[]{:S(2)}, u32[]{:S(2)}) %collective-permute-start.18) | collective-permute-done | bytes 65568 | tf_op jit(solution)/shard_map/ppermute | solution.py:223
  40.5 0.5 collective-permute-done.19.column_far_ref
  41.0 1.1 collective-permute-done.17.row_far_ref
  42.1 0.7 fold.2
  42.8 1.6 %collective-permute-start.21 = (f32[264,128]{1,0:T(8,128)S(1)}, f32[264,128]{1,0:T(8,128)S(1)}, u32[]{:S(2)}, u32[]{:S(2)}) collective-permute-start(f32[264,128]{1,0:T(8,128)S(1)} %get-tuple-element.67), channel_id=1, source_target_pairs={{0,8},{1,9},{2,10},{3,11},{4,12},{5,13},{6,14},{7,15},{8,0},{9,1},... | collective-permute-start | bytes 405512 | tf_op jit(solution)/shard_map/ppermute | solution.py:223
  44.4 1.2 collective-permute-start.22
  45.6 0.7 collective-permute-start.23
  46.3 1.0 collective-permute-start.20
  47.4 4.0 %collective-permute-done.20.step_ref = f32[2,128,128]{2,1,0:T(8,128)S(1)} collective-permute-done((f32[2,128,128]{2,1,0:T(8,128)S(1)}, f32[2,128,128]{2,1,0:T(8,128)S(1)}, u32[]{:S(2)}, u32[]{:S(2)}) %collective-permute-start.20) | collective-permute-done | bytes 131104 | tf_op jit(solution)/shard_map/ppermute | solution.py:223
  51.3 4.1 %collective-permute-done.21.refs_1_ = f32[264,128]{1,0:T(8,128)S(1)} collective-permute-done((f32[264,128]{1,0:T(8,128)S(1)}, f32[264,128]{1,0:T(8,128)S(1)}, u32[]{:S(2)}, u32[]{:S(2)}) %collective-permute-start.21) | collective-permute-done | bytes 135200 | tf_op jit(solution)/shard_map/ppermute | solution.py:223
  55.4 1.3 %collective-permute-done.23.refs_3_ = f32[264,128]{1,0:T(8,128)S(1)} collective-permute-done((f32[264,128]{1,0:T(8,128)S(1)}, f32[264,128]{1,0:T(8,128)S(1)}, u32[]{:S(2)}, u32[]{:S(2)}) %collective-permute-start.23) | collective-permute-done | bytes 135200 | tf_op jit(solution)/shard_map/ppermute | solution.py:223
  56.9 2.5 %collective-permute-start.35 = (f32[2,128,128]{2,1,0:T(8,128)S(1)}, f32[2,128,128]{2,1,0:T(8,128)S(1)}, u32[]{:S(2)}, u32[]{:S(2)}) collective-permute-start(f32[2,128,128]{2,1,0:T(8,128)S(1)} %step.1.refs_0_.vector_ref), channel_id=1, source_target_pairs={{0,12},{1,13},{2,14},{3,15},{4,8},{5,9},{6,10},{7,11},{8,4},{9,5},... | collective-permute-start | bytes 393224 | tf_op jit(solution)/shard_map/ppermute | solution.py:223
  59.4 1.1 collective-permute-start.31
  60.5 0.9 collective-permute-start.27
  61.4 0.9 collective-permute-start.25
  62.2 2.0 %collective-permute-done.35.refs_12_ = f32[2,128,128]{2,1,0:T(8,128)S(1)} collective-permute-done((f32[2,128,128]{2,1,0:T(8,128)S(1)}, f32[2,128,128]{2,1,0:T(8,128)S(1)}, u32[]{:S(2)}, u32[]{:S(2)}) %collective-permute-start.35) | collective-permute-done | bytes 131104 | tf_op jit(solution)/shard_map/ppermute | solution.py:223
  64.2 0.6 collective-permute-start.37
  64.8 6.9 %collective-permute-done.31.refs_8_ = f32[2,128,128]{2,1,0:T(8,128)S(1)} collective-permute-done((f32[2,128,128]{2,1,0:T(8,128)S(1)}, f32[2,128,128]{2,1,0:T(8,128)S(1)}, u32[]{:S(2)}, u32[]{:S(2)}) %collective-permute-start.31) | collective-permute-done | bytes 131104 | tf_op jit(solution)/shard_map/ppermute | solution.py:223
  71.7 0.8 collective-permute-start.33
  72.8 0.3 collective-permute-start.26
  73.4 4.3 %collective-permute-done.33.refs_10_ = f32[2,128,128]{2,1,0:T(8,128)S(1)} collective-permute-done((f32[2,128,128]{2,1,0:T(8,128)S(1)}, f32[2,128,128]{2,1,0:T(8,128)S(1)}, u32[]{:S(2)}, u32[]{:S(2)}) %collective-permute-start.33) | collective-permute-done | bytes 131104 | tf_op jit(solution)/shard_map/ppermute | solution.py:223
  77.6 0.5 collective-permute-start.34
  78.1 0.3 collective-permute-done.29.refs_6_
  78.5 0.5 collective-permute-done.38.refs_15_
  79.2 0.6 collective-permute-done.30.refs_7_
  79.8 6.8 %apply.3 = (f32[640,128]{1,0:T(8,128)S(1)}, f32[648,128]{1,0:T(8,128)S(1)}, f32[264,128]{1,0:T(8,128)S(1)}, f32[264,128]{1,0:T(8,128)S(1)}, f32[128,128]{1,0:T(8...) custom-call(s32[16]{0:T(128)S(1)} %get-tuple-element.44.pick_ref, s32[16]{0:T(128)S(1)} %get-tuple-element.45.mine_ref, ...), custom_call_target="tpu_custom_call" | custom-call | tf_op jit(solution)/shard_map/apply/pallas_call | solution.py:197
  86.6 0.2 collective-permute-start.39
  86.8 1.3 %collective-permute-start.40 = (f32[264,128]{1,0:T(8,128)S(1)}, f32[264,128]{1,0:T(8,128)S(1)}, u32[]{:S(2)}, u32[]{:S(2)}) collective-permute-start(f32[264,128]{1,0:T(8,128)S(1)} %get-tuple-element.71), channel_id=1, source_target_pairs={{0,2},{1,3},{2,0},{3,1},{4,6},{5,7},{6,4},{7,5},{8,10},{9,11},{10,... | collective-permute-start | bytes 405512 | tf_op jit(solution)/shard_map/ppermute | solution.py:223
  88.1 0.4 collective-permute-start.41
  88.5 0.3 collective-permute-start.42
  88.8 1.5 %collective-permute-start.43 = (f32[128,128]{1,0:T(8,128)S(1)}, f32[128,128]{1,0:T(8,128)S(1)}, u32[]{:S(2)}, u32[]{:S(2)}) collective-permute-start(f32[128,128]{1,0:T(8,128)S(1)} %get-tuple-element.74), channel_id=1, source_target_pairs={{0,5},{1,4},{2,7},{3,6},{4,1},{5,0},{6,3},{7,2},{8,13},{9,12},{10,... | collective-permute-start | bytes 196616 | tf_op jit(solution)/shard_map/ppermute | solution.py:223
  90.3 3.1 %collective-permute-done.42.column_ref = f32[128,128]{1,0:T(8,128)S(1)} collective-permute-done((f32[128,128]{1,0:T(8,128)S(1)}, f32[128,128]{1,0:T(8,128)S(1)}, u32[]{:S(2)}, u32[]{:S(2)}) %collective-permute-start.42) | collective-permute-done | bytes 65568 | tf_op jit(solution)/shard_map/ppermute | solution.py:223
  93.4 0.5 collective-permute-done.43.column_far_ref
  93.9 1.1 collective-permute-done.41.row_far_ref
  95.0 0.7 fold.3
  95.7 1.9 %collective-permute-start.45 = (f32[264,128]{1,0:T(8,128)S(1)}, f32[264,128]{1,0:T(8,128)S(1)}, u32[]{:S(2)}, u32[]{:S(2)}) collective-permute-start(f32[264,128]{1,0:T(8,128)S(1)} %get-tuple-element.79), channel_id=1, source_target_pairs={{0,8},{1,9},{2,10},{3,11},{4,12},{5,13},{6,14},{7,15},{8,0},{9,1},... | collective-permute-start | bytes 405512 | tf_op jit(solution)/shard_map/ppermute | solution.py:223
  97.5 1.0 collective-permute-start.46
  98.5 0.7 collective-permute-start.47
  99.2 1.5 %collective-permute-start.44 = (f32[2,128,128]{2,1,0:T(8,128)S(1)}, f32[2,128,128]{2,1,0:T(8,128)S(1)}, u32[]{:S(2)}, u32[]{:S(2)}) collective-permute-start(f32[2,128,128]{2,1,0:T(8,128)S(1)} %get-tuple-element.76), channel_id=1, source_target_pairs={{0,2},{1,3},{2,0},{3,1},{4,6},{5,7},{6,4},{7,5},{8,10},{9,11},{10,... | collective-permute-start | bytes 393224 | tf_op jit(solution)/shard_map/ppermute | solution.py:223
  100.7 3.6 %collective-permute-done.44.step_ref = f32[2,128,128]{2,1,0:T(8,128)S(1)} collective-permute-done((f32[2,128,128]{2,1,0:T(8,128)S(1)}, f32[2,128,128]{2,1,0:T(8,128)S(1)}, u32[]{:S(2)}, u32[]{:S(2)}) %collective-permute-start.44) | collective-permute-done | bytes 131104 | tf_op jit(solution)/shard_map/ppermute | solution.py:223
  104.3 4.3 %collective-permute-done.45.refs_1_ = f32[264,128]{1,0:T(8,128)S(1)} collective-permute-done((f32[264,128]{1,0:T(8,128)S(1)}, f32[264,128]{1,0:T(8,128)S(1)}, u32[]{:S(2)}, u32[]{:S(2)}) %collective-permute-start.45) | collective-permute-done | bytes 135200 | tf_op jit(solution)/shard_map/ppermute | solution.py:223
  108.6 1.3 %collective-permute-done.47.refs_3_ = f32[264,128]{1,0:T(8,128)S(1)} collective-permute-done((f32[264,128]{1,0:T(8,128)S(1)}, f32[264,128]{1,0:T(8,128)S(1)}, u32[]{:S(2)}, u32[]{:S(2)}) %collective-permute-start.47) | collective-permute-done | bytes 135200 | tf_op jit(solution)/shard_map/ppermute | solution.py:223
  109.8 0.9 last.1
  110.7 11.5 %all_to_all.5.tiles_ref = f32[16,8,128]{2,1,0:T(8,128)S(1)} all-to-all(f32[16,8,128]{2,1,0:T(8,128)S(1)} %broadcast_in_dim.2), channel_id=1, replica_groups=mesh['group'=2,'term'=16] {'term'}, dimensions={0} | all-to-all | bytes 131072 | tf_op jit(solution)/shard_map/all_to_all | solution.py:364
  122.2 0.9 norm.1
  (49 shorter events, 1.2 us)
Async XLA Ops:
  0.6 12.9 %collective-permute-start.11 = (f32[2,128,128]{2,1,0:T(8,128)}, f32[2,128,128]{2,1,0:T(8,128)S(1)}, u32[]{:S(2)}, u32[]{:S(2)}) collective-permute-start(f32[2,128,128]{2,1,0:T(8,128)} %vector_in.1), channel_id=1, source_target_pairs={{0,12},{1,13},{2,14},{3,15},{4,8},{5,9},{6,10},{7,11},{8,4},{9,5},... | collective-permute-start | bytes 393224 | tf_op jit(solution)/shard_map/ppermute | solution.py:223
  5.7 11.4 %collective-permute-start.7 = (f32[2,128,128]{2,1,0:T(8,128)}, f32[2,128,128]{2,1,0:T(8,128)S(1)}, u32[]{:S(2)}, u32[]{:S(2)}) collective-permute-start(f32[2,128,128]{2,1,0:T(8,128)} %vector_in.1), channel_id=1, source_target_pairs={{0,8},{1,9},{2,10},{3,11},{4,12},{5,13},{6,14},{7,15},{8,0},{9,1},... | collective-permute-start | bytes 393224 | tf_op jit(solution)/shard_map/ppermute | solution.py:223
  5.7 0.7 copy-start.2
  7.0 3.1 %copy-start.1 = (f32[2,128,128]{2,1,0:T(8,128)S(1)}, f32[2,128,128]{2,1,0:T(8,128)}, u32[]{:S(2)}) copy-start(f32[2,128,128]{2,1,0:T(8,128)} %vector_in.1) | copy-start | bytes 393220
  10.1 8.3 %collective-permute-start.3 = (f32[2,128,128]{2,1,0:T(8,128)S(1)}, f32[2,128,128]{2,1,0:T(8,128)S(1)}, u32[]{:S(2)}, u32[]{:S(2)}) collective-permute-start(f32[2,128,128]{2,1,0:T(8,128)S(1)} %copy-done.1), channel_id=1, source_target_pairs={{0,4},{1,5},{2,6},{3,7},{4,0},{5,1},{6,2},{7,3},{8,12},{9,13},{10,... | collective-permute-start | bytes 393224 | tf_op jit(solution)/shard_map/ppermute | solution.py:223
  11.4 8.4 %collective-permute-start.1 = (f32[2,128,128]{2,1,0:T(8,128)S(1)}, f32[2,128,128]{2,1,0:T(8,128)S(1)}, u32[]{:S(2)}, u32[]{:S(2)}) collective-permute-start(f32[2,128,128]{2,1,0:T(8,128)S(1)} %copy-done.1), channel_id=1, source_target_pairs={{0,2},{1,3},{2,0},{3,1},{4,6},{5,7},{6,4},{7,5},{8,10},{9,11},{10,... | collective-permute-start | bytes 393224 | tf_op jit(solution)/shard_map/ppermute | solution.py:223
  13.5 6.3 %collective-permute-start = (f32[2,128,128]{2,1,0:T(8,128)S(1)}, f32[2,128,128]{2,1,0:T(8,128)S(1)}, u32[]{:S(2)}, u32[]{:S(2)}) collective-permute-start(f32[2,128,128]{2,1,0:T(8,128)S(1)} %get-tuple-element.55.refs_0_.vector_ref), channel_id=1, source_target_pairs={{0,1},{1,0},{2,3},{3,2},{4,5},{5,4},{6,7},{7,6},{8,9},{9,8},{10,11... | collective-permute-start | bytes 393224 | tf_op jit(solution)/shard_map/ppermute | solution.py:223
  13.5 6.4 %collective-permute-start.13 = (f32[2,128,128]{2,1,0:T(8,128)S(1)}, f32[2,128,128]{2,1,0:T(8,128)S(1)}, u32[]{:S(2)}, u32[]{:S(2)}) collective-permute-start(f32[2,128,128]{2,1,0:T(8,128)S(1)} %collective-permute-done.11.refs_12_), channel_id=1, source_target_pairs={{0,2},{1,3},{2,0},{3,1},{4,6},{5,7},{6,4},{7,5},{8,10},{9,11},{10,... | collective-permute-start | bytes 393224 | tf_op jit(solution)/shard_map/ppermute | solution.py:223
  17.1 3.3 %collective-permute-start.12 = (f32[2,128,128]{2,1,0:T(8,128)S(1)}, f32[2,128,128]{2,1,0:T(8,128)S(1)}, u32[]{:S(2)}, u32[]{:S(2)}) collective-permute-start(f32[2,128,128]{2,1,0:T(8,128)S(1)} %collective-permute-done.11.refs_12_), channel_id=1, source_target_pairs={{0,1},{1,0},{2,3},{3,2},{4,5},{5,4},{6,7},{7,6},{8,9},{9,8},{10,11... | collective-permute-start | bytes 393224 | tf_op jit(solution)/shard_map/ppermute | solution.py:223
  18.4 5.0 %collective-permute-start.9 = (f32[2,128,128]{2,1,0:T(8,128)S(1)}, f32[2,128,128]{2,1,0:T(8,128)S(1)}, u32[]{:S(2)}, u32[]{:S(2)}) collective-permute-start(f32[2,128,128]{2,1,0:T(8,128)S(1)} %collective-permute-done.7.refs_8_), channel_id=1, source_target_pairs={{0,2},{1,3},{2,0},{3,1},{4,6},{5,7},{6,4},{7,5},{8,10},{9,11},{10,... | collective-permute-start | bytes 393224 | tf_op jit(solution)/shard_map/ppermute | solution.py:223
  19.8 3.5 %collective-permute-start.8 = (f32[2,128,128]{2,1,0:T(8,128)S(1)}, f32[2,128,128]{2,1,0:T(8,128)S(1)}, u32[]{:S(2)}, u32[]{:S(2)}) collective-permute-start(f32[2,128,128]{2,1,0:T(8,128)S(1)} %collective-permute-done.7.refs_8_), channel_id=1, source_target_pairs={{0,1},{1,0},{2,3},{3,2},{4,5},{5,4},{6,7},{7,6},{8,9},{9,8},{10,11... | collective-permute-start | bytes 393224 | tf_op jit(solution)/shard_map/ppermute | solution.py:223
  19.8 5.9 %collective-permute-start.5 = (f32[2,128,128]{2,1,0:T(8,128)S(1)}, f32[2,128,128]{2,1,0:T(8,128)S(1)}, u32[]{:S(2)}, u32[]{:S(2)}) collective-permute-start(f32[2,128,128]{2,1,0:T(8,128)S(1)} %collective-permute-done.1.refs_2_), channel_id=1, source_target_pairs={{0,4},{1,5},{2,6},{3,7},{4,0},{5,1},{6,2},{7,3},{8,12},{9,13},{10,... | collective-permute-start | bytes 393224 | tf_op jit(solution)/shard_map/ppermute | solution.py:223
  19.9 5.8 %collective-permute-start.2 = (f32[2,128,128]{2,1,0:T(8,128)S(1)}, f32[2,128,128]{2,1,0:T(8,128)S(1)}, u32[]{:S(2)}, u32[]{:S(2)}) collective-permute-start(f32[2,128,128]{2,1,0:T(8,128)S(1)} %collective-permute-done.1.refs_2_), channel_id=1, source_target_pairs={{0,1},{1,0},{2,3},{3,2},{4,5},{5,4},{6,7},{7,6},{8,9},{9,8},{10,11... | collective-permute-start | bytes 393224 | tf_op jit(solution)/shard_map/ppermute | solution.py:223
  20.4 5.3 %collective-permute-start.4 = (f32[2,128,128]{2,1,0:T(8,128)S(1)}, f32[2,128,128]{2,1,0:T(8,128)S(1)}, u32[]{:S(2)}, u32[]{:S(2)}) collective-permute-start(f32[2,128,128]{2,1,0:T(8,128)S(1)} %collective-permute-done.3.refs_4_), channel_id=1, source_target_pairs={{0,1},{1,0},{2,3},{3,2},{4,5},{5,4},{6,7},{7,6},{8,9},{9,8},{10,11... | collective-permute-start | bytes 393224 | tf_op jit(solution)/shard_map/ppermute | solution.py:223
  23.3 2.4 %collective-permute-start.14 = (f32[2,128,128]{2,1,0:T(8,128)S(1)}, f32[2,128,128]{2,1,0:T(8,128)S(1)}, u32[]{:S(2)}, u32[]{:S(2)}) collective-permute-start(f32[2,128,128]{2,1,0:T(8,128)S(1)} %collective-permute-done.13.refs_14_), channel_id=1, source_target_pairs={{0,1},{1,0},{2,3},{3,2},{4,5},{5,4},{6,7},{7,6},{8,9},{9,8},{10,11... | collective-permute-start | bytes 393224 | tf_op jit(solution)/shard_map/ppermute | solution.py:223
  23.4 2.4 %collective-permute-start.10 = (f32[2,128,128]{2,1,0:T(8,128)S(1)}, f32[2,128,128]{2,1,0:T(8,128)S(1)}, u32[]{:S(2)}, u32[]{:S(2)}) collective-permute-start(f32[2,128,128]{2,1,0:T(8,128)S(1)} %collective-permute-done.9.refs_10_), channel_id=1, source_target_pairs={{0,1},{1,0},{2,3},{3,2},{4,5},{5,4},{6,7},{7,6},{8,9},{9,8},{10,11... | collective-permute-start | bytes 393224 | tf_op jit(solution)/shard_map/ppermute | solution.py:223
  25.7 1.3 %collective-permute-start.6 = (f32[2,128,128]{2,1,0:T(8,128)S(1)}, f32[2,128,128]{2,1,0:T(8,128)S(1)}, u32[]{:S(2)}, u32[]{:S(2)}) collective-permute-start(f32[2,128,128]{2,1,0:T(8,128)S(1)} %collective-permute-done.5.refs_6_), channel_id=1, source_target_pairs={{0,1},{1,0},{2,3},{3,2},{4,5},{5,4},{6,7},{7,6},{8,9},{9,8},{10,11... | collective-permute-start | bytes 393224 | tf_op jit(solution)/shard_map/ppermute | solution.py:223
  33.7 8.4 %collective-permute-start.15 = (f32[648,128]{1,0:T(8,128)S(1)}, f32[648,128]{1,0:T(8,128)S(1)}, u32[]{:S(2)}, u32[]{:S(2)}) collective-permute-start(f32[648,128]{1,0:T(8,128)S(1)} %get-tuple-element.58.far_in), channel_id=1, source_target_pairs={{0,1},{1,0},{2,3},{3,2},{4,5},{5,4},{6,7},{7,6},{8,9},{9,8},{10,11... | collective-permute-start | bytes 995336 | tf_op jit(solution)/shard_map/ppermute | solution.py:223
  33.9 7.1 %collective-permute-start.16 = (f32[264,128]{1,0:T(8,128)S(1)}, f32[264,128]{1,0:T(8,128)S(1)}, u32[]{:S(2)}, u32[]{:S(2)}) collective-permute-start(f32[264,128]{1,0:T(8,128)S(1)} %get-tuple-element.59), channel_id=1, source_target_pairs={{0,2},{1,3},{2,0},{3,1},{4,6},{5,7},{6,4},{7,5},{8,10},{9,11},{10,... | collective-permute-start | bytes 405512 | tf_op jit(solution)/shard_map/ppermute | solution.py:223
  34.5 7.5 %collective-permute-start.17 = (f32[264,128]{1,0:T(8,128)S(1)}, f32[264,128]{1,0:T(8,128)S(1)}, u32[]{:S(2)}, u32[]{:S(2)}) collective-permute-start(f32[264,128]{1,0:T(8,128)S(1)} %get-tuple-element.60), channel_id=1, source_target_pairs={{0,3},{1,2},{2,1},{3,0},{4,7},{5,6},{6,5},{7,4},{8,11},{9,10},{10,... | collective-permute-start | bytes 405512 | tf_op jit(solution)/shard_map/ppermute | solution.py:223
  35.6 4.9 %collective-permute-start.18 = (f32[128,128]{1,0:T(8,128)S(1)}, f32[128,128]{1,0:T(8,128)S(1)}, u32[]{:S(2)}, u32[]{:S(2)}) collective-permute-start(f32[128,128]{1,0:T(8,128)S(1)} %get-tuple-element.61), channel_id=1, source_target_pairs={{0,4},{1,5},{2,6},{3,7},{4,0},{5,1},{6,2},{7,3},{8,12},{9,13},{10,... | collective-permute-start | bytes 196616 | tf_op jit(solution)/shard_map/ppermute | solution.py:223
  36.0 5.1 %collective-permute-start.19 = (f32[128,128]{1,0:T(8,128)S(1)}, f32[128,128]{1,0:T(8,128)S(1)}, u32[]{:S(2)}, u32[]{:S(2)}) collective-permute-start(f32[128,128]{1,0:T(8,128)S(1)} %get-tuple-element.62), channel_id=1, source_target_pairs={{0,5},{1,4},{2,7},{3,6},{4,1},{5,0},{6,3},{7,2},{8,13},{9,12},{10,... | collective-permute-start | bytes 196616 | tf_op jit(solution)/shard_map/ppermute | solution.py:223
  42.1 14.6 %copy-start = (f32[2,128,128]{2,1,0:T(8,128)S(1)}, f32[2,128,128]{2,1,0:T(8,128)}, u32[]{:S(2)}) copy-start(f32[2,128,128]{2,1,0:T(8,128)} %precond_ref.3) | copy-start | bytes 393220
  42.8 12.6 %collective-permute-start.21 = (f32[264,128]{1,0:T(8,128)S(1)}, f32[264,128]{1,0:T(8,128)S(1)}, u32[]{:S(2)}, u32[]{:S(2)}) collective-permute-start(f32[264,128]{1,0:T(8,128)S(1)} %get-tuple-element.67), channel_id=1, source_target_pairs={{0,8},{1,9},{2,10},{3,11},{4,12},{5,13},{6,14},{7,15},{8,0},{9,1},... | collective-permute-start | bytes 405512 | tf_op jit(solution)/shard_map/ppermute | solution.py:223
  44.4 11.0 %collective-permute-start.22 = (f32[264,128]{1,0:T(8,128)S(1)}, f32[264,128]{1,0:T(8,128)S(1)}, u32[]{:S(2)}, u32[]{:S(2)}) collective-permute-start(f32[264,128]{1,0:T(8,128)S(1)} %get-tuple-element.68), channel_id=1, source_target_pairs={{0,12},{1,13},{2,14},{3,15},{4,8},{5,9},{6,10},{7,11},{8,4},{9,5},... | collective-permute-start | bytes 405512 | tf_op jit(solution)/shard_map/ppermute | solution.py:223
  45.6 11.1 %collective-permute-start.23 = (f32[264,128]{1,0:T(8,128)S(1)}, f32[264,128]{1,0:T(8,128)S(1)}, u32[]{:S(2)}, u32[]{:S(2)}) collective-permute-start(f32[264,128]{1,0:T(8,128)S(1)} %get-tuple-element.66.refs_0_), channel_id=1, source_target_pairs={{0,4},{1,5},{2,6},{3,7},{4,0},{5,1},{6,2},{7,3},{8,12},{9,13},{10,... | collective-permute-start | bytes 405512 | tf_op jit(solution)/shard_map/ppermute | solution.py:223
  46.3 5.0 %collective-permute-start.20 = (f32[2,128,128]{2,1,0:T(8,128)S(1)}, f32[2,128,128]{2,1,0:T(8,128)S(1)}, u32[]{:S(2)}, u32[]{:S(2)}) collective-permute-start(f32[2,128,128]{2,1,0:T(8,128)S(1)} %get-tuple-element.64), channel_id=1, source_target_pairs={{0,2},{1,3},{2,0},{3,1},{4,6},{5,7},{6,4},{7,5},{8,10},{9,11},{10,... | collective-permute-start | bytes 393224 | tf_op jit(solution)/shard_map/ppermute | solution.py:223
  56.9 7.3 %collective-permute-start.35 = (f32[2,128,128]{2,1,0:T(8,128)S(1)}, f32[2,128,128]{2,1,0:T(8,128)S(1)}, u32[]{:S(2)}, u32[]{:S(2)}) collective-permute-start(f32[2,128,128]{2,1,0:T(8,128)S(1)} %step.1.refs_0_.vector_ref), channel_id=1, source_target_pairs={{0,12},{1,13},{2,14},{3,15},{4,8},{5,9},{6,10},{7,11},{8,4},{9,5},... | collective-permute-start | bytes 393224 | tf_op jit(solution)/shard_map/ppermute | solution.py:223
  59.4 12.3 %collective-permute-start.31 = (f32[2,128,128]{2,1,0:T(8,128)S(1)}, f32[2,128,128]{2,1,0:T(8,128)S(1)}, u32[]{:S(2)}, u32[]{:S(2)}) collective-permute-start(f32[2,128,128]{2,1,0:T(8,128)S(1)} %step.1.refs_0_.vector_ref), channel_id=1, source_target_pairs={{0,8},{1,9},{2,10},{3,11},{4,12},{5,13},{6,14},{7,15},{8,0},{9,1},... | collective-permute-start | bytes 393224 | tf_op jit(solution)/shard_map/ppermute | solution.py:223
  60.5 11.2 %collective-permute-start.27 = (f32[2,128,128]{2,1,0:T(8,128)S(1)}, f32[2,128,128]{2,1,0:T(8,128)S(1)}, u32[]{:S(2)}, u32[]{:S(2)}) collective-permute-start(f32[2,128,128]{2,1,0:T(8,128)S(1)} %step.1.refs_0_.vector_ref), channel_id=1, source_target_pairs={{0,4},{1,5},{2,6},{3,7},{4,0},{5,1},{6,2},{7,3},{8,12},{9,13},{10,... | collective-permute-start | bytes 393224 | tf_op jit(solution)/shard_map/ppermute | solution.py:223
  61.4 11.2 %collective-permute-start.25 = (f32[2,128,128]{2,1,0:T(8,128)S(1)}, f32[2,128,128]{2,1,0:T(8,128)S(1)}, u32[]{:S(2)}, u32[]{:S(2)}) collective-permute-start(f32[2,128,128]{2,1,0:T(8,128)S(1)} %step.1.refs_0_.vector_ref), channel_id=1, source_target_pairs={{0,2},{1,3},{2,0},{3,1},{4,6},{5,7},{6,4},{7,5},{8,10},{9,11},{10,... | collective-permute-start | bytes 393224 | tf_op jit(solution)/shard_map/ppermute | solution.py:223
  62.2 10.5 %collective-permute-start.24 = (f32[2,128,128]{2,1,0:T(8,128)S(1)}, f32[2,128,128]{2,1,0:T(8,128)S(1)}, u32[]{:S(2)}, u32[]{:S(2)}) collective-permute-start(f32[2,128,128]{2,1,0:T(8,128)S(1)} %step.1.refs_0_.vector_ref), channel_id=1, source_target_pairs={{0,1},{1,0},{2,3},{3,2},{4,5},{5,4},{6,7},{7,6},{8,9},{9,8},{10,11... | collective-permute-start | bytes 393224 | tf_op jit(solution)/shard_map/ppermute | solution.py:223
  64.2 8.6 %collective-permute-start.37 = (f32[2,128,128]{2,1,0:T(8,128)S(1)}, f32[2,128,128]{2,1,0:T(8,128)S(1)}, u32[]{:S(2)}, u32[]{:S(2)}) collective-permute-start(f32[2,128,128]{2,1,0:T(8,128)S(1)} %collective-permute-done.35.refs_12_), channel_id=1, source_target_pairs={{0,2},{1,3},{2,0},{3,1},{4,6},{5,7},{6,4},{7,5},{8,10},{9,11},{10,... | collective-permute-start | bytes 393224 | tf_op jit(solution)/shard_map/ppermute | solution.py:223
  71.7 1.4 %collective-permute-start.36 = (f32[2,128,128]{2,1,0:T(8,128)S(1)}, f32[2,128,128]{2,1,0:T(8,128)S(1)}, u32[]{:S(2)}, u32[]{:S(2)}) collective-permute-start(f32[2,128,128]{2,1,0:T(8,128)S(1)} %collective-permute-done.35.refs_12_), channel_id=1, source_target_pairs={{0,1},{1,0},{2,3},{3,2},{4,5},{5,4},{6,7},{7,6},{8,9},{9,8},{10,11... | collective-permute-start | bytes 393224 | tf_op jit(solution)/shard_map/ppermute | solution.py:223
  71.7 5.9 %collective-permute-start.33 = (f32[2,128,128]{2,1,0:T(8,128)S(1)}, f32[2,128,128]{2,1,0:T(8,128)S(1)}, u32[]{:S(2)}, u32[]{:S(2)}) collective-permute-start(f32[2,128,128]{2,1,0:T(8,128)S(1)} %collective-permute-done.31.refs_8_), channel_id=1, source_target_pairs={{0,2},{1,3},{2,0},{3,1},{4,6},{5,7},{6,4},{7,5},{8,10},{9,11},{10,... | collective-permute-start | bytes 393224 | tf_op jit(solution)/shard_map/ppermute | solution.py:223
  72.5 5.1 %collective-permute-start.32 = (f32[2,128,128]{2,1,0:T(8,128)S(1)}, f32[2,128,128]{2,1,0:T(8,128)S(1)}, u32[]{:S(2)}, u32[]{:S(2)}) collective-permute-start(f32[2,128,128]{2,1,0:T(8,128)S(1)} %collective-permute-done.31.refs_8_), channel_id=1, source_target_pairs={{0,1},{1,0},{2,3},{3,2},{4,5},{5,4},{6,7},{7,6},{8,9},{9,8},{10,11... | collective-permute-start | bytes 393224 | tf_op jit(solution)/shard_map/ppermute | solution.py:223
  72.8 5.7 %collective-permute-start.29 = (f32[2,128,128]{2,1,0:T(8,128)S(1)}, f32[2,128,128]{2,1,0:T(8,128)S(1)}, u32[]{:S(2)}, u32[]{:S(2)}) collective-permute-start(f32[2,128,128]{2,1,0:T(8,128)S(1)} %collective-permute-done.25.refs_2_), channel_id=1, source_target_pairs={{0,4},{1,5},{2,6},{3,7},{4,0},{5,1},{6,2},{7,3},{8,12},{9,13},{10,... | collective-permute-start | bytes 393224 | tf_op jit(solution)/shard_map/ppermute | solution.py:223
  72.8 5.7 %collective-permute-start.26 = (f32[2,128,128]{2,1,0:T(8,128)S(1)}, f32[2,128,128]{2,1,0:T(8,128)S(1)}, u32[]{:S(2)}, u32[]{:S(2)}) collective-permute-start(f32[2,128,128]{2,1,0:T(8,128)S(1)} %collective-permute-done.25.refs_2_), channel_id=1, source_target_pairs={{0,1},{1,0},{2,3},{3,2},{4,5},{5,4},{6,7},{7,6},{8,9},{9,8},{10,11... | collective-permute-start | bytes 393224 | tf_op jit(solution)/shard_map/ppermute | solution.py:223
  73.1 5.3 %collective-permute-start.28 = (f32[2,128,128]{2,1,0:T(8,128)S(1)}, f32[2,128,128]{2,1,0:T(8,128)S(1)}, u32[]{:S(2)}, u32[]{:S(2)}) collective-permute-start(f32[2,128,128]{2,1,0:T(8,128)S(1)} %collective-permute-done.27.refs_4_), channel_id=1, source_target_pairs={{0,1},{1,0},{2,3},{3,2},{4,5},{5,4},{6,7},{7,6},{8,9},{9,8},{10,11... | collective-permute-start | bytes 393224 | tf_op jit(solution)/shard_map/ppermute | solution.py:223
  77.6 1.3 %collective-permute-start.38 = (f32[2,128,128]{2,1,0:T(8,128)S(1)}, f32[2,128,128]{2,1,0:T(8,128)S(1)}, u32[]{:S(2)}, u32[]{:S(2)}) collective-permute-start(f32[2,128,128]{2,1,0:T(8,128)S(1)} %collective-permute-done.37.refs_14_), channel_id=1, source_target_pairs={{0,1},{1,0},{2,3},{3,2},{4,5},{5,4},{6,7},{7,6},{8,9},{9,8},{10,11... | collective-permute-start | bytes 393224 | tf_op jit(solution)/shard_map/ppermute | solution.py:223
  77.6 1.5 %collective-permute-start.34 = (f32[2,128,128]{2,1,0:T(8,128)S(1)}, f32[2,128,128]{2,1,0:T(8,128)S(1)}, u32[]{:S(2)}, u32[]{:S(2)}) collective-permute-start(f32[2,128,128]{2,1,0:T(8,128)S(1)} %collective-permute-done.33.refs_10_), channel_id=1, source_target_pairs={{0,1},{1,0},{2,3},{3,2},{4,5},{5,4},{6,7},{7,6},{8,9},{9,8},{10,11... | collective-permute-start | bytes 393224 | tf_op jit(solution)/shard_map/ppermute | solution.py:223
  78.5 1.3 %collective-permute-start.30 = (f32[2,128,128]{2,1,0:T(8,128)S(1)}, f32[2,128,128]{2,1,0:T(8,128)S(1)}, u32[]{:S(2)}, u32[]{:S(2)}) collective-permute-start(f32[2,128,128]{2,1,0:T(8,128)S(1)} %collective-permute-done.29.refs_6_), channel_id=1, source_target_pairs={{0,1},{1,0},{2,3},{3,2},{4,5},{5,4},{6,7},{7,6},{8,9},{9,8},{10,11... | collective-permute-start | bytes 393224 | tf_op jit(solution)/shard_map/ppermute | solution.py:223
  86.6 8.4 %collective-permute-start.39 = (f32[648,128]{1,0:T(8,128)S(1)}, f32[648,128]{1,0:T(8,128)S(1)}, u32[]{:S(2)}, u32[]{:S(2)}) collective-permute-start(f32[648,128]{1,0:T(8,128)S(1)} %get-tuple-element.70.far_in), channel_id=1, source_target_pairs={{0,1},{1,0},{2,3},{3,2},{4,5},{5,4},{6,7},{7,6},{8,9},{9,8},{10,11... | collective-permute-start | bytes 995336 | tf_op jit(solution)/shard_map/ppermute | solution.py:223
  86.8 7.1 %collective-permute-start.40 = (f32[264,128]{1,0:T(8,128)S(1)}, f32[264,128]{1,0:T(8,128)S(1)}, u32[]{:S(2)}, u32[]{:S(2)}) collective-permute-start(f32[264,128]{1,0:T(8,128)S(1)} %get-tuple-element.71), channel_id=1, source_target_pairs={{0,2},{1,3},{2,0},{3,1},{4,6},{5,7},{6,4},{7,5},{8,10},{9,11},{10,... | collective-permute-start | bytes 405512 | tf_op jit(solution)/shard_map/ppermute | solution.py:223
  88.1 6.9 %collective-permute-start.41 = (f32[264,128]{1,0:T(8,128)S(1)}, f32[264,128]{1,0:T(8,128)S(1)}, u32[]{:S(2)}, u32[]{:S(2)}) collective-permute-start(f32[264,128]{1,0:T(8,128)S(1)} %get-tuple-element.72), channel_id=1, source_target_pairs={{0,3},{1,2},{2,1},{3,0},{4,7},{5,6},{6,5},{7,4},{8,11},{9,10},{10,... | collective-permute-start | bytes 405512 | tf_op jit(solution)/shard_map/ppermute | solution.py:223
  88.5 4.9 %collective-permute-start.42 = (f32[128,128]{1,0:T(8,128)S(1)}, f32[128,128]{1,0:T(8,128)S(1)}, u32[]{:S(2)}, u32[]{:S(2)}) collective-permute-start(f32[128,128]{1,0:T(8,128)S(1)} %get-tuple-element.73), channel_id=1, source_target_pairs={{0,4},{1,5},{2,6},{3,7},{4,0},{5,1},{6,2},{7,3},{8,12},{9,13},{10,... | collective-permute-start | bytes 196616 | tf_op jit(solution)/shard_map/ppermute | solution.py:223
  88.8 5.1 %collective-permute-start.43 = (f32[128,128]{1,0:T(8,128)S(1)}, f32[128,128]{1,0:T(8,128)S(1)}, u32[]{:S(2)}, u32[]{:S(2)}) collective-permute-start(f32[128,128]{1,0:T(8,128)S(1)} %get-tuple-element.74), channel_id=1, source_target_pairs={{0,5},{1,4},{2,7},{3,6},{4,1},{5,0},{6,3},{7,2},{8,13},{9,12},{10,... | collective-permute-start | bytes 196616 | tf_op jit(solution)/shard_map/ppermute | solution.py:223
  95.7 12.9 %collective-permute-start.45 = (f32[264,128]{1,0:T(8,128)S(1)}, f32[264,128]{1,0:T(8,128)S(1)}, u32[]{:S(2)}, u32[]{:S(2)}) collective-permute-start(f32[264,128]{1,0:T(8,128)S(1)} %get-tuple-element.79), channel_id=1, source_target_pairs={{0,8},{1,9},{2,10},{3,11},{4,12},{5,13},{6,14},{7,15},{8,0},{9,1},... | collective-permute-start | bytes 405512 | tf_op jit(solution)/shard_map/ppermute | solution.py:223
  97.5 11.0 %collective-permute-start.46 = (f32[264,128]{1,0:T(8,128)S(1)}, f32[264,128]{1,0:T(8,128)S(1)}, u32[]{:S(2)}, u32[]{:S(2)}) collective-permute-start(f32[264,128]{1,0:T(8,128)S(1)} %get-tuple-element.80), channel_id=1, source_target_pairs={{0,12},{1,13},{2,14},{3,15},{4,8},{5,9},{6,10},{7,11},{8,4},{9,5},... | collective-permute-start | bytes 405512 | tf_op jit(solution)/shard_map/ppermute | solution.py:223
  98.5 11.3 %collective-permute-start.47 = (f32[264,128]{1,0:T(8,128)S(1)}, f32[264,128]{1,0:T(8,128)S(1)}, u32[]{:S(2)}, u32[]{:S(2)}) collective-permute-start(f32[264,128]{1,0:T(8,128)S(1)} %get-tuple-element.78.refs_0_), channel_id=1, source_target_pairs={{0,4},{1,5},{2,6},{3,7},{4,0},{5,1},{6,2},{7,3},{8,12},{9,13},{10,... | collective-permute-start | bytes 405512 | tf_op jit(solution)/shard_map/ppermute | solution.py:223
  99.2 5.1 %collective-permute-start.44 = (f32[2,128,128]{2,1,0:T(8,128)S(1)}, f32[2,128,128]{2,1,0:T(8,128)S(1)}, u32[]{:S(2)}, u32[]{:S(2)}) collective-permute-start(f32[2,128,128]{2,1,0:T(8,128)S(1)} %get-tuple-element.76), channel_id=1, source_target_pairs={{0,2},{1,3},{2,0},{3,1},{4,6},{5,7},{6,4},{7,5},{8,10},{9,11},{10,... | collective-permute-start | bytes 393224 | tf_op jit(solution)/shard_map/ppermute | solution.py:223

commit v8 on v7

--- a/solution.py
+++ b/solution.py
@@ -9,6 +9,7 @@
 
 ITERS = 2
 CORE, ROW, COLUMN = 1, 2, 4
+SPLIT = 8
 SENDERS = 6
 SMEM = pl.BlockSpec(memory_space=pltpu.SMEM)
 VMEM = pl.BlockSpec(memory_space=pltpu.VMEM)
@@ -136,9 +137,20 @@
     )(me, at_home(fetch), at_home(store), at_home(pairs), live, at_home(vector), at_home(left_ops), at_home(right_ops))
 
 
+def block_of(refs, which):
+    if len(refs) == 1:
+        return refs[0][which]
+    first = (which == 0).astype(jnp.float32)
+    return refs[0][0] * first + refs[1][0] * (1.0 - first)
+
+
 def apply_kernel(n, over_rows, rows, start, pick_ref, mine_ref, first_ref, second_ref, dst_ref, one_ref, two_ref, count_ref,
                  l4_ref, rr_ref, *refs):
-    pieces, (near_ref, far_ref, row_ref, row_far_ref, column_ref, column_far_ref, square_ref, block, total) = refs[:n], refs[n:]
+    refs = list(refs)
+    pieces, refs = [], refs
+    for r in range(n):
+        pieces.append([refs.pop(0) for _ in range(2 if SPLIT <= r < SPLIT + 4 else 1)])
+    (near_ref, far_ref, row_ref, row_far_ref, column_ref, column_far_ref, square_ref, block, total) = refs
     terms, width = l4_ref.shape[:2]
     square = jnp.zeros((8, width), jnp.float32)
     product = jnp.zeros((8, width), jnp.float32)
@@ -147,10 +159,11 @@
     for c in range(n // 2):
         columns = []
         for r in (2 * c, 2 * c + 1):
-            high, low = halves(pieces[r][pick_ref[r]])
+            high, low = halves(block_of(pieces[r], pick_ref[r]))
             columns.append(jnp.concatenate([high, high, low, low], axis=0))
-            held = pieces[r][:, start:start + rows, :]
-            square = square + tile_sum(held * held)
+            for ref in pieces[r]:
+                held = ref[:, start:start + rows, :]
+                square = square + tile_sum(held * held)
         both = jnp.dot(left, jnp.concatenate(columns, axis=1), preferred_element_type=jnp.float32)
         for k in range(2):
             at = (2 * c + k) * terms
@@ -175,7 +188,7 @@
         slots = both[:, :width] + both[:, width:]
         for r in range(low_end, low_end + 4):
             slot = slots[(r - low_end) * rows:(r - low_end + 1) * rows]
-            product = product + tile_sum(pieces[r][mine_ref[r], start:start + rows, :] * slot)
+            product = product + tile_sum(block_of(pieces[r], mine_ref[r])[start:start + rows] * slot)
             g, core = divmod(r, 2)
             if g == 3:
                 (column_far_ref if core else column_ref)[...] = slot
@@ -198,7 +211,7 @@
         functools.partial(apply_kernel, n, over_rows, rows, start),
         out_shape=(shape(late * rows, width), shape(late * rows + 8, width)) + (shape(len(over_rows) * rows + 8, width),) * 2
         + (shape(rows, width),) * 2 + (shape(8, width),),
-        in_specs=[SMEM] * 8 + [VMEM] * (2 + n),
+        in_specs=[SMEM] * 8 + [VMEM] * (2 + n + 4),
         out_specs=[VMEM] * 7,
         scratch_shapes=[
             pltpu.VMEM((terms * n + 1 + spare, rows, width), jnp.float32),
@@ -206,7 +219,7 @@
         ],
         compiler_params=params(32 if n <= 16 else 56),
         name="apply",
-    )(*tables[2:4], *tables[5:], *tables[:2], *pieces)
+    )(*tables[2:4], *tables[5:], *tables[:2], *(x for piece in pieces for x in piece))
 
 
 def joined(parts, count):
@@ -277,12 +290,14 @@
 
 
 def step_kernel(own_ref, step_ref, square_ref, vector_ref, precond_ref, *refs):
-    out_ref = refs[-1]
-    sigma, product = landed(own_ref, step_ref, refs[:-1])
+    out_ref, *half_refs = refs[-3:]
+    sigma, product = landed(own_ref, step_ref, refs[:-3])
     theta = product / jnp.sum(square_ref[...])
     for b in range(2):
         v = vector_ref[b]
-        out_ref[b] = v - precond_ref[b] * (sigma[b] - theta * v)
+        corrected = v - precond_ref[b] * (sigma[b] - theta * v)
+        out_ref[b] = corrected
+        half_refs[b][0] = corrected
 
 
 def last_kernel(cells, own_ref, step_ref, square_ref, vector_ref, precond_ref, *refs):
@@ -308,7 +323,7 @@
 
 
 def scattered(n, tables, pieces):
-    width = pieces[0].shape[1]
+    width = pieces[0][0].shape[1]
     chips = n // 2
     rows = width if n <= 16 else width // 4
     over_rows = list(range(chips - 1, 3, -2))
@@ -327,19 +342,23 @@
     return square, (own, swapped(step, ROW)), [sends[0], *came]
 
 
-def gathered(n, x, held=None):
-    pieces = {0: x}
+def gathered(n, x, blocks, held=None):
+    def through(arrays, k):
+        return [swapped(array, k) for array in arrays]
+
+    pieces = {0: [x]}
     for k in reversed(range(8, n, 4)):
-        pieces[k] = swapped(x, k)
+        pieces[k] = through(blocks if k == SPLIT else [x], k)
+    pieces[ROW] = through([x], ROW)
+    pieces[COLUMN] = through([x], COLUMN)
     if held is not None:
-        x, pieces[0] = lax.optimization_barrier((x, held))
-    pieces[COLUMN] = swapped(x, COLUMN)
-    pieces[ROW] = swapped(x, ROW)
+        (pieces[n - 4][0], held) = lax.optimization_barrier((pieces[n - 4][0], held))
+        pieces[0] = [held]
     for k in reversed(range(8, n, 4)):
-        pieces[k + ROW] = swapped(pieces[k], ROW)
-    pieces[COLUMN + ROW] = swapped(pieces[ROW], COLUMN)
+        pieces[k + ROW] = through(pieces[k], ROW)
+    pieces[COLUMN + ROW] = through(pieces[ROW], COLUMN)
     for k in range(0, n, 2):
-        pieces[k + CORE] = swapped(pieces[k], CORE)
+        pieces[k + CORE] = through(pieces[k], CORE)
     return [pieces[k] for k in range(n)]
 
 
@@ -352,13 +371,15 @@
     block = jax.ShapeDtypeStruct(wavefn.shape, jnp.float32)
     tile = jax.ShapeDtypeStruct((8, width), jnp.float32)
     vector = wavefn
+    blocks = [wavefn[b:b + 1] for b in range(2)]
     for iteration in range(ITERS):
-        pieces = gathered(n, vector, held if iteration == 0 else None)
-        vector = pieces[0]
+        pieces = gathered(n, vector, blocks, held if iteration == 0 else None)
+        vector = pieces[0][0]
         square, sums, parts = scattered(n, tables, pieces)
         arrays = (*sums, square, vector, precond, *parts)
         if iteration < ITERS - 1:
-            vector = local(step_kernel, "step", block, (), arrays)
+            half = jax.ShapeDtypeStruct((1, width, width), jnp.float32)
+            vector, *blocks = local(step_kernel, "step", (block, half, half), (), arrays)
     residual, corrected, partial = local(
         functools.partial(last_kernel, cells), "last", (block, block, tile), (), arrays)
     tiles = lax.all_to_all(jnp.broadcast_to(partial[None], (n, 8, width)), "term",

time: 123 us -> 131 us (1.065)
  starting transfers between devices: 36.4 us -> 44.7 us
  waiting for transfers between devices: 53.4 us -> 50.2 us
    ppermute x48 -> x56, starting transfers between devices: 36.4 us -> 44.7 us  [swapped(): return lax.ppermute(x, 'term', [(i, i ^ k) for i in range(n)])]
    ppermute x48 -> x56, waiting for transfers between devices: 53.4 us -> 50.2 us  [swapped(): return lax.ppermute(x, 'term', [(i, i ^ k) for i in range(n)])]
  transfers between devices with their start and end apart: 48 -> 56, of which waited for: 24 -> 27; matrix products, arithmetic and copies ran while one was open for 0% -> 0% of each run, Pallas kernels for 3% -> 3%
where the time goes in v8:
time: 131 us; the launch traced here: 130 us
  waiting for transfers between devices  50.2 us (38%)
  starting transfers between devices  44.7 us (34%)
  Pallas kernels  21.1 us (16%)
  blocking collectives  11.4 us (9%)
  local copies, waits for them, and re-layouts  1.53 us (1%)
  between operations  1.43 us (1%)
    ppermute x56, waiting for transfers between devices, swapped(): return lax.ppermute(x, 'term', [(i, i ^ k) for i in range(n)])  50.2 us
    ppermute x56, starting transfers between devices, swapped(): return lax.ppermute(x, 'term', [(i, i ^ k) for i in range(n)])  44.7 us
    pallas_call x2, Pallas kernels, apply(): pl.pallas_call(functools.partial(apply_kernel, n, over_rows, rows, start)...  13.6 us
    all_to_all x1, blocking collectives, shards(): lax.all_to_all(jnp.broadcast_to(partial[None], (n, 8, width)), 'term', sp...  11.4 us
    pallas_call x1, Pallas kernels, prep(): pl.pallas_call(functools.partial(prep_kernel, n, terms * n + 1), out_shap...  4.19 us
    pallas_call x5, Pallas kernels, local(): pl.pallas_call(kernel, out_shape=out_shape, in_specs=[SMEM] * len(scalars...  3.35 us
  transfers between devices with their start and end apart: 56, of which 27 were waited for; matrix products, arithmetic and copies ran while one was open for 0% of the time, Pallas kernels for 3%

profile of v8, /device:TPU:0, one launch (start us, length us, event | category | flops | bytes accessed | tf_op | source)
XLA Modules:
  0.0 130.3 jit_solution(15197182389153786250)
XLA Ops:
  0.6 0.9 fusion
  1.6 4.1 %collective-permute-start.9 = (f32[1,128,128]{2,1,0:T(8,128)S(1)}, f32[1,128,128]{2,1,0:T(8,128)S(1)}, u32[]{:S(2)}, u32[]{:S(2)}) collective-permute-start(f32[1,128,128]{2,1,0:T(8,128)S(1)} %get-tuple-element.90), channel_id=1, source_target_pairs={{0,8},{1,9},{2,10},{3,11},{4,12},{5,13},{6,14},{7,15},{8,0},{9,1},... | collective-permute-start | bytes 196616 | tf_op jit(solution)/shard_map/ppermute | solution.py:236
  5.7 1.3 %collective-permute-start = (f32[2,128,128]{2,1,0:T(8,128)S(1)}, f32[2,128,128]{2,1,0:T(8,128)S(1)}, u32[]{:S(2)}, u32[]{:S(2)}) collective-permute-start(f32[2,128,128]{2,1,0:T(8,128)S(1)} %copy-done.1), channel_id=1, source_target_pairs={{0,12},{1,13},{2,14},{3,15},{4,8},{5,9},{6,10},{7,11},{8,4},{9,5},... | collective-permute-start | bytes 393224 | tf_op jit(solution)/shard_map/ppermute | solution.py:236
  7.0 1.5 %collective-permute-start.2 = (f32[2,128,128]{2,1,0:T(8,128)S(1)}, f32[2,128,128]{2,1,0:T(8,128)S(1)}, u32[]{:S(2)}, u32[]{:S(2)}) collective-permute-start(f32[2,128,128]{2,1,0:T(8,128)S(1)} %copy-done.1), channel_id=1, source_target_pairs={{0,2},{1,3},{2,0},{3,1},{4,6},{5,7},{6,4},{7,5},{8,10},{9,11},{10,... | collective-permute-start | bytes 393224 | tf_op jit(solution)/shard_map/ppermute | solution.py:236
  8.5 1.7 %collective-permute-start.8 = (f32[1,128,128]{2,1,0:T(8,128)S(1)}, f32[1,128,128]{2,1,0:T(8,128)S(1)}, u32[]{:S(2)}, u32[]{:S(2)}) collective-permute-start(f32[1,128,128]{2,1,0:T(8,128)S(1)} %get-tuple-element.91), channel_id=1, source_target_pairs={{0,8},{1,9},{2,10},{3,11},{4,12},{5,13},{6,14},{7,15},{8,0},{9,1},... | collective-permute-start | bytes 196616 | tf_op jit(solution)/shard_map/ppermute | solution.py:236
  10.2 5.3 %collective-permute-start.13 = (f32[1,128,128]{2,1,0:T(8,128)S(1)}, f32[1,128,128]{2,1,0:T(8,128)S(1)}, u32[]{:S(2)}, u32[]{:S(2)}) collective-permute-start(f32[1,128,128]{2,1,0:T(8,128)S(1)} %collective-permute-done.9.refs_9_), channel_id=1, source_target_pairs={{0,2},{1,3},{2,0},{3,1},{4,6},{5,7},{6,4},{7,5},{8,10},{9,11},{10,... | collective-permute-start | bytes 196616 | tf_op jit(solution)/shard_map/ppermute | solution.py:236
  15.5 0.5 collective-permute-start.4
  16.0 1.8 %collective-permute-done.8.refs_8_ = f32[1,128,128]{2,1,0:T(8,128)S(1)} collective-permute-done((f32[1,128,128]{2,1,0:T(8,128)S(1)}, f32[1,128,128]{2,1,0:T(8,128)S(1)}, u32[]{:S(2)}, u32[]{:S(2)}) %collective-permute-start.8) | collective-permute-done | bytes 65568 | tf_op jit(solution)/shard_map/ppermute | solution.py:236
  17.9 1.9 %collective-permute-start.12 = (f32[1,128,128]{2,1,0:T(8,128)S(1)}, f32[1,128,128]{2,1,0:T(8,128)S(1)}, u32[]{:S(2)}, u32[]{:S(2)}) collective-permute-start(f32[1,128,128]{2,1,0:T(8,128)S(1)} %collective-permute-done.8.refs_8_), channel_id=1, source_target_pairs={{0,2},{1,3},{2,0},{3,1},{4,6},{5,7},{6,4},{7,5},{8,10},{9,11},{10,... | collective-permute-start | bytes 196616 | tf_op jit(solution)/shard_map/ppermute | solution.py:236
  20.4 0.6 copy.12
  21.0 4.2 %prep.1 = (bf16[8,128,512]{2,1,0:T(8,128)(2,1)S(1)}, bf16[2048,256]{1,0:T(8,128)(2,1)S(1)}, s32[16]{0:T(128)S(1)}, s32[16]{0:T(128)S(1)}, s32[48]{0:T(128)S(1)},...) custom-call(s32[1]{0:T(128)} %bitcast.me_ref, ...), custom_call_target="tpu_custom_call" | custom-call | tf_op jit(solution)/shard_map/prep/pallas_call | solution.py:114
  26.0 0.5 collective-permute-done.10.refs_10_
  26.7 0.4 collective-permute-start.14
  27.1 0.7 collective-permute-done.15.refs_15_
  28.0 0.4 collective-permute-start.1
  28.3 2.9 %collective-permute-done.6.refs_6_ = f32[2,128,128]{2,1,0:T(8,128)S(1)} collective-permute-done((f32[2,128,128]{2,1,0:T(8,128)S(1)}, f32[2,128,128]{2,1,0:T(8,128)S(1)}, u32[]{:S(2)}, u32[]{:S(2)}) %collective-permute-start.6) | collective-permute-done | bytes 131104 | tf_op jit(solution)/shard_map/ppermute | solution.py:236
  31.2 0.5 collective-permute-start.7
  31.8 0.8 collective-permute-done.5.refs_5_
  33.1 6.7 %apply.2 = (f32[640,128]{1,0:T(8,128)S(1)}, f32[648,128]{1,0:T(8,128)S(1)}, f32[264,128]{1,0:T(8,128)S(1)}, f32[264,128]{1,0:T(8,128)S(1)}, f32[128,128]{1,0:T(8...) custom-call(s32[16]{0:T(128)S(1)} %get-tuple-element.47.pick_ref, s32[16]{0:T(128)S(1)} %get-tuple-element.48.mine_ref, ...), custom_call_target="tpu_custom_call" | custom-call | tf_op jit(solution)/shard_map/apply/pallas_call | solution.py:210
  40.1 1.6 %collective-permute-start.21 = (f32[264,128]{1,0:T(8,128)S(1)}, f32[264,128]{1,0:T(8,128)S(1)}, u32[]{:S(2)}, u32[]{:S(2)}) collective-permute-start(f32[264,128]{1,0:T(8,128)S(1)} %get-tuple-element.63), channel_id=1, source_target_pairs={{0,3},{1,2},{2,1},{3,0},{4,7},{5,6},{6,5},{7,4},{8,11},{9,10},{10,... | collective-permute-start | bytes 405512 | tf_op jit(solution)/shard_map/ppermute | solution.py:236
  41.7 1.6 %collective-permute-start.22 = (f32[128,128]{1,0:T(8,128)S(1)}, f32[128,128]{1,0:T(8,128)S(1)}, u32[]{:S(2)}, u32[]{:S(2)}) collective-permute-start(f32[128,128]{1,0:T(8,128)S(1)} %get-tuple-element.64), channel_id=1, source_target_pairs={{0,4},{1,5},{2,6},{3,7},{4,0},{5,1},{6,2},{7,3},{8,12},{9,13},{10,... | collective-permute-start | bytes 196616 | tf_op jit(solution)/shard_map/ppermute | solution.py:236
  43.4 2.6 %collective-permute-done.22.column_ref = f32[128,128]{1,0:T(8,128)S(1)} collective-permute-done((f32[128,128]{1,0:T(8,128)S(1)}, f32[128,128]{1,0:T(8,128)S(1)}, u32[]{:S(2)}, u32[]{:S(2)}) %collective-permute-start.22) | collective-permute-done | bytes 65568 | tf_op jit(solution)/shard_map/ppermute | solution.py:236
  46.1 1.4 %collective-permute-done.23.column_far_ref = f32[128,128]{1,0:T(8,128)S(1)} collective-permute-done((f32[128,128]{1,0:T(8,128)S(1)}, f32[128,128]{1,0:T(8,128)S(1)}, u32[]{:S(2)}, u32[]{:S(2)}) %collective-permute-start.23) | collective-permute-done | bytes 65568 | tf_op jit(solution)/shard_map/ppermute | solution.py:236
  47.4 0.9 collective-permute-done.21.row_far_ref
  48.3 0.7 fold.2
  49.0 2.0 %collective-permute-start.25 = (f32[264,128]{1,0:T(8,128)S(1)}, f32[264,128]{1,0:T(8,128)S(1)}, u32[]{:S(2)}, u32[]{:S(2)}) collective-permute-start(f32[264,128]{1,0:T(8,128)S(1)} %get-tuple-element.70), channel_id=1, source_target_pairs={{0,8},{1,9},{2,10},{3,11},{4,12},{5,13},{6,14},{7,15},{8,0},{9,1},... | collective-permute-start | bytes 405512 | tf_op jit(solution)/shard_map/ppermute | solution.py:236
  51.0 2.0 %collective-permute-start.26 = (f32[264,128]{1,0:T(8,128)S(1)}, f32[264,128]{1,0:T(8,128)S(1)}, u32[]{:S(2)}, u32[]{:S(2)}) collective-permute-start(f32[264,128]{1,0:T(8,128)S(1)} %get-tuple-element.71), channel_id=1, source_target_pairs={{0,12},{1,13},{2,14},{3,15},{4,8},{5,9},{6,10},{7,11},{8,4},{9,5},... | collective-permute-start | bytes 405512 | tf_op jit(solution)/shard_map/ppermute | solution.py:236
  53.3 4.8 %collective-permute-done.24.step_ref = f32[2,128,128]{2,1,0:T(8,128)S(1)} collective-permute-done((f32[2,128,128]{2,1,0:T(8,128)S(1)}, f32[2,128,128]{2,1,0:T(8,128)S(1)}, u32[]{:S(2)}, u32[]{:S(2)}) %collective-permute-start.24) | collective-permute-done | bytes 131104 | tf_op jit(solution)/shard_map/ppermute | solution.py:236
  58.1 4.1 %collective-permute-done.25.refs_1_ = f32[264,128]{1,0:T(8,128)S(1)} collective-permute-done((f32[264,128]{1,0:T(8,128)S(1)}, f32[264,128]{1,0:T(8,128)S(1)}, u32[]{:S(2)}, u32[]{:S(2)}) %collective-permute-start.25) | collective-permute-done | bytes 135200 | tf_op jit(solution)/shard_map/ppermute | solution.py:236
  62.2 0.7 collective-permute-done.27.refs_3_
  63.1 2.9 %collective-permute-start.35 = (f32[1,128,128]{2,1,0:T(8,128)S(1)}, f32[1,128,128]{2,1,0:T(8,128)S(1)}, u32[]{:S(2)}, u32[]{:S(2)}) collective-permute-start(f32[1,128,128]{2,1,0:T(8,128)S(1)} %get-tuple-element.73), channel_id=1, source_target_pairs={{0,8},{1,9},{2,10},{3,11},{4,12},{5,13},{6,14},{7,15},{8,0},{9,1},... | collective-permute-start | bytes 196616 | tf_op jit(solution)/shard_map/ppermute | solution.py:236
  66.0 1.7 %collective-permute-start.43 = (f32[2,128,128]{2,1,0:T(8,128)S(1)}, f32[2,128,128]{2,1,0:T(8,128)S(1)}, u32[]{:S(2)}, u32[]{:S(2)}) collective-permute-start(f32[2,128,128]{2,1,0:T(8,128)S(1)} %get-tuple-element.72.refs_0_.vector_ref), channel_id=1, source_target_pairs={{0,12},{1,13},{2,14},{3,15},{4,8},{5,9},{6,10},{7,11},{8,4},{9,5},... | collective-permute-start | bytes 393224 | tf_op jit(solution)/shard_map/ppermute | solution.py:236
  67.7 0.5 collective-permute-start.29
  68.2 4.2 %collective-permute-done.35.refs_8_ = f32[1,128,128]{2,1,0:T(8,128)S(1)} collective-permute-done((f32[1,128,128]{2,1,0:T(8,128)S(1)}, f32[1,128,128]{2,1,0:T(8,128)S(1)}, u32[]{:S(2)}, u32[]{:S(2)}) %collective-permute-start.35) | collective-permute-done | bytes 65568 | tf_op jit(solution)/shard_map/ppermute | solution.py:236
  72.3 5.4 %collective-permute-done.36.refs_9_ = f32[1,128,128]{2,1,0:T(8,128)S(1)} collective-permute-done((f32[1,128,128]{2,1,0:T(8,128)S(1)}, f32[1,128,128]{2,1,0:T(8,128)S(1)}, u32[]{:S(2)}, u32[]{:S(2)}) %collective-permute-start.36) | collective-permute-done | bytes 65568 | tf_op jit(solution)/shard_map/ppermute | solution.py:236
  77.7 0.9 collective-permute-start.39
  78.7 1.2 collective-permute-start.40
  79.8 0.9 collective-permute-start.45
  80.8 1.5 %collective-permute-done.39.refs_12_ = f32[1,128,128]{2,1,0:T(8,128)S(1)} collective-permute-done((f32[1,128,128]{2,1,0:T(8,128)S(1)}, f32[1,128,128]{2,1,0:T(8,128)S(1)}, u32[]{:S(2)}, u32[]{:S(2)}) %collective-permute-start.39) | collective-permute-done | bytes 65568 | tf_op jit(solution)/shard_map/ppermute | solution.py:236
  82.3 0.5 collective-permute-start.41
  82.8 0.9 collective-permute-done.40.refs_13_
  83.7 0.5 collective-permute-start.44
  84.3 0.7 collective-permute-done.42.refs_15_
  85.1 1.1 collective-permute-done.45.refs_18_
  86.2 0.5 collective-permute-start.34
  86.7 0.8 collective-permute-done.46.refs_19_
  87.7 6.9 %apply.3 = (f32[640,128]{1,0:T(8,128)S(1)}, f32[648,128]{1,0:T(8,128)S(1)}, f32[264,128]{1,0:T(8,128)S(1)}, f32[264,128]{1,0:T(8,128)S(1)}, f32[128,128]{1,0:T(8...) custom-call(s32[16]{0:T(128)S(1)} %get-tuple-element.47.pick_ref, s32[16]{0:T(128)S(1)} %get-tuple-element.48.mine_ref, ...), custom_call_target="tpu_custom_call" | custom-call | tf_op jit(solution)/shard_map/apply/pallas_call | solution.py:210
  94.9 1.0 collective-permute-start.48
  95.8 0.7 collective-permute-start.49
  96.6 1.8 %collective-permute-start.51 = (f32[128,128]{1,0:T(8,128)S(1)}, f32[128,128]{1,0:T(8,128)S(1)}, u32[]{:S(2)}, u32[]{:S(2)}) collective-permute-start(f32[128,128]{1,0:T(8,128)S(1)} %get-tuple-element.80), channel_id=1, source_target_pairs={{0,5},{1,4},{2,7},{3,6},{4,1},{5,0},{6,3},{7,2},{8,13},{9,12},{10,... | collective-permute-start | bytes 196616 | tf_op jit(solution)/shard_map/ppermute | solution.py:236
  98.4 3.1 %collective-permute-done.50.column_ref = f32[128,128]{1,0:T(8,128)S(1)} collective-permute-done((f32[128,128]{1,0:T(8,128)S(1)}, f32[128,128]{1,0:T(8,128)S(1)}, u32[]{:S(2)}, u32[]{:S(2)}) %collective-permute-start.50) | collective-permute-done | bytes 65568 | tf_op jit(solution)/shard_map/ppermute | solution.py:236
  101.4 0.5 collective-permute-done.51.column_far_ref
  102.0 1.0 collective-permute-done.49.row_far_ref
  103.0 0.7 fold.3
  103.7 0.5 collective-permute-start.53
  104.2 1.8 %collective-permute-start.54 = (f32[264,128]{1,0:T(8,128)S(1)}, f32[264,128]{1,0:T(8,128)S(1)}, u32[]{:S(2)}, u32[]{:S(2)}) collective-permute-start(f32[264,128]{1,0:T(8,128)S(1)} %get-tuple-element.86), channel_id=1, source_target_pairs={{0,12},{1,13},{2,14},{3,15},{4,8},{5,9},{6,10},{7,11},{8,4},{9,5},... | collective-permute-start | bytes 405512 | tf_op jit(solution)/shard_map/ppermute | solution.py:236
  106.0 1.3 collective-permute-start.55
  107.2 1.0 collective-permute-start.52
  108.2 4.0 %collective-permute-done.52.step_ref = f32[2,128,128]{2,1,0:T(8,128)S(1)} collective-permute-done((f32[2,128,128]{2,1,0:T(8,128)S(1)}, f32[2,128,128]{2,1,0:T(8,128)S(1)}, u32[]{:S(2)}, u32[]{:S(2)}) %collective-permute-start.52) | collective-permute-done | bytes 131104 | tf_op jit(solution)/shard_map/ppermute | solution.py:236
  112.2 3.6 %collective-permute-done.53.refs_1_ = f32[264,128]{1,0:T(8,128)S(1)} collective-permute-done((f32[264,128]{1,0:T(8,128)S(1)}, f32[264,128]{1,0:T(8,128)S(1)}, u32[]{:S(2)}, u32[]{:S(2)}) %collective-permute-start.53) | collective-permute-done | bytes 135200 | tf_op jit(solution)/shard_map/ppermute | solution.py:236
  115.9 1.3 %collective-permute-done.55.refs_3_ = f32[264,128]{1,0:T(8,128)S(1)} collective-permute-done((f32[264,128]{1,0:T(8,128)S(1)}, f32[264,128]{1,0:T(8,128)S(1)}, u32[]{:S(2)}, u32[]{:S(2)}) %collective-permute-start.55) | collective-permute-done | bytes 135200 | tf_op jit(solution)/shard_map/ppermute | solution.py:236
  117.2 0.9 last.1
  118.1 11.4 %all_to_all.5.tiles_ref = f32[16,8,128]{2,1,0:T(8,128)S(1)} all-to-all(f32[16,8,128]{2,1,0:T(8,128)S(1)} %broadcast_in_dim.2), channel_id=1, replica_groups=mesh['group'=2,'term'=16] {'term'}, dimensions={0} | all-to-all | bytes 131072 | tf_op jit(solution)/shard_map/all_to_all | solution.py:385
  129.5 0.9 norm.1
  (66 shorter events, 3.4 us)
Async XLA Ops:
  0.6 5.0 %copy-start.1 = (f32[2,128,128]{2,1,0:T(8,128)S(1)}, f32[2,128,128]{2,1,0:T(8,128)}, u32[]{:S(2)}) copy-start(f32[2,128,128]{2,1,0:T(8,128)} %vector_in.1) | copy-start | bytes 393220
  1.6 8.7 %collective-permute-start.9 = (f32[1,128,128]{2,1,0:T(8,128)S(1)}, f32[1,128,128]{2,1,0:T(8,128)S(1)}, u32[]{:S(2)}, u32[]{:S(2)}) collective-permute-start(f32[1,128,128]{2,1,0:T(8,128)S(1)} %get-tuple-element.90), channel_id=1, source_target_pairs={{0,8},{1,9},{2,10},{3,11},{4,12},{5,13},{6,14},{7,15},{8,0},{9,1},... | collective-permute-start | bytes 196616 | tf_op jit(solution)/shard_map/ppermute | solution.py:236
  5.7 19.6 %collective-permute-start = (f32[2,128,128]{2,1,0:T(8,128)S(1)}, f32[2,128,128]{2,1,0:T(8,128)S(1)}, u32[]{:S(2)}, u32[]{:S(2)}) collective-permute-start(f32[2,128,128]{2,1,0:T(8,128)S(1)} %copy-done.1), channel_id=1, source_target_pairs={{0,12},{1,13},{2,14},{3,15},{4,8},{5,9},{6,10},{7,11},{8,4},{9,5},... | collective-permute-start | bytes 393224 | tf_op jit(solution)/shard_map/ppermute | solution.py:236
  7.0 18.3 %collective-permute-start.2 = (f32[2,128,128]{2,1,0:T(8,128)S(1)}, f32[2,128,128]{2,1,0:T(8,128)S(1)}, u32[]{:S(2)}, u32[]{:S(2)}) collective-permute-start(f32[2,128,128]{2,1,0:T(8,128)S(1)} %copy-done.1), channel_id=1, source_target_pairs={{0,2},{1,3},{2,0},{3,1},{4,6},{5,7},{6,4},{7,5},{8,10},{9,11},{10,... | collective-permute-start | bytes 393224 | tf_op jit(solution)/shard_map/ppermute | solution.py:236
  8.5 9.3 %collective-permute-start.8 = (f32[1,128,128]{2,1,0:T(8,128)S(1)}, f32[1,128,128]{2,1,0:T(8,128)S(1)}, u32[]{:S(2)}, u32[]{:S(2)}) collective-permute-start(f32[1,128,128]{2,1,0:T(8,128)S(1)} %get-tuple-element.91), channel_id=1, source_target_pairs={{0,8},{1,9},{2,10},{3,11},{4,12},{5,13},{6,14},{7,15},{8,0},{9,1},... | collective-permute-start | bytes 196616 | tf_op jit(solution)/shard_map/ppermute | solution.py:236
  10.2 7.6 %collective-permute-start.13 = (f32[1,128,128]{2,1,0:T(8,128)S(1)}, f32[1,128,128]{2,1,0:T(8,128)S(1)}, u32[]{:S(2)}, u32[]{:S(2)}) collective-permute-start(f32[1,128,128]{2,1,0:T(8,128)S(1)} %collective-permute-done.9.refs_9_), channel_id=1, source_target_pairs={{0,2},{1,3},{2,0},{3,1},{4,6},{5,7},{6,4},{7,5},{8,10},{9,11},{10,... | collective-permute-start | bytes 196616 | tf_op jit(solution)/shard_map/ppermute | solution.py:236
  15.5 11.2 %collective-permute-start.4 = (f32[2,128,128]{2,1,0:T(8,128)S(1)}, f32[2,128,128]{2,1,0:T(8,128)S(1)}, u32[]{:S(2)}, u32[]{:S(2)}) collective-permute-start(f32[2,128,128]{2,1,0:T(8,128)S(1)} %copy-done.1), channel_id=1, source_target_pairs={{0,4},{1,5},{2,6},{3,7},{4,0},{5,1},{6,2},{7,3},{8,12},{9,13},{10,... | collective-permute-start | bytes 393224 | tf_op jit(solution)/shard_map/ppermute | solution.py:236
  17.9 7.8 %collective-permute-start.11 = (f32[1,128,128]{2,1,0:T(8,128)S(1)}, f32[1,128,128]{2,1,0:T(8,128)S(1)}, u32[]{:S(2)}, u32[]{:S(2)}) collective-permute-start(f32[1,128,128]{2,1,0:T(8,128)S(1)} %collective-permute-done.9.refs_9_), channel_id=1, source_target_pairs={{0,1},{1,0},{2,3},{3,2},{4,5},{5,4},{6,7},{7,6},{8,9},{9,8},{10,11... | collective-permute-start | bytes 196616 | tf_op jit(solution)/shard_map/ppermute | solution.py:236
  17.9 8.0 %collective-permute-start.12 = (f32[1,128,128]{2,1,0:T(8,128)S(1)}, f32[1,128,128]{2,1,0:T(8,128)S(1)}, u32[]{:S(2)}, u32[]{:S(2)}) collective-permute-start(f32[1,128,128]{2,1,0:T(8,128)S(1)} %collective-permute-done.8.refs_8_), channel_id=1, source_target_pairs={{0,2},{1,3},{2,0},{3,1},{4,6},{5,7},{6,4},{7,5},{8,10},{9,11},{10,... | collective-permute-start | bytes 196616 | tf_op jit(solution)/shard_map/ppermute | solution.py:236
  19.8 0.7 copy-start.2
  25.2 1.3 %collective-permute-start.10 = (f32[1,128,128]{2,1,0:T(8,128)S(1)}, f32[1,128,128]{2,1,0:T(8,128)S(1)}, u32[]{:S(2)}, u32[]{:S(2)}) collective-permute-start(f32[1,128,128]{2,1,0:T(8,128)S(1)} %collective-permute-done.8.refs_8_), channel_id=1, source_target_pairs={{0,1},{1,0},{2,3},{3,2},{4,5},{5,4},{6,7},{7,6},{8,9},{9,8},{10,11... | collective-permute-start | bytes 196616 | tf_op jit(solution)/shard_map/ppermute | solution.py:236
  25.3 5.9 %collective-permute-start.6 = (f32[2,128,128]{2,1,0:T(8,128)S(1)}, f32[2,128,128]{2,1,0:T(8,128)S(1)}, u32[]{:S(2)}, u32[]{:S(2)}) collective-permute-start(f32[2,128,128]{2,1,0:T(8,128)S(1)} %collective-permute-done.2.refs_2_), channel_id=1, source_target_pairs={{0,4},{1,5},{2,6},{3,7},{4,0},{5,1},{6,2},{7,3},{8,12},{9,13},{10,... | collective-permute-start | bytes 393224 | tf_op jit(solution)/shard_map/ppermute | solution.py:236
  25.6 5.6 %collective-permute-start.3 = (f32[2,128,128]{2,1,0:T(8,128)S(1)}, f32[2,128,128]{2,1,0:T(8,128)S(1)}, u32[]{:S(2)}, u32[]{:S(2)}) collective-permute-start(f32[2,128,128]{2,1,0:T(8,128)S(1)} %collective-permute-done.2.refs_2_), channel_id=1, source_target_pairs={{0,1},{1,0},{2,3},{3,2},{4,5},{5,4},{6,7},{7,6},{8,9},{9,8},{10,11... | collective-permute-start | bytes 393224 | tf_op jit(solution)/shard_map/ppermute | solution.py:236
  25.9 5.9 %collective-permute-start.17 = (f32[2,128,128]{2,1,0:T(8,128)S(1)}, f32[2,128,128]{2,1,0:T(8,128)S(1)}, u32[]{:S(2)}, u32[]{:S(2)}) collective-permute-start(f32[2,128,128]{2,1,0:T(8,128)S(1)} %collective-permute-done.refs_16_), channel_id=1, source_target_pairs={{0,2},{1,3},{2,0},{3,1},{4,6},{5,7},{6,4},{7,5},{8,10},{9,11},{10,... | collective-permute-start | bytes 393224 | tf_op jit(solution)/shard_map/ppermute | solution.py:236
  26.5 1.3 collective-permute-start.15
  26.7 1.3 collective-permute-start.14
  27.8 4.8 %collective-permute-start.16 = (f32[2,128,128]{2,1,0:T(8,128)S(1)}, f32[2,128,128]{2,1,0:T(8,128)S(1)}, u32[]{:S(2)}, u32[]{:S(2)}) collective-permute-start(f32[2,128,128]{2,1,0:T(8,128)S(1)} %collective-permute-done.refs_16_), channel_id=1, source_target_pairs={{0,1},{1,0},{2,3},{3,2},{4,5},{5,4},{6,7},{7,6},{8,9},{9,8},{10,11... | collective-permute-start | bytes 393224 | tf_op jit(solution)/shard_map/ppermute | solution.py:236
  28.0 4.6 %collective-permute-start.1 = (f32[2,128,128]{2,1,0:T(8,128)S(1)}, f32[2,128,128]{2,1,0:T(8,128)S(1)}, u32[]{:S(2)}, u32[]{:S(2)}) collective-permute-start(f32[2,128,128]{2,1,0:T(8,128)S(1)} %get-tuple-element.58.refs_0_.vector_ref), channel_id=1, source_target_pairs={{0,1},{1,0},{2,3},{3,2},{4,5},{5,4},{6,7},{7,6},{8,9},{9,8},{10,11... | collective-permute-start | bytes 393224 | tf_op jit(solution)/shard_map/ppermute | solution.py:236
  31.2 1.3 %collective-permute-start.5 = (f32[2,128,128]{2,1,0:T(8,128)S(1)}, f32[2,128,128]{2,1,0:T(8,128)S(1)}, u32[]{:S(2)}, u32[]{:S(2)}) collective-permute-start(f32[2,128,128]{2,1,0:T(8,128)S(1)} %collective-permute-done.4.refs_4_), channel_id=1, source_target_pairs={{0,1},{1,0},{2,3},{3,2},{4,5},{5,4},{6,7},{7,6},{8,9},{9,8},{10,11... | collective-permute-start | bytes 393224 | tf_op jit(solution)/shard_map/ppermute | solution.py:236
  31.2 1.5 %collective-permute-start.7 = (f32[2,128,128]{2,1,0:T(8,128)S(1)}, f32[2,128,128]{2,1,0:T(8,128)S(1)}, u32[]{:S(2)}, u32[]{:S(2)}) collective-permute-start(f32[2,128,128]{2,1,0:T(8,128)S(1)} %collective-permute-done.6.refs_6_), channel_id=1, source_target_pairs={{0,1},{1,0},{2,3},{3,2},{4,5},{5,4},{6,7},{7,6},{8,9},{9,8},{10,11... | collective-permute-start | bytes 393224 | tf_op jit(solution)/shard_map/ppermute | solution.py:236
  31.7 1.3 %collective-permute-start.18 = (f32[2,128,128]{2,1,0:T(8,128)S(1)}, f32[2,128,128]{2,1,0:T(8,128)S(1)}, u32[]{:S(2)}, u32[]{:S(2)}) collective-permute-start(f32[2,128,128]{2,1,0:T(8,128)S(1)} %collective-permute-done.17.refs_18_), channel_id=1, source_target_pairs={{0,1},{1,0},{2,3},{3,2},{4,5},{5,4},{6,7},{7,6},{8,9},{9,8},{10,11... | collective-permute-start | bytes 393224 | tf_op jit(solution)/shard_map/ppermute | solution.py:236
  39.8 8.5 %collective-permute-start.19 = (f32[648,128]{1,0:T(8,128)S(1)}, f32[648,128]{1,0:T(8,128)S(1)}, u32[]{:S(2)}, u32[]{:S(2)}) collective-permute-start(f32[648,128]{1,0:T(8,128)S(1)} %get-tuple-element.61.far_in), channel_id=1, source_target_pairs={{0,1},{1,0},{2,3},{3,2},{4,5},{5,4},{6,7},{7,6},{8,9},{9,8},{10,11... | collective-permute-start | bytes 995336 | tf_op jit(solution)/shard_map/ppermute | solution.py:236
  39.9 7.5 %collective-permute-start.20 = (f32[264,128]{1,0:T(8,128)S(1)}, f32[264,128]{1,0:T(8,128)S(1)}, u32[]{:S(2)}, u32[]{:S(2)}) collective-permute-start(f32[264,128]{1,0:T(8,128)S(1)} %get-tuple-element.62), channel_id=1, source_target_pairs={{0,2},{1,3},{2,0},{3,1},{4,6},{5,7},{6,4},{7,5},{8,10},{9,11},{10,... | collective-permute-start | bytes 405512 | tf_op jit(solution)/shard_map/ppermute | solution.py:236
  40.1 8.2 %collective-permute-start.21 = (f32[264,128]{1,0:T(8,128)S(1)}, f32[264,128]{1,0:T(8,128)S(1)}, u32[]{:S(2)}, u32[]{:S(2)}) collective-permute-start(f32[264,128]{1,0:T(8,128)S(1)} %get-tuple-element.63), channel_id=1, source_target_pairs={{0,3},{1,2},{2,1},{3,0},{4,7},{5,6},{6,5},{7,4},{8,11},{9,10},{10,... | collective-permute-start | bytes 405512 | tf_op jit(solution)/shard_map/ppermute | solution.py:236
  41.7 4.3 %collective-permute-start.22 = (f32[128,128]{1,0:T(8,128)S(1)}, f32[128,128]{1,0:T(8,128)S(1)}, u32[]{:S(2)}, u32[]{:S(2)}) collective-permute-start(f32[128,128]{1,0:T(8,128)S(1)} %get-tuple-element.64), channel_id=1, source_target_pairs={{0,4},{1,5},{2,6},{3,7},{4,0},{5,1},{6,2},{7,3},{8,12},{9,13},{10,... | collective-permute-start | bytes 196616 | tf_op jit(solution)/shard_map/ppermute | solution.py:236
  43.3 4.1 %collective-permute-start.23 = (f32[128,128]{1,0:T(8,128)S(1)}, f32[128,128]{1,0:T(8,128)S(1)}, u32[]{:S(2)}, u32[]{:S(2)}) collective-permute-start(f32[128,128]{1,0:T(8,128)S(1)} %get-tuple-element.65), channel_id=1, source_target_pairs={{0,5},{1,4},{2,7},{3,6},{4,1},{5,0},{6,3},{7,2},{8,13},{9,12},{10,... | collective-permute-start | bytes 196616 | tf_op jit(solution)/shard_map/ppermute | solution.py:236
  48.3 14.6 %copy-start = (f32[2,128,128]{2,1,0:T(8,128)S(1)}, f32[2,128,128]{2,1,0:T(8,128)}, u32[]{:S(2)}) copy-start(f32[2,128,128]{2,1,0:T(8,128)} %precond_ref.3) | copy-start | bytes 393220
  49.0 13.2 %collective-permute-start.25 = (f32[264,128]{1,0:T(8,128)S(1)}, f32[264,128]{1,0:T(8,128)S(1)}, u32[]{:S(2)}, u32[]{:S(2)}) collective-permute-start(f32[264,128]{1,0:T(8,128)S(1)} %get-tuple-element.70), channel_id=1, source_target_pairs={{0,8},{1,9},{2,10},{3,11},{4,12},{5,13},{6,14},{7,15},{8,0},{9,1},... | collective-permute-start | bytes 405512 | tf_op jit(solution)/shard_map/ppermute | solution.py:236
  51.0 11.2 %collective-permute-start.26 = (f32[264,128]{1,0:T(8,128)S(1)}, f32[264,128]{1,0:T(8,128)S(1)}, u32[]{:S(2)}, u32[]{:S(2)}) collective-permute-start(f32[264,128]{1,0:T(8,128)S(1)} %get-tuple-element.71), channel_id=1, source_target_pairs={{0,12},{1,13},{2,14},{3,15},{4,8},{5,9},{6,10},{7,11},{8,4},{9,5},... | collective-permute-start | bytes 405512 | tf_op jit(solution)/shard_map/ppermute | solution.py:236
  53.0 9.9 %collective-permute-start.27 = (f32[264,128]{1,0:T(8,128)S(1)}, f32[264,128]{1,0:T(8,128)S(1)}, u32[]{:S(2)}, u32[]{:S(2)}) collective-permute-start(f32[264,128]{1,0:T(8,128)S(1)} %get-tuple-element.69.refs_0_), channel_id=1, source_target_pairs={{0,4},{1,5},{2,6},{3,7},{4,0},{5,1},{6,2},{7,3},{8,12},{9,13},{10,... | collective-permute-start | bytes 405512 | tf_op jit(solution)/shard_map/ppermute | solution.py:236
  53.0 5.1 %collective-permute-start.24 = (f32[2,128,128]{2,1,0:T(8,128)S(1)}, f32[2,128,128]{2,1,0:T(8,128)S(1)}, u32[]{:S(2)}, u32[]{:S(2)}) collective-permute-start(f32[2,128,128]{2,1,0:T(8,128)S(1)} %get-tuple-element.67), channel_id=1, source_target_pairs={{0,2},{1,3},{2,0},{3,1},{4,6},{5,7},{6,4},{7,5},{8,10},{9,11},{10,... | collective-permute-start | bytes 393224 | tf_op jit(solution)/shard_map/ppermute | solution.py:236
  63.1 9.2 %collective-permute-start.35 = (f32[1,128,128]{2,1,0:T(8,128)S(1)}, f32[1,128,128]{2,1,0:T(8,128)S(1)}, u32[]{:S(2)}, u32[]{:S(2)}) collective-permute-start(f32[1,128,128]{2,1,0:T(8,128)S(1)} %get-tuple-element.73), channel_id=1, source_target_pairs={{0,8},{1,9},{2,10},{3,11},{4,12},{5,13},{6,14},{7,15},{8,0},{9,1},... | collective-permute-start | bytes 196616 | tf_op jit(solution)/shard_map/ppermute | solution.py:236
  66.0 12.7 %collective-permute-start.43 = (f32[2,128,128]{2,1,0:T(8,128)S(1)}, f32[2,128,128]{2,1,0:T(8,128)S(1)}, u32[]{:S(2)}, u32[]{:S(2)}) collective-permute-start(f32[2,128,128]{2,1,0:T(8,128)S(1)} %get-tuple-element.72.refs_0_.vector_ref), channel_id=1, source_target_pairs={{0,12},{1,13},{2,14},{3,15},{4,8},{5,9},{6,10},{7,11},{8,4},{9,5},... | collective-permute-start | bytes 393224 | tf_op jit(solution)/shard_map/ppermute | solution.py:236
  67.7 11.0 %collective-permute-start.31 = (f32[2,128,128]{2,1,0:T(8,128)S(1)}, f32[2,128,128]{2,1,0:T(8,128)S(1)}, u32[]{:S(2)}, u32[]{:S(2)}) collective-permute-start(f32[2,128,128]{2,1,0:T(8,128)S(1)} %get-tuple-element.72.refs_0_.vector_ref), channel_id=1, source_target_pairs={{0,4},{1,5},{2,6},{3,7},{4,0},{5,1},{6,2},{7,3},{8,12},{9,13},{10,... | collective-permute-start | bytes 393224 | tf_op jit(solution)/shard_map/ppermute | solution.py:236
  67.7 12.1 %collective-permute-start.29 = (f32[2,128,128]{2,1,0:T(8,128)S(1)}, f32[2,128,128]{2,1,0:T(8,128)S(1)}, u32[]{:S(2)}, u32[]{:S(2)}) collective-permute-start(f32[2,128,128]{2,1,0:T(8,128)S(1)} %get-tuple-element.72.refs_0_.vector_ref), channel_id=1, source_target_pairs={{0,2},{1,3},{2,0},{3,1},{4,6},{5,7},{6,4},{7,5},{8,10},{9,11},{10,... | collective-permute-start | bytes 393224 | tf_op jit(solution)/shard_map/ppermute | solution.py:236
  68.2 12.6 %collective-permute-start.28 = (f32[2,128,128]{2,1,0:T(8,128)S(1)}, f32[2,128,128]{2,1,0:T(8,128)S(1)}, u32[]{:S(2)}, u32[]{:S(2)}) collective-permute-start(f32[2,128,128]{2,1,0:T(8,128)S(1)} %get-tuple-element.72.refs_0_.vector_ref), channel_id=1, source_target_pairs={{0,1},{1,0},{2,3},{3,2},{4,5},{5,4},{6,7},{7,6},{8,9},{9,8},{10,11... | collective-permute-start | bytes 393224 | tf_op jit(solution)/shard_map/ppermute | solution.py:236
  72.3 5.4 %collective-permute-start.36 = (f32[1,128,128]{2,1,0:T(8,128)S(1)}, f32[1,128,128]{2,1,0:T(8,128)S(1)}, u32[]{:S(2)}, u32[]{:S(2)}) collective-permute-start(f32[1,128,128]{2,1,0:T(8,128)S(1)} %get-tuple-element.74), channel_id=1, source_target_pairs={{0,8},{1,9},{2,10},{3,11},{4,12},{5,13},{6,14},{7,15},{8,0},{9,1},... | collective-permute-start | bytes 196616 | tf_op jit(solution)/shard_map/ppermute | solution.py:236
  77.7 4.6 %collective-permute-start.39 = (f32[1,128,128]{2,1,0:T(8,128)S(1)}, f32[1,128,128]{2,1,0:T(8,128)S(1)}, u32[]{:S(2)}, u32[]{:S(2)}) collective-permute-start(f32[1,128,128]{2,1,0:T(8,128)S(1)} %collective-permute-done.35.refs_8_), channel_id=1, source_target_pairs={{0,2},{1,3},{2,0},{3,1},{4,6},{5,7},{6,4},{7,5},{8,10},{9,11},{10,... | collective-permute-start | bytes 196616 | tf_op jit(solution)/shard_map/ppermute | solution.py:236
  78.7 3.6 %collective-permute-start.37 = (f32[1,128,128]{2,1,0:T(8,128)S(1)}, f32[1,128,128]{2,1,0:T(8,128)S(1)}, u32[]{:S(2)}, u32[]{:S(2)}) collective-permute-start(f32[1,128,128]{2,1,0:T(8,128)S(1)} %collective-permute-done.35.refs_8_), channel_id=1, source_target_pairs={{0,1},{1,0},{2,3},{3,2},{4,5},{5,4},{6,7},{7,6},{8,9},{9,8},{10,11... | collective-permute-start | bytes 196616 | tf_op jit(solution)/shard_map/ppermute | solution.py:236
  78.7 5.0 %collective-permute-start.40 = (f32[1,128,128]{2,1,0:T(8,128)S(1)}, f32[1,128,128]{2,1,0:T(8,128)S(1)}, u32[]{:S(2)}, u32[]{:S(2)}) collective-permute-start(f32[1,128,128]{2,1,0:T(8,128)S(1)} %collective-permute-done.36.refs_9_), channel_id=1, source_target_pairs={{0,2},{1,3},{2,0},{3,1},{4,6},{5,7},{6,4},{7,5},{8,10},{9,11},{10,... | collective-permute-start | bytes 196616 | tf_op jit(solution)/shard_map/ppermute | solution.py:236
  79.8 6.4 %collective-permute-start.45 = (f32[2,128,128]{2,1,0:T(8,128)S(1)}, f32[2,128,128]{2,1,0:T(8,128)S(1)}, u32[]{:S(2)}, u32[]{:S(2)}) collective-permute-start(f32[2,128,128]{2,1,0:T(8,128)S(1)} %collective-permute-done.43.refs_16_), channel_id=1, source_target_pairs={{0,2},{1,3},{2,0},{3,1},{4,6},{5,7},{6,4},{7,5},{8,10},{9,11},{10,... | collective-permute-start | bytes 393224 | tf_op jit(solution)/shard_map/ppermute | solution.py:236
  80.8 5.4 %collective-permute-start.33 = (f32[2,128,128]{2,1,0:T(8,128)S(1)}, f32[2,128,128]{2,1,0:T(8,128)S(1)}, u32[]{:S(2)}, u32[]{:S(2)}) collective-permute-start(f32[2,128,128]{2,1,0:T(8,128)S(1)} %collective-permute-done.29.refs_2_), channel_id=1, source_target_pairs={{0,4},{1,5},{2,6},{3,7},{4,0},{5,1},{6,2},{7,3},{8,12},{9,13},{10,... | collective-permute-start | bytes 393224 | tf_op jit(solution)/shard_map/ppermute | solution.py:236
  82.3 1.4 %collective-permute-start.38 = (f32[1,128,128]{2,1,0:T(8,128)S(1)}, f32[1,128,128]{2,1,0:T(8,128)S(1)}, u32[]{:S(2)}, u32[]{:S(2)}) collective-permute-start(f32[1,128,128]{2,1,0:T(8,128)S(1)} %collective-permute-done.36.refs_9_), channel_id=1, source_target_pairs={{0,1},{1,0},{2,3},{3,2},{4,5},{5,4},{6,7},{7,6},{8,9},{9,8},{10,11... | collective-permute-start | bytes 196616 | tf_op jit(solution)/shard_map/ppermute | solution.py:236
  82.3 1.9 %collective-permute-start.41 = (f32[1,128,128]{2,1,0:T(8,128)S(1)}, f32[1,128,128]{2,1,0:T(8,128)S(1)}, u32[]{:S(2)}, u32[]{:S(2)}) collective-permute-start(f32[1,128,128]{2,1,0:T(8,128)S(1)} %collective-permute-done.39.refs_12_), channel_id=1, source_target_pairs={{0,1},{1,0},{2,3},{3,2},{4,5},{5,4},{6,7},{7,6},{8,9},{9,8},{10,11... | collective-permute-start | bytes 196616 | tf_op jit(solution)/shard_map/ppermute | solution.py:236
  83.7 1.3 collective-permute-start.42
  83.7 3.0 %collective-permute-start.44 = (f32[2,128,128]{2,1,0:T(8,128)S(1)}, f32[2,128,128]{2,1,0:T(8,128)S(1)}, u32[]{:S(2)}, u32[]{:S(2)}) collective-permute-start(f32[2,128,128]{2,1,0:T(8,128)S(1)} %collective-permute-done.43.refs_16_), channel_id=1, source_target_pairs={{0,1},{1,0},{2,3},{3,2},{4,5},{5,4},{6,7},{7,6},{8,9},{9,8},{10,11... | collective-permute-start | bytes 393224 | tf_op jit(solution)/shard_map/ppermute | solution.py:236
  84.2 2.5 %collective-permute-start.30 = (f32[2,128,128]{2,1,0:T(8,128)S(1)}, f32[2,128,128]{2,1,0:T(8,128)S(1)}, u32[]{:S(2)}, u32[]{:S(2)}) collective-permute-start(f32[2,128,128]{2,1,0:T(8,128)S(1)} %collective-permute-done.29.refs_2_), channel_id=1, source_target_pairs={{0,1},{1,0},{2,3},{3,2},{4,5},{5,4},{6,7},{7,6},{8,9},{9,8},{10,11... | collective-permute-start | bytes 393224 | tf_op jit(solution)/shard_map/ppermute | solution.py:236
  84.9 1.8 %collective-permute-start.32 = (f32[2,128,128]{2,1,0:T(8,128)S(1)}, f32[2,128,128]{2,1,0:T(8,128)S(1)}, u32[]{:S(2)}, u32[]{:S(2)}) collective-permute-start(f32[2,128,128]{2,1,0:T(8,128)S(1)} %collective-permute-done.31.refs_4_), channel_id=1, source_target_pairs={{0,1},{1,0},{2,3},{3,2},{4,5},{5,4},{6,7},{7,6},{8,9},{9,8},{10,11... | collective-permute-start | bytes 393224 | tf_op jit(solution)/shard_map/ppermute | solution.py:236
  86.2 1.3 %collective-permute-start.46 = (f32[2,128,128]{2,1,0:T(8,128)S(1)}, f32[2,128,128]{2,1,0:T(8,128)S(1)}, u32[]{:S(2)}, u32[]{:S(2)}) collective-permute-start(f32[2,128,128]{2,1,0:T(8,128)S(1)} %collective-permute-done.45.refs_18_), channel_id=1, source_target_pairs={{0,1},{1,0},{2,3},{3,2},{4,5},{5,4},{6,7},{7,6},{8,9},{9,8},{10,11... | collective-permute-start | bytes 393224 | tf_op jit(solution)/shard_map/ppermute | solution.py:236
  86.2 1.5 %collective-permute-start.34 = (f32[2,128,128]{2,1,0:T(8,128)S(1)}, f32[2,128,128]{2,1,0:T(8,128)S(1)}, u32[]{:S(2)}, u32[]{:S(2)}) collective-permute-start(f32[2,128,128]{2,1,0:T(8,128)S(1)} %collective-permute-done.33.refs_6_), channel_id=1, source_target_pairs={{0,1},{1,0},{2,3},{3,2},{4,5},{5,4},{6,7},{7,6},{8,9},{9,8},{10,11... | collective-permute-start | bytes 393224 | tf_op jit(solution)/shard_map/ppermute | solution.py:236
  94.6 8.4 %collective-permute-start.47 = (f32[648,128]{1,0:T(8,128)S(1)}, f32[648,128]{1,0:T(8,128)S(1)}, u32[]{:S(2)}, u32[]{:S(2)}) collective-permute-start(f32[648,128]{1,0:T(8,128)S(1)} %get-tuple-element.76.far_in), channel_id=1, source_target_pairs={{0,1},{1,0},{2,3},{3,2},{4,5},{5,4},{6,7},{7,6},{8,9},{9,8},{10,11... | collective-permute-start | bytes 995336 | tf_op jit(solution)/shard_map/ppermute | solution.py:236
  94.9 7.1 %collective-permute-start.48 = (f32[264,128]{1,0:T(8,128)S(1)}, f32[264,128]{1,0:T(8,128)S(1)}, u32[]{:S(2)}, u32[]{:S(2)}) collective-permute-start(f32[264,128]{1,0:T(8,128)S(1)} %get-tuple-element.77), channel_id=1, source_target_pairs={{0,2},{1,3},{2,0},{3,1},{4,6},{5,7},{6,4},{7,5},{8,10},{9,11},{10,... | collective-permute-start | bytes 405512 | tf_op jit(solution)/shard_map/ppermute | solution.py:236
  95.8 7.1 %collective-permute-start.49 = (f32[264,128]{1,0:T(8,128)S(1)}, f32[264,128]{1,0:T(8,128)S(1)}, u32[]{:S(2)}, u32[]{:S(2)}) collective-permute-start(f32[264,128]{1,0:T(8,128)S(1)} %get-tuple-element.78), channel_id=1, source_target_pairs={{0,3},{1,2},{2,1},{3,0},{4,7},{5,6},{6,5},{7,4},{8,11},{9,10},{10,... | collective-permute-start | bytes 405512 | tf_op jit(solution)/shard_map/ppermute | solution.py:236
  96.5 4.9 %collective-permute-start.50 = (f32[128,128]{1,0:T(8,128)S(1)}, f32[128,128]{1,0:T(8,128)S(1)}, u32[]{:S(2)}, u32[]{:S(2)}) collective-permute-start(f32[128,128]{1,0:T(8,128)S(1)} %get-tuple-element.79), channel_id=1, source_target_pairs={{0,4},{1,5},{2,6},{3,7},{4,0},{5,1},{6,2},{7,3},{8,12},{9,13},{10,... | collective-permute-start | bytes 196616 | tf_op jit(solution)/shard_map/ppermute | solution.py:236
  96.6 5.4 %collective-permute-start.51 = (f32[128,128]{1,0:T(8,128)S(1)}, f32[128,128]{1,0:T(8,128)S(1)}, u32[]{:S(2)}, u32[]{:S(2)}) collective-permute-start(f32[128,128]{1,0:T(8,128)S(1)} %get-tuple-element.80), channel_id=1, source_target_pairs={{0,5},{1,4},{2,7},{3,6},{4,1},{5,0},{6,3},{7,2},{8,13},{9,12},{10,... | collective-permute-start | bytes 196616 | tf_op jit(solution)/shard_map/ppermute | solution.py:236
  103.7 12.2 %collective-permute-start.53 = (f32[264,128]{1,0:T(8,128)S(1)}, f32[264,128]{1,0:T(8,128)S(1)}, u32[]{:S(2)}, u32[]{:S(2)}) collective-permute-start(f32[264,128]{1,0:T(8,128)S(1)} %get-tuple-element.85), channel_id=1, source_target_pairs={{0,8},{1,9},{2,10},{3,11},{4,12},{5,13},{6,14},{7,15},{8,0},{9,1},... | collective-permute-start | bytes 405512 | tf_op jit(solution)/shard_map/ppermute | solution.py:236
  104.2 11.7 %collective-permute-start.54 = (f32[264,128]{1,0:T(8,128)S(1)}, f32[264,128]{1,0:T(8,128)S(1)}, u32[]{:S(2)}, u32[]{:S(2)}) collective-permute-start(f32[264,128]{1,0:T(8,128)S(1)} %get-tuple-element.86), channel_id=1, source_target_pairs={{0,12},{1,13},{2,14},{3,15},{4,8},{5,9},{6,10},{7,11},{8,4},{9,5},... | collective-permute-start | bytes 405512 | tf_op jit(solution)/shard_map/ppermute | solution.py:236
  106.0 11.2 %collective-permute-start.55 = (f32[264,128]{1,0:T(8,128)S(1)}, f32[264,128]{1,0:T(8,128)S(1)}, u32[]{:S(2)}, u32[]{:S(2)}) collective-permute-start(f32[264,128]{1,0:T(8,128)S(1)} %get-tuple-element.84.refs_0_), channel_id=1, source_target_pairs={{0,4},{1,5},{2,6},{3,7},{4,0},{5,1},{6,2},{7,3},{8,12},{9,13},{10,... | collective-permute-start | bytes 405512 | tf_op jit(solution)/shard_map/ppermute | solution.py:236
  107.2 5.0 %collective-permute-start.52 = (f32[2,128,128]{2,1,0:T(8,128)S(1)}, f32[2,128,128]{2,1,0:T(8,128)S(1)}, u32[]{:S(2)}, u32[]{:S(2)}) collective-permute-start(f32[2,128,128]{2,1,0:T(8,128)S(1)} %get-tuple-element.82), channel_id=1, source_target_pairs={{0,2},{1,3},{2,0},{3,1},{4,6},{5,7},{6,4},{7,5},{8,10},{9,11},{10,... | collective-permute-start | bytes 393224 | tf_op jit(solution)/shard_map/ppermute | solution.py:236

commit v9 on v4

--- a/solution.py
+++ b/solution.py
@@ -27,8 +27,28 @@
     return jnp.sum(x.reshape(-1, 8, x.shape[-1]), axis=0)
 
 
+class Part:
+    def __init__(self, ref, start):
+        self.ref, self.start = ref, start
+
+    def __getitem__(self, i):
+        return self.ref[self.start + i]
+
+    def __setitem__(self, i, value):
+        self.ref[self.start + i] = value
+
+
+def lengths(n, terms, npairs):
+    return n, n, SENDERS * n // 2, terms * n, terms * n, npairs, npairs, npairs, 1
+
+
+def parts(ref, n, terms, npairs):
+    sizes = lengths(n, terms, npairs)
+    return [Part(ref, sum(sizes[:i])) for i in range(len(sizes))]
+
+
 def prep_kernel(n, spare, me_ref, fetch_in, store_in, pairs_in, live_in, vector_in, left_in, right_in, l4_ref, rr_ref,
-                pick_ref, mine_ref, place_ref, first_ref, second_ref, dst_ref, one_ref, two_ref, count_ref, vector_ref,
+                table_ref, vector_ref,
                 seen_ref, fetch_ref, store_ref, pairs_ref, live_ref, left_ref, right_ref, sems):
     copies = [pltpu.make_async_copy(source, target, sems.at[i]) for i, (source, target) in enumerate((
         (fetch_in, fetch_ref), (store_in, store_ref), (pairs_in, pairs_ref), (live_in, live_ref),
@@ -40,6 +60,8 @@
     width = left_ref.shape[1]
     zero = terms * n
     npairs = pairs_ref.shape[0] // 3
+    pick_ref, mine_ref, place_ref, first_ref, second_ref, dst_ref, one_ref, two_ref, count_ref = parts(
+        table_ref, n, terms, npairs)
 
     def clear(cell, carry):
         first_ref[cell] = zero
@@ -107,20 +129,16 @@
 def prep(n, me, fetch, store, pairs, live, vector, left_ops, right_ops):
     terms, width = left_ops.shape[:2]
     npairs = pairs.shape[0] // 3
-    table = jax.ShapeDtypeStruct((terms * n,), jnp.int32)
-    listed = jax.ShapeDtypeStruct((npairs,), jnp.int32)
-    relative = jax.ShapeDtypeStruct((n,), jnp.int32)
     return pl.pallas_call(
         functools.partial(prep_kernel, n, terms * n + 1),
         out_shape=(
             jax.ShapeDtypeStruct((terms, width, 4 * width), jnp.bfloat16),
             jax.ShapeDtypeStruct((2 * terms * width, 2 * width), jnp.bfloat16),
-            relative, relative, jax.ShapeDtypeStruct((SENDERS * n // 2,), jnp.int32), table, table, listed, listed, listed,
-            jax.ShapeDtypeStruct((1,), jnp.int32),
+            jax.ShapeDtypeStruct((sum(lengths(n, terms, npairs)),), jnp.int32),
             jax.ShapeDtypeStruct(vector.shape, jnp.float32),
         ),
         in_specs=[SMEM] + [pl.BlockSpec(memory_space=pltpu.HBM)] * 7,
-        out_specs=[VMEM] * 2 + [SMEM] * 9 + [VMEM],
+        out_specs=[VMEM] * 2 + [SMEM, VMEM],
         scratch_shapes=[
             pltpu.SMEM((terms * n,), jnp.int32),
             pltpu.SMEM(fetch.shape, jnp.int32),
@@ -136,10 +154,10 @@
     )(me, at_home(fetch), at_home(store), at_home(pairs), live, at_home(vector), at_home(left_ops), at_home(right_ops))
 
 
-def apply_kernel(n, over_rows, rows, start, pick_ref, mine_ref, first_ref, second_ref, dst_ref, one_ref, two_ref, count_ref,
-                 l4_ref, rr_ref, *refs):
+def apply_kernel(n, npairs, over_rows, rows, start, table_ref, l4_ref, rr_ref, *refs):
     pieces, (near_ref, far_ref, row_ref, row_far_ref, column_ref, column_far_ref, square_ref, block, total) = refs[:n], refs[n:]
     terms, width = l4_ref.shape[:2]
+    pick_ref, mine_ref, _, first_ref, second_ref, dst_ref, one_ref, two_ref, count_ref = parts(table_ref, n, terms, npairs)
     square = jnp.zeros((8, width), jnp.float32)
     product = jnp.zeros((8, width), jnp.float32)
     block[terms * n] = jnp.zeros((rows, width), jnp.float32)
@@ -191,14 +209,15 @@
 
 def apply(n, over_rows, rows, start, tables, pieces):
     terms, width = tables[0].shape[:2]
-    spare = tables[7].shape[0] // 3
+    npairs = (tables[2].shape[0] - sum(lengths(n, terms, 0))) // 3
+    spare = npairs // 3
     late = n // 2 - 1 - len(over_rows)
     shape = lambda *dims: jax.ShapeDtypeStruct(dims, jnp.float32)
     return pl.pallas_call(
-        functools.partial(apply_kernel, n, over_rows, rows, start),
+        functools.partial(apply_kernel, n, npairs, over_rows, rows, start),
         out_shape=(shape(late * rows, width), shape(late * rows + 8, width)) + (shape(len(over_rows) * rows + 8, width),) * 2
         + (shape(rows, width),) * 2 + (shape(8, width),),
-        in_specs=[SMEM] * 8 + [VMEM] * (2 + n),
+        in_specs=[SMEM] + [VMEM] * (2 + n),
         out_specs=[VMEM] * 7,
         scratch_shapes=[
             pltpu.VMEM((terms * n + 1 + spare, rows, width), jnp.float32),
@@ -206,7 +225,7 @@
         ],
         compiler_params=params(32 if n <= 16 else 56),
         name="apply",
-    )(*tables[2:4], *tables[5:], *tables[:2], *pieces)
+    )(tables[2], *tables[:2], *pieces)
 
 
 def joined(parts, count):
@@ -235,10 +254,11 @@
     )(*scalars, *arrays)
 
 
-def fold_kernel(late, over_rows, place_ref, near_ref, far_in, far_ref, row_ref, row_far_ref, column_ref, column_far_ref,
+def fold_kernel(n, late, over_rows, table_ref, near_ref, far_in, far_ref, row_ref, row_far_ref, column_ref, column_far_ref,
                 own_ref, step_ref, *send_refs):
     width = near_ref.shape[1]
-    chips = place_ref.shape[0] // SENDERS
+    chips = n // 2
+    place_ref = Part(table_ref, 2 * n)
     end = len(late) * width
     over = len(over_rows) * width
     tile = far_in[end:] + far_ref[end:] + row_ref[over:] + row_far_ref[over:]
@@ -319,11 +339,11 @@
     near, far, row, row_far, column, column_far = (joined([x[i] for x in runs], k) for i, k in enumerate(counts))
     square = functools.reduce(jnp.add, [x[6] for x in runs])
     own, step, *sends = local(
-        functools.partial(fold_kernel, late, over_rows), "fold",
-        (shape(2, width, width),) * 2 + (shape(2 * width + 8, width),) * (chips // 2 - 1), tables[4:5],
+        functools.partial(fold_kernel, n, late, over_rows), "fold",
+        (shape(2, width, width),) * 2 + (shape(2 * width + 8, width),) * (chips // 2 - 1), tables[2:3],
         (near, far, swapped(far, CORE), swapped(row, ROW), swapped(row_far, ROW + CORE), swapped(column, COLUMN),
          swapped(column_far, COLUMN + CORE)))
-    came = [swapped(x, 2 * ROW * (i + 1)) for i, x in reversed(list(enumerate(sends)))]
+    came = [swapped(sends[i], 2 * ROW * (i + 1)) for i in (*range(1, len(sends)), 0)]
     return square, (own, swapped(step, ROW)), [sends[0], *came]
 
 
@@ -334,7 +354,7 @@
     pieces[ROW] = swapped(x, ROW)
     pieces[COLUMN] = swapped(x, COLUMN)
     if held is not None:
-        pieces[n - 4], pieces[0] = lax.optimization_barrier((pieces[n - 4], held))
+        pieces[COLUMN], pieces[0] = lax.optimization_barrier((pieces[COLUMN], held))
     for k in reversed(range(8, n, 4)):
         pieces[k + ROW] = swapped(pieces[k], ROW)
     pieces[COLUMN + ROW] = swapped(pieces[ROW], COLUMN)

time: 121 us -> 121 us (level)
  Pallas kernels: 21 us -> 18 us
  starting transfers between devices: 35.7 us -> 38.6 us
    ppermute x48, starting transfers between devices: 35.7 us -> 38.6 us  [swapped(): return lax.ppermute(x, 'term', [(i, i ^ k) for i in range(n)])]
    pallas_call x1, Pallas kernels: 4.19 us -> 2.51 us  [prep(): pl.pallas_call(functools.partial(prep_kernel, n, terms * n + 1), out_shap...]
    pallas_call x2, Pallas kernels: 13.5 us -> 12 us  [apply(): pl.pallas_call(functools.partial(apply_kernel, n, npairs, over_rows, rows...]
  transfers between devices with their start and end apart: 48 -> 48, of which waited for: 24 -> 27; matrix products, arithmetic and copies ran while one was open for 0% -> 0% of each run, Pallas kernels for 3% -> 2%
where the time goes in v9:
time: 121 us; the launch traced here: 122 us
  waiting for transfers between devices  51.9 us (43%)
  starting transfers between devices  38.6 us (32%)
  Pallas kernels  18 us (15%)
  blocking collectives  11.1 us (9%)
  between operations  1.39 us (1%)
    ppermute x48, waiting for transfers between devices, swapped(): return lax.ppermute(x, 'term', [(i, i ^ k) for i in range(n)])  51.9 us
    ppermute x48, starting transfers between devices, swapped(): return lax.ppermute(x, 'term', [(i, i ^ k) for i in range(n)])  38.6 us
    pallas_call x2, Pallas kernels, apply(): pl.pallas_call(functools.partial(apply_kernel, n, npairs, over_rows, rows...  12 us
    all_to_all x1, blocking collectives, shards(): lax.all_to_all(jnp.broadcast_to(partial[None], (n, 8, width)), 'term', sp...  11.1 us
    pallas_call x5, Pallas kernels, local(): pl.pallas_call(kernel, out_shape=out_shape, in_specs=[SMEM] * len(scalars...  3.42 us
    pallas_call x1, Pallas kernels, prep(): pl.pallas_call(functools.partial(prep_kernel, n, terms * n + 1), out_shap...  2.51 us
  transfers between devices with their start and end apart: 48, of which 27 were waited for; matrix products, arithmetic and copies ran while one was open for 0% of the time, Pallas kernels for 2%

profile of v9, /device:TPU:0, one launch (start us, length us, event | category | flops | bytes accessed | tf_op | source)
XLA Modules:
  0.0 121.5 jit_solution(861255446773624647)
XLA Ops:
  0.6 3.0 %collective-permute-start.2 = (f32[2,128,128]{2,1,0:T(8,128)}, f32[2,128,128]{2,1,0:T(8,128)S(1)}, u32[]{:S(2)}, u32[]{:S(2)}) collective-permute-start(f32[2,128,128]{2,1,0:T(8,128)} %vector_in.1), channel_id=1, source_target_pairs={{0,2},{1,3},{2,0},{3,1},{4,6},{5,7},{6,4},{7,5},{8,10},{9,11},{10,... | collective-permute-start | bytes 393224 | tf_op jit(solution)/shard_map/ppermute | solution.py:242
  3.7 3.6 %collective-permute-start.11 = (f32[2,128,128]{2,1,0:T(8,128)}, f32[2,128,128]{2,1,0:T(8,128)S(1)}, u32[]{:S(2)}, u32[]{:S(2)}) collective-permute-start(f32[2,128,128]{2,1,0:T(8,128)} %vector_in.1), channel_id=1, source_target_pairs={{0,12},{1,13},{2,14},{3,15},{4,8},{5,9},{6,10},{7,11},{8,4},{9,5},... | collective-permute-start | bytes 393224 | tf_op jit(solution)/shard_map/ppermute | solution.py:242
  7.3 0.8 collective-permute-start.7
  8.1 1.2 %collective-permute-start.5 = (f32[2,128,128]{2,1,0:T(8,128)S(1)}, f32[2,128,128]{2,1,0:T(8,128)S(1)}, u32[]{:S(2)}, u32[]{:S(2)}) collective-permute-start(f32[2,128,128]{2,1,0:T(8,128)S(1)} %collective-permute-done.2.refs_2_), channel_id=1, source_target_pairs={{0,4},{1,5},{2,6},{3,7},{4,0},{5,1},{6,2},{7,3},{8,12},{9,13},{10,... | collective-permute-start | bytes 393224 | tf_op jit(solution)/shard_map/ppermute | solution.py:242
  9.3 2.8 %collective-permute-done.11.refs_12_ = f32[2,128,128]{2,1,0:T(8,128)S(1)} collective-permute-done((f32[2,128,128]{2,1,0:T(8,128)}, f32[2,128,128]{2,1,0:T(8,128)S(1)}, u32[]{:S(2)}, u32[]{:S(2)}) %collective-permute-start.11) | collective-permute-done | bytes 131104 | tf_op jit(solution)/shard_map/ppermute | solution.py:242
  12.4 3.3 %collective-permute-done.refs_4_ = f32[2,128,128]{2,1,0:T(8,128)S(1)} collective-permute-done((f32[2,128,128]{2,1,0:T(8,128)}, f32[2,128,128]{2,1,0:T(8,128)S(1)}, u32[]{:S(2)}, u32[]{:S(2)}) %collective-permute-start) | collective-permute-done | bytes 131104 | tf_op jit(solution)/shard_map/ppermute | solution.py:242
  15.7 2.7 %collective-permute-done.7.refs_8_ = f32[2,128,128]{2,1,0:T(8,128)S(1)} collective-permute-done((f32[2,128,128]{2,1,0:T(8,128)}, f32[2,128,128]{2,1,0:T(8,128)S(1)}, u32[]{:S(2)}, u32[]{:S(2)}) %collective-permute-start.7) | collective-permute-done | bytes 131104 | tf_op jit(solution)/shard_map/ppermute | solution.py:242
  18.3 0.6 collective-permute-start.9
  18.9 0.4 collective-permute-done.5.refs_6_
  19.9 0.6 copy.12
  20.5 2.5 %prep.1 = (bf16[8,128,512]{2,1,0:T(8,128)(2,1)S(1)}, bf16[2048,256]{1,0:T(8,128)(2,1)S(1)}, s32[721]{0:T(1024)S(1)}, f32[2,128,128]{2,1,0:T(8,128)S(1)}) custom-call(s32[1]{0:T(128)} %bitcast.me_ref, s32[16,16]{1,0:T(8,128)} %fetch_in.1, s32[16,16]{1,0:T(8,128)} %store_in.1, s32[384]{0:T(512)} %bitcast.8, s32[1]{0:T(128)S(6)} %copy.13.live_in, ...), custom_call_target="tpu_custom_call" | custom-call | tf_op jit(solution)/shard_map/prep/pallas_call | solution.py:132
  23.0 1.8 %collective-permute-start.4 = (f32[2,128,128]{2,1,0:T(8,128)S(1)}, f32[2,128,128]{2,1,0:T(8,128)S(1)}, u32[]{:S(2)}, u32[]{:S(2)}) collective-permute-start(f32[2,128,128]{2,1,0:T(8,128)S(1)} %collective-permute-done.refs_4_), channel_id=1, source_target_pairs={{0,1},{1,0},{2,3},{3,2},{4,5},{5,4},{6,7},{7,6},{8,9},{9,8},{10,11... | collective-permute-start | bytes 393224 | tf_op jit(solution)/shard_map/ppermute | solution.py:242
  25.0 0.4 collective-permute-start.6
  25.5 0.4 collective-permute-start.10
  26.4 0.3 collective-permute-done.14.refs_15_
  26.9 5.9 %apply.2 = (f32[640,128]{1,0:T(8,128)S(1)}, f32[648,128]{1,0:T(8,128)S(1)}, f32[264,128]{1,0:T(8,128)S(1)}, f32[264,128]{1,0:T(8,128)S(1)}, f32[128,128]{1,0:T(8...) custom-call(s32[721]{0:T(1024)S(1)} %get-tuple-element.35.table_ref, ...), custom_call_target="tpu_custom_call" | custom-call | tf_op jit(solution)/shard_map/apply/pallas_call | solution.py:216
  32.9 0.5 collective-permute-start.15
  33.4 0.9 collective-permute-start.16
  34.3 0.5 collective-permute-start.17
  34.8 1.9 %collective-permute-start.18 = (f32[128,128]{1,0:T(8,128)S(1)}, f32[128,128]{1,0:T(8,128)S(1)}, u32[]{:S(2)}, u32[]{:S(2)}) collective-permute-start(f32[128,128]{1,0:T(8,128)S(1)} %get-tuple-element.45), channel_id=1, source_target_pairs={{0,4},{1,5},{2,6},{3,7},{4,0},{5,1},{6,2},{7,3},{8,12},{9,13},{10,... | collective-permute-start | bytes 196616 | tf_op jit(solution)/shard_map/ppermute | solution.py:242
  36.7 0.3 collective-permute-start.19
  37.1 2.6 %collective-permute-done.18.column_ref = f32[128,128]{1,0:T(8,128)S(1)} collective-permute-done((f32[128,128]{1,0:T(8,128)S(1)}, f32[128,128]{1,0:T(8,128)S(1)}, u32[]{:S(2)}, u32[]{:S(2)}) %collective-permute-start.18) | collective-permute-done | bytes 65568 | tf_op jit(solution)/shard_map/ppermute | solution.py:242
  39.7 0.8 collective-permute-done.19.column_far_ref
  40.5 0.4 collective-permute-done.17.row_far_ref
  41.0 0.7 fold.2
  41.7 1.7 %collective-permute-start.21 = (f32[264,128]{1,0:T(8,128)S(1)}, f32[264,128]{1,0:T(8,128)S(1)}, u32[]{:S(2)}, u32[]{:S(2)}) collective-permute-start(f32[264,128]{1,0:T(8,128)S(1)} %get-tuple-element.51), channel_id=1, source_target_pairs={{0,8},{1,9},{2,10},{3,11},{4,12},{5,13},{6,14},{7,15},{8,0},{9,1},... | collective-permute-start | bytes 405512 | tf_op jit(solution)/shard_map/ppermute | solution.py:242
  43.4 2.6 %collective-permute-start.22 = (f32[264,128]{1,0:T(8,128)S(1)}, f32[264,128]{1,0:T(8,128)S(1)}, u32[]{:S(2)}, u32[]{:S(2)}) collective-permute-start(f32[264,128]{1,0:T(8,128)S(1)} %get-tuple-element.52), channel_id=1, source_target_pairs={{0,12},{1,13},{2,14},{3,15},{4,8},{5,9},{6,10},{7,11},{8,4},{9,5},... | collective-permute-start | bytes 405512 | tf_op jit(solution)/shard_map/ppermute | solution.py:242
  46.1 0.7 collective-permute-start.20
  46.8 4.8 %collective-permute-done.20.step_ref = f32[2,128,128]{2,1,0:T(8,128)S(1)} collective-permute-done((f32[2,128,128]{2,1,0:T(8,128)S(1)}, f32[2,128,128]{2,1,0:T(8,128)S(1)}, u32[]{:S(2)}, u32[]{:S(2)}) %collective-permute-start.20) | collective-permute-done | bytes 131104 | tf_op jit(solution)/shard_map/ppermute | solution.py:242
  51.6 3.4 %collective-permute-done.21.refs_1_ = f32[264,128]{1,0:T(8,128)S(1)} collective-permute-done((f32[264,128]{1,0:T(8,128)S(1)}, f32[264,128]{1,0:T(8,128)S(1)}, u32[]{:S(2)}, u32[]{:S(2)}) %collective-permute-start.21) | collective-permute-done | bytes 135200 | tf_op jit(solution)/shard_map/ppermute | solution.py:242
  55.0 1.0 collective-permute-done.23.refs_3_
  56.2 1.9 %collective-permute-start.35 = (f32[2,128,128]{2,1,0:T(8,128)S(1)}, f32[2,128,128]{2,1,0:T(8,128)S(1)}, u32[]{:S(2)}, u32[]{:S(2)}) collective-permute-start(f32[2,128,128]{2,1,0:T(8,128)S(1)} %step.1.refs_0_.vector_ref), channel_id=1, source_target_pairs={{0,12},{1,13},{2,14},{3,15},{4,8},{5,9},{6,10},{7,11},{8,4},{9,5},... | collective-permute-start | bytes 393224 | tf_op jit(solution)/shard_map/ppermute | solution.py:242
  58.1 1.8 %collective-permute-start.31 = (f32[2,128,128]{2,1,0:T(8,128)S(1)}, f32[2,128,128]{2,1,0:T(8,128)S(1)}, u32[]{:S(2)}, u32[]{:S(2)}) collective-permute-start(f32[2,128,128]{2,1,0:T(8,128)S(1)} %step.1.refs_0_.vector_ref), channel_id=1, source_target_pairs={{0,8},{1,9},{2,10},{3,11},{4,12},{5,13},{6,14},{7,15},{8,0},{9,1},... | collective-permute-start | bytes 393224 | tf_op jit(solution)/shard_map/ppermute | solution.py:242
  59.9 0.8 collective-permute-start.27
  60.7 1.2 collective-permute-start.25
  61.8 2.7 %collective-permute-done.35.refs_12_ = f32[2,128,128]{2,1,0:T(8,128)S(1)} collective-permute-done((f32[2,128,128]{2,1,0:T(8,128)S(1)}, f32[2,128,128]{2,1,0:T(8,128)S(1)}, u32[]{:S(2)}, u32[]{:S(2)}) %collective-permute-start.35) | collective-permute-done | bytes 131104 | tf_op jit(solution)/shard_map/ppermute | solution.py:242
  64.6 0.4 collective-permute-start.37
  64.9 6.3 %collective-permute-done.31.refs_8_ = f32[2,128,128]{2,1,0:T(8,128)S(1)} collective-permute-done((f32[2,128,128]{2,1,0:T(8,128)S(1)}, f32[2,128,128]{2,1,0:T(8,128)S(1)}, u32[]{:S(2)}, u32[]{:S(2)}) %collective-permute-start.31) | collective-permute-done | bytes 131104 | tf_op jit(solution)/shard_map/ppermute | solution.py:242
  71.3 0.8 collective-permute-start.33
  72.3 0.3 collective-permute-start.26
  72.9 4.3 %collective-permute-done.33.refs_10_ = f32[2,128,128]{2,1,0:T(8,128)S(1)} collective-permute-done((f32[2,128,128]{2,1,0:T(8,128)S(1)}, f32[2,128,128]{2,1,0:T(8,128)S(1)}, u32[]{:S(2)}, u32[]{:S(2)}) %collective-permute-start.33) | collective-permute-done | bytes 131104 | tf_op jit(solution)/shard_map/ppermute | solution.py:242
  77.2 0.5 collective-permute-start.34
  78.0 0.5 collective-permute-done.38.refs_15_
  78.7 0.6 collective-permute-done.30.refs_7_
  79.3 6.1 %apply.3 = (f32[640,128]{1,0:T(8,128)S(1)}, f32[648,128]{1,0:T(8,128)S(1)}, f32[264,128]{1,0:T(8,128)S(1)}, f32[264,128]{1,0:T(8,128)S(1)}, f32[128,128]{1,0:T(8...) custom-call(s32[721]{0:T(1024)S(1)} %get-tuple-element.35.table_ref, ...), custom_call_target="tpu_custom_call" | custom-call | tf_op jit(solution)/shard_map/apply/pallas_call | solution.py:216
  85.5 0.3 collective-permute-start.39
  85.8 1.1 collective-permute-start.40
  86.9 0.5 collective-permute-start.41
  87.4 0.4 collective-permute-start.42
  87.7 1.5 %collective-permute-start.43 = (f32[128,128]{1,0:T(8,128)S(1)}, f32[128,128]{1,0:T(8,128)S(1)}, u32[]{:S(2)}, u32[]{:S(2)}) collective-permute-start(f32[128,128]{1,0:T(8,128)S(1)} %get-tuple-element.58), channel_id=1, source_target_pairs={{0,5},{1,4},{2,7},{3,6},{4,1},{5,0},{6,3},{7,2},{8,13},{9,12},{10,... | collective-permute-start | bytes 196616 | tf_op jit(solution)/shard_map/ppermute | solution.py:242
  89.3 3.0 %collective-permute-done.42.column_ref = f32[128,128]{1,0:T(8,128)S(1)} collective-permute-done((f32[128,128]{1,0:T(8,128)S(1)}, f32[128,128]{1,0:T(8,128)S(1)}, u32[]{:S(2)}, u32[]{:S(2)}) %collective-permute-start.42) | collective-permute-done | bytes 65568 | tf_op jit(solution)/shard_map/ppermute | solution.py:242
  92.3 0.7 collective-permute-done.43.column_far_ref
  93.0 0.8 collective-permute-done.41.row_far_ref
  93.7 0.7 fold.3
  94.5 1.7 %collective-permute-start.45 = (f32[264,128]{1,0:T(8,128)S(1)}, f32[264,128]{1,0:T(8,128)S(1)}, u32[]{:S(2)}, u32[]{:S(2)}) collective-permute-start(f32[264,128]{1,0:T(8,128)S(1)} %get-tuple-element.63), channel_id=1, source_target_pairs={{0,8},{1,9},{2,10},{3,11},{4,12},{5,13},{6,14},{7,15},{8,0},{9,1},... | collective-permute-start | bytes 405512 | tf_op jit(solution)/shard_map/ppermute | solution.py:242
  96.1 1.2 %collective-permute-start.46 = (f32[264,128]{1,0:T(8,128)S(1)}, f32[264,128]{1,0:T(8,128)S(1)}, u32[]{:S(2)}, u32[]{:S(2)}) collective-permute-start(f32[264,128]{1,0:T(8,128)S(1)} %get-tuple-element.64), channel_id=1, source_target_pairs={{0,12},{1,13},{2,14},{3,15},{4,8},{5,9},{6,10},{7,11},{8,4},{9,5},... | collective-permute-start | bytes 405512 | tf_op jit(solution)/shard_map/ppermute | solution.py:242
  97.4 0.7 collective-permute-start.47
  98.0 1.5 %collective-permute-start.44 = (f32[2,128,128]{2,1,0:T(8,128)S(1)}, f32[2,128,128]{2,1,0:T(8,128)S(1)}, u32[]{:S(2)}, u32[]{:S(2)}) collective-permute-start(f32[2,128,128]{2,1,0:T(8,128)S(1)} %get-tuple-element.60), channel_id=1, source_target_pairs={{0,2},{1,3},{2,0},{3,1},{4,6},{5,7},{6,4},{7,5},{8,10},{9,11},{10,... | collective-permute-start | bytes 393224 | tf_op jit(solution)/shard_map/ppermute | solution.py:242
  99.6 3.6 %collective-permute-done.44.step_ref = f32[2,128,128]{2,1,0:T(8,128)S(1)} collective-permute-done((f32[2,128,128]{2,1,0:T(8,128)S(1)}, f32[2,128,128]{2,1,0:T(8,128)S(1)}, u32[]{:S(2)}, u32[]{:S(2)}) %collective-permute-start.44) | collective-permute-done | bytes 131104 | tf_op jit(solution)/shard_map/ppermute | solution.py:242
  103.1 4.3 %collective-permute-done.45.refs_1_ = f32[264,128]{1,0:T(8,128)S(1)} collective-permute-done((f32[264,128]{1,0:T(8,128)S(1)}, f32[264,128]{1,0:T(8,128)S(1)}, u32[]{:S(2)}, u32[]{:S(2)}) %collective-permute-start.45) | collective-permute-done | bytes 135200 | tf_op jit(solution)/shard_map/ppermute | solution.py:242
  107.4 1.3 %collective-permute-done.47.refs_3_ = f32[264,128]{1,0:T(8,128)S(1)} collective-permute-done((f32[264,128]{1,0:T(8,128)S(1)}, f32[264,128]{1,0:T(8,128)S(1)}, u32[]{:S(2)}, u32[]{:S(2)}) %collective-permute-start.47) | collective-permute-done | bytes 135200 | tf_op jit(solution)/shard_map/ppermute | solution.py:242
  108.7 0.9 last.1
  109.6 11.1 %all_to_all.5.tiles_ref = f32[16,8,128]{2,1,0:T(8,128)S(1)} all-to-all(f32[16,8,128]{2,1,0:T(8,128)S(1)} %broadcast_in_dim.2), channel_id=1, replica_groups=mesh['group'=2,'term'=16] {'term'}, dimensions={0} | all-to-all | bytes 131072 | tf_op jit(solution)/shard_map/all_to_all | solution.py:384
  120.7 0.9 norm.1
  (47 shorter events, 2.4 us)
Async XLA Ops:
  0.6 7.4 %collective-permute-start.2 = (f32[2,128,128]{2,1,0:T(8,128)}, f32[2,128,128]{2,1,0:T(8,128)S(1)}, u32[]{:S(2)}, u32[]{:S(2)}) collective-permute-start(f32[2,128,128]{2,1,0:T(8,128)} %vector_in.1), channel_id=1, source_target_pairs={{0,2},{1,3},{2,0},{3,1},{4,6},{5,7},{6,4},{7,5},{8,10},{9,11},{10,... | collective-permute-start | bytes 393224 | tf_op jit(solution)/shard_map/ppermute | solution.py:242
  3.7 8.4 %collective-permute-start.11 = (f32[2,128,128]{2,1,0:T(8,128)}, f32[2,128,128]{2,1,0:T(8,128)S(1)}, u32[]{:S(2)}, u32[]{:S(2)}) collective-permute-start(f32[2,128,128]{2,1,0:T(8,128)} %vector_in.1), channel_id=1, source_target_pairs={{0,12},{1,13},{2,14},{3,15},{4,8},{5,9},{6,10},{7,11},{8,4},{9,5},... | collective-permute-start | bytes 393224 | tf_op jit(solution)/shard_map/ppermute | solution.py:242
  7.3 8.4 %collective-permute-start = (f32[2,128,128]{2,1,0:T(8,128)}, f32[2,128,128]{2,1,0:T(8,128)S(1)}, u32[]{:S(2)}, u32[]{:S(2)}) collective-permute-start(f32[2,128,128]{2,1,0:T(8,128)} %vector_in.1), channel_id=1, source_target_pairs={{0,4},{1,5},{2,6},{3,7},{4,0},{5,1},{6,2},{7,3},{8,12},{9,13},{10,... | collective-permute-start | bytes 393224 | tf_op jit(solution)/shard_map/ppermute | solution.py:242
  7.3 11.1 %collective-permute-start.7 = (f32[2,128,128]{2,1,0:T(8,128)}, f32[2,128,128]{2,1,0:T(8,128)S(1)}, u32[]{:S(2)}, u32[]{:S(2)}) collective-permute-start(f32[2,128,128]{2,1,0:T(8,128)} %vector_in.1), channel_id=1, source_target_pairs={{0,8},{1,9},{2,10},{3,11},{4,12},{5,13},{6,14},{7,15},{8,0},{9,1},... | collective-permute-start | bytes 393224 | tf_op jit(solution)/shard_map/ppermute | solution.py:242
  8.1 11.2 %collective-permute-start.5 = (f32[2,128,128]{2,1,0:T(8,128)S(1)}, f32[2,128,128]{2,1,0:T(8,128)S(1)}, u32[]{:S(2)}, u32[]{:S(2)}) collective-permute-start(f32[2,128,128]{2,1,0:T(8,128)S(1)} %collective-permute-done.2.refs_2_), channel_id=1, source_target_pairs={{0,4},{1,5},{2,6},{3,7},{4,0},{5,1},{6,2},{7,3},{8,12},{9,13},{10,... | collective-permute-start | bytes 393224 | tf_op jit(solution)/shard_map/ppermute | solution.py:242
  9.3 13.7 %collective-permute-start.3 = (f32[2,128,128]{2,1,0:T(8,128)S(1)}, f32[2,128,128]{2,1,0:T(8,128)S(1)}, u32[]{:S(2)}, u32[]{:S(2)}) collective-permute-start(f32[2,128,128]{2,1,0:T(8,128)S(1)} %collective-permute-done.2.refs_2_), channel_id=1, source_target_pairs={{0,1},{1,0},{2,3},{3,2},{4,5},{5,4},{6,7},{7,6},{8,9},{9,8},{10,11... | collective-permute-start | bytes 393224 | tf_op jit(solution)/shard_map/ppermute | solution.py:242
  12.1 12.8 %collective-permute-start.13 = (f32[2,128,128]{2,1,0:T(8,128)S(1)}, f32[2,128,128]{2,1,0:T(8,128)S(1)}, u32[]{:S(2)}, u32[]{:S(2)}) collective-permute-start(f32[2,128,128]{2,1,0:T(8,128)S(1)} %collective-permute-done.11.refs_12_), channel_id=1, source_target_pairs={{0,2},{1,3},{2,0},{3,1},{4,6},{5,7},{6,4},{7,5},{8,10},{9,11},{10,... | collective-permute-start | bytes 393224 | tf_op jit(solution)/shard_map/ppermute | solution.py:242
  15.7 9.3 %collective-permute-start.12 = (f32[2,128,128]{2,1,0:T(8,128)S(1)}, f32[2,128,128]{2,1,0:T(8,128)S(1)}, u32[]{:S(2)}, u32[]{:S(2)}) collective-permute-start(f32[2,128,128]{2,1,0:T(8,128)S(1)} %collective-permute-done.11.refs_12_), channel_id=1, source_target_pairs={{0,1},{1,0},{2,3},{3,2},{4,5},{5,4},{6,7},{7,6},{8,9},{9,8},{10,11... | collective-permute-start | bytes 393224 | tf_op jit(solution)/shard_map/ppermute | solution.py:242
  18.3 7.1 %collective-permute-start.9 = (f32[2,128,128]{2,1,0:T(8,128)S(1)}, f32[2,128,128]{2,1,0:T(8,128)S(1)}, u32[]{:S(2)}, u32[]{:S(2)}) collective-permute-start(f32[2,128,128]{2,1,0:T(8,128)S(1)} %collective-permute-done.7.refs_8_), channel_id=1, source_target_pairs={{0,2},{1,3},{2,0},{3,1},{4,6},{5,7},{6,4},{7,5},{8,10},{9,11},{10,... | collective-permute-start | bytes 393224 | tf_op jit(solution)/shard_map/ppermute | solution.py:242
  19.3 6.2 %collective-permute-start.8 = (f32[2,128,128]{2,1,0:T(8,128)S(1)}, f32[2,128,128]{2,1,0:T(8,128)S(1)}, u32[]{:S(2)}, u32[]{:S(2)}) collective-permute-start(f32[2,128,128]{2,1,0:T(8,128)S(1)} %collective-permute-done.7.refs_8_), channel_id=1, source_target_pairs={{0,1},{1,0},{2,3},{3,2},{4,5},{5,4},{6,7},{7,6},{8,9},{9,8},{10,11... | collective-permute-start | bytes 393224 | tf_op jit(solution)/shard_map/ppermute | solution.py:242
  19.3 0.7 copy-start.1
  23.0 2.9 %collective-permute-start.4 = (f32[2,128,128]{2,1,0:T(8,128)S(1)}, f32[2,128,128]{2,1,0:T(8,128)S(1)}, u32[]{:S(2)}, u32[]{:S(2)}) collective-permute-start(f32[2,128,128]{2,1,0:T(8,128)S(1)} %collective-permute-done.refs_4_), channel_id=1, source_target_pairs={{0,1},{1,0},{2,3},{3,2},{4,5},{5,4},{6,7},{7,6},{8,9},{9,8},{10,11... | collective-permute-start | bytes 393224 | tf_op jit(solution)/shard_map/ppermute | solution.py:242
  24.9 1.3 %collective-permute-start.1 = (f32[2,128,128]{2,1,0:T(8,128)S(1)}, f32[2,128,128]{2,1,0:T(8,128)S(1)}, u32[]{:S(2)}, u32[]{:S(2)}) collective-permute-start(f32[2,128,128]{2,1,0:T(8,128)S(1)} %get-tuple-element.39.refs_0_.vector_ref), channel_id=1, source_target_pairs={{0,1},{1,0},{2,3},{3,2},{4,5},{5,4},{6,7},{7,6},{8,9},{9,8},{10,11... | collective-permute-start | bytes 393224 | tf_op jit(solution)/shard_map/ppermute | solution.py:242
  25.0 1.4 %collective-permute-start.6 = (f32[2,128,128]{2,1,0:T(8,128)S(1)}, f32[2,128,128]{2,1,0:T(8,128)S(1)}, u32[]{:S(2)}, u32[]{:S(2)}) collective-permute-start(f32[2,128,128]{2,1,0:T(8,128)S(1)} %collective-permute-done.5.refs_6_), channel_id=1, source_target_pairs={{0,1},{1,0},{2,3},{3,2},{4,5},{5,4},{6,7},{7,6},{8,9},{9,8},{10,11... | collective-permute-start | bytes 393224 | tf_op jit(solution)/shard_map/ppermute | solution.py:242
  25.4 1.3 %collective-permute-start.14 = (f32[2,128,128]{2,1,0:T(8,128)S(1)}, f32[2,128,128]{2,1,0:T(8,128)S(1)}, u32[]{:S(2)}, u32[]{:S(2)}) collective-permute-start(f32[2,128,128]{2,1,0:T(8,128)S(1)} %collective-permute-done.13.refs_14_), channel_id=1, source_target_pairs={{0,1},{1,0},{2,3},{3,2},{4,5},{5,4},{6,7},{7,6},{8,9},{9,8},{10,11... | collective-permute-start | bytes 393224 | tf_op jit(solution)/shard_map/ppermute | solution.py:242
  25.5 1.4 %collective-permute-start.10 = (f32[2,128,128]{2,1,0:T(8,128)S(1)}, f32[2,128,128]{2,1,0:T(8,128)S(1)}, u32[]{:S(2)}, u32[]{:S(2)}) collective-permute-start(f32[2,128,128]{2,1,0:T(8,128)S(1)} %collective-permute-done.9.refs_10_), channel_id=1, source_target_pairs={{0,1},{1,0},{2,3},{3,2},{4,5},{5,4},{6,7},{7,6},{8,9},{9,8},{10,11... | collective-permute-start | bytes 393224 | tf_op jit(solution)/shard_map/ppermute | solution.py:242
  32.9 8.1 %collective-permute-start.15 = (f32[648,128]{1,0:T(8,128)S(1)}, f32[648,128]{1,0:T(8,128)S(1)}, u32[]{:S(2)}, u32[]{:S(2)}) collective-permute-start(f32[648,128]{1,0:T(8,128)S(1)} %get-tuple-element.42.far_in), channel_id=1, source_target_pairs={{0,1},{1,0},{2,3},{3,2},{4,5},{5,4},{6,7},{7,6},{8,9},{9,8},{10,11... | collective-permute-start | bytes 995336 | tf_op jit(solution)/shard_map/ppermute | solution.py:242
  33.4 7.2 %collective-permute-start.16 = (f32[264,128]{1,0:T(8,128)S(1)}, f32[264,128]{1,0:T(8,128)S(1)}, u32[]{:S(2)}, u32[]{:S(2)}) collective-permute-start(f32[264,128]{1,0:T(8,128)S(1)} %get-tuple-element.43), channel_id=1, source_target_pairs={{0,2},{1,3},{2,0},{3,1},{4,6},{5,7},{6,4},{7,5},{8,10},{9,11},{10,... | collective-permute-start | bytes 405512 | tf_op jit(solution)/shard_map/ppermute | solution.py:242
  34.3 6.7 %collective-permute-start.17 = (f32[264,128]{1,0:T(8,128)S(1)}, f32[264,128]{1,0:T(8,128)S(1)}, u32[]{:S(2)}, u32[]{:S(2)}) collective-permute-start(f32[264,128]{1,0:T(8,128)S(1)} %get-tuple-element.44), channel_id=1, source_target_pairs={{0,3},{1,2},{2,1},{3,0},{4,7},{5,6},{6,5},{7,4},{8,11},{9,10},{10,... | collective-permute-start | bytes 405512 | tf_op jit(solution)/shard_map/ppermute | solution.py:242
  34.8 4.9 %collective-permute-start.18 = (f32[128,128]{1,0:T(8,128)S(1)}, f32[128,128]{1,0:T(8,128)S(1)}, u32[]{:S(2)}, u32[]{:S(2)}) collective-permute-start(f32[128,128]{1,0:T(8,128)S(1)} %get-tuple-element.45), channel_id=1, source_target_pairs={{0,4},{1,5},{2,6},{3,7},{4,0},{5,1},{6,2},{7,3},{8,12},{9,13},{10,... | collective-permute-start | bytes 196616 | tf_op jit(solution)/shard_map/ppermute | solution.py:242
  36.7 3.8 %collective-permute-start.19 = (f32[128,128]{1,0:T(8,128)S(1)}, f32[128,128]{1,0:T(8,128)S(1)}, u32[]{:S(2)}, u32[]{:S(2)}) collective-permute-start(f32[128,128]{1,0:T(8,128)S(1)} %get-tuple-element.46), channel_id=1, source_target_pairs={{0,5},{1,4},{2,7},{3,6},{4,1},{5,0},{6,3},{7,2},{8,13},{9,12},{10,... | collective-permute-start | bytes 196616 | tf_op jit(solution)/shard_map/ppermute | solution.py:242
  41.0 15.1 %copy-start = (f32[2,128,128]{2,1,0:T(8,128)S(1)}, f32[2,128,128]{2,1,0:T(8,128)}, u32[]{:S(2)}) copy-start(f32[2,128,128]{2,1,0:T(8,128)} %precond_ref.3) | copy-start | bytes 393220
  41.7 13.3 %collective-permute-start.21 = (f32[264,128]{1,0:T(8,128)S(1)}, f32[264,128]{1,0:T(8,128)S(1)}, u32[]{:S(2)}, u32[]{:S(2)}) collective-permute-start(f32[264,128]{1,0:T(8,128)S(1)} %get-tuple-element.51), channel_id=1, source_target_pairs={{0,8},{1,9},{2,10},{3,11},{4,12},{5,13},{6,14},{7,15},{8,0},{9,1},... | collective-permute-start | bytes 405512 | tf_op jit(solution)/shard_map/ppermute | solution.py:242
  43.4 11.6 %collective-permute-start.22 = (f32[264,128]{1,0:T(8,128)S(1)}, f32[264,128]{1,0:T(8,128)S(1)}, u32[]{:S(2)}, u32[]{:S(2)}) collective-permute-start(f32[264,128]{1,0:T(8,128)S(1)} %get-tuple-element.52), channel_id=1, source_target_pairs={{0,12},{1,13},{2,14},{3,15},{4,8},{5,9},{6,10},{7,11},{8,4},{9,5},... | collective-permute-start | bytes 405512 | tf_op jit(solution)/shard_map/ppermute | solution.py:242
  46.1 10.0 %collective-permute-start.23 = (f32[264,128]{1,0:T(8,128)S(1)}, f32[264,128]{1,0:T(8,128)S(1)}, u32[]{:S(2)}, u32[]{:S(2)}) collective-permute-start(f32[264,128]{1,0:T(8,128)S(1)} %get-tuple-element.50.refs_0_), channel_id=1, source_target_pairs={{0,4},{1,5},{2,6},{3,7},{4,0},{5,1},{6,2},{7,3},{8,12},{9,13},{10,... | collective-permute-start | bytes 405512 | tf_op jit(solution)/shard_map/ppermute | solution.py:242
  46.1 5.6 %collective-permute-start.20 = (f32[2,128,128]{2,1,0:T(8,128)S(1)}, f32[2,128,128]{2,1,0:T(8,128)S(1)}, u32[]{:S(2)}, u32[]{:S(2)}) collective-permute-start(f32[2,128,128]{2,1,0:T(8,128)S(1)} %get-tuple-element.48), channel_id=1, source_target_pairs={{0,2},{1,3},{2,0},{3,1},{4,6},{5,7},{6,4},{7,5},{8,10},{9,11},{10,... | collective-permute-start | bytes 393224 | tf_op jit(solution)/shard_map/ppermute | solution.py:242
  56.2 8.3 %collective-permute-start.35 = (f32[2,128,128]{2,1,0:T(8,128)S(1)}, f32[2,128,128]{2,1,0:T(8,128)S(1)}, u32[]{:S(2)}, u32[]{:S(2)}) collective-permute-start(f32[2,128,128]{2,1,0:T(8,128)S(1)} %step.1.refs_0_.vector_ref), channel_id=1, source_target_pairs={{0,12},{1,13},{2,14},{3,15},{4,8},{5,9},{6,10},{7,11},{8,4},{9,5},... | collective-permute-start | bytes 393224 | tf_op jit(solution)/shard_map/ppermute | solution.py:242
  58.1 13.1 %collective-permute-start.31 = (f32[2,128,128]{2,1,0:T(8,128)S(1)}, f32[2,128,128]{2,1,0:T(8,128)S(1)}, u32[]{:S(2)}, u32[]{:S(2)}) collective-permute-start(f32[2,128,128]{2,1,0:T(8,128)S(1)} %step.1.refs_0_.vector_ref), channel_id=1, source_target_pairs={{0,8},{1,9},{2,10},{3,11},{4,12},{5,13},{6,14},{7,15},{8,0},{9,1},... | collective-permute-start | bytes 393224 | tf_op jit(solution)/shard_map/ppermute | solution.py:242
  59.9 11.4 %collective-permute-start.27 = (f32[2,128,128]{2,1,0:T(8,128)S(1)}, f32[2,128,128]{2,1,0:T(8,128)S(1)}, u32[]{:S(2)}, u32[]{:S(2)}) collective-permute-start(f32[2,128,128]{2,1,0:T(8,128)S(1)} %step.1.refs_0_.vector_ref), channel_id=1, source_target_pairs={{0,4},{1,5},{2,6},{3,7},{4,0},{5,1},{6,2},{7,3},{8,12},{9,13},{10,... | collective-permute-start | bytes 393224 | tf_op jit(solution)/shard_map/ppermute | solution.py:242
  60.7 11.4 %collective-permute-start.25 = (f32[2,128,128]{2,1,0:T(8,128)S(1)}, f32[2,128,128]{2,1,0:T(8,128)S(1)}, u32[]{:S(2)}, u32[]{:S(2)}) collective-permute-start(f32[2,128,128]{2,1,0:T(8,128)S(1)} %step.1.refs_0_.vector_ref), channel_id=1, source_target_pairs={{0,2},{1,3},{2,0},{3,1},{4,6},{5,7},{6,4},{7,5},{8,10},{9,11},{10,... | collective-permute-start | bytes 393224 | tf_op jit(solution)/shard_map/ppermute | solution.py:242
  61.8 10.5 %collective-permute-start.24 = (f32[2,128,128]{2,1,0:T(8,128)S(1)}, f32[2,128,128]{2,1,0:T(8,128)S(1)}, u32[]{:S(2)}, u32[]{:S(2)}) collective-permute-start(f32[2,128,128]{2,1,0:T(8,128)S(1)} %step.1.refs_0_.vector_ref), channel_id=1, source_target_pairs={{0,1},{1,0},{2,3},{3,2},{4,5},{5,4},{6,7},{7,6},{8,9},{9,8},{10,11... | collective-permute-start | bytes 393224 | tf_op jit(solution)/shard_map/ppermute | solution.py:242
  64.6 7.8 %collective-permute-start.37 = (f32[2,128,128]{2,1,0:T(8,128)S(1)}, f32[2,128,128]{2,1,0:T(8,128)S(1)}, u32[]{:S(2)}, u32[]{:S(2)}) collective-permute-start(f32[2,128,128]{2,1,0:T(8,128)S(1)} %collective-permute-done.35.refs_12_), channel_id=1, source_target_pairs={{0,2},{1,3},{2,0},{3,1},{4,6},{5,7},{6,4},{7,5},{8,10},{9,11},{10,... | collective-permute-start | bytes 393224 | tf_op jit(solution)/shard_map/ppermute | solution.py:242
  71.3 1.4 %collective-permute-start.36 = (f32[2,128,128]{2,1,0:T(8,128)S(1)}, f32[2,128,128]{2,1,0:T(8,128)S(1)}, u32[]{:S(2)}, u32[]{:S(2)}) collective-permute-start(f32[2,128,128]{2,1,0:T(8,128)S(1)} %collective-permute-done.35.refs_12_), channel_id=1, source_target_pairs={{0,1},{1,0},{2,3},{3,2},{4,5},{5,4},{6,7},{7,6},{8,9},{9,8},{10,11... | collective-permute-start | bytes 393224 | tf_op jit(solution)/shard_map/ppermute | solution.py:242
  71.3 5.9 %collective-permute-start.33 = (f32[2,128,128]{2,1,0:T(8,128)S(1)}, f32[2,128,128]{2,1,0:T(8,128)S(1)}, u32[]{:S(2)}, u32[]{:S(2)}) collective-permute-start(f32[2,128,128]{2,1,0:T(8,128)S(1)} %collective-permute-done.31.refs_8_), channel_id=1, source_target_pairs={{0,2},{1,3},{2,0},{3,1},{4,6},{5,7},{6,4},{7,5},{8,10},{9,11},{10,... | collective-permute-start | bytes 393224 | tf_op jit(solution)/shard_map/ppermute | solution.py:242
  72.1 5.1 %collective-permute-start.32 = (f32[2,128,128]{2,1,0:T(8,128)S(1)}, f32[2,128,128]{2,1,0:T(8,128)S(1)}, u32[]{:S(2)}, u32[]{:S(2)}) collective-permute-start(f32[2,128,128]{2,1,0:T(8,128)S(1)} %collective-permute-done.31.refs_8_), channel_id=1, source_target_pairs={{0,1},{1,0},{2,3},{3,2},{4,5},{5,4},{6,7},{7,6},{8,9},{9,8},{10,11... | collective-permute-start | bytes 393224 | tf_op jit(solution)/shard_map/ppermute | solution.py:242
  72.3 5.7 %collective-permute-start.29 = (f32[2,128,128]{2,1,0:T(8,128)S(1)}, f32[2,128,128]{2,1,0:T(8,128)S(1)}, u32[]{:S(2)}, u32[]{:S(2)}) collective-permute-start(f32[2,128,128]{2,1,0:T(8,128)S(1)} %collective-permute-done.25.refs_2_), channel_id=1, source_target_pairs={{0,4},{1,5},{2,6},{3,7},{4,0},{5,1},{6,2},{7,3},{8,12},{9,13},{10,... | collective-permute-start | bytes 393224 | tf_op jit(solution)/shard_map/ppermute | solution.py:242
  72.3 5.7 %collective-permute-start.26 = (f32[2,128,128]{2,1,0:T(8,128)S(1)}, f32[2,128,128]{2,1,0:T(8,128)S(1)}, u32[]{:S(2)}, u32[]{:S(2)}) collective-permute-start(f32[2,128,128]{2,1,0:T(8,128)S(1)} %collective-permute-done.25.refs_2_), channel_id=1, source_target_pairs={{0,1},{1,0},{2,3},{3,2},{4,5},{5,4},{6,7},{7,6},{8,9},{9,8},{10,11... | collective-permute-start | bytes 393224 | tf_op jit(solution)/shard_map/ppermute | solution.py:242
  72.7 5.3 %collective-permute-start.28 = (f32[2,128,128]{2,1,0:T(8,128)S(1)}, f32[2,128,128]{2,1,0:T(8,128)S(1)}, u32[]{:S(2)}, u32[]{:S(2)}) collective-permute-start(f32[2,128,128]{2,1,0:T(8,128)S(1)} %collective-permute-done.27.refs_4_), channel_id=1, source_target_pairs={{0,1},{1,0},{2,3},{3,2},{4,5},{5,4},{6,7},{7,6},{8,9},{9,8},{10,11... | collective-permute-start | bytes 393224 | tf_op jit(solution)/shard_map/ppermute | solution.py:242
  77.2 1.3 %collective-permute-start.38 = (f32[2,128,128]{2,1,0:T(8,128)S(1)}, f32[2,128,128]{2,1,0:T(8,128)S(1)}, u32[]{:S(2)}, u32[]{:S(2)}) collective-permute-start(f32[2,128,128]{2,1,0:T(8,128)S(1)} %collective-permute-done.37.refs_14_), channel_id=1, source_target_pairs={{0,1},{1,0},{2,3},{3,2},{4,5},{5,4},{6,7},{7,6},{8,9},{9,8},{10,11... | collective-permute-start | bytes 393224 | tf_op jit(solution)/shard_map/ppermute | solution.py:242
  77.2 1.5 %collective-permute-start.34 = (f32[2,128,128]{2,1,0:T(8,128)S(1)}, f32[2,128,128]{2,1,0:T(8,128)S(1)}, u32[]{:S(2)}, u32[]{:S(2)}) collective-permute-start(f32[2,128,128]{2,1,0:T(8,128)S(1)} %collective-permute-done.33.refs_10_), channel_id=1, source_target_pairs={{0,1},{1,0},{2,3},{3,2},{4,5},{5,4},{6,7},{7,6},{8,9},{9,8},{10,11... | collective-permute-start | bytes 393224 | tf_op jit(solution)/shard_map/ppermute | solution.py:242
  78.0 1.3 %collective-permute-start.30 = (f32[2,128,128]{2,1,0:T(8,128)S(1)}, f32[2,128,128]{2,1,0:T(8,128)S(1)}, u32[]{:S(2)}, u32[]{:S(2)}) collective-permute-start(f32[2,128,128]{2,1,0:T(8,128)S(1)} %collective-permute-done.29.refs_6_), channel_id=1, source_target_pairs={{0,1},{1,0},{2,3},{3,2},{4,5},{5,4},{6,7},{7,6},{8,9},{9,8},{10,11... | collective-permute-start | bytes 393224 | tf_op jit(solution)/shard_map/ppermute | solution.py:242
  85.5 8.3 %collective-permute-start.39 = (f32[648,128]{1,0:T(8,128)S(1)}, f32[648,128]{1,0:T(8,128)S(1)}, u32[]{:S(2)}, u32[]{:S(2)}) collective-permute-start(f32[648,128]{1,0:T(8,128)S(1)} %get-tuple-element.54.far_in), channel_id=1, source_target_pairs={{0,1},{1,0},{2,3},{3,2},{4,5},{5,4},{6,7},{7,6},{8,9},{9,8},{10,11... | collective-permute-start | bytes 995336 | tf_op jit(solution)/shard_map/ppermute | solution.py:242
  85.8 7.2 %collective-permute-start.40 = (f32[264,128]{1,0:T(8,128)S(1)}, f32[264,128]{1,0:T(8,128)S(1)}, u32[]{:S(2)}, u32[]{:S(2)}) collective-permute-start(f32[264,128]{1,0:T(8,128)S(1)} %get-tuple-element.55), channel_id=1, source_target_pairs={{0,2},{1,3},{2,0},{3,1},{4,6},{5,7},{6,4},{7,5},{8,10},{9,11},{10,... | collective-permute-start | bytes 405512 | tf_op jit(solution)/shard_map/ppermute | solution.py:242
  86.9 6.8 %collective-permute-start.41 = (f32[264,128]{1,0:T(8,128)S(1)}, f32[264,128]{1,0:T(8,128)S(1)}, u32[]{:S(2)}, u32[]{:S(2)}) collective-permute-start(f32[264,128]{1,0:T(8,128)S(1)} %get-tuple-element.56), channel_id=1, source_target_pairs={{0,3},{1,2},{2,1},{3,0},{4,7},{5,6},{6,5},{7,4},{8,11},{9,10},{10,... | collective-permute-start | bytes 405512 | tf_op jit(solution)/shard_map/ppermute | solution.py:242
  87.4 4.9 %collective-permute-start.42 = (f32[128,128]{1,0:T(8,128)S(1)}, f32[128,128]{1,0:T(8,128)S(1)}, u32[]{:S(2)}, u32[]{:S(2)}) collective-permute-start(f32[128,128]{1,0:T(8,128)S(1)} %get-tuple-element.57), channel_id=1, source_target_pairs={{0,4},{1,5},{2,6},{3,7},{4,0},{5,1},{6,2},{7,3},{8,12},{9,13},{10,... | collective-permute-start | bytes 196616 | tf_op jit(solution)/shard_map/ppermute | solution.py:242
  87.7 5.2 %collective-permute-start.43 = (f32[128,128]{1,0:T(8,128)S(1)}, f32[128,128]{1,0:T(8,128)S(1)}, u32[]{:S(2)}, u32[]{:S(2)}) collective-permute-start(f32[128,128]{1,0:T(8,128)S(1)} %get-tuple-element.58), channel_id=1, source_target_pairs={{0,5},{1,4},{2,7},{3,6},{4,1},{5,0},{6,3},{7,2},{8,13},{9,12},{10,... | collective-permute-start | bytes 196616 | tf_op jit(solution)/shard_map/ppermute | solution.py:242
  94.5 12.9 %collective-permute-start.45 = (f32[264,128]{1,0:T(8,128)S(1)}, f32[264,128]{1,0:T(8,128)S(1)}, u32[]{:S(2)}, u32[]{:S(2)}) collective-permute-start(f32[264,128]{1,0:T(8,128)S(1)} %get-tuple-element.63), channel_id=1, source_target_pairs={{0,8},{1,9},{2,10},{3,11},{4,12},{5,13},{6,14},{7,15},{8,0},{9,1},... | collective-permute-start | bytes 405512 | tf_op jit(solution)/shard_map/ppermute | solution.py:242
  96.1 11.3 %collective-permute-start.46 = (f32[264,128]{1,0:T(8,128)S(1)}, f32[264,128]{1,0:T(8,128)S(1)}, u32[]{:S(2)}, u32[]{:S(2)}) collective-permute-start(f32[264,128]{1,0:T(8,128)S(1)} %get-tuple-element.64), channel_id=1, source_target_pairs={{0,12},{1,13},{2,14},{3,15},{4,8},{5,9},{6,10},{7,11},{8,4},{9,5},... | collective-permute-start | bytes 405512 | tf_op jit(solution)/shard_map/ppermute | solution.py:242
  97.4 11.3 %collective-permute-start.47 = (f32[264,128]{1,0:T(8,128)S(1)}, f32[264,128]{1,0:T(8,128)S(1)}, u32[]{:S(2)}, u32[]{:S(2)}) collective-permute-start(f32[264,128]{1,0:T(8,128)S(1)} %get-tuple-element.62.refs_0_), channel_id=1, source_target_pairs={{0,4},{1,5},{2,6},{3,7},{4,0},{5,1},{6,2},{7,3},{8,12},{9,13},{10,... | collective-permute-start | bytes 405512 | tf_op jit(solution)/shard_map/ppermute | solution.py:242
  98.0 5.1 %collective-permute-start.44 = (f32[2,128,128]{2,1,0:T(8,128)S(1)}, f32[2,128,128]{2,1,0:T(8,128)S(1)}, u32[]{:S(2)}, u32[]{:S(2)}) collective-permute-start(f32[2,128,128]{2,1,0:T(8,128)S(1)} %get-tuple-element.60), channel_id=1, source_target_pairs={{0,2},{1,3},{2,0},{3,1},{4,6},{5,7},{6,4},{7,5},{8,10},{9,11},{10,... | collective-permute-start | bytes 393224 | tf_op jit(solution)/shard_map/ppermute | solution.py:242

commit v10 on v9

--- a/solution.py
+++ b/solution.py
@@ -327,7 +327,7 @@
     out_ref[...] = corrected_ref[...] * scale
 
 
-def scattered(n, tables, pieces):
+def scattered(n, tables, pieces, last):
     width = pieces[0].shape[1]
     chips = n // 2
     rows = width if n <= 16 else width // 4
@@ -343,7 +343,8 @@
         (shape(2, width, width),) * 2 + (shape(2 * width + 8, width),) * (chips // 2 - 1), tables[2:3],
         (near, far, swapped(far, CORE), swapped(row, ROW), swapped(row_far, ROW + CORE), swapped(column, COLUMN),
          swapped(column_far, COLUMN + CORE)))
-    came = [swapped(sends[i], 2 * ROW * (i + 1)) for i in (*range(1, len(sends)), 0)]
+    order = range(len(sends))
+    came = [swapped(sends[i], 2 * ROW * (i + 1)) for i in ((*order[1:], 0) if last else order[::-1])]
     return square, (own, swapped(step, ROW)), [sends[0], *came]
 
 
@@ -353,11 +354,11 @@
         pieces[k] = swapped(x, k)
     pieces[ROW] = swapped(x, ROW)
     pieces[COLUMN] = swapped(x, COLUMN)
-    if held is not None:
-        pieces[COLUMN], pieces[0] = lax.optimization_barrier((pieces[COLUMN], held))
     for k in reversed(range(8, n, 4)):
         pieces[k + ROW] = swapped(pieces[k], ROW)
     pieces[COLUMN + ROW] = swapped(pieces[ROW], COLUMN)
+    if held is not None:
+        pieces[n - 4 + ROW], pieces[0] = lax.optimization_barrier((pieces[n - 4 + ROW], held))
     for k in range(0, n, 2):
         pieces[k + CORE] = swapped(pieces[k], CORE)
     return [pieces[k] for k in range(n)]
@@ -375,7 +376,7 @@
     for iteration in range(ITERS):
         pieces = gathered(n, vector, held if iteration == 0 else None)
         vector = pieces[0]
-        square, sums, parts = scattered(n, tables, pieces)
+        square, sums, parts = scattered(n, tables, pieces, iteration == ITERS - 1)
         arrays = (*sums, square, vector, precond, *parts)
         if iteration < ITERS - 1:
             vector = local(step_kernel, "step", block, (), arrays)

time: 121 us -> 123 us (1.017)
  starting transfers between devices: 38.6 us -> 48.2 us
  waiting for transfers between devices: 51.9 us -> 44.1 us
    ppermute x48, starting transfers between devices: 38.6 us -> 48.2 us  [swapped(): return lax.ppermute(x, 'term', [(i, i ^ k) for i in range(n)])]
    ppermute x48, waiting for transfers between devices: 51.9 us -> 44.1 us  [swapped(): return lax.ppermute(x, 'term', [(i, i ^ k) for i in range(n)])]
  transfers between devices with their start and end apart: 48 -> 48, of which waited for: 27 -> 19; matrix products, arithmetic and copies ran while one was open for 0% -> 0% of each run, Pallas kernels for 2% -> 2%
where the time goes in v10:
time: 123 us
  starting transfers between devices  48.2 us (39%)
  waiting for transfers between devices  44.1 us (36%)
  Pallas kernels  18.2 us (15%)
  blocking collectives  10.3 us (8%)
  between operations  1.42 us (1%)
    ppermute x48, starting transfers between devices, swapped(): return lax.ppermute(x, 'term', [(i, i ^ k) for i in range(n)])  48.2 us
    ppermute x48, waiting for transfers between devices, swapped(): return lax.ppermute(x, 'term', [(i, i ^ k) for i in range(n)])  44.1 us
    pallas_call x2, Pallas kernels, apply(): pl.pallas_call(functools.partial(apply_kernel, n, npairs, over_rows, rows...  12 us
    all_to_all x1, blocking collectives, shards(): lax.all_to_all(jnp.broadcast_to(partial[None], (n, 8, width)), 'term', sp...  10.3 us
    pallas_call x5, Pallas kernels, local(): pl.pallas_call(kernel, out_shape=out_shape, in_specs=[SMEM] * len(scalars...  3.43 us
    pallas_call x1, Pallas kernels, prep(): pl.pallas_call(functools.partial(prep_kernel, n, terms * n + 1), out_shap...  2.76 us
  transfers between devices with their start and end apart: 48, of which 19 were waited for; matrix products, arithmetic and copies ran while one was open for 0% of the time, Pallas kernels for 2%

profile of v10, /device:TPU:0, one launch (start us, length us, event | category | flops | bytes accessed | tf_op | source)
XLA Modules:
  0.0 122.8 jit_solution(14201313084375142849)
XLA Ops:
  0.6 5.1 %collective-permute-start = (f32[2,128,128]{2,1,0:T(8,128)}, f32[2,128,128]{2,1,0:T(8,128)S(1)}, u32[]{:S(2)}, u32[]{:S(2)}) collective-permute-start(f32[2,128,128]{2,1,0:T(8,128)} %vector_in.1), channel_id=1, source_target_pairs={{0,12},{1,13},{2,14},{3,15},{4,8},{5,9},{6,10},{7,11},{8,4},{9,5},... | collective-permute-start | bytes 393224 | tf_op jit(solution)/shard_map/ppermute | solution.py:242
  5.7 1.5 %collective-permute-start.3 = (f32[2,128,128]{2,1,0:T(8,128)}, f32[2,128,128]{2,1,0:T(8,128)S(1)}, u32[]{:S(2)}, u32[]{:S(2)}) collective-permute-start(f32[2,128,128]{2,1,0:T(8,128)} %vector_in.1), channel_id=1, source_target_pairs={{0,2},{1,3},{2,0},{3,1},{4,6},{5,7},{6,4},{7,5},{8,10},{9,11},{10,... | collective-permute-start | bytes 393224 | tf_op jit(solution)/shard_map/ppermute | solution.py:242
  7.3 0.8 collective-permute-start.5
  8.1 1.9 %collective-permute-done.refs_12_ = f32[2,128,128]{2,1,0:T(8,128)S(1)} collective-permute-done((f32[2,128,128]{2,1,0:T(8,128)}, f32[2,128,128]{2,1,0:T(8,128)S(1)}, u32[]{:S(2)}, u32[]{:S(2)}) %collective-permute-start) | collective-permute-done | bytes 131104 | tf_op jit(solution)/shard_map/ppermute | solution.py:242
  10.0 2.1 %collective-permute-start.1 = (f32[2,128,128]{2,1,0:T(8,128)S(1)}, f32[2,128,128]{2,1,0:T(8,128)S(1)}, u32[]{:S(2)}, u32[]{:S(2)}) collective-permute-start(f32[2,128,128]{2,1,0:T(8,128)S(1)} %collective-permute-done.refs_12_), channel_id=1, source_target_pairs={{0,2},{1,3},{2,0},{3,1},{4,6},{5,7},{6,4},{7,5},{8,10},{9,11},{10,... | collective-permute-start | bytes 393224 | tf_op jit(solution)/shard_map/ppermute | solution.py:242
  12.1 5.2 %collective-permute-start.7 = (f32[2,128,128]{2,1,0:T(8,128)S(1)}, f32[2,128,128]{2,1,0:T(8,128)S(1)}, u32[]{:S(2)}, u32[]{:S(2)}) collective-permute-start(f32[2,128,128]{2,1,0:T(8,128)S(1)} %collective-permute-done.3.refs_2_), channel_id=1, source_target_pairs={{0,4},{1,5},{2,6},{3,7},{4,0},{5,1},{6,2},{7,3},{8,12},{9,13},{10,... | collective-permute-start | bytes 393224 | tf_op jit(solution)/shard_map/ppermute | solution.py:242
  17.3 0.5 collective-permute-start.13
  17.8 0.9 collective-permute-start.11
  18.7 0.2 collective-permute-start.10
  19.6 0.6 copy.12
  20.2 2.8 %prep.1 = (bf16[8,128,512]{2,1,0:T(8,128)(2,1)S(1)}, bf16[2048,256]{1,0:T(8,128)(2,1)S(1)}, s32[721]{0:T(1024)S(1)}, f32[2,128,128]{2,1,0:T(8,128)S(1)}) custom-call(s32[1]{0:T(128)} %bitcast.me_ref, s32[16,16]{1,0:T(8,128)} %fetch_in.1, s32[16,16]{1,0:T(8,128)} %store_in.1, s32[384]{0:T(512)} %bitcast.8, s32[1]{0:T(128)S(6)} %copy.13.live_in, ...), custom_call_target="tpu_custom_call" | custom-call | tf_op jit(solution)/shard_map/prep/pallas_call | solution.py:132
  22.9 0.7 collective-permute-start.6
  23.7 0.4 collective-permute-start.8
  24.2 0.4 collective-permute-start.2
  24.6 0.5 collective-permute-done.8.refs_7_
  25.1 0.3 collective-permute-done.12.refs_11_
  25.5 0.2 collective-permute-done.2.refs_1_
  25.7 5.9 %apply.2 = (f32[640,128]{1,0:T(8,128)S(1)}, f32[648,128]{1,0:T(8,128)S(1)}, f32[264,128]{1,0:T(8,128)S(1)}, f32[264,128]{1,0:T(8,128)S(1)}, f32[128,128]{1,0:T(8...) custom-call(s32[721]{0:T(1024)S(1)} %get-tuple-element.35.table_ref, ...), custom_call_target="tpu_custom_call" | custom-call | tf_op jit(solution)/shard_map/apply/pallas_call | solution.py:216
  31.6 0.4 collective-permute-start.15
  32.0 2.3 %collective-permute-start.16 = (f32[264,128]{1,0:T(8,128)S(1)}, f32[264,128]{1,0:T(8,128)S(1)}, u32[]{:S(2)}, u32[]{:S(2)}) collective-permute-start(f32[264,128]{1,0:T(8,128)S(1)} %get-tuple-element.43), channel_id=1, source_target_pairs={{0,2},{1,3},{2,0},{3,1},{4,6},{5,7},{6,4},{7,5},{8,10},{9,11},{10,... | collective-permute-start | bytes 405512 | tf_op jit(solution)/shard_map/ppermute | solution.py:242
  34.3 2.2 %collective-permute-start.18 = (f32[128,128]{1,0:T(8,128)S(1)}, f32[128,128]{1,0:T(8,128)S(1)}, u32[]{:S(2)}, u32[]{:S(2)}) collective-permute-start(f32[128,128]{1,0:T(8,128)S(1)} %get-tuple-element.45), channel_id=1, source_target_pairs={{0,4},{1,5},{2,6},{3,7},{4,0},{5,1},{6,2},{7,3},{8,12},{9,13},{10,... | collective-permute-start | bytes 196616 | tf_op jit(solution)/shard_map/ppermute | solution.py:242
  36.6 2.6 %collective-permute-done.18.column_ref = f32[128,128]{1,0:T(8,128)S(1)} collective-permute-done((f32[128,128]{1,0:T(8,128)S(1)}, f32[128,128]{1,0:T(8,128)S(1)}, u32[]{:S(2)}, u32[]{:S(2)}) %collective-permute-start.18) | collective-permute-done | bytes 65568 | tf_op jit(solution)/shard_map/ppermute | solution.py:242
  39.2 1.6 %collective-permute-done.19.column_far_ref = f32[128,128]{1,0:T(8,128)S(1)} collective-permute-done((f32[128,128]{1,0:T(8,128)S(1)}, f32[128,128]{1,0:T(8,128)S(1)}, u32[]{:S(2)}, u32[]{:S(2)}) %collective-permute-start.19) | collective-permute-done | bytes 65568 | tf_op jit(solution)/shard_map/ppermute | solution.py:242
  40.8 0.7 fold.2
  41.5 4.6 %collective-permute-start.21 = (f32[264,128]{1,0:T(8,128)S(1)}, f32[264,128]{1,0:T(8,128)S(1)}, u32[]{:S(2)}, u32[]{:S(2)}) collective-permute-start(f32[264,128]{1,0:T(8,128)S(1)} %get-tuple-element.51), channel_id=1, source_target_pairs={{0,12},{1,13},{2,14},{3,15},{4,8},{5,9},{6,10},{7,11},{8,4},{9,5},... | collective-permute-start | bytes 405512 | tf_op jit(solution)/shard_map/ppermute | solution.py:242
  46.1 0.5 collective-permute-start.22
  46.6 0.5 collective-permute-start.23
  47.1 1.4 %collective-permute-start.20 = (f32[2,128,128]{2,1,0:T(8,128)S(1)}, f32[2,128,128]{2,1,0:T(8,128)S(1)}, u32[]{:S(2)}, u32[]{:S(2)}) collective-permute-start(f32[2,128,128]{2,1,0:T(8,128)S(1)} %get-tuple-element.48), channel_id=1, source_target_pairs={{0,2},{1,3},{2,0},{3,1},{4,6},{5,7},{6,4},{7,5},{8,10},{9,11},{10,... | collective-permute-start | bytes 393224 | tf_op jit(solution)/shard_map/ppermute | solution.py:242
  48.5 3.7 %collective-permute-done.20.step_ref = f32[2,128,128]{2,1,0:T(8,128)S(1)} collective-permute-done((f32[2,128,128]{2,1,0:T(8,128)S(1)}, f32[2,128,128]{2,1,0:T(8,128)S(1)}, u32[]{:S(2)}, u32[]{:S(2)}) %collective-permute-start.20) | collective-permute-done | bytes 131104 | tf_op jit(solution)/shard_map/ppermute | solution.py:242
  52.2 6.4 %collective-permute-done.22.refs_2_ = f32[264,128]{1,0:T(8,128)S(1)} collective-permute-done((f32[264,128]{1,0:T(8,128)S(1)}, f32[264,128]{1,0:T(8,128)S(1)}, u32[]{:S(2)}, u32[]{:S(2)}) %collective-permute-start.22) | collective-permute-done | bytes 135200 | tf_op jit(solution)/shard_map/ppermute | solution.py:242
  58.6 0.2 step.1.refs_0_.vector_ref
  58.8 3.3 %collective-permute-start.35 = (f32[2,128,128]{2,1,0:T(8,128)S(1)}, f32[2,128,128]{2,1,0:T(8,128)S(1)}, u32[]{:S(2)}, u32[]{:S(2)}) collective-permute-start(f32[2,128,128]{2,1,0:T(8,128)S(1)} %step.1.refs_0_.vector_ref), channel_id=1, source_target_pairs={{0,12},{1,13},{2,14},{3,15},{4,8},{5,9},{6,10},{7,11},{8,4},{9,5},... | collective-permute-start | bytes 393224 | tf_op jit(solution)/shard_map/ppermute | solution.py:242
  62.2 1.1 collective-permute-start.27
  63.3 1.2 %collective-permute-start.25 = (f32[2,128,128]{2,1,0:T(8,128)S(1)}, f32[2,128,128]{2,1,0:T(8,128)S(1)}, u32[]{:S(2)}, u32[]{:S(2)}) collective-permute-start(f32[2,128,128]{2,1,0:T(8,128)S(1)} %step.1.refs_0_.vector_ref), channel_id=1, source_target_pairs={{0,2},{1,3},{2,0},{3,1},{4,6},{5,7},{6,4},{7,5},{8,10},{9,11},{10,... | collective-permute-start | bytes 393224 | tf_op jit(solution)/shard_map/ppermute | solution.py:242
  64.5 2.6 %collective-permute-done.35.refs_12_ = f32[2,128,128]{2,1,0:T(8,128)S(1)} collective-permute-done((f32[2,128,128]{2,1,0:T(8,128)S(1)}, f32[2,128,128]{2,1,0:T(8,128)S(1)}, u32[]{:S(2)}, u32[]{:S(2)}) %collective-permute-start.35) | collective-permute-done | bytes 131104 | tf_op jit(solution)/shard_map/ppermute | solution.py:242
  67.1 1.2 %collective-permute-start.37 = (f32[2,128,128]{2,1,0:T(8,128)S(1)}, f32[2,128,128]{2,1,0:T(8,128)S(1)}, u32[]{:S(2)}, u32[]{:S(2)}) collective-permute-start(f32[2,128,128]{2,1,0:T(8,128)S(1)} %collective-permute-done.35.refs_12_), channel_id=1, source_target_pairs={{0,2},{1,3},{2,0},{3,1},{4,6},{5,7},{6,4},{7,5},{8,10},{9,11},{10,... | collective-permute-start | bytes 393224 | tf_op jit(solution)/shard_map/ppermute | solution.py:242
  68.4 4.0 %collective-permute-done.31.refs_8_ = f32[2,128,128]{2,1,0:T(8,128)S(1)} collective-permute-done((f32[2,128,128]{2,1,0:T(8,128)S(1)}, f32[2,128,128]{2,1,0:T(8,128)S(1)}, u32[]{:S(2)}, u32[]{:S(2)}) %collective-permute-start.31) | collective-permute-done | bytes 131104 | tf_op jit(solution)/shard_map/ppermute | solution.py:242
  72.4 1.8 %collective-permute-start.33 = (f32[2,128,128]{2,1,0:T(8,128)S(1)}, f32[2,128,128]{2,1,0:T(8,128)S(1)}, u32[]{:S(2)}, u32[]{:S(2)}) collective-permute-start(f32[2,128,128]{2,1,0:T(8,128)S(1)} %collective-permute-done.31.refs_8_), channel_id=1, source_target_pairs={{0,2},{1,3},{2,0},{3,1},{4,6},{5,7},{6,4},{7,5},{8,10},{9,11},{10,... | collective-permute-start | bytes 393224 | tf_op jit(solution)/shard_map/ppermute | solution.py:242
  74.2 0.2 collective-permute-start.32
  74.4 0.5 collective-permute-start.29
  75.1 0.3 collective-permute-start.28
  75.5 2.9 %collective-permute-done.33.refs_10_ = f32[2,128,128]{2,1,0:T(8,128)S(1)} collective-permute-done((f32[2,128,128]{2,1,0:T(8,128)S(1)}, f32[2,128,128]{2,1,0:T(8,128)S(1)}, u32[]{:S(2)}, u32[]{:S(2)}) %collective-permute-start.33) | collective-permute-done | bytes 131104 | tf_op jit(solution)/shard_map/ppermute | solution.py:242
  78.4 0.5 collective-permute-start.34
  78.9 1.2 %collective-permute-done.29.refs_6_ = f32[2,128,128]{2,1,0:T(8,128)S(1)} collective-permute-done((f32[2,128,128]{2,1,0:T(8,128)S(1)}, f32[2,128,128]{2,1,0:T(8,128)S(1)}, u32[]{:S(2)}, u32[]{:S(2)}) %collective-permute-start.29) | collective-permute-done | bytes 131104 | tf_op jit(solution)/shard_map/ppermute | solution.py:242
  80.2 1.3 %collective-permute-done.30.refs_7_ = f32[2,128,128]{2,1,0:T(8,128)S(1)} collective-permute-done((f32[2,128,128]{2,1,0:T(8,128)S(1)}, f32[2,128,128]{2,1,0:T(8,128)S(1)}, u32[]{:S(2)}, u32[]{:S(2)}) %collective-permute-start.30) | collective-permute-done | bytes 131104 | tf_op jit(solution)/shard_map/ppermute | solution.py:242
  81.5 6.1 %apply.3 = (f32[640,128]{1,0:T(8,128)S(1)}, f32[648,128]{1,0:T(8,128)S(1)}, f32[264,128]{1,0:T(8,128)S(1)}, f32[264,128]{1,0:T(8,128)S(1)}, f32[128,128]{1,0:T(8...) custom-call(s32[721]{0:T(1024)S(1)} %get-tuple-element.35.table_ref, ...), custom_call_target="tpu_custom_call" | custom-call | tf_op jit(solution)/shard_map/apply/pallas_call | solution.py:216
  87.6 0.3 collective-permute-start.39
  87.8 0.7 collective-permute-start.40
  88.5 1.0 collective-permute-start.41
  89.5 0.8 collective-permute-start.42
  90.3 1.0 collective-permute-start.43
  91.3 3.1 %collective-permute-done.42.column_ref = f32[128,128]{1,0:T(8,128)S(1)} collective-permute-done((f32[128,128]{1,0:T(8,128)S(1)}, f32[128,128]{1,0:T(8,128)S(1)}, u32[]{:S(2)}, u32[]{:S(2)}) %collective-permute-start.42) | collective-permute-done | bytes 65568 | tf_op jit(solution)/shard_map/ppermute | solution.py:242
  94.4 0.6 collective-permute-done.43.column_far_ref
  95.0 1.0 collective-permute-done.41.row_far_ref
  95.9 0.7 fold.3
  96.7 0.3 collective-permute-start.45
  97.0 3.1 %collective-permute-start.46 = (f32[264,128]{1,0:T(8,128)S(1)}, f32[264,128]{1,0:T(8,128)S(1)}, u32[]{:S(2)}, u32[]{:S(2)}) collective-permute-start(f32[264,128]{1,0:T(8,128)S(1)} %get-tuple-element.64), channel_id=1, source_target_pairs={{0,12},{1,13},{2,14},{3,15},{4,8},{5,9},{6,10},{7,11},{8,4},{9,5},... | collective-permute-start | bytes 405512 | tf_op jit(solution)/shard_map/ppermute | solution.py:242
  100.2 0.4 collective-permute-start.44
  100.7 4.6 %collective-permute-done.44.step_ref = f32[2,128,128]{2,1,0:T(8,128)S(1)} collective-permute-done((f32[2,128,128]{2,1,0:T(8,128)S(1)}, f32[2,128,128]{2,1,0:T(8,128)S(1)}, u32[]{:S(2)}, u32[]{:S(2)}) %collective-permute-start.44) | collective-permute-done | bytes 131104 | tf_op jit(solution)/shard_map/ppermute | solution.py:242
  105.2 4.5 %collective-permute-done.45.refs_1_ = f32[264,128]{1,0:T(8,128)S(1)} collective-permute-done((f32[264,128]{1,0:T(8,128)S(1)}, f32[264,128]{1,0:T(8,128)S(1)}, u32[]{:S(2)}, u32[]{:S(2)}) %collective-permute-start.45) | collective-permute-done | bytes 135200 | tf_op jit(solution)/shard_map/ppermute | solution.py:242
  109.7 1.0 collective-permute-done.47.refs_3_
  110.7 0.9 last.1
  111.6 10.3 %all_to_all.5.tiles_ref = f32[16,8,128]{2,1,0:T(8,128)S(1)} all-to-all(f32[16,8,128]{2,1,0:T(8,128)S(1)} %broadcast_in_dim.2), channel_id=1, replica_groups=mesh['group'=2,'term'=16] {'term'}, dimensions={0} | all-to-all | bytes 131072 | tf_op jit(solution)/shard_map/all_to_all | solution.py:385
  121.9 0.9 norm.1
  (47 shorter events, 0.6 us)
Async XLA Ops:
  0.6 9.3 %collective-permute-start = (f32[2,128,128]{2,1,0:T(8,128)}, f32[2,128,128]{2,1,0:T(8,128)S(1)}, u32[]{:S(2)}, u32[]{:S(2)}) collective-permute-start(f32[2,128,128]{2,1,0:T(8,128)} %vector_in.1), channel_id=1, source_target_pairs={{0,12},{1,13},{2,14},{3,15},{4,8},{5,9},{6,10},{7,11},{8,4},{9,5},... | collective-permute-start | bytes 393224 | tf_op jit(solution)/shard_map/ppermute | solution.py:242
  5.7 6.4 %collective-permute-start.3 = (f32[2,128,128]{2,1,0:T(8,128)}, f32[2,128,128]{2,1,0:T(8,128)S(1)}, u32[]{:S(2)}, u32[]{:S(2)}) collective-permute-start(f32[2,128,128]{2,1,0:T(8,128)} %vector_in.1), channel_id=1, source_target_pairs={{0,2},{1,3},{2,0},{3,1},{4,6},{5,7},{6,4},{7,5},{8,10},{9,11},{10,... | collective-permute-start | bytes 393224 | tf_op jit(solution)/shard_map/ppermute | solution.py:242
  7.3 10.0 %collective-permute-start.9 = (f32[2,128,128]{2,1,0:T(8,128)}, f32[2,128,128]{2,1,0:T(8,128)S(1)}, u32[]{:S(2)}, u32[]{:S(2)}) collective-permute-start(f32[2,128,128]{2,1,0:T(8,128)} %vector_in.1), channel_id=1, source_target_pairs={{0,8},{1,9},{2,10},{3,11},{4,12},{5,13},{6,14},{7,15},{8,0},{9,1},... | collective-permute-start | bytes 393224 | tf_op jit(solution)/shard_map/ppermute | solution.py:242
  7.3 10.5 %collective-permute-start.5 = (f32[2,128,128]{2,1,0:T(8,128)}, f32[2,128,128]{2,1,0:T(8,128)S(1)}, u32[]{:S(2)}, u32[]{:S(2)}) collective-permute-start(f32[2,128,128]{2,1,0:T(8,128)} %vector_in.1), channel_id=1, source_target_pairs={{0,4},{1,5},{2,6},{3,7},{4,0},{5,1},{6,2},{7,3},{8,12},{9,13},{10,... | collective-permute-start | bytes 393224 | tf_op jit(solution)/shard_map/ppermute | solution.py:242
  10.0 8.7 %collective-permute-start.1 = (f32[2,128,128]{2,1,0:T(8,128)S(1)}, f32[2,128,128]{2,1,0:T(8,128)S(1)}, u32[]{:S(2)}, u32[]{:S(2)}) collective-permute-start(f32[2,128,128]{2,1,0:T(8,128)S(1)} %collective-permute-done.refs_12_), channel_id=1, source_target_pairs={{0,2},{1,3},{2,0},{3,1},{4,6},{5,7},{6,4},{7,5},{8,10},{9,11},{10,... | collective-permute-start | bytes 393224 | tf_op jit(solution)/shard_map/ppermute | solution.py:242
  12.1 10.8 %collective-permute-start.7 = (f32[2,128,128]{2,1,0:T(8,128)S(1)}, f32[2,128,128]{2,1,0:T(8,128)S(1)}, u32[]{:S(2)}, u32[]{:S(2)}) collective-permute-start(f32[2,128,128]{2,1,0:T(8,128)S(1)} %collective-permute-done.3.refs_2_), channel_id=1, source_target_pairs={{0,4},{1,5},{2,6},{3,7},{4,0},{5,1},{6,2},{7,3},{8,12},{9,13},{10,... | collective-permute-start | bytes 393224 | tf_op jit(solution)/shard_map/ppermute | solution.py:242
  17.3 6.3 %collective-permute-start.4 = (f32[2,128,128]{2,1,0:T(8,128)S(1)}, f32[2,128,128]{2,1,0:T(8,128)S(1)}, u32[]{:S(2)}, u32[]{:S(2)}) collective-permute-start(f32[2,128,128]{2,1,0:T(8,128)S(1)} %collective-permute-done.3.refs_2_), channel_id=1, source_target_pairs={{0,1},{1,0},{2,3},{3,2},{4,5},{5,4},{6,7},{7,6},{8,9},{9,8},{10,11... | collective-permute-start | bytes 393224 | tf_op jit(solution)/shard_map/ppermute | solution.py:242
  17.3 6.4 %collective-permute-start.13 = (f32[2,128,128]{2,1,0:T(8,128)S(1)}, f32[2,128,128]{2,1,0:T(8,128)S(1)}, u32[]{:S(2)}, u32[]{:S(2)}) collective-permute-start(f32[2,128,128]{2,1,0:T(8,128)S(1)} %collective-permute-done.refs_12_), channel_id=1, source_target_pairs={{0,1},{1,0},{2,3},{3,2},{4,5},{5,4},{6,7},{7,6},{8,9},{9,8},{10,11... | collective-permute-start | bytes 393224 | tf_op jit(solution)/shard_map/ppermute | solution.py:242
  17.8 6.3 %collective-permute-start.11 = (f32[2,128,128]{2,1,0:T(8,128)S(1)}, f32[2,128,128]{2,1,0:T(8,128)S(1)}, u32[]{:S(2)}, u32[]{:S(2)}) collective-permute-start(f32[2,128,128]{2,1,0:T(8,128)S(1)} %collective-permute-done.9.refs_8_), channel_id=1, source_target_pairs={{0,2},{1,3},{2,0},{3,1},{4,6},{5,7},{6,4},{7,5},{8,10},{9,11},{10,... | collective-permute-start | bytes 393224 | tf_op jit(solution)/shard_map/ppermute | solution.py:242
  18.7 5.6 %collective-permute-start.10 = (f32[2,128,128]{2,1,0:T(8,128)S(1)}, f32[2,128,128]{2,1,0:T(8,128)S(1)}, u32[]{:S(2)}, u32[]{:S(2)}) collective-permute-start(f32[2,128,128]{2,1,0:T(8,128)S(1)} %collective-permute-done.9.refs_8_), channel_id=1, source_target_pairs={{0,1},{1,0},{2,3},{3,2},{4,5},{5,4},{6,7},{7,6},{8,9},{9,8},{10,11... | collective-permute-start | bytes 393224 | tf_op jit(solution)/shard_map/ppermute | solution.py:242
  18.9 0.7 copy-start.1
  22.9 1.7 %collective-permute-start.6 = (f32[2,128,128]{2,1,0:T(8,128)S(1)}, f32[2,128,128]{2,1,0:T(8,128)S(1)}, u32[]{:S(2)}, u32[]{:S(2)}) collective-permute-start(f32[2,128,128]{2,1,0:T(8,128)S(1)} %collective-permute-done.5.refs_4_), channel_id=1, source_target_pairs={{0,1},{1,0},{2,3},{3,2},{4,5},{5,4},{6,7},{7,6},{8,9},{9,8},{10,11... | collective-permute-start | bytes 393224 | tf_op jit(solution)/shard_map/ppermute | solution.py:242
  23.6 1.9 %collective-permute-start.14 = (f32[2,128,128]{2,1,0:T(8,128)S(1)}, f32[2,128,128]{2,1,0:T(8,128)S(1)}, u32[]{:S(2)}, u32[]{:S(2)}) collective-permute-start(f32[2,128,128]{2,1,0:T(8,128)S(1)} %collective-permute-done.1.refs_14_), channel_id=1, source_target_pairs={{0,1},{1,0},{2,3},{3,2},{4,5},{5,4},{6,7},{7,6},{8,9},{9,8},{10,11... | collective-permute-start | bytes 393224 | tf_op jit(solution)/shard_map/ppermute | solution.py:242
  23.7 1.4 %collective-permute-start.8 = (f32[2,128,128]{2,1,0:T(8,128)S(1)}, f32[2,128,128]{2,1,0:T(8,128)S(1)}, u32[]{:S(2)}, u32[]{:S(2)}) collective-permute-start(f32[2,128,128]{2,1,0:T(8,128)S(1)} %collective-permute-done.7.refs_6_), channel_id=1, source_target_pairs={{0,1},{1,0},{2,3},{3,2},{4,5},{5,4},{6,7},{7,6},{8,9},{9,8},{10,11... | collective-permute-start | bytes 393224 | tf_op jit(solution)/shard_map/ppermute | solution.py:242
  24.1 1.3 %collective-permute-start.12 = (f32[2,128,128]{2,1,0:T(8,128)S(1)}, f32[2,128,128]{2,1,0:T(8,128)S(1)}, u32[]{:S(2)}, u32[]{:S(2)}) collective-permute-start(f32[2,128,128]{2,1,0:T(8,128)S(1)} %collective-permute-done.11.refs_10_), channel_id=1, source_target_pairs={{0,1},{1,0},{2,3},{3,2},{4,5},{5,4},{6,7},{7,6},{8,9},{9,8},{10,11... | collective-permute-start | bytes 393224 | tf_op jit(solution)/shard_map/ppermute | solution.py:242
  24.2 1.4 %collective-permute-start.2 = (f32[2,128,128]{2,1,0:T(8,128)S(1)}, f32[2,128,128]{2,1,0:T(8,128)S(1)}, u32[]{:S(2)}, u32[]{:S(2)}) collective-permute-start(f32[2,128,128]{2,1,0:T(8,128)S(1)} %get-tuple-element.39.refs_0_.vector_ref), channel_id=1, source_target_pairs={{0,1},{1,0},{2,3},{3,2},{4,5},{5,4},{6,7},{7,6},{8,9},{9,8},{10,11... | collective-permute-start | bytes 393224 | tf_op jit(solution)/shard_map/ppermute | solution.py:242
  31.6 9.2 %collective-permute-start.15 = (f32[648,128]{1,0:T(8,128)S(1)}, f32[648,128]{1,0:T(8,128)S(1)}, u32[]{:S(2)}, u32[]{:S(2)}) collective-permute-start(f32[648,128]{1,0:T(8,128)S(1)} %get-tuple-element.42.far_in), channel_id=1, source_target_pairs={{0,1},{1,0},{2,3},{3,2},{4,5},{5,4},{6,7},{7,6},{8,9},{9,8},{10,11... | collective-permute-start | bytes 995336 | tf_op jit(solution)/shard_map/ppermute | solution.py:242
  32.0 8.7 %collective-permute-start.16 = (f32[264,128]{1,0:T(8,128)S(1)}, f32[264,128]{1,0:T(8,128)S(1)}, u32[]{:S(2)}, u32[]{:S(2)}) collective-permute-start(f32[264,128]{1,0:T(8,128)S(1)} %get-tuple-element.43), channel_id=1, source_target_pairs={{0,2},{1,3},{2,0},{3,1},{4,6},{5,7},{6,4},{7,5},{8,10},{9,11},{10,... | collective-permute-start | bytes 405512 | tf_op jit(solution)/shard_map/ppermute | solution.py:242
  34.3 6.4 %collective-permute-start.17 = (f32[264,128]{1,0:T(8,128)S(1)}, f32[264,128]{1,0:T(8,128)S(1)}, u32[]{:S(2)}, u32[]{:S(2)}) collective-permute-start(f32[264,128]{1,0:T(8,128)S(1)} %get-tuple-element.44), channel_id=1, source_target_pairs={{0,3},{1,2},{2,1},{3,0},{4,7},{5,6},{6,5},{7,4},{8,11},{9,10},{10,... | collective-permute-start | bytes 405512 | tf_op jit(solution)/shard_map/ppermute | solution.py:242
  34.3 4.8 %collective-permute-start.18 = (f32[128,128]{1,0:T(8,128)S(1)}, f32[128,128]{1,0:T(8,128)S(1)}, u32[]{:S(2)}, u32[]{:S(2)}) collective-permute-start(f32[128,128]{1,0:T(8,128)S(1)} %get-tuple-element.45), channel_id=1, source_target_pairs={{0,4},{1,5},{2,6},{3,7},{4,0},{5,1},{6,2},{7,3},{8,12},{9,13},{10,... | collective-permute-start | bytes 196616 | tf_op jit(solution)/shard_map/ppermute | solution.py:242
  36.6 4.2 %collective-permute-start.19 = (f32[128,128]{1,0:T(8,128)S(1)}, f32[128,128]{1,0:T(8,128)S(1)}, u32[]{:S(2)}, u32[]{:S(2)}) collective-permute-start(f32[128,128]{1,0:T(8,128)S(1)} %get-tuple-element.46), channel_id=1, source_target_pairs={{0,5},{1,4},{2,7},{3,6},{4,1},{5,0},{6,3},{7,2},{8,13},{9,12},{10,... | collective-permute-start | bytes 196616 | tf_op jit(solution)/shard_map/ppermute | solution.py:242
  40.7 17.9 %copy-start = (f32[2,128,128]{2,1,0:T(8,128)S(1)}, f32[2,128,128]{2,1,0:T(8,128)}, u32[]{:S(2)}) copy-start(f32[2,128,128]{2,1,0:T(8,128)} %precond_ref.3) | copy-start | bytes 393220
  41.5 10.7 %collective-permute-start.21 = (f32[264,128]{1,0:T(8,128)S(1)}, f32[264,128]{1,0:T(8,128)S(1)}, u32[]{:S(2)}, u32[]{:S(2)}) collective-permute-start(f32[264,128]{1,0:T(8,128)S(1)} %get-tuple-element.51), channel_id=1, source_target_pairs={{0,12},{1,13},{2,14},{3,15},{4,8},{5,9},{6,10},{7,11},{8,4},{9,5},... | collective-permute-start | bytes 405512 | tf_op jit(solution)/shard_map/ppermute | solution.py:242
  46.1 12.6 %collective-permute-start.22 = (f32[264,128]{1,0:T(8,128)S(1)}, f32[264,128]{1,0:T(8,128)S(1)}, u32[]{:S(2)}, u32[]{:S(2)}) collective-permute-start(f32[264,128]{1,0:T(8,128)S(1)} %get-tuple-element.52), channel_id=1, source_target_pairs={{0,8},{1,9},{2,10},{3,11},{4,12},{5,13},{6,14},{7,15},{8,0},{9,1},... | collective-permute-start | bytes 405512 | tf_op jit(solution)/shard_map/ppermute | solution.py:242
  46.6 12.0 %collective-permute-start.23 = (f32[264,128]{1,0:T(8,128)S(1)}, f32[264,128]{1,0:T(8,128)S(1)}, u32[]{:S(2)}, u32[]{:S(2)}) collective-permute-start(f32[264,128]{1,0:T(8,128)S(1)} %get-tuple-element.50.refs_0_), channel_id=1, source_target_pairs={{0,4},{1,5},{2,6},{3,7},{4,0},{5,1},{6,2},{7,3},{8,12},{9,13},{10,... | collective-permute-start | bytes 405512 | tf_op jit(solution)/shard_map/ppermute | solution.py:242
  47.1 5.2 %collective-permute-start.20 = (f32[2,128,128]{2,1,0:T(8,128)S(1)}, f32[2,128,128]{2,1,0:T(8,128)S(1)}, u32[]{:S(2)}, u32[]{:S(2)}) collective-permute-start(f32[2,128,128]{2,1,0:T(8,128)S(1)} %get-tuple-element.48), channel_id=1, source_target_pairs={{0,2},{1,3},{2,0},{3,1},{4,6},{5,7},{6,4},{7,5},{8,10},{9,11},{10,... | collective-permute-start | bytes 393224 | tf_op jit(solution)/shard_map/ppermute | solution.py:242
  58.8 8.3 %collective-permute-start.35 = (f32[2,128,128]{2,1,0:T(8,128)S(1)}, f32[2,128,128]{2,1,0:T(8,128)S(1)}, u32[]{:S(2)}, u32[]{:S(2)}) collective-permute-start(f32[2,128,128]{2,1,0:T(8,128)S(1)} %step.1.refs_0_.vector_ref), channel_id=1, source_target_pairs={{0,12},{1,13},{2,14},{3,15},{4,8},{5,9},{6,10},{7,11},{8,4},{9,5},... | collective-permute-start | bytes 393224 | tf_op jit(solution)/shard_map/ppermute | solution.py:242
  62.2 10.3 %collective-permute-start.31 = (f32[2,128,128]{2,1,0:T(8,128)S(1)}, f32[2,128,128]{2,1,0:T(8,128)S(1)}, u32[]{:S(2)}, u32[]{:S(2)}) collective-permute-start(f32[2,128,128]{2,1,0:T(8,128)S(1)} %step.1.refs_0_.vector_ref), channel_id=1, source_target_pairs={{0,8},{1,9},{2,10},{3,11},{4,12},{5,13},{6,14},{7,15},{8,0},{9,1},... | collective-permute-start | bytes 393224 | tf_op jit(solution)/shard_map/ppermute | solution.py:242
  62.2 10.3 %collective-permute-start.27 = (f32[2,128,128]{2,1,0:T(8,128)S(1)}, f32[2,128,128]{2,1,0:T(8,128)S(1)}, u32[]{:S(2)}, u32[]{:S(2)}) collective-permute-start(f32[2,128,128]{2,1,0:T(8,128)S(1)} %step.1.refs_0_.vector_ref), channel_id=1, source_target_pairs={{0,4},{1,5},{2,6},{3,7},{4,0},{5,1},{6,2},{7,3},{8,12},{9,13},{10,... | collective-permute-start | bytes 393224 | tf_op jit(solution)/shard_map/ppermute | solution.py:242
  63.3 10.9 %collective-permute-start.25 = (f32[2,128,128]{2,1,0:T(8,128)S(1)}, f32[2,128,128]{2,1,0:T(8,128)S(1)}, u32[]{:S(2)}, u32[]{:S(2)}) collective-permute-start(f32[2,128,128]{2,1,0:T(8,128)S(1)} %step.1.refs_0_.vector_ref), channel_id=1, source_target_pairs={{0,2},{1,3},{2,0},{3,1},{4,6},{5,7},{6,4},{7,5},{8,10},{9,11},{10,... | collective-permute-start | bytes 393224 | tf_op jit(solution)/shard_map/ppermute | solution.py:242
  64.5 9.9 %collective-permute-start.24 = (f32[2,128,128]{2,1,0:T(8,128)S(1)}, f32[2,128,128]{2,1,0:T(8,128)S(1)}, u32[]{:S(2)}, u32[]{:S(2)}) collective-permute-start(f32[2,128,128]{2,1,0:T(8,128)S(1)} %step.1.refs_0_.vector_ref), channel_id=1, source_target_pairs={{0,1},{1,0},{2,3},{3,2},{4,5},{5,4},{6,7},{7,6},{8,9},{9,8},{10,11... | collective-permute-start | bytes 393224 | tf_op jit(solution)/shard_map/ppermute | solution.py:242
  67.1 7.8 %collective-permute-start.37 = (f32[2,128,128]{2,1,0:T(8,128)S(1)}, f32[2,128,128]{2,1,0:T(8,128)S(1)}, u32[]{:S(2)}, u32[]{:S(2)}) collective-permute-start(f32[2,128,128]{2,1,0:T(8,128)S(1)} %collective-permute-done.35.refs_12_), channel_id=1, source_target_pairs={{0,2},{1,3},{2,0},{3,1},{4,6},{5,7},{6,4},{7,5},{8,10},{9,11},{10,... | collective-permute-start | bytes 393224 | tf_op jit(solution)/shard_map/ppermute | solution.py:242
  72.4 2.7 %collective-permute-start.36 = (f32[2,128,128]{2,1,0:T(8,128)S(1)}, f32[2,128,128]{2,1,0:T(8,128)S(1)}, u32[]{:S(2)}, u32[]{:S(2)}) collective-permute-start(f32[2,128,128]{2,1,0:T(8,128)S(1)} %collective-permute-done.35.refs_12_), channel_id=1, source_target_pairs={{0,1},{1,0},{2,3},{3,2},{4,5},{5,4},{6,7},{7,6},{8,9},{9,8},{10,11... | collective-permute-start | bytes 393224 | tf_op jit(solution)/shard_map/ppermute | solution.py:242
  72.4 6.0 %collective-permute-start.33 = (f32[2,128,128]{2,1,0:T(8,128)S(1)}, f32[2,128,128]{2,1,0:T(8,128)S(1)}, u32[]{:S(2)}, u32[]{:S(2)}) collective-permute-start(f32[2,128,128]{2,1,0:T(8,128)S(1)} %collective-permute-done.31.refs_8_), channel_id=1, source_target_pairs={{0,2},{1,3},{2,0},{3,1},{4,6},{5,7},{6,4},{7,5},{8,10},{9,11},{10,... | collective-permute-start | bytes 393224 | tf_op jit(solution)/shard_map/ppermute | solution.py:242
  74.2 4.2 %collective-permute-start.32 = (f32[2,128,128]{2,1,0:T(8,128)S(1)}, f32[2,128,128]{2,1,0:T(8,128)S(1)}, u32[]{:S(2)}, u32[]{:S(2)}) collective-permute-start(f32[2,128,128]{2,1,0:T(8,128)S(1)} %collective-permute-done.31.refs_8_), channel_id=1, source_target_pairs={{0,1},{1,0},{2,3},{3,2},{4,5},{5,4},{6,7},{7,6},{8,9},{9,8},{10,11... | collective-permute-start | bytes 393224 | tf_op jit(solution)/shard_map/ppermute | solution.py:242
  74.4 5.7 %collective-permute-start.29 = (f32[2,128,128]{2,1,0:T(8,128)S(1)}, f32[2,128,128]{2,1,0:T(8,128)S(1)}, u32[]{:S(2)}, u32[]{:S(2)}) collective-permute-start(f32[2,128,128]{2,1,0:T(8,128)S(1)} %collective-permute-done.25.refs_2_), channel_id=1, source_target_pairs={{0,4},{1,5},{2,6},{3,7},{4,0},{5,1},{6,2},{7,3},{8,12},{9,13},{10,... | collective-permute-start | bytes 393224 | tf_op jit(solution)/shard_map/ppermute | solution.py:242
  74.9 5.2 %collective-permute-start.26 = (f32[2,128,128]{2,1,0:T(8,128)S(1)}, f32[2,128,128]{2,1,0:T(8,128)S(1)}, u32[]{:S(2)}, u32[]{:S(2)}) collective-permute-start(f32[2,128,128]{2,1,0:T(8,128)S(1)} %collective-permute-done.25.refs_2_), channel_id=1, source_target_pairs={{0,1},{1,0},{2,3},{3,2},{4,5},{5,4},{6,7},{7,6},{8,9},{9,8},{10,11... | collective-permute-start | bytes 393224 | tf_op jit(solution)/shard_map/ppermute | solution.py:242
  75.1 5.0 %collective-permute-start.28 = (f32[2,128,128]{2,1,0:T(8,128)S(1)}, f32[2,128,128]{2,1,0:T(8,128)S(1)}, u32[]{:S(2)}, u32[]{:S(2)}) collective-permute-start(f32[2,128,128]{2,1,0:T(8,128)S(1)} %collective-permute-done.27.refs_4_), channel_id=1, source_target_pairs={{0,1},{1,0},{2,3},{3,2},{4,5},{5,4},{6,7},{7,6},{8,9},{9,8},{10,11... | collective-permute-start | bytes 393224 | tf_op jit(solution)/shard_map/ppermute | solution.py:242
  78.4 1.8 %collective-permute-start.38 = (f32[2,128,128]{2,1,0:T(8,128)S(1)}, f32[2,128,128]{2,1,0:T(8,128)S(1)}, u32[]{:S(2)}, u32[]{:S(2)}) collective-permute-start(f32[2,128,128]{2,1,0:T(8,128)S(1)} %collective-permute-done.37.refs_14_), channel_id=1, source_target_pairs={{0,1},{1,0},{2,3},{3,2},{4,5},{5,4},{6,7},{7,6},{8,9},{9,8},{10,11... | collective-permute-start | bytes 393224 | tf_op jit(solution)/shard_map/ppermute | solution.py:242
  78.4 1.8 %collective-permute-start.34 = (f32[2,128,128]{2,1,0:T(8,128)S(1)}, f32[2,128,128]{2,1,0:T(8,128)S(1)}, u32[]{:S(2)}, u32[]{:S(2)}) collective-permute-start(f32[2,128,128]{2,1,0:T(8,128)S(1)} %collective-permute-done.33.refs_10_), channel_id=1, source_target_pairs={{0,1},{1,0},{2,3},{3,2},{4,5},{5,4},{6,7},{7,6},{8,9},{9,8},{10,11... | collective-permute-start | bytes 393224 | tf_op jit(solution)/shard_map/ppermute | solution.py:242
  80.1 1.3 %collective-permute-start.30 = (f32[2,128,128]{2,1,0:T(8,128)S(1)}, f32[2,128,128]{2,1,0:T(8,128)S(1)}, u32[]{:S(2)}, u32[]{:S(2)}) collective-permute-start(f32[2,128,128]{2,1,0:T(8,128)S(1)} %collective-permute-done.29.refs_6_), channel_id=1, source_target_pairs={{0,1},{1,0},{2,3},{3,2},{4,5},{5,4},{6,7},{7,6},{8,9},{9,8},{10,11... | collective-permute-start | bytes 393224 | tf_op jit(solution)/shard_map/ppermute | solution.py:242
  87.6 8.4 %collective-permute-start.39 = (f32[648,128]{1,0:T(8,128)S(1)}, f32[648,128]{1,0:T(8,128)S(1)}, u32[]{:S(2)}, u32[]{:S(2)}) collective-permute-start(f32[648,128]{1,0:T(8,128)S(1)} %get-tuple-element.54.far_in), channel_id=1, source_target_pairs={{0,1},{1,0},{2,3},{3,2},{4,5},{5,4},{6,7},{7,6},{8,9},{9,8},{10,11... | collective-permute-start | bytes 995336 | tf_op jit(solution)/shard_map/ppermute | solution.py:242
  87.8 7.1 %collective-permute-start.40 = (f32[264,128]{1,0:T(8,128)S(1)}, f32[264,128]{1,0:T(8,128)S(1)}, u32[]{:S(2)}, u32[]{:S(2)}) collective-permute-start(f32[264,128]{1,0:T(8,128)S(1)} %get-tuple-element.55), channel_id=1, source_target_pairs={{0,2},{1,3},{2,0},{3,1},{4,6},{5,7},{6,4},{7,5},{8,10},{9,11},{10,... | collective-permute-start | bytes 405512 | tf_op jit(solution)/shard_map/ppermute | solution.py:242
  88.5 7.4 %collective-permute-start.41 = (f32[264,128]{1,0:T(8,128)S(1)}, f32[264,128]{1,0:T(8,128)S(1)}, u32[]{:S(2)}, u32[]{:S(2)}) collective-permute-start(f32[264,128]{1,0:T(8,128)S(1)} %get-tuple-element.56), channel_id=1, source_target_pairs={{0,3},{1,2},{2,1},{3,0},{4,7},{5,6},{6,5},{7,4},{8,11},{9,10},{10,... | collective-permute-start | bytes 405512 | tf_op jit(solution)/shard_map/ppermute | solution.py:242
  89.5 4.9 %collective-permute-start.42 = (f32[128,128]{1,0:T(8,128)S(1)}, f32[128,128]{1,0:T(8,128)S(1)}, u32[]{:S(2)}, u32[]{:S(2)}) collective-permute-start(f32[128,128]{1,0:T(8,128)S(1)} %get-tuple-element.57), channel_id=1, source_target_pairs={{0,4},{1,5},{2,6},{3,7},{4,0},{5,1},{6,2},{7,3},{8,12},{9,13},{10,... | collective-permute-start | bytes 196616 | tf_op jit(solution)/shard_map/ppermute | solution.py:242
  90.3 4.6 %collective-permute-start.43 = (f32[128,128]{1,0:T(8,128)S(1)}, f32[128,128]{1,0:T(8,128)S(1)}, u32[]{:S(2)}, u32[]{:S(2)}) collective-permute-start(f32[128,128]{1,0:T(8,128)S(1)} %get-tuple-element.58), channel_id=1, source_target_pairs={{0,5},{1,4},{2,7},{3,6},{4,1},{5,0},{6,3},{7,2},{8,13},{9,12},{10,... | collective-permute-start | bytes 196616 | tf_op jit(solution)/shard_map/ppermute | solution.py:242
  96.7 13.1 %collective-permute-start.45 = (f32[264,128]{1,0:T(8,128)S(1)}, f32[264,128]{1,0:T(8,128)S(1)}, u32[]{:S(2)}, u32[]{:S(2)}) collective-permute-start(f32[264,128]{1,0:T(8,128)S(1)} %get-tuple-element.63), channel_id=1, source_target_pairs={{0,8},{1,9},{2,10},{3,11},{4,12},{5,13},{6,14},{7,15},{8,0},{9,1},... | collective-permute-start | bytes 405512 | tf_op jit(solution)/shard_map/ppermute | solution.py:242
  97.0 12.7 %collective-permute-start.46 = (f32[264,128]{1,0:T(8,128)S(1)}, f32[264,128]{1,0:T(8,128)S(1)}, u32[]{:S(2)}, u32[]{:S(2)}) collective-permute-start(f32[264,128]{1,0:T(8,128)S(1)} %get-tuple-element.64), channel_id=1, source_target_pairs={{0,12},{1,13},{2,14},{3,15},{4,8},{5,9},{6,10},{7,11},{8,4},{9,5},... | collective-permute-start | bytes 405512 | tf_op jit(solution)/shard_map/ppermute | solution.py:242
  100.1 10.7 %collective-permute-start.47 = (f32[264,128]{1,0:T(8,128)S(1)}, f32[264,128]{1,0:T(8,128)S(1)}, u32[]{:S(2)}, u32[]{:S(2)}) collective-permute-start(f32[264,128]{1,0:T(8,128)S(1)} %get-tuple-element.62.refs_0_), channel_id=1, source_target_pairs={{0,4},{1,5},{2,6},{3,7},{4,0},{5,1},{6,2},{7,3},{8,12},{9,13},{10,... | collective-permute-start | bytes 405512 | tf_op jit(solution)/shard_map/ppermute | solution.py:242
  100.2 5.0 %collective-permute-start.44 = (f32[2,128,128]{2,1,0:T(8,128)S(1)}, f32[2,128,128]{2,1,0:T(8,128)S(1)}, u32[]{:S(2)}, u32[]{:S(2)}) collective-permute-start(f32[2,128,128]{2,1,0:T(8,128)S(1)} %get-tuple-element.60), channel_id=1, source_target_pairs={{0,2},{1,3},{2,0},{3,1},{4,6},{5,7},{6,4},{7,5},{8,10},{9,11},{10,... | collective-permute-start | bytes 393224 | tf_op jit(solution)/shard_map/ppermute | solution.py:242

commit v11 on v9

--- a/solution.py
+++ b/solution.py
@@ -343,7 +343,7 @@
         (shape(2, width, width),) * 2 + (shape(2 * width + 8, width),) * (chips // 2 - 1), tables[2:3],
         (near, far, swapped(far, CORE), swapped(row, ROW), swapped(row_far, ROW + CORE), swapped(column, COLUMN),
          swapped(column_far, COLUMN + CORE)))
-    came = [swapped(sends[i], 2 * ROW * (i + 1)) for i in (*range(1, len(sends)), 0)]
+    came = [swapped(x, 2 * ROW * (i + 1)) for i, x in reversed(list(enumerate(sends)))]
     return square, (own, swapped(step, ROW)), [sends[0], *came]
 
 
@@ -354,7 +354,7 @@
     pieces[ROW] = swapped(x, ROW)
     pieces[COLUMN] = swapped(x, COLUMN)
     if held is not None:
-        pieces[COLUMN], pieces[0] = lax.optimization_barrier((pieces[COLUMN], held))
+        pieces[n - 4], pieces[0] = lax.optimization_barrier((pieces[n - 4], held))
     for k in reversed(range(8, n, 4)):
         pieces[k + ROW] = swapped(pieces[k], ROW)
     pieces[COLUMN + ROW] = swapped(pieces[ROW], COLUMN)

time: 121 us -> 120 us (level)
  starting transfers between devices: 38.6 us -> 37.2 us
    ppermute x48, starting transfers between devices: 38.6 us -> 37.2 us  [swapped(): return lax.ppermute(x, 'term', [(i, i ^ k) for i in range(n)])]
  transfers between devices with their start and end apart: 48 -> 48, of which waited for: 27 -> 23; matrix products, arithmetic and copies ran while one was open for 0% -> 0% of each run, Pallas kernels for 2% -> 3%
where the time goes in v11:
time: 120 us
  waiting for transfers between devices  50.8 us (42%)
  starting transfers between devices  37.2 us (31%)
  Pallas kernels  18.9 us (16%)
  blocking collectives  10.8 us (9%)
  between operations  1.41 us (1%)
    ppermute x48, waiting for transfers between devices, swapped(): return lax.ppermute(x, 'term', [(i, i ^ k) for i in range(n)])  50.8 us
    ppermute x48, starting transfers between devices, swapped(): return lax.ppermute(x, 'term', [(i, i ^ k) for i in range(n)])  37.2 us
    pallas_call x2, Pallas kernels, apply(): pl.pallas_call(functools.partial(apply_kernel, n, npairs, over_rows, rows...  12.1 us
    all_to_all x1, blocking collectives, shards(): lax.all_to_all(jnp.broadcast_to(partial[None], (n, 8, width)), 'term', sp...  10.8 us
    pallas_call x5, Pallas kernels, local(): pl.pallas_call(kernel, out_shape=out_shape, in_specs=[SMEM] * len(scalars...  3.42 us
    pallas_call x1, Pallas kernels, prep(): pl.pallas_call(functools.partial(prep_kernel, n, terms * n + 1), out_shap...  3.4 us
  transfers between devices with their start and end apart: 48, of which 23 were waited for; matrix products, arithmetic and copies ran while one was open for 0% of the time, Pallas kernels for 3%

profile of v11, /device:TPU:0, one launch (start us, length us, event | category | flops | bytes accessed | tf_op | source)
XLA Modules:
  0.0 119.6 jit_solution(1697266445089477736)
XLA Ops:
  0.6 3.0 %collective-permute-start.2 = (f32[2,128,128]{2,1,0:T(8,128)}, f32[2,128,128]{2,1,0:T(8,128)S(1)}, u32[]{:S(2)}, u32[]{:S(2)}) collective-permute-start(f32[2,128,128]{2,1,0:T(8,128)} %vector_in.1), channel_id=1, source_target_pairs={{0,2},{1,3},{2,0},{3,1},{4,6},{5,7},{6,4},{7,5},{8,10},{9,11},{10,... | collective-permute-start | bytes 393224 | tf_op jit(solution)/shard_map/ppermute | solution.py:242
  3.7 2.6 %collective-permute-start.8 = (f32[2,128,128]{2,1,0:T(8,128)}, f32[2,128,128]{2,1,0:T(8,128)S(1)}, u32[]{:S(2)}, u32[]{:S(2)}) collective-permute-start(f32[2,128,128]{2,1,0:T(8,128)} %vector_in.1), channel_id=1, source_target_pairs={{0,8},{1,9},{2,10},{3,11},{4,12},{5,13},{6,14},{7,15},{8,0},{9,1},... | collective-permute-start | bytes 393224 | tf_op jit(solution)/shard_map/ppermute | solution.py:242
  6.3 1.3 %collective-permute-start = (f32[2,128,128]{2,1,0:T(8,128)}, f32[2,128,128]{2,1,0:T(8,128)S(1)}, u32[]{:S(2)}, u32[]{:S(2)}) collective-permute-start(f32[2,128,128]{2,1,0:T(8,128)} %vector_in.1), channel_id=1, source_target_pairs={{0,12},{1,13},{2,14},{3,15},{4,8},{5,9},{6,10},{7,11},{8,4},{9,5},... | collective-permute-start | bytes 393224 | tf_op jit(solution)/shard_map/ppermute | solution.py:242
  7.6 0.2 collective-permute-start.4
  7.8 1.8 %collective-permute-start.6 = (f32[2,128,128]{2,1,0:T(8,128)S(1)}, f32[2,128,128]{2,1,0:T(8,128)S(1)}, u32[]{:S(2)}, u32[]{:S(2)}) collective-permute-start(f32[2,128,128]{2,1,0:T(8,128)S(1)} %collective-permute-done.2.refs_2_), channel_id=1, source_target_pairs={{0,4},{1,5},{2,6},{3,7},{4,0},{5,1},{6,2},{7,3},{8,12},{9,13},{10,... | collective-permute-start | bytes 393224 | tf_op jit(solution)/shard_map/ppermute | solution.py:242
  10.3 0.6 copy.12
  10.9 3.4 %prep.1 = (bf16[8,128,512]{2,1,0:T(8,128)(2,1)S(1)}, bf16[2048,256]{1,0:T(8,128)(2,1)S(1)}, s32[721]{0:T(1024)S(1)}, f32[2,128,128]{2,1,0:T(8,128)S(1)}) custom-call(s32[1]{0:T(128)} %bitcast.me_ref, s32[16,16]{1,0:T(8,128)} %fetch_in.1, s32[16,16]{1,0:T(8,128)} %store_in.1, s32[384]{0:T(512)} %bitcast.8, s32[1]{0:T(128)S(6)} %copy.13.live_in, ...), custom_call_target="tpu_custom_call" | custom-call | tf_op jit(solution)/shard_map/prep/pallas_call | solution.py:132
  14.4 2.2 %collective-permute-done.8.refs_8_ = f32[2,128,128]{2,1,0:T(8,128)S(1)} collective-permute-done((f32[2,128,128]{2,1,0:T(8,128)}, f32[2,128,128]{2,1,0:T(8,128)S(1)}, u32[]{:S(2)}, u32[]{:S(2)}) %collective-permute-start.8) | collective-permute-done | bytes 131104 | tf_op jit(solution)/shard_map/ppermute | solution.py:242
  16.5 0.4 collective-permute-start.10
  17.0 1.1 collective-permute-done.4.refs_4_
  18.1 1.4 %collective-permute-done.6.refs_6_ = f32[2,128,128]{2,1,0:T(8,128)S(1)} collective-permute-done((f32[2,128,128]{2,1,0:T(8,128)S(1)}, f32[2,128,128]{2,1,0:T(8,128)S(1)}, u32[]{:S(2)}, u32[]{:S(2)}) %collective-permute-start.6) | collective-permute-done | bytes 131104 | tf_op jit(solution)/shard_map/ppermute | solution.py:242
  19.5 0.5 collective-permute-start.13
  20.0 1.8 %collective-permute-done.10.refs_10_ = f32[2,128,128]{2,1,0:T(8,128)S(1)} collective-permute-done((f32[2,128,128]{2,1,0:T(8,128)S(1)}, f32[2,128,128]{2,1,0:T(8,128)S(1)}, u32[]{:S(2)}, u32[]{:S(2)}) %collective-permute-start.10) | collective-permute-done | bytes 131104 | tf_op jit(solution)/shard_map/ppermute | solution.py:242
  21.8 0.5 collective-permute-start.7
  22.3 2.1 %collective-permute-done.13.refs_14_ = f32[2,128,128]{2,1,0:T(8,128)S(1)} collective-permute-done((f32[2,128,128]{2,1,0:T(8,128)S(1)}, f32[2,128,128]{2,1,0:T(8,128)S(1)}, u32[]{:S(2)}, u32[]{:S(2)}) %collective-permute-start.13) | collective-permute-done | bytes 131104 | tf_op jit(solution)/shard_map/ppermute | solution.py:242
  24.5 1.3 %collective-permute-done.14.refs_15_ = f32[2,128,128]{2,1,0:T(8,128)S(1)} collective-permute-done((f32[2,128,128]{2,1,0:T(8,128)S(1)}, f32[2,128,128]{2,1,0:T(8,128)S(1)}, u32[]{:S(2)}, u32[]{:S(2)}) %collective-permute-start.14) | collective-permute-done | bytes 131104 | tf_op jit(solution)/shard_map/ppermute | solution.py:242
  25.8 6.0 %apply.2 = (f32[640,128]{1,0:T(8,128)S(1)}, f32[648,128]{1,0:T(8,128)S(1)}, f32[264,128]{1,0:T(8,128)S(1)}, f32[264,128]{1,0:T(8,128)S(1)}, f32[128,128]{1,0:T(8...) custom-call(s32[721]{0:T(1024)S(1)} %get-tuple-element.35.table_ref, ...), custom_call_target="tpu_custom_call" | custom-call | tf_op jit(solution)/shard_map/apply/pallas_call | solution.py:216
  31.8 0.3 collective-permute-start.15
  32.1 0.4 collective-permute-start.16
  32.6 1.2 collective-permute-start.17
  33.7 0.7 collective-permute-start.18
  34.4 1.2 %collective-permute-start.19 = (f32[128,128]{1,0:T(8,128)S(1)}, f32[128,128]{1,0:T(8,128)S(1)}, u32[]{:S(2)}, u32[]{:S(2)}) collective-permute-start(f32[128,128]{1,0:T(8,128)S(1)} %get-tuple-element.46), channel_id=1, source_target_pairs={{0,5},{1,4},{2,7},{3,6},{4,1},{5,0},{6,3},{7,2},{8,13},{9,12},{10,... | collective-permute-start | bytes 196616 | tf_op jit(solution)/shard_map/ppermute | solution.py:242
  35.6 3.0 %collective-permute-done.18.column_ref = f32[128,128]{1,0:T(8,128)S(1)} collective-permute-done((f32[128,128]{1,0:T(8,128)S(1)}, f32[128,128]{1,0:T(8,128)S(1)}, u32[]{:S(2)}, u32[]{:S(2)}) %collective-permute-start.18) | collective-permute-done | bytes 65568 | tf_op jit(solution)/shard_map/ppermute | solution.py:242
  38.6 0.7 collective-permute-done.19.column_far_ref
  39.3 0.8 collective-permute-done.17.row_far_ref
  40.1 0.7 fold.2
  40.9 3.7 %collective-permute-start.21 = (f32[264,128]{1,0:T(8,128)S(1)}, f32[264,128]{1,0:T(8,128)S(1)}, u32[]{:S(2)}, u32[]{:S(2)}) collective-permute-start(f32[264,128]{1,0:T(8,128)S(1)} %get-tuple-element.51), channel_id=1, source_target_pairs={{0,12},{1,13},{2,14},{3,15},{4,8},{5,9},{6,10},{7,11},{8,4},{9,5},... | collective-permute-start | bytes 405512 | tf_op jit(solution)/shard_map/ppermute | solution.py:242
  44.6 0.7 collective-permute-start.23
  45.3 0.8 collective-permute-start.20
  46.1 4.4 %collective-permute-done.20.step_ref = f32[2,128,128]{2,1,0:T(8,128)S(1)} collective-permute-done((f32[2,128,128]{2,1,0:T(8,128)S(1)}, f32[2,128,128]{2,1,0:T(8,128)S(1)}, u32[]{:S(2)}, u32[]{:S(2)}) %collective-permute-start.20) | collective-permute-done | bytes 131104 | tf_op jit(solution)/shard_map/ppermute | solution.py:242
  50.5 5.6 %collective-permute-done.22.refs_2_ = f32[264,128]{1,0:T(8,128)S(1)} collective-permute-done((f32[264,128]{1,0:T(8,128)S(1)}, f32[264,128]{1,0:T(8,128)S(1)}, u32[]{:S(2)}, u32[]{:S(2)}) %collective-permute-start.22) | collective-permute-done | bytes 135200 | tf_op jit(solution)/shard_map/ppermute | solution.py:242
  56.1 0.2 step.1.refs_0_.vector_ref
  56.3 2.7 %collective-permute-start.35 = (f32[2,128,128]{2,1,0:T(8,128)S(1)}, f32[2,128,128]{2,1,0:T(8,128)S(1)}, u32[]{:S(2)}, u32[]{:S(2)}) collective-permute-start(f32[2,128,128]{2,1,0:T(8,128)S(1)} %step.1.refs_0_.vector_ref), channel_id=1, source_target_pairs={{0,12},{1,13},{2,14},{3,15},{4,8},{5,9},{6,10},{7,11},{8,4},{9,5},... | collective-permute-start | bytes 393224 | tf_op jit(solution)/shard_map/ppermute | solution.py:242
  59.0 1.7 %collective-permute-start.27 = (f32[2,128,128]{2,1,0:T(8,128)S(1)}, f32[2,128,128]{2,1,0:T(8,128)S(1)}, u32[]{:S(2)}, u32[]{:S(2)}) collective-permute-start(f32[2,128,128]{2,1,0:T(8,128)S(1)} %step.1.refs_0_.vector_ref), channel_id=1, source_target_pairs={{0,4},{1,5},{2,6},{3,7},{4,0},{5,1},{6,2},{7,3},{8,12},{9,13},{10,... | collective-permute-start | bytes 393224 | tf_op jit(solution)/shard_map/ppermute | solution.py:242
  60.7 0.6 collective-permute-start.25
  61.3 3.3 %collective-permute-done.35.refs_12_ = f32[2,128,128]{2,1,0:T(8,128)S(1)} collective-permute-done((f32[2,128,128]{2,1,0:T(8,128)S(1)}, f32[2,128,128]{2,1,0:T(8,128)S(1)}, u32[]{:S(2)}, u32[]{:S(2)}) %collective-permute-start.35) | collective-permute-done | bytes 131104 | tf_op jit(solution)/shard_map/ppermute | solution.py:242
  64.6 0.6 collective-permute-start.37
  65.1 4.4 %collective-permute-done.31.refs_8_ = f32[2,128,128]{2,1,0:T(8,128)S(1)} collective-permute-done((f32[2,128,128]{2,1,0:T(8,128)S(1)}, f32[2,128,128]{2,1,0:T(8,128)S(1)}, u32[]{:S(2)}, u32[]{:S(2)}) %collective-permute-start.31) | collective-permute-done | bytes 131104 | tf_op jit(solution)/shard_map/ppermute | solution.py:242
  69.6 0.4 collective-permute-start.33
  70.0 0.2 collective-permute-start.32
  70.3 0.2 collective-permute-start.26
  70.6 0.4 collective-permute-done.36.refs_13_
  71.1 4.4 %collective-permute-done.33.refs_10_ = f32[2,128,128]{2,1,0:T(8,128)S(1)} collective-permute-done((f32[2,128,128]{2,1,0:T(8,128)S(1)}, f32[2,128,128]{2,1,0:T(8,128)S(1)}, u32[]{:S(2)}, u32[]{:S(2)}) %collective-permute-start.33) | collective-permute-done | bytes 131104 | tf_op jit(solution)/shard_map/ppermute | solution.py:242
  75.5 0.5 collective-permute-start.34
  76.1 0.8 collective-permute-done.38.refs_15_
  76.8 0.2 collective-permute-done.34.refs_11_
  77.0 0.3 collective-permute-done.30.refs_7_
  77.4 6.1 %apply.3 = (f32[640,128]{1,0:T(8,128)S(1)}, f32[648,128]{1,0:T(8,128)S(1)}, f32[264,128]{1,0:T(8,128)S(1)}, f32[264,128]{1,0:T(8,128)S(1)}, f32[128,128]{1,0:T(8...) custom-call(s32[721]{0:T(1024)S(1)} %get-tuple-element.35.table_ref, ...), custom_call_target="tpu_custom_call" | custom-call | tf_op jit(solution)/shard_map/apply/pallas_call | solution.py:216
  83.5 0.3 collective-permute-start.39
  83.8 1.5 %collective-permute-start.40 = (f32[264,128]{1,0:T(8,128)S(1)}, f32[264,128]{1,0:T(8,128)S(1)}, u32[]{:S(2)}, u32[]{:S(2)}) collective-permute-start(f32[264,128]{1,0:T(8,128)S(1)} %get-tuple-element.55), channel_id=1, source_target_pairs={{0,2},{1,3},{2,0},{3,1},{4,6},{5,7},{6,4},{7,5},{8,10},{9,11},{10,... | collective-permute-start | bytes 405512 | tf_op jit(solution)/shard_map/ppermute | solution.py:242
  85.4 0.4 collective-permute-start.42
  85.8 1.5 %collective-permute-start.43 = (f32[128,128]{1,0:T(8,128)S(1)}, f32[128,128]{1,0:T(8,128)S(1)}, u32[]{:S(2)}, u32[]{:S(2)}) collective-permute-start(f32[128,128]{1,0:T(8,128)S(1)} %get-tuple-element.58), channel_id=1, source_target_pairs={{0,5},{1,4},{2,7},{3,6},{4,1},{5,0},{6,3},{7,2},{8,13},{9,12},{10,... | collective-permute-start | bytes 196616 | tf_op jit(solution)/shard_map/ppermute | solution.py:242
  87.3 3.0 %collective-permute-done.42.column_ref = f32[128,128]{1,0:T(8,128)S(1)} collective-permute-done((f32[128,128]{1,0:T(8,128)S(1)}, f32[128,128]{1,0:T(8,128)S(1)}, u32[]{:S(2)}, u32[]{:S(2)}) %collective-permute-start.42) | collective-permute-done | bytes 65568 | tf_op jit(solution)/shard_map/ppermute | solution.py:242
  90.3 0.8 collective-permute-done.43.column_far_ref
  91.1 0.7 collective-permute-done.41.row_far_ref
  91.7 0.7 fold.3
  92.5 2.2 %collective-permute-start.45 = (f32[264,128]{1,0:T(8,128)S(1)}, f32[264,128]{1,0:T(8,128)S(1)}, u32[]{:S(2)}, u32[]{:S(2)}) collective-permute-start(f32[264,128]{1,0:T(8,128)S(1)} %get-tuple-element.63), channel_id=1, source_target_pairs={{0,12},{1,13},{2,14},{3,15},{4,8},{5,9},{6,10},{7,11},{8,4},{9,5},... | collective-permute-start | bytes 405512 | tf_op jit(solution)/shard_map/ppermute | solution.py:242
  94.7 2.2 %collective-permute-start.47 = (f32[264,128]{1,0:T(8,128)S(1)}, f32[264,128]{1,0:T(8,128)S(1)}, u32[]{:S(2)}, u32[]{:S(2)}) collective-permute-start(f32[264,128]{1,0:T(8,128)S(1)} %get-tuple-element.62.refs_0_), channel_id=1, source_target_pairs={{0,4},{1,5},{2,6},{3,7},{4,0},{5,1},{6,2},{7,3},{8,12},{9,13},{10,... | collective-permute-start | bytes 405512 | tf_op jit(solution)/shard_map/ppermute | solution.py:242
  96.9 1.9 %collective-permute-start.44 = (f32[2,128,128]{2,1,0:T(8,128)S(1)}, f32[2,128,128]{2,1,0:T(8,128)S(1)}, u32[]{:S(2)}, u32[]{:S(2)}) collective-permute-start(f32[2,128,128]{2,1,0:T(8,128)S(1)} %get-tuple-element.60), channel_id=1, source_target_pairs={{0,2},{1,3},{2,0},{3,1},{4,6},{5,7},{6,4},{7,5},{8,10},{9,11},{10,... | collective-permute-start | bytes 393224 | tf_op jit(solution)/shard_map/ppermute | solution.py:242
  98.9 3.1 %collective-permute-done.44.step_ref = f32[2,128,128]{2,1,0:T(8,128)S(1)} collective-permute-done((f32[2,128,128]{2,1,0:T(8,128)S(1)}, f32[2,128,128]{2,1,0:T(8,128)S(1)}, u32[]{:S(2)}, u32[]{:S(2)}) %collective-permute-start.44) | collective-permute-done | bytes 131104 | tf_op jit(solution)/shard_map/ppermute | solution.py:242
  102.0 5.1 %collective-permute-done.46.refs_2_ = f32[264,128]{1,0:T(8,128)S(1)} collective-permute-done((f32[264,128]{1,0:T(8,128)S(1)}, f32[264,128]{1,0:T(8,128)S(1)}, u32[]{:S(2)}, u32[]{:S(2)}) %collective-permute-start.46) | collective-permute-done | bytes 135200 | tf_op jit(solution)/shard_map/ppermute | solution.py:242
  107.1 0.9 last.1
  108.0 10.8 %all_to_all.5.tiles_ref = f32[16,8,128]{2,1,0:T(8,128)S(1)} all-to-all(f32[16,8,128]{2,1,0:T(8,128)S(1)} %broadcast_in_dim.2), channel_id=1, replica_groups=mesh['group'=2,'term'=16] {'term'}, dimensions={0} | all-to-all | bytes 131072 | tf_op jit(solution)/shard_map/all_to_all | solution.py:384
  118.8 0.9 norm.1
  (47 shorter events, 0.7 us)
Async XLA Ops:
  0.6 7.2 %collective-permute-start.2 = (f32[2,128,128]{2,1,0:T(8,128)}, f32[2,128,128]{2,1,0:T(8,128)S(1)}, u32[]{:S(2)}, u32[]{:S(2)}) collective-permute-start(f32[2,128,128]{2,1,0:T(8,128)} %vector_in.1), channel_id=1, source_target_pairs={{0,2},{1,3},{2,0},{3,1},{4,6},{5,7},{6,4},{7,5},{8,10},{9,11},{10,... | collective-permute-start | bytes 393224 | tf_op jit(solution)/shard_map/ppermute | solution.py:242
  3.7 12.9 %collective-permute-start.8 = (f32[2,128,128]{2,1,0:T(8,128)}, f32[2,128,128]{2,1,0:T(8,128)S(1)}, u32[]{:S(2)}, u32[]{:S(2)}) collective-permute-start(f32[2,128,128]{2,1,0:T(8,128)} %vector_in.1), channel_id=1, source_target_pairs={{0,8},{1,9},{2,10},{3,11},{4,12},{5,13},{6,14},{7,15},{8,0},{9,1},... | collective-permute-start | bytes 393224 | tf_op jit(solution)/shard_map/ppermute | solution.py:242
  6.3 10.7 %collective-permute-start = (f32[2,128,128]{2,1,0:T(8,128)}, f32[2,128,128]{2,1,0:T(8,128)S(1)}, u32[]{:S(2)}, u32[]{:S(2)}) collective-permute-start(f32[2,128,128]{2,1,0:T(8,128)} %vector_in.1), channel_id=1, source_target_pairs={{0,12},{1,13},{2,14},{3,15},{4,8},{5,9},{6,10},{7,11},{8,4},{9,5},... | collective-permute-start | bytes 393224 | tf_op jit(solution)/shard_map/ppermute | solution.py:242
  7.6 10.5 %collective-permute-start.4 = (f32[2,128,128]{2,1,0:T(8,128)}, f32[2,128,128]{2,1,0:T(8,128)S(1)}, u32[]{:S(2)}, u32[]{:S(2)}) collective-permute-start(f32[2,128,128]{2,1,0:T(8,128)} %vector_in.1), channel_id=1, source_target_pairs={{0,4},{1,5},{2,6},{3,7},{4,0},{5,1},{6,2},{7,3},{8,12},{9,13},{10,... | collective-permute-start | bytes 393224 | tf_op jit(solution)/shard_map/ppermute | solution.py:242
  7.8 11.7 %collective-permute-start.6 = (f32[2,128,128]{2,1,0:T(8,128)S(1)}, f32[2,128,128]{2,1,0:T(8,128)S(1)}, u32[]{:S(2)}, u32[]{:S(2)}) collective-permute-start(f32[2,128,128]{2,1,0:T(8,128)S(1)} %collective-permute-done.2.refs_2_), channel_id=1, source_target_pairs={{0,4},{1,5},{2,6},{3,7},{4,0},{5,1},{6,2},{7,3},{8,12},{9,13},{10,... | collective-permute-start | bytes 393224 | tf_op jit(solution)/shard_map/ppermute | solution.py:242
  9.6 0.7 copy-start.1
  14.3 5.7 %collective-permute-start.3 = (f32[2,128,128]{2,1,0:T(8,128)S(1)}, f32[2,128,128]{2,1,0:T(8,128)S(1)}, u32[]{:S(2)}, u32[]{:S(2)}) collective-permute-start(f32[2,128,128]{2,1,0:T(8,128)S(1)} %collective-permute-done.2.refs_2_), channel_id=1, source_target_pairs={{0,1},{1,0},{2,3},{3,2},{4,5},{5,4},{6,7},{7,6},{8,9},{9,8},{10,11... | collective-permute-start | bytes 393224 | tf_op jit(solution)/shard_map/ppermute | solution.py:242
  16.5 5.2 %collective-permute-start.10 = (f32[2,128,128]{2,1,0:T(8,128)S(1)}, f32[2,128,128]{2,1,0:T(8,128)S(1)}, u32[]{:S(2)}, u32[]{:S(2)}) collective-permute-start(f32[2,128,128]{2,1,0:T(8,128)S(1)} %collective-permute-done.8.refs_8_), channel_id=1, source_target_pairs={{0,2},{1,3},{2,0},{3,1},{4,6},{5,7},{6,4},{7,5},{8,10},{9,11},{10,... | collective-permute-start | bytes 393224 | tf_op jit(solution)/shard_map/ppermute | solution.py:242
  17.0 4.8 %collective-permute-start.9 = (f32[2,128,128]{2,1,0:T(8,128)S(1)}, f32[2,128,128]{2,1,0:T(8,128)S(1)}, u32[]{:S(2)}, u32[]{:S(2)}) collective-permute-start(f32[2,128,128]{2,1,0:T(8,128)S(1)} %collective-permute-done.8.refs_8_), channel_id=1, source_target_pairs={{0,1},{1,0},{2,3},{3,2},{4,5},{5,4},{6,7},{7,6},{8,9},{9,8},{10,11... | collective-permute-start | bytes 393224 | tf_op jit(solution)/shard_map/ppermute | solution.py:242
  18.1 4.2 %collective-permute-start.5 = (f32[2,128,128]{2,1,0:T(8,128)S(1)}, f32[2,128,128]{2,1,0:T(8,128)S(1)}, u32[]{:S(2)}, u32[]{:S(2)}) collective-permute-start(f32[2,128,128]{2,1,0:T(8,128)S(1)} %collective-permute-done.4.refs_4_), channel_id=1, source_target_pairs={{0,1},{1,0},{2,3},{3,2},{4,5},{5,4},{6,7},{7,6},{8,9},{9,8},{10,11... | collective-permute-start | bytes 393224 | tf_op jit(solution)/shard_map/ppermute | solution.py:242
  19.5 5.0 %collective-permute-start.13 = (f32[2,128,128]{2,1,0:T(8,128)S(1)}, f32[2,128,128]{2,1,0:T(8,128)S(1)}, u32[]{:S(2)}, u32[]{:S(2)}) collective-permute-start(f32[2,128,128]{2,1,0:T(8,128)S(1)} %collective-permute-done.refs_12_), channel_id=1, source_target_pairs={{0,2},{1,3},{2,0},{3,1},{4,6},{5,7},{6,4},{7,5},{8,10},{9,11},{10,... | collective-permute-start | bytes 393224 | tf_op jit(solution)/shard_map/ppermute | solution.py:242
  20.0 4.5 %collective-permute-start.12 = (f32[2,128,128]{2,1,0:T(8,128)S(1)}, f32[2,128,128]{2,1,0:T(8,128)S(1)}, u32[]{:S(2)}, u32[]{:S(2)}) collective-permute-start(f32[2,128,128]{2,1,0:T(8,128)S(1)} %collective-permute-done.refs_12_), channel_id=1, source_target_pairs={{0,1},{1,0},{2,3},{3,2},{4,5},{5,4},{6,7},{7,6},{8,9},{9,8},{10,11... | collective-permute-start | bytes 393224 | tf_op jit(solution)/shard_map/ppermute | solution.py:242
  21.8 2.7 %collective-permute-start.1 = (f32[2,128,128]{2,1,0:T(8,128)S(1)}, f32[2,128,128]{2,1,0:T(8,128)S(1)}, u32[]{:S(2)}, u32[]{:S(2)}) collective-permute-start(f32[2,128,128]{2,1,0:T(8,128)S(1)} %get-tuple-element.39.refs_0_.vector_ref), channel_id=1, source_target_pairs={{0,1},{1,0},{2,3},{3,2},{4,5},{5,4},{6,7},{7,6},{8,9},{9,8},{10,11... | collective-permute-start | bytes 393224 | tf_op jit(solution)/shard_map/ppermute | solution.py:242
  21.8 2.7 %collective-permute-start.7 = (f32[2,128,128]{2,1,0:T(8,128)S(1)}, f32[2,128,128]{2,1,0:T(8,128)S(1)}, u32[]{:S(2)}, u32[]{:S(2)}) collective-permute-start(f32[2,128,128]{2,1,0:T(8,128)S(1)} %collective-permute-done.6.refs_6_), channel_id=1, source_target_pairs={{0,1},{1,0},{2,3},{3,2},{4,5},{5,4},{6,7},{7,6},{8,9},{9,8},{10,11... | collective-permute-start | bytes 393224 | tf_op jit(solution)/shard_map/ppermute | solution.py:242
  22.3 2.2 %collective-permute-start.11 = (f32[2,128,128]{2,1,0:T(8,128)S(1)}, f32[2,128,128]{2,1,0:T(8,128)S(1)}, u32[]{:S(2)}, u32[]{:S(2)}) collective-permute-start(f32[2,128,128]{2,1,0:T(8,128)S(1)} %collective-permute-done.10.refs_10_), channel_id=1, source_target_pairs={{0,1},{1,0},{2,3},{3,2},{4,5},{5,4},{6,7},{7,6},{8,9},{9,8},{10,11... | collective-permute-start | bytes 393224 | tf_op jit(solution)/shard_map/ppermute | solution.py:242
  24.5 1.3 %collective-permute-start.14 = (f32[2,128,128]{2,1,0:T(8,128)S(1)}, f32[2,128,128]{2,1,0:T(8,128)S(1)}, u32[]{:S(2)}, u32[]{:S(2)}) collective-permute-start(f32[2,128,128]{2,1,0:T(8,128)S(1)} %collective-permute-done.13.refs_14_), channel_id=1, source_target_pairs={{0,1},{1,0},{2,3},{3,2},{4,5},{5,4},{6,7},{7,6},{8,9},{9,8},{10,11... | collective-permute-start | bytes 393224 | tf_op jit(solution)/shard_map/ppermute | solution.py:242
  31.8 8.3 %collective-permute-start.15 = (f32[648,128]{1,0:T(8,128)S(1)}, f32[648,128]{1,0:T(8,128)S(1)}, u32[]{:S(2)}, u32[]{:S(2)}) collective-permute-start(f32[648,128]{1,0:T(8,128)S(1)} %get-tuple-element.42.far_in), channel_id=1, source_target_pairs={{0,1},{1,0},{2,3},{3,2},{4,5},{5,4},{6,7},{7,6},{8,9},{9,8},{10,11... | collective-permute-start | bytes 995336 | tf_op jit(solution)/shard_map/ppermute | solution.py:242
  32.1 7.2 %collective-permute-start.16 = (f32[264,128]{1,0:T(8,128)S(1)}, f32[264,128]{1,0:T(8,128)S(1)}, u32[]{:S(2)}, u32[]{:S(2)}) collective-permute-start(f32[264,128]{1,0:T(8,128)S(1)} %get-tuple-element.43), channel_id=1, source_target_pairs={{0,2},{1,3},{2,0},{3,1},{4,6},{5,7},{6,4},{7,5},{8,10},{9,11},{10,... | collective-permute-start | bytes 405512 | tf_op jit(solution)/shard_map/ppermute | solution.py:242
  32.6 7.6 %collective-permute-start.17 = (f32[264,128]{1,0:T(8,128)S(1)}, f32[264,128]{1,0:T(8,128)S(1)}, u32[]{:S(2)}, u32[]{:S(2)}) collective-permute-start(f32[264,128]{1,0:T(8,128)S(1)} %get-tuple-element.44), channel_id=1, source_target_pairs={{0,3},{1,2},{2,1},{3,0},{4,7},{5,6},{6,5},{7,4},{8,11},{9,10},{10,... | collective-permute-start | bytes 405512 | tf_op jit(solution)/shard_map/ppermute | solution.py:242
  33.7 4.9 %collective-permute-start.18 = (f32[128,128]{1,0:T(8,128)S(1)}, f32[128,128]{1,0:T(8,128)S(1)}, u32[]{:S(2)}, u32[]{:S(2)}) collective-permute-start(f32[128,128]{1,0:T(8,128)S(1)} %get-tuple-element.45), channel_id=1, source_target_pairs={{0,4},{1,5},{2,6},{3,7},{4,0},{5,1},{6,2},{7,3},{8,12},{9,13},{10,... | collective-permute-start | bytes 196616 | tf_op jit(solution)/shard_map/ppermute | solution.py:242
  34.4 4.9 %collective-permute-start.19 = (f32[128,128]{1,0:T(8,128)S(1)}, f32[128,128]{1,0:T(8,128)S(1)}, u32[]{:S(2)}, u32[]{:S(2)}) collective-permute-start(f32[128,128]{1,0:T(8,128)S(1)} %get-tuple-element.46), channel_id=1, source_target_pairs={{0,5},{1,4},{2,7},{3,6},{4,1},{5,0},{6,3},{7,2},{8,13},{9,12},{10,... | collective-permute-start | bytes 196616 | tf_op jit(solution)/shard_map/ppermute | solution.py:242
  40.1 15.9 %copy-start = (f32[2,128,128]{2,1,0:T(8,128)S(1)}, f32[2,128,128]{2,1,0:T(8,128)}, u32[]{:S(2)}) copy-start(f32[2,128,128]{2,1,0:T(8,128)} %precond_ref.3) | copy-start | bytes 393220
  40.9 9.6 %collective-permute-start.21 = (f32[264,128]{1,0:T(8,128)S(1)}, f32[264,128]{1,0:T(8,128)S(1)}, u32[]{:S(2)}, u32[]{:S(2)}) collective-permute-start(f32[264,128]{1,0:T(8,128)S(1)} %get-tuple-element.51), channel_id=1, source_target_pairs={{0,12},{1,13},{2,14},{3,15},{4,8},{5,9},{6,10},{7,11},{8,4},{9,5},... | collective-permute-start | bytes 405512 | tf_op jit(solution)/shard_map/ppermute | solution.py:242
  44.6 11.4 %collective-permute-start.22 = (f32[264,128]{1,0:T(8,128)S(1)}, f32[264,128]{1,0:T(8,128)S(1)}, u32[]{:S(2)}, u32[]{:S(2)}) collective-permute-start(f32[264,128]{1,0:T(8,128)S(1)} %get-tuple-element.52), channel_id=1, source_target_pairs={{0,8},{1,9},{2,10},{3,11},{4,12},{5,13},{6,14},{7,15},{8,0},{9,1},... | collective-permute-start | bytes 405512 | tf_op jit(solution)/shard_map/ppermute | solution.py:242
  44.6 11.4 %collective-permute-start.23 = (f32[264,128]{1,0:T(8,128)S(1)}, f32[264,128]{1,0:T(8,128)S(1)}, u32[]{:S(2)}, u32[]{:S(2)}) collective-permute-start(f32[264,128]{1,0:T(8,128)S(1)} %get-tuple-element.50.refs_0_), channel_id=1, source_target_pairs={{0,4},{1,5},{2,6},{3,7},{4,0},{5,1},{6,2},{7,3},{8,12},{9,13},{10,... | collective-permute-start | bytes 405512 | tf_op jit(solution)/shard_map/ppermute | solution.py:242
  45.3 5.2 %collective-permute-start.20 = (f32[2,128,128]{2,1,0:T(8,128)S(1)}, f32[2,128,128]{2,1,0:T(8,128)S(1)}, u32[]{:S(2)}, u32[]{:S(2)}) collective-permute-start(f32[2,128,128]{2,1,0:T(8,128)S(1)} %get-tuple-element.48), channel_id=1, source_target_pairs={{0,2},{1,3},{2,0},{3,1},{4,6},{5,7},{6,4},{7,5},{8,10},{9,11},{10,... | collective-permute-start | bytes 393224 | tf_op jit(solution)/shard_map/ppermute | solution.py:242
  56.3 8.3 %collective-permute-start.35 = (f32[2,128,128]{2,1,0:T(8,128)S(1)}, f32[2,128,128]{2,1,0:T(8,128)S(1)}, u32[]{:S(2)}, u32[]{:S(2)}) collective-permute-start(f32[2,128,128]{2,1,0:T(8,128)S(1)} %step.1.refs_0_.vector_ref), channel_id=1, source_target_pairs={{0,12},{1,13},{2,14},{3,15},{4,8},{5,9},{6,10},{7,11},{8,4},{9,5},... | collective-permute-start | bytes 393224 | tf_op jit(solution)/shard_map/ppermute | solution.py:242
  59.0 10.6 %collective-permute-start.31 = (f32[2,128,128]{2,1,0:T(8,128)S(1)}, f32[2,128,128]{2,1,0:T(8,128)S(1)}, u32[]{:S(2)}, u32[]{:S(2)}) collective-permute-start(f32[2,128,128]{2,1,0:T(8,128)S(1)} %step.1.refs_0_.vector_ref), channel_id=1, source_target_pairs={{0,8},{1,9},{2,10},{3,11},{4,12},{5,13},{6,14},{7,15},{8,0},{9,1},... | collective-permute-start | bytes 393224 | tf_op jit(solution)/shard_map/ppermute | solution.py:242
  59.0 10.6 %collective-permute-start.27 = (f32[2,128,128]{2,1,0:T(8,128)S(1)}, f32[2,128,128]{2,1,0:T(8,128)S(1)}, u32[]{:S(2)}, u32[]{:S(2)}) collective-permute-start(f32[2,128,128]{2,1,0:T(8,128)S(1)} %step.1.refs_0_.vector_ref), channel_id=1, source_target_pairs={{0,4},{1,5},{2,6},{3,7},{4,0},{5,1},{6,2},{7,3},{8,12},{9,13},{10,... | collective-permute-start | bytes 393224 | tf_op jit(solution)/shard_map/ppermute | solution.py:242
  60.7 9.3 %collective-permute-start.25 = (f32[2,128,128]{2,1,0:T(8,128)S(1)}, f32[2,128,128]{2,1,0:T(8,128)S(1)}, u32[]{:S(2)}, u32[]{:S(2)}) collective-permute-start(f32[2,128,128]{2,1,0:T(8,128)S(1)} %step.1.refs_0_.vector_ref), channel_id=1, source_target_pairs={{0,2},{1,3},{2,0},{3,1},{4,6},{5,7},{6,4},{7,5},{8,10},{9,11},{10,... | collective-permute-start | bytes 393224 | tf_op jit(solution)/shard_map/ppermute | solution.py:242
  61.3 8.9 %collective-permute-start.24 = (f32[2,128,128]{2,1,0:T(8,128)S(1)}, f32[2,128,128]{2,1,0:T(8,128)S(1)}, u32[]{:S(2)}, u32[]{:S(2)}) collective-permute-start(f32[2,128,128]{2,1,0:T(8,128)S(1)} %step.1.refs_0_.vector_ref), channel_id=1, source_target_pairs={{0,1},{1,0},{2,3},{3,2},{4,5},{5,4},{6,7},{7,6},{8,9},{9,8},{10,11... | collective-permute-start | bytes 393224 | tf_op jit(solution)/shard_map/ppermute | solution.py:242
  64.6 5.8 %collective-permute-start.37 = (f32[2,128,128]{2,1,0:T(8,128)S(1)}, f32[2,128,128]{2,1,0:T(8,128)S(1)}, u32[]{:S(2)}, u32[]{:S(2)}) collective-permute-start(f32[2,128,128]{2,1,0:T(8,128)S(1)} %collective-permute-done.35.refs_12_), channel_id=1, source_target_pairs={{0,2},{1,3},{2,0},{3,1},{4,6},{5,7},{6,4},{7,5},{8,10},{9,11},{10,... | collective-permute-start | bytes 393224 | tf_op jit(solution)/shard_map/ppermute | solution.py:242
  69.6 1.3 %collective-permute-start.36 = (f32[2,128,128]{2,1,0:T(8,128)S(1)}, f32[2,128,128]{2,1,0:T(8,128)S(1)}, u32[]{:S(2)}, u32[]{:S(2)}) collective-permute-start(f32[2,128,128]{2,1,0:T(8,128)S(1)} %collective-permute-done.35.refs_12_), channel_id=1, source_target_pairs={{0,1},{1,0},{2,3},{3,2},{4,5},{5,4},{6,7},{7,6},{8,9},{9,8},{10,11... | collective-permute-start | bytes 393224 | tf_op jit(solution)/shard_map/ppermute | solution.py:242
  69.6 5.9 %collective-permute-start.33 = (f32[2,128,128]{2,1,0:T(8,128)S(1)}, f32[2,128,128]{2,1,0:T(8,128)S(1)}, u32[]{:S(2)}, u32[]{:S(2)}) collective-permute-start(f32[2,128,128]{2,1,0:T(8,128)S(1)} %collective-permute-done.31.refs_8_), channel_id=1, source_target_pairs={{0,2},{1,3},{2,0},{3,1},{4,6},{5,7},{6,4},{7,5},{8,10},{9,11},{10,... | collective-permute-start | bytes 393224 | tf_op jit(solution)/shard_map/ppermute | solution.py:242
  70.0 5.5 %collective-permute-start.32 = (f32[2,128,128]{2,1,0:T(8,128)S(1)}, f32[2,128,128]{2,1,0:T(8,128)S(1)}, u32[]{:S(2)}, u32[]{:S(2)}) collective-permute-start(f32[2,128,128]{2,1,0:T(8,128)S(1)} %collective-permute-done.31.refs_8_), channel_id=1, source_target_pairs={{0,1},{1,0},{2,3},{3,2},{4,5},{5,4},{6,7},{7,6},{8,9},{9,8},{10,11... | collective-permute-start | bytes 393224 | tf_op jit(solution)/shard_map/ppermute | solution.py:242
  70.2 5.8 %collective-permute-start.29 = (f32[2,128,128]{2,1,0:T(8,128)S(1)}, f32[2,128,128]{2,1,0:T(8,128)S(1)}, u32[]{:S(2)}, u32[]{:S(2)}) collective-permute-start(f32[2,128,128]{2,1,0:T(8,128)S(1)} %collective-permute-done.25.refs_2_), channel_id=1, source_target_pairs={{0,4},{1,5},{2,6},{3,7},{4,0},{5,1},{6,2},{7,3},{8,12},{9,13},{10,... | collective-permute-start | bytes 393224 | tf_op jit(solution)/shard_map/ppermute | solution.py:242
  70.3 5.7 %collective-permute-start.26 = (f32[2,128,128]{2,1,0:T(8,128)S(1)}, f32[2,128,128]{2,1,0:T(8,128)S(1)}, u32[]{:S(2)}, u32[]{:S(2)}) collective-permute-start(f32[2,128,128]{2,1,0:T(8,128)S(1)} %collective-permute-done.25.refs_2_), channel_id=1, source_target_pairs={{0,1},{1,0},{2,3},{3,2},{4,5},{5,4},{6,7},{7,6},{8,9},{9,8},{10,11... | collective-permute-start | bytes 393224 | tf_op jit(solution)/shard_map/ppermute | solution.py:242
  70.9 5.2 %collective-permute-start.28 = (f32[2,128,128]{2,1,0:T(8,128)S(1)}, f32[2,128,128]{2,1,0:T(8,128)S(1)}, u32[]{:S(2)}, u32[]{:S(2)}) collective-permute-start(f32[2,128,128]{2,1,0:T(8,128)S(1)} %collective-permute-done.27.refs_4_), channel_id=1, source_target_pairs={{0,1},{1,0},{2,3},{3,2},{4,5},{5,4},{6,7},{7,6},{8,9},{9,8},{10,11... | collective-permute-start | bytes 393224 | tf_op jit(solution)/shard_map/ppermute | solution.py:242
  75.5 1.3 %collective-permute-start.38 = (f32[2,128,128]{2,1,0:T(8,128)S(1)}, f32[2,128,128]{2,1,0:T(8,128)S(1)}, u32[]{:S(2)}, u32[]{:S(2)}) collective-permute-start(f32[2,128,128]{2,1,0:T(8,128)S(1)} %collective-permute-done.37.refs_14_), channel_id=1, source_target_pairs={{0,1},{1,0},{2,3},{3,2},{4,5},{5,4},{6,7},{7,6},{8,9},{9,8},{10,11... | collective-permute-start | bytes 393224 | tf_op jit(solution)/shard_map/ppermute | solution.py:242
  75.5 1.5 %collective-permute-start.34 = (f32[2,128,128]{2,1,0:T(8,128)S(1)}, f32[2,128,128]{2,1,0:T(8,128)S(1)}, u32[]{:S(2)}, u32[]{:S(2)}) collective-permute-start(f32[2,128,128]{2,1,0:T(8,128)S(1)} %collective-permute-done.33.refs_10_), channel_id=1, source_target_pairs={{0,1},{1,0},{2,3},{3,2},{4,5},{5,4},{6,7},{7,6},{8,9},{9,8},{10,11... | collective-permute-start | bytes 393224 | tf_op jit(solution)/shard_map/ppermute | solution.py:242
  76.0 1.3 %collective-permute-start.30 = (f32[2,128,128]{2,1,0:T(8,128)S(1)}, f32[2,128,128]{2,1,0:T(8,128)S(1)}, u32[]{:S(2)}, u32[]{:S(2)}) collective-permute-start(f32[2,128,128]{2,1,0:T(8,128)S(1)} %collective-permute-done.29.refs_6_), channel_id=1, source_target_pairs={{0,1},{1,0},{2,3},{3,2},{4,5},{5,4},{6,7},{7,6},{8,9},{9,8},{10,11... | collective-permute-start | bytes 393224 | tf_op jit(solution)/shard_map/ppermute | solution.py:242
  83.5 8.3 %collective-permute-start.39 = (f32[648,128]{1,0:T(8,128)S(1)}, f32[648,128]{1,0:T(8,128)S(1)}, u32[]{:S(2)}, u32[]{:S(2)}) collective-permute-start(f32[648,128]{1,0:T(8,128)S(1)} %get-tuple-element.54.far_in), channel_id=1, source_target_pairs={{0,1},{1,0},{2,3},{3,2},{4,5},{5,4},{6,7},{7,6},{8,9},{9,8},{10,11... | collective-permute-start | bytes 995336 | tf_op jit(solution)/shard_map/ppermute | solution.py:242
  83.8 7.2 %collective-permute-start.40 = (f32[264,128]{1,0:T(8,128)S(1)}, f32[264,128]{1,0:T(8,128)S(1)}, u32[]{:S(2)}, u32[]{:S(2)}) collective-permute-start(f32[264,128]{1,0:T(8,128)S(1)} %get-tuple-element.55), channel_id=1, source_target_pairs={{0,2},{1,3},{2,0},{3,1},{4,6},{5,7},{6,4},{7,5},{8,10},{9,11},{10,... | collective-permute-start | bytes 405512 | tf_op jit(solution)/shard_map/ppermute | solution.py:242
  85.3 6.4 %collective-permute-start.41 = (f32[264,128]{1,0:T(8,128)S(1)}, f32[264,128]{1,0:T(8,128)S(1)}, u32[]{:S(2)}, u32[]{:S(2)}) collective-permute-start(f32[264,128]{1,0:T(8,128)S(1)} %get-tuple-element.56), channel_id=1, source_target_pairs={{0,3},{1,2},{2,1},{3,0},{4,7},{5,6},{6,5},{7,4},{8,11},{9,10},{10,... | collective-permute-start | bytes 405512 | tf_op jit(solution)/shard_map/ppermute | solution.py:242
  85.4 4.9 %collective-permute-start.42 = (f32[128,128]{1,0:T(8,128)S(1)}, f32[128,128]{1,0:T(8,128)S(1)}, u32[]{:S(2)}, u32[]{:S(2)}) collective-permute-start(f32[128,128]{1,0:T(8,128)S(1)} %get-tuple-element.57), channel_id=1, source_target_pairs={{0,4},{1,5},{2,6},{3,7},{4,0},{5,1},{6,2},{7,3},{8,12},{9,13},{10,... | collective-permute-start | bytes 196616 | tf_op jit(solution)/shard_map/ppermute | solution.py:242
  85.8 5.2 %collective-permute-start.43 = (f32[128,128]{1,0:T(8,128)S(1)}, f32[128,128]{1,0:T(8,128)S(1)}, u32[]{:S(2)}, u32[]{:S(2)}) collective-permute-start(f32[128,128]{1,0:T(8,128)S(1)} %get-tuple-element.58), channel_id=1, source_target_pairs={{0,5},{1,4},{2,7},{3,6},{4,1},{5,0},{6,3},{7,2},{8,13},{9,12},{10,... | collective-permute-start | bytes 196616 | tf_op jit(solution)/shard_map/ppermute | solution.py:242
  92.5 9.5 %collective-permute-start.45 = (f32[264,128]{1,0:T(8,128)S(1)}, f32[264,128]{1,0:T(8,128)S(1)}, u32[]{:S(2)}, u32[]{:S(2)}) collective-permute-start(f32[264,128]{1,0:T(8,128)S(1)} %get-tuple-element.63), channel_id=1, source_target_pairs={{0,12},{1,13},{2,14},{3,15},{4,8},{5,9},{6,10},{7,11},{8,4},{9,5},... | collective-permute-start | bytes 405512 | tf_op jit(solution)/shard_map/ppermute | solution.py:242
  94.7 12.4 %collective-permute-start.46 = (f32[264,128]{1,0:T(8,128)S(1)}, f32[264,128]{1,0:T(8,128)S(1)}, u32[]{:S(2)}, u32[]{:S(2)}) collective-permute-start(f32[264,128]{1,0:T(8,128)S(1)} %get-tuple-element.64), channel_id=1, source_target_pairs={{0,8},{1,9},{2,10},{3,11},{4,12},{5,13},{6,14},{7,15},{8,0},{9,1},... | collective-permute-start | bytes 405512 | tf_op jit(solution)/shard_map/ppermute | solution.py:242
  94.7 12.4 %collective-permute-start.47 = (f32[264,128]{1,0:T(8,128)S(1)}, f32[264,128]{1,0:T(8,128)S(1)}, u32[]{:S(2)}, u32[]{:S(2)}) collective-permute-start(f32[264,128]{1,0:T(8,128)S(1)} %get-tuple-element.62.refs_0_), channel_id=1, source_target_pairs={{0,4},{1,5},{2,6},{3,7},{4,0},{5,1},{6,2},{7,3},{8,12},{9,13},{10,... | collective-permute-start | bytes 405512 | tf_op jit(solution)/shard_map/ppermute | solution.py:242
  96.9 5.1 %collective-permute-start.44 = (f32[2,128,128]{2,1,0:T(8,128)S(1)}, f32[2,128,128]{2,1,0:T(8,128)S(1)}, u32[]{:S(2)}, u32[]{:S(2)}) collective-permute-start(f32[2,128,128]{2,1,0:T(8,128)S(1)} %get-tuple-element.60), channel_id=1, source_target_pairs={{0,2},{1,3},{2,0},{3,1},{4,6},{5,7},{6,4},{7,5},{8,10},{9,11},{10,... | collective-permute-start | bytes 393224 | tf_op jit(solution)/shard_map/ppermute | solution.py:242

commit v12 on v11

--- a/solution.py
+++ b/solution.py
@@ -355,9 +355,13 @@
     pieces[COLUMN] = swapped(x, COLUMN)
     if held is not None:
         pieces[n - 4], pieces[0] = lax.optimization_barrier((pieces[n - 4], held))
+    else:
+        pieces[COLUMN + ROW] = swapped(x, COLUMN + ROW)
+        pieces[0], pieces[8] = lax.optimization_barrier((pieces[0], pieces[8]))
     for k in reversed(range(8, n, 4)):
         pieces[k + ROW] = swapped(pieces[k], ROW)
-    pieces[COLUMN + ROW] = swapped(pieces[ROW], COLUMN)
+    if held is not None:
+        pieces[COLUMN + ROW] = swapped(pieces[ROW], COLUMN)
     for k in range(0, n, 2):
         pieces[k + CORE] = swapped(pieces[k], CORE)
     return [pieces[k] for k in range(n)]

time: 120 us -> 121 us (level)
  waiting for transfers between devices: 50.8 us -> 54 us
  blocking collectives: 10.8 us -> 9.47 us
    ppermute x48, waiting for transfers between devices: 50.8 us -> 54 us  [swapped(): return lax.ppermute(x, 'term', [(i, i ^ k) for i in range(n)])]
    all_to_all x1, blocking collectives: 10.8 us -> 9.47 us  [shards(): lax.all_to_all(jnp.broadcast_to(partial[None], (n, 8, width)), 'term', sp...]
  transfers between devices with their start and end apart: 48 -> 48, of which waited for: 23 -> 22; matrix products, arithmetic and copies ran while one was open for 0% -> 0% of each run, Pallas kernels for 3% -> 2%
where the time goes in v12:
time: 121 us
  waiting for transfers between devices  54 us (45%)
  starting transfers between devices  37.1 us (31%)
  Pallas kernels  18 us (15%)
  blocking collectives  9.47 us (8%)
  between operations  1.42 us (1%)
    ppermute x48, waiting for transfers between devices, swapped(): return lax.ppermute(x, 'term', [(i, i ^ k) for i in range(n)])  54 us
    ppermute x48, starting transfers between devices, swapped(): return lax.ppermute(x, 'term', [(i, i ^ k) for i in range(n)])  37.1 us
    pallas_call x2, Pallas kernels, apply(): pl.pallas_call(functools.partial(apply_kernel, n, npairs, over_rows, rows...  12 us
    all_to_all x1, blocking collectives, shards(): lax.all_to_all(jnp.broadcast_to(partial[None], (n, 8, width)), 'term', sp...  9.47 us
    pallas_call x5, Pallas kernels, local(): pl.pallas_call(kernel, out_shape=out_shape, in_specs=[SMEM] * len(scalars...  3.42 us
    pallas_call x1, Pallas kernels, prep(): pl.pallas_call(functools.partial(prep_kernel, n, terms * n + 1), out_shap...  2.51 us
  transfers between devices with their start and end apart: 48, of which 22 were waited for; matrix products, arithmetic and copies ran while one was open for 0% of the time, Pallas kernels for 2%

profile of v12, /device:TPU:0, one launch (start us, length us, event | category | flops | bytes accessed | tf_op | source)
XLA Modules:
  0.0 120.7 jit_solution(16205193964102047493)
XLA Ops:
  0.6 3.0 %collective-permute-start.2 = (f32[2,128,128]{2,1,0:T(8,128)}, f32[2,128,128]{2,1,0:T(8,128)S(1)}, u32[]{:S(2)}, u32[]{:S(2)}) collective-permute-start(f32[2,128,128]{2,1,0:T(8,128)} %vector_in.1), channel_id=1, source_target_pairs={{0,2},{1,3},{2,0},{3,1},{4,6},{5,7},{6,4},{7,5},{8,10},{9,11},{10,... | collective-permute-start | bytes 393224 | tf_op jit(solution)/shard_map/ppermute | solution.py:242
  3.7 2.6 %collective-permute-start.8 = (f32[2,128,128]{2,1,0:T(8,128)}, f32[2,128,128]{2,1,0:T(8,128)S(1)}, u32[]{:S(2)}, u32[]{:S(2)}) collective-permute-start(f32[2,128,128]{2,1,0:T(8,128)} %vector_in.1), channel_id=1, source_target_pairs={{0,8},{1,9},{2,10},{3,11},{4,12},{5,13},{6,14},{7,15},{8,0},{9,1},... | collective-permute-start | bytes 393224 | tf_op jit(solution)/shard_map/ppermute | solution.py:242
  6.3 1.3 %collective-permute-start = (f32[2,128,128]{2,1,0:T(8,128)}, f32[2,128,128]{2,1,0:T(8,128)S(1)}, u32[]{:S(2)}, u32[]{:S(2)}) collective-permute-start(f32[2,128,128]{2,1,0:T(8,128)} %vector_in.1), channel_id=1, source_target_pairs={{0,12},{1,13},{2,14},{3,15},{4,8},{5,9},{6,10},{7,11},{8,4},{9,5},... | collective-permute-start | bytes 393224 | tf_op jit(solution)/shard_map/ppermute | solution.py:242
  7.8 1.8 %collective-permute-start.6 = (f32[2,128,128]{2,1,0:T(8,128)S(1)}, f32[2,128,128]{2,1,0:T(8,128)S(1)}, u32[]{:S(2)}, u32[]{:S(2)}) collective-permute-start(f32[2,128,128]{2,1,0:T(8,128)S(1)} %collective-permute-done.2.refs_2_), channel_id=1, source_target_pairs={{0,4},{1,5},{2,6},{3,7},{4,0},{5,1},{6,2},{7,3},{8,12},{9,13},{10,... | collective-permute-start | bytes 393224 | tf_op jit(solution)/shard_map/ppermute | solution.py:242
  10.3 0.6 copy.12
  10.9 2.5 %prep.1 = (bf16[8,128,512]{2,1,0:T(8,128)(2,1)S(1)}, bf16[2048,256]{1,0:T(8,128)(2,1)S(1)}, s32[721]{0:T(1024)S(1)}, f32[2,128,128]{2,1,0:T(8,128)S(1)}) custom-call(s32[1]{0:T(128)} %bitcast.me_ref, s32[16,16]{1,0:T(8,128)} %fetch_in.1, s32[16,16]{1,0:T(8,128)} %store_in.1, s32[384]{0:T(512)} %bitcast.8, s32[1]{0:T(128)S(6)} %copy.13.live_in, ...), custom_call_target="tpu_custom_call" | custom-call | tf_op jit(solution)/shard_map/prep/pallas_call | solution.py:132
  13.5 3.0 %collective-permute-done.8.refs_8_ = f32[2,128,128]{2,1,0:T(8,128)S(1)} collective-permute-done((f32[2,128,128]{2,1,0:T(8,128)}, f32[2,128,128]{2,1,0:T(8,128)S(1)}, u32[]{:S(2)}, u32[]{:S(2)}) %collective-permute-start.8) | collective-permute-done | bytes 131104 | tf_op jit(solution)/shard_map/ppermute | solution.py:242
  16.5 0.4 collective-permute-start.10
  17.0 1.1 collective-permute-done.4.refs_4_
  18.1 1.4 %collective-permute-done.6.refs_6_ = f32[2,128,128]{2,1,0:T(8,128)S(1)} collective-permute-done((f32[2,128,128]{2,1,0:T(8,128)S(1)}, f32[2,128,128]{2,1,0:T(8,128)S(1)}, u32[]{:S(2)}, u32[]{:S(2)}) %collective-permute-start.6) | collective-permute-done | bytes 131104 | tf_op jit(solution)/shard_map/ppermute | solution.py:242
  19.5 0.5 collective-permute-start.13
  20.0 1.8 %collective-permute-done.10.refs_10_ = f32[2,128,128]{2,1,0:T(8,128)S(1)} collective-permute-done((f32[2,128,128]{2,1,0:T(8,128)S(1)}, f32[2,128,128]{2,1,0:T(8,128)S(1)}, u32[]{:S(2)}, u32[]{:S(2)}) %collective-permute-start.10) | collective-permute-done | bytes 131104 | tf_op jit(solution)/shard_map/ppermute | solution.py:242
  21.8 0.5 collective-permute-start.7
  22.3 2.1 %collective-permute-done.13.refs_14_ = f32[2,128,128]{2,1,0:T(8,128)S(1)} collective-permute-done((f32[2,128,128]{2,1,0:T(8,128)S(1)}, f32[2,128,128]{2,1,0:T(8,128)S(1)}, u32[]{:S(2)}, u32[]{:S(2)}) %collective-permute-start.13) | collective-permute-done | bytes 131104 | tf_op jit(solution)/shard_map/ppermute | solution.py:242
  24.5 1.3 %collective-permute-done.14.refs_15_ = f32[2,128,128]{2,1,0:T(8,128)S(1)} collective-permute-done((f32[2,128,128]{2,1,0:T(8,128)S(1)}, f32[2,128,128]{2,1,0:T(8,128)S(1)}, u32[]{:S(2)}, u32[]{:S(2)}) %collective-permute-start.14) | collective-permute-done | bytes 131104 | tf_op jit(solution)/shard_map/ppermute | solution.py:242
  25.8 5.9 %apply.2 = (f32[640,128]{1,0:T(8,128)S(1)}, f32[648,128]{1,0:T(8,128)S(1)}, f32[264,128]{1,0:T(8,128)S(1)}, f32[264,128]{1,0:T(8,128)S(1)}, f32[128,128]{1,0:T(8...) custom-call(s32[721]{0:T(1024)S(1)} %get-tuple-element.37.table_ref, ...), custom_call_target="tpu_custom_call" | custom-call | tf_op jit(solution)/shard_map/apply/pallas_call | solution.py:216
  31.8 0.3 collective-permute-start.15
  32.1 0.4 collective-permute-start.16
  32.5 1.2 collective-permute-start.17
  33.7 0.6 collective-permute-start.18
  34.3 1.3 %collective-permute-start.19 = (f32[128,128]{1,0:T(8,128)S(1)}, f32[128,128]{1,0:T(8,128)S(1)}, u32[]{:S(2)}, u32[]{:S(2)}) collective-permute-start(f32[128,128]{1,0:T(8,128)S(1)} %get-tuple-element.48), channel_id=1, source_target_pairs={{0,5},{1,4},{2,7},{3,6},{4,1},{5,0},{6,3},{7,2},{8,13},{9,12},{10,... | collective-permute-start | bytes 196616 | tf_op jit(solution)/shard_map/ppermute | solution.py:242
  35.6 3.0 %collective-permute-done.18.column_ref = f32[128,128]{1,0:T(8,128)S(1)} collective-permute-done((f32[128,128]{1,0:T(8,128)S(1)}, f32[128,128]{1,0:T(8,128)S(1)}, u32[]{:S(2)}, u32[]{:S(2)}) %collective-permute-start.18) | collective-permute-done | bytes 65568 | tf_op jit(solution)/shard_map/ppermute | solution.py:242
  38.6 0.7 collective-permute-done.19.column_far_ref
  39.3 0.8 collective-permute-done.17.row_far_ref
  40.1 0.7 fold.2
  40.8 3.5 %collective-permute-start.21 = (f32[264,128]{1,0:T(8,128)S(1)}, f32[264,128]{1,0:T(8,128)S(1)}, u32[]{:S(2)}, u32[]{:S(2)}) collective-permute-start(f32[264,128]{1,0:T(8,128)S(1)} %get-tuple-element.53), channel_id=1, source_target_pairs={{0,12},{1,13},{2,14},{3,15},{4,8},{5,9},{6,10},{7,11},{8,4},{9,5},... | collective-permute-start | bytes 405512 | tf_op jit(solution)/shard_map/ppermute | solution.py:242
  44.3 1.0 collective-permute-start.23
  45.3 0.8 collective-permute-start.20
  46.1 4.3 %collective-permute-done.20.step_ref = f32[2,128,128]{2,1,0:T(8,128)S(1)} collective-permute-done((f32[2,128,128]{2,1,0:T(8,128)S(1)}, f32[2,128,128]{2,1,0:T(8,128)S(1)}, u32[]{:S(2)}, u32[]{:S(2)}) %collective-permute-start.20) | collective-permute-done | bytes 131104 | tf_op jit(solution)/shard_map/ppermute | solution.py:242
  50.4 5.7 %collective-permute-done.22.refs_2_ = f32[264,128]{1,0:T(8,128)S(1)} collective-permute-done((f32[264,128]{1,0:T(8,128)S(1)}, f32[264,128]{1,0:T(8,128)S(1)}, u32[]{:S(2)}, u32[]{:S(2)}) %collective-permute-start.22) | collective-permute-done | bytes 135200 | tf_op jit(solution)/shard_map/ppermute | solution.py:242
  56.3 2.7 %collective-permute-start.35 = (f32[2,128,128]{2,1,0:T(8,128)S(1)}, f32[2,128,128]{2,1,0:T(8,128)S(1)}, u32[]{:S(2)}, u32[]{:S(2)}) collective-permute-start(f32[2,128,128]{2,1,0:T(8,128)S(1)} %step.1.refs_0_.vector_ref), channel_id=1, source_target_pairs={{0,12},{1,13},{2,14},{3,15},{4,8},{5,9},{6,10},{7,11},{8,4},{9,5},... | collective-permute-start | bytes 393224 | tf_op jit(solution)/shard_map/ppermute | solution.py:242
  59.0 1.7 %collective-permute-start.30 = (f32[2,128,128]{2,1,0:T(8,128)S(1)}, f32[2,128,128]{2,1,0:T(8,128)S(1)}, u32[]{:S(2)}, u32[]{:S(2)}) collective-permute-start(f32[2,128,128]{2,1,0:T(8,128)S(1)} %step.1.refs_0_.vector_ref), channel_id=1, source_target_pairs={{0,6},{1,7},{2,4},{3,5},{4,2},{5,3},{6,0},{7,1},{8,14},{9,15},{10,... | collective-permute-start | bytes 393224 | tf_op jit(solution)/shard_map/ppermute | solution.py:242
  60.6 0.3 collective-permute-start.28
  60.9 1.6 %collective-permute-start.26 = (f32[2,128,128]{2,1,0:T(8,128)S(1)}, f32[2,128,128]{2,1,0:T(8,128)S(1)}, u32[]{:S(2)}, u32[]{:S(2)}) collective-permute-start(f32[2,128,128]{2,1,0:T(8,128)S(1)} %step.1.refs_0_.vector_ref), channel_id=1, source_target_pairs={{0,2},{1,3},{2,0},{3,1},{4,6},{5,7},{6,4},{7,5},{8,10},{9,11},{10,... | collective-permute-start | bytes 393224 | tf_op jit(solution)/shard_map/ppermute | solution.py:242
  62.5 2.1 %collective-permute-done.35.refs_12_ = f32[2,128,128]{2,1,0:T(8,128)S(1)} collective-permute-done((f32[2,128,128]{2,1,0:T(8,128)S(1)}, f32[2,128,128]{2,1,0:T(8,128)S(1)}, u32[]{:S(2)}, u32[]{:S(2)}) %collective-permute-start.35) | collective-permute-done | bytes 131104 | tf_op jit(solution)/shard_map/ppermute | solution.py:242
  64.6 0.5 collective-permute-start.37
  65.1 4.6 %collective-permute-done.24.refs_8_ = f32[2,128,128]{2,1,0:T(8,128)S(1)} collective-permute-done((f32[2,128,128]{2,1,0:T(8,128)S(1)}, f32[2,128,128]{2,1,0:T(8,128)S(1)}, u32[]{:S(2)}, u32[]{:S(2)}) %collective-permute-start.24) | collective-permute-done | bytes 131104 | tf_op jit(solution)/shard_map/ppermute | solution.py:242
  69.7 0.5 collective-permute-start.31
  70.2 1.9 %collective-permute-done.28.refs_4_ = f32[2,128,128]{2,1,0:T(8,128)S(1)} collective-permute-done((f32[2,128,128]{2,1,0:T(8,128)S(1)}, f32[2,128,128]{2,1,0:T(8,128)S(1)}, u32[]{:S(2)}, u32[]{:S(2)}) %collective-permute-start.28) | collective-permute-done | bytes 131104 | tf_op jit(solution)/shard_map/ppermute | solution.py:242
  72.0 0.3 collective-permute-start.33
  72.4 0.2 collective-permute-start.32
  72.6 0.3 collective-permute-start.25
  72.9 0.2 collective-permute-start.27
  73.1 0.2 collective-permute-done.29.refs_5_
  73.5 4.4 %collective-permute-done.33.refs_10_ = f32[2,128,128]{2,1,0:T(8,128)S(1)} collective-permute-done((f32[2,128,128]{2,1,0:T(8,128)S(1)}, f32[2,128,128]{2,1,0:T(8,128)S(1)}, u32[]{:S(2)}, u32[]{:S(2)}) %collective-permute-start.33) | collective-permute-done | bytes 131104 | tf_op jit(solution)/shard_map/ppermute | solution.py:242
  78.0 1.3 %collective-permute-done.34.refs_11_ = f32[2,128,128]{2,1,0:T(8,128)S(1)} collective-permute-done((f32[2,128,128]{2,1,0:T(8,128)S(1)}, f32[2,128,128]{2,1,0:T(8,128)S(1)}, u32[]{:S(2)}, u32[]{:S(2)}) %collective-permute-start.34) | collective-permute-done | bytes 131104 | tf_op jit(solution)/shard_map/ppermute | solution.py:242
  79.3 6.1 %apply.3 = (f32[640,128]{1,0:T(8,128)S(1)}, f32[648,128]{1,0:T(8,128)S(1)}, f32[264,128]{1,0:T(8,128)S(1)}, f32[264,128]{1,0:T(8,128)S(1)}, f32[128,128]{1,0:T(8...) custom-call(s32[721]{0:T(1024)S(1)} %get-tuple-element.37.table_ref, ...), custom_call_target="tpu_custom_call" | custom-call | tf_op jit(solution)/shard_map/apply/pallas_call | solution.py:216
  85.4 0.3 collective-permute-start.39
  85.7 0.3 collective-permute-start.40
  86.0 1.3 %collective-permute-start.41 = (f32[264,128]{1,0:T(8,128)S(1)}, f32[264,128]{1,0:T(8,128)S(1)}, u32[]{:S(2)}, u32[]{:S(2)}) collective-permute-start(f32[264,128]{1,0:T(8,128)S(1)} %get-tuple-element.60), channel_id=1, source_target_pairs={{0,3},{1,2},{2,1},{3,0},{4,7},{5,6},{6,5},{7,4},{8,11},{9,10},{10,... | collective-permute-start | bytes 405512 | tf_op jit(solution)/shard_map/ppermute | solution.py:242
  87.3 0.8 collective-permute-start.42
  88.1 1.1 collective-permute-start.43
  89.2 3.0 %collective-permute-done.42.column_ref = f32[128,128]{1,0:T(8,128)S(1)} collective-permute-done((f32[128,128]{1,0:T(8,128)S(1)}, f32[128,128]{1,0:T(8,128)S(1)}, u32[]{:S(2)}, u32[]{:S(2)}) %collective-permute-start.42) | collective-permute-done | bytes 65568 | tf_op jit(solution)/shard_map/ppermute | solution.py:242
  92.2 0.7 collective-permute-done.43.column_far_ref
  92.9 0.7 collective-permute-done.41.row_far_ref
  93.7 0.7 fold.3
  94.4 2.4 %collective-permute-start.45 = (f32[264,128]{1,0:T(8,128)S(1)}, f32[264,128]{1,0:T(8,128)S(1)}, u32[]{:S(2)}, u32[]{:S(2)}) collective-permute-start(f32[264,128]{1,0:T(8,128)S(1)} %get-tuple-element.67), channel_id=1, source_target_pairs={{0,12},{1,13},{2,14},{3,15},{4,8},{5,9},{6,10},{7,11},{8,4},{9,5},... | collective-permute-start | bytes 405512 | tf_op jit(solution)/shard_map/ppermute | solution.py:242
  97.0 1.9 %collective-permute-start.47 = (f32[264,128]{1,0:T(8,128)S(1)}, f32[264,128]{1,0:T(8,128)S(1)}, u32[]{:S(2)}, u32[]{:S(2)}) collective-permute-start(f32[264,128]{1,0:T(8,128)S(1)} %get-tuple-element.66.refs_0_), channel_id=1, source_target_pairs={{0,4},{1,5},{2,6},{3,7},{4,0},{5,1},{6,2},{7,3},{8,12},{9,13},{10,... | collective-permute-start | bytes 405512 | tf_op jit(solution)/shard_map/ppermute | solution.py:242
  98.9 0.8 collective-permute-start.44
  99.6 4.3 %collective-permute-done.44.step_ref = f32[2,128,128]{2,1,0:T(8,128)S(1)} collective-permute-done((f32[2,128,128]{2,1,0:T(8,128)S(1)}, f32[2,128,128]{2,1,0:T(8,128)S(1)}, u32[]{:S(2)}, u32[]{:S(2)}) %collective-permute-start.44) | collective-permute-done | bytes 131104 | tf_op jit(solution)/shard_map/ppermute | solution.py:242
  103.9 5.5 %collective-permute-done.46.refs_2_ = f32[264,128]{1,0:T(8,128)S(1)} collective-permute-done((f32[264,128]{1,0:T(8,128)S(1)}, f32[264,128]{1,0:T(8,128)S(1)}, u32[]{:S(2)}, u32[]{:S(2)}) %collective-permute-start.46) | collective-permute-done | bytes 135200 | tf_op jit(solution)/shard_map/ppermute | solution.py:242
  109.4 0.9 last.1
  110.3 9.5 %all_to_all.5.tiles_ref = f32[16,8,128]{2,1,0:T(8,128)S(1)} all-to-all(f32[16,8,128]{2,1,0:T(8,128)S(1)} %broadcast_in_dim.2), channel_id=1, replica_groups=mesh['group'=2,'term'=16] {'term'}, dimensions={0} | all-to-all | bytes 131072 | tf_op jit(solution)/shard_map/all_to_all | solution.py:388
  119.8 0.9 norm.1
  (47 shorter events, 1.0 us)
Async XLA Ops:
  0.6 7.2 %collective-permute-start.2 = (f32[2,128,128]{2,1,0:T(8,128)}, f32[2,128,128]{2,1,0:T(8,128)S(1)}, u32[]{:S(2)}, u32[]{:S(2)}) collective-permute-start(f32[2,128,128]{2,1,0:T(8,128)} %vector_in.1), channel_id=1, source_target_pairs={{0,2},{1,3},{2,0},{3,1},{4,6},{5,7},{6,4},{7,5},{8,10},{9,11},{10,... | collective-permute-start | bytes 393224 | tf_op jit(solution)/shard_map/ppermute | solution.py:242
  3.7 12.9 %collective-permute-start.8 = (f32[2,128,128]{2,1,0:T(8,128)}, f32[2,128,128]{2,1,0:T(8,128)S(1)}, u32[]{:S(2)}, u32[]{:S(2)}) collective-permute-start(f32[2,128,128]{2,1,0:T(8,128)} %vector_in.1), channel_id=1, source_target_pairs={{0,8},{1,9},{2,10},{3,11},{4,12},{5,13},{6,14},{7,15},{8,0},{9,1},... | collective-permute-start | bytes 393224 | tf_op jit(solution)/shard_map/ppermute | solution.py:242
  6.3 10.7 %collective-permute-start = (f32[2,128,128]{2,1,0:T(8,128)}, f32[2,128,128]{2,1,0:T(8,128)S(1)}, u32[]{:S(2)}, u32[]{:S(2)}) collective-permute-start(f32[2,128,128]{2,1,0:T(8,128)} %vector_in.1), channel_id=1, source_target_pairs={{0,12},{1,13},{2,14},{3,15},{4,8},{5,9},{6,10},{7,11},{8,4},{9,5},... | collective-permute-start | bytes 393224 | tf_op jit(solution)/shard_map/ppermute | solution.py:242
  7.6 10.5 %collective-permute-start.4 = (f32[2,128,128]{2,1,0:T(8,128)}, f32[2,128,128]{2,1,0:T(8,128)S(1)}, u32[]{:S(2)}, u32[]{:S(2)}) collective-permute-start(f32[2,128,128]{2,1,0:T(8,128)} %vector_in.1), channel_id=1, source_target_pairs={{0,4},{1,5},{2,6},{3,7},{4,0},{5,1},{6,2},{7,3},{8,12},{9,13},{10,... | collective-permute-start | bytes 393224 | tf_op jit(solution)/shard_map/ppermute | solution.py:242
  7.8 11.7 %collective-permute-start.6 = (f32[2,128,128]{2,1,0:T(8,128)S(1)}, f32[2,128,128]{2,1,0:T(8,128)S(1)}, u32[]{:S(2)}, u32[]{:S(2)}) collective-permute-start(f32[2,128,128]{2,1,0:T(8,128)S(1)} %collective-permute-done.2.refs_2_), channel_id=1, source_target_pairs={{0,4},{1,5},{2,6},{3,7},{4,0},{5,1},{6,2},{7,3},{8,12},{9,13},{10,... | collective-permute-start | bytes 393224 | tf_op jit(solution)/shard_map/ppermute | solution.py:242
  9.6 0.7 copy-start.1
  13.4 6.6 %collective-permute-start.3 = (f32[2,128,128]{2,1,0:T(8,128)S(1)}, f32[2,128,128]{2,1,0:T(8,128)S(1)}, u32[]{:S(2)}, u32[]{:S(2)}) collective-permute-start(f32[2,128,128]{2,1,0:T(8,128)S(1)} %collective-permute-done.2.refs_2_), channel_id=1, source_target_pairs={{0,1},{1,0},{2,3},{3,2},{4,5},{5,4},{6,7},{7,6},{8,9},{9,8},{10,11... | collective-permute-start | bytes 393224 | tf_op jit(solution)/shard_map/ppermute | solution.py:242
  16.5 5.2 %collective-permute-start.10 = (f32[2,128,128]{2,1,0:T(8,128)S(1)}, f32[2,128,128]{2,1,0:T(8,128)S(1)}, u32[]{:S(2)}, u32[]{:S(2)}) collective-permute-start(f32[2,128,128]{2,1,0:T(8,128)S(1)} %collective-permute-done.8.refs_8_), channel_id=1, source_target_pairs={{0,2},{1,3},{2,0},{3,1},{4,6},{5,7},{6,4},{7,5},{8,10},{9,11},{10,... | collective-permute-start | bytes 393224 | tf_op jit(solution)/shard_map/ppermute | solution.py:242
  17.0 4.8 %collective-permute-start.9 = (f32[2,128,128]{2,1,0:T(8,128)S(1)}, f32[2,128,128]{2,1,0:T(8,128)S(1)}, u32[]{:S(2)}, u32[]{:S(2)}) collective-permute-start(f32[2,128,128]{2,1,0:T(8,128)S(1)} %collective-permute-done.8.refs_8_), channel_id=1, source_target_pairs={{0,1},{1,0},{2,3},{3,2},{4,5},{5,4},{6,7},{7,6},{8,9},{9,8},{10,11... | collective-permute-start | bytes 393224 | tf_op jit(solution)/shard_map/ppermute | solution.py:242
  18.1 4.2 %collective-permute-start.5 = (f32[2,128,128]{2,1,0:T(8,128)S(1)}, f32[2,128,128]{2,1,0:T(8,128)S(1)}, u32[]{:S(2)}, u32[]{:S(2)}) collective-permute-start(f32[2,128,128]{2,1,0:T(8,128)S(1)} %collective-permute-done.4.refs_4_), channel_id=1, source_target_pairs={{0,1},{1,0},{2,3},{3,2},{4,5},{5,4},{6,7},{7,6},{8,9},{9,8},{10,11... | collective-permute-start | bytes 393224 | tf_op jit(solution)/shard_map/ppermute | solution.py:242
  19.5 5.0 %collective-permute-start.13 = (f32[2,128,128]{2,1,0:T(8,128)S(1)}, f32[2,128,128]{2,1,0:T(8,128)S(1)}, u32[]{:S(2)}, u32[]{:S(2)}) collective-permute-start(f32[2,128,128]{2,1,0:T(8,128)S(1)} %collective-permute-done.refs_12_), channel_id=1, source_target_pairs={{0,2},{1,3},{2,0},{3,1},{4,6},{5,7},{6,4},{7,5},{8,10},{9,11},{10,... | collective-permute-start | bytes 393224 | tf_op jit(solution)/shard_map/ppermute | solution.py:242
  20.0 4.5 %collective-permute-start.12 = (f32[2,128,128]{2,1,0:T(8,128)S(1)}, f32[2,128,128]{2,1,0:T(8,128)S(1)}, u32[]{:S(2)}, u32[]{:S(2)}) collective-permute-start(f32[2,128,128]{2,1,0:T(8,128)S(1)} %collective-permute-done.refs_12_), channel_id=1, source_target_pairs={{0,1},{1,0},{2,3},{3,2},{4,5},{5,4},{6,7},{7,6},{8,9},{9,8},{10,11... | collective-permute-start | bytes 393224 | tf_op jit(solution)/shard_map/ppermute | solution.py:242
  21.8 2.7 %collective-permute-start.1 = (f32[2,128,128]{2,1,0:T(8,128)S(1)}, f32[2,128,128]{2,1,0:T(8,128)S(1)}, u32[]{:S(2)}, u32[]{:S(2)}) collective-permute-start(f32[2,128,128]{2,1,0:T(8,128)S(1)} %get-tuple-element.41.refs_0_.vector_ref), channel_id=1, source_target_pairs={{0,1},{1,0},{2,3},{3,2},{4,5},{5,4},{6,7},{7,6},{8,9},{9,8},{10,11... | collective-permute-start | bytes 393224 | tf_op jit(solution)/shard_map/ppermute | solution.py:242
  21.8 2.7 %collective-permute-start.7 = (f32[2,128,128]{2,1,0:T(8,128)S(1)}, f32[2,128,128]{2,1,0:T(8,128)S(1)}, u32[]{:S(2)}, u32[]{:S(2)}) collective-permute-start(f32[2,128,128]{2,1,0:T(8,128)S(1)} %collective-permute-done.6.refs_6_), channel_id=1, source_target_pairs={{0,1},{1,0},{2,3},{3,2},{4,5},{5,4},{6,7},{7,6},{8,9},{9,8},{10,11... | collective-permute-start | bytes 393224 | tf_op jit(solution)/shard_map/ppermute | solution.py:242
  22.3 2.2 %collective-permute-start.11 = (f32[2,128,128]{2,1,0:T(8,128)S(1)}, f32[2,128,128]{2,1,0:T(8,128)S(1)}, u32[]{:S(2)}, u32[]{:S(2)}) collective-permute-start(f32[2,128,128]{2,1,0:T(8,128)S(1)} %collective-permute-done.10.refs_10_), channel_id=1, source_target_pairs={{0,1},{1,0},{2,3},{3,2},{4,5},{5,4},{6,7},{7,6},{8,9},{9,8},{10,11... | collective-permute-start | bytes 393224 | tf_op jit(solution)/shard_map/ppermute | solution.py:242
  24.5 1.3 %collective-permute-start.14 = (f32[2,128,128]{2,1,0:T(8,128)S(1)}, f32[2,128,128]{2,1,0:T(8,128)S(1)}, u32[]{:S(2)}, u32[]{:S(2)}) collective-permute-start(f32[2,128,128]{2,1,0:T(8,128)S(1)} %collective-permute-done.13.refs_14_), channel_id=1, source_target_pairs={{0,1},{1,0},{2,3},{3,2},{4,5},{5,4},{6,7},{7,6},{8,9},{9,8},{10,11... | collective-permute-start | bytes 393224 | tf_op jit(solution)/shard_map/ppermute | solution.py:242
  31.8 8.3 %collective-permute-start.15 = (f32[648,128]{1,0:T(8,128)S(1)}, f32[648,128]{1,0:T(8,128)S(1)}, u32[]{:S(2)}, u32[]{:S(2)}) collective-permute-start(f32[648,128]{1,0:T(8,128)S(1)} %get-tuple-element.44.far_in), channel_id=1, source_target_pairs={{0,1},{1,0},{2,3},{3,2},{4,5},{5,4},{6,7},{7,6},{8,9},{9,8},{10,11... | collective-permute-start | bytes 995336 | tf_op jit(solution)/shard_map/ppermute | solution.py:242
  32.1 7.2 %collective-permute-start.16 = (f32[264,128]{1,0:T(8,128)S(1)}, f32[264,128]{1,0:T(8,128)S(1)}, u32[]{:S(2)}, u32[]{:S(2)}) collective-permute-start(f32[264,128]{1,0:T(8,128)S(1)} %get-tuple-element.45), channel_id=1, source_target_pairs={{0,2},{1,3},{2,0},{3,1},{4,6},{5,7},{6,4},{7,5},{8,10},{9,11},{10,... | collective-permute-start | bytes 405512 | tf_op jit(solution)/shard_map/ppermute | solution.py:242
  32.5 7.5 %collective-permute-start.17 = (f32[264,128]{1,0:T(8,128)S(1)}, f32[264,128]{1,0:T(8,128)S(1)}, u32[]{:S(2)}, u32[]{:S(2)}) collective-permute-start(f32[264,128]{1,0:T(8,128)S(1)} %get-tuple-element.46), channel_id=1, source_target_pairs={{0,3},{1,2},{2,1},{3,0},{4,7},{5,6},{6,5},{7,4},{8,11},{9,10},{10,... | collective-permute-start | bytes 405512 | tf_op jit(solution)/shard_map/ppermute | solution.py:242
  33.7 4.9 %collective-permute-start.18 = (f32[128,128]{1,0:T(8,128)S(1)}, f32[128,128]{1,0:T(8,128)S(1)}, u32[]{:S(2)}, u32[]{:S(2)}) collective-permute-start(f32[128,128]{1,0:T(8,128)S(1)} %get-tuple-element.47), channel_id=1, source_target_pairs={{0,4},{1,5},{2,6},{3,7},{4,0},{5,1},{6,2},{7,3},{8,12},{9,13},{10,... | collective-permute-start | bytes 196616 | tf_op jit(solution)/shard_map/ppermute | solution.py:242
  34.3 5.0 %collective-permute-start.19 = (f32[128,128]{1,0:T(8,128)S(1)}, f32[128,128]{1,0:T(8,128)S(1)}, u32[]{:S(2)}, u32[]{:S(2)}) collective-permute-start(f32[128,128]{1,0:T(8,128)S(1)} %get-tuple-element.48), channel_id=1, source_target_pairs={{0,5},{1,4},{2,7},{3,6},{4,1},{5,0},{6,3},{7,2},{8,13},{9,12},{10,... | collective-permute-start | bytes 196616 | tf_op jit(solution)/shard_map/ppermute | solution.py:242
  40.1 16.0 %copy-start = (f32[2,128,128]{2,1,0:T(8,128)S(1)}, f32[2,128,128]{2,1,0:T(8,128)}, u32[]{:S(2)}) copy-start(f32[2,128,128]{2,1,0:T(8,128)} %precond_ref.3) | copy-start | bytes 393220
  40.8 9.6 %collective-permute-start.21 = (f32[264,128]{1,0:T(8,128)S(1)}, f32[264,128]{1,0:T(8,128)S(1)}, u32[]{:S(2)}, u32[]{:S(2)}) collective-permute-start(f32[264,128]{1,0:T(8,128)S(1)} %get-tuple-element.53), channel_id=1, source_target_pairs={{0,12},{1,13},{2,14},{3,15},{4,8},{5,9},{6,10},{7,11},{8,4},{9,5},... | collective-permute-start | bytes 405512 | tf_op jit(solution)/shard_map/ppermute | solution.py:242
  44.3 11.8 %collective-permute-start.22 = (f32[264,128]{1,0:T(8,128)S(1)}, f32[264,128]{1,0:T(8,128)S(1)}, u32[]{:S(2)}, u32[]{:S(2)}) collective-permute-start(f32[264,128]{1,0:T(8,128)S(1)} %get-tuple-element.54), channel_id=1, source_target_pairs={{0,8},{1,9},{2,10},{3,11},{4,12},{5,13},{6,14},{7,15},{8,0},{9,1},... | collective-permute-start | bytes 405512 | tf_op jit(solution)/shard_map/ppermute | solution.py:242
  44.3 11.8 %collective-permute-start.23 = (f32[264,128]{1,0:T(8,128)S(1)}, f32[264,128]{1,0:T(8,128)S(1)}, u32[]{:S(2)}, u32[]{:S(2)}) collective-permute-start(f32[264,128]{1,0:T(8,128)S(1)} %get-tuple-element.52.refs_0_), channel_id=1, source_target_pairs={{0,4},{1,5},{2,6},{3,7},{4,0},{5,1},{6,2},{7,3},{8,12},{9,13},{10,... | collective-permute-start | bytes 405512 | tf_op jit(solution)/shard_map/ppermute | solution.py:242
  45.3 5.1 %collective-permute-start.20 = (f32[2,128,128]{2,1,0:T(8,128)S(1)}, f32[2,128,128]{2,1,0:T(8,128)S(1)}, u32[]{:S(2)}, u32[]{:S(2)}) collective-permute-start(f32[2,128,128]{2,1,0:T(8,128)S(1)} %get-tuple-element.50), channel_id=1, source_target_pairs={{0,2},{1,3},{2,0},{3,1},{4,6},{5,7},{6,4},{7,5},{8,10},{9,11},{10,... | collective-permute-start | bytes 393224 | tf_op jit(solution)/shard_map/ppermute | solution.py:242
  56.3 8.3 %collective-permute-start.35 = (f32[2,128,128]{2,1,0:T(8,128)S(1)}, f32[2,128,128]{2,1,0:T(8,128)S(1)}, u32[]{:S(2)}, u32[]{:S(2)}) collective-permute-start(f32[2,128,128]{2,1,0:T(8,128)S(1)} %step.1.refs_0_.vector_ref), channel_id=1, source_target_pairs={{0,12},{1,13},{2,14},{3,15},{4,8},{5,9},{6,10},{7,11},{8,4},{9,5},... | collective-permute-start | bytes 393224 | tf_op jit(solution)/shard_map/ppermute | solution.py:242
  59.0 10.7 %collective-permute-start.24 = (f32[2,128,128]{2,1,0:T(8,128)S(1)}, f32[2,128,128]{2,1,0:T(8,128)S(1)}, u32[]{:S(2)}, u32[]{:S(2)}) collective-permute-start(f32[2,128,128]{2,1,0:T(8,128)S(1)} %step.1.refs_0_.vector_ref), channel_id=1, source_target_pairs={{0,8},{1,9},{2,10},{3,11},{4,12},{5,13},{6,14},{7,15},{8,0},{9,1},... | collective-permute-start | bytes 393224 | tf_op jit(solution)/shard_map/ppermute | solution.py:242
  59.0 10.7 %collective-permute-start.30 = (f32[2,128,128]{2,1,0:T(8,128)S(1)}, f32[2,128,128]{2,1,0:T(8,128)S(1)}, u32[]{:S(2)}, u32[]{:S(2)}) collective-permute-start(f32[2,128,128]{2,1,0:T(8,128)S(1)} %step.1.refs_0_.vector_ref), channel_id=1, source_target_pairs={{0,6},{1,7},{2,4},{3,5},{4,2},{5,3},{6,0},{7,1},{8,14},{9,15},{10,... | collective-permute-start | bytes 393224 | tf_op jit(solution)/shard_map/ppermute | solution.py:242
  60.6 11.4 %collective-permute-start.28 = (f32[2,128,128]{2,1,0:T(8,128)S(1)}, f32[2,128,128]{2,1,0:T(8,128)S(1)}, u32[]{:S(2)}, u32[]{:S(2)}) collective-permute-start(f32[2,128,128]{2,1,0:T(8,128)S(1)} %step.1.refs_0_.vector_ref), channel_id=1, source_target_pairs={{0,4},{1,5},{2,6},{3,7},{4,0},{5,1},{6,2},{7,3},{8,12},{9,13},{10,... | collective-permute-start | bytes 393224 | tf_op jit(solution)/shard_map/ppermute | solution.py:242
  60.9 11.1 %collective-permute-start.26 = (f32[2,128,128]{2,1,0:T(8,128)S(1)}, f32[2,128,128]{2,1,0:T(8,128)S(1)}, u32[]{:S(2)}, u32[]{:S(2)}) collective-permute-start(f32[2,128,128]{2,1,0:T(8,128)S(1)} %step.1.refs_0_.vector_ref), channel_id=1, source_target_pairs={{0,2},{1,3},{2,0},{3,1},{4,6},{5,7},{6,4},{7,5},{8,10},{9,11},{10,... | collective-permute-start | bytes 393224 | tf_op jit(solution)/shard_map/ppermute | solution.py:242
  64.6 7.8 %collective-permute-start.37 = (f32[2,128,128]{2,1,0:T(8,128)S(1)}, f32[2,128,128]{2,1,0:T(8,128)S(1)}, u32[]{:S(2)}, u32[]{:S(2)}) collective-permute-start(f32[2,128,128]{2,1,0:T(8,128)S(1)} %collective-permute-done.35.refs_12_), channel_id=1, source_target_pairs={{0,2},{1,3},{2,0},{3,1},{4,6},{5,7},{6,4},{7,5},{8,10},{9,11},{10,... | collective-permute-start | bytes 393224 | tf_op jit(solution)/shard_map/ppermute | solution.py:242
  69.7 3.0 %collective-permute-start.36 = (f32[2,128,128]{2,1,0:T(8,128)S(1)}, f32[2,128,128]{2,1,0:T(8,128)S(1)}, u32[]{:S(2)}, u32[]{:S(2)}) collective-permute-start(f32[2,128,128]{2,1,0:T(8,128)S(1)} %collective-permute-done.35.refs_12_), channel_id=1, source_target_pairs={{0,1},{1,0},{2,3},{3,2},{4,5},{5,4},{6,7},{7,6},{8,9},{9,8},{10,11... | collective-permute-start | bytes 393224 | tf_op jit(solution)/shard_map/ppermute | solution.py:242
  69.7 3.2 %collective-permute-start.31 = (f32[2,128,128]{2,1,0:T(8,128)S(1)}, f32[2,128,128]{2,1,0:T(8,128)S(1)}, u32[]{:S(2)}, u32[]{:S(2)}) collective-permute-start(f32[2,128,128]{2,1,0:T(8,128)S(1)} %collective-permute-done.30.refs_6_), channel_id=1, source_target_pairs={{0,1},{1,0},{2,3},{3,2},{4,5},{5,4},{6,7},{7,6},{8,9},{9,8},{10,11... | collective-permute-start | bytes 393224 | tf_op jit(solution)/shard_map/ppermute | solution.py:242
  72.0 1.3 %collective-permute-start.29 = (f32[2,128,128]{2,1,0:T(8,128)S(1)}, f32[2,128,128]{2,1,0:T(8,128)S(1)}, u32[]{:S(2)}, u32[]{:S(2)}) collective-permute-start(f32[2,128,128]{2,1,0:T(8,128)S(1)} %collective-permute-done.28.refs_4_), channel_id=1, source_target_pairs={{0,1},{1,0},{2,3},{3,2},{4,5},{5,4},{6,7},{7,6},{8,9},{9,8},{10,11... | collective-permute-start | bytes 393224 | tf_op jit(solution)/shard_map/ppermute | solution.py:242
  72.0 5.9 %collective-permute-start.33 = (f32[2,128,128]{2,1,0:T(8,128)S(1)}, f32[2,128,128]{2,1,0:T(8,128)S(1)}, u32[]{:S(2)}, u32[]{:S(2)}) collective-permute-start(f32[2,128,128]{2,1,0:T(8,128)S(1)} %collective-permute-done.24.refs_8_), channel_id=1, source_target_pairs={{0,2},{1,3},{2,0},{3,1},{4,6},{5,7},{6,4},{7,5},{8,10},{9,11},{10,... | collective-permute-start | bytes 393224 | tf_op jit(solution)/shard_map/ppermute | solution.py:242
  72.4 5.6 %collective-permute-start.32 = (f32[2,128,128]{2,1,0:T(8,128)S(1)}, f32[2,128,128]{2,1,0:T(8,128)S(1)}, u32[]{:S(2)}, u32[]{:S(2)}) collective-permute-start(f32[2,128,128]{2,1,0:T(8,128)S(1)} %collective-permute-done.24.refs_8_), channel_id=1, source_target_pairs={{0,1},{1,0},{2,3},{3,2},{4,5},{5,4},{6,7},{7,6},{8,9},{9,8},{10,11... | collective-permute-start | bytes 393224 | tf_op jit(solution)/shard_map/ppermute | solution.py:242
  72.6 5.3 %collective-permute-start.25 = (f32[2,128,128]{2,1,0:T(8,128)S(1)}, f32[2,128,128]{2,1,0:T(8,128)S(1)}, u32[]{:S(2)}, u32[]{:S(2)}) collective-permute-start(f32[2,128,128]{2,1,0:T(8,128)S(1)} %step.1.refs_0_.vector_ref), channel_id=1, source_target_pairs={{0,1},{1,0},{2,3},{3,2},{4,5},{5,4},{6,7},{7,6},{8,9},{9,8},{10,11... | collective-permute-start | bytes 393224 | tf_op jit(solution)/shard_map/ppermute | solution.py:242
  72.9 5.1 %collective-permute-start.27 = (f32[2,128,128]{2,1,0:T(8,128)S(1)}, f32[2,128,128]{2,1,0:T(8,128)S(1)}, u32[]{:S(2)}, u32[]{:S(2)}) collective-permute-start(f32[2,128,128]{2,1,0:T(8,128)S(1)} %collective-permute-done.26.refs_2_), channel_id=1, source_target_pairs={{0,1},{1,0},{2,3},{3,2},{4,5},{5,4},{6,7},{7,6},{8,9},{9,8},{10,11... | collective-permute-start | bytes 393224 | tf_op jit(solution)/shard_map/ppermute | solution.py:242
  73.4 4.6 %collective-permute-start.38 = (f32[2,128,128]{2,1,0:T(8,128)S(1)}, f32[2,128,128]{2,1,0:T(8,128)S(1)}, u32[]{:S(2)}, u32[]{:S(2)}) collective-permute-start(f32[2,128,128]{2,1,0:T(8,128)S(1)} %collective-permute-done.37.refs_14_), channel_id=1, source_target_pairs={{0,1},{1,0},{2,3},{3,2},{4,5},{5,4},{6,7},{7,6},{8,9},{9,8},{10,11... | collective-permute-start | bytes 393224 | tf_op jit(solution)/shard_map/ppermute | solution.py:242
  77.9 1.3 %collective-permute-start.34 = (f32[2,128,128]{2,1,0:T(8,128)S(1)}, f32[2,128,128]{2,1,0:T(8,128)S(1)}, u32[]{:S(2)}, u32[]{:S(2)}) collective-permute-start(f32[2,128,128]{2,1,0:T(8,128)S(1)} %collective-permute-done.33.refs_10_), channel_id=1, source_target_pairs={{0,1},{1,0},{2,3},{3,2},{4,5},{5,4},{6,7},{7,6},{8,9},{9,8},{10,11... | collective-permute-start | bytes 393224 | tf_op jit(solution)/shard_map/ppermute | solution.py:242
  85.4 8.3 %collective-permute-start.39 = (f32[648,128]{1,0:T(8,128)S(1)}, f32[648,128]{1,0:T(8,128)S(1)}, u32[]{:S(2)}, u32[]{:S(2)}) collective-permute-start(f32[648,128]{1,0:T(8,128)S(1)} %get-tuple-element.58.far_in), channel_id=1, source_target_pairs={{0,1},{1,0},{2,3},{3,2},{4,5},{5,4},{6,7},{7,6},{8,9},{9,8},{10,11... | collective-permute-start | bytes 995336 | tf_op jit(solution)/shard_map/ppermute | solution.py:242
  85.7 7.2 %collective-permute-start.40 = (f32[264,128]{1,0:T(8,128)S(1)}, f32[264,128]{1,0:T(8,128)S(1)}, u32[]{:S(2)}, u32[]{:S(2)}) collective-permute-start(f32[264,128]{1,0:T(8,128)S(1)} %get-tuple-element.59), channel_id=1, source_target_pairs={{0,2},{1,3},{2,0},{3,1},{4,6},{5,7},{6,4},{7,5},{8,10},{9,11},{10,... | collective-permute-start | bytes 405512 | tf_op jit(solution)/shard_map/ppermute | solution.py:242
  86.0 7.6 %collective-permute-start.41 = (f32[264,128]{1,0:T(8,128)S(1)}, f32[264,128]{1,0:T(8,128)S(1)}, u32[]{:S(2)}, u32[]{:S(2)}) collective-permute-start(f32[264,128]{1,0:T(8,128)S(1)} %get-tuple-element.60), channel_id=1, source_target_pairs={{0,3},{1,2},{2,1},{3,0},{4,7},{5,6},{6,5},{7,4},{8,11},{9,10},{10,... | collective-permute-start | bytes 405512 | tf_op jit(solution)/shard_map/ppermute | solution.py:242
  87.3 4.9 %collective-permute-start.42 = (f32[128,128]{1,0:T(8,128)S(1)}, f32[128,128]{1,0:T(8,128)S(1)}, u32[]{:S(2)}, u32[]{:S(2)}) collective-permute-start(f32[128,128]{1,0:T(8,128)S(1)} %get-tuple-element.61), channel_id=1, source_target_pairs={{0,4},{1,5},{2,6},{3,7},{4,0},{5,1},{6,2},{7,3},{8,12},{9,13},{10,... | collective-permute-start | bytes 196616 | tf_op jit(solution)/shard_map/ppermute | solution.py:242
  88.1 4.8 %collective-permute-start.43 = (f32[128,128]{1,0:T(8,128)S(1)}, f32[128,128]{1,0:T(8,128)S(1)}, u32[]{:S(2)}, u32[]{:S(2)}) collective-permute-start(f32[128,128]{1,0:T(8,128)S(1)} %get-tuple-element.62), channel_id=1, source_target_pairs={{0,5},{1,4},{2,7},{3,6},{4,1},{5,0},{6,3},{7,2},{8,13},{9,12},{10,... | collective-permute-start | bytes 196616 | tf_op jit(solution)/shard_map/ppermute | solution.py:242
  94.4 9.5 %collective-permute-start.45 = (f32[264,128]{1,0:T(8,128)S(1)}, f32[264,128]{1,0:T(8,128)S(1)}, u32[]{:S(2)}, u32[]{:S(2)}) collective-permute-start(f32[264,128]{1,0:T(8,128)S(1)} %get-tuple-element.67), channel_id=1, source_target_pairs={{0,12},{1,13},{2,14},{3,15},{4,8},{5,9},{6,10},{7,11},{8,4},{9,5},... | collective-permute-start | bytes 405512 | tf_op jit(solution)/shard_map/ppermute | solution.py:242
  96.8 12.6 %collective-permute-start.46 = (f32[264,128]{1,0:T(8,128)S(1)}, f32[264,128]{1,0:T(8,128)S(1)}, u32[]{:S(2)}, u32[]{:S(2)}) collective-permute-start(f32[264,128]{1,0:T(8,128)S(1)} %get-tuple-element.68), channel_id=1, source_target_pairs={{0,8},{1,9},{2,10},{3,11},{4,12},{5,13},{6,14},{7,15},{8,0},{9,1},... | collective-permute-start | bytes 405512 | tf_op jit(solution)/shard_map/ppermute | solution.py:242
  97.0 12.4 %collective-permute-start.47 = (f32[264,128]{1,0:T(8,128)S(1)}, f32[264,128]{1,0:T(8,128)S(1)}, u32[]{:S(2)}, u32[]{:S(2)}) collective-permute-start(f32[264,128]{1,0:T(8,128)S(1)} %get-tuple-element.66.refs_0_), channel_id=1, source_target_pairs={{0,4},{1,5},{2,6},{3,7},{4,0},{5,1},{6,2},{7,3},{8,12},{9,13},{10,... | collective-permute-start | bytes 405512 | tf_op jit(solution)/shard_map/ppermute | solution.py:242
  98.9 5.1 %collective-permute-start.44 = (f32[2,128,128]{2,1,0:T(8,128)S(1)}, f32[2,128,128]{2,1,0:T(8,128)S(1)}, u32[]{:S(2)}, u32[]{:S(2)}) collective-permute-start(f32[2,128,128]{2,1,0:T(8,128)S(1)} %get-tuple-element.64), channel_id=1, source_target_pairs={{0,2},{1,3},{2,0},{3,1},{4,6},{5,7},{6,4},{7,5},{8,10},{9,11},{10,... | collective-permute-start | bytes 393224 | tf_op jit(solution)/shard_map/ppermute | solution.py:242

commit v13 on v11

--- a/solution.py
+++ b/solution.py
@@ -357,7 +357,10 @@
         pieces[n - 4], pieces[0] = lax.optimization_barrier((pieces[n - 4], held))
     for k in reversed(range(8, n, 4)):
         pieces[k + ROW] = swapped(pieces[k], ROW)
-    pieces[COLUMN + ROW] = swapped(pieces[ROW], COLUMN)
+    pieces[COLUMN + ROW] = swapped(x, COLUMN + ROW) if held is None else swapped(pieces[ROW], COLUMN)
+    if held is None:
+        late = [0, 8, n - 4, n - 4 + ROW]
+        pieces.update(zip(late, lax.optimization_barrier([pieces[k] for k in late])))
     for k in range(0, n, 2):
         pieces[k + CORE] = swapped(pieces[k], CORE)
     return [pieces[k] for k in range(n)]

time: 120 us -> 121 us (level)
  transfers between devices with their start and end apart: 48 -> 48, of which waited for: 23 -> 21; matrix products, arithmetic and copies ran while one was open for 0% -> 0% of each run, Pallas kernels for 3% -> 3%
where the time goes in v13:
time: 121 us
  waiting for transfers between devices  51.6 us (43%)
  starting transfers between devices  36.5 us (30%)
  Pallas kernels  20 us (17%)
  blocking collectives  10.4 us (9%)
  between operations  1.44 us (1%)
    ppermute x48, waiting for transfers between devices, swapped(): return lax.ppermute(x, 'term', [(i, i ^ k) for i in range(n)])  51.6 us
    ppermute x48, starting transfers between devices, swapped(): return lax.ppermute(x, 'term', [(i, i ^ k) for i in range(n)])  36.5 us
    pallas_call x2, Pallas kernels, apply(): pl.pallas_call(functools.partial(apply_kernel, n, npairs, over_rows, rows...  12.4 us
    all_to_all x1, blocking collectives, shards(): lax.all_to_all(jnp.broadcast_to(partial[None], (n, 8, width)), 'term', sp...  10.4 us
    pallas_call x1, Pallas kernels, prep(): pl.pallas_call(functools.partial(prep_kernel, n, terms * n + 1), out_shap...  4.18 us
    pallas_call x5, Pallas kernels, local(): pl.pallas_call(kernel, out_shape=out_shape, in_specs=[SMEM] * len(scalars...  3.42 us
  transfers between devices with their start and end apart: 48, of which 21 were waited for; matrix products, arithmetic and copies ran while one was open for 0% of the time, Pallas kernels for 3%

profile of v13, /device:TPU:0, one launch (start us, length us, event | category | flops | bytes accessed | tf_op | source)
XLA Modules:
  0.0 120.5 jit_solution(15670046639962400018)
XLA Ops:
  0.6 3.0 %collective-permute-start.2 = (f32[2,128,128]{2,1,0:T(8,128)}, f32[2,128,128]{2,1,0:T(8,128)S(1)}, u32[]{:S(2)}, u32[]{:S(2)}) collective-permute-start(f32[2,128,128]{2,1,0:T(8,128)} %vector_in.1), channel_id=1, source_target_pairs={{0,2},{1,3},{2,0},{3,1},{4,6},{5,7},{6,4},{7,5},{8,10},{9,11},{10,... | collective-permute-start | bytes 393224 | tf_op jit(solution)/shard_map/ppermute | solution.py:242
  3.7 2.6 %collective-permute-start.8 = (f32[2,128,128]{2,1,0:T(8,128)}, f32[2,128,128]{2,1,0:T(8,128)S(1)}, u32[]{:S(2)}, u32[]{:S(2)}) collective-permute-start(f32[2,128,128]{2,1,0:T(8,128)} %vector_in.1), channel_id=1, source_target_pairs={{0,8},{1,9},{2,10},{3,11},{4,12},{5,13},{6,14},{7,15},{8,0},{9,1},... | collective-permute-start | bytes 393224 | tf_op jit(solution)/shard_map/ppermute | solution.py:242
  6.3 1.3 %collective-permute-start = (f32[2,128,128]{2,1,0:T(8,128)}, f32[2,128,128]{2,1,0:T(8,128)S(1)}, u32[]{:S(2)}, u32[]{:S(2)}) collective-permute-start(f32[2,128,128]{2,1,0:T(8,128)} %vector_in.1), channel_id=1, source_target_pairs={{0,12},{1,13},{2,14},{3,15},{4,8},{5,9},{6,10},{7,11},{8,4},{9,5},... | collective-permute-start | bytes 393224 | tf_op jit(solution)/shard_map/ppermute | solution.py:242
  7.6 0.2 collective-permute-start.4
  7.8 1.8 %collective-permute-start.6 = (f32[2,128,128]{2,1,0:T(8,128)S(1)}, f32[2,128,128]{2,1,0:T(8,128)S(1)}, u32[]{:S(2)}, u32[]{:S(2)}) collective-permute-start(f32[2,128,128]{2,1,0:T(8,128)S(1)} %collective-permute-done.2.refs_2_), channel_id=1, source_target_pairs={{0,4},{1,5},{2,6},{3,7},{4,0},{5,1},{6,2},{7,3},{8,12},{9,13},{10,... | collective-permute-start | bytes 393224 | tf_op jit(solution)/shard_map/ppermute | solution.py:242
  10.3 0.6 copy.12
  10.9 4.2 %prep.1 = (bf16[8,128,512]{2,1,0:T(8,128)(2,1)S(1)}, bf16[2048,256]{1,0:T(8,128)(2,1)S(1)}, s32[721]{0:T(1024)S(1)}, f32[2,128,128]{2,1,0:T(8,128)S(1)}) custom-call(s32[1]{0:T(128)} %bitcast.me_ref, s32[16,16]{1,0:T(8,128)} %fetch_in.1, s32[16,16]{1,0:T(8,128)} %store_in.1, s32[384]{0:T(512)} %bitcast.8, s32[1]{0:T(128)S(6)} %copy.13.live_in, ...), custom_call_target="tpu_custom_call" | custom-call | tf_op jit(solution)/shard_map/prep/pallas_call | solution.py:132
  15.1 0.1 collective-permute-start.3
  15.2 1.4 %collective-permute-done.8.refs_8_ = f32[2,128,128]{2,1,0:T(8,128)S(1)} collective-permute-done((f32[2,128,128]{2,1,0:T(8,128)}, f32[2,128,128]{2,1,0:T(8,128)S(1)}, u32[]{:S(2)}, u32[]{:S(2)}) %collective-permute-start.8) | collective-permute-done | bytes 131104 | tf_op jit(solution)/shard_map/ppermute | solution.py:242
  16.5 0.4 collective-permute-start.10
  17.0 1.1 collective-permute-done.4.refs_4_
  18.1 1.4 %collective-permute-done.6.refs_6_ = f32[2,128,128]{2,1,0:T(8,128)S(1)} collective-permute-done((f32[2,128,128]{2,1,0:T(8,128)S(1)}, f32[2,128,128]{2,1,0:T(8,128)S(1)}, u32[]{:S(2)}, u32[]{:S(2)}) %collective-permute-start.6) | collective-permute-done | bytes 131104 | tf_op jit(solution)/shard_map/ppermute | solution.py:242
  19.5 0.5 collective-permute-start.13
  20.0 1.8 %collective-permute-done.10.refs_10_ = f32[2,128,128]{2,1,0:T(8,128)S(1)} collective-permute-done((f32[2,128,128]{2,1,0:T(8,128)S(1)}, f32[2,128,128]{2,1,0:T(8,128)S(1)}, u32[]{:S(2)}, u32[]{:S(2)}) %collective-permute-start.10) | collective-permute-done | bytes 131104 | tf_op jit(solution)/shard_map/ppermute | solution.py:242
  21.8 0.5 collective-permute-start.7
  22.3 0.1 collective-permute-start.11
  22.3 2.1 %collective-permute-done.13.refs_14_ = f32[2,128,128]{2,1,0:T(8,128)S(1)} collective-permute-done((f32[2,128,128]{2,1,0:T(8,128)S(1)}, f32[2,128,128]{2,1,0:T(8,128)S(1)}, u32[]{:S(2)}, u32[]{:S(2)}) %collective-permute-start.13) | collective-permute-done | bytes 131104 | tf_op jit(solution)/shard_map/ppermute | solution.py:242
  24.5 1.3 %collective-permute-done.14.refs_15_ = f32[2,128,128]{2,1,0:T(8,128)S(1)} collective-permute-done((f32[2,128,128]{2,1,0:T(8,128)S(1)}, f32[2,128,128]{2,1,0:T(8,128)S(1)}, u32[]{:S(2)}, u32[]{:S(2)}) %collective-permute-start.14) | collective-permute-done | bytes 131104 | tf_op jit(solution)/shard_map/ppermute | solution.py:242
  25.8 6.1 %apply.2 = (f32[640,128]{1,0:T(8,128)S(1)}, f32[648,128]{1,0:T(8,128)S(1)}, f32[264,128]{1,0:T(8,128)S(1)}, f32[264,128]{1,0:T(8,128)S(1)}, f32[128,128]{1,0:T(8...) custom-call(s32[721]{0:T(1024)S(1)} %get-tuple-element.39.table_ref, ...), custom_call_target="tpu_custom_call" | custom-call | tf_op jit(solution)/shard_map/apply/pallas_call | solution.py:216
  32.0 0.1 collective-permute-start.15
  32.0 0.5 collective-permute-start.16
  32.6 1.3 %collective-permute-start.17 = (f32[264,128]{1,0:T(8,128)S(1)}, f32[264,128]{1,0:T(8,128)S(1)}, u32[]{:S(2)}, u32[]{:S(2)}) collective-permute-start(f32[264,128]{1,0:T(8,128)S(1)} %get-tuple-element.48), channel_id=1, source_target_pairs={{0,3},{1,2},{2,1},{3,0},{4,7},{5,6},{6,5},{7,4},{8,11},{9,10},{10,... | collective-permute-start | bytes 405512 | tf_op jit(solution)/shard_map/ppermute | solution.py:242
  33.9 0.3 collective-permute-start.18
  34.2 1.4 %collective-permute-start.19 = (f32[128,128]{1,0:T(8,128)S(1)}, f32[128,128]{1,0:T(8,128)S(1)}, u32[]{:S(2)}, u32[]{:S(2)}) collective-permute-start(f32[128,128]{1,0:T(8,128)S(1)} %get-tuple-element.50), channel_id=1, source_target_pairs={{0,5},{1,4},{2,7},{3,6},{4,1},{5,0},{6,3},{7,2},{8,13},{9,12},{10,... | collective-permute-start | bytes 196616 | tf_op jit(solution)/shard_map/ppermute | solution.py:242
  35.6 3.2 %collective-permute-done.18.column_ref = f32[128,128]{1,0:T(8,128)S(1)} collective-permute-done((f32[128,128]{1,0:T(8,128)S(1)}, f32[128,128]{1,0:T(8,128)S(1)}, u32[]{:S(2)}, u32[]{:S(2)}) %collective-permute-start.18) | collective-permute-done | bytes 65568 | tf_op jit(solution)/shard_map/ppermute | solution.py:242
  38.8 0.3 collective-permute-done.19.column_far_ref
  39.1 1.4 %collective-permute-done.17.row_far_ref = f32[264,128]{1,0:T(8,128)S(1)} collective-permute-done((f32[264,128]{1,0:T(8,128)S(1)}, f32[264,128]{1,0:T(8,128)S(1)}, u32[]{:S(2)}, u32[]{:S(2)}) %collective-permute-start.17) | collective-permute-done | bytes 135200 | tf_op jit(solution)/shard_map/ppermute | solution.py:242
  40.5 0.7 fold.2
  41.2 3.3 %collective-permute-start.21 = (f32[264,128]{1,0:T(8,128)S(1)}, f32[264,128]{1,0:T(8,128)S(1)}, u32[]{:S(2)}, u32[]{:S(2)}) collective-permute-start(f32[264,128]{1,0:T(8,128)S(1)} %get-tuple-element.55), channel_id=1, source_target_pairs={{0,12},{1,13},{2,14},{3,15},{4,8},{5,9},{6,10},{7,11},{8,4},{9,5},... | collective-permute-start | bytes 405512 | tf_op jit(solution)/shard_map/ppermute | solution.py:242
  44.5 1.2 collective-permute-start.23
  45.7 0.4 collective-permute-start.20
  46.1 4.5 %collective-permute-done.20.step_ref = f32[2,128,128]{2,1,0:T(8,128)S(1)} collective-permute-done((f32[2,128,128]{2,1,0:T(8,128)S(1)}, f32[2,128,128]{2,1,0:T(8,128)S(1)}, u32[]{:S(2)}, u32[]{:S(2)}) %collective-permute-start.20) | collective-permute-done | bytes 131104 | tf_op jit(solution)/shard_map/ppermute | solution.py:242
  50.6 5.5 %collective-permute-done.22.refs_2_ = f32[264,128]{1,0:T(8,128)S(1)} collective-permute-done((f32[264,128]{1,0:T(8,128)S(1)}, f32[264,128]{1,0:T(8,128)S(1)}, u32[]{:S(2)}, u32[]{:S(2)}) %collective-permute-start.22) | collective-permute-done | bytes 135200 | tf_op jit(solution)/shard_map/ppermute | solution.py:242
  56.2 0.2 step.1.refs_0_.vector_ref
  56.4 2.7 %collective-permute-start.25 = (f32[2,128,128]{2,1,0:T(8,128)S(1)}, f32[2,128,128]{2,1,0:T(8,128)S(1)}, u32[]{:S(2)}, u32[]{:S(2)}) collective-permute-start(f32[2,128,128]{2,1,0:T(8,128)S(1)} %step.1.refs_0_.vector_ref), channel_id=1, source_target_pairs={{0,12},{1,13},{2,14},{3,15},{4,8},{5,9},{6,10},{7,11},{8,4},{9,5},... | collective-permute-start | bytes 393224 | tf_op jit(solution)/shard_map/ppermute | solution.py:242
  59.1 1.9 %collective-permute-start.30 = (f32[2,128,128]{2,1,0:T(8,128)S(1)}, f32[2,128,128]{2,1,0:T(8,128)S(1)}, u32[]{:S(2)}, u32[]{:S(2)}) collective-permute-start(f32[2,128,128]{2,1,0:T(8,128)S(1)} %step.1.refs_0_.vector_ref), channel_id=1, source_target_pairs={{0,4},{1,5},{2,6},{3,7},{4,0},{5,1},{6,2},{7,3},{8,12},{9,13},{10,... | collective-permute-start | bytes 393224 | tf_op jit(solution)/shard_map/ppermute | solution.py:242
  61.1 1.5 %collective-permute-start.28 = (f32[2,128,128]{2,1,0:T(8,128)S(1)}, f32[2,128,128]{2,1,0:T(8,128)S(1)}, u32[]{:S(2)}, u32[]{:S(2)}) collective-permute-start(f32[2,128,128]{2,1,0:T(8,128)S(1)} %step.1.refs_0_.vector_ref), channel_id=1, source_target_pairs={{0,2},{1,3},{2,0},{3,1},{4,6},{5,7},{6,4},{7,5},{8,10},{9,11},{10,... | collective-permute-start | bytes 393224 | tf_op jit(solution)/shard_map/ppermute | solution.py:242
  62.6 2.1 %collective-permute-done.25.refs_12_ = f32[2,128,128]{2,1,0:T(8,128)S(1)} collective-permute-done((f32[2,128,128]{2,1,0:T(8,128)S(1)}, f32[2,128,128]{2,1,0:T(8,128)S(1)}, u32[]{:S(2)}, u32[]{:S(2)}) %collective-permute-start.25) | collective-permute-done | bytes 131104 | tf_op jit(solution)/shard_map/ppermute | solution.py:242
  64.7 0.5 collective-permute-start.26
  65.1 4.7 %collective-permute-done.32.refs_6_ = f32[2,128,128]{2,1,0:T(8,128)S(1)} collective-permute-done((f32[2,128,128]{2,1,0:T(8,128)S(1)}, f32[2,128,128]{2,1,0:T(8,128)S(1)}, u32[]{:S(2)}, u32[]{:S(2)}) %collective-permute-start.32) | collective-permute-done | bytes 131104 | tf_op jit(solution)/shard_map/ppermute | solution.py:242
  69.8 2.2 %collective-permute-done.30.refs_4_ = f32[2,128,128]{2,1,0:T(8,128)S(1)} collective-permute-done((f32[2,128,128]{2,1,0:T(8,128)S(1)}, f32[2,128,128]{2,1,0:T(8,128)S(1)}, u32[]{:S(2)}, u32[]{:S(2)}) %collective-permute-start.30) | collective-permute-done | bytes 131104 | tf_op jit(solution)/shard_map/ppermute | solution.py:242
  72.0 0.5 collective-permute-start.29
  72.5 0.6 collective-permute-start.35
  73.1 0.5 collective-permute-start.37
  73.7 0.4 collective-permute-start.27
  74.2 3.8 %collective-permute-done.35.refs_10_ = f32[2,128,128]{2,1,0:T(8,128)S(1)} collective-permute-done((f32[2,128,128]{2,1,0:T(8,128)S(1)}, f32[2,128,128]{2,1,0:T(8,128)S(1)}, u32[]{:S(2)}, u32[]{:S(2)}) %collective-permute-start.35) | collective-permute-done | bytes 131104 | tf_op jit(solution)/shard_map/ppermute | solution.py:242
  78.0 1.3 %collective-permute-done.36.refs_11_ = f32[2,128,128]{2,1,0:T(8,128)S(1)} collective-permute-done((f32[2,128,128]{2,1,0:T(8,128)S(1)}, f32[2,128,128]{2,1,0:T(8,128)S(1)}, u32[]{:S(2)}, u32[]{:S(2)}) %collective-permute-start.36) | collective-permute-done | bytes 131104 | tf_op jit(solution)/shard_map/ppermute | solution.py:242
  79.4 6.3 %apply.3 = (f32[640,128]{1,0:T(8,128)S(1)}, f32[648,128]{1,0:T(8,128)S(1)}, f32[264,128]{1,0:T(8,128)S(1)}, f32[264,128]{1,0:T(8,128)S(1)}, f32[128,128]{1,0:T(8...) custom-call(s32[721]{0:T(1024)S(1)} %get-tuple-element.39.table_ref, ...), custom_call_target="tpu_custom_call" | custom-call | tf_op jit(solution)/shard_map/apply/pallas_call | solution.py:216
  85.6 0.1 collective-permute-start.39
  85.7 0.6 collective-permute-start.40
  86.4 1.2 %collective-permute-start.41 = (f32[264,128]{1,0:T(8,128)S(1)}, f32[264,128]{1,0:T(8,128)S(1)}, u32[]{:S(2)}, u32[]{:S(2)}) collective-permute-start(f32[264,128]{1,0:T(8,128)S(1)} %get-tuple-element.64), channel_id=1, source_target_pairs={{0,3},{1,2},{2,1},{3,0},{4,7},{5,6},{6,5},{7,4},{8,11},{9,10},{10,... | collective-permute-start | bytes 405512 | tf_op jit(solution)/shard_map/ppermute | solution.py:242
  87.6 1.7 %collective-permute-start.43 = (f32[128,128]{1,0:T(8,128)S(1)}, f32[128,128]{1,0:T(8,128)S(1)}, u32[]{:S(2)}, u32[]{:S(2)}) collective-permute-start(f32[128,128]{1,0:T(8,128)S(1)} %get-tuple-element.66), channel_id=1, source_target_pairs={{0,5},{1,4},{2,7},{3,6},{4,1},{5,0},{6,3},{7,2},{8,13},{9,12},{10,... | collective-permute-start | bytes 196616 | tf_op jit(solution)/shard_map/ppermute | solution.py:242
  89.3 3.2 %collective-permute-done.42.column_ref = f32[128,128]{1,0:T(8,128)S(1)} collective-permute-done((f32[128,128]{1,0:T(8,128)S(1)}, f32[128,128]{1,0:T(8,128)S(1)}, u32[]{:S(2)}, u32[]{:S(2)}) %collective-permute-start.42) | collective-permute-done | bytes 65568 | tf_op jit(solution)/shard_map/ppermute | solution.py:242
  92.5 0.2 collective-permute-done.43.column_far_ref
  92.7 1.4 %collective-permute-done.41.row_far_ref = f32[264,128]{1,0:T(8,128)S(1)} collective-permute-done((f32[264,128]{1,0:T(8,128)S(1)}, f32[264,128]{1,0:T(8,128)S(1)}, u32[]{:S(2)}, u32[]{:S(2)}) %collective-permute-start.41) | collective-permute-done | bytes 135200 | tf_op jit(solution)/shard_map/ppermute | solution.py:242
  94.2 0.7 fold.3
  94.9 1.4 %collective-permute-start.45 = (f32[264,128]{1,0:T(8,128)S(1)}, f32[264,128]{1,0:T(8,128)S(1)}, u32[]{:S(2)}, u32[]{:S(2)}) collective-permute-start(f32[264,128]{1,0:T(8,128)S(1)} %get-tuple-element.71), channel_id=1, source_target_pairs={{0,12},{1,13},{2,14},{3,15},{4,8},{5,9},{6,10},{7,11},{8,4},{9,5},... | collective-permute-start | bytes 405512 | tf_op jit(solution)/shard_map/ppermute | solution.py:242
  96.3 3.0 %collective-permute-start.47 = (f32[264,128]{1,0:T(8,128)S(1)}, f32[264,128]{1,0:T(8,128)S(1)}, u32[]{:S(2)}, u32[]{:S(2)}) collective-permute-start(f32[264,128]{1,0:T(8,128)S(1)} %get-tuple-element.70.refs_0_), channel_id=1, source_target_pairs={{0,4},{1,5},{2,6},{3,7},{4,0},{5,1},{6,2},{7,3},{8,12},{9,13},{10,... | collective-permute-start | bytes 405512 | tf_op jit(solution)/shard_map/ppermute | solution.py:242
  99.3 0.6 collective-permute-start.44
  99.9 4.4 %collective-permute-done.44.step_ref = f32[2,128,128]{2,1,0:T(8,128)S(1)} collective-permute-done((f32[2,128,128]{2,1,0:T(8,128)S(1)}, f32[2,128,128]{2,1,0:T(8,128)S(1)}, u32[]{:S(2)}, u32[]{:S(2)}) %collective-permute-start.44) | collective-permute-done | bytes 131104 | tf_op jit(solution)/shard_map/ppermute | solution.py:242
  104.3 4.0 %collective-permute-done.46.refs_2_ = f32[264,128]{1,0:T(8,128)S(1)} collective-permute-done((f32[264,128]{1,0:T(8,128)S(1)}, f32[264,128]{1,0:T(8,128)S(1)}, u32[]{:S(2)}, u32[]{:S(2)}) %collective-permute-start.46) | collective-permute-done | bytes 135200 | tf_op jit(solution)/shard_map/ppermute | solution.py:242
  108.4 0.9 last.1
  109.3 10.4 %all_to_all.5.tiles_ref = f32[16,8,128]{2,1,0:T(8,128)S(1)} all-to-all(f32[16,8,128]{2,1,0:T(8,128)S(1)} %broadcast_in_dim.2), channel_id=1, replica_groups=mesh['group'=2,'term'=16] {'term'}, dimensions={0} | all-to-all | bytes 131072 | tf_op jit(solution)/shard_map/all_to_all | solution.py:387
  119.6 0.9 norm.1
  (47 shorter events, 0.2 us)
Async XLA Ops:
  0.6 7.2 %collective-permute-start.2 = (f32[2,128,128]{2,1,0:T(8,128)}, f32[2,128,128]{2,1,0:T(8,128)S(1)}, u32[]{:S(2)}, u32[]{:S(2)}) collective-permute-start(f32[2,128,128]{2,1,0:T(8,128)} %vector_in.1), channel_id=1, source_target_pairs={{0,2},{1,3},{2,0},{3,1},{4,6},{5,7},{6,4},{7,5},{8,10},{9,11},{10,... | collective-permute-start | bytes 393224 | tf_op jit(solution)/shard_map/ppermute | solution.py:242
  3.7 12.9 %collective-permute-start.8 = (f32[2,128,128]{2,1,0:T(8,128)}, f32[2,128,128]{2,1,0:T(8,128)S(1)}, u32[]{:S(2)}, u32[]{:S(2)}) collective-permute-start(f32[2,128,128]{2,1,0:T(8,128)} %vector_in.1), channel_id=1, source_target_pairs={{0,8},{1,9},{2,10},{3,11},{4,12},{5,13},{6,14},{7,15},{8,0},{9,1},... | collective-permute-start | bytes 393224 | tf_op jit(solution)/shard_map/ppermute | solution.py:242
  6.3 10.7 %collective-permute-start = (f32[2,128,128]{2,1,0:T(8,128)}, f32[2,128,128]{2,1,0:T(8,128)S(1)}, u32[]{:S(2)}, u32[]{:S(2)}) collective-permute-start(f32[2,128,128]{2,1,0:T(8,128)} %vector_in.1), channel_id=1, source_target_pairs={{0,12},{1,13},{2,14},{3,15},{4,8},{5,9},{6,10},{7,11},{8,4},{9,5},... | collective-permute-start | bytes 393224 | tf_op jit(solution)/shard_map/ppermute | solution.py:242
  7.6 10.5 %collective-permute-start.4 = (f32[2,128,128]{2,1,0:T(8,128)}, f32[2,128,128]{2,1,0:T(8,128)S(1)}, u32[]{:S(2)}, u32[]{:S(2)}) collective-permute-start(f32[2,128,128]{2,1,0:T(8,128)} %vector_in.1), channel_id=1, source_target_pairs={{0,4},{1,5},{2,6},{3,7},{4,0},{5,1},{6,2},{7,3},{8,12},{9,13},{10,... | collective-permute-start | bytes 393224 | tf_op jit(solution)/shard_map/ppermute | solution.py:242
  7.8 11.7 %collective-permute-start.6 = (f32[2,128,128]{2,1,0:T(8,128)S(1)}, f32[2,128,128]{2,1,0:T(8,128)S(1)}, u32[]{:S(2)}, u32[]{:S(2)}) collective-permute-start(f32[2,128,128]{2,1,0:T(8,128)S(1)} %collective-permute-done.2.refs_2_), channel_id=1, source_target_pairs={{0,4},{1,5},{2,6},{3,7},{4,0},{5,1},{6,2},{7,3},{8,12},{9,13},{10,... | collective-permute-start | bytes 393224 | tf_op jit(solution)/shard_map/ppermute | solution.py:242
  9.6 0.7 copy-start.1
  15.1 4.9 %collective-permute-start.3 = (f32[2,128,128]{2,1,0:T(8,128)S(1)}, f32[2,128,128]{2,1,0:T(8,128)S(1)}, u32[]{:S(2)}, u32[]{:S(2)}) collective-permute-start(f32[2,128,128]{2,1,0:T(8,128)S(1)} %collective-permute-done.2.refs_2_), channel_id=1, source_target_pairs={{0,1},{1,0},{2,3},{3,2},{4,5},{5,4},{6,7},{7,6},{8,9},{9,8},{10,11... | collective-permute-start | bytes 393224 | tf_op jit(solution)/shard_map/ppermute | solution.py:242
  16.5 5.2 %collective-permute-start.10 = (f32[2,128,128]{2,1,0:T(8,128)S(1)}, f32[2,128,128]{2,1,0:T(8,128)S(1)}, u32[]{:S(2)}, u32[]{:S(2)}) collective-permute-start(f32[2,128,128]{2,1,0:T(8,128)S(1)} %collective-permute-done.8.refs_8_), channel_id=1, source_target_pairs={{0,2},{1,3},{2,0},{3,1},{4,6},{5,7},{6,4},{7,5},{8,10},{9,11},{10,... | collective-permute-start | bytes 393224 | tf_op jit(solution)/shard_map/ppermute | solution.py:242
  17.0 4.8 %collective-permute-start.9 = (f32[2,128,128]{2,1,0:T(8,128)S(1)}, f32[2,128,128]{2,1,0:T(8,128)S(1)}, u32[]{:S(2)}, u32[]{:S(2)}) collective-permute-start(f32[2,128,128]{2,1,0:T(8,128)S(1)} %collective-permute-done.8.refs_8_), channel_id=1, source_target_pairs={{0,1},{1,0},{2,3},{3,2},{4,5},{5,4},{6,7},{7,6},{8,9},{9,8},{10,11... | collective-permute-start | bytes 393224 | tf_op jit(solution)/shard_map/ppermute | solution.py:242
  18.1 4.2 %collective-permute-start.5 = (f32[2,128,128]{2,1,0:T(8,128)S(1)}, f32[2,128,128]{2,1,0:T(8,128)S(1)}, u32[]{:S(2)}, u32[]{:S(2)}) collective-permute-start(f32[2,128,128]{2,1,0:T(8,128)S(1)} %collective-permute-done.4.refs_4_), channel_id=1, source_target_pairs={{0,1},{1,0},{2,3},{3,2},{4,5},{5,4},{6,7},{7,6},{8,9},{9,8},{10,11... | collective-permute-start | bytes 393224 | tf_op jit(solution)/shard_map/ppermute | solution.py:242
  19.5 5.0 %collective-permute-start.13 = (f32[2,128,128]{2,1,0:T(8,128)S(1)}, f32[2,128,128]{2,1,0:T(8,128)S(1)}, u32[]{:S(2)}, u32[]{:S(2)}) collective-permute-start(f32[2,128,128]{2,1,0:T(8,128)S(1)} %collective-permute-done.refs_12_), channel_id=1, source_target_pairs={{0,2},{1,3},{2,0},{3,1},{4,6},{5,7},{6,4},{7,5},{8,10},{9,11},{10,... | collective-permute-start | bytes 393224 | tf_op jit(solution)/shard_map/ppermute | solution.py:242
  20.0 4.5 %collective-permute-start.12 = (f32[2,128,128]{2,1,0:T(8,128)S(1)}, f32[2,128,128]{2,1,0:T(8,128)S(1)}, u32[]{:S(2)}, u32[]{:S(2)}) collective-permute-start(f32[2,128,128]{2,1,0:T(8,128)S(1)} %collective-permute-done.refs_12_), channel_id=1, source_target_pairs={{0,1},{1,0},{2,3},{3,2},{4,5},{5,4},{6,7},{7,6},{8,9},{9,8},{10,11... | collective-permute-start | bytes 393224 | tf_op jit(solution)/shard_map/ppermute | solution.py:242
  21.8 2.7 %collective-permute-start.1 = (f32[2,128,128]{2,1,0:T(8,128)S(1)}, f32[2,128,128]{2,1,0:T(8,128)S(1)}, u32[]{:S(2)}, u32[]{:S(2)}) collective-permute-start(f32[2,128,128]{2,1,0:T(8,128)S(1)} %get-tuple-element.43.refs_0_.vector_ref), channel_id=1, source_target_pairs={{0,1},{1,0},{2,3},{3,2},{4,5},{5,4},{6,7},{7,6},{8,9},{9,8},{10,11... | collective-permute-start | bytes 393224 | tf_op jit(solution)/shard_map/ppermute | solution.py:242
  21.8 2.7 %collective-permute-start.7 = (f32[2,128,128]{2,1,0:T(8,128)S(1)}, f32[2,128,128]{2,1,0:T(8,128)S(1)}, u32[]{:S(2)}, u32[]{:S(2)}) collective-permute-start(f32[2,128,128]{2,1,0:T(8,128)S(1)} %collective-permute-done.6.refs_6_), channel_id=1, source_target_pairs={{0,1},{1,0},{2,3},{3,2},{4,5},{5,4},{6,7},{7,6},{8,9},{9,8},{10,11... | collective-permute-start | bytes 393224 | tf_op jit(solution)/shard_map/ppermute | solution.py:242
  22.3 2.2 %collective-permute-start.11 = (f32[2,128,128]{2,1,0:T(8,128)S(1)}, f32[2,128,128]{2,1,0:T(8,128)S(1)}, u32[]{:S(2)}, u32[]{:S(2)}) collective-permute-start(f32[2,128,128]{2,1,0:T(8,128)S(1)} %collective-permute-done.10.refs_10_), channel_id=1, source_target_pairs={{0,1},{1,0},{2,3},{3,2},{4,5},{5,4},{6,7},{7,6},{8,9},{9,8},{10,11... | collective-permute-start | bytes 393224 | tf_op jit(solution)/shard_map/ppermute | solution.py:242
  24.5 1.3 %collective-permute-start.14 = (f32[2,128,128]{2,1,0:T(8,128)S(1)}, f32[2,128,128]{2,1,0:T(8,128)S(1)}, u32[]{:S(2)}, u32[]{:S(2)}) collective-permute-start(f32[2,128,128]{2,1,0:T(8,128)S(1)} %collective-permute-done.13.refs_14_), channel_id=1, source_target_pairs={{0,1},{1,0},{2,3},{3,2},{4,5},{5,4},{6,7},{7,6},{8,9},{9,8},{10,11... | collective-permute-start | bytes 393224 | tf_op jit(solution)/shard_map/ppermute | solution.py:242
  32.0 8.5 %collective-permute-start.15 = (f32[648,128]{1,0:T(8,128)S(1)}, f32[648,128]{1,0:T(8,128)S(1)}, u32[]{:S(2)}, u32[]{:S(2)}) collective-permute-start(f32[648,128]{1,0:T(8,128)S(1)} %get-tuple-element.46.far_in), channel_id=1, source_target_pairs={{0,1},{1,0},{2,3},{3,2},{4,5},{5,4},{6,7},{7,6},{8,9},{9,8},{10,11... | collective-permute-start | bytes 995336 | tf_op jit(solution)/shard_map/ppermute | solution.py:242
  32.0 7.0 %collective-permute-start.16 = (f32[264,128]{1,0:T(8,128)S(1)}, f32[264,128]{1,0:T(8,128)S(1)}, u32[]{:S(2)}, u32[]{:S(2)}) collective-permute-start(f32[264,128]{1,0:T(8,128)S(1)} %get-tuple-element.47), channel_id=1, source_target_pairs={{0,2},{1,3},{2,0},{3,1},{4,6},{5,7},{6,4},{7,5},{8,10},{9,11},{10,... | collective-permute-start | bytes 405512 | tf_op jit(solution)/shard_map/ppermute | solution.py:242
  32.6 7.9 %collective-permute-start.17 = (f32[264,128]{1,0:T(8,128)S(1)}, f32[264,128]{1,0:T(8,128)S(1)}, u32[]{:S(2)}, u32[]{:S(2)}) collective-permute-start(f32[264,128]{1,0:T(8,128)S(1)} %get-tuple-element.48), channel_id=1, source_target_pairs={{0,3},{1,2},{2,1},{3,0},{4,7},{5,6},{6,5},{7,4},{8,11},{9,10},{10,... | collective-permute-start | bytes 405512 | tf_op jit(solution)/shard_map/ppermute | solution.py:242
  33.9 4.9 %collective-permute-start.18 = (f32[128,128]{1,0:T(8,128)S(1)}, f32[128,128]{1,0:T(8,128)S(1)}, u32[]{:S(2)}, u32[]{:S(2)}) collective-permute-start(f32[128,128]{1,0:T(8,128)S(1)} %get-tuple-element.49), channel_id=1, source_target_pairs={{0,4},{1,5},{2,6},{3,7},{4,0},{5,1},{6,2},{7,3},{8,12},{9,13},{10,... | collective-permute-start | bytes 196616 | tf_op jit(solution)/shard_map/ppermute | solution.py:242
  34.2 4.9 %collective-permute-start.19 = (f32[128,128]{1,0:T(8,128)S(1)}, f32[128,128]{1,0:T(8,128)S(1)}, u32[]{:S(2)}, u32[]{:S(2)}) collective-permute-start(f32[128,128]{1,0:T(8,128)S(1)} %get-tuple-element.50), channel_id=1, source_target_pairs={{0,5},{1,4},{2,7},{3,6},{4,1},{5,0},{6,3},{7,2},{8,13},{9,12},{10,... | collective-permute-start | bytes 196616 | tf_op jit(solution)/shard_map/ppermute | solution.py:242
  40.5 15.7 %copy-start = (f32[2,128,128]{2,1,0:T(8,128)S(1)}, f32[2,128,128]{2,1,0:T(8,128)}, u32[]{:S(2)}) copy-start(f32[2,128,128]{2,1,0:T(8,128)} %precond_ref.3) | copy-start | bytes 393220
  41.2 9.4 %collective-permute-start.21 = (f32[264,128]{1,0:T(8,128)S(1)}, f32[264,128]{1,0:T(8,128)S(1)}, u32[]{:S(2)}, u32[]{:S(2)}) collective-permute-start(f32[264,128]{1,0:T(8,128)S(1)} %get-tuple-element.55), channel_id=1, source_target_pairs={{0,12},{1,13},{2,14},{3,15},{4,8},{5,9},{6,10},{7,11},{8,4},{9,5},... | collective-permute-start | bytes 405512 | tf_op jit(solution)/shard_map/ppermute | solution.py:242
  44.5 11.7 %collective-permute-start.22 = (f32[264,128]{1,0:T(8,128)S(1)}, f32[264,128]{1,0:T(8,128)S(1)}, u32[]{:S(2)}, u32[]{:S(2)}) collective-permute-start(f32[264,128]{1,0:T(8,128)S(1)} %get-tuple-element.56), channel_id=1, source_target_pairs={{0,8},{1,9},{2,10},{3,11},{4,12},{5,13},{6,14},{7,15},{8,0},{9,1},... | collective-permute-start | bytes 405512 | tf_op jit(solution)/shard_map/ppermute | solution.py:242
  44.5 11.7 %collective-permute-start.23 = (f32[264,128]{1,0:T(8,128)S(1)}, f32[264,128]{1,0:T(8,128)S(1)}, u32[]{:S(2)}, u32[]{:S(2)}) collective-permute-start(f32[264,128]{1,0:T(8,128)S(1)} %get-tuple-element.54.refs_0_), channel_id=1, source_target_pairs={{0,4},{1,5},{2,6},{3,7},{4,0},{5,1},{6,2},{7,3},{8,12},{9,13},{10,... | collective-permute-start | bytes 405512 | tf_op jit(solution)/shard_map/ppermute | solution.py:242
  45.7 5.0 %collective-permute-start.20 = (f32[2,128,128]{2,1,0:T(8,128)S(1)}, f32[2,128,128]{2,1,0:T(8,128)S(1)}, u32[]{:S(2)}, u32[]{:S(2)}) collective-permute-start(f32[2,128,128]{2,1,0:T(8,128)S(1)} %get-tuple-element.52), channel_id=1, source_target_pairs={{0,2},{1,3},{2,0},{3,1},{4,6},{5,7},{6,4},{7,5},{8,10},{9,11},{10,... | collective-permute-start | bytes 393224 | tf_op jit(solution)/shard_map/ppermute | solution.py:242
  56.4 8.3 %collective-permute-start.25 = (f32[2,128,128]{2,1,0:T(8,128)S(1)}, f32[2,128,128]{2,1,0:T(8,128)S(1)}, u32[]{:S(2)}, u32[]{:S(2)}) collective-permute-start(f32[2,128,128]{2,1,0:T(8,128)S(1)} %step.1.refs_0_.vector_ref), channel_id=1, source_target_pairs={{0,12},{1,13},{2,14},{3,15},{4,8},{5,9},{6,10},{7,11},{8,4},{9,5},... | collective-permute-start | bytes 393224 | tf_op jit(solution)/shard_map/ppermute | solution.py:242
  59.1 10.7 %collective-permute-start.32 = (f32[2,128,128]{2,1,0:T(8,128)S(1)}, f32[2,128,128]{2,1,0:T(8,128)S(1)}, u32[]{:S(2)}, u32[]{:S(2)}) collective-permute-start(f32[2,128,128]{2,1,0:T(8,128)S(1)} %step.1.refs_0_.vector_ref), channel_id=1, source_target_pairs={{0,6},{1,7},{2,4},{3,5},{4,2},{5,3},{6,0},{7,1},{8,14},{9,15},{10,... | collective-permute-start | bytes 393224 | tf_op jit(solution)/shard_map/ppermute | solution.py:242
  59.1 12.9 %collective-permute-start.30 = (f32[2,128,128]{2,1,0:T(8,128)S(1)}, f32[2,128,128]{2,1,0:T(8,128)S(1)}, u32[]{:S(2)}, u32[]{:S(2)}) collective-permute-start(f32[2,128,128]{2,1,0:T(8,128)S(1)} %step.1.refs_0_.vector_ref), channel_id=1, source_target_pairs={{0,4},{1,5},{2,6},{3,7},{4,0},{5,1},{6,2},{7,3},{8,12},{9,13},{10,... | collective-permute-start | bytes 393224 | tf_op jit(solution)/shard_map/ppermute | solution.py:242
  61.1 11.0 %collective-permute-start.28 = (f32[2,128,128]{2,1,0:T(8,128)S(1)}, f32[2,128,128]{2,1,0:T(8,128)S(1)}, u32[]{:S(2)}, u32[]{:S(2)}) collective-permute-start(f32[2,128,128]{2,1,0:T(8,128)S(1)} %step.1.refs_0_.vector_ref), channel_id=1, source_target_pairs={{0,2},{1,3},{2,0},{3,1},{4,6},{5,7},{6,4},{7,5},{8,10},{9,11},{10,... | collective-permute-start | bytes 393224 | tf_op jit(solution)/shard_map/ppermute | solution.py:242
  62.6 9.9 %collective-permute-start.24 = (f32[2,128,128]{2,1,0:T(8,128)S(1)}, f32[2,128,128]{2,1,0:T(8,128)S(1)}, u32[]{:S(2)}, u32[]{:S(2)}) collective-permute-start(f32[2,128,128]{2,1,0:T(8,128)S(1)} %step.1.refs_0_.vector_ref), channel_id=1, source_target_pairs={{0,8},{1,9},{2,10},{3,11},{4,12},{5,13},{6,14},{7,15},{8,0},{9,1},... | collective-permute-start | bytes 393224 | tf_op jit(solution)/shard_map/ppermute | solution.py:242
  64.7 8.5 %collective-permute-start.26 = (f32[2,128,128]{2,1,0:T(8,128)S(1)}, f32[2,128,128]{2,1,0:T(8,128)S(1)}, u32[]{:S(2)}, u32[]{:S(2)}) collective-permute-start(f32[2,128,128]{2,1,0:T(8,128)S(1)} %collective-permute-done.25.refs_12_), channel_id=1, source_target_pairs={{0,2},{1,3},{2,0},{3,1},{4,6},{5,7},{6,4},{7,5},{8,10},{9,11},{10,... | collective-permute-start | bytes 393224 | tf_op jit(solution)/shard_map/ppermute | solution.py:242
  69.8 3.3 %collective-permute-start.33 = (f32[2,128,128]{2,1,0:T(8,128)S(1)}, f32[2,128,128]{2,1,0:T(8,128)S(1)}, u32[]{:S(2)}, u32[]{:S(2)}) collective-permute-start(f32[2,128,128]{2,1,0:T(8,128)S(1)} %collective-permute-done.32.refs_6_), channel_id=1, source_target_pairs={{0,1},{1,0},{2,3},{3,2},{4,5},{5,4},{6,7},{7,6},{8,9},{9,8},{10,11... | collective-permute-start | bytes 393224 | tf_op jit(solution)/shard_map/ppermute | solution.py:242
  72.0 1.6 %collective-permute-start.31 = (f32[2,128,128]{2,1,0:T(8,128)S(1)}, f32[2,128,128]{2,1,0:T(8,128)S(1)}, u32[]{:S(2)}, u32[]{:S(2)}) collective-permute-start(f32[2,128,128]{2,1,0:T(8,128)S(1)} %collective-permute-done.30.refs_4_), channel_id=1, source_target_pairs={{0,1},{1,0},{2,3},{3,2},{4,5},{5,4},{6,7},{7,6},{8,9},{9,8},{10,11... | collective-permute-start | bytes 393224 | tf_op jit(solution)/shard_map/ppermute | solution.py:242
  72.0 1.7 %collective-permute-start.29 = (f32[2,128,128]{2,1,0:T(8,128)S(1)}, f32[2,128,128]{2,1,0:T(8,128)S(1)}, u32[]{:S(2)}, u32[]{:S(2)}) collective-permute-start(f32[2,128,128]{2,1,0:T(8,128)S(1)} %collective-permute-done.28.refs_2_), channel_id=1, source_target_pairs={{0,1},{1,0},{2,3},{3,2},{4,5},{5,4},{6,7},{7,6},{8,9},{9,8},{10,11... | collective-permute-start | bytes 393224 | tf_op jit(solution)/shard_map/ppermute | solution.py:242
  72.5 5.5 %collective-permute-start.35 = (f32[2,128,128]{2,1,0:T(8,128)S(1)}, f32[2,128,128]{2,1,0:T(8,128)S(1)}, u32[]{:S(2)}, u32[]{:S(2)}) collective-permute-start(f32[2,128,128]{2,1,0:T(8,128)S(1)} %collective-permute-done.24.refs_8_), channel_id=1, source_target_pairs={{0,2},{1,3},{2,0},{3,1},{4,6},{5,7},{6,4},{7,5},{8,10},{9,11},{10,... | collective-permute-start | bytes 393224 | tf_op jit(solution)/shard_map/ppermute | solution.py:242
  73.1 4.9 %collective-permute-start.34 = (f32[2,128,128]{2,1,0:T(8,128)S(1)}, f32[2,128,128]{2,1,0:T(8,128)S(1)}, u32[]{:S(2)}, u32[]{:S(2)}) collective-permute-start(f32[2,128,128]{2,1,0:T(8,128)S(1)} %collective-permute-done.24.refs_8_), channel_id=1, source_target_pairs={{0,1},{1,0},{2,3},{3,2},{4,5},{5,4},{6,7},{7,6},{8,9},{9,8},{10,11... | collective-permute-start | bytes 393224 | tf_op jit(solution)/shard_map/ppermute | solution.py:242
  73.1 4.9 %collective-permute-start.37 = (f32[2,128,128]{2,1,0:T(8,128)S(1)}, f32[2,128,128]{2,1,0:T(8,128)S(1)}, u32[]{:S(2)}, u32[]{:S(2)}) collective-permute-start(f32[2,128,128]{2,1,0:T(8,128)S(1)} %collective-permute-done.25.refs_12_), channel_id=1, source_target_pairs={{0,1},{1,0},{2,3},{3,2},{4,5},{5,4},{6,7},{7,6},{8,9},{9,8},{10,11... | collective-permute-start | bytes 393224 | tf_op jit(solution)/shard_map/ppermute | solution.py:242
  73.6 4.4 %collective-permute-start.38 = (f32[2,128,128]{2,1,0:T(8,128)S(1)}, f32[2,128,128]{2,1,0:T(8,128)S(1)}, u32[]{:S(2)}, u32[]{:S(2)}) collective-permute-start(f32[2,128,128]{2,1,0:T(8,128)S(1)} %collective-permute-done.26.refs_14_), channel_id=1, source_target_pairs={{0,1},{1,0},{2,3},{3,2},{4,5},{5,4},{6,7},{7,6},{8,9},{9,8},{10,11... | collective-permute-start | bytes 393224 | tf_op jit(solution)/shard_map/ppermute | solution.py:242
  73.7 4.3 %collective-permute-start.27 = (f32[2,128,128]{2,1,0:T(8,128)S(1)}, f32[2,128,128]{2,1,0:T(8,128)S(1)}, u32[]{:S(2)}, u32[]{:S(2)}) collective-permute-start(f32[2,128,128]{2,1,0:T(8,128)S(1)} %step.1.refs_0_.vector_ref), channel_id=1, source_target_pairs={{0,1},{1,0},{2,3},{3,2},{4,5},{5,4},{6,7},{7,6},{8,9},{9,8},{10,11... | collective-permute-start | bytes 393224 | tf_op jit(solution)/shard_map/ppermute | solution.py:242
  78.0 1.3 %collective-permute-start.36 = (f32[2,128,128]{2,1,0:T(8,128)S(1)}, f32[2,128,128]{2,1,0:T(8,128)S(1)}, u32[]{:S(2)}, u32[]{:S(2)}) collective-permute-start(f32[2,128,128]{2,1,0:T(8,128)S(1)} %collective-permute-done.35.refs_10_), channel_id=1, source_target_pairs={{0,1},{1,0},{2,3},{3,2},{4,5},{5,4},{6,7},{7,6},{8,9},{9,8},{10,11... | collective-permute-start | bytes 393224 | tf_op jit(solution)/shard_map/ppermute | solution.py:242
  85.6 8.5 %collective-permute-start.39 = (f32[648,128]{1,0:T(8,128)S(1)}, f32[648,128]{1,0:T(8,128)S(1)}, u32[]{:S(2)}, u32[]{:S(2)}) collective-permute-start(f32[648,128]{1,0:T(8,128)S(1)} %get-tuple-element.62.far_in), channel_id=1, source_target_pairs={{0,1},{1,0},{2,3},{3,2},{4,5},{5,4},{6,7},{7,6},{8,9},{9,8},{10,11... | collective-permute-start | bytes 995336 | tf_op jit(solution)/shard_map/ppermute | solution.py:242
  85.7 7.0 %collective-permute-start.40 = (f32[264,128]{1,0:T(8,128)S(1)}, f32[264,128]{1,0:T(8,128)S(1)}, u32[]{:S(2)}, u32[]{:S(2)}) collective-permute-start(f32[264,128]{1,0:T(8,128)S(1)} %get-tuple-element.63), channel_id=1, source_target_pairs={{0,2},{1,3},{2,0},{3,1},{4,6},{5,7},{6,4},{7,5},{8,10},{9,11},{10,... | collective-permute-start | bytes 405512 | tf_op jit(solution)/shard_map/ppermute | solution.py:242
  86.4 7.8 %collective-permute-start.41 = (f32[264,128]{1,0:T(8,128)S(1)}, f32[264,128]{1,0:T(8,128)S(1)}, u32[]{:S(2)}, u32[]{:S(2)}) collective-permute-start(f32[264,128]{1,0:T(8,128)S(1)} %get-tuple-element.64), channel_id=1, source_target_pairs={{0,3},{1,2},{2,1},{3,0},{4,7},{5,6},{6,5},{7,4},{8,11},{9,10},{10,... | collective-permute-start | bytes 405512 | tf_op jit(solution)/shard_map/ppermute | solution.py:242
  87.6 4.9 %collective-permute-start.42 = (f32[128,128]{1,0:T(8,128)S(1)}, f32[128,128]{1,0:T(8,128)S(1)}, u32[]{:S(2)}, u32[]{:S(2)}) collective-permute-start(f32[128,128]{1,0:T(8,128)S(1)} %get-tuple-element.65), channel_id=1, source_target_pairs={{0,4},{1,5},{2,6},{3,7},{4,0},{5,1},{6,2},{7,3},{8,12},{9,13},{10,... | collective-permute-start | bytes 196616 | tf_op jit(solution)/shard_map/ppermute | solution.py:242
  87.6 5.2 %collective-permute-start.43 = (f32[128,128]{1,0:T(8,128)S(1)}, f32[128,128]{1,0:T(8,128)S(1)}, u32[]{:S(2)}, u32[]{:S(2)}) collective-permute-start(f32[128,128]{1,0:T(8,128)S(1)} %get-tuple-element.66), channel_id=1, source_target_pairs={{0,5},{1,4},{2,7},{3,6},{4,1},{5,0},{6,3},{7,2},{8,13},{9,12},{10,... | collective-permute-start | bytes 196616 | tf_op jit(solution)/shard_map/ppermute | solution.py:242
  94.9 9.4 %collective-permute-start.45 = (f32[264,128]{1,0:T(8,128)S(1)}, f32[264,128]{1,0:T(8,128)S(1)}, u32[]{:S(2)}, u32[]{:S(2)}) collective-permute-start(f32[264,128]{1,0:T(8,128)S(1)} %get-tuple-element.71), channel_id=1, source_target_pairs={{0,12},{1,13},{2,14},{3,15},{4,8},{5,9},{6,10},{7,11},{8,4},{9,5},... | collective-permute-start | bytes 405512 | tf_op jit(solution)/shard_map/ppermute | solution.py:242
  96.3 12.0 %collective-permute-start.46 = (f32[264,128]{1,0:T(8,128)S(1)}, f32[264,128]{1,0:T(8,128)S(1)}, u32[]{:S(2)}, u32[]{:S(2)}) collective-permute-start(f32[264,128]{1,0:T(8,128)S(1)} %get-tuple-element.72), channel_id=1, source_target_pairs={{0,8},{1,9},{2,10},{3,11},{4,12},{5,13},{6,14},{7,15},{8,0},{9,1},... | collective-permute-start | bytes 405512 | tf_op jit(solution)/shard_map/ppermute | solution.py:242
  96.3 12.0 %collective-permute-start.47 = (f32[264,128]{1,0:T(8,128)S(1)}, f32[264,128]{1,0:T(8,128)S(1)}, u32[]{:S(2)}, u32[]{:S(2)}) collective-permute-start(f32[264,128]{1,0:T(8,128)S(1)} %get-tuple-element.70.refs_0_), channel_id=1, source_target_pairs={{0,4},{1,5},{2,6},{3,7},{4,0},{5,1},{6,2},{7,3},{8,12},{9,13},{10,... | collective-permute-start | bytes 405512 | tf_op jit(solution)/shard_map/ppermute | solution.py:242
  99.3 5.0 %collective-permute-start.44 = (f32[2,128,128]{2,1,0:T(8,128)S(1)}, f32[2,128,128]{2,1,0:T(8,128)S(1)}, u32[]{:S(2)}, u32[]{:S(2)}) collective-permute-start(f32[2,128,128]{2,1,0:T(8,128)S(1)} %get-tuple-element.68), channel_id=1, source_target_pairs={{0,2},{1,3},{2,0},{3,1},{4,6},{5,7},{6,4},{7,5},{8,10},{9,11},{10,... | collective-permute-start | bytes 393224 | tf_op jit(solution)/shard_map/ppermute | solution.py:242

commit v14 on v11

--- a/solution.py
+++ b/solution.py
@@ -353,11 +353,13 @@
         pieces[k] = swapped(x, k)
     pieces[ROW] = swapped(x, ROW)
     pieces[COLUMN] = swapped(x, COLUMN)
-    if held is not None:
-        pieces[n - 4], pieces[0] = lax.optimization_barrier((pieces[n - 4], held))
+    pieces[COLUMN + ROW] = swapped(x, COLUMN + ROW)
     for k in reversed(range(8, n, 4)):
         pieces[k + ROW] = swapped(pieces[k], ROW)
-    pieces[COLUMN + ROW] = swapped(pieces[ROW], COLUMN)
+    late = [0, 8, n - 4, n - 4 + ROW]
+    pieces.update(zip(late, lax.optimization_barrier([pieces[k] for k in late])))
+    if held is not None:
+        pieces[COLUMN], pieces[0] = lax.optimization_barrier((pieces[COLUMN], held))
     for k in range(0, n, 2):
         pieces[k + CORE] = swapped(pieces[k], CORE)
     return [pieces[k] for k in range(n)]

time: 120 us -> 122 us (1.017)
  starting transfers between devices: 37.2 us -> 44.3 us
  waiting for transfers between devices: 50.8 us -> 43.9 us
    ppermute x48, starting transfers between devices: 37.2 us -> 44.3 us  [swapped(): return lax.ppermute(x, 'term', [(i, i ^ k) for i in range(n)])]
    ppermute x48, waiting for transfers between devices: 50.8 us -> 43.9 us  [swapped(): return lax.ppermute(x, 'term', [(i, i ^ k) for i in range(n)])]
  transfers between devices with their start and end apart: 48 -> 48, of which waited for: 23 -> 18; matrix products, arithmetic and copies ran while one was open for 0% -> 0% of each run, Pallas kernels for 3% -> 3%
where the time goes in v14:
time: 122 us
  starting transfers between devices  44.3 us (36%)
  waiting for transfers between devices  43.9 us (36%)
  Pallas kernels  20 us (16%)
  blocking collectives  11.4 us (9%)
  between operations  1.42 us (1%)
    ppermute x48, starting transfers between devices, swapped(): return lax.ppermute(x, 'term', [(i, i ^ k) for i in range(n)])  44.3 us
    ppermute x48, waiting for transfers between devices, swapped(): return lax.ppermute(x, 'term', [(i, i ^ k) for i in range(n)])  43.9 us
    pallas_call x2, Pallas kernels, apply(): pl.pallas_call(functools.partial(apply_kernel, n, npairs, over_rows, rows...  12.4 us
    all_to_all x1, blocking collectives, shards(): lax.all_to_all(jnp.broadcast_to(partial[None], (n, 8, width)), 'term', sp...  11.4 us
    pallas_call x1, Pallas kernels, prep(): pl.pallas_call(functools.partial(prep_kernel, n, terms * n + 1), out_shap...  4.18 us
    pallas_call x5, Pallas kernels, local(): pl.pallas_call(kernel, out_shape=out_shape, in_specs=[SMEM] * len(scalars...  3.42 us
  transfers between devices with their start and end apart: 48, of which 18 were waited for; matrix products, arithmetic and copies ran while one was open for 0% of the time, Pallas kernels for 3%

profile of v14, /device:TPU:0, one launch (start us, length us, event | category | flops | bytes accessed | tf_op | source)
XLA Modules:
  0.0 121.7 jit_solution(8599412833802928257)
XLA Ops:
  0.6 5.1 %collective-permute-start.8 = (f32[2,128,128]{2,1,0:T(8,128)}, f32[2,128,128]{2,1,0:T(8,128)S(1)}, u32[]{:S(2)}, u32[]{:S(2)}) collective-permute-start(f32[2,128,128]{2,1,0:T(8,128)} %vector_in.1), channel_id=1, source_target_pairs={{0,12},{1,13},{2,14},{3,15},{4,8},{5,9},{6,10},{7,11},{8,4},{9,5},... | collective-permute-start | bytes 393224 | tf_op jit(solution)/shard_map/ppermute | solution.py:242
  5.7 1.7 %collective-permute-start.5 = (f32[2,128,128]{2,1,0:T(8,128)}, f32[2,128,128]{2,1,0:T(8,128)S(1)}, u32[]{:S(2)}, u32[]{:S(2)}) collective-permute-start(f32[2,128,128]{2,1,0:T(8,128)} %vector_in.1), channel_id=1, source_target_pairs={{0,6},{1,7},{2,4},{3,5},{4,2},{5,3},{6,0},{7,1},{8,14},{9,15},{10,... | collective-permute-start | bytes 393224 | tf_op jit(solution)/shard_map/ppermute | solution.py:242
  7.5 1.2 %collective-permute-start = (f32[2,128,128]{2,1,0:T(8,128)}, f32[2,128,128]{2,1,0:T(8,128)S(1)}, u32[]{:S(2)}, u32[]{:S(2)}) collective-permute-start(f32[2,128,128]{2,1,0:T(8,128)} %vector_in.1), channel_id=1, source_target_pairs={{0,4},{1,5},{2,6},{3,7},{4,0},{5,1},{6,2},{7,3},{8,12},{9,13},{10,... | collective-permute-start | bytes 393224 | tf_op jit(solution)/shard_map/ppermute | solution.py:242
  8.7 0.5 collective-permute-start.2
  9.9 0.6 copy.12
  10.5 1.6 %collective-permute-start.9 = (f32[2,128,128]{2,1,0:T(8,128)S(1)}, f32[2,128,128]{2,1,0:T(8,128)S(1)}, u32[]{:S(2)}, u32[]{:S(2)}) collective-permute-start(f32[2,128,128]{2,1,0:T(8,128)S(1)} %collective-permute-done.8.refs_12_), channel_id=1, source_target_pairs={{0,2},{1,3},{2,0},{3,1},{4,6},{5,7},{6,4},{7,5},{8,10},{9,11},{10,... | collective-permute-start | bytes 393224 | tf_op jit(solution)/shard_map/ppermute | solution.py:242
  12.1 4.2 %prep.1 = (bf16[8,128,512]{2,1,0:T(8,128)(2,1)S(1)}, bf16[2048,256]{1,0:T(8,128)(2,1)S(1)}, s32[721]{0:T(1024)S(1)}, f32[2,128,128]{2,1,0:T(8,128)S(1)}) custom-call(s32[1]{0:T(128)} %bitcast.me_ref, s32[16,16]{1,0:T(8,128)} %fetch_in.1, s32[16,16]{1,0:T(8,128)} %store_in.1, s32[384]{0:T(512)} %bitcast.8, s32[1]{0:T(128)S(6)} %copy.13.live_in, ...), custom_call_target="tpu_custom_call" | custom-call | tf_op jit(solution)/shard_map/prep/pallas_call | solution.py:132
  16.3 0.8 collective-permute-done.7.refs_8_
  17.1 1.5 %collective-permute-start.11 = (f32[2,128,128]{2,1,0:T(8,128)S(1)}, f32[2,128,128]{2,1,0:T(8,128)S(1)}, u32[]{:S(2)}, u32[]{:S(2)}) collective-permute-start(f32[2,128,128]{2,1,0:T(8,128)S(1)} %collective-permute-done.7.refs_8_), channel_id=1, source_target_pairs={{0,2},{1,3},{2,0},{3,1},{4,6},{5,7},{6,4},{7,5},{8,10},{9,11},{10,... | collective-permute-start | bytes 393224 | tf_op jit(solution)/shard_map/ppermute | solution.py:242
  18.7 0.5 collective-permute-start.3
  19.2 0.1 collective-permute-start.4
  19.3 0.4 collective-permute-start.1
  19.7 2.4 %collective-permute-done.11.refs_10_ = f32[2,128,128]{2,1,0:T(8,128)S(1)} collective-permute-done((f32[2,128,128]{2,1,0:T(8,128)S(1)}, f32[2,128,128]{2,1,0:T(8,128)S(1)}, u32[]{:S(2)}, u32[]{:S(2)}) %collective-permute-start.11) | collective-permute-done | bytes 131104 | tf_op jit(solution)/shard_map/ppermute | solution.py:242
  22.1 0.5 collective-permute-start.13
  22.6 0.1 collective-permute-start.12
  22.7 0.4 collective-permute-start.14
  23.1 0.8 collective-permute-done.12.refs_11_
  24.0 0.2 collective-permute-done.14.refs_15_
  24.2 6.1 %apply.2 = (f32[640,128]{1,0:T(8,128)S(1)}, f32[648,128]{1,0:T(8,128)S(1)}, f32[264,128]{1,0:T(8,128)S(1)}, f32[264,128]{1,0:T(8,128)S(1)}, f32[128,128]{1,0:T(8...) custom-call(s32[721]{0:T(1024)S(1)} %get-tuple-element.42.table_ref, ...), custom_call_target="tpu_custom_call" | custom-call | tf_op jit(solution)/shard_map/apply/pallas_call | solution.py:216
  30.3 0.3 collective-permute-start.15
  30.6 1.4 %collective-permute-start.16 = (f32[264,128]{1,0:T(8,128)S(1)}, f32[264,128]{1,0:T(8,128)S(1)}, u32[]{:S(2)}, u32[]{:S(2)}) collective-permute-start(f32[264,128]{1,0:T(8,128)S(1)} %get-tuple-element.53), channel_id=1, source_target_pairs={{0,2},{1,3},{2,0},{3,1},{4,6},{5,7},{6,4},{7,5},{8,10},{9,11},{10,... | collective-permute-start | bytes 405512 | tf_op jit(solution)/shard_map/ppermute | solution.py:242
  32.0 0.2 collective-permute-start.17
  32.2 2.8 %collective-permute-start.18 = (f32[128,128]{1,0:T(8,128)S(1)}, f32[128,128]{1,0:T(8,128)S(1)}, u32[]{:S(2)}, u32[]{:S(2)}) collective-permute-start(f32[128,128]{1,0:T(8,128)S(1)} %get-tuple-element.55), channel_id=1, source_target_pairs={{0,4},{1,5},{2,6},{3,7},{4,0},{5,1},{6,2},{7,3},{8,12},{9,13},{10,... | collective-permute-start | bytes 196616 | tf_op jit(solution)/shard_map/ppermute | solution.py:242
  35.0 0.3 collective-permute-start.19
  35.3 2.6 %collective-permute-done.18.column_ref = f32[128,128]{1,0:T(8,128)S(1)} collective-permute-done((f32[128,128]{1,0:T(8,128)S(1)}, f32[128,128]{1,0:T(8,128)S(1)}, u32[]{:S(2)}, u32[]{:S(2)}) %collective-permute-start.18) | collective-permute-done | bytes 65568 | tf_op jit(solution)/shard_map/ppermute | solution.py:242
  37.9 1.0 collective-permute-done.19.column_far_ref
  39.0 0.7 fold.2
  39.7 2.6 %collective-permute-start.21 = (f32[264,128]{1,0:T(8,128)S(1)}, f32[264,128]{1,0:T(8,128)S(1)}, u32[]{:S(2)}, u32[]{:S(2)}) collective-permute-start(f32[264,128]{1,0:T(8,128)S(1)} %get-tuple-element.61), channel_id=1, source_target_pairs={{0,12},{1,13},{2,14},{3,15},{4,8},{5,9},{6,10},{7,11},{8,4},{9,5},... | collective-permute-start | bytes 405512 | tf_op jit(solution)/shard_map/ppermute | solution.py:242
  42.3 1.3 %collective-permute-start.22 = (f32[264,128]{1,0:T(8,128)S(1)}, f32[264,128]{1,0:T(8,128)S(1)}, u32[]{:S(2)}, u32[]{:S(2)}) collective-permute-start(f32[264,128]{1,0:T(8,128)S(1)} %get-tuple-element.62), channel_id=1, source_target_pairs={{0,8},{1,9},{2,10},{3,11},{4,12},{5,13},{6,14},{7,15},{8,0},{9,1},... | collective-permute-start | bytes 405512 | tf_op jit(solution)/shard_map/ppermute | solution.py:242
  43.5 0.6 collective-permute-start.23
  44.2 1.5 %collective-permute-start.20 = (f32[2,128,128]{2,1,0:T(8,128)S(1)}, f32[2,128,128]{2,1,0:T(8,128)S(1)}, u32[]{:S(2)}, u32[]{:S(2)}) collective-permute-start(f32[2,128,128]{2,1,0:T(8,128)S(1)} %get-tuple-element.58), channel_id=1, source_target_pairs={{0,2},{1,3},{2,0},{3,1},{4,6},{5,7},{6,4},{7,5},{8,10},{9,11},{10,... | collective-permute-start | bytes 393224 | tf_op jit(solution)/shard_map/ppermute | solution.py:242
  45.7 3.5 %collective-permute-done.20.step_ref = f32[2,128,128]{2,1,0:T(8,128)S(1)} collective-permute-done((f32[2,128,128]{2,1,0:T(8,128)S(1)}, f32[2,128,128]{2,1,0:T(8,128)S(1)}, u32[]{:S(2)}, u32[]{:S(2)}) %collective-permute-start.20) | collective-permute-done | bytes 131104 | tf_op jit(solution)/shard_map/ppermute | solution.py:242
  49.1 6.9 %collective-permute-done.22.refs_2_ = f32[264,128]{1,0:T(8,128)S(1)} collective-permute-done((f32[264,128]{1,0:T(8,128)S(1)}, f32[264,128]{1,0:T(8,128)S(1)}, u32[]{:S(2)}, u32[]{:S(2)}) %collective-permute-start.22) | collective-permute-done | bytes 135200 | tf_op jit(solution)/shard_map/ppermute | solution.py:242
  56.1 0.2 step.1.refs_0_.vector_ref
  56.2 2.5 %collective-permute-start.25 = (f32[2,128,128]{2,1,0:T(8,128)S(1)}, f32[2,128,128]{2,1,0:T(8,128)S(1)}, u32[]{:S(2)}, u32[]{:S(2)}) collective-permute-start(f32[2,128,128]{2,1,0:T(8,128)S(1)} %step.1.refs_0_.vector_ref), channel_id=1, source_target_pairs={{0,12},{1,13},{2,14},{3,15},{4,8},{5,9},{6,10},{7,11},{8,4},{9,5},... | collective-permute-start | bytes 393224 | tf_op jit(solution)/shard_map/ppermute | solution.py:242
  58.8 3.0 %collective-permute-start.30 = (f32[2,128,128]{2,1,0:T(8,128)S(1)}, f32[2,128,128]{2,1,0:T(8,128)S(1)}, u32[]{:S(2)}, u32[]{:S(2)}) collective-permute-start(f32[2,128,128]{2,1,0:T(8,128)S(1)} %step.1.refs_0_.vector_ref), channel_id=1, source_target_pairs={{0,4},{1,5},{2,6},{3,7},{4,0},{5,1},{6,2},{7,3},{8,12},{9,13},{10,... | collective-permute-start | bytes 393224 | tf_op jit(solution)/shard_map/ppermute | solution.py:242
  61.8 0.5 collective-permute-start.28
  62.3 2.2 %collective-permute-done.25.refs_12_ = f32[2,128,128]{2,1,0:T(8,128)S(1)} collective-permute-done((f32[2,128,128]{2,1,0:T(8,128)S(1)}, f32[2,128,128]{2,1,0:T(8,128)S(1)}, u32[]{:S(2)}, u32[]{:S(2)}) %collective-permute-start.25) | collective-permute-done | bytes 131104 | tf_op jit(solution)/shard_map/ppermute | solution.py:242
  64.5 1.4 %collective-permute-start.26 = (f32[2,128,128]{2,1,0:T(8,128)S(1)}, f32[2,128,128]{2,1,0:T(8,128)S(1)}, u32[]{:S(2)}, u32[]{:S(2)}) collective-permute-start(f32[2,128,128]{2,1,0:T(8,128)S(1)} %collective-permute-done.25.refs_12_), channel_id=1, source_target_pairs={{0,2},{1,3},{2,0},{3,1},{4,6},{5,7},{6,4},{7,5},{8,10},{9,11},{10,... | collective-permute-start | bytes 393224 | tf_op jit(solution)/shard_map/ppermute | solution.py:242
  65.9 4.3 %collective-permute-done.32.refs_6_ = f32[2,128,128]{2,1,0:T(8,128)S(1)} collective-permute-done((f32[2,128,128]{2,1,0:T(8,128)S(1)}, f32[2,128,128]{2,1,0:T(8,128)S(1)}, u32[]{:S(2)}, u32[]{:S(2)}) %collective-permute-start.32) | collective-permute-done | bytes 131104 | tf_op jit(solution)/shard_map/ppermute | solution.py:242
  70.3 1.9 %collective-permute-done.30.refs_4_ = f32[2,128,128]{2,1,0:T(8,128)S(1)} collective-permute-done((f32[2,128,128]{2,1,0:T(8,128)S(1)}, f32[2,128,128]{2,1,0:T(8,128)S(1)}, u32[]{:S(2)}, u32[]{:S(2)}) %collective-permute-start.30) | collective-permute-done | bytes 131104 | tf_op jit(solution)/shard_map/ppermute | solution.py:242
  72.1 0.5 collective-permute-start.29
  72.6 1.4 %collective-permute-start.35 = (f32[2,128,128]{2,1,0:T(8,128)S(1)}, f32[2,128,128]{2,1,0:T(8,128)S(1)}, u32[]{:S(2)}, u32[]{:S(2)}) collective-permute-start(f32[2,128,128]{2,1,0:T(8,128)S(1)} %collective-permute-done.24.refs_8_), channel_id=1, source_target_pairs={{0,2},{1,3},{2,0},{3,1},{4,6},{5,7},{6,4},{7,5},{8,10},{9,11},{10,... | collective-permute-start | bytes 393224 | tf_op jit(solution)/shard_map/ppermute | solution.py:242
  74.1 0.5 collective-permute-start.37
  74.6 0.4 collective-permute-start.27
  75.1 3.0 %collective-permute-done.35.refs_10_ = f32[2,128,128]{2,1,0:T(8,128)S(1)} collective-permute-done((f32[2,128,128]{2,1,0:T(8,128)S(1)}, f32[2,128,128]{2,1,0:T(8,128)S(1)}, u32[]{:S(2)}, u32[]{:S(2)}) %collective-permute-start.35) | collective-permute-done | bytes 131104 | tf_op jit(solution)/shard_map/ppermute | solution.py:242
  78.1 1.3 %collective-permute-done.36.refs_11_ = f32[2,128,128]{2,1,0:T(8,128)S(1)} collective-permute-done((f32[2,128,128]{2,1,0:T(8,128)S(1)}, f32[2,128,128]{2,1,0:T(8,128)S(1)}, u32[]{:S(2)}, u32[]{:S(2)}) %collective-permute-start.36) | collective-permute-done | bytes 131104 | tf_op jit(solution)/shard_map/ppermute | solution.py:242
  79.5 6.3 %apply.3 = (f32[640,128]{1,0:T(8,128)S(1)}, f32[648,128]{1,0:T(8,128)S(1)}, f32[264,128]{1,0:T(8,128)S(1)}, f32[264,128]{1,0:T(8,128)S(1)}, f32[128,128]{1,0:T(8...) custom-call(s32[721]{0:T(1024)S(1)} %get-tuple-element.42.table_ref, ...), custom_call_target="tpu_custom_call" | custom-call | tf_op jit(solution)/shard_map/apply/pallas_call | solution.py:216
  85.8 0.2 collective-permute-start.39
  85.9 1.3 %collective-permute-start.40 = (f32[264,128]{1,0:T(8,128)S(1)}, f32[264,128]{1,0:T(8,128)S(1)}, u32[]{:S(2)}, u32[]{:S(2)}) collective-permute-start(f32[264,128]{1,0:T(8,128)S(1)} %get-tuple-element.69), channel_id=1, source_target_pairs={{0,2},{1,3},{2,0},{3,1},{4,6},{5,7},{6,4},{7,5},{8,10},{9,11},{10,... | collective-permute-start | bytes 405512 | tf_op jit(solution)/shard_map/ppermute | solution.py:242
  87.2 0.5 collective-permute-start.41
  87.7 1.7 %collective-permute-start.43 = (f32[128,128]{1,0:T(8,128)S(1)}, f32[128,128]{1,0:T(8,128)S(1)}, u32[]{:S(2)}, u32[]{:S(2)}) collective-permute-start(f32[128,128]{1,0:T(8,128)S(1)} %get-tuple-element.72), channel_id=1, source_target_pairs={{0,5},{1,4},{2,7},{3,6},{4,1},{5,0},{6,3},{7,2},{8,13},{9,12},{10,... | collective-permute-start | bytes 196616 | tf_op jit(solution)/shard_map/ppermute | solution.py:242
  89.4 3.2 %collective-permute-done.42.column_ref = f32[128,128]{1,0:T(8,128)S(1)} collective-permute-done((f32[128,128]{1,0:T(8,128)S(1)}, f32[128,128]{1,0:T(8,128)S(1)}, u32[]{:S(2)}, u32[]{:S(2)}) %collective-permute-start.42) | collective-permute-done | bytes 65568 | tf_op jit(solution)/shard_map/ppermute | solution.py:242
  92.6 0.3 collective-permute-done.43.column_far_ref
  92.9 1.4 %collective-permute-done.41.row_far_ref = f32[264,128]{1,0:T(8,128)S(1)} collective-permute-done((f32[264,128]{1,0:T(8,128)S(1)}, f32[264,128]{1,0:T(8,128)S(1)}, u32[]{:S(2)}, u32[]{:S(2)}) %collective-permute-start.41) | collective-permute-done | bytes 135200 | tf_op jit(solution)/shard_map/ppermute | solution.py:242
  94.3 0.7 fold.3
  95.0 2.2 %collective-permute-start.45 = (f32[264,128]{1,0:T(8,128)S(1)}, f32[264,128]{1,0:T(8,128)S(1)}, u32[]{:S(2)}, u32[]{:S(2)}) collective-permute-start(f32[264,128]{1,0:T(8,128)S(1)} %get-tuple-element.77), channel_id=1, source_target_pairs={{0,12},{1,13},{2,14},{3,15},{4,8},{5,9},{6,10},{7,11},{8,4},{9,5},... | collective-permute-start | bytes 405512 | tf_op jit(solution)/shard_map/ppermute | solution.py:242
  97.2 2.2 %collective-permute-start.47 = (f32[264,128]{1,0:T(8,128)S(1)}, f32[264,128]{1,0:T(8,128)S(1)}, u32[]{:S(2)}, u32[]{:S(2)}) collective-permute-start(f32[264,128]{1,0:T(8,128)S(1)} %get-tuple-element.76.refs_0_), channel_id=1, source_target_pairs={{0,4},{1,5},{2,6},{3,7},{4,0},{5,1},{6,2},{7,3},{8,12},{9,13},{10,... | collective-permute-start | bytes 405512 | tf_op jit(solution)/shard_map/ppermute | solution.py:242
  99.4 1.1 collective-permute-start.44
  100.6 3.8 %collective-permute-done.44.step_ref = f32[2,128,128]{2,1,0:T(8,128)S(1)} collective-permute-done((f32[2,128,128]{2,1,0:T(8,128)S(1)}, f32[2,128,128]{2,1,0:T(8,128)S(1)}, u32[]{:S(2)}, u32[]{:S(2)}) %collective-permute-start.44) | collective-permute-done | bytes 131104 | tf_op jit(solution)/shard_map/ppermute | solution.py:242
  104.4 4.1 %collective-permute-done.46.refs_2_ = f32[264,128]{1,0:T(8,128)S(1)} collective-permute-done((f32[264,128]{1,0:T(8,128)S(1)}, f32[264,128]{1,0:T(8,128)S(1)}, u32[]{:S(2)}, u32[]{:S(2)}) %collective-permute-start.46) | collective-permute-done | bytes 135200 | tf_op jit(solution)/shard_map/ppermute | solution.py:242
  108.5 0.9 last.1
  109.4 11.4 %all_to_all.5.tiles_ref = f32[16,8,128]{2,1,0:T(8,128)S(1)} all-to-all(f32[16,8,128]{2,1,0:T(8,128)S(1)} %broadcast_in_dim.2), channel_id=1, replica_groups=mesh['group'=2,'term'=16] {'term'}, dimensions={0} | all-to-all | bytes 131072 | tf_op jit(solution)/shard_map/all_to_all | solution.py:386
  120.8 0.9 norm.1
  (47 shorter events, 0.2 us)
Async XLA Ops:
  0.6 9.9 %collective-permute-start.8 = (f32[2,128,128]{2,1,0:T(8,128)}, f32[2,128,128]{2,1,0:T(8,128)S(1)}, u32[]{:S(2)}, u32[]{:S(2)}) collective-permute-start(f32[2,128,128]{2,1,0:T(8,128)} %vector_in.1), channel_id=1, source_target_pairs={{0,12},{1,13},{2,14},{3,15},{4,8},{5,9},{6,10},{7,11},{8,4},{9,5},... | collective-permute-start | bytes 393224 | tf_op jit(solution)/shard_map/ppermute | solution.py:242
  5.7 11.4 %collective-permute-start.7 = (f32[2,128,128]{2,1,0:T(8,128)}, f32[2,128,128]{2,1,0:T(8,128)S(1)}, u32[]{:S(2)}, u32[]{:S(2)}) collective-permute-start(f32[2,128,128]{2,1,0:T(8,128)} %vector_in.1), channel_id=1, source_target_pairs={{0,8},{1,9},{2,10},{3,11},{4,12},{5,13},{6,14},{7,15},{8,0},{9,1},... | collective-permute-start | bytes 393224 | tf_op jit(solution)/shard_map/ppermute | solution.py:242
  5.7 12.9 %collective-permute-start.5 = (f32[2,128,128]{2,1,0:T(8,128)}, f32[2,128,128]{2,1,0:T(8,128)S(1)}, u32[]{:S(2)}, u32[]{:S(2)}) collective-permute-start(f32[2,128,128]{2,1,0:T(8,128)} %vector_in.1), channel_id=1, source_target_pairs={{0,6},{1,7},{2,4},{3,5},{4,2},{5,3},{6,0},{7,1},{8,14},{9,15},{10,... | collective-permute-start | bytes 393224 | tf_op jit(solution)/shard_map/ppermute | solution.py:242
  7.5 11.2 %collective-permute-start = (f32[2,128,128]{2,1,0:T(8,128)}, f32[2,128,128]{2,1,0:T(8,128)S(1)}, u32[]{:S(2)}, u32[]{:S(2)}) collective-permute-start(f32[2,128,128]{2,1,0:T(8,128)} %vector_in.1), channel_id=1, source_target_pairs={{0,4},{1,5},{2,6},{3,7},{4,0},{5,1},{6,2},{7,3},{8,12},{9,13},{10,... | collective-permute-start | bytes 393224 | tf_op jit(solution)/shard_map/ppermute | solution.py:242
  8.7 9.9 %collective-permute-start.2 = (f32[2,128,128]{2,1,0:T(8,128)}, f32[2,128,128]{2,1,0:T(8,128)S(1)}, u32[]{:S(2)}, u32[]{:S(2)}) collective-permute-start(f32[2,128,128]{2,1,0:T(8,128)} %vector_in.1), channel_id=1, source_target_pairs={{0,2},{1,3},{2,0},{3,1},{4,6},{5,7},{6,4},{7,5},{8,10},{9,11},{10,... | collective-permute-start | bytes 393224 | tf_op jit(solution)/shard_map/ppermute | solution.py:242
  9.2 0.7 copy-start.1
  10.5 8.8 %collective-permute-start.9 = (f32[2,128,128]{2,1,0:T(8,128)S(1)}, f32[2,128,128]{2,1,0:T(8,128)S(1)}, u32[]{:S(2)}, u32[]{:S(2)}) collective-permute-start(f32[2,128,128]{2,1,0:T(8,128)S(1)} %collective-permute-done.8.refs_12_), channel_id=1, source_target_pairs={{0,2},{1,3},{2,0},{3,1},{4,6},{5,7},{6,4},{7,5},{8,10},{9,11},{10,... | collective-permute-start | bytes 393224 | tf_op jit(solution)/shard_map/ppermute | solution.py:242
  17.1 5.0 %collective-permute-start.11 = (f32[2,128,128]{2,1,0:T(8,128)S(1)}, f32[2,128,128]{2,1,0:T(8,128)S(1)}, u32[]{:S(2)}, u32[]{:S(2)}) collective-permute-start(f32[2,128,128]{2,1,0:T(8,128)S(1)} %collective-permute-done.7.refs_8_), channel_id=1, source_target_pairs={{0,2},{1,3},{2,0},{3,1},{4,6},{5,7},{6,4},{7,5},{8,10},{9,11},{10,... | collective-permute-start | bytes 393224 | tf_op jit(solution)/shard_map/ppermute | solution.py:242
  18.7 3.5 %collective-permute-start.6 = (f32[2,128,128]{2,1,0:T(8,128)S(1)}, f32[2,128,128]{2,1,0:T(8,128)S(1)}, u32[]{:S(2)}, u32[]{:S(2)}) collective-permute-start(f32[2,128,128]{2,1,0:T(8,128)S(1)} %collective-permute-done.5.refs_6_), channel_id=1, source_target_pairs={{0,1},{1,0},{2,3},{3,2},{4,5},{5,4},{6,7},{7,6},{8,9},{9,8},{10,11... | collective-permute-start | bytes 393224 | tf_op jit(solution)/shard_map/ppermute | solution.py:242
  18.7 3.9 %collective-permute-start.3 = (f32[2,128,128]{2,1,0:T(8,128)S(1)}, f32[2,128,128]{2,1,0:T(8,128)S(1)}, u32[]{:S(2)}, u32[]{:S(2)}) collective-permute-start(f32[2,128,128]{2,1,0:T(8,128)S(1)} %collective-permute-done.2.refs_2_), channel_id=1, source_target_pairs={{0,1},{1,0},{2,3},{3,2},{4,5},{5,4},{6,7},{7,6},{8,9},{9,8},{10,11... | collective-permute-start | bytes 393224 | tf_op jit(solution)/shard_map/ppermute | solution.py:242
  19.2 3.5 %collective-permute-start.4 = (f32[2,128,128]{2,1,0:T(8,128)S(1)}, f32[2,128,128]{2,1,0:T(8,128)S(1)}, u32[]{:S(2)}, u32[]{:S(2)}) collective-permute-start(f32[2,128,128]{2,1,0:T(8,128)S(1)} %collective-permute-done.refs_4_), channel_id=1, source_target_pairs={{0,1},{1,0},{2,3},{3,2},{4,5},{5,4},{6,7},{7,6},{8,9},{9,8},{10,11... | collective-permute-start | bytes 393224 | tf_op jit(solution)/shard_map/ppermute | solution.py:242
  19.3 3.9 %collective-permute-start.1 = (f32[2,128,128]{2,1,0:T(8,128)S(1)}, f32[2,128,128]{2,1,0:T(8,128)S(1)}, u32[]{:S(2)}, u32[]{:S(2)}) collective-permute-start(f32[2,128,128]{2,1,0:T(8,128)S(1)} %get-tuple-element.46.refs_0_.vector_ref), channel_id=1, source_target_pairs={{0,1},{1,0},{2,3},{3,2},{4,5},{5,4},{6,7},{7,6},{8,9},{9,8},{10,11... | collective-permute-start | bytes 393224 | tf_op jit(solution)/shard_map/ppermute | solution.py:242
  22.1 1.9 %collective-permute-start.10 = (f32[2,128,128]{2,1,0:T(8,128)S(1)}, f32[2,128,128]{2,1,0:T(8,128)S(1)}, u32[]{:S(2)}, u32[]{:S(2)}) collective-permute-start(f32[2,128,128]{2,1,0:T(8,128)S(1)} %collective-permute-done.7.refs_8_), channel_id=1, source_target_pairs={{0,1},{1,0},{2,3},{3,2},{4,5},{5,4},{6,7},{7,6},{8,9},{9,8},{10,11... | collective-permute-start | bytes 393224 | tf_op jit(solution)/shard_map/ppermute | solution.py:242
  22.1 1.9 %collective-permute-start.13 = (f32[2,128,128]{2,1,0:T(8,128)S(1)}, f32[2,128,128]{2,1,0:T(8,128)S(1)}, u32[]{:S(2)}, u32[]{:S(2)}) collective-permute-start(f32[2,128,128]{2,1,0:T(8,128)S(1)} %collective-permute-done.8.refs_12_), channel_id=1, source_target_pairs={{0,1},{1,0},{2,3},{3,2},{4,5},{5,4},{6,7},{7,6},{8,9},{9,8},{10,11... | collective-permute-start | bytes 393224 | tf_op jit(solution)/shard_map/ppermute | solution.py:242
  22.6 1.3 %collective-permute-start.12 = (f32[2,128,128]{2,1,0:T(8,128)S(1)}, f32[2,128,128]{2,1,0:T(8,128)S(1)}, u32[]{:S(2)}, u32[]{:S(2)}) collective-permute-start(f32[2,128,128]{2,1,0:T(8,128)S(1)} %collective-permute-done.11.refs_10_), channel_id=1, source_target_pairs={{0,1},{1,0},{2,3},{3,2},{4,5},{5,4},{6,7},{7,6},{8,9},{9,8},{10,11... | collective-permute-start | bytes 393224 | tf_op jit(solution)/shard_map/ppermute | solution.py:242
  22.7 1.5 %collective-permute-start.14 = (f32[2,128,128]{2,1,0:T(8,128)S(1)}, f32[2,128,128]{2,1,0:T(8,128)S(1)}, u32[]{:S(2)}, u32[]{:S(2)}) collective-permute-start(f32[2,128,128]{2,1,0:T(8,128)S(1)} %collective-permute-done.9.refs_14_), channel_id=1, source_target_pairs={{0,1},{1,0},{2,3},{3,2},{4,5},{5,4},{6,7},{7,6},{8,9},{9,8},{10,11... | collective-permute-start | bytes 393224 | tf_op jit(solution)/shard_map/ppermute | solution.py:242
  30.3 8.7 %collective-permute-start.15 = (f32[648,128]{1,0:T(8,128)S(1)}, f32[648,128]{1,0:T(8,128)S(1)}, u32[]{:S(2)}, u32[]{:S(2)}) collective-permute-start(f32[648,128]{1,0:T(8,128)S(1)} %get-tuple-element.52.far_in), channel_id=1, source_target_pairs={{0,1},{1,0},{2,3},{3,2},{4,5},{5,4},{6,7},{7,6},{8,9},{9,8},{10,11... | collective-permute-start | bytes 995336 | tf_op jit(solution)/shard_map/ppermute | solution.py:242
  30.6 8.3 %collective-permute-start.16 = (f32[264,128]{1,0:T(8,128)S(1)}, f32[264,128]{1,0:T(8,128)S(1)}, u32[]{:S(2)}, u32[]{:S(2)}) collective-permute-start(f32[264,128]{1,0:T(8,128)S(1)} %get-tuple-element.53), channel_id=1, source_target_pairs={{0,2},{1,3},{2,0},{3,1},{4,6},{5,7},{6,4},{7,5},{8,10},{9,11},{10,... | collective-permute-start | bytes 405512 | tf_op jit(solution)/shard_map/ppermute | solution.py:242
  32.0 6.9 %collective-permute-start.17 = (f32[264,128]{1,0:T(8,128)S(1)}, f32[264,128]{1,0:T(8,128)S(1)}, u32[]{:S(2)}, u32[]{:S(2)}) collective-permute-start(f32[264,128]{1,0:T(8,128)S(1)} %get-tuple-element.54), channel_id=1, source_target_pairs={{0,3},{1,2},{2,1},{3,0},{4,7},{5,6},{6,5},{7,4},{8,11},{9,10},{10,... | collective-permute-start | bytes 405512 | tf_op jit(solution)/shard_map/ppermute | solution.py:242
  32.2 5.7 %collective-permute-start.18 = (f32[128,128]{1,0:T(8,128)S(1)}, f32[128,128]{1,0:T(8,128)S(1)}, u32[]{:S(2)}, u32[]{:S(2)}) collective-permute-start(f32[128,128]{1,0:T(8,128)S(1)} %get-tuple-element.55), channel_id=1, source_target_pairs={{0,4},{1,5},{2,6},{3,7},{4,0},{5,1},{6,2},{7,3},{8,12},{9,13},{10,... | collective-permute-start | bytes 196616 | tf_op jit(solution)/shard_map/ppermute | solution.py:242
  35.0 3.9 %collective-permute-start.19 = (f32[128,128]{1,0:T(8,128)S(1)}, f32[128,128]{1,0:T(8,128)S(1)}, u32[]{:S(2)}, u32[]{:S(2)}) collective-permute-start(f32[128,128]{1,0:T(8,128)S(1)} %get-tuple-element.56), channel_id=1, source_target_pairs={{0,5},{1,4},{2,7},{3,6},{4,1},{5,0},{6,3},{7,2},{8,13},{9,12},{10,... | collective-permute-start | bytes 196616 | tf_op jit(solution)/shard_map/ppermute | solution.py:242
  39.0 17.1 %copy-start = (f32[2,128,128]{2,1,0:T(8,128)S(1)}, f32[2,128,128]{2,1,0:T(8,128)}, u32[]{:S(2)}) copy-start(f32[2,128,128]{2,1,0:T(8,128)} %precond_ref.3) | copy-start | bytes 393220
  39.7 9.4 %collective-permute-start.21 = (f32[264,128]{1,0:T(8,128)S(1)}, f32[264,128]{1,0:T(8,128)S(1)}, u32[]{:S(2)}, u32[]{:S(2)}) collective-permute-start(f32[264,128]{1,0:T(8,128)S(1)} %get-tuple-element.61), channel_id=1, source_target_pairs={{0,12},{1,13},{2,14},{3,15},{4,8},{5,9},{6,10},{7,11},{8,4},{9,5},... | collective-permute-start | bytes 405512 | tf_op jit(solution)/shard_map/ppermute | solution.py:242
  42.3 13.8 %collective-permute-start.22 = (f32[264,128]{1,0:T(8,128)S(1)}, f32[264,128]{1,0:T(8,128)S(1)}, u32[]{:S(2)}, u32[]{:S(2)}) collective-permute-start(f32[264,128]{1,0:T(8,128)S(1)} %get-tuple-element.62), channel_id=1, source_target_pairs={{0,8},{1,9},{2,10},{3,11},{4,12},{5,13},{6,14},{7,15},{8,0},{9,1},... | collective-permute-start | bytes 405512 | tf_op jit(solution)/shard_map/ppermute | solution.py:242
  43.5 12.5 %collective-permute-start.23 = (f32[264,128]{1,0:T(8,128)S(1)}, f32[264,128]{1,0:T(8,128)S(1)}, u32[]{:S(2)}, u32[]{:S(2)}) collective-permute-start(f32[264,128]{1,0:T(8,128)S(1)} %get-tuple-element.60.refs_0_), channel_id=1, source_target_pairs={{0,4},{1,5},{2,6},{3,7},{4,0},{5,1},{6,2},{7,3},{8,12},{9,13},{10,... | collective-permute-start | bytes 405512 | tf_op jit(solution)/shard_map/ppermute | solution.py:242
  44.2 5.0 %collective-permute-start.20 = (f32[2,128,128]{2,1,0:T(8,128)S(1)}, f32[2,128,128]{2,1,0:T(8,128)S(1)}, u32[]{:S(2)}, u32[]{:S(2)}) collective-permute-start(f32[2,128,128]{2,1,0:T(8,128)S(1)} %get-tuple-element.58), channel_id=1, source_target_pairs={{0,2},{1,3},{2,0},{3,1},{4,6},{5,7},{6,4},{7,5},{8,10},{9,11},{10,... | collective-permute-start | bytes 393224 | tf_op jit(solution)/shard_map/ppermute | solution.py:242
  56.2 8.3 %collective-permute-start.25 = (f32[2,128,128]{2,1,0:T(8,128)S(1)}, f32[2,128,128]{2,1,0:T(8,128)S(1)}, u32[]{:S(2)}, u32[]{:S(2)}) collective-permute-start(f32[2,128,128]{2,1,0:T(8,128)S(1)} %step.1.refs_0_.vector_ref), channel_id=1, source_target_pairs={{0,12},{1,13},{2,14},{3,15},{4,8},{5,9},{6,10},{7,11},{8,4},{9,5},... | collective-permute-start | bytes 393224 | tf_op jit(solution)/shard_map/ppermute | solution.py:242
  58.8 11.5 %collective-permute-start.32 = (f32[2,128,128]{2,1,0:T(8,128)S(1)}, f32[2,128,128]{2,1,0:T(8,128)S(1)}, u32[]{:S(2)}, u32[]{:S(2)}) collective-permute-start(f32[2,128,128]{2,1,0:T(8,128)S(1)} %step.1.refs_0_.vector_ref), channel_id=1, source_target_pairs={{0,6},{1,7},{2,4},{3,5},{4,2},{5,3},{6,0},{7,1},{8,14},{9,15},{10,... | collective-permute-start | bytes 393224 | tf_op jit(solution)/shard_map/ppermute | solution.py:242
  58.8 13.3 %collective-permute-start.30 = (f32[2,128,128]{2,1,0:T(8,128)S(1)}, f32[2,128,128]{2,1,0:T(8,128)S(1)}, u32[]{:S(2)}, u32[]{:S(2)}) collective-permute-start(f32[2,128,128]{2,1,0:T(8,128)S(1)} %step.1.refs_0_.vector_ref), channel_id=1, source_target_pairs={{0,4},{1,5},{2,6},{3,7},{4,0},{5,1},{6,2},{7,3},{8,12},{9,13},{10,... | collective-permute-start | bytes 393224 | tf_op jit(solution)/shard_map/ppermute | solution.py:242
  61.8 10.3 %collective-permute-start.28 = (f32[2,128,128]{2,1,0:T(8,128)S(1)}, f32[2,128,128]{2,1,0:T(8,128)S(1)}, u32[]{:S(2)}, u32[]{:S(2)}) collective-permute-start(f32[2,128,128]{2,1,0:T(8,128)S(1)} %step.1.refs_0_.vector_ref), channel_id=1, source_target_pairs={{0,2},{1,3},{2,0},{3,1},{4,6},{5,7},{6,4},{7,5},{8,10},{9,11},{10,... | collective-permute-start | bytes 393224 | tf_op jit(solution)/shard_map/ppermute | solution.py:242
  62.3 10.4 %collective-permute-start.24 = (f32[2,128,128]{2,1,0:T(8,128)S(1)}, f32[2,128,128]{2,1,0:T(8,128)S(1)}, u32[]{:S(2)}, u32[]{:S(2)}) collective-permute-start(f32[2,128,128]{2,1,0:T(8,128)S(1)} %step.1.refs_0_.vector_ref), channel_id=1, source_target_pairs={{0,8},{1,9},{2,10},{3,11},{4,12},{5,13},{6,14},{7,15},{8,0},{9,1},... | collective-permute-start | bytes 393224 | tf_op jit(solution)/shard_map/ppermute | solution.py:242
  64.5 9.5 %collective-permute-start.26 = (f32[2,128,128]{2,1,0:T(8,128)S(1)}, f32[2,128,128]{2,1,0:T(8,128)S(1)}, u32[]{:S(2)}, u32[]{:S(2)}) collective-permute-start(f32[2,128,128]{2,1,0:T(8,128)S(1)} %collective-permute-done.25.refs_12_), channel_id=1, source_target_pairs={{0,2},{1,3},{2,0},{3,1},{4,6},{5,7},{6,4},{7,5},{8,10},{9,11},{10,... | collective-permute-start | bytes 393224 | tf_op jit(solution)/shard_map/ppermute | solution.py:242
  70.3 3.8 %collective-permute-start.33 = (f32[2,128,128]{2,1,0:T(8,128)S(1)}, f32[2,128,128]{2,1,0:T(8,128)S(1)}, u32[]{:S(2)}, u32[]{:S(2)}) collective-permute-start(f32[2,128,128]{2,1,0:T(8,128)S(1)} %collective-permute-done.32.refs_6_), channel_id=1, source_target_pairs={{0,1},{1,0},{2,3},{3,2},{4,5},{5,4},{6,7},{7,6},{8,9},{9,8},{10,11... | collective-permute-start | bytes 393224 | tf_op jit(solution)/shard_map/ppermute | solution.py:242
  72.1 2.4 %collective-permute-start.31 = (f32[2,128,128]{2,1,0:T(8,128)S(1)}, f32[2,128,128]{2,1,0:T(8,128)S(1)}, u32[]{:S(2)}, u32[]{:S(2)}) collective-permute-start(f32[2,128,128]{2,1,0:T(8,128)S(1)} %collective-permute-done.30.refs_4_), channel_id=1, source_target_pairs={{0,1},{1,0},{2,3},{3,2},{4,5},{5,4},{6,7},{7,6},{8,9},{9,8},{10,11... | collective-permute-start | bytes 393224 | tf_op jit(solution)/shard_map/ppermute | solution.py:242
  72.1 2.5 %collective-permute-start.29 = (f32[2,128,128]{2,1,0:T(8,128)S(1)}, f32[2,128,128]{2,1,0:T(8,128)S(1)}, u32[]{:S(2)}, u32[]{:S(2)}) collective-permute-start(f32[2,128,128]{2,1,0:T(8,128)S(1)} %collective-permute-done.28.refs_2_), channel_id=1, source_target_pairs={{0,1},{1,0},{2,3},{3,2},{4,5},{5,4},{6,7},{7,6},{8,9},{9,8},{10,11... | collective-permute-start | bytes 393224 | tf_op jit(solution)/shard_map/ppermute | solution.py:242
  72.6 5.5 %collective-permute-start.35 = (f32[2,128,128]{2,1,0:T(8,128)S(1)}, f32[2,128,128]{2,1,0:T(8,128)S(1)}, u32[]{:S(2)}, u32[]{:S(2)}) collective-permute-start(f32[2,128,128]{2,1,0:T(8,128)S(1)} %collective-permute-done.24.refs_8_), channel_id=1, source_target_pairs={{0,2},{1,3},{2,0},{3,1},{4,6},{5,7},{6,4},{7,5},{8,10},{9,11},{10,... | collective-permute-start | bytes 393224 | tf_op jit(solution)/shard_map/ppermute | solution.py:242
  74.0 4.1 %collective-permute-start.34 = (f32[2,128,128]{2,1,0:T(8,128)S(1)}, f32[2,128,128]{2,1,0:T(8,128)S(1)}, u32[]{:S(2)}, u32[]{:S(2)}) collective-permute-start(f32[2,128,128]{2,1,0:T(8,128)S(1)} %collective-permute-done.24.refs_8_), channel_id=1, source_target_pairs={{0,1},{1,0},{2,3},{3,2},{4,5},{5,4},{6,7},{7,6},{8,9},{9,8},{10,11... | collective-permute-start | bytes 393224 | tf_op jit(solution)/shard_map/ppermute | solution.py:242
  74.1 4.1 %collective-permute-start.37 = (f32[2,128,128]{2,1,0:T(8,128)S(1)}, f32[2,128,128]{2,1,0:T(8,128)S(1)}, u32[]{:S(2)}, u32[]{:S(2)}) collective-permute-start(f32[2,128,128]{2,1,0:T(8,128)S(1)} %collective-permute-done.25.refs_12_), channel_id=1, source_target_pairs={{0,1},{1,0},{2,3},{3,2},{4,5},{5,4},{6,7},{7,6},{8,9},{9,8},{10,11... | collective-permute-start | bytes 393224 | tf_op jit(solution)/shard_map/ppermute | solution.py:242
  74.6 3.6 %collective-permute-start.38 = (f32[2,128,128]{2,1,0:T(8,128)S(1)}, f32[2,128,128]{2,1,0:T(8,128)S(1)}, u32[]{:S(2)}, u32[]{:S(2)}) collective-permute-start(f32[2,128,128]{2,1,0:T(8,128)S(1)} %collective-permute-done.26.refs_14_), channel_id=1, source_target_pairs={{0,1},{1,0},{2,3},{3,2},{4,5},{5,4},{6,7},{7,6},{8,9},{9,8},{10,11... | collective-permute-start | bytes 393224 | tf_op jit(solution)/shard_map/ppermute | solution.py:242
  74.6 3.5 %collective-permute-start.27 = (f32[2,128,128]{2,1,0:T(8,128)S(1)}, f32[2,128,128]{2,1,0:T(8,128)S(1)}, u32[]{:S(2)}, u32[]{:S(2)}) collective-permute-start(f32[2,128,128]{2,1,0:T(8,128)S(1)} %step.1.refs_0_.vector_ref), channel_id=1, source_target_pairs={{0,1},{1,0},{2,3},{3,2},{4,5},{5,4},{6,7},{7,6},{8,9},{9,8},{10,11... | collective-permute-start | bytes 393224 | tf_op jit(solution)/shard_map/ppermute | solution.py:242
  78.1 1.3 %collective-permute-start.36 = (f32[2,128,128]{2,1,0:T(8,128)S(1)}, f32[2,128,128]{2,1,0:T(8,128)S(1)}, u32[]{:S(2)}, u32[]{:S(2)}) collective-permute-start(f32[2,128,128]{2,1,0:T(8,128)S(1)} %collective-permute-done.35.refs_10_), channel_id=1, source_target_pairs={{0,1},{1,0},{2,3},{3,2},{4,5},{5,4},{6,7},{7,6},{8,9},{9,8},{10,11... | collective-permute-start | bytes 393224 | tf_op jit(solution)/shard_map/ppermute | solution.py:242
  85.8 8.5 %collective-permute-start.39 = (f32[648,128]{1,0:T(8,128)S(1)}, f32[648,128]{1,0:T(8,128)S(1)}, u32[]{:S(2)}, u32[]{:S(2)}) collective-permute-start(f32[648,128]{1,0:T(8,128)S(1)} %get-tuple-element.68.far_in), channel_id=1, source_target_pairs={{0,1},{1,0},{2,3},{3,2},{4,5},{5,4},{6,7},{7,6},{8,9},{9,8},{10,11... | collective-permute-start | bytes 995336 | tf_op jit(solution)/shard_map/ppermute | solution.py:242
  85.9 7.0 %collective-permute-start.40 = (f32[264,128]{1,0:T(8,128)S(1)}, f32[264,128]{1,0:T(8,128)S(1)}, u32[]{:S(2)}, u32[]{:S(2)}) collective-permute-start(f32[264,128]{1,0:T(8,128)S(1)} %get-tuple-element.69), channel_id=1, source_target_pairs={{0,2},{1,3},{2,0},{3,1},{4,6},{5,7},{6,4},{7,5},{8,10},{9,11},{10,... | collective-permute-start | bytes 405512 | tf_op jit(solution)/shard_map/ppermute | solution.py:242
  87.2 7.1 %collective-permute-start.41 = (f32[264,128]{1,0:T(8,128)S(1)}, f32[264,128]{1,0:T(8,128)S(1)}, u32[]{:S(2)}, u32[]{:S(2)}) collective-permute-start(f32[264,128]{1,0:T(8,128)S(1)} %get-tuple-element.70), channel_id=1, source_target_pairs={{0,3},{1,2},{2,1},{3,0},{4,7},{5,6},{6,5},{7,4},{8,11},{9,10},{10,... | collective-permute-start | bytes 405512 | tf_op jit(solution)/shard_map/ppermute | solution.py:242
  87.7 4.9 %collective-permute-start.42 = (f32[128,128]{1,0:T(8,128)S(1)}, f32[128,128]{1,0:T(8,128)S(1)}, u32[]{:S(2)}, u32[]{:S(2)}) collective-permute-start(f32[128,128]{1,0:T(8,128)S(1)} %get-tuple-element.71), channel_id=1, source_target_pairs={{0,4},{1,5},{2,6},{3,7},{4,0},{5,1},{6,2},{7,3},{8,12},{9,13},{10,... | collective-permute-start | bytes 196616 | tf_op jit(solution)/shard_map/ppermute | solution.py:242
  87.7 5.2 %collective-permute-start.43 = (f32[128,128]{1,0:T(8,128)S(1)}, f32[128,128]{1,0:T(8,128)S(1)}, u32[]{:S(2)}, u32[]{:S(2)}) collective-permute-start(f32[128,128]{1,0:T(8,128)S(1)} %get-tuple-element.72), channel_id=1, source_target_pairs={{0,5},{1,4},{2,7},{3,6},{4,1},{5,0},{6,3},{7,2},{8,13},{9,12},{10,... | collective-permute-start | bytes 196616 | tf_op jit(solution)/shard_map/ppermute | solution.py:242
  95.0 9.4 %collective-permute-start.45 = (f32[264,128]{1,0:T(8,128)S(1)}, f32[264,128]{1,0:T(8,128)S(1)}, u32[]{:S(2)}, u32[]{:S(2)}) collective-permute-start(f32[264,128]{1,0:T(8,128)S(1)} %get-tuple-element.77), channel_id=1, source_target_pairs={{0,12},{1,13},{2,14},{3,15},{4,8},{5,9},{6,10},{7,11},{8,4},{9,5},... | collective-permute-start | bytes 405512 | tf_op jit(solution)/shard_map/ppermute | solution.py:242
  97.2 11.2 %collective-permute-start.46 = (f32[264,128]{1,0:T(8,128)S(1)}, f32[264,128]{1,0:T(8,128)S(1)}, u32[]{:S(2)}, u32[]{:S(2)}) collective-permute-start(f32[264,128]{1,0:T(8,128)S(1)} %get-tuple-element.78), channel_id=1, source_target_pairs={{0,8},{1,9},{2,10},{3,11},{4,12},{5,13},{6,14},{7,15},{8,0},{9,1},... | collective-permute-start | bytes 405512 | tf_op jit(solution)/shard_map/ppermute | solution.py:242
  97.2 11.2 %collective-permute-start.47 = (f32[264,128]{1,0:T(8,128)S(1)}, f32[264,128]{1,0:T(8,128)S(1)}, u32[]{:S(2)}, u32[]{:S(2)}) collective-permute-start(f32[264,128]{1,0:T(8,128)S(1)} %get-tuple-element.76.refs_0_), channel_id=1, source_target_pairs={{0,4},{1,5},{2,6},{3,7},{4,0},{5,1},{6,2},{7,3},{8,12},{9,13},{10,... | collective-permute-start | bytes 405512 | tf_op jit(solution)/shard_map/ppermute | solution.py:242
  99.4 5.0 %collective-permute-start.44 = (f32[2,128,128]{2,1,0:T(8,128)S(1)}, f32[2,128,128]{2,1,0:T(8,128)S(1)}, u32[]{:S(2)}, u32[]{:S(2)}) collective-permute-start(f32[2,128,128]{2,1,0:T(8,128)S(1)} %get-tuple-element.74), channel_id=1, source_target_pairs={{0,2},{1,3},{2,0},{3,1},{4,6},{5,7},{6,4},{7,5},{8,10},{9,11},{10,... | collective-permute-start | bytes 393224 | tf_op jit(solution)/shard_map/ppermute | solution.py:242

commit v15 on v10

--- a/solution.py
+++ b/solution.py
@@ -354,11 +354,11 @@
         pieces[k] = swapped(x, k)
     pieces[ROW] = swapped(x, ROW)
     pieces[COLUMN] = swapped(x, COLUMN)
+    if held is not None:
+        pieces[n - 4], pieces[0] = lax.optimization_barrier((pieces[n - 4], held))
     for k in reversed(range(8, n, 4)):
         pieces[k + ROW] = swapped(pieces[k], ROW)
     pieces[COLUMN + ROW] = swapped(pieces[ROW], COLUMN)
-    if held is not None:
-        pieces[n - 4 + ROW], pieces[0] = lax.optimization_barrier((pieces[n - 4 + ROW], held))
     for k in range(0, n, 2):
         pieces[k + CORE] = swapped(pieces[k], CORE)
     return [pieces[k] for k in range(n)]

time: 123 us -> 120 us (0.976)
  starting transfers between devices: 48.2 us -> 35.9 us
  waiting for transfers between devices: 44.1 us -> 52.1 us
  blocking collectives: 10.3 us -> 11.8 us
    ppermute x48, starting transfers between devices: 48.2 us -> 35.9 us  [swapped(): return lax.ppermute(x, 'term', [(i, i ^ k) for i in range(n)])]
    ppermute x48, waiting for transfers between devices: 44.1 us -> 52.1 us  [swapped(): return lax.ppermute(x, 'term', [(i, i ^ k) for i in range(n)])]
    all_to_all x1, blocking collectives: 10.3 us -> 11.8 us  [shards(): lax.all_to_all(jnp.broadcast_to(partial[None], (n, 8, width)), 'term', sp...]
  transfers between devices with their start and end apart: 48 -> 48, of which waited for: 19 -> 24; matrix products, arithmetic and copies ran while one was open for 0% -> 0% of each run, Pallas kernels for 2% -> 2%
where the time goes in v15:
time: 120 us
  waiting for transfers between devices  52.1 us (43%)
  starting transfers between devices  35.9 us (30%)
  Pallas kernels  18 us (15%)
  blocking collectives  11.8 us (10%)
  between operations  1.41 us (1%)
    ppermute x48, waiting for transfers between devices, swapped(): return lax.ppermute(x, 'term', [(i, i ^ k) for i in range(n)])  52.1 us
    ppermute x48, starting transfers between devices, swapped(): return lax.ppermute(x, 'term', [(i, i ^ k) for i in range(n)])  35.9 us
    pallas_call x2, Pallas kernels, apply(): pl.pallas_call(functools.partial(apply_kernel, n, npairs, over_rows, rows...  12 us
    all_to_all x1, blocking collectives, shards(): lax.all_to_all(jnp.broadcast_to(partial[None], (n, 8, width)), 'term', sp...  11.8 us
    pallas_call x5, Pallas kernels, local(): pl.pallas_call(kernel, out_shape=out_shape, in_specs=[SMEM] * len(scalars...  3.42 us
    pallas_call x1, Pallas kernels, prep(): pl.pallas_call(functools.partial(prep_kernel, n, terms * n + 1), out_shap...  2.51 us
  transfers between devices with their start and end apart: 48, of which 24 were waited for; matrix products, arithmetic and copies ran while one was open for 0% of the time, Pallas kernels for 2%

profile of v15, /device:TPU:0, one launch (start us, length us, event | category | flops | bytes accessed | tf_op | source)
XLA Modules:
  0.0 119.8 jit_solution(3852705920481856616)
XLA Ops:
  0.6 3.0 %collective-permute-start.2 = (f32[2,128,128]{2,1,0:T(8,128)}, f32[2,128,128]{2,1,0:T(8,128)S(1)}, u32[]{:S(2)}, u32[]{:S(2)}) collective-permute-start(f32[2,128,128]{2,1,0:T(8,128)} %vector_in.1), channel_id=1, source_target_pairs={{0,2},{1,3},{2,0},{3,1},{4,6},{5,7},{6,4},{7,5},{8,10},{9,11},{10,... | collective-permute-start | bytes 393224 | tf_op jit(solution)/shard_map/ppermute | solution.py:242
  3.7 2.6 %collective-permute-start.8 = (f32[2,128,128]{2,1,0:T(8,128)}, f32[2,128,128]{2,1,0:T(8,128)S(1)}, u32[]{:S(2)}, u32[]{:S(2)}) collective-permute-start(f32[2,128,128]{2,1,0:T(8,128)} %vector_in.1), channel_id=1, source_target_pairs={{0,8},{1,9},{2,10},{3,11},{4,12},{5,13},{6,14},{7,15},{8,0},{9,1},... | collective-permute-start | bytes 393224 | tf_op jit(solution)/shard_map/ppermute | solution.py:242
  6.3 1.3 %collective-permute-start = (f32[2,128,128]{2,1,0:T(8,128)}, f32[2,128,128]{2,1,0:T(8,128)S(1)}, u32[]{:S(2)}, u32[]{:S(2)}) collective-permute-start(f32[2,128,128]{2,1,0:T(8,128)} %vector_in.1), channel_id=1, source_target_pairs={{0,12},{1,13},{2,14},{3,15},{4,8},{5,9},{6,10},{7,11},{8,4},{9,5},... | collective-permute-start | bytes 393224 | tf_op jit(solution)/shard_map/ppermute | solution.py:242
  7.6 0.2 collective-permute-start.4
  7.8 1.8 %collective-permute-start.6 = (f32[2,128,128]{2,1,0:T(8,128)S(1)}, f32[2,128,128]{2,1,0:T(8,128)S(1)}, u32[]{:S(2)}, u32[]{:S(2)}) collective-permute-start(f32[2,128,128]{2,1,0:T(8,128)S(1)} %collective-permute-done.2.refs_2_), channel_id=1, source_target_pairs={{0,4},{1,5},{2,6},{3,7},{4,0},{5,1},{6,2},{7,3},{8,12},{9,13},{10,... | collective-permute-start | bytes 393224 | tf_op jit(solution)/shard_map/ppermute | solution.py:242
  10.3 0.6 copy.12
  10.9 2.5 %prep.1 = (bf16[8,128,512]{2,1,0:T(8,128)(2,1)S(1)}, bf16[2048,256]{1,0:T(8,128)(2,1)S(1)}, s32[721]{0:T(1024)S(1)}, f32[2,128,128]{2,1,0:T(8,128)S(1)}) custom-call(s32[1]{0:T(128)} %bitcast.me_ref, s32[16,16]{1,0:T(8,128)} %fetch_in.1, s32[16,16]{1,0:T(8,128)} %store_in.1, s32[384]{0:T(512)} %bitcast.8, s32[1]{0:T(128)S(6)} %copy.13.live_in, ...), custom_call_target="tpu_custom_call" | custom-call | tf_op jit(solution)/shard_map/prep/pallas_call | solution.py:132
  13.5 3.0 %collective-permute-done.8.refs_8_ = f32[2,128,128]{2,1,0:T(8,128)S(1)} collective-permute-done((f32[2,128,128]{2,1,0:T(8,128)}, f32[2,128,128]{2,1,0:T(8,128)S(1)}, u32[]{:S(2)}, u32[]{:S(2)}) %collective-permute-start.8) | collective-permute-done | bytes 131104 | tf_op jit(solution)/shard_map/ppermute | solution.py:242
  16.5 0.4 collective-permute-start.10
  17.0 1.1 collective-permute-done.4.refs_4_
  18.1 1.4 %collective-permute-done.6.refs_6_ = f32[2,128,128]{2,1,0:T(8,128)S(1)} collective-permute-done((f32[2,128,128]{2,1,0:T(8,128)S(1)}, f32[2,128,128]{2,1,0:T(8,128)S(1)}, u32[]{:S(2)}, u32[]{:S(2)}) %collective-permute-start.6) | collective-permute-done | bytes 131104 | tf_op jit(solution)/shard_map/ppermute | solution.py:242
  19.5 0.5 collective-permute-start.13
  20.0 1.8 %collective-permute-done.10.refs_10_ = f32[2,128,128]{2,1,0:T(8,128)S(1)} collective-permute-done((f32[2,128,128]{2,1,0:T(8,128)S(1)}, f32[2,128,128]{2,1,0:T(8,128)S(1)}, u32[]{:S(2)}, u32[]{:S(2)}) %collective-permute-start.10) | collective-permute-done | bytes 131104 | tf_op jit(solution)/shard_map/ppermute | solution.py:242
  21.8 0.5 collective-permute-start.7
  22.3 2.1 %collective-permute-done.13.refs_14_ = f32[2,128,128]{2,1,0:T(8,128)S(1)} collective-permute-done((f32[2,128,128]{2,1,0:T(8,128)S(1)}, f32[2,128,128]{2,1,0:T(8,128)S(1)}, u32[]{:S(2)}, u32[]{:S(2)}) %collective-permute-start.13) | collective-permute-done | bytes 131104 | tf_op jit(solution)/shard_map/ppermute | solution.py:242
  24.5 1.3 %collective-permute-done.14.refs_15_ = f32[2,128,128]{2,1,0:T(8,128)S(1)} collective-permute-done((f32[2,128,128]{2,1,0:T(8,128)S(1)}, f32[2,128,128]{2,1,0:T(8,128)S(1)}, u32[]{:S(2)}, u32[]{:S(2)}) %collective-permute-start.14) | collective-permute-done | bytes 131104 | tf_op jit(solution)/shard_map/ppermute | solution.py:242
  25.8 5.9 %apply.2 = (f32[640,128]{1,0:T(8,128)S(1)}, f32[648,128]{1,0:T(8,128)S(1)}, f32[264,128]{1,0:T(8,128)S(1)}, f32[264,128]{1,0:T(8,128)S(1)}, f32[128,128]{1,0:T(8...) custom-call(s32[721]{0:T(1024)S(1)} %get-tuple-element.35.table_ref, ...), custom_call_target="tpu_custom_call" | custom-call | tf_op jit(solution)/shard_map/apply/pallas_call | solution.py:216
  31.8 0.3 collective-permute-start.15
  32.1 0.4 collective-permute-start.16
  32.5 1.2 collective-permute-start.17
  33.7 0.5 collective-permute-start.18
  34.2 1.4 %collective-permute-start.19 = (f32[128,128]{1,0:T(8,128)S(1)}, f32[128,128]{1,0:T(8,128)S(1)}, u32[]{:S(2)}, u32[]{:S(2)}) collective-permute-start(f32[128,128]{1,0:T(8,128)S(1)} %get-tuple-element.46), channel_id=1, source_target_pairs={{0,5},{1,4},{2,7},{3,6},{4,1},{5,0},{6,3},{7,2},{8,13},{9,12},{10,... | collective-permute-start | bytes 196616 | tf_op jit(solution)/shard_map/ppermute | solution.py:242
  35.6 3.0 %collective-permute-done.18.column_ref = f32[128,128]{1,0:T(8,128)S(1)} collective-permute-done((f32[128,128]{1,0:T(8,128)S(1)}, f32[128,128]{1,0:T(8,128)S(1)}, u32[]{:S(2)}, u32[]{:S(2)}) %collective-permute-start.18) | collective-permute-done | bytes 65568 | tf_op jit(solution)/shard_map/ppermute | solution.py:242
  38.6 0.7 collective-permute-done.19.column_far_ref
  39.3 0.8 collective-permute-done.17.row_far_ref
  40.1 0.7 fold.2
  40.8 4.0 %collective-permute-start.21 = (f32[264,128]{1,0:T(8,128)S(1)}, f32[264,128]{1,0:T(8,128)S(1)}, u32[]{:S(2)}, u32[]{:S(2)}) collective-permute-start(f32[264,128]{1,0:T(8,128)S(1)} %get-tuple-element.51), channel_id=1, source_target_pairs={{0,12},{1,13},{2,14},{3,15},{4,8},{5,9},{6,10},{7,11},{8,4},{9,5},... | collective-permute-start | bytes 405512 | tf_op jit(solution)/shard_map/ppermute | solution.py:242
  44.8 0.6 collective-permute-start.23
  45.4 0.7 collective-permute-start.20
  46.1 4.4 %collective-permute-done.20.step_ref = f32[2,128,128]{2,1,0:T(8,128)S(1)} collective-permute-done((f32[2,128,128]{2,1,0:T(8,128)S(1)}, f32[2,128,128]{2,1,0:T(8,128)S(1)}, u32[]{:S(2)}, u32[]{:S(2)}) %collective-permute-start.20) | collective-permute-done | bytes 131104 | tf_op jit(solution)/shard_map/ppermute | solution.py:242
  50.5 5.7 %collective-permute-done.22.refs_2_ = f32[264,128]{1,0:T(8,128)S(1)} collective-permute-done((f32[264,128]{1,0:T(8,128)S(1)}, f32[264,128]{1,0:T(8,128)S(1)}, u32[]{:S(2)}, u32[]{:S(2)}) %collective-permute-start.22) | collective-permute-done | bytes 135200 | tf_op jit(solution)/shard_map/ppermute | solution.py:242
  56.4 2.7 %collective-permute-start.35 = (f32[2,128,128]{2,1,0:T(8,128)S(1)}, f32[2,128,128]{2,1,0:T(8,128)S(1)}, u32[]{:S(2)}, u32[]{:S(2)}) collective-permute-start(f32[2,128,128]{2,1,0:T(8,128)S(1)} %step.1.refs_0_.vector_ref), channel_id=1, source_target_pairs={{0,12},{1,13},{2,14},{3,15},{4,8},{5,9},{6,10},{7,11},{8,4},{9,5},... | collective-permute-start | bytes 393224 | tf_op jit(solution)/shard_map/ppermute | solution.py:242
  59.2 1.7 %collective-permute-start.27 = (f32[2,128,128]{2,1,0:T(8,128)S(1)}, f32[2,128,128]{2,1,0:T(8,128)S(1)}, u32[]{:S(2)}, u32[]{:S(2)}) collective-permute-start(f32[2,128,128]{2,1,0:T(8,128)S(1)} %step.1.refs_0_.vector_ref), channel_id=1, source_target_pairs={{0,4},{1,5},{2,6},{3,7},{4,0},{5,1},{6,2},{7,3},{8,12},{9,13},{10,... | collective-permute-start | bytes 393224 | tf_op jit(solution)/shard_map/ppermute | solution.py:242
  60.9 0.4 collective-permute-start.25
  61.3 3.5 %collective-permute-done.35.refs_12_ = f32[2,128,128]{2,1,0:T(8,128)S(1)} collective-permute-done((f32[2,128,128]{2,1,0:T(8,128)S(1)}, f32[2,128,128]{2,1,0:T(8,128)S(1)}, u32[]{:S(2)}, u32[]{:S(2)}) %collective-permute-start.35) | collective-permute-done | bytes 131104 | tf_op jit(solution)/shard_map/ppermute | solution.py:242
  64.8 0.4 collective-permute-start.37
  65.2 4.4 %collective-permute-done.31.refs_8_ = f32[2,128,128]{2,1,0:T(8,128)S(1)} collective-permute-done((f32[2,128,128]{2,1,0:T(8,128)S(1)}, f32[2,128,128]{2,1,0:T(8,128)S(1)}, u32[]{:S(2)}, u32[]{:S(2)}) %collective-permute-start.31) | collective-permute-done | bytes 131104 | tf_op jit(solution)/shard_map/ppermute | solution.py:242
  69.5 0.3 collective-permute-start.33
  69.9 0.3 collective-permute-start.32
  70.2 0.3 collective-permute-start.26
  70.4 0.4 collective-permute-done.36.refs_13_
  71.0 4.4 %collective-permute-done.33.refs_10_ = f32[2,128,128]{2,1,0:T(8,128)S(1)} collective-permute-done((f32[2,128,128]{2,1,0:T(8,128)S(1)}, f32[2,128,128]{2,1,0:T(8,128)S(1)}, u32[]{:S(2)}, u32[]{:S(2)}) %collective-permute-start.33) | collective-permute-done | bytes 131104 | tf_op jit(solution)/shard_map/ppermute | solution.py:242
  75.4 0.5 collective-permute-start.34
  76.0 0.8 collective-permute-done.38.refs_15_
  77.0 0.3 collective-permute-done.30.refs_7_
  77.3 6.1 %apply.3 = (f32[640,128]{1,0:T(8,128)S(1)}, f32[648,128]{1,0:T(8,128)S(1)}, f32[264,128]{1,0:T(8,128)S(1)}, f32[264,128]{1,0:T(8,128)S(1)}, f32[128,128]{1,0:T(8...) custom-call(s32[721]{0:T(1024)S(1)} %get-tuple-element.35.table_ref, ...), custom_call_target="tpu_custom_call" | custom-call | tf_op jit(solution)/shard_map/apply/pallas_call | solution.py:216
  83.4 0.4 collective-permute-start.39
  83.8 1.5 %collective-permute-start.40 = (f32[264,128]{1,0:T(8,128)S(1)}, f32[264,128]{1,0:T(8,128)S(1)}, u32[]{:S(2)}, u32[]{:S(2)}) collective-permute-start(f32[264,128]{1,0:T(8,128)S(1)} %get-tuple-element.55), channel_id=1, source_target_pairs={{0,2},{1,3},{2,0},{3,1},{4,6},{5,7},{6,4},{7,5},{8,10},{9,11},{10,... | collective-permute-start | bytes 405512 | tf_op jit(solution)/shard_map/ppermute | solution.py:242
  85.3 0.2 collective-permute-start.42
  85.6 1.7 %collective-permute-start.43 = (f32[128,128]{1,0:T(8,128)S(1)}, f32[128,128]{1,0:T(8,128)S(1)}, u32[]{:S(2)}, u32[]{:S(2)}) collective-permute-start(f32[128,128]{1,0:T(8,128)S(1)} %get-tuple-element.58), channel_id=1, source_target_pairs={{0,5},{1,4},{2,7},{3,6},{4,1},{5,0},{6,3},{7,2},{8,13},{9,12},{10,... | collective-permute-start | bytes 196616 | tf_op jit(solution)/shard_map/ppermute | solution.py:242
  87.3 2.9 %collective-permute-done.42.column_ref = f32[128,128]{1,0:T(8,128)S(1)} collective-permute-done((f32[128,128]{1,0:T(8,128)S(1)}, f32[128,128]{1,0:T(8,128)S(1)}, u32[]{:S(2)}, u32[]{:S(2)}) %collective-permute-start.42) | collective-permute-done | bytes 65568 | tf_op jit(solution)/shard_map/ppermute | solution.py:242
  90.2 0.8 collective-permute-done.43.column_far_ref
  91.0 0.6 collective-permute-done.41.row_far_ref
  91.7 0.7 fold.3
  92.4 1.1 collective-permute-start.45
  93.5 1.6 %collective-permute-start.46 = (f32[264,128]{1,0:T(8,128)S(1)}, f32[264,128]{1,0:T(8,128)S(1)}, u32[]{:S(2)}, u32[]{:S(2)}) collective-permute-start(f32[264,128]{1,0:T(8,128)S(1)} %get-tuple-element.64), channel_id=1, source_target_pairs={{0,12},{1,13},{2,14},{3,15},{4,8},{5,9},{6,10},{7,11},{8,4},{9,5},... | collective-permute-start | bytes 405512 | tf_op jit(solution)/shard_map/ppermute | solution.py:242
  95.2 0.8 collective-permute-start.47
  95.9 2.0 %collective-permute-start.44 = (f32[2,128,128]{2,1,0:T(8,128)S(1)}, f32[2,128,128]{2,1,0:T(8,128)S(1)}, u32[]{:S(2)}, u32[]{:S(2)}) collective-permute-start(f32[2,128,128]{2,1,0:T(8,128)S(1)} %get-tuple-element.60), channel_id=1, source_target_pairs={{0,2},{1,3},{2,0},{3,1},{4,6},{5,7},{6,4},{7,5},{8,10},{9,11},{10,... | collective-permute-start | bytes 393224 | tf_op jit(solution)/shard_map/ppermute | solution.py:242
  97.9 3.1 %collective-permute-done.44.step_ref = f32[2,128,128]{2,1,0:T(8,128)S(1)} collective-permute-done((f32[2,128,128]{2,1,0:T(8,128)S(1)}, f32[2,128,128]{2,1,0:T(8,128)S(1)}, u32[]{:S(2)}, u32[]{:S(2)}) %collective-permute-start.44) | collective-permute-done | bytes 131104 | tf_op jit(solution)/shard_map/ppermute | solution.py:242
  101.0 3.9 %collective-permute-done.45.refs_1_ = f32[264,128]{1,0:T(8,128)S(1)} collective-permute-done((f32[264,128]{1,0:T(8,128)S(1)}, f32[264,128]{1,0:T(8,128)S(1)}, u32[]{:S(2)}, u32[]{:S(2)}) %collective-permute-start.45) | collective-permute-done | bytes 135200 | tf_op jit(solution)/shard_map/ppermute | solution.py:242
  105.0 1.3 %collective-permute-done.47.refs_3_ = f32[264,128]{1,0:T(8,128)S(1)} collective-permute-done((f32[264,128]{1,0:T(8,128)S(1)}, f32[264,128]{1,0:T(8,128)S(1)}, u32[]{:S(2)}, u32[]{:S(2)}) %collective-permute-start.47) | collective-permute-done | bytes 135200 | tf_op jit(solution)/shard_map/ppermute | solution.py:242
  106.2 0.9 last.1
  107.1 11.8 %all_to_all.5.tiles_ref = f32[16,8,128]{2,1,0:T(8,128)S(1)} all-to-all(f32[16,8,128]{2,1,0:T(8,128)S(1)} %broadcast_in_dim.2), channel_id=1, replica_groups=mesh['group'=2,'term'=16] {'term'}, dimensions={0} | all-to-all | bytes 131072 | tf_op jit(solution)/shard_map/all_to_all | solution.py:385
  118.9 0.9 norm.1
  (47 shorter events, 1.0 us)
Async XLA Ops:
  0.6 7.2 %collective-permute-start.2 = (f32[2,128,128]{2,1,0:T(8,128)}, f32[2,128,128]{2,1,0:T(8,128)S(1)}, u32[]{:S(2)}, u32[]{:S(2)}) collective-permute-start(f32[2,128,128]{2,1,0:T(8,128)} %vector_in.1), channel_id=1, source_target_pairs={{0,2},{1,3},{2,0},{3,1},{4,6},{5,7},{6,4},{7,5},{8,10},{9,11},{10,... | collective-permute-start | bytes 393224 | tf_op jit(solution)/shard_map/ppermute | solution.py:242
  3.7 12.9 %collective-permute-start.8 = (f32[2,128,128]{2,1,0:T(8,128)}, f32[2,128,128]{2,1,0:T(8,128)S(1)}, u32[]{:S(2)}, u32[]{:S(2)}) collective-permute-start(f32[2,128,128]{2,1,0:T(8,128)} %vector_in.1), channel_id=1, source_target_pairs={{0,8},{1,9},{2,10},{3,11},{4,12},{5,13},{6,14},{7,15},{8,0},{9,1},... | collective-permute-start | bytes 393224 | tf_op jit(solution)/shard_map/ppermute | solution.py:242
  6.3 10.7 %collective-permute-start = (f32[2,128,128]{2,1,0:T(8,128)}, f32[2,128,128]{2,1,0:T(8,128)S(1)}, u32[]{:S(2)}, u32[]{:S(2)}) collective-permute-start(f32[2,128,128]{2,1,0:T(8,128)} %vector_in.1), channel_id=1, source_target_pairs={{0,12},{1,13},{2,14},{3,15},{4,8},{5,9},{6,10},{7,11},{8,4},{9,5},... | collective-permute-start | bytes 393224 | tf_op jit(solution)/shard_map/ppermute | solution.py:242
  7.6 10.5 %collective-permute-start.4 = (f32[2,128,128]{2,1,0:T(8,128)}, f32[2,128,128]{2,1,0:T(8,128)S(1)}, u32[]{:S(2)}, u32[]{:S(2)}) collective-permute-start(f32[2,128,128]{2,1,0:T(8,128)} %vector_in.1), channel_id=1, source_target_pairs={{0,4},{1,5},{2,6},{3,7},{4,0},{5,1},{6,2},{7,3},{8,12},{9,13},{10,... | collective-permute-start | bytes 393224 | tf_op jit(solution)/shard_map/ppermute | solution.py:242
  7.8 11.7 %collective-permute-start.6 = (f32[2,128,128]{2,1,0:T(8,128)S(1)}, f32[2,128,128]{2,1,0:T(8,128)S(1)}, u32[]{:S(2)}, u32[]{:S(2)}) collective-permute-start(f32[2,128,128]{2,1,0:T(8,128)S(1)} %collective-permute-done.2.refs_2_), channel_id=1, source_target_pairs={{0,4},{1,5},{2,6},{3,7},{4,0},{5,1},{6,2},{7,3},{8,12},{9,13},{10,... | collective-permute-start | bytes 393224 | tf_op jit(solution)/shard_map/ppermute | solution.py:242
  9.6 0.7 copy-start.1
  13.4 6.6 %collective-permute-start.3 = (f32[2,128,128]{2,1,0:T(8,128)S(1)}, f32[2,128,128]{2,1,0:T(8,128)S(1)}, u32[]{:S(2)}, u32[]{:S(2)}) collective-permute-start(f32[2,128,128]{2,1,0:T(8,128)S(1)} %collective-permute-done.2.refs_2_), channel_id=1, source_target_pairs={{0,1},{1,0},{2,3},{3,2},{4,5},{5,4},{6,7},{7,6},{8,9},{9,8},{10,11... | collective-permute-start | bytes 393224 | tf_op jit(solution)/shard_map/ppermute | solution.py:242
  16.5 5.2 %collective-permute-start.10 = (f32[2,128,128]{2,1,0:T(8,128)S(1)}, f32[2,128,128]{2,1,0:T(8,128)S(1)}, u32[]{:S(2)}, u32[]{:S(2)}) collective-permute-start(f32[2,128,128]{2,1,0:T(8,128)S(1)} %collective-permute-done.8.refs_8_), channel_id=1, source_target_pairs={{0,2},{1,3},{2,0},{3,1},{4,6},{5,7},{6,4},{7,5},{8,10},{9,11},{10,... | collective-permute-start | bytes 393224 | tf_op jit(solution)/shard_map/ppermute | solution.py:242
  17.0 4.8 %collective-permute-start.9 = (f32[2,128,128]{2,1,0:T(8,128)S(1)}, f32[2,128,128]{2,1,0:T(8,128)S(1)}, u32[]{:S(2)}, u32[]{:S(2)}) collective-permute-start(f32[2,128,128]{2,1,0:T(8,128)S(1)} %collective-permute-done.8.refs_8_), channel_id=1, source_target_pairs={{0,1},{1,0},{2,3},{3,2},{4,5},{5,4},{6,7},{7,6},{8,9},{9,8},{10,11... | collective-permute-start | bytes 393224 | tf_op jit(solution)/shard_map/ppermute | solution.py:242
  18.1 4.2 %collective-permute-start.5 = (f32[2,128,128]{2,1,0:T(8,128)S(1)}, f32[2,128,128]{2,1,0:T(8,128)S(1)}, u32[]{:S(2)}, u32[]{:S(2)}) collective-permute-start(f32[2,128,128]{2,1,0:T(8,128)S(1)} %collective-permute-done.4.refs_4_), channel_id=1, source_target_pairs={{0,1},{1,0},{2,3},{3,2},{4,5},{5,4},{6,7},{7,6},{8,9},{9,8},{10,11... | collective-permute-start | bytes 393224 | tf_op jit(solution)/shard_map/ppermute | solution.py:242
  19.5 5.0 %collective-permute-start.13 = (f32[2,128,128]{2,1,0:T(8,128)S(1)}, f32[2,128,128]{2,1,0:T(8,128)S(1)}, u32[]{:S(2)}, u32[]{:S(2)}) collective-permute-start(f32[2,128,128]{2,1,0:T(8,128)S(1)} %collective-permute-done.refs_12_), channel_id=1, source_target_pairs={{0,2},{1,3},{2,0},{3,1},{4,6},{5,7},{6,4},{7,5},{8,10},{9,11},{10,... | collective-permute-start | bytes 393224 | tf_op jit(solution)/shard_map/ppermute | solution.py:242
  20.0 4.5 %collective-permute-start.12 = (f32[2,128,128]{2,1,0:T(8,128)S(1)}, f32[2,128,128]{2,1,0:T(8,128)S(1)}, u32[]{:S(2)}, u32[]{:S(2)}) collective-permute-start(f32[2,128,128]{2,1,0:T(8,128)S(1)} %collective-permute-done.refs_12_), channel_id=1, source_target_pairs={{0,1},{1,0},{2,3},{3,2},{4,5},{5,4},{6,7},{7,6},{8,9},{9,8},{10,11... | collective-permute-start | bytes 393224 | tf_op jit(solution)/shard_map/ppermute | solution.py:242
  21.8 2.7 %collective-permute-start.1 = (f32[2,128,128]{2,1,0:T(8,128)S(1)}, f32[2,128,128]{2,1,0:T(8,128)S(1)}, u32[]{:S(2)}, u32[]{:S(2)}) collective-permute-start(f32[2,128,128]{2,1,0:T(8,128)S(1)} %get-tuple-element.39.refs_0_.vector_ref), channel_id=1, source_target_pairs={{0,1},{1,0},{2,3},{3,2},{4,5},{5,4},{6,7},{7,6},{8,9},{9,8},{10,11... | collective-permute-start | bytes 393224 | tf_op jit(solution)/shard_map/ppermute | solution.py:242
  21.8 2.7 %collective-permute-start.7 = (f32[2,128,128]{2,1,0:T(8,128)S(1)}, f32[2,128,128]{2,1,0:T(8,128)S(1)}, u32[]{:S(2)}, u32[]{:S(2)}) collective-permute-start(f32[2,128,128]{2,1,0:T(8,128)S(1)} %collective-permute-done.6.refs_6_), channel_id=1, source_target_pairs={{0,1},{1,0},{2,3},{3,2},{4,5},{5,4},{6,7},{7,6},{8,9},{9,8},{10,11... | collective-permute-start | bytes 393224 | tf_op jit(solution)/shard_map/ppermute | solution.py:242
  22.3 2.2 %collective-permute-start.11 = (f32[2,128,128]{2,1,0:T(8,128)S(1)}, f32[2,128,128]{2,1,0:T(8,128)S(1)}, u32[]{:S(2)}, u32[]{:S(2)}) collective-permute-start(f32[2,128,128]{2,1,0:T(8,128)S(1)} %collective-permute-done.10.refs_10_), channel_id=1, source_target_pairs={{0,1},{1,0},{2,3},{3,2},{4,5},{5,4},{6,7},{7,6},{8,9},{9,8},{10,11... | collective-permute-start | bytes 393224 | tf_op jit(solution)/shard_map/ppermute | solution.py:242
  24.5 1.3 %collective-permute-start.14 = (f32[2,128,128]{2,1,0:T(8,128)S(1)}, f32[2,128,128]{2,1,0:T(8,128)S(1)}, u32[]{:S(2)}, u32[]{:S(2)}) collective-permute-start(f32[2,128,128]{2,1,0:T(8,128)S(1)} %collective-permute-done.13.refs_14_), channel_id=1, source_target_pairs={{0,1},{1,0},{2,3},{3,2},{4,5},{5,4},{6,7},{7,6},{8,9},{9,8},{10,11... | collective-permute-start | bytes 393224 | tf_op jit(solution)/shard_map/ppermute | solution.py:242
  31.8 8.3 %collective-permute-start.15 = (f32[648,128]{1,0:T(8,128)S(1)}, f32[648,128]{1,0:T(8,128)S(1)}, u32[]{:S(2)}, u32[]{:S(2)}) collective-permute-start(f32[648,128]{1,0:T(8,128)S(1)} %get-tuple-element.42.far_in), channel_id=1, source_target_pairs={{0,1},{1,0},{2,3},{3,2},{4,5},{5,4},{6,7},{7,6},{8,9},{9,8},{10,11... | collective-permute-start | bytes 995336 | tf_op jit(solution)/shard_map/ppermute | solution.py:242
  32.1 7.2 %collective-permute-start.16 = (f32[264,128]{1,0:T(8,128)S(1)}, f32[264,128]{1,0:T(8,128)S(1)}, u32[]{:S(2)}, u32[]{:S(2)}) collective-permute-start(f32[264,128]{1,0:T(8,128)S(1)} %get-tuple-element.43), channel_id=1, source_target_pairs={{0,2},{1,3},{2,0},{3,1},{4,6},{5,7},{6,4},{7,5},{8,10},{9,11},{10,... | collective-permute-start | bytes 405512 | tf_op jit(solution)/shard_map/ppermute | solution.py:242
  32.5 7.5 %collective-permute-start.17 = (f32[264,128]{1,0:T(8,128)S(1)}, f32[264,128]{1,0:T(8,128)S(1)}, u32[]{:S(2)}, u32[]{:S(2)}) collective-permute-start(f32[264,128]{1,0:T(8,128)S(1)} %get-tuple-element.44), channel_id=1, source_target_pairs={{0,3},{1,2},{2,1},{3,0},{4,7},{5,6},{6,5},{7,4},{8,11},{9,10},{10,... | collective-permute-start | bytes 405512 | tf_op jit(solution)/shard_map/ppermute | solution.py:242
  33.7 4.9 %collective-permute-start.18 = (f32[128,128]{1,0:T(8,128)S(1)}, f32[128,128]{1,0:T(8,128)S(1)}, u32[]{:S(2)}, u32[]{:S(2)}) collective-permute-start(f32[128,128]{1,0:T(8,128)S(1)} %get-tuple-element.45), channel_id=1, source_target_pairs={{0,4},{1,5},{2,6},{3,7},{4,0},{5,1},{6,2},{7,3},{8,12},{9,13},{10,... | collective-permute-start | bytes 196616 | tf_op jit(solution)/shard_map/ppermute | solution.py:242
  34.2 5.1 %collective-permute-start.19 = (f32[128,128]{1,0:T(8,128)S(1)}, f32[128,128]{1,0:T(8,128)S(1)}, u32[]{:S(2)}, u32[]{:S(2)}) collective-permute-start(f32[128,128]{1,0:T(8,128)S(1)} %get-tuple-element.46), channel_id=1, source_target_pairs={{0,5},{1,4},{2,7},{3,6},{4,1},{5,0},{6,3},{7,2},{8,13},{9,12},{10,... | collective-permute-start | bytes 196616 | tf_op jit(solution)/shard_map/ppermute | solution.py:242
  40.1 16.2 %copy-start = (f32[2,128,128]{2,1,0:T(8,128)S(1)}, f32[2,128,128]{2,1,0:T(8,128)}, u32[]{:S(2)}) copy-start(f32[2,128,128]{2,1,0:T(8,128)} %precond_ref.3) | copy-start | bytes 393220
  40.8 9.7 %collective-permute-start.21 = (f32[264,128]{1,0:T(8,128)S(1)}, f32[264,128]{1,0:T(8,128)S(1)}, u32[]{:S(2)}, u32[]{:S(2)}) collective-permute-start(f32[264,128]{1,0:T(8,128)S(1)} %get-tuple-element.51), channel_id=1, source_target_pairs={{0,12},{1,13},{2,14},{3,15},{4,8},{5,9},{6,10},{7,11},{8,4},{9,5},... | collective-permute-start | bytes 405512 | tf_op jit(solution)/shard_map/ppermute | solution.py:242
  44.8 11.5 %collective-permute-start.22 = (f32[264,128]{1,0:T(8,128)S(1)}, f32[264,128]{1,0:T(8,128)S(1)}, u32[]{:S(2)}, u32[]{:S(2)}) collective-permute-start(f32[264,128]{1,0:T(8,128)S(1)} %get-tuple-element.52), channel_id=1, source_target_pairs={{0,8},{1,9},{2,10},{3,11},{4,12},{5,13},{6,14},{7,15},{8,0},{9,1},... | collective-permute-start | bytes 405512 | tf_op jit(solution)/shard_map/ppermute | solution.py:242
  44.8 11.5 %collective-permute-start.23 = (f32[264,128]{1,0:T(8,128)S(1)}, f32[264,128]{1,0:T(8,128)S(1)}, u32[]{:S(2)}, u32[]{:S(2)}) collective-permute-start(f32[264,128]{1,0:T(8,128)S(1)} %get-tuple-element.50.refs_0_), channel_id=1, source_target_pairs={{0,4},{1,5},{2,6},{3,7},{4,0},{5,1},{6,2},{7,3},{8,12},{9,13},{10,... | collective-permute-start | bytes 405512 | tf_op jit(solution)/shard_map/ppermute | solution.py:242
  45.4 5.1 %collective-permute-start.20 = (f32[2,128,128]{2,1,0:T(8,128)S(1)}, f32[2,128,128]{2,1,0:T(8,128)S(1)}, u32[]{:S(2)}, u32[]{:S(2)}) collective-permute-start(f32[2,128,128]{2,1,0:T(8,128)S(1)} %get-tuple-element.48), channel_id=1, source_target_pairs={{0,2},{1,3},{2,0},{3,1},{4,6},{5,7},{6,4},{7,5},{8,10},{9,11},{10,... | collective-permute-start | bytes 393224 | tf_op jit(solution)/shard_map/ppermute | solution.py:242
  56.4 8.3 %collective-permute-start.35 = (f32[2,128,128]{2,1,0:T(8,128)S(1)}, f32[2,128,128]{2,1,0:T(8,128)S(1)}, u32[]{:S(2)}, u32[]{:S(2)}) collective-permute-start(f32[2,128,128]{2,1,0:T(8,128)S(1)} %step.1.refs_0_.vector_ref), channel_id=1, source_target_pairs={{0,12},{1,13},{2,14},{3,15},{4,8},{5,9},{6,10},{7,11},{8,4},{9,5},... | collective-permute-start | bytes 393224 | tf_op jit(solution)/shard_map/ppermute | solution.py:242
  59.2 10.3 %collective-permute-start.31 = (f32[2,128,128]{2,1,0:T(8,128)S(1)}, f32[2,128,128]{2,1,0:T(8,128)S(1)}, u32[]{:S(2)}, u32[]{:S(2)}) collective-permute-start(f32[2,128,128]{2,1,0:T(8,128)S(1)} %step.1.refs_0_.vector_ref), channel_id=1, source_target_pairs={{0,8},{1,9},{2,10},{3,11},{4,12},{5,13},{6,14},{7,15},{8,0},{9,1},... | collective-permute-start | bytes 393224 | tf_op jit(solution)/shard_map/ppermute | solution.py:242
  59.2 10.3 %collective-permute-start.27 = (f32[2,128,128]{2,1,0:T(8,128)S(1)}, f32[2,128,128]{2,1,0:T(8,128)S(1)}, u32[]{:S(2)}, u32[]{:S(2)}) collective-permute-start(f32[2,128,128]{2,1,0:T(8,128)S(1)} %step.1.refs_0_.vector_ref), channel_id=1, source_target_pairs={{0,4},{1,5},{2,6},{3,7},{4,0},{5,1},{6,2},{7,3},{8,12},{9,13},{10,... | collective-permute-start | bytes 393224 | tf_op jit(solution)/shard_map/ppermute | solution.py:242
  60.9 9.0 %collective-permute-start.25 = (f32[2,128,128]{2,1,0:T(8,128)S(1)}, f32[2,128,128]{2,1,0:T(8,128)S(1)}, u32[]{:S(2)}, u32[]{:S(2)}) collective-permute-start(f32[2,128,128]{2,1,0:T(8,128)S(1)} %step.1.refs_0_.vector_ref), channel_id=1, source_target_pairs={{0,2},{1,3},{2,0},{3,1},{4,6},{5,7},{6,4},{7,5},{8,10},{9,11},{10,... | collective-permute-start | bytes 393224 | tf_op jit(solution)/shard_map/ppermute | solution.py:242
  61.3 8.8 %collective-permute-start.24 = (f32[2,128,128]{2,1,0:T(8,128)S(1)}, f32[2,128,128]{2,1,0:T(8,128)S(1)}, u32[]{:S(2)}, u32[]{:S(2)}) collective-permute-start(f32[2,128,128]{2,1,0:T(8,128)S(1)} %step.1.refs_0_.vector_ref), channel_id=1, source_target_pairs={{0,1},{1,0},{2,3},{3,2},{4,5},{5,4},{6,7},{7,6},{8,9},{9,8},{10,11... | collective-permute-start | bytes 393224 | tf_op jit(solution)/shard_map/ppermute | solution.py:242
  64.8 5.4 %collective-permute-start.37 = (f32[2,128,128]{2,1,0:T(8,128)S(1)}, f32[2,128,128]{2,1,0:T(8,128)S(1)}, u32[]{:S(2)}, u32[]{:S(2)}) collective-permute-start(f32[2,128,128]{2,1,0:T(8,128)S(1)} %collective-permute-done.35.refs_12_), channel_id=1, source_target_pairs={{0,2},{1,3},{2,0},{3,1},{4,6},{5,7},{6,4},{7,5},{8,10},{9,11},{10,... | collective-permute-start | bytes 393224 | tf_op jit(solution)/shard_map/ppermute | solution.py:242
  69.5 1.3 %collective-permute-start.36 = (f32[2,128,128]{2,1,0:T(8,128)S(1)}, f32[2,128,128]{2,1,0:T(8,128)S(1)}, u32[]{:S(2)}, u32[]{:S(2)}) collective-permute-start(f32[2,128,128]{2,1,0:T(8,128)S(1)} %collective-permute-done.35.refs_12_), channel_id=1, source_target_pairs={{0,1},{1,0},{2,3},{3,2},{4,5},{5,4},{6,7},{7,6},{8,9},{9,8},{10,11... | collective-permute-start | bytes 393224 | tf_op jit(solution)/shard_map/ppermute | solution.py:242
  69.5 5.9 %collective-permute-start.33 = (f32[2,128,128]{2,1,0:T(8,128)S(1)}, f32[2,128,128]{2,1,0:T(8,128)S(1)}, u32[]{:S(2)}, u32[]{:S(2)}) collective-permute-start(f32[2,128,128]{2,1,0:T(8,128)S(1)} %collective-permute-done.31.refs_8_), channel_id=1, source_target_pairs={{0,2},{1,3},{2,0},{3,1},{4,6},{5,7},{6,4},{7,5},{8,10},{9,11},{10,... | collective-permute-start | bytes 393224 | tf_op jit(solution)/shard_map/ppermute | solution.py:242
  69.9 5.6 %collective-permute-start.32 = (f32[2,128,128]{2,1,0:T(8,128)S(1)}, f32[2,128,128]{2,1,0:T(8,128)S(1)}, u32[]{:S(2)}, u32[]{:S(2)}) collective-permute-start(f32[2,128,128]{2,1,0:T(8,128)S(1)} %collective-permute-done.31.refs_8_), channel_id=1, source_target_pairs={{0,1},{1,0},{2,3},{3,2},{4,5},{5,4},{6,7},{7,6},{8,9},{9,8},{10,11... | collective-permute-start | bytes 393224 | tf_op jit(solution)/shard_map/ppermute | solution.py:242
  70.1 5.8 %collective-permute-start.29 = (f32[2,128,128]{2,1,0:T(8,128)S(1)}, f32[2,128,128]{2,1,0:T(8,128)S(1)}, u32[]{:S(2)}, u32[]{:S(2)}) collective-permute-start(f32[2,128,128]{2,1,0:T(8,128)S(1)} %collective-permute-done.25.refs_2_), channel_id=1, source_target_pairs={{0,4},{1,5},{2,6},{3,7},{4,0},{5,1},{6,2},{7,3},{8,12},{9,13},{10,... | collective-permute-start | bytes 393224 | tf_op jit(solution)/shard_map/ppermute | solution.py:242
  70.2 5.9 %collective-permute-start.26 = (f32[2,128,128]{2,1,0:T(8,128)S(1)}, f32[2,128,128]{2,1,0:T(8,128)S(1)}, u32[]{:S(2)}, u32[]{:S(2)}) collective-permute-start(f32[2,128,128]{2,1,0:T(8,128)S(1)} %collective-permute-done.25.refs_2_), channel_id=1, source_target_pairs={{0,1},{1,0},{2,3},{3,2},{4,5},{5,4},{6,7},{7,6},{8,9},{9,8},{10,11... | collective-permute-start | bytes 393224 | tf_op jit(solution)/shard_map/ppermute | solution.py:242
  70.9 5.2 %collective-permute-start.28 = (f32[2,128,128]{2,1,0:T(8,128)S(1)}, f32[2,128,128]{2,1,0:T(8,128)S(1)}, u32[]{:S(2)}, u32[]{:S(2)}) collective-permute-start(f32[2,128,128]{2,1,0:T(8,128)S(1)} %collective-permute-done.27.refs_4_), channel_id=1, source_target_pairs={{0,1},{1,0},{2,3},{3,2},{4,5},{5,4},{6,7},{7,6},{8,9},{9,8},{10,11... | collective-permute-start | bytes 393224 | tf_op jit(solution)/shard_map/ppermute | solution.py:242
  75.4 1.3 %collective-permute-start.38 = (f32[2,128,128]{2,1,0:T(8,128)S(1)}, f32[2,128,128]{2,1,0:T(8,128)S(1)}, u32[]{:S(2)}, u32[]{:S(2)}) collective-permute-start(f32[2,128,128]{2,1,0:T(8,128)S(1)} %collective-permute-done.37.refs_14_), channel_id=1, source_target_pairs={{0,1},{1,0},{2,3},{3,2},{4,5},{5,4},{6,7},{7,6},{8,9},{9,8},{10,11... | collective-permute-start | bytes 393224 | tf_op jit(solution)/shard_map/ppermute | solution.py:242
  75.4 1.5 %collective-permute-start.34 = (f32[2,128,128]{2,1,0:T(8,128)S(1)}, f32[2,128,128]{2,1,0:T(8,128)S(1)}, u32[]{:S(2)}, u32[]{:S(2)}) collective-permute-start(f32[2,128,128]{2,1,0:T(8,128)S(1)} %collective-permute-done.33.refs_10_), channel_id=1, source_target_pairs={{0,1},{1,0},{2,3},{3,2},{4,5},{5,4},{6,7},{7,6},{8,9},{9,8},{10,11... | collective-permute-start | bytes 393224 | tf_op jit(solution)/shard_map/ppermute | solution.py:242
  76.0 1.3 %collective-permute-start.30 = (f32[2,128,128]{2,1,0:T(8,128)S(1)}, f32[2,128,128]{2,1,0:T(8,128)S(1)}, u32[]{:S(2)}, u32[]{:S(2)}) collective-permute-start(f32[2,128,128]{2,1,0:T(8,128)S(1)} %collective-permute-done.29.refs_6_), channel_id=1, source_target_pairs={{0,1},{1,0},{2,3},{3,2},{4,5},{5,4},{6,7},{7,6},{8,9},{9,8},{10,11... | collective-permute-start | bytes 393224 | tf_op jit(solution)/shard_map/ppermute | solution.py:242
  83.4 8.2 %collective-permute-start.39 = (f32[648,128]{1,0:T(8,128)S(1)}, f32[648,128]{1,0:T(8,128)S(1)}, u32[]{:S(2)}, u32[]{:S(2)}) collective-permute-start(f32[648,128]{1,0:T(8,128)S(1)} %get-tuple-element.54.far_in), channel_id=1, source_target_pairs={{0,1},{1,0},{2,3},{3,2},{4,5},{5,4},{6,7},{7,6},{8,9},{9,8},{10,11... | collective-permute-start | bytes 995336 | tf_op jit(solution)/shard_map/ppermute | solution.py:242
  83.8 7.2 %collective-permute-start.40 = (f32[264,128]{1,0:T(8,128)S(1)}, f32[264,128]{1,0:T(8,128)S(1)}, u32[]{:S(2)}, u32[]{:S(2)}) collective-permute-start(f32[264,128]{1,0:T(8,128)S(1)} %get-tuple-element.55), channel_id=1, source_target_pairs={{0,2},{1,3},{2,0},{3,1},{4,6},{5,7},{6,4},{7,5},{8,10},{9,11},{10,... | collective-permute-start | bytes 405512 | tf_op jit(solution)/shard_map/ppermute | solution.py:242
  85.2 6.4 %collective-permute-start.41 = (f32[264,128]{1,0:T(8,128)S(1)}, f32[264,128]{1,0:T(8,128)S(1)}, u32[]{:S(2)}, u32[]{:S(2)}) collective-permute-start(f32[264,128]{1,0:T(8,128)S(1)} %get-tuple-element.56), channel_id=1, source_target_pairs={{0,3},{1,2},{2,1},{3,0},{4,7},{5,6},{6,5},{7,4},{8,11},{9,10},{10,... | collective-permute-start | bytes 405512 | tf_op jit(solution)/shard_map/ppermute | solution.py:242
  85.3 4.9 %collective-permute-start.42 = (f32[128,128]{1,0:T(8,128)S(1)}, f32[128,128]{1,0:T(8,128)S(1)}, u32[]{:S(2)}, u32[]{:S(2)}) collective-permute-start(f32[128,128]{1,0:T(8,128)S(1)} %get-tuple-element.57), channel_id=1, source_target_pairs={{0,4},{1,5},{2,6},{3,7},{4,0},{5,1},{6,2},{7,3},{8,12},{9,13},{10,... | collective-permute-start | bytes 196616 | tf_op jit(solution)/shard_map/ppermute | solution.py:242
  85.6 5.4 %collective-permute-start.43 = (f32[128,128]{1,0:T(8,128)S(1)}, f32[128,128]{1,0:T(8,128)S(1)}, u32[]{:S(2)}, u32[]{:S(2)}) collective-permute-start(f32[128,128]{1,0:T(8,128)S(1)} %get-tuple-element.58), channel_id=1, source_target_pairs={{0,5},{1,4},{2,7},{3,6},{4,1},{5,0},{6,3},{7,2},{8,13},{9,12},{10,... | collective-permute-start | bytes 196616 | tf_op jit(solution)/shard_map/ppermute | solution.py:242
  92.4 12.6 %collective-permute-start.45 = (f32[264,128]{1,0:T(8,128)S(1)}, f32[264,128]{1,0:T(8,128)S(1)}, u32[]{:S(2)}, u32[]{:S(2)}) collective-permute-start(f32[264,128]{1,0:T(8,128)S(1)} %get-tuple-element.63), channel_id=1, source_target_pairs={{0,8},{1,9},{2,10},{3,11},{4,12},{5,13},{6,14},{7,15},{8,0},{9,1},... | collective-permute-start | bytes 405512 | tf_op jit(solution)/shard_map/ppermute | solution.py:242
  93.5 11.4 %collective-permute-start.46 = (f32[264,128]{1,0:T(8,128)S(1)}, f32[264,128]{1,0:T(8,128)S(1)}, u32[]{:S(2)}, u32[]{:S(2)}) collective-permute-start(f32[264,128]{1,0:T(8,128)S(1)} %get-tuple-element.64), channel_id=1, source_target_pairs={{0,12},{1,13},{2,14},{3,15},{4,8},{5,9},{6,10},{7,11},{8,4},{9,5},... | collective-permute-start | bytes 405512 | tf_op jit(solution)/shard_map/ppermute | solution.py:242
  95.2 11.1 %collective-permute-start.47 = (f32[264,128]{1,0:T(8,128)S(1)}, f32[264,128]{1,0:T(8,128)S(1)}, u32[]{:S(2)}, u32[]{:S(2)}) collective-permute-start(f32[264,128]{1,0:T(8,128)S(1)} %get-tuple-element.62.refs_0_), channel_id=1, source_target_pairs={{0,4},{1,5},{2,6},{3,7},{4,0},{5,1},{6,2},{7,3},{8,12},{9,13},{10,... | collective-permute-start | bytes 405512 | tf_op jit(solution)/shard_map/ppermute | solution.py:242
  95.9 5.1 %collective-permute-start.44 = (f32[2,128,128]{2,1,0:T(8,128)S(1)}, f32[2,128,128]{2,1,0:T(8,128)S(1)}, u32[]{:S(2)}, u32[]{:S(2)}) collective-permute-start(f32[2,128,128]{2,1,0:T(8,128)S(1)} %get-tuple-element.60), channel_id=1, source_target_pairs={{0,2},{1,3},{2,0},{3,1},{4,6},{5,7},{6,4},{7,5},{8,10},{9,11},{10,... | collective-permute-start | bytes 393224 | tf_op jit(solution)/shard_map/ppermute | solution.py:242

commit v16 on v10

--- a/solution.py
+++ b/solution.py
@@ -358,9 +358,11 @@
         pieces[k + ROW] = swapped(pieces[k], ROW)
     pieces[COLUMN + ROW] = swapped(pieces[ROW], COLUMN)
     if held is not None:
-        pieces[n - 4 + ROW], pieces[0] = lax.optimization_barrier((pieces[n - 4 + ROW], held))
+        pieces[n - 4], held = lax.optimization_barrier((pieces[n - 4], held))
     for k in range(0, n, 2):
         pieces[k + CORE] = swapped(pieces[k], CORE)
+    if held is not None:
+        pieces[0] = held
     return [pieces[k] for k in range(n)]
 
 

time: 123 us -> 121 us (0.984)
  starting transfers between devices: 48.2 us -> 35.2 us
  waiting for transfers between devices: 44.1 us -> 52.5 us
  Pallas kernels: 18.2 us -> 19.9 us
    ppermute x48, starting transfers between devices: 48.2 us -> 35.2 us  [swapped(): return lax.ppermute(x, 'term', [(i, i ^ k) for i in range(n)])]
    ppermute x48, waiting for transfers between devices: 44.1 us -> 52.5 us  [swapped(): return lax.ppermute(x, 'term', [(i, i ^ k) for i in range(n)])]
    pallas_call x1, Pallas kernels: 2.76 us -> 4.11 us  [prep(): pl.pallas_call(functools.partial(prep_kernel, n, terms * n + 1), out_shap...]
  transfers between devices with their start and end apart: 48 -> 48, of which waited for: 19 -> 24; matrix products, arithmetic and copies ran while one was open for 0% -> 0% of each run, Pallas kernels for 2% -> 3%
where the time goes in v16:
time: 121 us; the launch traced here: 120 us
  waiting for transfers between devices  52.5 us (43%)
  starting transfers between devices  35.2 us (29%)
  Pallas kernels  19.9 us (16%)
  blocking collectives  10.8 us (9%)
  between operations  1.42 us (1%)
    ppermute x48, waiting for transfers between devices, swapped(): return lax.ppermute(x, 'term', [(i, i ^ k) for i in range(n)])  52.5 us
    ppermute x48, starting transfers between devices, swapped(): return lax.ppermute(x, 'term', [(i, i ^ k) for i in range(n)])  35.2 us
    pallas_call x2, Pallas kernels, apply(): pl.pallas_call(functools.partial(apply_kernel, n, npairs, over_rows, rows...  12.4 us
    all_to_all x1, blocking collectives, shards(): lax.all_to_all(jnp.broadcast_to(partial[None], (n, 8, width)), 'term', sp...  10.8 us
    pallas_call x1, Pallas kernels, prep(): pl.pallas_call(functools.partial(prep_kernel, n, terms * n + 1), out_shap...  4.11 us
    pallas_call x5, Pallas kernels, local(): pl.pallas_call(kernel, out_shape=out_shape, in_specs=[SMEM] * len(scalars...  3.42 us
  transfers between devices with their start and end apart: 48, of which 24 were waited for; matrix products, arithmetic and copies ran while one was open for 0% of the time, Pallas kernels for 3%

profile of v16, /device:TPU:0, one launch (start us, length us, event | category | flops | bytes accessed | tf_op | source)
XLA Modules:
  0.0 120.5 jit_solution(3065651618315938918)
XLA Ops:
  0.6 3.0 %collective-permute-start.2 = (f32[2,128,128]{2,1,0:T(8,128)}, f32[2,128,128]{2,1,0:T(8,128)S(1)}, u32[]{:S(2)}, u32[]{:S(2)}) collective-permute-start(f32[2,128,128]{2,1,0:T(8,128)} %vector_in.1), channel_id=1, source_target_pairs={{0,2},{1,3},{2,0},{3,1},{4,6},{5,7},{6,4},{7,5},{8,10},{9,11},{10,... | collective-permute-start | bytes 393224 | tf_op jit(solution)/shard_map/ppermute | solution.py:242
  3.7 3.6 %collective-permute-start = (f32[2,128,128]{2,1,0:T(8,128)}, f32[2,128,128]{2,1,0:T(8,128)S(1)}, u32[]{:S(2)}, u32[]{:S(2)}) collective-permute-start(f32[2,128,128]{2,1,0:T(8,128)} %vector_in.1), channel_id=1, source_target_pairs={{0,12},{1,13},{2,14},{3,15},{4,8},{5,9},{6,10},{7,11},{8,4},{9,5},... | collective-permute-start | bytes 393224 | tf_op jit(solution)/shard_map/ppermute | solution.py:242
  7.3 0.8 collective-permute-start.4
  8.1 1.2 %collective-permute-start.6 = (f32[2,128,128]{2,1,0:T(8,128)S(1)}, f32[2,128,128]{2,1,0:T(8,128)S(1)}, u32[]{:S(2)}, u32[]{:S(2)}) collective-permute-start(f32[2,128,128]{2,1,0:T(8,128)S(1)} %collective-permute-done.2.refs_2_), channel_id=1, source_target_pairs={{0,4},{1,5},{2,6},{3,7},{4,0},{5,1},{6,2},{7,3},{8,12},{9,13},{10,... | collective-permute-start | bytes 393224 | tf_op jit(solution)/shard_map/ppermute | solution.py:242
  9.3 2.8 %collective-permute-done.refs_12_ = f32[2,128,128]{2,1,0:T(8,128)S(1)} collective-permute-done((f32[2,128,128]{2,1,0:T(8,128)}, f32[2,128,128]{2,1,0:T(8,128)S(1)}, u32[]{:S(2)}, u32[]{:S(2)}) %collective-permute-start) | collective-permute-done | bytes 131104 | tf_op jit(solution)/shard_map/ppermute | solution.py:242
  12.1 0.4 collective-permute-start.13
  12.5 6.9 %collective-permute-done.8.refs_8_ = f32[2,128,128]{2,1,0:T(8,128)S(1)} collective-permute-done((f32[2,128,128]{2,1,0:T(8,128)}, f32[2,128,128]{2,1,0:T(8,128)S(1)}, u32[]{:S(2)}, u32[]{:S(2)}) %collective-permute-start.8) | collective-permute-done | bytes 131104 | tf_op jit(solution)/shard_map/ppermute | solution.py:242
  19.3 0.5 collective-permute-start.10
  20.5 0.6 copy.12
  21.1 4.1 %prep.1 = (bf16[8,128,512]{2,1,0:T(8,128)(2,1)S(1)}, bf16[2048,256]{1,0:T(8,128)(2,1)S(1)}, s32[721]{0:T(1024)S(1)}, f32[2,128,128]{2,1,0:T(8,128)S(1)}) custom-call(s32[1]{0:T(128)} %bitcast.me_ref, s32[16,16]{1,0:T(8,128)} %fetch_in.1, s32[16,16]{1,0:T(8,128)} %store_in.1, s32[384]{0:T(512)} %bitcast.8, s32[1]{0:T(128)S(6)} %copy.13.live_in, ...), custom_call_target="tpu_custom_call" | custom-call | tf_op jit(solution)/shard_map/prep/pallas_call | solution.py:132
  25.3 0.5 collective-permute-start.5
  25.9 0.4 collective-permute-start.14
  26.4 0.4 collective-permute-done.5.refs_5_
  26.8 0.3 collective-permute-done.7.refs_7_
  27.2 0.2 collective-permute-done.14.refs_15_
  27.4 0.3 collective-permute-done.11.refs_11_
  27.7 6.1 %apply.2 = (f32[640,128]{1,0:T(8,128)S(1)}, f32[648,128]{1,0:T(8,128)S(1)}, f32[264,128]{1,0:T(8,128)S(1)}, f32[264,128]{1,0:T(8,128)S(1)}, f32[128,128]{1,0:T(8...) custom-call(s32[721]{0:T(1024)S(1)} %get-tuple-element.35.table_ref, ...), custom_call_target="tpu_custom_call" | custom-call | tf_op jit(solution)/shard_map/apply/pallas_call | solution.py:216
  33.8 0.1 collective-permute-start.15
  34.0 0.6 collective-permute-start.16
  34.5 1.2 %collective-permute-start.17 = (f32[264,128]{1,0:T(8,128)S(1)}, f32[264,128]{1,0:T(8,128)S(1)}, u32[]{:S(2)}, u32[]{:S(2)}) collective-permute-start(f32[264,128]{1,0:T(8,128)S(1)} %get-tuple-element.44), channel_id=1, source_target_pairs={{0,3},{1,2},{2,1},{3,0},{4,7},{5,6},{6,5},{7,4},{8,11},{9,10},{10,... | collective-permute-start | bytes 405512 | tf_op jit(solution)/shard_map/ppermute | solution.py:242
  35.8 1.7 %collective-permute-start.19 = (f32[128,128]{1,0:T(8,128)S(1)}, f32[128,128]{1,0:T(8,128)S(1)}, u32[]{:S(2)}, u32[]{:S(2)}) collective-permute-start(f32[128,128]{1,0:T(8,128)S(1)} %get-tuple-element.46), channel_id=1, source_target_pairs={{0,5},{1,4},{2,7},{3,6},{4,1},{5,0},{6,3},{7,2},{8,13},{9,12},{10,... | collective-permute-start | bytes 196616 | tf_op jit(solution)/shard_map/ppermute | solution.py:242
  37.4 3.2 %collective-permute-done.18.column_ref = f32[128,128]{1,0:T(8,128)S(1)} collective-permute-done((f32[128,128]{1,0:T(8,128)S(1)}, f32[128,128]{1,0:T(8,128)S(1)}, u32[]{:S(2)}, u32[]{:S(2)}) %collective-permute-start.18) | collective-permute-done | bytes 65568 | tf_op jit(solution)/shard_map/ppermute | solution.py:242
  40.7 0.2 collective-permute-done.19.column_far_ref
  40.9 1.4 %collective-permute-done.17.row_far_ref = f32[264,128]{1,0:T(8,128)S(1)} collective-permute-done((f32[264,128]{1,0:T(8,128)S(1)}, f32[264,128]{1,0:T(8,128)S(1)}, u32[]{:S(2)}, u32[]{:S(2)}) %collective-permute-start.17) | collective-permute-done | bytes 135200 | tf_op jit(solution)/shard_map/ppermute | solution.py:242
  42.3 0.7 fold.2
  43.1 2.0 %collective-permute-start.21 = (f32[264,128]{1,0:T(8,128)S(1)}, f32[264,128]{1,0:T(8,128)S(1)}, u32[]{:S(2)}, u32[]{:S(2)}) collective-permute-start(f32[264,128]{1,0:T(8,128)S(1)} %get-tuple-element.51), channel_id=1, source_target_pairs={{0,12},{1,13},{2,14},{3,15},{4,8},{5,9},{6,10},{7,11},{8,4},{9,5},... | collective-permute-start | bytes 405512 | tf_op jit(solution)/shard_map/ppermute | solution.py:242
  45.1 2.4 %collective-permute-start.23 = (f32[264,128]{1,0:T(8,128)S(1)}, f32[264,128]{1,0:T(8,128)S(1)}, u32[]{:S(2)}, u32[]{:S(2)}) collective-permute-start(f32[264,128]{1,0:T(8,128)S(1)} %get-tuple-element.50.refs_0_), channel_id=1, source_target_pairs={{0,4},{1,5},{2,6},{3,7},{4,0},{5,1},{6,2},{7,3},{8,12},{9,13},{10,... | collective-permute-start | bytes 405512 | tf_op jit(solution)/shard_map/ppermute | solution.py:242
  47.5 5.0 %collective-permute-done.20.step_ref = f32[2,128,128]{2,1,0:T(8,128)S(1)} collective-permute-done((f32[2,128,128]{2,1,0:T(8,128)S(1)}, f32[2,128,128]{2,1,0:T(8,128)S(1)}, u32[]{:S(2)}, u32[]{:S(2)}) %collective-permute-start.20) | collective-permute-done | bytes 131104 | tf_op jit(solution)/shard_map/ppermute | solution.py:242
  52.5 4.2 %collective-permute-done.22.refs_2_ = f32[264,128]{1,0:T(8,128)S(1)} collective-permute-done((f32[264,128]{1,0:T(8,128)S(1)}, f32[264,128]{1,0:T(8,128)S(1)}, u32[]{:S(2)}, u32[]{:S(2)}) %collective-permute-start.22) | collective-permute-done | bytes 135200 | tf_op jit(solution)/shard_map/ppermute | solution.py:242
  56.7 0.2 step.1.refs_0_.vector_ref
  56.9 2.4 %collective-permute-start.35 = (f32[2,128,128]{2,1,0:T(8,128)S(1)}, f32[2,128,128]{2,1,0:T(8,128)S(1)}, u32[]{:S(2)}, u32[]{:S(2)}) collective-permute-start(f32[2,128,128]{2,1,0:T(8,128)S(1)} %step.1.refs_0_.vector_ref), channel_id=1, source_target_pairs={{0,12},{1,13},{2,14},{3,15},{4,8},{5,9},{6,10},{7,11},{8,4},{9,5},... | collective-permute-start | bytes 393224 | tf_op jit(solution)/shard_map/ppermute | solution.py:242
  59.4 2.0 %collective-permute-start.27 = (f32[2,128,128]{2,1,0:T(8,128)S(1)}, f32[2,128,128]{2,1,0:T(8,128)S(1)}, u32[]{:S(2)}, u32[]{:S(2)}) collective-permute-start(f32[2,128,128]{2,1,0:T(8,128)S(1)} %step.1.refs_0_.vector_ref), channel_id=1, source_target_pairs={{0,4},{1,5},{2,6},{3,7},{4,0},{5,1},{6,2},{7,3},{8,12},{9,13},{10,... | collective-permute-start | bytes 393224 | tf_op jit(solution)/shard_map/ppermute | solution.py:242
  61.4 0.9 collective-permute-start.25
  62.2 3.0 %collective-permute-done.35.refs_12_ = f32[2,128,128]{2,1,0:T(8,128)S(1)} collective-permute-done((f32[2,128,128]{2,1,0:T(8,128)S(1)}, f32[2,128,128]{2,1,0:T(8,128)S(1)}, u32[]{:S(2)}, u32[]{:S(2)}) %collective-permute-start.35) | collective-permute-done | bytes 131104 | tf_op jit(solution)/shard_map/ppermute | solution.py:242
  65.3 0.8 collective-permute-start.37
  66.1 4.4 %collective-permute-done.31.refs_8_ = f32[2,128,128]{2,1,0:T(8,128)S(1)} collective-permute-done((f32[2,128,128]{2,1,0:T(8,128)S(1)}, f32[2,128,128]{2,1,0:T(8,128)S(1)}, u32[]{:S(2)}, u32[]{:S(2)}) %collective-permute-start.31) | collective-permute-done | bytes 131104 | tf_op jit(solution)/shard_map/ppermute | solution.py:242
  70.5 1.0 collective-permute-start.33
  71.6 0.2 collective-permute-start.32
  71.8 0.3 collective-permute-start.26
  72.2 0.2 collective-permute-start.28
  72.4 4.1 %collective-permute-done.33.refs_10_ = f32[2,128,128]{2,1,0:T(8,128)S(1)} collective-permute-done((f32[2,128,128]{2,1,0:T(8,128)S(1)}, f32[2,128,128]{2,1,0:T(8,128)S(1)}, u32[]{:S(2)}, u32[]{:S(2)}) %collective-permute-start.33) | collective-permute-done | bytes 131104 | tf_op jit(solution)/shard_map/ppermute | solution.py:242
  76.5 0.5 collective-permute-start.34
  77.0 0.5 collective-permute-done.29.refs_6_
  77.5 0.3 collective-permute-done.38.refs_15_
  77.8 0.2 collective-permute-done.34.refs_11_
  78.0 0.9 collective-permute-done.30.refs_7_
  78.8 6.3 %apply.3 = (f32[640,128]{1,0:T(8,128)S(1)}, f32[648,128]{1,0:T(8,128)S(1)}, f32[264,128]{1,0:T(8,128)S(1)}, f32[264,128]{1,0:T(8,128)S(1)}, f32[128,128]{1,0:T(8...) custom-call(s32[721]{0:T(1024)S(1)} %get-tuple-element.35.table_ref, ...), custom_call_target="tpu_custom_call" | custom-call | tf_op jit(solution)/shard_map/apply/pallas_call | solution.py:216
  85.2 0.9 collective-permute-start.40
  86.2 0.9 collective-permute-start.41
  87.1 0.2 collective-permute-start.42
  87.3 1.5 %collective-permute-start.43 = (f32[128,128]{1,0:T(8,128)S(1)}, f32[128,128]{1,0:T(8,128)S(1)}, u32[]{:S(2)}, u32[]{:S(2)}) collective-permute-start(f32[128,128]{1,0:T(8,128)S(1)} %get-tuple-element.58), channel_id=1, source_target_pairs={{0,5},{1,4},{2,7},{3,6},{4,1},{5,0},{6,3},{7,2},{8,13},{9,12},{10,... | collective-permute-start | bytes 196616 | tf_op jit(solution)/shard_map/ppermute | solution.py:242
  88.8 3.2 %collective-permute-done.42.column_ref = f32[128,128]{1,0:T(8,128)S(1)} collective-permute-done((f32[128,128]{1,0:T(8,128)S(1)}, f32[128,128]{1,0:T(8,128)S(1)}, u32[]{:S(2)}, u32[]{:S(2)}) %collective-permute-start.42) | collective-permute-done | bytes 65568 | tf_op jit(solution)/shard_map/ppermute | solution.py:242
  92.0 0.2 collective-permute-done.43.column_far_ref
  92.2 1.4 %collective-permute-done.41.row_far_ref = f32[264,128]{1,0:T(8,128)S(1)} collective-permute-done((f32[264,128]{1,0:T(8,128)S(1)}, f32[264,128]{1,0:T(8,128)S(1)}, u32[]{:S(2)}, u32[]{:S(2)}) %collective-permute-start.41) | collective-permute-done | bytes 135200 | tf_op jit(solution)/shard_map/ppermute | solution.py:242
  93.6 0.7 fold.3
  94.5 2.5 %collective-permute-start.46 = (f32[264,128]{1,0:T(8,128)S(1)}, f32[264,128]{1,0:T(8,128)S(1)}, u32[]{:S(2)}, u32[]{:S(2)}) collective-permute-start(f32[264,128]{1,0:T(8,128)S(1)} %get-tuple-element.64), channel_id=1, source_target_pairs={{0,12},{1,13},{2,14},{3,15},{4,8},{5,9},{6,10},{7,11},{8,4},{9,5},... | collective-permute-start | bytes 405512 | tf_op jit(solution)/shard_map/ppermute | solution.py:242
  97.0 0.9 collective-permute-start.47
  97.9 0.7 collective-permute-start.44
  98.6 4.3 %collective-permute-done.44.step_ref = f32[2,128,128]{2,1,0:T(8,128)S(1)} collective-permute-done((f32[2,128,128]{2,1,0:T(8,128)S(1)}, f32[2,128,128]{2,1,0:T(8,128)S(1)}, u32[]{:S(2)}, u32[]{:S(2)}) %collective-permute-start.44) | collective-permute-done | bytes 131104 | tf_op jit(solution)/shard_map/ppermute | solution.py:242
  102.9 3.7 %collective-permute-done.45.refs_1_ = f32[264,128]{1,0:T(8,128)S(1)} collective-permute-done((f32[264,128]{1,0:T(8,128)S(1)}, f32[264,128]{1,0:T(8,128)S(1)}, u32[]{:S(2)}, u32[]{:S(2)}) %collective-permute-start.45) | collective-permute-done | bytes 135200 | tf_op jit(solution)/shard_map/ppermute | solution.py:242
  106.7 1.3 %collective-permute-done.47.refs_3_ = f32[264,128]{1,0:T(8,128)S(1)} collective-permute-done((f32[264,128]{1,0:T(8,128)S(1)}, f32[264,128]{1,0:T(8,128)S(1)}, u32[]{:S(2)}, u32[]{:S(2)}) %collective-permute-start.47) | collective-permute-done | bytes 135200 | tf_op jit(solution)/shard_map/ppermute | solution.py:242
  107.9 0.9 last.1
  108.8 10.8 %all_to_all.5.tiles_ref = f32[16,8,128]{2,1,0:T(8,128)S(1)} all-to-all(f32[16,8,128]{2,1,0:T(8,128)S(1)} %broadcast_in_dim.2), channel_id=1, replica_groups=mesh['group'=2,'term'=16] {'term'}, dimensions={0} | all-to-all | bytes 131072 | tf_op jit(solution)/shard_map/all_to_all | solution.py:387
  119.6 0.9 norm.1
  (47 shorter events, 0.5 us)
Async XLA Ops:
  0.6 7.4 %collective-permute-start.2 = (f32[2,128,128]{2,1,0:T(8,128)}, f32[2,128,128]{2,1,0:T(8,128)S(1)}, u32[]{:S(2)}, u32[]{:S(2)}) collective-permute-start(f32[2,128,128]{2,1,0:T(8,128)} %vector_in.1), channel_id=1, source_target_pairs={{0,2},{1,3},{2,0},{3,1},{4,6},{5,7},{6,4},{7,5},{8,10},{9,11},{10,... | collective-permute-start | bytes 393224 | tf_op jit(solution)/shard_map/ppermute | solution.py:242
  3.7 5.6 %collective-permute-start.1 = (f32[2,128,128]{2,1,0:T(8,128)}, f32[2,128,128]{2,1,0:T(8,128)S(1)}, u32[]{:S(2)}, u32[]{:S(2)}) collective-permute-start(f32[2,128,128]{2,1,0:T(8,128)} %vector_in.1), channel_id=1, source_target_pairs={{0,1},{1,0},{2,3},{3,2},{4,5},{5,4},{6,7},{7,6},{8,9},{9,8},{10,11... | collective-permute-start | bytes 393224 | tf_op jit(solution)/shard_map/ppermute | solution.py:242
  3.7 8.4 %collective-permute-start = (f32[2,128,128]{2,1,0:T(8,128)}, f32[2,128,128]{2,1,0:T(8,128)S(1)}, u32[]{:S(2)}, u32[]{:S(2)}) collective-permute-start(f32[2,128,128]{2,1,0:T(8,128)} %vector_in.1), channel_id=1, source_target_pairs={{0,12},{1,13},{2,14},{3,15},{4,8},{5,9},{6,10},{7,11},{8,4},{9,5},... | collective-permute-start | bytes 393224 | tf_op jit(solution)/shard_map/ppermute | solution.py:242
  7.3 12.1 %collective-permute-start.8 = (f32[2,128,128]{2,1,0:T(8,128)}, f32[2,128,128]{2,1,0:T(8,128)S(1)}, u32[]{:S(2)}, u32[]{:S(2)}) collective-permute-start(f32[2,128,128]{2,1,0:T(8,128)} %vector_in.1), channel_id=1, source_target_pairs={{0,8},{1,9},{2,10},{3,11},{4,12},{5,13},{6,14},{7,15},{8,0},{9,1},... | collective-permute-start | bytes 393224 | tf_op jit(solution)/shard_map/ppermute | solution.py:242
  7.3 12.6 %collective-permute-start.4 = (f32[2,128,128]{2,1,0:T(8,128)}, f32[2,128,128]{2,1,0:T(8,128)S(1)}, u32[]{:S(2)}, u32[]{:S(2)}) collective-permute-start(f32[2,128,128]{2,1,0:T(8,128)} %vector_in.1), channel_id=1, source_target_pairs={{0,4},{1,5},{2,6},{3,7},{4,0},{5,1},{6,2},{7,3},{8,12},{9,13},{10,... | collective-permute-start | bytes 393224 | tf_op jit(solution)/shard_map/ppermute | solution.py:242
  8.1 17.2 %collective-permute-start.6 = (f32[2,128,128]{2,1,0:T(8,128)S(1)}, f32[2,128,128]{2,1,0:T(8,128)S(1)}, u32[]{:S(2)}, u32[]{:S(2)}) collective-permute-start(f32[2,128,128]{2,1,0:T(8,128)S(1)} %collective-permute-done.2.refs_2_), channel_id=1, source_target_pairs={{0,4},{1,5},{2,6},{3,7},{4,0},{5,1},{6,2},{7,3},{8,12},{9,13},{10,... | collective-permute-start | bytes 393224 | tf_op jit(solution)/shard_map/ppermute | solution.py:242
  9.3 16.0 %collective-permute-start.3 = (f32[2,128,128]{2,1,0:T(8,128)S(1)}, f32[2,128,128]{2,1,0:T(8,128)S(1)}, u32[]{:S(2)}, u32[]{:S(2)}) collective-permute-start(f32[2,128,128]{2,1,0:T(8,128)S(1)} %collective-permute-done.2.refs_2_), channel_id=1, source_target_pairs={{0,1},{1,0},{2,3},{3,2},{4,5},{5,4},{6,7},{7,6},{8,9},{9,8},{10,11... | collective-permute-start | bytes 393224 | tf_op jit(solution)/shard_map/ppermute | solution.py:242
  12.1 13.8 %collective-permute-start.13 = (f32[2,128,128]{2,1,0:T(8,128)S(1)}, f32[2,128,128]{2,1,0:T(8,128)S(1)}, u32[]{:S(2)}, u32[]{:S(2)}) collective-permute-start(f32[2,128,128]{2,1,0:T(8,128)S(1)} %collective-permute-done.refs_12_), channel_id=1, source_target_pairs={{0,2},{1,3},{2,0},{3,1},{4,6},{5,7},{6,4},{7,5},{8,10},{9,11},{10,... | collective-permute-start | bytes 393224 | tf_op jit(solution)/shard_map/ppermute | solution.py:242
  19.3 6.6 %collective-permute-start.10 = (f32[2,128,128]{2,1,0:T(8,128)S(1)}, f32[2,128,128]{2,1,0:T(8,128)S(1)}, u32[]{:S(2)}, u32[]{:S(2)}) collective-permute-start(f32[2,128,128]{2,1,0:T(8,128)S(1)} %collective-permute-done.8.refs_8_), channel_id=1, source_target_pairs={{0,2},{1,3},{2,0},{3,1},{4,6},{5,7},{6,4},{7,5},{8,10},{9,11},{10,... | collective-permute-start | bytes 393224 | tf_op jit(solution)/shard_map/ppermute | solution.py:242
  19.8 6.5 %collective-permute-start.9 = (f32[2,128,128]{2,1,0:T(8,128)S(1)}, f32[2,128,128]{2,1,0:T(8,128)S(1)}, u32[]{:S(2)}, u32[]{:S(2)}) collective-permute-start(f32[2,128,128]{2,1,0:T(8,128)S(1)} %collective-permute-done.8.refs_8_), channel_id=1, source_target_pairs={{0,1},{1,0},{2,3},{3,2},{4,5},{5,4},{6,7},{7,6},{8,9},{9,8},{10,11... | collective-permute-start | bytes 393224 | tf_op jit(solution)/shard_map/ppermute | solution.py:242
  19.8 0.7 copy-start.1
  25.2 1.6 %collective-permute-start.12 = (f32[2,128,128]{2,1,0:T(8,128)S(1)}, f32[2,128,128]{2,1,0:T(8,128)S(1)}, u32[]{:S(2)}, u32[]{:S(2)}) collective-permute-start(f32[2,128,128]{2,1,0:T(8,128)S(1)} %collective-permute-done.refs_12_), channel_id=1, source_target_pairs={{0,1},{1,0},{2,3},{3,2},{4,5},{5,4},{6,7},{7,6},{8,9},{9,8},{10,11... | collective-permute-start | bytes 393224 | tf_op jit(solution)/shard_map/ppermute | solution.py:242
  25.3 1.5 %collective-permute-start.5 = (f32[2,128,128]{2,1,0:T(8,128)S(1)}, f32[2,128,128]{2,1,0:T(8,128)S(1)}, u32[]{:S(2)}, u32[]{:S(2)}) collective-permute-start(f32[2,128,128]{2,1,0:T(8,128)S(1)} %collective-permute-done.4.refs_4_), channel_id=1, source_target_pairs={{0,1},{1,0},{2,3},{3,2},{4,5},{5,4},{6,7},{7,6},{8,9},{9,8},{10,11... | collective-permute-start | bytes 393224 | tf_op jit(solution)/shard_map/ppermute | solution.py:242
  25.8 1.3 %collective-permute-start.7 = (f32[2,128,128]{2,1,0:T(8,128)S(1)}, f32[2,128,128]{2,1,0:T(8,128)S(1)}, u32[]{:S(2)}, u32[]{:S(2)}) collective-permute-start(f32[2,128,128]{2,1,0:T(8,128)S(1)} %collective-permute-done.6.refs_6_), channel_id=1, source_target_pairs={{0,1},{1,0},{2,3},{3,2},{4,5},{5,4},{6,7},{7,6},{8,9},{9,8},{10,11... | collective-permute-start | bytes 393224 | tf_op jit(solution)/shard_map/ppermute | solution.py:242
  25.9 1.4 %collective-permute-start.14 = (f32[2,128,128]{2,1,0:T(8,128)S(1)}, f32[2,128,128]{2,1,0:T(8,128)S(1)}, u32[]{:S(2)}, u32[]{:S(2)}) collective-permute-start(f32[2,128,128]{2,1,0:T(8,128)S(1)} %collective-permute-done.13.refs_14_), channel_id=1, source_target_pairs={{0,1},{1,0},{2,3},{3,2},{4,5},{5,4},{6,7},{7,6},{8,9},{9,8},{10,11... | collective-permute-start | bytes 393224 | tf_op jit(solution)/shard_map/ppermute | solution.py:242
  26.3 1.3 %collective-permute-start.11 = (f32[2,128,128]{2,1,0:T(8,128)S(1)}, f32[2,128,128]{2,1,0:T(8,128)S(1)}, u32[]{:S(2)}, u32[]{:S(2)}) collective-permute-start(f32[2,128,128]{2,1,0:T(8,128)S(1)} %collective-permute-done.10.refs_10_), channel_id=1, source_target_pairs={{0,1},{1,0},{2,3},{3,2},{4,5},{5,4},{6,7},{7,6},{8,9},{9,8},{10,11... | collective-permute-start | bytes 393224 | tf_op jit(solution)/shard_map/ppermute | solution.py:242
  33.8 8.5 %collective-permute-start.15 = (f32[648,128]{1,0:T(8,128)S(1)}, f32[648,128]{1,0:T(8,128)S(1)}, u32[]{:S(2)}, u32[]{:S(2)}) collective-permute-start(f32[648,128]{1,0:T(8,128)S(1)} %get-tuple-element.42.far_in), channel_id=1, source_target_pairs={{0,1},{1,0},{2,3},{3,2},{4,5},{5,4},{6,7},{7,6},{8,9},{9,8},{10,11... | collective-permute-start | bytes 995336 | tf_op jit(solution)/shard_map/ppermute | solution.py:242
  34.0 7.0 %collective-permute-start.16 = (f32[264,128]{1,0:T(8,128)S(1)}, f32[264,128]{1,0:T(8,128)S(1)}, u32[]{:S(2)}, u32[]{:S(2)}) collective-permute-start(f32[264,128]{1,0:T(8,128)S(1)} %get-tuple-element.43), channel_id=1, source_target_pairs={{0,2},{1,3},{2,0},{3,1},{4,6},{5,7},{6,4},{7,5},{8,10},{9,11},{10,... | collective-permute-start | bytes 405512 | tf_op jit(solution)/shard_map/ppermute | solution.py:242
  34.5 7.8 %collective-permute-start.17 = (f32[264,128]{1,0:T(8,128)S(1)}, f32[264,128]{1,0:T(8,128)S(1)}, u32[]{:S(2)}, u32[]{:S(2)}) collective-permute-start(f32[264,128]{1,0:T(8,128)S(1)} %get-tuple-element.44), channel_id=1, source_target_pairs={{0,3},{1,2},{2,1},{3,0},{4,7},{5,6},{6,5},{7,4},{8,11},{9,10},{10,... | collective-permute-start | bytes 405512 | tf_op jit(solution)/shard_map/ppermute | solution.py:242
  35.8 4.9 %collective-permute-start.18 = (f32[128,128]{1,0:T(8,128)S(1)}, f32[128,128]{1,0:T(8,128)S(1)}, u32[]{:S(2)}, u32[]{:S(2)}) collective-permute-start(f32[128,128]{1,0:T(8,128)S(1)} %get-tuple-element.45), channel_id=1, source_target_pairs={{0,4},{1,5},{2,6},{3,7},{4,0},{5,1},{6,2},{7,3},{8,12},{9,13},{10,... | collective-permute-start | bytes 196616 | tf_op jit(solution)/shard_map/ppermute | solution.py:242
  35.8 5.2 %collective-permute-start.19 = (f32[128,128]{1,0:T(8,128)S(1)}, f32[128,128]{1,0:T(8,128)S(1)}, u32[]{:S(2)}, u32[]{:S(2)}) collective-permute-start(f32[128,128]{1,0:T(8,128)S(1)} %get-tuple-element.46), channel_id=1, source_target_pairs={{0,5},{1,4},{2,7},{3,6},{4,1},{5,0},{6,3},{7,2},{8,13},{9,12},{10,... | collective-permute-start | bytes 196616 | tf_op jit(solution)/shard_map/ppermute | solution.py:242
  42.3 14.4 %copy-start = (f32[2,128,128]{2,1,0:T(8,128)S(1)}, f32[2,128,128]{2,1,0:T(8,128)}, u32[]{:S(2)}) copy-start(f32[2,128,128]{2,1,0:T(8,128)} %precond_ref.3) | copy-start | bytes 393220
  43.1 9.4 %collective-permute-start.21 = (f32[264,128]{1,0:T(8,128)S(1)}, f32[264,128]{1,0:T(8,128)S(1)}, u32[]{:S(2)}, u32[]{:S(2)}) collective-permute-start(f32[264,128]{1,0:T(8,128)S(1)} %get-tuple-element.51), channel_id=1, source_target_pairs={{0,12},{1,13},{2,14},{3,15},{4,8},{5,9},{6,10},{7,11},{8,4},{9,5},... | collective-permute-start | bytes 405512 | tf_op jit(solution)/shard_map/ppermute | solution.py:242
  45.1 11.6 %collective-permute-start.22 = (f32[264,128]{1,0:T(8,128)S(1)}, f32[264,128]{1,0:T(8,128)S(1)}, u32[]{:S(2)}, u32[]{:S(2)}) collective-permute-start(f32[264,128]{1,0:T(8,128)S(1)} %get-tuple-element.52), channel_id=1, source_target_pairs={{0,8},{1,9},{2,10},{3,11},{4,12},{5,13},{6,14},{7,15},{8,0},{9,1},... | collective-permute-start | bytes 405512 | tf_op jit(solution)/shard_map/ppermute | solution.py:242
  45.1 11.6 %collective-permute-start.23 = (f32[264,128]{1,0:T(8,128)S(1)}, f32[264,128]{1,0:T(8,128)S(1)}, u32[]{:S(2)}, u32[]{:S(2)}) collective-permute-start(f32[264,128]{1,0:T(8,128)S(1)} %get-tuple-element.50.refs_0_), channel_id=1, source_target_pairs={{0,4},{1,5},{2,6},{3,7},{4,0},{5,1},{6,2},{7,3},{8,12},{9,13},{10,... | collective-permute-start | bytes 405512 | tf_op jit(solution)/shard_map/ppermute | solution.py:242
  47.5 5.0 %collective-permute-start.20 = (f32[2,128,128]{2,1,0:T(8,128)S(1)}, f32[2,128,128]{2,1,0:T(8,128)S(1)}, u32[]{:S(2)}, u32[]{:S(2)}) collective-permute-start(f32[2,128,128]{2,1,0:T(8,128)S(1)} %get-tuple-element.48), channel_id=1, source_target_pairs={{0,2},{1,3},{2,0},{3,1},{4,6},{5,7},{6,4},{7,5},{8,10},{9,11},{10,... | collective-permute-start | bytes 393224 | tf_op jit(solution)/shard_map/ppermute | solution.py:242
  56.9 8.3 %collective-permute-start.35 = (f32[2,128,128]{2,1,0:T(8,128)S(1)}, f32[2,128,128]{2,1,0:T(8,128)S(1)}, u32[]{:S(2)}, u32[]{:S(2)}) collective-permute-start(f32[2,128,128]{2,1,0:T(8,128)S(1)} %step.1.refs_0_.vector_ref), channel_id=1, source_target_pairs={{0,12},{1,13},{2,14},{3,15},{4,8},{5,9},{6,10},{7,11},{8,4},{9,5},... | collective-permute-start | bytes 393224 | tf_op jit(solution)/shard_map/ppermute | solution.py:242
  59.4 11.2 %collective-permute-start.31 = (f32[2,128,128]{2,1,0:T(8,128)S(1)}, f32[2,128,128]{2,1,0:T(8,128)S(1)}, u32[]{:S(2)}, u32[]{:S(2)}) collective-permute-start(f32[2,128,128]{2,1,0:T(8,128)S(1)} %step.1.refs_0_.vector_ref), channel_id=1, source_target_pairs={{0,8},{1,9},{2,10},{3,11},{4,12},{5,13},{6,14},{7,15},{8,0},{9,1},... | collective-permute-start | bytes 393224 | tf_op jit(solution)/shard_map/ppermute | solution.py:242
  59.4 11.2 %collective-permute-start.27 = (f32[2,128,128]{2,1,0:T(8,128)S(1)}, f32[2,128,128]{2,1,0:T(8,128)S(1)}, u32[]{:S(2)}, u32[]{:S(2)}) collective-permute-start(f32[2,128,128]{2,1,0:T(8,128)S(1)} %step.1.refs_0_.vector_ref), channel_id=1, source_target_pairs={{0,4},{1,5},{2,6},{3,7},{4,0},{5,1},{6,2},{7,3},{8,12},{9,13},{10,... | collective-permute-start | bytes 393224 | tf_op jit(solution)/shard_map/ppermute | solution.py:242
  61.4 10.2 %collective-permute-start.25 = (f32[2,128,128]{2,1,0:T(8,128)S(1)}, f32[2,128,128]{2,1,0:T(8,128)S(1)}, u32[]{:S(2)}, u32[]{:S(2)}) collective-permute-start(f32[2,128,128]{2,1,0:T(8,128)S(1)} %step.1.refs_0_.vector_ref), channel_id=1, source_target_pairs={{0,2},{1,3},{2,0},{3,1},{4,6},{5,7},{6,4},{7,5},{8,10},{9,11},{10,... | collective-permute-start | bytes 393224 | tf_op jit(solution)/shard_map/ppermute | solution.py:242
  62.2 9.6 %collective-permute-start.24 = (f32[2,128,128]{2,1,0:T(8,128)S(1)}, f32[2,128,128]{2,1,0:T(8,128)S(1)}, u32[]{:S(2)}, u32[]{:S(2)}) collective-permute-start(f32[2,128,128]{2,1,0:T(8,128)S(1)} %step.1.refs_0_.vector_ref), channel_id=1, source_target_pairs={{0,1},{1,0},{2,3},{3,2},{4,5},{5,4},{6,7},{7,6},{8,9},{9,8},{10,11... | collective-permute-start | bytes 393224 | tf_op jit(solution)/shard_map/ppermute | solution.py:242
  65.3 6.6 %collective-permute-start.37 = (f32[2,128,128]{2,1,0:T(8,128)S(1)}, f32[2,128,128]{2,1,0:T(8,128)S(1)}, u32[]{:S(2)}, u32[]{:S(2)}) collective-permute-start(f32[2,128,128]{2,1,0:T(8,128)S(1)} %collective-permute-done.35.refs_12_), channel_id=1, source_target_pairs={{0,2},{1,3},{2,0},{3,1},{4,6},{5,7},{6,4},{7,5},{8,10},{9,11},{10,... | collective-permute-start | bytes 393224 | tf_op jit(solution)/shard_map/ppermute | solution.py:242
  70.5 1.6 %collective-permute-start.36 = (f32[2,128,128]{2,1,0:T(8,128)S(1)}, f32[2,128,128]{2,1,0:T(8,128)S(1)}, u32[]{:S(2)}, u32[]{:S(2)}) collective-permute-start(f32[2,128,128]{2,1,0:T(8,128)S(1)} %collective-permute-done.35.refs_12_), channel_id=1, source_target_pairs={{0,1},{1,0},{2,3},{3,2},{4,5},{5,4},{6,7},{7,6},{8,9},{9,8},{10,11... | collective-permute-start | bytes 393224 | tf_op jit(solution)/shard_map/ppermute | solution.py:242
  70.5 5.9 %collective-permute-start.33 = (f32[2,128,128]{2,1,0:T(8,128)S(1)}, f32[2,128,128]{2,1,0:T(8,128)S(1)}, u32[]{:S(2)}, u32[]{:S(2)}) collective-permute-start(f32[2,128,128]{2,1,0:T(8,128)S(1)} %collective-permute-done.31.refs_8_), channel_id=1, source_target_pairs={{0,2},{1,3},{2,0},{3,1},{4,6},{5,7},{6,4},{7,5},{8,10},{9,11},{10,... | collective-permute-start | bytes 393224 | tf_op jit(solution)/shard_map/ppermute | solution.py:242
  71.6 4.9 %collective-permute-start.32 = (f32[2,128,128]{2,1,0:T(8,128)S(1)}, f32[2,128,128]{2,1,0:T(8,128)S(1)}, u32[]{:S(2)}, u32[]{:S(2)}) collective-permute-start(f32[2,128,128]{2,1,0:T(8,128)S(1)} %collective-permute-done.31.refs_8_), channel_id=1, source_target_pairs={{0,1},{1,0},{2,3},{3,2},{4,5},{5,4},{6,7},{7,6},{8,9},{9,8},{10,11... | collective-permute-start | bytes 393224 | tf_op jit(solution)/shard_map/ppermute | solution.py:242
  71.8 5.7 %collective-permute-start.29 = (f32[2,128,128]{2,1,0:T(8,128)S(1)}, f32[2,128,128]{2,1,0:T(8,128)S(1)}, u32[]{:S(2)}, u32[]{:S(2)}) collective-permute-start(f32[2,128,128]{2,1,0:T(8,128)S(1)} %collective-permute-done.25.refs_2_), channel_id=1, source_target_pairs={{0,4},{1,5},{2,6},{3,7},{4,0},{5,1},{6,2},{7,3},{8,12},{9,13},{10,... | collective-permute-start | bytes 393224 | tf_op jit(solution)/shard_map/ppermute | solution.py:242
  71.8 5.7 %collective-permute-start.26 = (f32[2,128,128]{2,1,0:T(8,128)S(1)}, f32[2,128,128]{2,1,0:T(8,128)S(1)}, u32[]{:S(2)}, u32[]{:S(2)}) collective-permute-start(f32[2,128,128]{2,1,0:T(8,128)S(1)} %collective-permute-done.25.refs_2_), channel_id=1, source_target_pairs={{0,1},{1,0},{2,3},{3,2},{4,5},{5,4},{6,7},{7,6},{8,9},{9,8},{10,11... | collective-permute-start | bytes 393224 | tf_op jit(solution)/shard_map/ppermute | solution.py:242
  72.2 5.3 %collective-permute-start.28 = (f32[2,128,128]{2,1,0:T(8,128)S(1)}, f32[2,128,128]{2,1,0:T(8,128)S(1)}, u32[]{:S(2)}, u32[]{:S(2)}) collective-permute-start(f32[2,128,128]{2,1,0:T(8,128)S(1)} %collective-permute-done.27.refs_4_), channel_id=1, source_target_pairs={{0,1},{1,0},{2,3},{3,2},{4,5},{5,4},{6,7},{7,6},{8,9},{9,8},{10,11... | collective-permute-start | bytes 393224 | tf_op jit(solution)/shard_map/ppermute | solution.py:242
  76.4 1.3 %collective-permute-start.38 = (f32[2,128,128]{2,1,0:T(8,128)S(1)}, f32[2,128,128]{2,1,0:T(8,128)S(1)}, u32[]{:S(2)}, u32[]{:S(2)}) collective-permute-start(f32[2,128,128]{2,1,0:T(8,128)S(1)} %collective-permute-done.37.refs_14_), channel_id=1, source_target_pairs={{0,1},{1,0},{2,3},{3,2},{4,5},{5,4},{6,7},{7,6},{8,9},{9,8},{10,11... | collective-permute-start | bytes 393224 | tf_op jit(solution)/shard_map/ppermute | solution.py:242
  76.5 1.5 %collective-permute-start.34 = (f32[2,128,128]{2,1,0:T(8,128)S(1)}, f32[2,128,128]{2,1,0:T(8,128)S(1)}, u32[]{:S(2)}, u32[]{:S(2)}) collective-permute-start(f32[2,128,128]{2,1,0:T(8,128)S(1)} %collective-permute-done.33.refs_10_), channel_id=1, source_target_pairs={{0,1},{1,0},{2,3},{3,2},{4,5},{5,4},{6,7},{7,6},{8,9},{9,8},{10,11... | collective-permute-start | bytes 393224 | tf_op jit(solution)/shard_map/ppermute | solution.py:242
  77.5 1.3 %collective-permute-start.30 = (f32[2,128,128]{2,1,0:T(8,128)S(1)}, f32[2,128,128]{2,1,0:T(8,128)S(1)}, u32[]{:S(2)}, u32[]{:S(2)}) collective-permute-start(f32[2,128,128]{2,1,0:T(8,128)S(1)} %collective-permute-done.29.refs_6_), channel_id=1, source_target_pairs={{0,1},{1,0},{2,3},{3,2},{4,5},{5,4},{6,7},{7,6},{8,9},{9,8},{10,11... | collective-permute-start | bytes 393224 | tf_op jit(solution)/shard_map/ppermute | solution.py:242
  85.1 8.5 %collective-permute-start.39 = (f32[648,128]{1,0:T(8,128)S(1)}, f32[648,128]{1,0:T(8,128)S(1)}, u32[]{:S(2)}, u32[]{:S(2)}) collective-permute-start(f32[648,128]{1,0:T(8,128)S(1)} %get-tuple-element.54.far_in), channel_id=1, source_target_pairs={{0,1},{1,0},{2,3},{3,2},{4,5},{5,4},{6,7},{7,6},{8,9},{9,8},{10,11... | collective-permute-start | bytes 995336 | tf_op jit(solution)/shard_map/ppermute | solution.py:242
  85.2 7.0 %collective-permute-start.40 = (f32[264,128]{1,0:T(8,128)S(1)}, f32[264,128]{1,0:T(8,128)S(1)}, u32[]{:S(2)}, u32[]{:S(2)}) collective-permute-start(f32[264,128]{1,0:T(8,128)S(1)} %get-tuple-element.55), channel_id=1, source_target_pairs={{0,2},{1,3},{2,0},{3,1},{4,6},{5,7},{6,4},{7,5},{8,10},{9,11},{10,... | collective-permute-start | bytes 405512 | tf_op jit(solution)/shard_map/ppermute | solution.py:242
  86.2 7.5 %collective-permute-start.41 = (f32[264,128]{1,0:T(8,128)S(1)}, f32[264,128]{1,0:T(8,128)S(1)}, u32[]{:S(2)}, u32[]{:S(2)}) collective-permute-start(f32[264,128]{1,0:T(8,128)S(1)} %get-tuple-element.56), channel_id=1, source_target_pairs={{0,3},{1,2},{2,1},{3,0},{4,7},{5,6},{6,5},{7,4},{8,11},{9,10},{10,... | collective-permute-start | bytes 405512 | tf_op jit(solution)/shard_map/ppermute | solution.py:242
  87.1 4.9 %collective-permute-start.42 = (f32[128,128]{1,0:T(8,128)S(1)}, f32[128,128]{1,0:T(8,128)S(1)}, u32[]{:S(2)}, u32[]{:S(2)}) collective-permute-start(f32[128,128]{1,0:T(8,128)S(1)} %get-tuple-element.57), channel_id=1, source_target_pairs={{0,4},{1,5},{2,6},{3,7},{4,0},{5,1},{6,2},{7,3},{8,12},{9,13},{10,... | collective-permute-start | bytes 196616 | tf_op jit(solution)/shard_map/ppermute | solution.py:242
  87.3 5.0 %collective-permute-start.43 = (f32[128,128]{1,0:T(8,128)S(1)}, f32[128,128]{1,0:T(8,128)S(1)}, u32[]{:S(2)}, u32[]{:S(2)}) collective-permute-start(f32[128,128]{1,0:T(8,128)S(1)} %get-tuple-element.58), channel_id=1, source_target_pairs={{0,5},{1,4},{2,7},{3,6},{4,1},{5,0},{6,3},{7,2},{8,13},{9,12},{10,... | collective-permute-start | bytes 196616 | tf_op jit(solution)/shard_map/ppermute | solution.py:242
  94.4 12.3 %collective-permute-start.45 = (f32[264,128]{1,0:T(8,128)S(1)}, f32[264,128]{1,0:T(8,128)S(1)}, u32[]{:S(2)}, u32[]{:S(2)}) collective-permute-start(f32[264,128]{1,0:T(8,128)S(1)} %get-tuple-element.63), channel_id=1, source_target_pairs={{0,8},{1,9},{2,10},{3,11},{4,12},{5,13},{6,14},{7,15},{8,0},{9,1},... | collective-permute-start | bytes 405512 | tf_op jit(solution)/shard_map/ppermute | solution.py:242
  94.5 12.2 %collective-permute-start.46 = (f32[264,128]{1,0:T(8,128)S(1)}, f32[264,128]{1,0:T(8,128)S(1)}, u32[]{:S(2)}, u32[]{:S(2)}) collective-permute-start(f32[264,128]{1,0:T(8,128)S(1)} %get-tuple-element.64), channel_id=1, source_target_pairs={{0,12},{1,13},{2,14},{3,15},{4,8},{5,9},{6,10},{7,11},{8,4},{9,5},... | collective-permute-start | bytes 405512 | tf_op jit(solution)/shard_map/ppermute | solution.py:242
  97.0 10.9 %collective-permute-start.47 = (f32[264,128]{1,0:T(8,128)S(1)}, f32[264,128]{1,0:T(8,128)S(1)}, u32[]{:S(2)}, u32[]{:S(2)}) collective-permute-start(f32[264,128]{1,0:T(8,128)S(1)} %get-tuple-element.62.refs_0_), channel_id=1, source_target_pairs={{0,4},{1,5},{2,6},{3,7},{4,0},{5,1},{6,2},{7,3},{8,12},{9,13},{10,... | collective-permute-start | bytes 405512 | tf_op jit(solution)/shard_map/ppermute | solution.py:242
  97.9 5.0 %collective-permute-start.44 = (f32[2,128,128]{2,1,0:T(8,128)S(1)}, f32[2,128,128]{2,1,0:T(8,128)S(1)}, u32[]{:S(2)}, u32[]{:S(2)}) collective-permute-start(f32[2,128,128]{2,1,0:T(8,128)S(1)} %get-tuple-element.60), channel_id=1, source_target_pairs={{0,2},{1,3},{2,0},{3,1},{4,6},{5,7},{6,4},{7,5},{8,10},{9,11},{10,... | collective-permute-start | bytes 393224 | tf_op jit(solution)/shard_map/ppermute | solution.py:242

commit v17 on v15

--- a/solution.py
+++ b/solution.py
@@ -181,17 +181,17 @@
 
     lax.fori_loop(0, count_ref[0], add, 0)
     late = 0
-    for low_end in range(0, n, 4):
-        for r in range(low_end, low_end + 4):
+    for low_end in range(0, n, 2):
+        for r in range(low_end, low_end + 2):
             for j in range(terms):
                 at = j * n + r
                 high, low = halves(block[first_ref[at]] + block[second_ref[at]])
                 total[r, :, j * width:(j + 1) * width] = high
                 total[r, :, (terms + j) * width:(terms + j + 1) * width] = low
-        both = jnp.dot(total[low_end:low_end + 4].reshape(4 * rows, 2 * terms * width), rr_ref[...],
+        both = jnp.dot(total[low_end:low_end + 2].reshape(2 * rows, 2 * terms * width), rr_ref[...],
                        preferred_element_type=jnp.float32)
         slots = both[:, :width] + both[:, width:]
-        for r in range(low_end, low_end + 4):
+        for r in range(low_end, low_end + 2):
             slot = slots[(r - low_end) * rows:(r - low_end + 1) * rows]
             product = product + tile_sum(pieces[r][mine_ref[r], start:start + rows, :] * slot)
             g, core = divmod(r, 2)

time: 120 us -> 120 us (level)
  transfers between devices with their start and end apart: 48 -> 48, of which waited for: 24 -> 24; matrix products, arithmetic and copies ran while one was open for 0% -> 0% of each run, Pallas kernels for 2% -> 3%
where the time goes in v17:
time: 120 us
  waiting for transfers between devices  51.9 us (43%)
  starting transfers between devices  35.3 us (29%)
  Pallas kernels  18.9 us (16%)
  blocking collectives  11.7 us (10%)
  between operations  1.41 us (1%)
    ppermute x48, waiting for transfers between devices, swapped(): return lax.ppermute(x, 'term', [(i, i ^ k) for i in range(n)])  51.9 us
    ppermute x48, starting transfers between devices, swapped(): return lax.ppermute(x, 'term', [(i, i ^ k) for i in range(n)])  35.3 us
    pallas_call x2, Pallas kernels, apply(): pl.pallas_call(functools.partial(apply_kernel, n, npairs, over_rows, rows...  12.1 us
    all_to_all x1, blocking collectives, shards(): lax.all_to_all(jnp.broadcast_to(partial[None], (n, 8, width)), 'term', sp...  11.7 us
    pallas_call x5, Pallas kernels, local(): pl.pallas_call(kernel, out_shape=out_shape, in_specs=[SMEM] * len(scalars...  3.42 us
    pallas_call x1, Pallas kernels, prep(): pl.pallas_call(functools.partial(prep_kernel, n, terms * n + 1), out_shap...  3.4 us
  transfers between devices with their start and end apart: 48, of which 24 were waited for; matrix products, arithmetic and copies ran while one was open for 0% of the time, Pallas kernels for 3%

profile of v17, /device:TPU:0, one launch (start us, length us, event | category | flops | bytes accessed | tf_op | source)
XLA Modules:
  0.0 119.7 jit_solution(10716004247996448800)
XLA Ops:
  0.6 3.0 %collective-permute-start.2 = (f32[2,128,128]{2,1,0:T(8,128)}, f32[2,128,128]{2,1,0:T(8,128)S(1)}, u32[]{:S(2)}, u32[]{:S(2)}) collective-permute-start(f32[2,128,128]{2,1,0:T(8,128)} %vector_in.1), channel_id=1, source_target_pairs={{0,2},{1,3},{2,0},{3,1},{4,6},{5,7},{6,4},{7,5},{8,10},{9,11},{10,... | collective-permute-start | bytes 393224 | tf_op jit(solution)/shard_map/ppermute | solution.py:242
  3.7 2.6 %collective-permute-start.8 = (f32[2,128,128]{2,1,0:T(8,128)}, f32[2,128,128]{2,1,0:T(8,128)S(1)}, u32[]{:S(2)}, u32[]{:S(2)}) collective-permute-start(f32[2,128,128]{2,1,0:T(8,128)} %vector_in.1), channel_id=1, source_target_pairs={{0,8},{1,9},{2,10},{3,11},{4,12},{5,13},{6,14},{7,15},{8,0},{9,1},... | collective-permute-start | bytes 393224 | tf_op jit(solution)/shard_map/ppermute | solution.py:242
  6.3 1.3 %collective-permute-start = (f32[2,128,128]{2,1,0:T(8,128)}, f32[2,128,128]{2,1,0:T(8,128)S(1)}, u32[]{:S(2)}, u32[]{:S(2)}) collective-permute-start(f32[2,128,128]{2,1,0:T(8,128)} %vector_in.1), channel_id=1, source_target_pairs={{0,12},{1,13},{2,14},{3,15},{4,8},{5,9},{6,10},{7,11},{8,4},{9,5},... | collective-permute-start | bytes 393224 | tf_op jit(solution)/shard_map/ppermute | solution.py:242
  7.6 0.2 collective-permute-start.4
  7.8 1.8 %collective-permute-start.6 = (f32[2,128,128]{2,1,0:T(8,128)S(1)}, f32[2,128,128]{2,1,0:T(8,128)S(1)}, u32[]{:S(2)}, u32[]{:S(2)}) collective-permute-start(f32[2,128,128]{2,1,0:T(8,128)S(1)} %collective-permute-done.2.refs_2_), channel_id=1, source_target_pairs={{0,4},{1,5},{2,6},{3,7},{4,0},{5,1},{6,2},{7,3},{8,12},{9,13},{10,... | collective-permute-start | bytes 393224 | tf_op jit(solution)/shard_map/ppermute | solution.py:242
  10.3 0.6 copy.12
  10.9 3.4 %prep.1 = (bf16[8,128,512]{2,1,0:T(8,128)(2,1)S(1)}, bf16[2048,256]{1,0:T(8,128)(2,1)S(1)}, s32[721]{0:T(1024)S(1)}, f32[2,128,128]{2,1,0:T(8,128)S(1)}) custom-call(s32[1]{0:T(128)} %bitcast.me_ref, s32[16,16]{1,0:T(8,128)} %fetch_in.1, s32[16,16]{1,0:T(8,128)} %store_in.1, s32[384]{0:T(512)} %bitcast.8, s32[1]{0:T(128)S(6)} %copy.13.live_in, ...), custom_call_target="tpu_custom_call" | custom-call | tf_op jit(solution)/shard_map/prep/pallas_call | solution.py:132
  14.4 2.2 %collective-permute-done.8.refs_8_ = f32[2,128,128]{2,1,0:T(8,128)S(1)} collective-permute-done((f32[2,128,128]{2,1,0:T(8,128)}, f32[2,128,128]{2,1,0:T(8,128)S(1)}, u32[]{:S(2)}, u32[]{:S(2)}) %collective-permute-start.8) | collective-permute-done | bytes 131104 | tf_op jit(solution)/shard_map/ppermute | solution.py:242
  16.5 0.4 collective-permute-start.10
  17.0 1.1 collective-permute-done.4.refs_4_
  18.1 1.4 %collective-permute-done.6.refs_6_ = f32[2,128,128]{2,1,0:T(8,128)S(1)} collective-permute-done((f32[2,128,128]{2,1,0:T(8,128)S(1)}, f32[2,128,128]{2,1,0:T(8,128)S(1)}, u32[]{:S(2)}, u32[]{:S(2)}) %collective-permute-start.6) | collective-permute-done | bytes 131104 | tf_op jit(solution)/shard_map/ppermute | solution.py:242
  19.5 0.5 collective-permute-start.13
  20.0 1.8 %collective-permute-done.10.refs_10_ = f32[2,128,128]{2,1,0:T(8,128)S(1)} collective-permute-done((f32[2,128,128]{2,1,0:T(8,128)S(1)}, f32[2,128,128]{2,1,0:T(8,128)S(1)}, u32[]{:S(2)}, u32[]{:S(2)}) %collective-permute-start.10) | collective-permute-done | bytes 131104 | tf_op jit(solution)/shard_map/ppermute | solution.py:242
  21.8 0.5 collective-permute-start.7
  22.3 2.1 %collective-permute-done.13.refs_14_ = f32[2,128,128]{2,1,0:T(8,128)S(1)} collective-permute-done((f32[2,128,128]{2,1,0:T(8,128)S(1)}, f32[2,128,128]{2,1,0:T(8,128)S(1)}, u32[]{:S(2)}, u32[]{:S(2)}) %collective-permute-start.13) | collective-permute-done | bytes 131104 | tf_op jit(solution)/shard_map/ppermute | solution.py:242
  24.5 1.3 %collective-permute-done.14.refs_15_ = f32[2,128,128]{2,1,0:T(8,128)S(1)} collective-permute-done((f32[2,128,128]{2,1,0:T(8,128)S(1)}, f32[2,128,128]{2,1,0:T(8,128)S(1)}, u32[]{:S(2)}, u32[]{:S(2)}) %collective-permute-start.14) | collective-permute-done | bytes 131104 | tf_op jit(solution)/shard_map/ppermute | solution.py:242
  25.8 6.0 %apply.2 = (f32[640,128]{1,0:T(8,128)S(1)}, f32[648,128]{1,0:T(8,128)S(1)}, f32[264,128]{1,0:T(8,128)S(1)}, f32[264,128]{1,0:T(8,128)S(1)}, f32[128,128]{1,0:T(8...) custom-call(s32[721]{0:T(1024)S(1)} %get-tuple-element.35.table_ref, ...), custom_call_target="tpu_custom_call" | custom-call | tf_op jit(solution)/shard_map/apply/pallas_call | solution.py:216
  32.0 0.5 collective-permute-start.16
  32.5 1.2 %collective-permute-start.17 = (f32[264,128]{1,0:T(8,128)S(1)}, f32[264,128]{1,0:T(8,128)S(1)}, u32[]{:S(2)}, u32[]{:S(2)}) collective-permute-start(f32[264,128]{1,0:T(8,128)S(1)} %get-tuple-element.44), channel_id=1, source_target_pairs={{0,3},{1,2},{2,1},{3,0},{4,7},{5,6},{6,5},{7,4},{8,11},{9,10},{10,... | collective-permute-start | bytes 405512 | tf_op jit(solution)/shard_map/ppermute | solution.py:242
  33.8 0.4 collective-permute-start.18
  34.2 1.3 %collective-permute-start.19 = (f32[128,128]{1,0:T(8,128)S(1)}, f32[128,128]{1,0:T(8,128)S(1)}, u32[]{:S(2)}, u32[]{:S(2)}) collective-permute-start(f32[128,128]{1,0:T(8,128)S(1)} %get-tuple-element.46), channel_id=1, source_target_pairs={{0,5},{1,4},{2,7},{3,6},{4,1},{5,0},{6,3},{7,2},{8,13},{9,12},{10,... | collective-permute-start | bytes 196616 | tf_op jit(solution)/shard_map/ppermute | solution.py:242
  35.5 3.2 %collective-permute-done.18.column_ref = f32[128,128]{1,0:T(8,128)S(1)} collective-permute-done((f32[128,128]{1,0:T(8,128)S(1)}, f32[128,128]{1,0:T(8,128)S(1)}, u32[]{:S(2)}, u32[]{:S(2)}) %collective-permute-start.18) | collective-permute-done | bytes 65568 | tf_op jit(solution)/shard_map/ppermute | solution.py:242
  38.7 0.3 collective-permute-done.19.column_far_ref
  39.0 1.4 %collective-permute-done.17.row_far_ref = f32[264,128]{1,0:T(8,128)S(1)} collective-permute-done((f32[264,128]{1,0:T(8,128)S(1)}, f32[264,128]{1,0:T(8,128)S(1)}, u32[]{:S(2)}, u32[]{:S(2)}) %collective-permute-start.17) | collective-permute-done | bytes 135200 | tf_op jit(solution)/shard_map/ppermute | solution.py:242
  40.3 0.7 fold.2
  41.1 3.7 %collective-permute-start.21 = (f32[264,128]{1,0:T(8,128)S(1)}, f32[264,128]{1,0:T(8,128)S(1)}, u32[]{:S(2)}, u32[]{:S(2)}) collective-permute-start(f32[264,128]{1,0:T(8,128)S(1)} %get-tuple-element.51), channel_id=1, source_target_pairs={{0,12},{1,13},{2,14},{3,15},{4,8},{5,9},{6,10},{7,11},{8,4},{9,5},... | collective-permute-start | bytes 405512 | tf_op jit(solution)/shard_map/ppermute | solution.py:242
  44.7 0.8 collective-permute-start.23
  45.5 0.6 collective-permute-start.20
  46.1 4.4 %collective-permute-done.20.step_ref = f32[2,128,128]{2,1,0:T(8,128)S(1)} collective-permute-done((f32[2,128,128]{2,1,0:T(8,128)S(1)}, f32[2,128,128]{2,1,0:T(8,128)S(1)}, u32[]{:S(2)}, u32[]{:S(2)}) %collective-permute-start.20) | collective-permute-done | bytes 131104 | tf_op jit(solution)/shard_map/ppermute | solution.py:242
  50.5 5.8 %collective-permute-done.22.refs_2_ = f32[264,128]{1,0:T(8,128)S(1)} collective-permute-done((f32[264,128]{1,0:T(8,128)S(1)}, f32[264,128]{1,0:T(8,128)S(1)}, u32[]{:S(2)}, u32[]{:S(2)}) %collective-permute-start.22) | collective-permute-done | bytes 135200 | tf_op jit(solution)/shard_map/ppermute | solution.py:242
  56.3 0.2 step.1.refs_0_.vector_ref
  56.5 2.7 %collective-permute-start.35 = (f32[2,128,128]{2,1,0:T(8,128)S(1)}, f32[2,128,128]{2,1,0:T(8,128)S(1)}, u32[]{:S(2)}, u32[]{:S(2)}) collective-permute-start(f32[2,128,128]{2,1,0:T(8,128)S(1)} %step.1.refs_0_.vector_ref), channel_id=1, source_target_pairs={{0,12},{1,13},{2,14},{3,15},{4,8},{5,9},{6,10},{7,11},{8,4},{9,5},... | collective-permute-start | bytes 393224 | tf_op jit(solution)/shard_map/ppermute | solution.py:242
  59.2 1.7 %collective-permute-start.27 = (f32[2,128,128]{2,1,0:T(8,128)S(1)}, f32[2,128,128]{2,1,0:T(8,128)S(1)}, u32[]{:S(2)}, u32[]{:S(2)}) collective-permute-start(f32[2,128,128]{2,1,0:T(8,128)S(1)} %step.1.refs_0_.vector_ref), channel_id=1, source_target_pairs={{0,4},{1,5},{2,6},{3,7},{4,0},{5,1},{6,2},{7,3},{8,12},{9,13},{10,... | collective-permute-start | bytes 393224 | tf_op jit(solution)/shard_map/ppermute | solution.py:242
  60.9 0.4 collective-permute-start.25
  61.3 3.5 %collective-permute-done.35.refs_12_ = f32[2,128,128]{2,1,0:T(8,128)S(1)} collective-permute-done((f32[2,128,128]{2,1,0:T(8,128)S(1)}, f32[2,128,128]{2,1,0:T(8,128)S(1)}, u32[]{:S(2)}, u32[]{:S(2)}) %collective-permute-start.35) | collective-permute-done | bytes 131104 | tf_op jit(solution)/shard_map/ppermute | solution.py:242
  64.8 0.4 collective-permute-start.37
  65.2 4.3 %collective-permute-done.31.refs_8_ = f32[2,128,128]{2,1,0:T(8,128)S(1)} collective-permute-done((f32[2,128,128]{2,1,0:T(8,128)S(1)}, f32[2,128,128]{2,1,0:T(8,128)S(1)}, u32[]{:S(2)}, u32[]{:S(2)}) %collective-permute-start.31) | collective-permute-done | bytes 131104 | tf_op jit(solution)/shard_map/ppermute | solution.py:242
  69.5 0.5 collective-permute-start.33
  70.0 0.2 collective-permute-start.32
  70.2 0.3 collective-permute-start.29
  70.6 0.2 collective-permute-done.36.refs_13_
  71.0 4.4 %collective-permute-done.33.refs_10_ = f32[2,128,128]{2,1,0:T(8,128)S(1)} collective-permute-done((f32[2,128,128]{2,1,0:T(8,128)S(1)}, f32[2,128,128]{2,1,0:T(8,128)S(1)}, u32[]{:S(2)}, u32[]{:S(2)}) %collective-permute-start.33) | collective-permute-done | bytes 131104 | tf_op jit(solution)/shard_map/ppermute | solution.py:242
  75.4 0.5 collective-permute-start.34
  76.0 0.8 collective-permute-done.38.refs_15_
  76.9 0.3 collective-permute-done.30.refs_7_
  77.3 6.1 %apply.3 = (f32[640,128]{1,0:T(8,128)S(1)}, f32[648,128]{1,0:T(8,128)S(1)}, f32[264,128]{1,0:T(8,128)S(1)}, f32[264,128]{1,0:T(8,128)S(1)}, f32[128,128]{1,0:T(8...) custom-call(s32[721]{0:T(1024)S(1)} %get-tuple-element.35.table_ref, ...), custom_call_target="tpu_custom_call" | custom-call | tf_op jit(solution)/shard_map/apply/pallas_call | solution.py:216
  83.4 0.2 collective-permute-start.39
  83.6 1.6 %collective-permute-start.40 = (f32[264,128]{1,0:T(8,128)S(1)}, f32[264,128]{1,0:T(8,128)S(1)}, u32[]{:S(2)}, u32[]{:S(2)}) collective-permute-start(f32[264,128]{1,0:T(8,128)S(1)} %get-tuple-element.55), channel_id=1, source_target_pairs={{0,2},{1,3},{2,0},{3,1},{4,6},{5,7},{6,4},{7,5},{8,10},{9,11},{10,... | collective-permute-start | bytes 405512 | tf_op jit(solution)/shard_map/ppermute | solution.py:242
  85.3 0.3 collective-permute-start.42
  85.7 1.5 %collective-permute-start.43 = (f32[128,128]{1,0:T(8,128)S(1)}, f32[128,128]{1,0:T(8,128)S(1)}, u32[]{:S(2)}, u32[]{:S(2)}) collective-permute-start(f32[128,128]{1,0:T(8,128)S(1)} %get-tuple-element.58), channel_id=1, source_target_pairs={{0,5},{1,4},{2,7},{3,6},{4,1},{5,0},{6,3},{7,2},{8,13},{9,12},{10,... | collective-permute-start | bytes 196616 | tf_op jit(solution)/shard_map/ppermute | solution.py:242
  87.1 3.1 %collective-permute-done.42.column_ref = f32[128,128]{1,0:T(8,128)S(1)} collective-permute-done((f32[128,128]{1,0:T(8,128)S(1)}, f32[128,128]{1,0:T(8,128)S(1)}, u32[]{:S(2)}, u32[]{:S(2)}) %collective-permute-start.42) | collective-permute-done | bytes 65568 | tf_op jit(solution)/shard_map/ppermute | solution.py:242
  90.2 0.5 collective-permute-done.43.column_far_ref
  90.7 1.1 collective-permute-done.41.row_far_ref
  91.8 0.7 fold.3
  92.6 1.3 %collective-permute-start.45 = (f32[264,128]{1,0:T(8,128)S(1)}, f32[264,128]{1,0:T(8,128)S(1)}, u32[]{:S(2)}, u32[]{:S(2)}) collective-permute-start(f32[264,128]{1,0:T(8,128)S(1)} %get-tuple-element.63), channel_id=1, source_target_pairs={{0,8},{1,9},{2,10},{3,11},{4,12},{5,13},{6,14},{7,15},{8,0},{9,1},... | collective-permute-start | bytes 405512 | tf_op jit(solution)/shard_map/ppermute | solution.py:242
  93.8 1.3 %collective-permute-start.46 = (f32[264,128]{1,0:T(8,128)S(1)}, f32[264,128]{1,0:T(8,128)S(1)}, u32[]{:S(2)}, u32[]{:S(2)}) collective-permute-start(f32[264,128]{1,0:T(8,128)S(1)} %get-tuple-element.64), channel_id=1, source_target_pairs={{0,12},{1,13},{2,14},{3,15},{4,8},{5,9},{6,10},{7,11},{8,4},{9,5},... | collective-permute-start | bytes 405512 | tf_op jit(solution)/shard_map/ppermute | solution.py:242
  95.2 1.0 collective-permute-start.47
  96.1 1.7 %collective-permute-start.44 = (f32[2,128,128]{2,1,0:T(8,128)S(1)}, f32[2,128,128]{2,1,0:T(8,128)S(1)}, u32[]{:S(2)}, u32[]{:S(2)}) collective-permute-start(f32[2,128,128]{2,1,0:T(8,128)S(1)} %get-tuple-element.60), channel_id=1, source_target_pairs={{0,2},{1,3},{2,0},{3,1},{4,6},{5,7},{6,4},{7,5},{8,10},{9,11},{10,... | collective-permute-start | bytes 393224 | tf_op jit(solution)/shard_map/ppermute | solution.py:242
  97.8 3.3 %collective-permute-done.44.step_ref = f32[2,128,128]{2,1,0:T(8,128)S(1)} collective-permute-done((f32[2,128,128]{2,1,0:T(8,128)S(1)}, f32[2,128,128]{2,1,0:T(8,128)S(1)}, u32[]{:S(2)}, u32[]{:S(2)}) %collective-permute-start.44) | collective-permute-done | bytes 131104 | tf_op jit(solution)/shard_map/ppermute | solution.py:242
  101.1 3.9 %collective-permute-done.45.refs_1_ = f32[264,128]{1,0:T(8,128)S(1)} collective-permute-done((f32[264,128]{1,0:T(8,128)S(1)}, f32[264,128]{1,0:T(8,128)S(1)}, u32[]{:S(2)}, u32[]{:S(2)}) %collective-permute-start.45) | collective-permute-done | bytes 135200 | tf_op jit(solution)/shard_map/ppermute | solution.py:242
  105.1 1.3 %collective-permute-done.47.refs_3_ = f32[264,128]{1,0:T(8,128)S(1)} collective-permute-done((f32[264,128]{1,0:T(8,128)S(1)}, f32[264,128]{1,0:T(8,128)S(1)}, u32[]{:S(2)}, u32[]{:S(2)}) %collective-permute-start.47) | collective-permute-done | bytes 135200 | tf_op jit(solution)/shard_map/ppermute | solution.py:242
  106.3 0.9 last.1
  107.2 11.7 %all_to_all.5.tiles_ref = f32[16,8,128]{2,1,0:T(8,128)S(1)} all-to-all(f32[16,8,128]{2,1,0:T(8,128)S(1)} %broadcast_in_dim.2), channel_id=1, replica_groups=mesh['group'=2,'term'=16] {'term'}, dimensions={0} | all-to-all | bytes 131072 | tf_op jit(solution)/shard_map/all_to_all | solution.py:385
  118.9 0.9 norm.1
  (47 shorter events, 1.2 us)
Async XLA Ops:
  0.6 7.2 %collective-permute-start.2 = (f32[2,128,128]{2,1,0:T(8,128)}, f32[2,128,128]{2,1,0:T(8,128)S(1)}, u32[]{:S(2)}, u32[]{:S(2)}) collective-permute-start(f32[2,128,128]{2,1,0:T(8,128)} %vector_in.1), channel_id=1, source_target_pairs={{0,2},{1,3},{2,0},{3,1},{4,6},{5,7},{6,4},{7,5},{8,10},{9,11},{10,... | collective-permute-start | bytes 393224 | tf_op jit(solution)/shard_map/ppermute | solution.py:242
  3.7 12.9 %collective-permute-start.8 = (f32[2,128,128]{2,1,0:T(8,128)}, f32[2,128,128]{2,1,0:T(8,128)S(1)}, u32[]{:S(2)}, u32[]{:S(2)}) collective-permute-start(f32[2,128,128]{2,1,0:T(8,128)} %vector_in.1), channel_id=1, source_target_pairs={{0,8},{1,9},{2,10},{3,11},{4,12},{5,13},{6,14},{7,15},{8,0},{9,1},... | collective-permute-start | bytes 393224 | tf_op jit(solution)/shard_map/ppermute | solution.py:242
  6.3 10.7 %collective-permute-start = (f32[2,128,128]{2,1,0:T(8,128)}, f32[2,128,128]{2,1,0:T(8,128)S(1)}, u32[]{:S(2)}, u32[]{:S(2)}) collective-permute-start(f32[2,128,128]{2,1,0:T(8,128)} %vector_in.1), channel_id=1, source_target_pairs={{0,12},{1,13},{2,14},{3,15},{4,8},{5,9},{6,10},{7,11},{8,4},{9,5},... | collective-permute-start | bytes 393224 | tf_op jit(solution)/shard_map/ppermute | solution.py:242
  7.6 10.5 %collective-permute-start.4 = (f32[2,128,128]{2,1,0:T(8,128)}, f32[2,128,128]{2,1,0:T(8,128)S(1)}, u32[]{:S(2)}, u32[]{:S(2)}) collective-permute-start(f32[2,128,128]{2,1,0:T(8,128)} %vector_in.1), channel_id=1, source_target_pairs={{0,4},{1,5},{2,6},{3,7},{4,0},{5,1},{6,2},{7,3},{8,12},{9,13},{10,... | collective-permute-start | bytes 393224 | tf_op jit(solution)/shard_map/ppermute | solution.py:242
  7.8 11.7 %collective-permute-start.6 = (f32[2,128,128]{2,1,0:T(8,128)S(1)}, f32[2,128,128]{2,1,0:T(8,128)S(1)}, u32[]{:S(2)}, u32[]{:S(2)}) collective-permute-start(f32[2,128,128]{2,1,0:T(8,128)S(1)} %collective-permute-done.2.refs_2_), channel_id=1, source_target_pairs={{0,4},{1,5},{2,6},{3,7},{4,0},{5,1},{6,2},{7,3},{8,12},{9,13},{10,... | collective-permute-start | bytes 393224 | tf_op jit(solution)/shard_map/ppermute | solution.py:242
  9.6 0.7 copy-start.1
  14.3 5.7 %collective-permute-start.3 = (f32[2,128,128]{2,1,0:T(8,128)S(1)}, f32[2,128,128]{2,1,0:T(8,128)S(1)}, u32[]{:S(2)}, u32[]{:S(2)}) collective-permute-start(f32[2,128,128]{2,1,0:T(8,128)S(1)} %collective-permute-done.2.refs_2_), channel_id=1, source_target_pairs={{0,1},{1,0},{2,3},{3,2},{4,5},{5,4},{6,7},{7,6},{8,9},{9,8},{10,11... | collective-permute-start | bytes 393224 | tf_op jit(solution)/shard_map/ppermute | solution.py:242
  16.5 5.2 %collective-permute-start.10 = (f32[2,128,128]{2,1,0:T(8,128)S(1)}, f32[2,128,128]{2,1,0:T(8,128)S(1)}, u32[]{:S(2)}, u32[]{:S(2)}) collective-permute-start(f32[2,128,128]{2,1,0:T(8,128)S(1)} %collective-permute-done.8.refs_8_), channel_id=1, source_target_pairs={{0,2},{1,3},{2,0},{3,1},{4,6},{5,7},{6,4},{7,5},{8,10},{9,11},{10,... | collective-permute-start | bytes 393224 | tf_op jit(solution)/shard_map/ppermute | solution.py:242
  17.0 4.8 %collective-permute-start.9 = (f32[2,128,128]{2,1,0:T(8,128)S(1)}, f32[2,128,128]{2,1,0:T(8,128)S(1)}, u32[]{:S(2)}, u32[]{:S(2)}) collective-permute-start(f32[2,128,128]{2,1,0:T(8,128)S(1)} %collective-permute-done.8.refs_8_), channel_id=1, source_target_pairs={{0,1},{1,0},{2,3},{3,2},{4,5},{5,4},{6,7},{7,6},{8,9},{9,8},{10,11... | collective-permute-start | bytes 393224 | tf_op jit(solution)/shard_map/ppermute | solution.py:242
  18.1 4.2 %collective-permute-start.5 = (f32[2,128,128]{2,1,0:T(8,128)S(1)}, f32[2,128,128]{2,1,0:T(8,128)S(1)}, u32[]{:S(2)}, u32[]{:S(2)}) collective-permute-start(f32[2,128,128]{2,1,0:T(8,128)S(1)} %collective-permute-done.4.refs_4_), channel_id=1, source_target_pairs={{0,1},{1,0},{2,3},{3,2},{4,5},{5,4},{6,7},{7,6},{8,9},{9,8},{10,11... | collective-permute-start | bytes 393224 | tf_op jit(solution)/shard_map/ppermute | solution.py:242
  19.5 5.0 %collective-permute-start.13 = (f32[2,128,128]{2,1,0:T(8,128)S(1)}, f32[2,128,128]{2,1,0:T(8,128)S(1)}, u32[]{:S(2)}, u32[]{:S(2)}) collective-permute-start(f32[2,128,128]{2,1,0:T(8,128)S(1)} %collective-permute-done.refs_12_), channel_id=1, source_target_pairs={{0,2},{1,3},{2,0},{3,1},{4,6},{5,7},{6,4},{7,5},{8,10},{9,11},{10,... | collective-permute-start | bytes 393224 | tf_op jit(solution)/shard_map/ppermute | solution.py:242
  20.0 4.5 %collective-permute-start.12 = (f32[2,128,128]{2,1,0:T(8,128)S(1)}, f32[2,128,128]{2,1,0:T(8,128)S(1)}, u32[]{:S(2)}, u32[]{:S(2)}) collective-permute-start(f32[2,128,128]{2,1,0:T(8,128)S(1)} %collective-permute-done.refs_12_), channel_id=1, source_target_pairs={{0,1},{1,0},{2,3},{3,2},{4,5},{5,4},{6,7},{7,6},{8,9},{9,8},{10,11... | collective-permute-start | bytes 393224 | tf_op jit(solution)/shard_map/ppermute | solution.py:242
  21.8 2.7 %collective-permute-start.1 = (f32[2,128,128]{2,1,0:T(8,128)S(1)}, f32[2,128,128]{2,1,0:T(8,128)S(1)}, u32[]{:S(2)}, u32[]{:S(2)}) collective-permute-start(f32[2,128,128]{2,1,0:T(8,128)S(1)} %get-tuple-element.39.refs_0_.vector_ref), channel_id=1, source_target_pairs={{0,1},{1,0},{2,3},{3,2},{4,5},{5,4},{6,7},{7,6},{8,9},{9,8},{10,11... | collective-permute-start | bytes 393224 | tf_op jit(solution)/shard_map/ppermute | solution.py:242
  21.8 2.7 %collective-permute-start.7 = (f32[2,128,128]{2,1,0:T(8,128)S(1)}, f32[2,128,128]{2,1,0:T(8,128)S(1)}, u32[]{:S(2)}, u32[]{:S(2)}) collective-permute-start(f32[2,128,128]{2,1,0:T(8,128)S(1)} %collective-permute-done.6.refs_6_), channel_id=1, source_target_pairs={{0,1},{1,0},{2,3},{3,2},{4,5},{5,4},{6,7},{7,6},{8,9},{9,8},{10,11... | collective-permute-start | bytes 393224 | tf_op jit(solution)/shard_map/ppermute | solution.py:242
  22.3 2.2 %collective-permute-start.11 = (f32[2,128,128]{2,1,0:T(8,128)S(1)}, f32[2,128,128]{2,1,0:T(8,128)S(1)}, u32[]{:S(2)}, u32[]{:S(2)}) collective-permute-start(f32[2,128,128]{2,1,0:T(8,128)S(1)} %collective-permute-done.10.refs_10_), channel_id=1, source_target_pairs={{0,1},{1,0},{2,3},{3,2},{4,5},{5,4},{6,7},{7,6},{8,9},{9,8},{10,11... | collective-permute-start | bytes 393224 | tf_op jit(solution)/shard_map/ppermute | solution.py:242
  24.5 1.3 %collective-permute-start.14 = (f32[2,128,128]{2,1,0:T(8,128)S(1)}, f32[2,128,128]{2,1,0:T(8,128)S(1)}, u32[]{:S(2)}, u32[]{:S(2)}) collective-permute-start(f32[2,128,128]{2,1,0:T(8,128)S(1)} %collective-permute-done.13.refs_14_), channel_id=1, source_target_pairs={{0,1},{1,0},{2,3},{3,2},{4,5},{5,4},{6,7},{7,6},{8,9},{9,8},{10,11... | collective-permute-start | bytes 393224 | tf_op jit(solution)/shard_map/ppermute | solution.py:242
  31.8 8.5 %collective-permute-start.15 = (f32[648,128]{1,0:T(8,128)S(1)}, f32[648,128]{1,0:T(8,128)S(1)}, u32[]{:S(2)}, u32[]{:S(2)}) collective-permute-start(f32[648,128]{1,0:T(8,128)S(1)} %get-tuple-element.42.far_in), channel_id=1, source_target_pairs={{0,1},{1,0},{2,3},{3,2},{4,5},{5,4},{6,7},{7,6},{8,9},{9,8},{10,11... | collective-permute-start | bytes 995336 | tf_op jit(solution)/shard_map/ppermute | solution.py:242
  32.0 7.0 %collective-permute-start.16 = (f32[264,128]{1,0:T(8,128)S(1)}, f32[264,128]{1,0:T(8,128)S(1)}, u32[]{:S(2)}, u32[]{:S(2)}) collective-permute-start(f32[264,128]{1,0:T(8,128)S(1)} %get-tuple-element.43), channel_id=1, source_target_pairs={{0,2},{1,3},{2,0},{3,1},{4,6},{5,7},{6,4},{7,5},{8,10},{9,11},{10,... | collective-permute-start | bytes 405512 | tf_op jit(solution)/shard_map/ppermute | solution.py:242
  32.5 7.8 %collective-permute-start.17 = (f32[264,128]{1,0:T(8,128)S(1)}, f32[264,128]{1,0:T(8,128)S(1)}, u32[]{:S(2)}, u32[]{:S(2)}) collective-permute-start(f32[264,128]{1,0:T(8,128)S(1)} %get-tuple-element.44), channel_id=1, source_target_pairs={{0,3},{1,2},{2,1},{3,0},{4,7},{5,6},{6,5},{7,4},{8,11},{9,10},{10,... | collective-permute-start | bytes 405512 | tf_op jit(solution)/shard_map/ppermute | solution.py:242
  33.8 4.9 %collective-permute-start.18 = (f32[128,128]{1,0:T(8,128)S(1)}, f32[128,128]{1,0:T(8,128)S(1)}, u32[]{:S(2)}, u32[]{:S(2)}) collective-permute-start(f32[128,128]{1,0:T(8,128)S(1)} %get-tuple-element.45), channel_id=1, source_target_pairs={{0,4},{1,5},{2,6},{3,7},{4,0},{5,1},{6,2},{7,3},{8,12},{9,13},{10,... | collective-permute-start | bytes 196616 | tf_op jit(solution)/shard_map/ppermute | solution.py:242
  34.2 4.8 %collective-permute-start.19 = (f32[128,128]{1,0:T(8,128)S(1)}, f32[128,128]{1,0:T(8,128)S(1)}, u32[]{:S(2)}, u32[]{:S(2)}) collective-permute-start(f32[128,128]{1,0:T(8,128)S(1)} %get-tuple-element.46), channel_id=1, source_target_pairs={{0,5},{1,4},{2,7},{3,6},{4,1},{5,0},{6,3},{7,2},{8,13},{9,12},{10,... | collective-permute-start | bytes 196616 | tf_op jit(solution)/shard_map/ppermute | solution.py:242
  40.3 15.9 %copy-start = (f32[2,128,128]{2,1,0:T(8,128)S(1)}, f32[2,128,128]{2,1,0:T(8,128)}, u32[]{:S(2)}) copy-start(f32[2,128,128]{2,1,0:T(8,128)} %precond_ref.3) | copy-start | bytes 393220
  41.1 9.4 %collective-permute-start.21 = (f32[264,128]{1,0:T(8,128)S(1)}, f32[264,128]{1,0:T(8,128)S(1)}, u32[]{:S(2)}, u32[]{:S(2)}) collective-permute-start(f32[264,128]{1,0:T(8,128)S(1)} %get-tuple-element.51), channel_id=1, source_target_pairs={{0,12},{1,13},{2,14},{3,15},{4,8},{5,9},{6,10},{7,11},{8,4},{9,5},... | collective-permute-start | bytes 405512 | tf_op jit(solution)/shard_map/ppermute | solution.py:242
  44.7 11.5 %collective-permute-start.22 = (f32[264,128]{1,0:T(8,128)S(1)}, f32[264,128]{1,0:T(8,128)S(1)}, u32[]{:S(2)}, u32[]{:S(2)}) collective-permute-start(f32[264,128]{1,0:T(8,128)S(1)} %get-tuple-element.52), channel_id=1, source_target_pairs={{0,8},{1,9},{2,10},{3,11},{4,12},{5,13},{6,14},{7,15},{8,0},{9,1},... | collective-permute-start | bytes 405512 | tf_op jit(solution)/shard_map/ppermute | solution.py:242
  44.7 11.5 %collective-permute-start.23 = (f32[264,128]{1,0:T(8,128)S(1)}, f32[264,128]{1,0:T(8,128)S(1)}, u32[]{:S(2)}, u32[]{:S(2)}) collective-permute-start(f32[264,128]{1,0:T(8,128)S(1)} %get-tuple-element.50.refs_0_), channel_id=1, source_target_pairs={{0,4},{1,5},{2,6},{3,7},{4,0},{5,1},{6,2},{7,3},{8,12},{9,13},{10,... | collective-permute-start | bytes 405512 | tf_op jit(solution)/shard_map/ppermute | solution.py:242
  45.5 5.0 %collective-permute-start.20 = (f32[2,128,128]{2,1,0:T(8,128)S(1)}, f32[2,128,128]{2,1,0:T(8,128)S(1)}, u32[]{:S(2)}, u32[]{:S(2)}) collective-permute-start(f32[2,128,128]{2,1,0:T(8,128)S(1)} %get-tuple-element.48), channel_id=1, source_target_pairs={{0,2},{1,3},{2,0},{3,1},{4,6},{5,7},{6,4},{7,5},{8,10},{9,11},{10,... | collective-permute-start | bytes 393224 | tf_op jit(solution)/shard_map/ppermute | solution.py:242
  56.5 8.3 %collective-permute-start.35 = (f32[2,128,128]{2,1,0:T(8,128)S(1)}, f32[2,128,128]{2,1,0:T(8,128)S(1)}, u32[]{:S(2)}, u32[]{:S(2)}) collective-permute-start(f32[2,128,128]{2,1,0:T(8,128)S(1)} %step.1.refs_0_.vector_ref), channel_id=1, source_target_pairs={{0,12},{1,13},{2,14},{3,15},{4,8},{5,9},{6,10},{7,11},{8,4},{9,5},... | collective-permute-start | bytes 393224 | tf_op jit(solution)/shard_map/ppermute | solution.py:242
  59.2 10.3 %collective-permute-start.31 = (f32[2,128,128]{2,1,0:T(8,128)S(1)}, f32[2,128,128]{2,1,0:T(8,128)S(1)}, u32[]{:S(2)}, u32[]{:S(2)}) collective-permute-start(f32[2,128,128]{2,1,0:T(8,128)S(1)} %step.1.refs_0_.vector_ref), channel_id=1, source_target_pairs={{0,8},{1,9},{2,10},{3,11},{4,12},{5,13},{6,14},{7,15},{8,0},{9,1},... | collective-permute-start | bytes 393224 | tf_op jit(solution)/shard_map/ppermute | solution.py:242
  59.2 10.3 %collective-permute-start.27 = (f32[2,128,128]{2,1,0:T(8,128)S(1)}, f32[2,128,128]{2,1,0:T(8,128)S(1)}, u32[]{:S(2)}, u32[]{:S(2)}) collective-permute-start(f32[2,128,128]{2,1,0:T(8,128)S(1)} %step.1.refs_0_.vector_ref), channel_id=1, source_target_pairs={{0,4},{1,5},{2,6},{3,7},{4,0},{5,1},{6,2},{7,3},{8,12},{9,13},{10,... | collective-permute-start | bytes 393224 | tf_op jit(solution)/shard_map/ppermute | solution.py:242
  60.9 9.0 %collective-permute-start.25 = (f32[2,128,128]{2,1,0:T(8,128)S(1)}, f32[2,128,128]{2,1,0:T(8,128)S(1)}, u32[]{:S(2)}, u32[]{:S(2)}) collective-permute-start(f32[2,128,128]{2,1,0:T(8,128)S(1)} %step.1.refs_0_.vector_ref), channel_id=1, source_target_pairs={{0,2},{1,3},{2,0},{3,1},{4,6},{5,7},{6,4},{7,5},{8,10},{9,11},{10,... | collective-permute-start | bytes 393224 | tf_op jit(solution)/shard_map/ppermute | solution.py:242
  61.3 8.8 %collective-permute-start.24 = (f32[2,128,128]{2,1,0:T(8,128)S(1)}, f32[2,128,128]{2,1,0:T(8,128)S(1)}, u32[]{:S(2)}, u32[]{:S(2)}) collective-permute-start(f32[2,128,128]{2,1,0:T(8,128)S(1)} %step.1.refs_0_.vector_ref), channel_id=1, source_target_pairs={{0,1},{1,0},{2,3},{3,2},{4,5},{5,4},{6,7},{7,6},{8,9},{9,8},{10,11... | collective-permute-start | bytes 393224 | tf_op jit(solution)/shard_map/ppermute | solution.py:242
  64.8 5.7 %collective-permute-start.37 = (f32[2,128,128]{2,1,0:T(8,128)S(1)}, f32[2,128,128]{2,1,0:T(8,128)S(1)}, u32[]{:S(2)}, u32[]{:S(2)}) collective-permute-start(f32[2,128,128]{2,1,0:T(8,128)S(1)} %collective-permute-done.35.refs_12_), channel_id=1, source_target_pairs={{0,2},{1,3},{2,0},{3,1},{4,6},{5,7},{6,4},{7,5},{8,10},{9,11},{10,... | collective-permute-start | bytes 393224 | tf_op jit(solution)/shard_map/ppermute | solution.py:242
  69.5 1.3 %collective-permute-start.36 = (f32[2,128,128]{2,1,0:T(8,128)S(1)}, f32[2,128,128]{2,1,0:T(8,128)S(1)}, u32[]{:S(2)}, u32[]{:S(2)}) collective-permute-start(f32[2,128,128]{2,1,0:T(8,128)S(1)} %collective-permute-done.35.refs_12_), channel_id=1, source_target_pairs={{0,1},{1,0},{2,3},{3,2},{4,5},{5,4},{6,7},{7,6},{8,9},{9,8},{10,11... | collective-permute-start | bytes 393224 | tf_op jit(solution)/shard_map/ppermute | solution.py:242
  69.5 5.9 %collective-permute-start.33 = (f32[2,128,128]{2,1,0:T(8,128)S(1)}, f32[2,128,128]{2,1,0:T(8,128)S(1)}, u32[]{:S(2)}, u32[]{:S(2)}) collective-permute-start(f32[2,128,128]{2,1,0:T(8,128)S(1)} %collective-permute-done.31.refs_8_), channel_id=1, source_target_pairs={{0,2},{1,3},{2,0},{3,1},{4,6},{5,7},{6,4},{7,5},{8,10},{9,11},{10,... | collective-permute-start | bytes 393224 | tf_op jit(solution)/shard_map/ppermute | solution.py:242
  70.0 5.5 %collective-permute-start.32 = (f32[2,128,128]{2,1,0:T(8,128)S(1)}, f32[2,128,128]{2,1,0:T(8,128)S(1)}, u32[]{:S(2)}, u32[]{:S(2)}) collective-permute-start(f32[2,128,128]{2,1,0:T(8,128)S(1)} %collective-permute-done.31.refs_8_), channel_id=1, source_target_pairs={{0,1},{1,0},{2,3},{3,2},{4,5},{5,4},{6,7},{7,6},{8,9},{9,8},{10,11... | collective-permute-start | bytes 393224 | tf_op jit(solution)/shard_map/ppermute | solution.py:242
  70.2 5.8 %collective-permute-start.29 = (f32[2,128,128]{2,1,0:T(8,128)S(1)}, f32[2,128,128]{2,1,0:T(8,128)S(1)}, u32[]{:S(2)}, u32[]{:S(2)}) collective-permute-start(f32[2,128,128]{2,1,0:T(8,128)S(1)} %collective-permute-done.25.refs_2_), channel_id=1, source_target_pairs={{0,4},{1,5},{2,6},{3,7},{4,0},{5,1},{6,2},{7,3},{8,12},{9,13},{10,... | collective-permute-start | bytes 393224 | tf_op jit(solution)/shard_map/ppermute | solution.py:242
  70.4 5.6 %collective-permute-start.26 = (f32[2,128,128]{2,1,0:T(8,128)S(1)}, f32[2,128,128]{2,1,0:T(8,128)S(1)}, u32[]{:S(2)}, u32[]{:S(2)}) collective-permute-start(f32[2,128,128]{2,1,0:T(8,128)S(1)} %collective-permute-done.25.refs_2_), channel_id=1, source_target_pairs={{0,1},{1,0},{2,3},{3,2},{4,5},{5,4},{6,7},{7,6},{8,9},{9,8},{10,11... | collective-permute-start | bytes 393224 | tf_op jit(solution)/shard_map/ppermute | solution.py:242
  70.8 5.2 %collective-permute-start.28 = (f32[2,128,128]{2,1,0:T(8,128)S(1)}, f32[2,128,128]{2,1,0:T(8,128)S(1)}, u32[]{:S(2)}, u32[]{:S(2)}) collective-permute-start(f32[2,128,128]{2,1,0:T(8,128)S(1)} %collective-permute-done.27.refs_4_), channel_id=1, source_target_pairs={{0,1},{1,0},{2,3},{3,2},{4,5},{5,4},{6,7},{7,6},{8,9},{9,8},{10,11... | collective-permute-start | bytes 393224 | tf_op jit(solution)/shard_map/ppermute | solution.py:242
  75.4 1.3 %collective-permute-start.38 = (f32[2,128,128]{2,1,0:T(8,128)S(1)}, f32[2,128,128]{2,1,0:T(8,128)S(1)}, u32[]{:S(2)}, u32[]{:S(2)}) collective-permute-start(f32[2,128,128]{2,1,0:T(8,128)S(1)} %collective-permute-done.37.refs_14_), channel_id=1, source_target_pairs={{0,1},{1,0},{2,3},{3,2},{4,5},{5,4},{6,7},{7,6},{8,9},{9,8},{10,11... | collective-permute-start | bytes 393224 | tf_op jit(solution)/shard_map/ppermute | solution.py:242
  75.4 1.5 %collective-permute-start.34 = (f32[2,128,128]{2,1,0:T(8,128)S(1)}, f32[2,128,128]{2,1,0:T(8,128)S(1)}, u32[]{:S(2)}, u32[]{:S(2)}) collective-permute-start(f32[2,128,128]{2,1,0:T(8,128)S(1)} %collective-permute-done.33.refs_10_), channel_id=1, source_target_pairs={{0,1},{1,0},{2,3},{3,2},{4,5},{5,4},{6,7},{7,6},{8,9},{9,8},{10,11... | collective-permute-start | bytes 393224 | tf_op jit(solution)/shard_map/ppermute | solution.py:242
  75.9 1.3 %collective-permute-start.30 = (f32[2,128,128]{2,1,0:T(8,128)S(1)}, f32[2,128,128]{2,1,0:T(8,128)S(1)}, u32[]{:S(2)}, u32[]{:S(2)}) collective-permute-start(f32[2,128,128]{2,1,0:T(8,128)S(1)} %collective-permute-done.29.refs_6_), channel_id=1, source_target_pairs={{0,1},{1,0},{2,3},{3,2},{4,5},{5,4},{6,7},{7,6},{8,9},{9,8},{10,11... | collective-permute-start | bytes 393224 | tf_op jit(solution)/shard_map/ppermute | solution.py:242
  83.4 8.4 %collective-permute-start.39 = (f32[648,128]{1,0:T(8,128)S(1)}, f32[648,128]{1,0:T(8,128)S(1)}, u32[]{:S(2)}, u32[]{:S(2)}) collective-permute-start(f32[648,128]{1,0:T(8,128)S(1)} %get-tuple-element.54.far_in), channel_id=1, source_target_pairs={{0,1},{1,0},{2,3},{3,2},{4,5},{5,4},{6,7},{7,6},{8,9},{9,8},{10,11... | collective-permute-start | bytes 995336 | tf_op jit(solution)/shard_map/ppermute | solution.py:242
  83.6 7.1 %collective-permute-start.40 = (f32[264,128]{1,0:T(8,128)S(1)}, f32[264,128]{1,0:T(8,128)S(1)}, u32[]{:S(2)}, u32[]{:S(2)}) collective-permute-start(f32[264,128]{1,0:T(8,128)S(1)} %get-tuple-element.55), channel_id=1, source_target_pairs={{0,2},{1,3},{2,0},{3,1},{4,6},{5,7},{6,4},{7,5},{8,10},{9,11},{10,... | collective-permute-start | bytes 405512 | tf_op jit(solution)/shard_map/ppermute | solution.py:242
  85.2 6.7 %collective-permute-start.41 = (f32[264,128]{1,0:T(8,128)S(1)}, f32[264,128]{1,0:T(8,128)S(1)}, u32[]{:S(2)}, u32[]{:S(2)}) collective-permute-start(f32[264,128]{1,0:T(8,128)S(1)} %get-tuple-element.56), channel_id=1, source_target_pairs={{0,3},{1,2},{2,1},{3,0},{4,7},{5,6},{6,5},{7,4},{8,11},{9,10},{10,... | collective-permute-start | bytes 405512 | tf_op jit(solution)/shard_map/ppermute | solution.py:242
  85.3 4.9 %collective-permute-start.42 = (f32[128,128]{1,0:T(8,128)S(1)}, f32[128,128]{1,0:T(8,128)S(1)}, u32[]{:S(2)}, u32[]{:S(2)}) collective-permute-start(f32[128,128]{1,0:T(8,128)S(1)} %get-tuple-element.57), channel_id=1, source_target_pairs={{0,4},{1,5},{2,6},{3,7},{4,0},{5,1},{6,2},{7,3},{8,12},{9,13},{10,... | collective-permute-start | bytes 196616 | tf_op jit(solution)/shard_map/ppermute | solution.py:242
  85.7 5.1 %collective-permute-start.43 = (f32[128,128]{1,0:T(8,128)S(1)}, f32[128,128]{1,0:T(8,128)S(1)}, u32[]{:S(2)}, u32[]{:S(2)}) collective-permute-start(f32[128,128]{1,0:T(8,128)S(1)} %get-tuple-element.58), channel_id=1, source_target_pairs={{0,5},{1,4},{2,7},{3,6},{4,1},{5,0},{6,3},{7,2},{8,13},{9,12},{10,... | collective-permute-start | bytes 196616 | tf_op jit(solution)/shard_map/ppermute | solution.py:242
  92.6 12.5 %collective-permute-start.45 = (f32[264,128]{1,0:T(8,128)S(1)}, f32[264,128]{1,0:T(8,128)S(1)}, u32[]{:S(2)}, u32[]{:S(2)}) collective-permute-start(f32[264,128]{1,0:T(8,128)S(1)} %get-tuple-element.63), channel_id=1, source_target_pairs={{0,8},{1,9},{2,10},{3,11},{4,12},{5,13},{6,14},{7,15},{8,0},{9,1},... | collective-permute-start | bytes 405512 | tf_op jit(solution)/shard_map/ppermute | solution.py:242
  93.8 11.2 %collective-permute-start.46 = (f32[264,128]{1,0:T(8,128)S(1)}, f32[264,128]{1,0:T(8,128)S(1)}, u32[]{:S(2)}, u32[]{:S(2)}) collective-permute-start(f32[264,128]{1,0:T(8,128)S(1)} %get-tuple-element.64), channel_id=1, source_target_pairs={{0,12},{1,13},{2,14},{3,15},{4,8},{5,9},{6,10},{7,11},{8,4},{9,5},... | collective-permute-start | bytes 405512 | tf_op jit(solution)/shard_map/ppermute | solution.py:242
  95.2 11.2 %collective-permute-start.47 = (f32[264,128]{1,0:T(8,128)S(1)}, f32[264,128]{1,0:T(8,128)S(1)}, u32[]{:S(2)}, u32[]{:S(2)}) collective-permute-start(f32[264,128]{1,0:T(8,128)S(1)} %get-tuple-element.62.refs_0_), channel_id=1, source_target_pairs={{0,4},{1,5},{2,6},{3,7},{4,0},{5,1},{6,2},{7,3},{8,12},{9,13},{10,... | collective-permute-start | bytes 405512 | tf_op jit(solution)/shard_map/ppermute | solution.py:242
  96.1 5.0 %collective-permute-start.44 = (f32[2,128,128]{2,1,0:T(8,128)S(1)}, f32[2,128,128]{2,1,0:T(8,128)S(1)}, u32[]{:S(2)}, u32[]{:S(2)}) collective-permute-start(f32[2,128,128]{2,1,0:T(8,128)S(1)} %get-tuple-element.60), channel_id=1, source_target_pairs={{0,2},{1,3},{2,0},{3,1},{4,6},{5,7},{6,4},{7,5},{8,10},{9,11},{10,... | collective-permute-start | bytes 393224 | tf_op jit(solution)/shard_map/ppermute | solution.py:242
